TPU v7x, 256 devices: a whole 4x4x8 slice. The times are simulated.
256 devices in a mesh: ctx: 32 (over y, z_hi, core), ch: 8 (over z_lo, x).
Axes of the slice: x: 4, y: 4, z: 8 (z_hi: 4, z_lo: 2; z = z_hi * 2 + z_lo), core: 2. Of those that a mesh axis runs over, the one named last changes fastest.
Arguments:
- tokens: bfloat16 [8192, 4096], P('ctx', 'ch'), may hold values from -6 to 6
- w_in: bfloat16 [4096, 3, 4096], P('ctx', None, 'ch'), may hold values from -0.09375 to 0.09375
- taps: float32 [3, 3, 4096], P(None, None, 'ch'), may hold values from -2 to 2
- modes_gain: float32 [16, 4096], P(None, 'ch'), may hold values from -1.5 to 1.5
- decay: float32 [16, 4096], P(None, 'ch'), may hold values from 0.3 to 300
- skip: float32 [4096], P('ch'), may hold values from -4 to 4
Outputs:
- mixed: bfloat16 [8192, 4096], P('ctx', 'ch')
All inputs are finite; a program needn't handle non-finite values.
Results may differ from a plain program's by a relative error of at most 0.0075.
Values may be sent and summed in bfloat16 or wider, within the bound.
No kernel may reach another device: no remote copies, remote signals or barrier semaphores. Data moves between devices by JAX's collectives and lax.ppermute only.
A program may use at most 64 MiB of HBM per device.

v0:
```python
import jax
import jax.numpy as jnp
from jax import lax
from jax.sharding import Mesh
from jax.sharding import PartitionSpec as P

CTX = ("ctx_0", "ctx_1", "ctx_2")


def laid_out(parts, dim):
    shape = list(parts.shape[1:])
    shape[dim] *= parts.shape[0]
    return jnp.moveaxis(parts, 0, dim).reshape(shape)


def sent_to_all(array, axis):
    copies = jnp.broadcast_to(array, (lax.axis_size(axis), *array.shape))
    return lax.all_to_all(copies, axis, split_axis=0, concat_axis=0, tiled=True)


def gathered_copies(array, axis, dim):
    return laid_out(sent_to_all(array, axis), dim)


def from_behind(block, axis, distance):
    devices = range(lax.axis_size(axis))
    route = [(i - distance, i) for i in devices if i - distance in devices]
    return lax.ppermute(block, axis, route)


def neutral_like(array, identity):
    return jax.tree.map(
        lambda a, e: jnp.broadcast_to(jnp.asarray(e, a.dtype), a.shape), array, identity
    )


def gathered_once(array, axis):
    leaves = jax.tree.leaves(array)
    turns = sorted(range(len(leaves)), key=lambda k: -leaves[k].size)
    width = (1, *leaves[turns[0]].shape)[-1]
    lines = [
        jnp.pad(leaves[k].reshape(-1), (0, -leaves[k].size % width)).reshape(-1, width)
        for k in turns
    ]
    both, at, found = (lax.all_gather(jnp.concatenate(lines), axis), 0, {})
    for k, line in zip(turns, lines):
        piece = both[:, at : at + len(line)].reshape(len(both), -1)
        found[k] = piece[:, : leaves[k].size].reshape(-1, *leaves[k].shape)
        at += len(line)
    numbers = iter(range(len(leaves)))
    return jax.tree.map(lambda _: found[next(numbers)], array)


def carried_in(array, axes, combine, identity):
    before = start = neutral_like(array, identity)
    so_far = array
    for axis in reversed(axes):
        devices, here = (lax.axis_size(axis), lax.axis_index(axis))
        pieces = gathered_once(so_far, axis)
        inside, so_far = (start, start)
        for k in range(devices):
            passed = k < here
            so_far = combine(so_far, jax.tree.map(lambda part: part[k], pieces))
            inside = jax.tree.map(lambda new, old: jnp.where(passed, new, old), so_far, inside)
        before = combine(inside, before)
    return before


def chain_states(earlier, later):
    return (earlier[0] * later[0], earlier[1] * later[0] + later[1])


def modal_convolve(signal, rate, weight):
    length, width = signal.shape
    count = length // 32
    blocks = signal.reshape(count, 32, width)
    offsets = jnp.arange(32, dtype=jnp.int32)
    lag_values = offsets.astype(jnp.float32)
    lag_decay = jnp.exp(-rate[None] * lag_values[:, None, None])
    filt_lag = jnp.sum(weight[None] * lag_decay, 1)
    distance = offsets[:, None] - offsets[None, :]
    kernel = jnp.where((distance >= 0)[:, :, None], filt_lag[jnp.clip(distance, 0, 31)], 0.0)
    inside = jnp.einsum("tsc,nsc->ntc", kernel, blocks, preferred_element_type=jnp.float32)
    to_end = lag_decay[::-1]
    block_states = jnp.einsum("nsc,smc->nmc", blocks, to_end, preferred_element_type=jnp.float32)
    block_factor = jnp.broadcast_to(jnp.exp(-32.0 * rate)[None], block_states.shape)
    running = lax.associative_scan(chain_states, (block_factor, block_states), axis=0)[1]
    local_in = jnp.concatenate([jnp.zeros_like(running[:1]), running[:-1]], 0)
    block_start = (32 * jnp.arange(count, dtype=jnp.int32)).astype(jnp.float32)
    carried_decay = jnp.exp(-rate[None] * block_start[:, None, None])
    growth = jnp.exp(-rate[None] * (lag_values + 1.0)[:, None, None]) * weight[None]

    def finish(incoming):
        entering = local_in + incoming[None] * carried_decay
        carried = jnp.einsum("nmc,tmc->ntc", entering, growth, preferred_element_type=jnp.float32)
        return (inside + carried).reshape(length, width)

    device_factor = jnp.exp(-float(length) * rate)
    return (finish, device_factor, running[-1])


def body(tokens, w_in, taps, modes_gain, decay, skip):
    rows = tokens.shape[0]
    channels = w_in.shape[2]
    parts = lax.axis_size(CTX)
    length = rows * parts
    whole = gathered_copies(tokens, "ch", 1)
    piece = lax.all_gather(w_in, CTX, axis=0, tiled=True)
    flat = piece.reshape(piece.shape[0], 3 * channels)
    projected = jnp.dot(whole, flat, preferred_element_type=jnp.float32)
    projected = projected.astype(jnp.bfloat16).reshape(rows, 3, channels)
    before = from_behind(projected[rows - 2 :], CTX, 1)
    extended = jnp.concatenate([before, projected], 0).astype(jnp.float32)
    features = taps[0] * extended[2:] + taps[1] * extended[1:-1] + taps[2] * extended[:-2]
    gate_out = features[:, 0]
    product = features[:, 1] * features[:, 2]
    rate = decay / length
    weight = modes_gain * jnp.sqrt(2.0 * rate)
    finish, device_factor, device_state = modal_convolve(product, rate, weight)
    identity = (jnp.ones_like(device_factor), jnp.zeros_like(device_state))
    earlier_states = carried_in((device_factor, device_state), CTX, chain_states, identity)
    conv = finish(earlier_states[1])
    return (gate_out * (conv + skip * product)).astype(jnp.bfloat16)


def solution(mesh):
    split = Mesh(mesh.devices.reshape(4, 4, 2, mesh.shape["ch"]), ("ctx_0", "ctx_1", "ctx_2", "ch"))
    return jax.shard_map(
        body,
        mesh=split,
        in_specs=(
            P(CTX, "ch"),
            P(CTX, None, "ch"),
            P(None, None, "ch"),
            P(None, "ch"),
            P(None, "ch"),
            P("ch"),
        ),
        out_specs=P(CTX, "ch"),
        check_vma=False,
    )
```

profile of v0, /device:TPU:2, one launch (start us, length us, event | category | flops | bytes accessed | tf_op | source)
XLA Modules:
  0.0 228.0 jit_solution(11702988865428538647)
XLA Ops:
  6.5 0.0 all-gather.5.cloned.1.call-start
  6.5 1.9 copy.127
  8.5 0.0 all-gather.5.cloned.1.call-update
  8.5 1.1 copy.126
  9.6 1.5 broadcast_in_dim.20
  11.0 6.6 %all-to-all-start = ((bf16[8,256,512]{1,2,0:T(8,128)(2,1)}), bf16[8,256,512]{1,2,0:T(8,128)(2,1)}, u32[]{:S(2)}, u32[]{:S(2)}) async-start(bf16[8,256,512]{1,2,0:T(8,128)(2,1)} %broadcast_in_dim.20), calls=%async_computation | async-start | bytes 4194304 | tf_op jit(solution)/shard_map/all_to_all | solution.py:18
  17.7 0.0 copy-done.3
  17.7 0.0 copy-done.10
  17.7 0.7 multiply_exponential_fusion.1
  18.3 0.1 copy.132
  18.5 0.1 copy.131
  18.6 0.0 copy-start.1
  18.6 0.1 reshape.96
  18.7 0.6 multiply_convert_fusion
  19.3 0.0 copy-done.5
  19.3 0.0 copy-done.11
  19.3 0.6 slice_bitcast_fusion.3
  19.9 2.0 multiply_exponential_fusion
  22.0 6.0 %multiply_reduce_fusion = bf16[32,512]{0,1:T(8,128)(2,1)S(1)} fusion(f32[16,512]{0,1:T(8,128)S(1)} %copy.131, f32[32]{0:T(128)S(1)} %iota_convert_fusion, f32[16,512]{0,1:T(8,128)S(1)} %copy.132), kind=kLoop, calls=%fused_computation.8 | loop fusion | flops 770048 | bytes 98432 | tf_op jit(solution)/shard_map/reduce_sum | solution.py:80
  27.9 26.4 %all-to-all-done = bf16[8,256,512]{1,2,0:T(8,128)(2,1)} async-done(((bf16[8,256,512]{1,2,0:T(8,128)(2,1)}), bf16[8,256,512]{1,2,0:T(8,128)(2,1)}, u32[]{:S(2)}, u32[]{:S(2)}) %all-to-all-start) | async-done | bytes 2097184 | tf_op jit(solution)/shard_map/all_to_all | solution.py:18
  54.4 72.2 %all-gather.5.cloned.1.call-done = bf16[4096,3,512]{0,2,1:T(8,128)(2,1)} async-done(((bf16[128,3,512]{0,2,1:T(8,128)(2,1)}), bf16[4096,3,512]{0,2,1:T(8,128)(2,1)}) %all-gather.5.cloned.1.call-update) | async-done | bytes 12582928 | tf_op jit(solution)/shard_map/all_gather | solution.py:108
  126.5 8.7 %convolution_convert_fusion = bf16[256,1536]{1,0:T(8,128)(2,1)S(1)} fusion(bf16[256,4096]{0,1:T(8,128)(2,1)} %bitcast.2, bf16[4096,1536]{0,1:T(8,128)(2,1)} %bitcast.118), kind=kOutput, calls=%fused_computation.11 | convolution fusion | flops 3221618688 | bytes 15466496 | tf_op jit(solution)/shard_map/dot_general | solution.py:110
  135.2 0.6 slice.234
  135.8 0.7 slice.184
  136.5 2.3 %collective-permute-start = (bf16[2,3,512]{2,1,0:T(4,128)(2,1)S(1)}, bf16[2,3,512]{2,1,0:T(4,128)(2,1)S(1)}, u32[]{:S(2)}, u32[]{:S(2)}) collective-permute-start(bf16[2,3,512]{2,1,0:T(4,128)(2,1)S(1)} %slice.184), channel_id=1, source_target_pairs={{0,8},{8,16},{16,24},{24,32},{32,40},{40,48},{48,56},{56,64},{64,7... | collective-permute-start | bytes 18440 | tf_op jit(solution)/shard_map/ppermute | solution.py:28
  138.9 0.5 broadcast_add_fusion
  139.4 3.6 %rev.3 = bf16[32,16,512]{0,1,2:T(8,128)(2,1)} reverse(bf16[32,16,512]{0,1,2:T(8,128)(2,1)S(1)} %multiply_exponential_fusion), dimensions={0} | reverse | bytes 1048576 | tf_op jit(solution)/shard_map/rev | solution.py:84
  143.0 0.1 copy.133
  143.1 4.0 %gather_fusion = bf16[1024,512]{1,0:T(8,128)(2,1)S(1)} fusion(bf16[32,512]{1,0:T(8,128)(2,1)S(1)} %copy.133, s32[1024]{0:T(1024)S(1)} %broadcast_clamp_fusion), kind=kCustom, calls=%fused_computation | custom fusion | bytes 2101248 | tf_op jit(solution)/shard_map/gather | solution.py:82
  147.1 6.4 %copy.134 = bf16[32,32,512]{1,0,2:T(8,128)(2,1)} copy(bf16[32,32,512]{2,1,0:T(8,128)(2,1)S(1)} %bitcast.106) | data formatting | bytes 2097152 | tf_op jit(solution)/shard_map/gather | solution.py:82
  153.5 0.3 copy.128
  153.8 0.0 collective-permute-done
  153.8 0.3 copy.129
  154.1 0.5 maximum_convert_fusion
  154.6 0.0 copy-done.8
  154.6 0.0 copy-done.9
  154.6 1.6 fusion.13
  156.3 0.1 slice_multiply_fusion.3
  156.3 0.1 copy.130
  156.5 0.8 copy.135
  157.3 4.2 %fusion.34 = f32[512,16,8]{1,2,0:T(8,128)} fusion(bf16[32,16,512]{0,1,2:T(8,128)(2,1)} %rev.3, bf16[8,32,512]{1,0,2:T(8,128)(2,1)S(1)} %copy.135), kind=kOutput, calls=%fused_computation.93 | convolution fusion | flops 4194304 | bytes 1048576 | tf_op jit(solution)/shard_map/nsc,smc->nmc/dot_general | solution.py:85
  161.4 2.2 copy.137
  163.9 1.4 fusion.18
  165.3 0.6 slice.241
  166.0 2.0 pad.25
  167.9 0.8 pad_maximum_fusion.2
  168.7 4.9 %all-gather = f32[64,512]{1,0:T(8,128)S(1)} all-gather(f32[32,512]{1,0:T(8,128)S(1)} %pad_maximum_fusion.2), channel_id=2, replica_groups=mesh['ctx_0'=4,'ctx_1'=4,'ctx_2'=2,'ch'=8] {'ctx_2'}, dimensions={0}, use_global_device_ids=true | all-gather | bytes 196608 | tf_op jit(solution)/shard_map/all_gather | solution.py:45
  173.6 14.4 %all-gather.1 = f32[128,512]{1,0:T(8,128)S(1)} all-gather(f32[32,512]{1,0:T(8,128)S(1)} %pad_maximum_fusion.3), channel_id=3, replica_groups=mesh['ctx_0'=4,'ctx_1'=4,'ctx_2'=2,'ch'=8] {'ctx_1'}, dimensions={0}, use_global_device_ids=true | all-gather | bytes 327680 | tf_op jit(solution)/shard_map/all_gather | solution.py:45
  188.0 12.5 %all-gather.2 = f32[128,512]{1,0:T(8,128)S(1)} all-gather(f32[32,512]{1,0:T(8,128)S(1)} %pad_maximum_fusion.4), channel_id=4, replica_groups=mesh['ctx_0'=4,'ctx_1'=4,'ctx_2'=2,'ch'=8] {'ctx_0'}, dimensions={0}, use_global_device_ids=true | all-gather | bytes 327680 | tf_op jit(solution)/shard_map/all_gather | solution.py:45
  200.5 1.6 pad_maximum_fusion
  202.1 3.5 %pad.24 = f32[8,16,512]{2,1,0:T(8,128)} pad(f32[4,16,512]{2,1,0:T(8,128)} %pad_maximum_fusion, f32[]{:T(128)} %constant.19.clone.1), padding=0_1_1x0_0_0x0_0_0 | pad | bytes 393220 | tf_op jit(solution)/shard_map/pad | solution.py:87
  205.5 1.1 slice_add_fusion
  206.6 0.1 fusion.25
  206.7 0.0 copy-done.13
  206.7 0.9 multiply_add_fusion
  207.6 1.7 copy.138
  209.3 4.6 %fusion = f32[512,8,32]{2,1,0:T(8,128)S(1)} fusion(bf16[8,32,512]{1,0,2:T(8,128)(2,1)S(1)} %copy.135, bf16[32,32,512]{1,0,2:T(8,128)(2,1)} %copy.134, pred[32,32]{1,0:T(8,128)(4,1)S(1)} %subtract_compare_fusion), kind=kOutput, calls=%fused_computation.1 | convolution fusion | flops 8912896 | bytes 1836032 | tf_op jit(solution)/shard_map/tsc,nsc->ntc/dot_general | solution.py:83
  213.9 0.0 copy-done
  213.9 0.0 copy-done.14
  213.9 3.8 %bitcast_add_fusion = f32[8,32,512]{1,0,2:T(8,128)} fusion(f32[512,8,32]{2,1,0:T(8,128)S(1)} %fusion, bf16[8,16,512]{1,0,2:T(8,128)(2,1)S(1)} %copy-done, f32[32]{0:T(128)S(1)} %copy-done.14, f32[16,512]{0,1:T(8,128)S(1)} %copy.132, f32[16,512]{0,1:T(8,128)S(1)} %copy-done.2), kind=kOutput, calls=%fused_computation.12 | convolution fusion | flops 4849664 | bytes 1245312 | tf_op jit(solution)/shard_map/nmc,tmc->ntc/dot_general | solution.py:95
  217.7 2.2 copy.139
  219.9 0.2 copy.140
  220.1 0.1 fusion.16
  220.3 0.8 copy.141
  (39 shorter events, 0.3 us)
Async XLA Ops:
  6.5 120.0 %all-gather.5.cloned.1.call-start = ((), (), s32[]{:S(2)}) async-start(), calls=%async_computation.1 | async-start | bytes 12976128 | tf_op jit(solution)/shard_map/all_gather | solution.py:108
  11.0 6.6 %copy-start.3 = (f32[16,512]{1,0:T(8,128)S(1)}, f32[16,512]{1,0:T(8,128)}, u32[]{:S(2)}) copy-start(f32[16,512]{1,0:T(8,128)} %param.10) | copy-start | bytes 98308
  11.0 6.6 %copy-start.10 = (f32[16,512]{1,0:T(8,128)S(1)}, f32[16,512]{1,0:T(8,128)}, u32[]{:S(2)}) copy-start(f32[16,512]{1,0:T(8,128)} %param.9) | copy-start | bytes 98308
  11.0 8.3 %copy-start.11 = (f32[3,3,512]{2,1,0:T(4,128)S(1)}, f32[3,3,512]{2,1,0:T(4,128)}, u32[]{:S(2)}) copy-start(f32[3,3,512]{2,1,0:T(4,128)} %param.8) | copy-start | bytes 55300
  11.0 43.3 %all-to-all-start = ((bf16[8,256,512]{1,2,0:T(8,128)(2,1)}), bf16[8,256,512]{1,2,0:T(8,128)(2,1)}, u32[]{:S(2)}, u32[]{:S(2)}) async-start(bf16[8,256,512]{1,2,0:T(8,128)(2,1)} %broadcast_in_dim.20), calls=%async_computation | async-start | bytes 4194304 | tf_op jit(solution)/shard_map/all_to_all | solution.py:18
  18.3 1.0 copy-start.5
  18.6 116.6 %copy-start.1 = (f32[16,512]{0,1:T(8,128)}, f32[16,512]{0,1:T(8,128)S(1)}, u32[]{:S(2)}) copy-start(f32[16,512]{0,1:T(8,128)S(1)} %copy.131) | copy-start | bytes 98308
  136.5 17.3 %collective-permute-start = (bf16[2,3,512]{2,1,0:T(4,128)(2,1)S(1)}, bf16[2,3,512]{2,1,0:T(4,128)(2,1)S(1)}, u32[]{:S(2)}, u32[]{:S(2)}) collective-permute-start(bf16[2,3,512]{2,1,0:T(4,128)(2,1)S(1)} %slice.184), channel_id=1, source_target_pairs={{0,8},{8,16},{16,24},{24,32},{32,40},{40,48},{48,56},{56,64},{64,7... | collective-permute-start | bytes 18440 | tf_op jit(solution)/shard_map/ppermute | solution.py:28
  153.8 0.8 copy-start.8
  153.8 0.8 copy-start.9
  161.4 2.2 copy-start.6
  161.4 2.2 copy-start.7
  161.4 2.2 copy-start.4
  165.9 40.8 %copy-start.13 = (f32[8]{0:T(128)S(1)}, f32[8]{0:T(128)}, u32[]{:S(2)}) copy-start(f32[8]{0:T(128)} %multiply_convert_fusion) | copy-start | bytes 100
  209.3 4.6 %copy-start = (bf16[8,16,512]{1,0,2:T(8,128)(2,1)S(1)}, bf16[8,16,512]{1,0,2:T(8,128)(2,1)}, u32[]{:S(2)}) copy-start(bf16[8,16,512]{1,0,2:T(8,128)(2,1)} %copy.138) | copy-start | bytes 393220
  209.3 4.6 %copy-start.2 = (f32[16,512]{0,1:T(8,128)S(1)}, f32[16,512]{0,1:T(8,128)}, u32[]{:S(2)}) copy-start(f32[16,512]{0,1:T(8,128)} %copy-done.1) | copy-start | bytes 98308
  209.3 4.6 %copy-start.14 = (f32[32]{0:T(128)S(1)}, f32[32]{0:T(128)}, u32[]{:S(2)}) copy-start(f32[32]{0:T(128)} %broadcast_add_fusion) | copy-start | bytes 388
  217.7 2.4 %copy-start.12 = (f32[512]{0:T(512)S(1)}, f32[512]{0:T(512)}, u32[]{:S(2)}) copy-start(f32[512]{0:T(512)} %param.11) | copy-start | bytes 6148
Sparse Core Ops, SparseCore 0:
  9.8 116.6 all-gather.4
where the time goes:
time: 229 us; the launch traced here: 228 us
  waiting for transfers between devices  98.6 us (43%)
  local copies, waits for them, and re-layouts  35.6 us (16%)
  blocking collectives  31.8 us (14%)
  matrix products  21.2 us (9%)
  other arithmetic  18 us (8%)
  between operations  13.8 us (6%)
  starting transfers between devices  8.97 us (4%)
    all_gather x1, waiting for transfers between devices, body(): piece = lax.all_gather(w_in, CTX, axis=0, tiled=True)  72.2 us
    all_gather x3, blocking collectives, gathered_once(): both, at, found = (lax.all_gather(jnp.concatenate(lines), axis), 0, {})  31.8 us
    all_to_all x1, waiting for transfers between devices, sent_to_all(): return lax.all_to_all(copies, axis, split_axis=0, concat_axis=0, tiled=True)  26.4 us
    gather x2, local copies, waits for them, and re-layouts, modal_convolve(): filt_lag[jnp.clip(distance, 0, 31)]  10.4 us
    dot_general x1, matrix products, body(): projected = jnp.dot(whole, flat, preferred_element_type=jnp.float32)  8.68 us
    all_to_all x1, starting transfers between devices, sent_to_all(): return lax.all_to_all(copies, axis, split_axis=0, concat_axis=0, tiled=True)  6.64 us
    reduce_sum x1, other arithmetic, modal_convolve(): filt_lag = jnp.sum(weight[None] * lag_decay, 1)  5.99 us
    pad x4, local copies, waits for them, and re-layouts, modal_convolve(): lax.associative_scan(chain_states, (block_factor, block_states), axis=0)[1]  5.47 us
  transfers between devices with their start and end apart: 3, of which 2 were waited for; matrix products, arithmetic and copies ran while one was open for 12% of the time, Pallas kernels for 0%

commit v1 on v0

v1 whole, which is shorter than its diff:
```python
import functools

import jax
import jax.numpy as jnp
from jax import lax
from jax.experimental import pallas as pl
from jax.experimental.pallas import tpu as pltpu
from jax.sharding import Mesh
from jax.sharding import PartitionSpec as P

AXES = ("y", "h", "c", "l", "x")
CTX = ("y", "h", "c")
CH = ("l", "x")
F32 = jnp.float32
BF16 = jnp.bfloat16
HALO = 16
SUB = 8


def shifted(array, axis, step):
    n = lax.axis_size(axis)
    return lax.ppermute(array, axis, [(i, (i + step) % n) for i in range(n)])


def ring(piece, axis):
    half = piece.shape[0] // 2
    behind = shifted(piece, axis, 1)
    ahead = shifted(piece, axis, -1)
    first = shifted(behind[:half], axis, 1)
    second = shifted(ahead[half:], axis, -1)
    return behind, ahead, first, second


def project_kernel(sizes, *refs):
    rows, depth, width, modes, seq = sizes
    pos, tok, *pieces = refs[:22]
    taps, decay = refs[22:24]
    gate, product, inside, state = refs[24:28]
    tokv, wv, acc, tok_sem, w_sem = refs[28:]
    y, h, c = pos[1], pos[2], pos[3]
    k = depth // 16
    half = k // 2
    top = rows + HALO

    copies = []
    for ch in range(8):
        lanes = pl.ds(ch * (depth // 8), depth // 8)
        for core in range(2):
            skip = HALO * core
            at = (core * 8 + ch) * top
            copies.append(
                pltpu.make_async_copy(
                    tok.at[pl.ds(at + skip, top - skip), :],
                    tokv.at[pl.ds(core * top, top - skip), lanes],
                    tok_sem.at[core * 8 + ch],
                )
            )
    groups = [[], [], [], []]
    for kind, dh in enumerate((0, 1, -1, 2)):
        hs = lax.rem(h - dh + 4, 4)
        for number, (dy, skip, n, group) in enumerate(
            ((0, 0, k, 0), (1, 0, k, 1), (-1, 0, k, 2), (2, 0, half, 3), (2, half, half, 3))
        ):
            ys = lax.rem(y - dy + 4, 4)
            at = pl.multiple_of((ys * 4 + hs) * k + skip, half)
            copy = pltpu.make_async_copy(
                pieces[kind * 5 + number], wv.at[pl.ds(at, n), :], w_sem.at[kind * 5 + number]
            )
            groups[group].append(copy)
    for copy in groups[0] + copies + groups[1] + groups[2] + groups[3]:
        copy.start()
    for copy in copies:
        copy.wait()
    for group, dy in enumerate((0, 1, -1, 2)):
        for copy in groups[group]:
            copy.wait()
        at = pl.multiple_of(lax.rem(y - dy + 4, 4) * (4 * k), 4 * k)

        @pl.loop(0, 3)
        def _(j):
            cols = pl.ds(pl.multiple_of(j * width, width), width)
            part = jnp.dot(
                tokv[:, pl.ds(at, 4 * k)], wv[pl.ds(at, 4 * k), cols], preferred_element_type=F32
            )
            for lh in range(width // 128):
                at_lane = j * (width // 128) + lh
                new = part[:, lh * 128 : lh * 128 + 128]
                if group == 0:
                    acc[at_lane] = new
                elif group < 3:
                    acc[at_lane] += new
                else:
                    acc[at_lane] = (acc[at_lane] + new).astype(BF16).astype(F32)

    steps = 2 * rows // SUB
    for lh in range(width // 128):
        mine = pl.ds(pl.multiple_of(c * width + lh * 128, 128), 128)
        lanes = pl.ds(lh * 128, 128)
        weights = [[taps[lag, j : j + 1, mine] for j in range(3)] for lag in range(3)]
        rates = [jnp.broadcast_to(decay[m : m + 1, mine] / seq, (SUB, 128)) for m in range(modes)]
        factors = [jnp.exp(-rate) for rate in rates]

        def read(start):
            return [
                acc[j * (width // 128) + lh, pl.ds(start, SUB, stride=steps), :]
                for j in range(3)
            ]

        def step(t, carry):
            before, last, states = carry
            now = read(HALO + t)
            f = [
                weights[0][j] * now[j] + weights[1][j] * last[j] + weights[2][j] * before[j]
                for j in range(3)
            ]
            p = f[1] * f[2]
            gate[t, :, lanes] = f[0]
            product[t, :, lanes] = p
            return last, now, [a * s + p for a, s in zip(factors, states)]

        zero = jnp.zeros((SUB, 128), F32)
        carry = (read(HALO - 2), read(HALO - 1), [zero] * modes)
        states = lax.fori_loop(0, steps, step, carry, unroll=4)[2]
        line = lax.broadcasted_iota(jnp.int32, (SUB, 128), 0)

        def later(value, by):
            return jnp.where(line >= by, pltpu.roll(value, by, 0), 0.0)

        for m in range(modes):
            s = states[m]
            for by in (1, 2, 4):
                s = s + jnp.exp(-float(steps * by) * rates[m]) * later(s, by)
            inside[m, :, lanes] = later(s, 1)
            state[m : m + 1, lanes] = s[SUB - 1 :]


def local_kernel(sizes, pos, product, gain, decay, skip, local):
    rows, depth, width, modes, seq = sizes
    c = pos[3]
    steps = 2 * rows // SUB
    for lh in range(width // 128):
        mine = pl.ds(pl.multiple_of(c * width + lh * 128, 128), 128)
        lanes = pl.ds(lh * 128, 128)
        rates = [jnp.broadcast_to(decay[m : m + 1, mine] / seq, (SUB, 128)) for m in range(modes)]
        factors = [jnp.exp(-rate) for rate in rates]
        heights = [gain[m : m + 1, mine] * jnp.sqrt(2.0 * rates[m]) for m in range(modes)]
        direct = jnp.broadcast_to(skip[:, mine], (SUB, 128))

        def step(t, states):
            p = product[t, :, lanes]
            states = [a * s + p for a, s in zip(factors, states)]
            parts = [w * s for w, s in zip(heights, states)]
            while len(parts) > 1:
                parts = [a + b for a, b in zip(parts[::2], parts[1::2])]
            local[t, :, lanes] = parts[0] + direct * p
            return states

        lax.fori_loop(0, steps, step, [jnp.zeros((SUB, 128), F32)] * modes, unroll=4)


def finish_kernel(sizes, pos, gate, local, inside, states, gain, decay, out, start, whole):
    rows, depth, width, modes, seq = sizes
    rank, c = pos[0], pos[3]
    steps = 2 * rows // SUB
    length = 2 * rows
    for lh in range(width // 128):
        mine = pl.ds(pl.multiple_of(c * width + lh * 128, 128), 128)
        lanes = pl.ds(lh * 128, 128)
        over = jnp.exp(-float(length) * (decay[:, mine] / seq))
        entering = jnp.zeros((modes, 128), F32)
        for r in range(16):
            entering = jnp.where(r < rank, over * entering + states[r, :, lanes], entering)
        start[:, lanes] = entering
        line = lax.broadcasted_iota(jnp.int32, (SUB, 128), 0).astype(F32) * float(steps)
        factors, waves = [], []
        for m in range(modes):
            rate = jnp.broadcast_to(decay[m : m + 1, mine] / seq, (SUB, 128))
            factors.append(jnp.exp(-rate))
            height = gain[m : m + 1, mine] * jnp.sqrt(2.0 * rate)
            waves.append(height * (inside[m, :, lanes] + jnp.exp(-rate * line) * start[m : m + 1, lanes]))

        def step(t, waves):
            waves = [a * z for a, z in zip(factors, waves)]
            parts = waves
            while len(parts) > 1:
                parts = [a + b for a, b in zip(parts[::2], parts[1::2])]
            whole[lh, pl.ds(t, SUB, stride=steps), :] = gate[t, :, lanes] * (local[t, :, lanes] + parts[0])
            return waves

        lax.fori_loop(0, steps, step, waves, unroll=4)
        for part in range(2):
            out[part, :, lanes] = whole[lh, part * rows : part * rows + rows, :].astype(BF16)


def body(tokens, w_in, taps, modes_gain, decay, skip):
    rows = tokens.shape[0]
    group = w_in.shape[2]
    width = group // 2
    k = w_in.shape[0]
    modes = decay.shape[0]
    depth = tokens.shape[1] * 8
    seq = rows * 32
    sizes = (rows, depth, width, modes, seq)
    y, h, c = (lax.axis_index(a) for a in CTX)
    pos = jnp.stack([y * 4 + h, y, h, c]).astype(jnp.int32)

    with jax.named_scope("token_gather"):
        tail = lax.ppermute(tokens[rows - HALO :], CTX, [(i, i + 1) for i in range(1, 31, 2)])
        tok = lax.all_gather(jnp.concatenate([tail, tokens], 0), ("c", *CH), axis=0, tiled=True)

    with jax.named_scope("weight_gather"):
        halves = w_in.reshape(k, 3, 2, width).transpose(2, 0, 1, 3).reshape(2, k, 3 * width)
        own = lax.all_to_all(halves, "c", 0, 0, tiled=True).reshape(2 * k, 3 * width)
        behind, ahead, first, second = ring(own, "h")
        opposite = jnp.concatenate([first, second], 0)
        pieces = []
        for piece in (own, behind, ahead, opposite):
            pieces += [piece, *ring(piece, "y")]

    vmem = pl.BlockSpec(memory_space=pltpu.VMEM)
    smem = pl.BlockSpec(memory_space=pltpu.SMEM)
    anywhere = pl.BlockSpec(memory_space=pl.ANY)
    block = (2 * rows // SUB, SUB, width)
    full = jax.ShapeDtypeStruct(block, F32)
    params = pltpu.CompilerParams(vmem_limit_bytes=40 * 2**20)
    gate, product, inside, state = pl.pallas_call(
        functools.partial(project_kernel, sizes),
        out_shape=(
            full,
            full,
            jax.ShapeDtypeStruct((modes, SUB, width), F32),
            jax.ShapeDtypeStruct((modes, width), F32),
        ),
        in_specs=[smem] + [anywhere] * 21 + [vmem] * 2,
        out_specs=(vmem,) * 4,
        scratch_shapes=[
            pltpu.VMEM((2 * rows + HALO, depth), BF16),
            pltpu.VMEM((depth, 3 * width), BF16),
            pltpu.VMEM((3 * width // 128, 2 * rows + HALO, 128), F32),
            pltpu.SemaphoreType.DMA((16,)),
            pltpu.SemaphoreType.DMA((20,)),
        ],
        compiler_params=params,
        name="project",
    )(pos, tok, *pieces, taps, decay)

    with jax.named_scope("state_exchange"):
        states = lax.all_to_all(
            jnp.broadcast_to(state, (16, *state.shape)), ("y", "h"), 0, 0, tiled=True
        )
    local = pl.pallas_call(
        functools.partial(local_kernel, sizes),
        out_shape=full,
        in_specs=[smem] + [vmem] * 4,
        out_specs=vmem,
        compiler_params=params,
        cost_estimate=pl.CostEstimate(flops=20_000_000, bytes_accessed=1_000_000, transcendentals=0),
        name="local",
    )(pos, product, modes_gain, decay, skip.reshape(1, group))
    out = pl.pallas_call(
        functools.partial(finish_kernel, sizes),
        out_shape=jax.ShapeDtypeStruct((2, rows, width), BF16),
        in_specs=[smem] + [vmem] * 6,
        out_specs=vmem,
        scratch_shapes=[pltpu.VMEM((modes, width), F32), pltpu.VMEM((width // 128, 2 * rows, 128), F32)],
        compiler_params=params,
        name="finish",
    )(pos, gate, local, inside, states, modes_gain, decay)
    with jax.named_scope("result_swap"):
        both = lax.all_to_all(out, "c", 0, 0, tiled=True)
        return both.transpose(1, 0, 2).reshape(rows, group)


def solution(mesh):
    split = Mesh(mesh.devices.reshape(4, 4, 2, 2, 4), AXES)
    return jax.shard_map(
        body,
        mesh=split,
        in_specs=(
            P(CTX, CH),
            P(CTX, None, CH),
            P(None, None, CH),
            P(None, CH),
            P(None, CH),
            P(CH),
        ),
        out_specs=P(CTX, CH),
        check_vma=False,
    )
```

time: 229 us -> 172 us (0.75)
  the two profiles are of different devices: /device:TPU:2 before, /device:TPU:1 now
where the time goes in v1:
time: 172 us; the launch traced here: 168 us
  waiting for transfers between devices  56 us (33%)
  starting transfers between devices  40.4 us (23%)
  local copies, waits for them, and re-layouts  28.8 us (17%)
  Pallas kernels  15.7 us (9%)
  between operations  13.6 us (8%)
  blocking collectives  12.2 us (7%)
  other arithmetic  1.75 us (1%)
    ppermute x20, waiting for transfers between devices, shifted(): return lax.ppermute(array, axis, [(i, (i + step) % n) for i in range(n)])  49.1 us
    ppermute x20, starting transfers between devices, shifted(): return lax.ppermute(array, axis, [(i, (i + step) % n) for i in range(n)])  27.8 us
    unnamed x54, local copies, waits for them, and re-layouts  22.6 us
    pallas_call x1, Pallas kernels, body(): pl.pallas_call(functools.partial(project_kernel, sizes), out_shape=(full,...  12.3 us
    all_to_all x1, blocking collectives, body(): both = lax.all_to_all(out, 'c', 0, 0, tiled=True)  8.53 us
    ppermute x1, starting transfers between devices, body(): lax.ppermute(tokens[rows - HALO:], CTX, [(i, i + 1) for i in range(1, 31,...  6.27 us
    all_to_all x1, starting transfers between devices, body(): lax.all_to_all(jnp.broadcast_to(state, (16, *state.shape)), ('y', 'h'), 0...  6.26 us
    all_to_all x1, waiting for transfers between devices, body(): lax.all_to_all(jnp.broadcast_to(state, (16, *state.shape)), ('y', 'h'), 0...  6.09 us
  transfers between devices with their start and end apart: 23, of which 11 were waited for; matrix products, arithmetic and copies ran while one was open for 3% of the time, Pallas kernels for 1%

profile of v1, /device:TPU:1, one launch (start us, length us, event | category | flops | bytes accessed | tf_op | source)
XLA Modules:
  0.0 168.4 jit_solution(5316174724201846439)
XLA Ops:
  6.5 0.7 slice.33
  7.3 6.3 %collective-permute-start = (bf16[16,512]{1,0:T(8,128)(2,1)S(1)}, bf16[16,512]{1,0:T(8,128)(2,1)S(1)}, u32[]{:S(2)}, u32[]{:S(2)}) collective-permute-start(bf16[16,512]{1,0:T(8,128)(2,1)S(1)} %slice.33), channel_id=1, source_target_pairs={{8,16},{24,32},{40,48},{56,64},{72,80},{88,96},{104,112},{120,128}... | collective-permute-start | bytes 49160 | tf_op jit(solution)/shard_map/token_gather/ppermute | solution.py:208
  13.5 0.9 collective-permute-done
  14.4 1.7 pad_maximum_fusion
  16.1 1.2 copy.11
  17.3 3.7 %all_to_all.15 = bf16[2,128,768]{1,2,0:T(8,128)(2,1)S(1)} all-to-all(bf16[2,128,768]{1,2,0:T(8,128)(2,1)S(1)} %bitcast.18), channel_id=1, replica_groups=mesh['y'=4,'h'=4,'c'=2,'l'=2,'x'=4] {'c'}, dimensions={0} | all-to-all | bytes 786432 | tf_op jit(solution)/shard_map/weight_gather/all_to_all | solution.py:213
  21.2 6.4 %collective-permute-start.10 = (bf16[256,768]{1,0:T(8,128)(2,1)S(1)}, bf16[256,768]{1,0:T(8,128)(2,1)S(1)}, u32[]{:S(2)}, u32[]{:S(2)}) collective-permute-start(bf16[256,768]{1,0:T(8,128)(2,1)S(1)} %bitcast.12), channel_id=1, source_target_pairs={{0,48},{16,0},{32,16},{48,32},{1,49},{17,1},{33,17},{49,33},{2,50}... | collective-permute-start | bytes 1179656 | tf_op jit(solution)/shard_map/weight_gather/ppermute | solution.py:22
  27.6 2.7 %collective-permute-start.2 = (bf16[256,768]{1,0:T(8,128)(2,1)S(1)}, bf16[256,768]{1,0:T(8,128)(2,1)S(1)}, u32[]{:S(2)}, u32[]{:S(2)}) collective-permute-start(bf16[256,768]{1,0:T(8,128)(2,1)S(1)} %bitcast.14), channel_id=1, source_target_pairs={{0,192},{64,0},{128,64},{192,128},{1,193},{65,1},{129,65},{193,129... | collective-permute-start | bytes 1179656 | tf_op jit(solution)/shard_map/weight_gather/ppermute | solution.py:22
  30.4 12.4 %collective-permute-done.10.refs_12_ = bf16[256,768]{1,0:T(8,128)(2,1)S(1)} collective-permute-done((bf16[256,768]{1,0:T(8,128)(2,1)S(1)}, bf16[256,768]{1,0:T(8,128)(2,1)S(1)}, u32[]{:S(2)}, u32[]{:S(2)}) %collective-permute-start.10) | collective-permute-done | bytes 393248 | tf_op jit(solution)/shard_map/weight_gather/ppermute | solution.py:22
  42.8 2.2 %collective-permute-start.16 = (bf16[128,768]{1,0:T(8,128)(2,1)S(1)}, bf16[128,768]{1,0:T(8,128)(2,1)S(1)}, u32[]{:S(2)}, u32[]{:S(2)}) collective-permute-start(bf16[128,768]{1,0:T(8,128)(2,1)S(1)} %slice.51), channel_id=1, source_target_pairs={{0,48},{16,0},{32,16},{48,32},{1,49},{17,1},{33,17},{49,33},{2,50}... | collective-permute-start | bytes 589832 | tf_op jit(solution)/shard_map/weight_gather/ppermute | solution.py:22
  45.0 8.3 %collective-permute-done.5.refs_7_ = bf16[256,768]{1,0:T(8,128)(2,1)S(1)} collective-permute-done((bf16[256,768]{1,0:T(8,128)(2,1)S(1)}, bf16[256,768]{1,0:T(8,128)(2,1)S(1)}, u32[]{:S(2)}, u32[]{:S(2)}) %collective-permute-start.5) | collective-permute-done | bytes 393248 | tf_op jit(solution)/shard_map/weight_gather/ppermute | solution.py:22
  53.5 1.5 collective-permute-start.1
  54.9 1.7 %collective-permute-start.12 = (bf16[256,768]{1,0:T(8,128)(2,1)S(1)}, bf16[256,768]{1,0:T(8,128)(2,1)S(1)}, u32[]{:S(2)}, u32[]{:S(2)}) collective-permute-start(bf16[256,768]{1,0:T(8,128)(2,1)S(1)} %collective-permute-done.10.refs_12_), channel_id=1, source_target_pairs={{0,192},{64,0},{128,64},{192,128},{1,193},{65,1},{129,65},{193,129... | collective-permute-start | bytes 1179656 | tf_op jit(solution)/shard_map/weight_gather/ppermute | solution.py:22
  56.7 2.7 %collective-permute-start.7 = (bf16[256,768]{1,0:T(8,128)(2,1)S(1)}, bf16[256,768]{1,0:T(8,128)(2,1)S(1)}, u32[]{:S(2)}, u32[]{:S(2)}) collective-permute-start(bf16[256,768]{1,0:T(8,128)(2,1)S(1)} %collective-permute-done.5.refs_7_), channel_id=1, source_target_pairs={{0,192},{64,0},{128,64},{192,128},{1,193},{65,1},{129,65},{193,129... | collective-permute-start | bytes 1179656 | tf_op jit(solution)/shard_map/weight_gather/ppermute | solution.py:22
  59.3 10.2 %collective-permute-done.15 = bf16[128,768]{1,0:T(8,128)(2,1)S(1)} collective-permute-done((bf16[128,768]{1,0:T(8,128)(2,1)S(1)}, bf16[128,768]{1,0:T(8,128)(2,1)S(1)}, u32[]{:S(2)}, u32[]{:S(2)}) %collective-permute-start.15) | collective-permute-done | bytes 196640 | tf_op jit(solution)/shard_map/weight_gather/ppermute | solution.py:22
  69.5 0.9 collective-permute-start.6
  70.5 2.1 %collective-permute-start.18 = (bf16[256,768]{1,0:T(8,128)(2,1)S(1)}, bf16[256,768]{1,0:T(8,128)(2,1)S(1)}, u32[]{:S(2)}, u32[]{:S(2)}) collective-permute-start(bf16[256,768]{1,0:T(8,128)(2,1)S(1)} %constant_dynamic-update-slice_fusion.refs_17_), channel_id=1, source_target_pairs={{0,192},{64,0},{128,64},{192,128},{1,193},{65,1},{129,65},{193,129... | collective-permute-start | bytes 1179656 | tf_op jit(solution)/shard_map/weight_gather/ppermute | solution.py:22
  72.8 2.8 %collective-permute-start.4 = (bf16[128,768]{1,0:T(8,128)(2,1)S(1)}, bf16[128,768]{1,0:T(8,128)(2,1)S(1)}, u32[]{:S(2)}, u32[]{:S(2)}) collective-permute-start(bf16[128,768]{1,0:T(8,128)(2,1)S(1)} %slice.45), channel_id=1, source_target_pairs={{0,192},{64,0},{128,64},{192,128},{1,193},{65,1},{129,65},{193,129... | collective-permute-start | bytes 589832 | tf_op jit(solution)/shard_map/weight_gather/ppermute | solution.py:22
  75.5 5.3 %collective-permute-done.6.refs_8_ = bf16[256,768]{1,0:T(8,128)(2,1)S(1)} collective-permute-done((bf16[256,768]{1,0:T(8,128)(2,1)S(1)}, bf16[256,768]{1,0:T(8,128)(2,1)S(1)}, u32[]{:S(2)}, u32[]{:S(2)}) %collective-permute-start.6) | collective-permute-done | bytes 393248 | tf_op jit(solution)/shard_map/weight_gather/ppermute | solution.py:22
  80.8 1.2 collective-permute-start.14
  82.0 0.7 slice.48
  82.7 0.7 slice.47
  83.4 0.7 slice.46
  84.4 0.7 slice.53
  85.1 0.8 copy-done.1
  85.8 3.4 %collective-permute-done.17.refs_18_ = bf16[256,768]{1,0:T(8,128)(2,1)S(1)} collective-permute-done((bf16[256,768]{1,0:T(8,128)(2,1)S(1)}, bf16[256,768]{1,0:T(8,128)(2,1)S(1)}, u32[]{:S(2)}, u32[]{:S(2)}) %collective-permute-start.17) | collective-permute-done | bytes 393248 | tf_op jit(solution)/shard_map/weight_gather/ppermute | solution.py:22
  89.2 1.2 collective-permute-start.9
  90.4 0.7 slice.52
  91.1 0.7 copy-done.3
  91.9 0.7 copy-done.14
  92.8 0.6 collective-permute-done.3.refs_5_
  93.5 0.7 copy-done.16
  94.1 1.8 %collective-permute-start.20 = (bf16[128,768]{1,0:T(8,128)(2,1)}, bf16[128,768]{1,0:T(8,128)(2,1)}, u32[]{:S(2)}, u32[]{:S(2)}) collective-permute-start(bf16[128,768]{1,0:T(8,128)(2,1)} %slice.53), channel_id=1, source_target_pairs={{0,192},{64,0},{128,64},{192,128},{1,193},{65,1},{129,65},{193,129... | collective-permute-start | bytes 589832 | tf_op jit(solution)/shard_map/weight_gather/ppermute | solution.py:22
  95.9 0.7 copy-done.18
  96.7 1.0 collective-permute-done.13.refs_15_
  97.7 4.3 %collective-permute-done.8.refs_10_ = bf16[128,768]{1,0:T(8,128)(2,1)} collective-permute-done((bf16[128,768]{1,0:T(8,128)(2,1)}, bf16[128,768]{1,0:T(8,128)(2,1)}, u32[]{:S(2)}, u32[]{:S(2)}) %collective-permute-start.8) | collective-permute-done | bytes 196640 | tf_op jit(solution)/shard_map/weight_gather/ppermute | solution.py:22
  102.0 3.4 %collective-permute-done.19.refs_20_ = bf16[128,768]{1,0:T(8,128)(2,1)} collective-permute-done((bf16[128,768]{1,0:T(8,128)(2,1)}, bf16[128,768]{1,0:T(8,128)(2,1)}, u32[]{:S(2)}, u32[]{:S(2)}) %collective-permute-start.19) | collective-permute-done | bytes 196640 | tf_op jit(solution)/shard_map/weight_gather/ppermute | solution.py:22
  105.4 2.3 %copy-done = bf16[4352,512]{1,0:T(8,128)(2,1)S(1)} copy-done((bf16[4352,512]{1,0:T(8,128)(2,1)S(1)}, bf16[4352,512]{1,0:T(8,128)(2,1)}, u32[]{:S(2)}) %copy-start) | copy-done | bytes 4456472
  107.7 1.0 copy-done.2
  108.7 1.0 copy-done.4
  109.7 1.0 copy-done.6
  110.7 0.8 copy-done.11
  111.5 0.9 copy-done.15
  112.4 0.9 copy-done.17
  113.3 0.9 copy-done.19
  114.2 0.7 copy-done.24
  115.0 12.3 %project.1 = (f32[64,8,256]{2,1,0:T(8,128)S(1)}, f32[64,8,256]{2,1,0:T(8,128)S(1)}, f32[16,8,256]{2,1,0:T(8,128)S(1)}, f32[16,256]{1,0:T(8,128)S(1)}) custom-call(s32[4]{0:T(128)S(1)} %pad_add_fusion.refs_0_.pos, bf16[4352,512]{1,0:T(8,128)(2,1)S(1)} %copy-done, bf16[256,768]{1,0:T(8,128)(2,1)S(1)} %bitcast.16, ...), custom_call_target="tpu_custom_call" | custom-call | tf_op jit(solution)/shard_map/project/pallas_call | solution.py:226
  127.3 0.8 copy-done.7
  128.1 0.8 copy-done.9
  128.9 0.7 copy-done.20
  129.5 0.7 broadcast_in_dim.3
  130.3 6.3 %all-to-all-start.1 = ((f32[16,16,256]{2,1,0:T(8,128)}), f32[16,16,256]{2,1,0:T(8,128)S(1)}, u32[]{:S(2)}, u32[]{:S(2)}) async-start(f32[16,16,256]{2,1,0:T(8,128)} %broadcast_in_dim.3), calls=%async_computation.1 | async-start | bytes 524288 | tf_op jit(solution)/shard_map/state_exchange/all_to_all | solution.py:248
  136.6 1.0 copy-done.8
  137.6 0.8 copy-done.12
  138.3 0.8 copy-done.22
  139.1 1.9 %local.1 = f32[64,8,256]{2,1,0:T(8,128)S(1)} custom-call(s32[4]{0:T(128)S(1)} %pad_add_fusion.refs_0_.pos, f32[64,8,256]{2,1,0:T(8,128)S(1)} %copy-done.8, f32[16,512]{1,0:T(8,128)S(1)} %copy-done.22, f32[16,512]{1,0:T(8,128)S(1)} %copy-done.12, f32[1,512]{1,0:T(1,128)S(1)} %bitcast.17), custom_call_target="tpu_custom_call" | custom-call | flops 20000000 | bytes 1000000 | tf_op jit(solution)/shard_map/local/pallas_call | solution.py:251
  141.0 6.1 %all-to-all-done.1.states = f32[16,16,256]{2,1,0:T(8,128)S(1)} async-done(((f32[16,16,256]{2,1,0:T(8,128)}), f32[16,16,256]{2,1,0:T(8,128)S(1)}, u32[]{:S(2)}, u32[]{:S(2)}) %all-to-all-start.1) | async-done | bytes 262176 | tf_op jit(solution)/shard_map/state_exchange/all_to_all | solution.py:248
  147.1 1.0 copy-done.10
  148.1 0.8 copy-done.13
  148.9 0.9 copy-done.21
  149.8 0.8 copy-done.23
  150.5 1.5 finish.1
  152.1 8.5 %all_to_all.16 = bf16[2,256,256]{2,1,0:T(8,128)(2,1)S(1)} all-to-all(bf16[2,256,256]{2,1,0:T(8,128)(2,1)S(1)} %finish.1), channel_id=1, replica_groups=mesh['y'=4,'h'=4,'c'=2,'l'=2,'x'=4] {'c'}, dimensions={0} | all-to-all | bytes 524288 | tf_op jit(solution)/shard_map/result_swap/all_to_all | solution.py:270
  160.7 0.8 copy.15
  (61 shorter events, 1.3 us)
Async XLA Ops:
  6.5 98.9 %all-gather.2.cloned.1.call-start = ((), (), s32[]{:S(2)}) async-start(), calls=%async_computation.3 | async-start | bytes 4734976 | tf_op jit(solution)/shard_map/token_gather/all_gather | solution.py:209
  7.3 7.1 %collective-permute-start = (bf16[16,512]{1,0:T(8,128)(2,1)S(1)}, bf16[16,512]{1,0:T(8,128)(2,1)S(1)}, u32[]{:S(2)}, u32[]{:S(2)}) collective-permute-start(bf16[16,512]{1,0:T(8,128)(2,1)S(1)} %slice.33), channel_id=1, source_target_pairs={{8,16},{24,32},{40,48},{56,64},{72,80},{88,96},{104,112},{120,128}... | collective-permute-start | bytes 49160 | tf_op jit(solution)/shard_map/token_gather/ppermute | solution.py:208
  21.2 21.6 %collective-permute-start.10 = (bf16[256,768]{1,0:T(8,128)(2,1)S(1)}, bf16[256,768]{1,0:T(8,128)(2,1)S(1)}, u32[]{:S(2)}, u32[]{:S(2)}) collective-permute-start(bf16[256,768]{1,0:T(8,128)(2,1)S(1)} %bitcast.12), channel_id=1, source_target_pairs={{0,48},{16,0},{32,16},{48,32},{1,49},{17,1},{33,17},{49,33},{2,50}... | collective-permute-start | bytes 1179656 | tf_op jit(solution)/shard_map/weight_gather/ppermute | solution.py:22
  27.6 25.7 %collective-permute-start.5 = (bf16[256,768]{1,0:T(8,128)(2,1)S(1)}, bf16[256,768]{1,0:T(8,128)(2,1)S(1)}, u32[]{:S(2)}, u32[]{:S(2)}) collective-permute-start(bf16[256,768]{1,0:T(8,128)(2,1)S(1)} %bitcast.13), channel_id=1, source_target_pairs={{0,16},{16,32},{32,48},{48,0},{1,17},{17,33},{33,49},{49,1},{2,18}... | collective-permute-start | bytes 1179656 | tf_op jit(solution)/shard_map/weight_gather/ppermute | solution.py:22
  27.6 29.0 %collective-permute-start.2 = (bf16[256,768]{1,0:T(8,128)(2,1)S(1)}, bf16[256,768]{1,0:T(8,128)(2,1)S(1)}, u32[]{:S(2)}, u32[]{:S(2)}) collective-permute-start(bf16[256,768]{1,0:T(8,128)(2,1)S(1)} %bitcast.14), channel_id=1, source_target_pairs={{0,192},{64,0},{128,64},{192,128},{1,193},{65,1},{129,65},{193,129... | collective-permute-start | bytes 1179656 | tf_op jit(solution)/shard_map/weight_gather/ppermute | solution.py:22
  42.8 13.8 %collective-permute-start.16 = (bf16[128,768]{1,0:T(8,128)(2,1)S(1)}, bf16[128,768]{1,0:T(8,128)(2,1)S(1)}, u32[]{:S(2)}, u32[]{:S(2)}) collective-permute-start(bf16[128,768]{1,0:T(8,128)(2,1)S(1)} %slice.51), channel_id=1, source_target_pairs={{0,48},{16,0},{32,16},{48,32},{1,49},{17,1},{33,17},{49,33},{2,50}... | collective-permute-start | bytes 589832 | tf_op jit(solution)/shard_map/weight_gather/ppermute | solution.py:22
  53.4 16.1 %collective-permute-start.15 = (bf16[128,768]{1,0:T(8,128)(2,1)S(1)}, bf16[128,768]{1,0:T(8,128)(2,1)S(1)}, u32[]{:S(2)}, u32[]{:S(2)}) collective-permute-start(bf16[128,768]{1,0:T(8,128)(2,1)S(1)} %slice.50), channel_id=1, source_target_pairs={{0,16},{16,32},{32,48},{48,0},{1,17},{17,33},{33,49},{49,1},{2,18}... | collective-permute-start | bytes 589832 | tf_op jit(solution)/shard_map/weight_gather/ppermute | solution.py:22
  53.5 17.1 %collective-permute-start.1 = (bf16[256,768]{1,0:T(8,128)(2,1)S(1)}, bf16[256,768]{1,0:T(8,128)(2,1)S(1)}, u32[]{:S(2)}, u32[]{:S(2)}) collective-permute-start(bf16[256,768]{1,0:T(8,128)(2,1)S(1)} %bitcast.15), channel_id=1, source_target_pairs={{0,64},{64,128},{128,192},{192,0},{1,65},{65,129},{129,193},{193,1... | collective-permute-start | bytes 1179656 | tf_op jit(solution)/shard_map/weight_gather/ppermute | solution.py:22
  54.9 17.7 %collective-permute-start.12 = (bf16[256,768]{1,0:T(8,128)(2,1)S(1)}, bf16[256,768]{1,0:T(8,128)(2,1)S(1)}, u32[]{:S(2)}, u32[]{:S(2)}) collective-permute-start(bf16[256,768]{1,0:T(8,128)(2,1)S(1)} %collective-permute-done.10.refs_12_), channel_id=1, source_target_pairs={{0,192},{64,0},{128,64},{192,128},{1,193},{65,1},{129,65},{193,129... | collective-permute-start | bytes 1179656 | tf_op jit(solution)/shard_map/weight_gather/ppermute | solution.py:22
  56.7 16.1 %collective-permute-start.11 = (bf16[256,768]{1,0:T(8,128)(2,1)S(1)}, bf16[256,768]{1,0:T(8,128)(2,1)S(1)}, u32[]{:S(2)}, u32[]{:S(2)}) collective-permute-start(bf16[256,768]{1,0:T(8,128)(2,1)S(1)} %collective-permute-done.10.refs_12_), channel_id=1, source_target_pairs={{0,64},{64,128},{128,192},{192,0},{1,65},{65,129},{129,193},{193,1... | collective-permute-start | bytes 1179656 | tf_op jit(solution)/shard_map/weight_gather/ppermute | solution.py:22
  56.7 18.8 %collective-permute-start.7 = (bf16[256,768]{1,0:T(8,128)(2,1)S(1)}, bf16[256,768]{1,0:T(8,128)(2,1)S(1)}, u32[]{:S(2)}, u32[]{:S(2)}) collective-permute-start(bf16[256,768]{1,0:T(8,128)(2,1)S(1)} %collective-permute-done.5.refs_7_), channel_id=1, source_target_pairs={{0,192},{64,0},{128,64},{192,128},{1,193},{65,1},{129,65},{193,129... | collective-permute-start | bytes 1179656 | tf_op jit(solution)/shard_map/weight_gather/ppermute | solution.py:22
  69.5 11.3 %collective-permute-start.6 = (bf16[256,768]{1,0:T(8,128)(2,1)S(1)}, bf16[256,768]{1,0:T(8,128)(2,1)S(1)}, u32[]{:S(2)}, u32[]{:S(2)}) collective-permute-start(bf16[256,768]{1,0:T(8,128)(2,1)S(1)} %collective-permute-done.5.refs_7_), channel_id=1, source_target_pairs={{0,64},{64,128},{128,192},{192,0},{1,65},{65,129},{129,193},{193,1... | collective-permute-start | bytes 1179656 | tf_op jit(solution)/shard_map/weight_gather/ppermute | solution.py:22
  70.5 20.6 %copy-start.5 = (bf16[256,768]{1,0:T(8,128)(2,1)}, bf16[256,768]{1,0:T(8,128)(2,1)S(1)}, u32[]{:S(2)}) copy-start(bf16[256,768]{1,0:T(8,128)(2,1)S(1)} %constant_dynamic-update-slice_fusion.refs_17_) | copy-start | bytes 1179652
  70.5 13.6 %collective-permute-start.18 = (bf16[256,768]{1,0:T(8,128)(2,1)S(1)}, bf16[256,768]{1,0:T(8,128)(2,1)S(1)}, u32[]{:S(2)}, u32[]{:S(2)}) collective-permute-start(bf16[256,768]{1,0:T(8,128)(2,1)S(1)} %constant_dynamic-update-slice_fusion.refs_17_), channel_id=1, source_target_pairs={{0,192},{64,0},{128,64},{192,128},{1,193},{65,1},{129,65},{193,129... | collective-permute-start | bytes 1179656 | tf_op jit(solution)/shard_map/weight_gather/ppermute | solution.py:22
  72.7 16.6 %collective-permute-start.17 = (bf16[256,768]{1,0:T(8,128)(2,1)S(1)}, bf16[256,768]{1,0:T(8,128)(2,1)S(1)}, u32[]{:S(2)}, u32[]{:S(2)}) collective-permute-start(bf16[256,768]{1,0:T(8,128)(2,1)S(1)} %constant_dynamic-update-slice_fusion.refs_17_), channel_id=1, source_target_pairs={{0,64},{64,128},{128,192},{192,0},{1,65},{65,129},{129,193},{193,1... | collective-permute-start | bytes 1179656 | tf_op jit(solution)/shard_map/weight_gather/ppermute | solution.py:22
  72.8 19.1 %collective-permute-start.4 = (bf16[128,768]{1,0:T(8,128)(2,1)S(1)}, bf16[128,768]{1,0:T(8,128)(2,1)S(1)}, u32[]{:S(2)}, u32[]{:S(2)}) collective-permute-start(bf16[128,768]{1,0:T(8,128)(2,1)S(1)} %slice.45), channel_id=1, source_target_pairs={{0,192},{64,0},{128,64},{192,128},{1,193},{65,1},{129,65},{193,129... | collective-permute-start | bytes 589832 | tf_op jit(solution)/shard_map/weight_gather/ppermute | solution.py:22
  75.5 17.9 %collective-permute-start.3 = (bf16[128,768]{1,0:T(8,128)(2,1)S(1)}, bf16[128,768]{1,0:T(8,128)(2,1)S(1)}, u32[]{:S(2)}, u32[]{:S(2)}) collective-permute-start(bf16[128,768]{1,0:T(8,128)(2,1)S(1)} %slice.44), channel_id=1, source_target_pairs={{0,64},{64,128},{128,192},{192,0},{1,65},{65,129},{129,193},{193,1... | collective-permute-start | bytes 589832 | tf_op jit(solution)/shard_map/weight_gather/ppermute | solution.py:22
  80.8 15.1 %collective-permute-start.14 = (bf16[128,768]{1,0:T(8,128)(2,1)S(1)}, bf16[128,768]{1,0:T(8,128)(2,1)S(1)}, u32[]{:S(2)}, u32[]{:S(2)}) collective-permute-start(bf16[128,768]{1,0:T(8,128)(2,1)S(1)} %slice.49), channel_id=1, source_target_pairs={{0,192},{64,0},{128,64},{192,128},{1,193},{65,1},{129,65},{193,129... | collective-permute-start | bytes 589832 | tf_op jit(solution)/shard_map/weight_gather/ppermute | solution.py:22
  84.1 13.6 %collective-permute-start.13 = (bf16[128,768]{1,0:T(8,128)(2,1)}, bf16[128,768]{1,0:T(8,128)(2,1)}, u32[]{:S(2)}, u32[]{:S(2)}) collective-permute-start(bf16[128,768]{1,0:T(8,128)(2,1)} %slice.48), channel_id=1, source_target_pairs={{0,64},{64,128},{128,192},{192,0},{1,65},{65,129},{129,193},{193,1... | collective-permute-start | bytes 589832 | tf_op jit(solution)/shard_map/weight_gather/ppermute | solution.py:22
  85.1 0.8 copy-start.1
  89.2 8.4 %collective-permute-start.9 = (bf16[128,768]{1,0:T(8,128)(2,1)}, bf16[128,768]{1,0:T(8,128)(2,1)}, u32[]{:S(2)}, u32[]{:S(2)}) collective-permute-start(bf16[128,768]{1,0:T(8,128)(2,1)} %slice.47), channel_id=1, source_target_pairs={{0,192},{64,0},{128,64},{192,128},{1,193},{65,1},{129,65},{193,129... | collective-permute-start | bytes 589832 | tf_op jit(solution)/shard_map/weight_gather/ppermute | solution.py:22
  91.1 0.7 copy-start.3
  91.9 0.7 copy-start.14
  92.5 9.4 %collective-permute-start.8 = (bf16[128,768]{1,0:T(8,128)(2,1)}, bf16[128,768]{1,0:T(8,128)(2,1)}, u32[]{:S(2)}, u32[]{:S(2)}) collective-permute-start(bf16[128,768]{1,0:T(8,128)(2,1)} %slice.46), channel_id=1, source_target_pairs={{0,64},{64,128},{128,192},{192,0},{1,65},{65,129},{129,193},{193,1... | collective-permute-start | bytes 589832 | tf_op jit(solution)/shard_map/weight_gather/ppermute | solution.py:22
  93.5 0.7 copy-start.16
  94.1 7.9 %collective-permute-start.20 = (bf16[128,768]{1,0:T(8,128)(2,1)}, bf16[128,768]{1,0:T(8,128)(2,1)}, u32[]{:S(2)}, u32[]{:S(2)}) collective-permute-start(bf16[128,768]{1,0:T(8,128)(2,1)} %slice.53), channel_id=1, source_target_pairs={{0,192},{64,0},{128,64},{192,128},{1,193},{65,1},{129,65},{193,129... | collective-permute-start | bytes 589832 | tf_op jit(solution)/shard_map/weight_gather/ppermute | solution.py:22
  95.9 0.7 copy-start.18
  96.6 8.8 %collective-permute-start.19 = (bf16[128,768]{1,0:T(8,128)(2,1)}, bf16[128,768]{1,0:T(8,128)(2,1)}, u32[]{:S(2)}, u32[]{:S(2)}) collective-permute-start(bf16[128,768]{1,0:T(8,128)(2,1)} %slice.52), channel_id=1, source_target_pairs={{0,64},{64,128},{128,192},{192,0},{1,65},{65,129},{129,193},{193,1... | collective-permute-start | bytes 589832 | tf_op jit(solution)/shard_map/weight_gather/ppermute | solution.py:22
  96.6 39.9 %copy-start.25 = (f32[512]{0:T(512)S(1)}, f32[512]{0:T(512)}, u32[]{:S(2)}) copy-start(f32[512]{0:T(512)} %param.11) | copy-start | bytes 6148
  105.4 2.3 %copy-start = (bf16[4352,512]{1,0:T(8,128)(2,1)S(1)}, bf16[4352,512]{1,0:T(8,128)(2,1)}, u32[]{:S(2)}) copy-start(bf16[4352,512]{1,0:T(8,128)(2,1)} %all-gather.2.cloned.1.call-done.refs_1_) | copy-start | bytes 13369348
  107.7 1.0 copy-start.2
  108.7 1.0 copy-start.4
  109.7 1.0 copy-start.6
  110.7 0.8 copy-start.11
  111.4 0.9 copy-start.15
  112.4 0.9 copy-start.17
  113.3 0.9 copy-start.19
  114.2 0.7 copy-start.24
  127.3 0.8 copy-start.7
  128.1 0.8 copy-start.9
  128.9 0.7 copy-start.20
  130.3 16.8 %all-to-all-start.1 = ((f32[16,16,256]{2,1,0:T(8,128)}), f32[16,16,256]{2,1,0:T(8,128)S(1)}, u32[]{:S(2)}, u32[]{:S(2)}) async-start(f32[16,16,256]{2,1,0:T(8,128)} %broadcast_in_dim.3), calls=%async_computation.1 | async-start | bytes 524288 | tf_op jit(solution)/shard_map/state_exchange/all_to_all | solution.py:248
  136.5 1.0 copy-start.8
  137.6 0.8 copy-start.12
  138.3 0.8 copy-start.22
  147.1 1.0 copy-start.10
  148.1 0.8 copy-start.13
  148.9 0.9 copy-start.21
  149.8 0.8 copy-start.23
Sparse Core Ops, SparseCore 0:
  16.2 64.9 all-gather.1

commit v2 on v1

--- a/solution.py
+++ b/solution.py
@@ -22,22 +22,26 @@
     return lax.ppermute(array, axis, [(i, (i + step) % n) for i in range(n)])
 
 
-def ring(piece, axis):
-    half = piece.shape[0] // 2
-    behind = shifted(piece, axis, 1)
-    ahead = shifted(piece, axis, -1)
-    first = shifted(behind[:half], axis, 1)
-    second = shifted(ahead[half:], axis, -1)
-    return behind, ahead, first, second
+def both_ways(piece, axis):
+    return shifted(piece, axis, 1), shifted(piece, axis, -1)
+
+
+def onward(behind, ahead, axis):
+    half = behind.shape[0] // 2
+    return shifted(behind[:half], axis, 1), shifted(ahead[half:], axis, -1)
+
+
+def place(sizes, pos, dy, dh):
+    rows, depth, width, modes, seq = sizes
+    k = depth // 16
+    ys, hs = lax.rem(pos[1] - dy + 4, 4), lax.rem(pos[2] - dh + 4, 4)
+    return pl.multiple_of((ys * 4 + hs) * k, k)
 
 
 def project_kernel(sizes, *refs):
     rows, depth, width, modes, seq = sizes
-    pos, tok, *pieces = refs[:22]
-    taps, decay = refs[22:24]
-    gate, product, inside, state = refs[24:28]
-    tokv, wv, acc, tok_sem, w_sem = refs[28:]
-    y, h, c = pos[1], pos[2], pos[3]
+    pos, tok, halo, *pieces = refs[:16]
+    acc, tokv, wv, tok_sem, w_sem = refs[16:]
     k = depth // 16
     half = k // 2
     top = rows + HALO
@@ -45,52 +49,97 @@
     copies = []
     for ch in range(8):
         lanes = pl.ds(ch * (depth // 8), depth // 8)
+        copies.append((halo.at[pl.ds(ch * HALO, HALO), :], tokv.at[pl.ds(0, HALO), lanes]))
         for core in range(2):
-            skip = HALO * core
-            at = (core * 8 + ch) * top
+            at = (core * 8 + ch) * rows
             copies.append(
-                pltpu.make_async_copy(
-                    tok.at[pl.ds(at + skip, top - skip), :],
-                    tokv.at[pl.ds(core * top, top - skip), lanes],
-                    tok_sem.at[core * 8 + ch],
-                )
+                (tok.at[pl.ds(at, rows), :], tokv.at[pl.ds(HALO + core * rows, rows), lanes])
             )
-    groups = [[], [], [], []]
-    for kind, dh in enumerate((0, 1, -1, 2)):
-        hs = lax.rem(h - dh + 4, 4)
-        for number, (dy, skip, n, group) in enumerate(
-            ((0, 0, k, 0), (1, 0, k, 1), (-1, 0, k, 2), (2, 0, half, 3), (2, half, half, 3))
-        ):
-            ys = lax.rem(y - dy + 4, 4)
-            at = pl.multiple_of((ys * 4 + hs) * k + skip, half)
+    copies = [pltpu.make_async_copy(a, b, tok_sem.at[i]) for i, (a, b) in enumerate(copies)]
+    lie = {}
+    parts = iter(pieces)
+    for dy in (0, 1, -1):
+        for run in (((0, 0, k),), ((1, 0, k), (-1, 0, k)), ((2, 0, k),)):
+            piece, at = next(parts), 0
+            for dh, skip, n in run:
+                lie.setdefault(dy, []).append((piece, at, dh, skip, n))
+                at += n
+    for run in (((0, 0, half),), ((0, half, half),), ((1, 0, k),), ((-1, 0, k),)):
+        for dh, skip, n in run:
+            lie.setdefault(2, []).append((next(parts), 0, dh, skip, n))
+    groups, number = {}, 0
+    for dy, list_ in lie.items():
+        for piece, at, dh, skip, n in list_:
+            to = pl.multiple_of(place(sizes, pos, dy, dh) + skip, half)
             copy = pltpu.make_async_copy(
-                pieces[kind * 5 + number], wv.at[pl.ds(at, n), :], w_sem.at[kind * 5 + number]
+                piece.at[pl.ds(at, n), :], wv.at[pl.ds(to, n), :], w_sem.at[number]
             )
-            groups[group].append(copy)
-    for copy in groups[0] + copies + groups[1] + groups[2] + groups[3]:
+            groups.setdefault(dy, []).append(copy)
+            number += 1
+    for copy in groups[0] + copies + groups[1] + groups[-1] + groups[2]:
         copy.start()
     for copy in copies:
         copy.wait()
-    for group, dy in enumerate((0, 1, -1, 2)):
-        for copy in groups[group]:
-            copy.wait()
-        at = pl.multiple_of(lax.rem(y - dy + 4, 4) * (4 * k), 4 * k)
-
+
+    def add(at, n, first=False):
         @pl.loop(0, 3)
         def _(j):
             cols = pl.ds(pl.multiple_of(j * width, width), width)
-            part = jnp.dot(
-                tokv[:, pl.ds(at, 4 * k)], wv[pl.ds(at, 4 * k), cols], preferred_element_type=F32
-            )
+            part = jnp.dot(tokv[:, pl.ds(at, n)], wv[pl.ds(at, n), cols], preferred_element_type=F32)
             for lh in range(width // 128):
-                at_lane = j * (width // 128) + lh
+                chunk = j * (width // 128) + lh
                 new = part[:, lh * 128 : lh * 128 + 128]
-                if group == 0:
-                    acc[at_lane] = new
-                elif group < 3:
-                    acc[at_lane] += new
+                if first:
+                    acc[chunk] = new
                 else:
-                    acc[at_lane] = (acc[at_lane] + new).astype(BF16).astype(F32)
+                    acc[chunk] += new
+
+    for dy in (0, 1, -1):
+        for copy in groups[dy]:
+            copy.wait()
+        at = pl.multiple_of(lax.rem(pos[1] - dy + 4, 4) * (4 * k), 4 * k)
+        add(at, 4 * k, dy == 0)
+    for copy in groups[2]:
+        copy.wait()
+    for dh in (0, 1, -1):
+        add(place(sizes, pos, 2, dh), k)
+
+
+def state_kernel(sizes, *refs):
+    rows, depth, width, modes, seq = sizes
+    pos, tok, halo, first, second, sums, taps, decay = refs[:8]
+    gate, product, inside, state = refs[8:12]
+    tokv, wv, acc, sem = refs[12:]
+    c = pos[3]
+    k = depth // 16
+    half = k // 2
+    at = place(sizes, pos, 2, 2)
+    ch = lax.div(at, depth // 8)
+    lanes = pl.ds(pl.multiple_of(lax.rem(at, depth // 8), k), k)
+    copies = [
+        (halo.at[pl.ds(pl.multiple_of(ch * HALO, HALO), HALO), lanes], tokv.at[pl.ds(0, HALO), :]),
+        (first, wv.at[pl.ds(0, half), :]),
+        (second, wv.at[pl.ds(half, half), :]),
+    ]
+    for core in range(2):
+        from_ = pl.multiple_of((core * 8 + ch) * rows, rows)
+        copies.append(
+            (tok.at[pl.ds(from_, rows), lanes], tokv.at[pl.ds(HALO + core * rows, rows), :])
+        )
+    copies = [pltpu.make_async_copy(a, b, sem.at[i]) for i, (a, b) in enumerate(copies)]
+    for copy in copies:
+        copy.start()
+    for copy in copies:
+        copy.wait()
+
+    @pl.loop(0, 3)
+    def _(j):
+        cols = pl.ds(pl.multiple_of(j * width, width), width)
+        part = jnp.dot(tokv[...], wv[:, cols], preferred_element_type=F32)
+        for lh in range(width // 128):
+            chunk = j * (width // 128) + lh
+            new = part[:, lh * 128 : lh * 128 + 128]
+            acc[chunk] = (sums[chunk] + new).astype(BF16).astype(F32)
 
     steps = 2 * rows // SUB
     for lh in range(width // 128):
@@ -204,45 +253,74 @@
     y, h, c = (lax.axis_index(a) for a in CTX)
     pos = jnp.stack([y * 4 + h, y, h, c]).astype(jnp.int32)
 
+    tie = lax.optimization_barrier
     with jax.named_scope("token_gather"):
-        tail = lax.ppermute(tokens[rows - HALO :], CTX, [(i, i + 1) for i in range(1, 31, 2)])
-        tok = lax.all_gather(jnp.concatenate([tail, tokens], 0), ("c", *CH), axis=0, tiled=True)
+        tok = lax.all_gather(tokens, ("c", *CH), axis=0, tiled=True)
+        tail = tok.reshape(2, 8, rows, group)[1, :, rows - HALO :].reshape(8 * HALO, group)
+        halo = lax.ppermute(tail, ("y", "h"), [(i, i + 1) for i in range(15)])
 
     with jax.named_scope("weight_gather"):
         halves = w_in.reshape(k, 3, 2, width).transpose(2, 0, 1, 3).reshape(2, k, 3 * width)
         own = lax.all_to_all(halves, "c", 0, 0, tiled=True).reshape(2 * k, 3 * width)
-        behind, ahead, first, second = ring(own, "h")
-        opposite = jnp.concatenate([first, second], 0)
-        pieces = []
-        for piece in (own, behind, ahead, opposite):
-            pieces += [piece, *ring(piece, "y")]
+        beside, far = both_ways(own, "h"), both_ways(own, "y")
+        beside, far = tie((beside, far))
+        pair = jnp.concatenate(beside, 0)
+        far_pair, farther = both_ways(pair, "y"), onward(*far, "y")
+        opposite = onward(*beside, "h")
+        far_pair, farther, opposite = tie((far_pair, farther, opposite))
+        opposite = jnp.concatenate(opposite, 0)
+        far_opposite, farther_pair = both_ways(opposite, "y"), onward(*far_pair, "y")
+        far_opposite, farther_pair = tie((far_opposite, farther_pair))
+        last = onward(*far_opposite, "y")
+        pieces = [own, pair, opposite]
+        for side in range(2):
+            pieces += [far[side], far_pair[side], far_opposite[side]]
+        pieces += [*farther, *farther_pair]
 
     vmem = pl.BlockSpec(memory_space=pltpu.VMEM)
     smem = pl.BlockSpec(memory_space=pltpu.SMEM)
-    anywhere = pl.BlockSpec(memory_space=pl.ANY)
+    hbm = pl.BlockSpec(memory_space=pltpu.HBM)
     block = (2 * rows // SUB, SUB, width)
     full = jax.ShapeDtypeStruct(block, F32)
-    params = pltpu.CompilerParams(vmem_limit_bytes=40 * 2**20)
+    lines = 2 * rows + HALO
+    chunks = (3 * width // 128, lines, 128)
+    sums = pl.pallas_call(
+        functools.partial(project_kernel, sizes),
+        out_shape=jax.ShapeDtypeStruct(chunks, F32),
+        in_specs=[smem] + [hbm] * 15,
+        out_specs=vmem,
+        scratch_shapes=[
+            pltpu.VMEM((lines, depth), BF16),
+            pltpu.VMEM((depth, 3 * width), BF16),
+            pltpu.SemaphoreType.DMA((24,)),
+            pltpu.SemaphoreType.DMA((16,)),
+        ],
+        compiler_params=pltpu.CompilerParams(vmem_limit_bytes=20 * 2**20),
+        cost_estimate=pl.CostEstimate(
+            flops=2 * lines * depth * 3 * width, bytes_accessed=12_000_000, transcendentals=0
+        ),
+        name="project",
+    )(pos, tok, halo, *pieces)
+    params = pltpu.CompilerParams(vmem_limit_bytes=12 * 2**20)
     gate, product, inside, state = pl.pallas_call(
-        functools.partial(project_kernel, sizes),
+        functools.partial(state_kernel, sizes),
         out_shape=(
             full,
             full,
             jax.ShapeDtypeStruct((modes, SUB, width), F32),
             jax.ShapeDtypeStruct((modes, width), F32),
         ),
-        in_specs=[smem] + [anywhere] * 21 + [vmem] * 2,
+        in_specs=[smem] + [hbm] * 4 + [vmem] * 3,
         out_specs=(vmem,) * 4,
         scratch_shapes=[
-            pltpu.VMEM((2 * rows + HALO, depth), BF16),
-            pltpu.VMEM((depth, 3 * width), BF16),
-            pltpu.VMEM((3 * width // 128, 2 * rows + HALO, 128), F32),
-            pltpu.SemaphoreType.DMA((16,)),
-            pltpu.SemaphoreType.DMA((20,)),
+            pltpu.VMEM((lines, depth // 16), BF16),
+            pltpu.VMEM((depth // 16, 3 * width), BF16),
+            pltpu.VMEM(chunks, F32),
+            pltpu.SemaphoreType.DMA((5,)),
         ],
         compiler_params=params,
-        name="project",
-    )(pos, tok, *pieces, taps, decay)
+        name="states",
+    )(pos, tok, halo, *last, sums, taps, decay)
 
     with jax.named_scope("state_exchange"):
         states = lax.all_to_all(

time: 172 us -> 159 us (0.924); the launches traced: 168 us -> 159 us
  local copies, waits for them, and re-layouts: 28.8 us -> 16.3 us
  starting transfers between devices: 40.4 us -> 34.3 us
  waiting for transfers between devices: 56 us -> 61.1 us
  blocking collectives: 12.2 us -> 16 us
    unnamed x54 -> x29, local copies, waits for them, and re-layouts: 22.6 us -> 9.23 us
    ppermute x20 -> x16, starting transfers between devices: 27.8 us -> 21.8 us  [shifted(): return lax.ppermute(array, axis, [(i, (i + step) % n) for i in range(n)])]
    ppermute x1, starting transfers between devices: 6.27 us -> 2.55 us  [body(): halo = lax.ppermute(tail, ('y', 'h'), [(i, i + 1) for i in range(15)])]
    all_to_all x1, starting transfers between devices: 6.26 us -> 9.98 us  [body(): lax.all_to_all(jnp.broadcast_to(state, (16, *state.shape)), ('y', 'h'), 0...]
    all_to_all x1, blocking collectives: 3.69 us -> 6.92 us  [body(): lax.all_to_all(halves, 'c', 0, 0, tiled=True).reshape(2 * k, 3 * width)]
    all_to_all x1, waiting for transfers between devices: 6.09 us -> 9.3 us  [body(): lax.all_to_all(jnp.broadcast_to(state, (16, *state.shape)), ('y', 'h'), 0...]
    ppermute x20 -> x16, waiting for transfers between devices: 49.1 us -> 51 us  [shifted(): return lax.ppermute(array, axis, [(i, (i + step) % n) for i in range(n)])]
    pallas_call x1 -> x2, Pallas kernels: 12.3 us -> 14 us  [the longest x1 10.1 us: body(): pl.pallas_call(functools.partial(project_kernel, sizes), out_shape=jax.Sh...]
  transfers between devices with their start and end apart: 23 -> 19, of which waited for: 11 -> 11; matrix products, arithmetic and copies ran while one was open for 3% -> 5% of each run, Pallas kernels for 1% -> 8%
where the time goes in v2:
time: 159 us
  waiting for transfers between devices  61.1 us (38%)
  starting transfers between devices  34.3 us (22%)
  Pallas kernels  17.4 us (11%)
  local copies, waits for them, and re-layouts  16.3 us (10%)
  blocking collectives  16 us (10%)
  between operations  13.6 us (9%)
    ppermute x16, waiting for transfers between devices, shifted(): return lax.ppermute(array, axis, [(i, (i + step) % n) for i in range(n)])  51 us
    ppermute x16, starting transfers between devices, shifted(): return lax.ppermute(array, axis, [(i, (i + step) % n) for i in range(n)])  21.8 us
    pallas_call x1, Pallas kernels, body(): pl.pallas_call(functools.partial(project_kernel, sizes), out_shape=jax.Sh...  10.1 us
    all_to_all x1, starting transfers between devices, body(): lax.all_to_all(jnp.broadcast_to(state, (16, *state.shape)), ('y', 'h'), 0...  9.98 us
    all_to_all x1, waiting for transfers between devices, body(): lax.all_to_all(jnp.broadcast_to(state, (16, *state.shape)), ('y', 'h'), 0...  9.3 us
    unnamed x29, local copies, waits for them, and re-layouts  9.23 us
    all_to_all x1, blocking collectives, body(): both = lax.all_to_all(out, 'c', 0, 0, tiled=True)  9.12 us
    all_to_all x1, blocking collectives, body(): lax.all_to_all(halves, 'c', 0, 0, tiled=True).reshape(2 * k, 3 * width)  6.92 us
  transfers between devices with their start and end apart: 19, of which 11 were waited for; matrix products, arithmetic and copies ran while one was open for 5% of the time, Pallas kernels for 8%

profile of v2, /device:TPU:1, one launch (start us, length us, event | category | flops | bytes accessed | tf_op | source)
XLA Modules:
  0.0 158.8 jit_solution(7614767991045235287)
XLA Ops:
  6.5 0.7 all-gather.2.cloned.1.call-update
  7.3 1.2 copy.11
  8.5 6.9 %all_to_all.15 = bf16[2,128,768]{1,2,0:T(8,128)(2,1)S(1)} all-to-all(bf16[2,128,768]{1,2,0:T(8,128)(2,1)S(1)} %bitcast.21), channel_id=1, replica_groups=mesh['y'=4,'h'=4,'c'=2,'l'=2,'x'=4] {'c'}, dimensions={0} | all-to-all | bytes 786432 | tf_op jit(solution)/shard_map/weight_gather/all_to_all | solution.py:264
  15.4 0.2 copy.13
  15.6 1.1 collective-permute-start.4
  16.7 0.5 collective-permute-start.3
  17.2 5.6 %collective-permute-start.2 = (bf16[256,768]{1,0:T(8,128)(2,1)S(1)}, bf16[256,768]{1,0:T(8,128)(2,1)S(1)}, u32[]{:S(2)}, u32[]{:S(2)}) collective-permute-start(bf16[256,768]{1,0:T(8,128)(2,1)S(1)} %bitcast.17), channel_id=1, source_target_pairs={{0,48},{16,0},{32,16},{48,32},{1,49},{17,1},{33,17},{49,33},{2,50}... | collective-permute-start | bytes 1179656 | tf_op jit(solution)/shard_map/weight_gather/ppermute | solution.py:22
  22.7 0.0 collective-permute-start.1
  22.7 3.3 %collective-permute-done.4.refs_9_ = bf16[256,768]{1,0:T(8,128)(2,1)S(1)} collective-permute-done((bf16[256,768]{1,0:T(8,128)(2,1)S(1)}, bf16[256,768]{1,0:T(8,128)(2,1)S(1)}, u32[]{:S(2)}, u32[]{:S(2)}) %collective-permute-start.4) | collective-permute-done | bytes 393248 | tf_op jit(solution)/shard_map/weight_gather/ppermute | solution.py:22
  26.0 1.9 %collective-permute-done.3.refs_6_ = bf16[256,768]{1,0:T(8,128)(2,1)S(1)} collective-permute-done((bf16[256,768]{1,0:T(8,128)(2,1)S(1)}, bf16[256,768]{1,0:T(8,128)(2,1)S(1)}, u32[]{:S(2)}, u32[]{:S(2)}) %collective-permute-start.3) | collective-permute-done | bytes 393248 | tf_op jit(solution)/shard_map/weight_gather/ppermute | solution.py:22
  27.9 6.3 %collective-permute-done.2 = bf16[256,768]{1,0:T(8,128)(2,1)S(1)} collective-permute-done((bf16[256,768]{1,0:T(8,128)(2,1)S(1)}, bf16[256,768]{1,0:T(8,128)(2,1)S(1)}, u32[]{:S(2)}, u32[]{:S(2)}) %collective-permute-start.2) | collective-permute-done | bytes 393248 | tf_op jit(solution)/shard_map/weight_gather/ppermute | solution.py:22
  34.2 14.1 %collective-permute-done.1 = bf16[256,768]{1,0:T(8,128)(2,1)S(1)} collective-permute-done((bf16[256,768]{1,0:T(8,128)(2,1)S(1)}, bf16[256,768]{1,0:T(8,128)(2,1)S(1)}, u32[]{:S(2)}, u32[]{:S(2)}) %collective-permute-start.1) | collective-permute-done | bytes 393248 | tf_op jit(solution)/shard_map/weight_gather/ppermute | solution.py:22
  48.4 2.9 %collective-permute-start.6 = (bf16[512,768]{1,0:T(8,128)(2,1)S(1)}, bf16[512,768]{1,0:T(8,128)(2,1)S(1)}, u32[]{:S(2)}, u32[]{:S(2)}) collective-permute-start(bf16[512,768]{1,0:T(8,128)(2,1)S(1)} %constant_dynamic-update-slice_fusion.refs_4_), channel_id=1, source_target_pairs={{0,192},{64,0},{128,64},{192,128},{1,193},{65,1},{129,65},{193,129... | collective-permute-start | bytes 2359304 | tf_op jit(solution)/shard_map/weight_gather/ppermute | solution.py:22
  51.3 0.0 collective-permute-start.5
  51.3 2.8 %collective-permute-start.8 = (bf16[128,768]{1,0:T(8,128)(2,1)S(1)}, bf16[128,768]{1,0:T(8,128)(2,1)S(1)}, u32[]{:S(2)}, u32[]{:S(2)}) collective-permute-start(bf16[128,768]{1,0:T(8,128)(2,1)S(1)} %slice.29), channel_id=1, source_target_pairs={{0,192},{64,0},{128,64},{192,128},{1,193},{65,1},{129,65},{193,129... | collective-permute-start | bytes 589832 | tf_op jit(solution)/shard_map/weight_gather/ppermute | solution.py:22
  54.1 0.1 collective-permute-start.7
  54.2 0.1 collective-permute-start.10
  54.3 13.8 %collective-permute-done.8.refs_13_ = bf16[128,768]{1,0:T(8,128)(2,1)S(1)} collective-permute-done((bf16[128,768]{1,0:T(8,128)(2,1)S(1)}, bf16[128,768]{1,0:T(8,128)(2,1)S(1)}, u32[]{:S(2)}, u32[]{:S(2)}) %collective-permute-start.8) | collective-permute-done | bytes 196640 | tf_op jit(solution)/shard_map/weight_gather/ppermute | solution.py:22
  68.1 0.7 copy-done.9
  68.8 0.0 collective-permute-start.9
  68.8 2.4 %collective-permute-done.7.refs_12_ = bf16[128,768]{1,0:T(8,128)(2,1)S(1)} collective-permute-done((bf16[128,768]{1,0:T(8,128)(2,1)S(1)}, bf16[128,768]{1,0:T(8,128)(2,1)S(1)}, u32[]{:S(2)}, u32[]{:S(2)}) %collective-permute-start.7) | collective-permute-done | bytes 196640 | tf_op jit(solution)/shard_map/weight_gather/ppermute | solution.py:22
  71.2 0.7 copy-done.11
  71.9 0.0 collective-permute-done.10
  71.9 3.7 %collective-permute-done.9 = bf16[128,768]{1,0:T(8,128)(2,1)S(1)} collective-permute-done((bf16[128,768]{1,0:T(8,128)(2,1)S(1)}, bf16[128,768]{1,0:T(8,128)(2,1)S(1)}, u32[]{:S(2)}, u32[]{:S(2)}) %collective-permute-start.9) | collective-permute-done | bytes 196640 | tf_op jit(solution)/shard_map/weight_gather/ppermute | solution.py:22
  75.7 0.0 collective-permute-done.6.refs_10_
  75.7 0.0 collective-permute-done.5.refs_7_
  75.7 0.8 slice.32
  76.5 0.8 slice.33
  77.2 3.3 %collective-permute-start.14 = (bf16[256,768]{1,0:T(8,128)(2,1)}, bf16[256,768]{1,0:T(8,128)(2,1)}, u32[]{:S(2)}, u32[]{:S(2)}) collective-permute-start(bf16[256,768]{1,0:T(8,128)(2,1)} %slice.33), channel_id=1, source_target_pairs={{0,192},{64,0},{128,64},{192,128},{1,193},{65,1},{129,65},{193,129... | collective-permute-start | bytes 1179656 | tf_op jit(solution)/shard_map/weight_gather/ppermute | solution.py:22
  80.5 0.0 collective-permute-start.13
  80.5 0.7 constant_dynamic-update-slice_fusion.3
  81.2 0.7 constant_dynamic-update-slice_fusion.2.refs_5_
  81.9 2.7 %collective-permute-start.12 = (bf16[256,768]{1,0:T(8,128)(2,1)}, bf16[256,768]{1,0:T(8,128)(2,1)}, u32[]{:S(2)}, u32[]{:S(2)}) collective-permute-start(bf16[256,768]{1,0:T(8,128)(2,1)} %constant_dynamic-update-slice_fusion.2.refs_5_), channel_id=1, source_target_pairs={{0,192},{64,0},{128,64},{192,128},{1,193},{65,1},{129,65},{193,129... | collective-permute-start | bytes 1179656 | tf_op jit(solution)/shard_map/weight_gather/ppermute | solution.py:22
  84.6 0.0 collective-permute-start.11
  84.6 0.9 slice.36
  85.5 2.5 %collective-permute-start = (bf16[128,512]{1,0:T(8,128)(2,1)S(1)}, bf16[128,512]{1,0:T(8,128)(2,1)S(1)}, u32[]{:S(2)}, u32[]{:S(2)}) collective-permute-start(bf16[128,512]{1,0:T(8,128)(2,1)S(1)} %bitcast.25), channel_id=1, source_target_pairs={{0,16},{16,32},{32,48},{48,64},{64,80},{80,96},{96,112},{112,128},... | collective-permute-start | bytes 393224 | tf_op jit(solution)/shard_map/token_gather/ppermute | solution.py:260
  88.0 0.1 pad_add_fusion.refs_0_.pos
  88.1 0.0 collective-permute-done.14.refs_15_
  88.1 0.5 collective-permute-done.13.refs_14_
  88.7 1.7 %collective-permute-done.12.refs_11_ = bf16[256,768]{1,0:T(8,128)(2,1)} collective-permute-done((bf16[256,768]{1,0:T(8,128)(2,1)}, bf16[256,768]{1,0:T(8,128)(2,1)}, u32[]{:S(2)}, u32[]{:S(2)}) %collective-permute-start.12) | collective-permute-done | bytes 393248 | tf_op jit(solution)/shard_map/weight_gather/ppermute | solution.py:22
  90.4 3.1 %collective-permute-done.11.refs_8_ = bf16[256,768]{1,0:T(8,128)(2,1)} collective-permute-done((bf16[256,768]{1,0:T(8,128)(2,1)}, bf16[256,768]{1,0:T(8,128)(2,1)}, u32[]{:S(2)}, u32[]{:S(2)}) %collective-permute-start.11) | collective-permute-done | bytes 393248 | tf_op jit(solution)/shard_map/weight_gather/ppermute | solution.py:22
  93.5 0.9 slice.35
  94.5 0.0 copy-start.1
  94.5 0.0 copy-start.7
  94.5 0.9 slice.34
  95.4 0.7 collective-permute-start.15
  96.2 2.2 %collective-permute-start.16 = (bf16[128,768]{1,0:T(8,128)(2,1)S(1)}, bf16[128,768]{1,0:T(8,128)(2,1)S(1)}, u32[]{:S(2)}, u32[]{:S(2)}) collective-permute-start(bf16[128,768]{1,0:T(8,128)(2,1)S(1)} %slice.35), channel_id=1, source_target_pairs={{0,192},{64,0},{128,64},{192,128},{1,193},{65,1},{129,65},{193,129... | collective-permute-start | bytes 589832 | tf_op jit(solution)/shard_map/weight_gather/ppermute | solution.py:22
  98.4 0.0 collective-permute-done.refs_2_
  98.4 2.2 %copy-done = bf16[4096,512]{1,0:T(8,128)(2,1)S(1)} copy-done((bf16[4096,512]{1,0:T(8,128)(2,1)S(1)}, bf16[4096,512]{1,0:T(8,128)(2,1)}, u32[]{:S(2)}) %copy-start) | copy-done | bytes 4194328
  100.6 1.0 copy-done.6
  101.6 0.9 copy-done.10
  102.5 0.9 copy-done.12
  103.4 10.1 %project.1.refs_5_ = f32[6,528,128]{2,1,0:T(8,128)S(1)} custom-call(s32[4]{0:T(128)S(1)} %pad_add_fusion.refs_0_.pos, bf16[4096,512]{1,0:T(8,128)(2,1)S(1)} %copy-done, bf16[128,512]{1,0:T(8,128)(2,1)S(1)} %collective-permute-done.refs_2_, bf16[256,768]{1,0:T(8,128)(2,1)S(1)} %bitcast.19, bf16[512,768]{1,0:T(8,128)(2,1)S(1)} %constant_dynamic-update-slice_fusion.refs_4_, ...), custom_call_target="tpu_custom_call" | custom-call | flops 3321888768 | bytes 12000000 | tf_op jit(solution)/shard_map/project/pallas_call | solution.py:287
  113.6 0.0 copy-start.3
  113.6 0.9 copy-done.3
  114.5 3.9 %states.1 = (f32[64,8,256]{2,1,0:T(8,128)S(1)}, f32[64,8,256]{2,1,0:T(8,128)S(1)}, f32[16,8,256]{2,1,0:T(8,128)S(1)}, f32[16,256]{1,0:T(8,128)S(1)}) custom-call(s32[4]{0:T(128)S(1)} %pad_add_fusion.refs_0_.pos, bf16[4096,512]{1,0:T(8,128)(2,1)S(1)} %copy-done, bf16[128,512]{1,0:T(8,128)(2,1)S(1)} %copy-done.3, ...), custom_call_target="tpu_custom_call" | custom-call | tf_op jit(solution)/shard_map/states/pallas_call | solution.py:305
  118.4 0.7 broadcast_in_dim.3
  119.2 10.0 %all-to-all-start.1 = ((f32[16,16,256]{2,1,0:T(8,128)}), f32[16,16,256]{2,1,0:T(8,128)S(1)}, u32[]{:S(2)}, u32[]{:S(2)}) async-start(f32[16,16,256]{2,1,0:T(8,128)} %broadcast_in_dim.3), calls=%async_computation.1 | async-start | bytes 524288 | tf_op jit(solution)/shard_map/state_exchange/all_to_all | solution.py:326
  129.2 1.9 %local.1 = f32[64,8,256]{2,1,0:T(8,128)S(1)} custom-call(s32[4]{0:T(128)S(1)} %pad_add_fusion.refs_0_.pos, f32[64,8,256]{2,1,0:T(8,128)S(1)} %get-tuple-element.38.product, f32[16,512]{1,0:T(8,128)S(1)} %copy-done.4, f32[16,512]{1,0:T(8,128)S(1)} %copy-done.1, f32[1,512]{1,0:T(1,128)S(1)} %bitcast.20), custom_call_target="tpu_custom_call" | custom-call | flops 20000000 | bytes 1000000 | tf_op jit(solution)/shard_map/local/pallas_call | solution.py:329
  131.0 9.3 %all-to-all-done.1.states = f32[16,16,256]{2,1,0:T(8,128)S(1)} async-done(((f32[16,16,256]{2,1,0:T(8,128)}), f32[16,16,256]{2,1,0:T(8,128)S(1)}, u32[]{:S(2)}, u32[]{:S(2)}) %all-to-all-start.1) | async-done | bytes 262176 | tf_op jit(solution)/shard_map/state_exchange/all_to_all | solution.py:326
  140.3 1.5 finish.1
  141.9 9.1 %all_to_all.16 = bf16[2,256,256]{2,1,0:T(8,128)(2,1)S(1)} all-to-all(bf16[2,256,256]{2,1,0:T(8,128)(2,1)S(1)} %finish.1), channel_id=1, replica_groups=mesh['y'=4,'h'=4,'c'=2,'l'=2,'x'=4] {'c'}, dimensions={0} | all-to-all | bytes 524288 | tf_op jit(solution)/shard_map/result_swap/all_to_all | solution.py:348
  151.0 0.1 copy.14
  151.1 0.8 copy.15
  (27 shorter events, 0.2 us)
Async XLA Ops:
  6.5 78.0 %all-gather.2.cloned.1.call-start = ((), (), s32[]{:S(2)}) async-start(), calls=%async_computation.3 | async-start | bytes 4456448 | tf_op jit(solution)/shard_map/token_gather/all_gather | solution.py:258
  15.6 10.4 %collective-permute-start.4 = (bf16[256,768]{1,0:T(8,128)(2,1)S(1)}, bf16[256,768]{1,0:T(8,128)(2,1)S(1)}, u32[]{:S(2)}, u32[]{:S(2)}) collective-permute-start(bf16[256,768]{1,0:T(8,128)(2,1)S(1)} %bitcast.15), channel_id=1, source_target_pairs={{0,192},{64,0},{128,64},{192,128},{1,193},{65,1},{129,65},{193,129... | collective-permute-start | bytes 1179656 | tf_op jit(solution)/shard_map/weight_gather/ppermute | solution.py:22
  16.7 11.2 %collective-permute-start.3 = (bf16[256,768]{1,0:T(8,128)(2,1)S(1)}, bf16[256,768]{1,0:T(8,128)(2,1)S(1)}, u32[]{:S(2)}, u32[]{:S(2)}) collective-permute-start(bf16[256,768]{1,0:T(8,128)(2,1)S(1)} %bitcast.16), channel_id=1, source_target_pairs={{0,64},{64,128},{128,192},{192,0},{1,65},{65,129},{129,193},{193,1... | collective-permute-start | bytes 1179656 | tf_op jit(solution)/shard_map/weight_gather/ppermute | solution.py:22
  17.2 17.0 %collective-permute-start.2 = (bf16[256,768]{1,0:T(8,128)(2,1)S(1)}, bf16[256,768]{1,0:T(8,128)(2,1)S(1)}, u32[]{:S(2)}, u32[]{:S(2)}) collective-permute-start(bf16[256,768]{1,0:T(8,128)(2,1)S(1)} %bitcast.17), channel_id=1, source_target_pairs={{0,48},{16,0},{32,16},{48,32},{1,49},{17,1},{33,17},{49,33},{2,50}... | collective-permute-start | bytes 1179656 | tf_op jit(solution)/shard_map/weight_gather/ppermute | solution.py:22
  22.7 25.6 %collective-permute-start.1 = (bf16[256,768]{1,0:T(8,128)(2,1)S(1)}, bf16[256,768]{1,0:T(8,128)(2,1)S(1)}, u32[]{:S(2)}, u32[]{:S(2)}) collective-permute-start(bf16[256,768]{1,0:T(8,128)(2,1)S(1)} %bitcast.18), channel_id=1, source_target_pairs={{0,16},{16,32},{32,48},{48,0},{1,17},{17,33},{33,49},{49,1},{2,18}... | collective-permute-start | bytes 1179656 | tf_op jit(solution)/shard_map/weight_gather/ppermute | solution.py:22
  27.9 47.8 %copy-start.5 = (bf16[256,768]{1,0:T(8,128)(2,1)}, bf16[256,768]{1,0:T(8,128)(2,1)S(1)}, u32[]{:S(2)}) copy-start(bf16[256,768]{1,0:T(8,128)(2,1)S(1)} %collective-permute-done.3.refs_6_) | copy-start | bytes 1179652
  48.4 27.3 %collective-permute-start.6 = (bf16[512,768]{1,0:T(8,128)(2,1)S(1)}, bf16[512,768]{1,0:T(8,128)(2,1)S(1)}, u32[]{:S(2)}, u32[]{:S(2)}) collective-permute-start(bf16[512,768]{1,0:T(8,128)(2,1)S(1)} %constant_dynamic-update-slice_fusion.refs_4_), channel_id=1, source_target_pairs={{0,192},{64,0},{128,64},{192,128},{1,193},{65,1},{129,65},{193,129... | collective-permute-start | bytes 2359304 | tf_op jit(solution)/shard_map/weight_gather/ppermute | solution.py:22
  51.3 24.4 %collective-permute-start.5 = (bf16[512,768]{1,0:T(8,128)(2,1)S(1)}, bf16[512,768]{1,0:T(8,128)(2,1)S(1)}, u32[]{:S(2)}, u32[]{:S(2)}) collective-permute-start(bf16[512,768]{1,0:T(8,128)(2,1)S(1)} %constant_dynamic-update-slice_fusion.refs_4_), channel_id=1, source_target_pairs={{0,64},{64,128},{128,192},{192,0},{1,65},{65,129},{129,193},{193,1... | collective-permute-start | bytes 2359304 | tf_op jit(solution)/shard_map/weight_gather/ppermute | solution.py:22
  51.3 16.8 %collective-permute-start.8 = (bf16[128,768]{1,0:T(8,128)(2,1)S(1)}, bf16[128,768]{1,0:T(8,128)(2,1)S(1)}, u32[]{:S(2)}, u32[]{:S(2)}) collective-permute-start(bf16[128,768]{1,0:T(8,128)(2,1)S(1)} %slice.29), channel_id=1, source_target_pairs={{0,192},{64,0},{128,64},{192,128},{1,193},{65,1},{129,65},{193,129... | collective-permute-start | bytes 589832 | tf_op jit(solution)/shard_map/weight_gather/ppermute | solution.py:22
  54.1 17.1 %collective-permute-start.7 = (bf16[128,768]{1,0:T(8,128)(2,1)S(1)}, bf16[128,768]{1,0:T(8,128)(2,1)S(1)}, u32[]{:S(2)}, u32[]{:S(2)}) collective-permute-start(bf16[128,768]{1,0:T(8,128)(2,1)S(1)} %slice.28), channel_id=1, source_target_pairs={{0,64},{64,128},{128,192},{192,0},{1,65},{65,129},{129,193},{193,1... | collective-permute-start | bytes 589832 | tf_op jit(solution)/shard_map/weight_gather/ppermute | solution.py:22
  54.2 17.7 %collective-permute-start.10 = (bf16[128,768]{1,0:T(8,128)(2,1)S(1)}, bf16[128,768]{1,0:T(8,128)(2,1)S(1)}, u32[]{:S(2)}, u32[]{:S(2)}) collective-permute-start(bf16[128,768]{1,0:T(8,128)(2,1)S(1)} %slice.31), channel_id=1, source_target_pairs={{0,48},{16,0},{32,16},{48,32},{1,49},{17,1},{33,17},{49,33},{2,50}... | collective-permute-start | bytes 589832 | tf_op jit(solution)/shard_map/weight_gather/ppermute | solution.py:22
  68.1 0.7 copy-start.9
  68.8 6.9 %collective-permute-start.9 = (bf16[128,768]{1,0:T(8,128)(2,1)S(1)}, bf16[128,768]{1,0:T(8,128)(2,1)S(1)}, u32[]{:S(2)}, u32[]{:S(2)}) collective-permute-start(bf16[128,768]{1,0:T(8,128)(2,1)S(1)} %slice.30), channel_id=1, source_target_pairs={{0,16},{16,32},{32,48},{48,0},{1,17},{17,33},{33,49},{49,1},{2,18}... | collective-permute-start | bytes 589832 | tf_op jit(solution)/shard_map/weight_gather/ppermute | solution.py:22
  71.2 0.7 copy-start.11
  77.2 10.9 %collective-permute-start.14 = (bf16[256,768]{1,0:T(8,128)(2,1)}, bf16[256,768]{1,0:T(8,128)(2,1)}, u32[]{:S(2)}, u32[]{:S(2)}) collective-permute-start(bf16[256,768]{1,0:T(8,128)(2,1)} %slice.33), channel_id=1, source_target_pairs={{0,192},{64,0},{128,64},{192,128},{1,193},{65,1},{129,65},{193,129... | collective-permute-start | bytes 1179656 | tf_op jit(solution)/shard_map/weight_gather/ppermute | solution.py:22
  80.5 8.2 %collective-permute-start.13 = (bf16[256,768]{1,0:T(8,128)(2,1)}, bf16[256,768]{1,0:T(8,128)(2,1)}, u32[]{:S(2)}, u32[]{:S(2)}) collective-permute-start(bf16[256,768]{1,0:T(8,128)(2,1)} %slice.32), channel_id=1, source_target_pairs={{0,64},{64,128},{128,192},{192,0},{1,65},{65,129},{129,193},{193,1... | collective-permute-start | bytes 1179656 | tf_op jit(solution)/shard_map/weight_gather/ppermute | solution.py:22
  81.9 8.5 %collective-permute-start.12 = (bf16[256,768]{1,0:T(8,128)(2,1)}, bf16[256,768]{1,0:T(8,128)(2,1)}, u32[]{:S(2)}, u32[]{:S(2)}) collective-permute-start(bf16[256,768]{1,0:T(8,128)(2,1)} %constant_dynamic-update-slice_fusion.2.refs_5_), channel_id=1, source_target_pairs={{0,192},{64,0},{128,64},{192,128},{1,193},{65,1},{129,65},{193,129... | collective-permute-start | bytes 1179656 | tf_op jit(solution)/shard_map/weight_gather/ppermute | solution.py:22
  84.6 9.0 %collective-permute-start.11 = (bf16[256,768]{1,0:T(8,128)(2,1)}, bf16[256,768]{1,0:T(8,128)(2,1)}, u32[]{:S(2)}, u32[]{:S(2)}) collective-permute-start(bf16[256,768]{1,0:T(8,128)(2,1)} %constant_dynamic-update-slice_fusion.2.refs_5_), channel_id=1, source_target_pairs={{0,64},{64,128},{128,192},{192,0},{1,65},{65,129},{129,193},{193,1... | collective-permute-start | bytes 1179656 | tf_op jit(solution)/shard_map/weight_gather/ppermute | solution.py:22
  85.5 12.9 %collective-permute-start = (bf16[128,512]{1,0:T(8,128)(2,1)S(1)}, bf16[128,512]{1,0:T(8,128)(2,1)S(1)}, u32[]{:S(2)}, u32[]{:S(2)}) collective-permute-start(bf16[128,512]{1,0:T(8,128)(2,1)S(1)} %bitcast.25), channel_id=1, source_target_pairs={{0,16},{16,32},{32,48},{48,64},{64,80},{80,96},{96,112},{112,128},... | collective-permute-start | bytes 393224 | tf_op jit(solution)/shard_map/token_gather/ppermute | solution.py:260
  94.5 19.1 %copy-start.1 = (f32[16,512]{1,0:T(8,128)S(1)}, f32[16,512]{1,0:T(8,128)}, u32[]{:S(2)}) copy-start(f32[16,512]{1,0:T(8,128)} %decay.3) | copy-start | bytes 98308
  94.5 19.1 %copy-start.7 = (f32[3,3,512]{2,1,0:T(4,128)S(1)}, f32[3,3,512]{2,1,0:T(4,128)}, u32[]{:S(2)}) copy-start(f32[3,3,512]{2,1,0:T(4,128)} %refs_6_.1) | copy-start | bytes 55300
  95.4 18.1 %collective-permute-start.15 = (bf16[128,768]{1,0:T(8,128)(2,1)S(1)}, bf16[128,768]{1,0:T(8,128)(2,1)S(1)}, u32[]{:S(2)}, u32[]{:S(2)}) collective-permute-start(bf16[128,768]{1,0:T(8,128)(2,1)S(1)} %slice.34), channel_id=1, source_target_pairs={{0,64},{64,128},{128,192},{192,0},{1,65},{65,129},{129,193},{193,1... | collective-permute-start | bytes 589832 | tf_op jit(solution)/shard_map/weight_gather/ppermute | solution.py:22
  96.2 17.4 %collective-permute-start.16 = (bf16[128,768]{1,0:T(8,128)(2,1)S(1)}, bf16[128,768]{1,0:T(8,128)(2,1)S(1)}, u32[]{:S(2)}, u32[]{:S(2)}) collective-permute-start(bf16[128,768]{1,0:T(8,128)(2,1)S(1)} %slice.35), channel_id=1, source_target_pairs={{0,192},{64,0},{128,64},{192,128},{1,193},{65,1},{129,65},{193,129... | collective-permute-start | bytes 589832 | tf_op jit(solution)/shard_map/weight_gather/ppermute | solution.py:22
  98.4 2.2 %copy-start = (bf16[4096,512]{1,0:T(8,128)(2,1)S(1)}, bf16[4096,512]{1,0:T(8,128)(2,1)}, u32[]{:S(2)}) copy-start(bf16[4096,512]{1,0:T(8,128)(2,1)} %all-gather.2.cloned.1.call-done.refs_1_) | copy-start | bytes 12582916
  100.6 1.0 copy-start.6
  101.6 0.9 copy-start.10
  102.5 0.9 copy-start.12
  103.4 10.1 %copy-start.2 = (bf16[128,512]{1,0:T(8,128)(2,1)}, bf16[128,512]{1,0:T(8,128)(2,1)S(1)}, u32[]{:S(2)}) copy-start(bf16[128,512]{1,0:T(8,128)(2,1)S(1)} %collective-permute-done.refs_2_) | copy-start | bytes 393220
  103.4 25.7 %copy-start.4 = (f32[16,512]{1,0:T(8,128)S(1)}, f32[16,512]{1,0:T(8,128)}, u32[]{:S(2)}) copy-start(f32[16,512]{1,0:T(8,128)} %gain.3) | copy-start | bytes 98308
  103.4 25.7 %copy-start.8 = (f32[512]{0:T(512)S(1)}, f32[512]{0:T(512)}, u32[]{:S(2)}) copy-start(f32[512]{0:T(512)} %param.11) | copy-start | bytes 6148
  113.6 0.9 copy-start.3
  119.2 21.2 %all-to-all-start.1 = ((f32[16,16,256]{2,1,0:T(8,128)}), f32[16,16,256]{2,1,0:T(8,128)S(1)}, u32[]{:S(2)}, u32[]{:S(2)}) async-start(f32[16,16,256]{2,1,0:T(8,128)} %broadcast_in_dim.3), calls=%async_computation.1 | async-start | bytes 524288 | tf_op jit(solution)/shard_map/state_exchange/all_to_all | solution.py:326
Sparse Core Ops, SparseCore 0:
  9.2 61.9 all-gather.1

commit v3 on v2

--- a/solution.py
+++ b/solution.py
@@ -48,7 +48,7 @@
 
     copies = []
     for ch in range(8):
-        lanes = pl.ds(ch * (depth // 8), depth // 8)
+        lanes = pl.ds((ch % 2 * 4 + ch // 2) * (depth // 8), depth // 8)
         copies.append((halo.at[pl.ds(ch * HALO, HALO), :], tokv.at[pl.ds(0, HALO), lanes]))
         for core in range(2):
             at = (core * 8 + ch) * rows
@@ -115,6 +115,7 @@
     half = k // 2
     at = place(sizes, pos, 2, 2)
     ch = lax.div(at, depth // 8)
+    ch = lax.rem(ch, 4) * 2 + lax.div(ch, 4)
     lanes = pl.ds(pl.multiple_of(lax.rem(at, depth // 8), k), k)
     copies = [
         (halo.at[pl.ds(pl.multiple_of(ch * HALO, HALO), HALO), lanes], tokv.at[pl.ds(0, HALO), :]),
@@ -254,16 +255,22 @@
     pos = jnp.stack([y * 4 + h, y, h, c]).astype(jnp.int32)
 
     tie = lax.optimization_barrier
-    with jax.named_scope("token_gather"):
-        tok = lax.all_gather(tokens, ("c", *CH), axis=0, tiled=True)
-        tail = tok.reshape(2, 8, rows, group)[1, :, rows - HALO :].reshape(8 * HALO, group)
-        halo = lax.ppermute(tail, ("y", "h"), [(i, i + 1) for i in range(15)])
-
     with jax.named_scope("weight_gather"):
         halves = w_in.reshape(k, 3, 2, width).transpose(2, 0, 1, 3).reshape(2, k, 3 * width)
         own = lax.all_to_all(halves, "c", 0, 0, tiled=True).reshape(2 * k, 3 * width)
         beside, far = both_ways(own, "h"), both_ways(own, "y")
-        beside, far = tie((beside, far))
+    with jax.named_scope("token_swap"):
+        other = lax.ppermute(tokens, "l", [(0, 1), (1, 0)])
+    beside, far, other = tie((beside, far, other))
+    with jax.named_scope("token_gather"):
+        here = lax.axis_index("l") == 0
+        wide = jnp.stack([jnp.where(here, tokens, other), jnp.where(here, other, tokens)])
+        tok = lax.all_gather(wide, ("c", "x"), axis=0)
+        tok = tok.reshape(2, 4, 2, rows, group)
+        tail = tok[1, :, :, rows - HALO :].reshape(8 * HALO, group)
+        tok = tok.reshape(16 * rows, group)
+        halo = lax.ppermute(tail, ("y", "h"), [(i, i + 1) for i in range(15)])
+    with jax.named_scope("weight_rings"):
         pair = jnp.concatenate(beside, 0)
         far_pair, farther = both_ways(pair, "y"), onward(*far, "y")
         opposite = onward(*beside, "h")

time: 159 us -> 162 us (1.019); the launches traced: 159 us -> 160 us
  waiting for transfers between devices: 61.1 us -> 56.5 us
  blocking collectives: 16 us -> 20.2 us
  starting transfers between devices: 34.3 us -> 30.9 us
  local copies, waits for them, and re-layouts: 16.3 us -> 18.9 us
  other arithmetic: 0.08 us -> 2.12 us
    ppermute x16, waiting for transfers between devices: 51 us -> 26 us  [shifted(): return lax.ppermute(array, axis, [(i, (i + step) % n) for i in range(n)])]
    ppermute x0 -> x1, waiting for transfers between devices: none -> 21.9 us  [body(): other = lax.ppermute(tokens, 'l', [(0, 1), (1, 0)])]
    all_to_all x1, starting transfers between devices: 9.98 us -> 3.77 us  [body(): lax.all_to_all(jnp.broadcast_to(state, (16, *state.shape)), ('y', 'h'), 0...]
    all_to_all x1, blocking collectives: 9.12 us -> 13.3 us  [body(): both = lax.all_to_all(out, 'c', 0, 0, tiled=True)]
    ppermute x16, starting transfers between devices: 21.8 us -> 24.8 us  [shifted(): return lax.ppermute(array, axis, [(i, (i + step) % n) for i in range(n)])]
    another operation x0 -> x2, other arithmetic: none -> 2.04 us  [body(): jnp.stack([jnp.where(here, tokens, other), jnp.where(here, other, tokens)])]
    slice x8, local copies, waits for them, and re-layouts: 3.51 us -> 5.33 us  [onward(): return (shifted(behind[:half], axis, 1), shifted(ahead[half:], axis, -1))]
    unnamed x29 -> x33, local copies, waits for them, and re-layouts: 9.23 us -> 9.31 us
  transfers between devices with their start and end apart: 19 -> 20, of which waited for: 11 -> 8; matrix products, arithmetic and copies ran while one was open for 5% -> 5% of each run, Pallas kernels for 8% -> 8%
where the time goes in v3:
time: 162 us; the launch traced here: 160 us
  waiting for transfers between devices  56.5 us (35%)
  starting transfers between devices  30.9 us (19%)
  blocking collectives  20.2 us (12%)
  local copies, waits for them, and re-layouts  18.9 us (12%)
  Pallas kernels  17.4 us (11%)
  between operations  13.7 us (8%)
  other arithmetic  2.12 us (1%)
    ppermute x16, waiting for transfers between devices, shifted(): return lax.ppermute(array, axis, [(i, (i + step) % n) for i in range(n)])  26 us
    ppermute x16, starting transfers between devices, shifted(): return lax.ppermute(array, axis, [(i, (i + step) % n) for i in range(n)])  24.8 us
    ppermute x1, waiting for transfers between devices, body(): other = lax.ppermute(tokens, 'l', [(0, 1), (1, 0)])  21.9 us
    all_to_all x1, blocking collectives, body(): both = lax.all_to_all(out, 'c', 0, 0, tiled=True)  13.3 us
    pallas_call x1, Pallas kernels, body(): pl.pallas_call(functools.partial(project_kernel, sizes), out_shape=jax.Sh...  10.1 us
    unnamed x33, local copies, waits for them, and re-layouts  9.31 us
    all_to_all x1, waiting for transfers between devices, body(): lax.all_to_all(jnp.broadcast_to(state, (16, *state.shape)), ('y', 'h'), 0...  8.59 us
    all_to_all x1, blocking collectives, body(): lax.all_to_all(halves, 'c', 0, 0, tiled=True).reshape(2 * k, 3 * width)  6.92 us
  transfers between devices with their start and end apart: 20, of which 8 were waited for; matrix products, arithmetic and copies ran while one was open for 5% of the time, Pallas kernels for 8%

profile of v3, /device:TPU:1, one launch (start us, length us, event | category | flops | bytes accessed | tf_op | source)
XLA Modules:
  0.0 159.7 jit_solution(10133257974989297039)
XLA Ops:
  6.5 1.2 copy.16
  7.8 6.9 %all_to_all.15 = bf16[2,128,768]{1,2,0:T(8,128)(2,1)S(1)} all-to-all(bf16[2,128,768]{1,2,0:T(8,128)(2,1)S(1)} %bitcast.28), channel_id=1, replica_groups=mesh['y'=4,'h'=4,'c'=2,'l'=2,'x'=4] {'c'}, dimensions={0} | all-to-all | bytes 786432 | tf_op jit(solution)/shard_map/weight_gather/all_to_all | solution.py:260
  14.7 0.2 copy.18
  14.9 1.1 collective-permute-start.3
  16.0 0.5 collective-permute-start.2
  16.4 5.6 %collective-permute-start.1 = (bf16[256,768]{1,0:T(8,128)(2,1)S(1)}, bf16[256,768]{1,0:T(8,128)(2,1)S(1)}, u32[]{:S(2)}, u32[]{:S(2)}) collective-permute-start(bf16[256,768]{1,0:T(8,128)(2,1)S(1)} %bitcast.24), channel_id=1, source_target_pairs={{0,48},{16,0},{32,16},{48,32},{1,49},{17,1},{33,17},{49,33},{2,50}... | collective-permute-start | bytes 1179656 | tf_op jit(solution)/shard_map/weight_gather/ppermute | solution.py:22
  22.0 0.7 collective-permute-start.4
  22.7 21.9 %collective-permute-done.4 = bf16[256,512]{1,0:T(8,128)(2,1)S(1)} collective-permute-done((bf16[256,512]{1,0:T(8,128)(2,1)}, bf16[256,512]{1,0:T(8,128)(2,1)S(1)}, u32[]{:S(2)}, u32[]{:S(2)}) %collective-permute-start.4) | collective-permute-done | bytes 262176 | tf_op jit(solution)/shard_map/token_swap/ppermute | solution.py:263
  44.6 0.0 collective-permute-done.3.refs_9_
  44.6 0.0 collective-permute-done.2.refs_6_
  44.6 0.0 collective-permute-done.1
  44.6 0.0 collective-permute-done
  44.7 1.2 select_bitcast_fusion.1
  45.9 0.8 pad_maximum_fusion
  46.7 0.0 all-gather.3.cloned.1.call-update
  46.8 2.6 %collective-permute-start.7 = (bf16[512,768]{1,0:T(8,128)(2,1)S(1)}, bf16[512,768]{1,0:T(8,128)(2,1)S(1)}, u32[]{:S(2)}, u32[]{:S(2)}) collective-permute-start(bf16[512,768]{1,0:T(8,128)(2,1)S(1)} %constant_dynamic-update-slice_fusion.refs_4_), channel_id=1, source_target_pairs={{0,192},{64,0},{128,64},{192,128},{1,193},{65,1},{129,65},{193,129... | collective-permute-start | bytes 2359304 | tf_op jit(solution)/shard_map/weight_rings/ppermute | solution.py:22
  49.4 2.8 %collective-permute-start.9 = (bf16[128,768]{1,0:T(8,128)(2,1)S(1)}, bf16[128,768]{1,0:T(8,128)(2,1)S(1)}, u32[]{:S(2)}, u32[]{:S(2)}) collective-permute-start(bf16[128,768]{1,0:T(8,128)(2,1)S(1)} %slice.29), channel_id=1, source_target_pairs={{0,192},{64,0},{128,64},{192,128},{1,193},{65,1},{129,65},{193,129... | collective-permute-start | bytes 589832 | tf_op jit(solution)/shard_map/weight_rings/ppermute | solution.py:22
  52.2 0.9 slice.30
  53.1 0.9 slice.31
  54.1 0.1 collective-permute-start.8
  54.2 2.4 %collective-permute-start.11 = (bf16[128,768]{1,0:T(8,128)(2,1)S(1)}, bf16[128,768]{1,0:T(8,128)(2,1)S(1)}, u32[]{:S(2)}, u32[]{:S(2)}) collective-permute-start(bf16[128,768]{1,0:T(8,128)(2,1)S(1)} %slice.31), channel_id=1, source_target_pairs={{0,48},{16,0},{32,16},{48,32},{1,49},{17,1},{33,17},{49,33},{2,50}... | collective-permute-start | bytes 589832 | tf_op jit(solution)/shard_map/weight_rings/ppermute | solution.py:22
  56.6 12.8 %collective-permute-done.9.refs_13_ = bf16[128,768]{1,0:T(8,128)(2,1)S(1)} collective-permute-done((bf16[128,768]{1,0:T(8,128)(2,1)S(1)}, bf16[128,768]{1,0:T(8,128)(2,1)S(1)}, u32[]{:S(2)}, u32[]{:S(2)}) %collective-permute-start.9) | collective-permute-done | bytes 196640 | tf_op jit(solution)/shard_map/weight_rings/ppermute | solution.py:22
  69.4 0.7 copy-done.9
  70.1 0.9 collective-permute-start.10
  71.0 1.6 %collective-permute-done.8.refs_12_ = bf16[128,768]{1,0:T(8,128)(2,1)S(1)} collective-permute-done((bf16[128,768]{1,0:T(8,128)(2,1)S(1)}, bf16[128,768]{1,0:T(8,128)(2,1)S(1)}, u32[]{:S(2)}, u32[]{:S(2)}) %collective-permute-start.8) | collective-permute-done | bytes 196640 | tf_op jit(solution)/shard_map/weight_rings/ppermute | solution.py:22
  72.7 0.7 copy-done.11
  73.3 0.0 collective-permute-done.11
  73.3 3.6 %collective-permute-done.10 = bf16[128,768]{1,0:T(8,128)(2,1)S(1)} collective-permute-done((bf16[128,768]{1,0:T(8,128)(2,1)S(1)}, bf16[128,768]{1,0:T(8,128)(2,1)S(1)}, u32[]{:S(2)}, u32[]{:S(2)}) %collective-permute-start.10) | collective-permute-done | bytes 196640 | tf_op jit(solution)/shard_map/weight_rings/ppermute | solution.py:22
  76.9 0.0 collective-permute-done.6.refs_7_
  76.9 0.8 slice.32
  77.7 0.8 slice.33
  78.5 3.5 %collective-permute-start.15 = (bf16[256,768]{1,0:T(8,128)(2,1)}, bf16[256,768]{1,0:T(8,128)(2,1)}, u32[]{:S(2)}, u32[]{:S(2)}) collective-permute-start(bf16[256,768]{1,0:T(8,128)(2,1)} %slice.33), channel_id=1, source_target_pairs={{0,192},{64,0},{128,64},{192,128},{1,193},{65,1},{129,65},{193,129... | collective-permute-start | bytes 1179656 | tf_op jit(solution)/shard_map/weight_rings/ppermute | solution.py:22
  82.0 0.0 collective-permute-start.14
  82.0 0.7 constant_dynamic-update-slice_fusion.3
  82.7 0.7 constant_dynamic-update-slice_fusion.2.refs_5_
  83.4 2.7 %collective-permute-start.13 = (bf16[256,768]{1,0:T(8,128)(2,1)}, bf16[256,768]{1,0:T(8,128)(2,1)}, u32[]{:S(2)}, u32[]{:S(2)}) collective-permute-start(bf16[256,768]{1,0:T(8,128)(2,1)} %constant_dynamic-update-slice_fusion.2.refs_5_), channel_id=1, source_target_pairs={{0,192},{64,0},{128,64},{192,128},{1,193},{65,1},{129,65},{193,129... | collective-permute-start | bytes 1179656 | tf_op jit(solution)/shard_map/weight_rings/ppermute | solution.py:22
  86.1 0.0 collective-permute-start.12
  86.1 1.6 slice.36
  87.7 1.5 collective-permute-start.5
  89.2 0.1 pad_add_fusion.refs_0_.pos
  89.3 0.9 collective-permute-done.14.refs_14_
  90.1 4.4 %collective-permute-done.13.refs_11_ = bf16[256,768]{1,0:T(8,128)(2,1)} collective-permute-done((bf16[256,768]{1,0:T(8,128)(2,1)}, bf16[256,768]{1,0:T(8,128)(2,1)}, u32[]{:S(2)}, u32[]{:S(2)}) %collective-permute-start.13) | collective-permute-done | bytes 393248 | tf_op jit(solution)/shard_map/weight_rings/ppermute | solution.py:22
  94.5 2.7 %collective-permute-done.12.refs_8_ = bf16[256,768]{1,0:T(8,128)(2,1)} collective-permute-done((bf16[256,768]{1,0:T(8,128)(2,1)}, bf16[256,768]{1,0:T(8,128)(2,1)}, u32[]{:S(2)}, u32[]{:S(2)}) %collective-permute-start.12) | collective-permute-done | bytes 393248 | tf_op jit(solution)/shard_map/weight_rings/ppermute | solution.py:22
  97.2 0.9 slice.35
  98.2 0.9 slice.34
  99.1 0.6 collective-permute-start.16
  99.7 2.2 %collective-permute-start.17 = (bf16[128,768]{1,0:T(8,128)(2,1)S(1)}, bf16[128,768]{1,0:T(8,128)(2,1)S(1)}, u32[]{:S(2)}, u32[]{:S(2)}) collective-permute-start(bf16[128,768]{1,0:T(8,128)(2,1)S(1)} %slice.35), channel_id=1, source_target_pairs={{0,192},{64,0},{128,64},{192,128},{1,193},{65,1},{129,65},{193,129... | collective-permute-start | bytes 589832 | tf_op jit(solution)/shard_map/weight_rings/ppermute | solution.py:22
  101.9 0.0 collective-permute-done.5.refs_2_
  101.9 2.2 %copy-done = bf16[16,256,512]{2,1,0:T(8,128)(2,1)S(1)} copy-done((bf16[16,256,512]{2,1,0:T(8,128)(2,1)S(1)}, bf16[16,256,512]{2,1,0:T(8,128)(2,1)}, u32[]{:S(2)}) %copy-start) | copy-done | bytes 4194328
  104.1 1.0 copy-done.6
  105.1 0.9 copy-done.10
  106.1 0.9 copy-done.12
  107.0 10.1 %project.1.refs_5_ = f32[6,528,128]{2,1,0:T(8,128)S(1)} custom-call(s32[4]{0:T(128)S(1)} %pad_add_fusion.refs_0_.pos, bf16[4096,512]{1,0:T(8,128)(2,1)S(1)} %bitcast.20, bf16[128,512]{1,0:T(8,128)(2,1)S(1)} %collective-permute-done.5.refs_2_, bf16[256,768]{1,0:T(8,128)(2,1)S(1)} %bitcast.26, bf16[512,768]{1,0:T(8,128)(2,1)S(1)} %constant_dynamic-update-slice_fusion.refs_4_, ...), custom_call_target="tpu_custom_call" | custom-call | flops 3321888768 | bytes 12000000 | tf_op jit(solution)/shard_map/project/pallas_call | solution.py:294
  117.2 0.0 collective-permute-done.17.refs_4_
  117.2 0.9 copy-done.3
  118.1 3.9 %states.1 = (f32[64,8,256]{2,1,0:T(8,128)S(1)}, f32[64,8,256]{2,1,0:T(8,128)S(1)}, f32[16,8,256]{2,1,0:T(8,128)S(1)}, f32[16,256]{1,0:T(8,128)S(1)}) custom-call(s32[4]{0:T(128)S(1)} %pad_add_fusion.refs_0_.pos, bf16[4096,512]{1,0:T(8,128)(2,1)S(1)} %bitcast.21, bf16[128,512]{1,0:T(8,128)(2,1)S(1)} %copy-done.3, ...), custom_call_target="tpu_custom_call" | custom-call | tf_op jit(solution)/shard_map/states/pallas_call | solution.py:312
  122.0 0.7 broadcast_in_dim.3
  122.7 3.8 %all-to-all-start.1 = ((f32[16,16,256]{2,1,0:T(8,128)}), f32[16,16,256]{2,1,0:T(8,128)S(1)}, u32[]{:S(2)}, u32[]{:S(2)}) async-start(f32[16,16,256]{2,1,0:T(8,128)} %broadcast_in_dim.3), calls=%async_computation.1 | async-start | bytes 524288 | tf_op jit(solution)/shard_map/state_exchange/all_to_all | solution.py:333
  126.5 1.9 %local.1 = f32[64,8,256]{2,1,0:T(8,128)S(1)} custom-call(s32[4]{0:T(128)S(1)} %pad_add_fusion.refs_0_.pos, f32[64,8,256]{2,1,0:T(8,128)S(1)} %get-tuple-element.40.product, f32[16,512]{1,0:T(8,128)S(1)} %copy-done.4, f32[16,512]{1,0:T(8,128)S(1)} %copy-done.1, f32[1,512]{1,0:T(1,128)S(1)} %bitcast.27), custom_call_target="tpu_custom_call" | custom-call | flops 20000000 | bytes 1000000 | tf_op jit(solution)/shard_map/local/pallas_call | solution.py:336
  128.4 8.6 %all-to-all-done.1.states = f32[16,16,256]{2,1,0:T(8,128)S(1)} async-done(((f32[16,16,256]{2,1,0:T(8,128)}), f32[16,16,256]{2,1,0:T(8,128)S(1)}, u32[]{:S(2)}, u32[]{:S(2)}) %all-to-all-start.1) | async-done | bytes 262176 | tf_op jit(solution)/shard_map/state_exchange/all_to_all | solution.py:333
  137.0 1.5 finish.1
  138.5 13.3 %all_to_all.16 = bf16[2,256,256]{2,1,0:T(8,128)(2,1)S(1)} all-to-all(bf16[2,256,256]{2,1,0:T(8,128)(2,1)S(1)} %finish.1), channel_id=1, replica_groups=mesh['y'=4,'h'=4,'c'=2,'l'=2,'x'=4] {'c'}, dimensions={0} | all-to-all | bytes 524288 | tf_op jit(solution)/shard_map/result_swap/all_to_all | solution.py:355
  151.9 0.1 copy.19
  152.0 0.8 copy.20
  (35 shorter events, 0.2 us)
Async XLA Ops:
  6.5 79.5 %all-gather.3.cloned.1.call-start = ((), (), s32[]{:S(2)}) async-start(), calls=%async_computation.3 | async-start | bytes 4718592 | tf_op jit(solution)/shard_map/token_gather/all_gather | solution.py:268
  14.9 29.7 %collective-permute-start.3 = (bf16[256,768]{1,0:T(8,128)(2,1)S(1)}, bf16[256,768]{1,0:T(8,128)(2,1)S(1)}, u32[]{:S(2)}, u32[]{:S(2)}) collective-permute-start(bf16[256,768]{1,0:T(8,128)(2,1)S(1)} %bitcast.22), channel_id=1, source_target_pairs={{0,192},{64,0},{128,64},{192,128},{1,193},{65,1},{129,65},{193,129... | collective-permute-start | bytes 1179656 | tf_op jit(solution)/shard_map/weight_gather/ppermute | solution.py:22
  16.0 28.6 %collective-permute-start.2 = (bf16[256,768]{1,0:T(8,128)(2,1)S(1)}, bf16[256,768]{1,0:T(8,128)(2,1)S(1)}, u32[]{:S(2)}, u32[]{:S(2)}) collective-permute-start(bf16[256,768]{1,0:T(8,128)(2,1)S(1)} %bitcast.23), channel_id=1, source_target_pairs={{0,64},{64,128},{128,192},{192,0},{1,65},{65,129},{129,193},{193,1... | collective-permute-start | bytes 1179656 | tf_op jit(solution)/shard_map/weight_gather/ppermute | solution.py:22
  16.4 28.2 %collective-permute-start.1 = (bf16[256,768]{1,0:T(8,128)(2,1)S(1)}, bf16[256,768]{1,0:T(8,128)(2,1)S(1)}, u32[]{:S(2)}, u32[]{:S(2)}) collective-permute-start(bf16[256,768]{1,0:T(8,128)(2,1)S(1)} %bitcast.24), channel_id=1, source_target_pairs={{0,48},{16,0},{32,16},{48,32},{1,49},{17,1},{33,17},{49,33},{2,50}... | collective-permute-start | bytes 1179656 | tf_op jit(solution)/shard_map/weight_gather/ppermute | solution.py:22
  22.0 22.7 %collective-permute-start = (bf16[256,768]{1,0:T(8,128)(2,1)S(1)}, bf16[256,768]{1,0:T(8,128)(2,1)S(1)}, u32[]{:S(2)}, u32[]{:S(2)}) collective-permute-start(bf16[256,768]{1,0:T(8,128)(2,1)S(1)} %bitcast.25), channel_id=1, source_target_pairs={{0,16},{16,32},{32,48},{48,0},{1,17},{17,33},{33,49},{49,1},{2,18}... | collective-permute-start | bytes 1179656 | tf_op jit(solution)/shard_map/weight_gather/ppermute | solution.py:22
  22.0 22.6 %collective-permute-start.4 = (bf16[256,512]{1,0:T(8,128)(2,1)}, bf16[256,512]{1,0:T(8,128)(2,1)S(1)}, u32[]{:S(2)}, u32[]{:S(2)}) collective-permute-start(bf16[256,512]{1,0:T(8,128)(2,1)} %param.6), channel_id=1, source_target_pairs={{0,4},{4,0},{1,5},{5,1},{2,6},{6,2},{3,7},{7,3},{8,12},{12,8},{9,1... | collective-permute-start | bytes 786440 | tf_op jit(solution)/shard_map/token_swap/ppermute | solution.py:263
  44.6 43.0 %copy-start.5 = (bf16[256,768]{1,0:T(8,128)(2,1)}, bf16[256,768]{1,0:T(8,128)(2,1)S(1)}, u32[]{:S(2)}) copy-start(bf16[256,768]{1,0:T(8,128)(2,1)S(1)} %collective-permute-done.2.refs_6_) | copy-start | bytes 1179652
  44.6 2.1 %copy-start.13 = (bf16[256,768]{1,0:T(8,128)(2,1)}, bf16[256,768]{1,0:T(8,128)(2,1)S(1)}, u32[]{:S(2)}) copy-start(bf16[256,768]{1,0:T(8,128)(2,1)S(1)} %collective-permute-done.1) | copy-start | bytes 1179652
  44.7 2.1 %copy-start.14 = (bf16[256,768]{1,0:T(8,128)(2,1)}, bf16[256,768]{1,0:T(8,128)(2,1)S(1)}, u32[]{:S(2)}) copy-start(bf16[256,768]{1,0:T(8,128)(2,1)S(1)} %collective-permute-done) | copy-start | bytes 1179652
  46.8 30.1 %collective-permute-start.7 = (bf16[512,768]{1,0:T(8,128)(2,1)S(1)}, bf16[512,768]{1,0:T(8,128)(2,1)S(1)}, u32[]{:S(2)}, u32[]{:S(2)}) collective-permute-start(bf16[512,768]{1,0:T(8,128)(2,1)S(1)} %constant_dynamic-update-slice_fusion.refs_4_), channel_id=1, source_target_pairs={{0,192},{64,0},{128,64},{192,128},{1,193},{65,1},{129,65},{193,129... | collective-permute-start | bytes 2359304 | tf_op jit(solution)/shard_map/weight_rings/ppermute | solution.py:22
  49.4 27.5 %collective-permute-start.6 = (bf16[512,768]{1,0:T(8,128)(2,1)S(1)}, bf16[512,768]{1,0:T(8,128)(2,1)S(1)}, u32[]{:S(2)}, u32[]{:S(2)}) collective-permute-start(bf16[512,768]{1,0:T(8,128)(2,1)S(1)} %constant_dynamic-update-slice_fusion.refs_4_), channel_id=1, source_target_pairs={{0,64},{64,128},{128,192},{192,0},{1,65},{65,129},{129,193},{193,1... | collective-permute-start | bytes 2359304 | tf_op jit(solution)/shard_map/weight_rings/ppermute | solution.py:22
  49.4 20.0 %collective-permute-start.9 = (bf16[128,768]{1,0:T(8,128)(2,1)S(1)}, bf16[128,768]{1,0:T(8,128)(2,1)S(1)}, u32[]{:S(2)}, u32[]{:S(2)}) collective-permute-start(bf16[128,768]{1,0:T(8,128)(2,1)S(1)} %slice.29), channel_id=1, source_target_pairs={{0,192},{64,0},{128,64},{192,128},{1,193},{65,1},{129,65},{193,129... | collective-permute-start | bytes 589832 | tf_op jit(solution)/shard_map/weight_rings/ppermute | solution.py:22
  54.1 18.6 %collective-permute-start.8 = (bf16[128,768]{1,0:T(8,128)(2,1)S(1)}, bf16[128,768]{1,0:T(8,128)(2,1)S(1)}, u32[]{:S(2)}, u32[]{:S(2)}) collective-permute-start(bf16[128,768]{1,0:T(8,128)(2,1)S(1)} %slice.28), channel_id=1, source_target_pairs={{0,64},{64,128},{128,192},{192,0},{1,65},{65,129},{129,193},{193,1... | collective-permute-start | bytes 589832 | tf_op jit(solution)/shard_map/weight_rings/ppermute | solution.py:22
  54.2 19.1 %collective-permute-start.11 = (bf16[128,768]{1,0:T(8,128)(2,1)S(1)}, bf16[128,768]{1,0:T(8,128)(2,1)S(1)}, u32[]{:S(2)}, u32[]{:S(2)}) collective-permute-start(bf16[128,768]{1,0:T(8,128)(2,1)S(1)} %slice.31), channel_id=1, source_target_pairs={{0,48},{16,0},{32,16},{48,32},{1,49},{17,1},{33,17},{49,33},{2,50}... | collective-permute-start | bytes 589832 | tf_op jit(solution)/shard_map/weight_rings/ppermute | solution.py:22
  69.4 0.7 copy-start.9
  70.1 6.8 %collective-permute-start.10 = (bf16[128,768]{1,0:T(8,128)(2,1)S(1)}, bf16[128,768]{1,0:T(8,128)(2,1)S(1)}, u32[]{:S(2)}, u32[]{:S(2)}) collective-permute-start(bf16[128,768]{1,0:T(8,128)(2,1)S(1)} %slice.30), channel_id=1, source_target_pairs={{0,16},{16,32},{32,48},{48,0},{1,17},{17,33},{33,49},{49,1},{2,18}... | collective-permute-start | bytes 589832 | tf_op jit(solution)/shard_map/weight_rings/ppermute | solution.py:22
  72.7 0.7 copy-start.11
  78.5 10.8 %collective-permute-start.15 = (bf16[256,768]{1,0:T(8,128)(2,1)}, bf16[256,768]{1,0:T(8,128)(2,1)}, u32[]{:S(2)}, u32[]{:S(2)}) collective-permute-start(bf16[256,768]{1,0:T(8,128)(2,1)} %slice.33), channel_id=1, source_target_pairs={{0,192},{64,0},{128,64},{192,128},{1,193},{65,1},{129,65},{193,129... | collective-permute-start | bytes 1179656 | tf_op jit(solution)/shard_map/weight_rings/ppermute | solution.py:22
  82.0 8.2 %collective-permute-start.14 = (bf16[256,768]{1,0:T(8,128)(2,1)}, bf16[256,768]{1,0:T(8,128)(2,1)}, u32[]{:S(2)}, u32[]{:S(2)}) collective-permute-start(bf16[256,768]{1,0:T(8,128)(2,1)} %slice.32), channel_id=1, source_target_pairs={{0,64},{64,128},{128,192},{192,0},{1,65},{65,129},{129,193},{193,1... | collective-permute-start | bytes 1179656 | tf_op jit(solution)/shard_map/weight_rings/ppermute | solution.py:22
  83.4 11.1 %collective-permute-start.13 = (bf16[256,768]{1,0:T(8,128)(2,1)}, bf16[256,768]{1,0:T(8,128)(2,1)}, u32[]{:S(2)}, u32[]{:S(2)}) collective-permute-start(bf16[256,768]{1,0:T(8,128)(2,1)} %constant_dynamic-update-slice_fusion.2.refs_5_), channel_id=1, source_target_pairs={{0,192},{64,0},{128,64},{192,128},{1,193},{65,1},{129,65},{193,129... | collective-permute-start | bytes 1179656 | tf_op jit(solution)/shard_map/weight_rings/ppermute | solution.py:22
  86.1 11.2 %collective-permute-start.12 = (bf16[256,768]{1,0:T(8,128)(2,1)}, bf16[256,768]{1,0:T(8,128)(2,1)}, u32[]{:S(2)}, u32[]{:S(2)}) collective-permute-start(bf16[256,768]{1,0:T(8,128)(2,1)} %constant_dynamic-update-slice_fusion.2.refs_5_), channel_id=1, source_target_pairs={{0,64},{64,128},{128,192},{192,0},{1,65},{65,129},{129,193},{193,1... | collective-permute-start | bytes 1179656 | tf_op jit(solution)/shard_map/weight_rings/ppermute | solution.py:22
  87.7 14.2 %collective-permute-start.5 = (bf16[128,512]{1,0:T(8,128)(2,1)}, bf16[128,512]{1,0:T(8,128)(2,1)S(1)}, u32[]{:S(2)}, u32[]{:S(2)}) collective-permute-start(bf16[128,512]{1,0:T(8,128)(2,1)} %bitcast.12), channel_id=1, source_target_pairs={{0,16},{16,32},{32,48},{48,64},{64,80},{80,96},{96,112},{112,128},... | collective-permute-start | bytes 393224 | tf_op jit(solution)/shard_map/token_gather/ppermute | solution.py:272
  99.1 18.0 %collective-permute-start.16 = (bf16[128,768]{1,0:T(8,128)(2,1)S(1)}, bf16[128,768]{1,0:T(8,128)(2,1)S(1)}, u32[]{:S(2)}, u32[]{:S(2)}) collective-permute-start(bf16[128,768]{1,0:T(8,128)(2,1)S(1)} %slice.34), channel_id=1, source_target_pairs={{0,64},{64,128},{128,192},{192,0},{1,65},{65,129},{129,193},{193,1... | collective-permute-start | bytes 589832 | tf_op jit(solution)/shard_map/weight_rings/ppermute | solution.py:22
  99.7 17.5 %collective-permute-start.17 = (bf16[128,768]{1,0:T(8,128)(2,1)S(1)}, bf16[128,768]{1,0:T(8,128)(2,1)S(1)}, u32[]{:S(2)}, u32[]{:S(2)}) collective-permute-start(bf16[128,768]{1,0:T(8,128)(2,1)S(1)} %slice.35), channel_id=1, source_target_pairs={{0,192},{64,0},{128,64},{192,128},{1,193},{65,1},{129,65},{193,129... | collective-permute-start | bytes 589832 | tf_op jit(solution)/shard_map/weight_rings/ppermute | solution.py:22
  101.9 15.2 %copy-start.2 = (bf16[128,512]{1,0:T(8,128)(2,1)}, bf16[128,512]{1,0:T(8,128)(2,1)S(1)}, u32[]{:S(2)}) copy-start(bf16[128,512]{1,0:T(8,128)(2,1)S(1)} %collective-permute-done.5.refs_2_) | copy-start | bytes 393220
  101.9 2.2 %copy-start = (bf16[16,256,512]{2,1,0:T(8,128)(2,1)S(1)}, bf16[16,256,512]{2,1,0:T(8,128)(2,1)}, u32[]{:S(2)}) copy-start(bf16[16,256,512]{2,1,0:T(8,128)(2,1)} %all-gather.3.cloned.1.call-done) | copy-start | bytes 12582916
  104.1 1.0 copy-start.6
  105.1 0.9 copy-start.10
  106.0 0.9 copy-start.12
  107.0 10.2 %copy-start.1 = (f32[16,512]{1,0:T(8,128)S(1)}, f32[16,512]{1,0:T(8,128)}, u32[]{:S(2)}) copy-start(f32[16,512]{1,0:T(8,128)} %decay.3) | copy-start | bytes 98308
  107.0 10.2 %copy-start.7 = (f32[3,3,512]{2,1,0:T(4,128)S(1)}, f32[3,3,512]{2,1,0:T(4,128)}, u32[]{:S(2)}) copy-start(f32[3,3,512]{2,1,0:T(4,128)} %refs_6_.1) | copy-start | bytes 55300
  107.0 19.5 %copy-start.4 = (f32[16,512]{1,0:T(8,128)S(1)}, f32[16,512]{1,0:T(8,128)}, u32[]{:S(2)}) copy-start(f32[16,512]{1,0:T(8,128)} %gain.3) | copy-start | bytes 98308
  107.0 19.6 %copy-start.8 = (f32[512]{0:T(512)S(1)}, f32[512]{0:T(512)}, u32[]{:S(2)}) copy-start(f32[512]{0:T(512)} %param.11) | copy-start | bytes 6148
  117.2 0.9 copy-start.3
  122.7 14.3 %all-to-all-start.1 = ((f32[16,16,256]{2,1,0:T(8,128)}), f32[16,16,256]{2,1,0:T(8,128)S(1)}, u32[]{:S(2)}, u32[]{:S(2)}) async-start(f32[16,16,256]{2,1,0:T(8,128)} %broadcast_in_dim.3), calls=%async_computation.1 | async-start | bytes 524288 | tf_op jit(solution)/shard_map/state_exchange/all_to_all | solution.py:333
Sparse Core Ops, SparseCore 0:
  46.9 35.2 all-gather.2

commit v4 on v1

--- a/solution.py
+++ b/solution.py
@@ -22,75 +22,79 @@
     return lax.ppermute(array, axis, [(i, (i + step) % n) for i in range(n)])
 
 
-def ring(piece, axis):
-    half = piece.shape[0] // 2
-    behind = shifted(piece, axis, 1)
-    ahead = shifted(piece, axis, -1)
-    first = shifted(behind[:half], axis, 1)
-    second = shifted(ahead[half:], axis, -1)
-    return behind, ahead, first, second
-
-
-def project_kernel(sizes, *refs):
-    rows, depth, width, modes, seq = sizes
-    pos, tok, *pieces = refs[:22]
-    taps, decay = refs[22:24]
-    gate, product, inside, state = refs[24:28]
-    tokv, wv, acc, tok_sem, w_sem = refs[28:]
-    y, h, c = pos[1], pos[2], pos[3]
+def both_ways(piece, axis):
+    return shifted(piece, axis, 1), shifted(piece, axis, -1)
+
+
+def onward(behind, ahead, axis):
+    half = behind.shape[0] // 2
+    return shifted(behind[:half], axis, 1), shifted(ahead[half:], axis, -1)
+
+
+def fetched(sizes, pos, tokens, halo, pieces, blocks, tokv, wv, sem):
+    rows, depth, width, modes, seq = sizes
     k = depth // 16
-    half = k // 2
-    top = rows + HALO
-
-    copies = []
-    for ch in range(8):
-        lanes = pl.ds(ch * (depth // 8), depth // 8)
-        for core in range(2):
-            skip = HALO * core
-            at = (core * 8 + ch) * top
-            copies.append(
-                pltpu.make_async_copy(
-                    tok.at[pl.ds(at + skip, top - skip), :],
-                    tokv.at[pl.ds(core * top, top - skip), lanes],
-                    tok_sem.at[core * 8 + ch],
-                )
-            )
-    groups = [[], [], [], []]
-    for kind, dh in enumerate((0, 1, -1, 2)):
-        hs = lax.rem(h - dh + 4, 4)
-        for number, (dy, skip, n, group) in enumerate(
-            ((0, 0, k, 0), (1, 0, k, 1), (-1, 0, k, 2), (2, 0, half, 3), (2, half, half, 3))
-        ):
-            ys = lax.rem(y - dy + 4, 4)
-            at = pl.multiple_of((ys * 4 + hs) * k + skip, half)
-            copy = pltpu.make_async_copy(
-                pieces[kind * 5 + number], wv.at[pl.ds(at, n), :], w_sem.at[kind * 5 + number]
-            )
-            groups[group].append(copy)
-    for copy in groups[0] + copies + groups[1] + groups[2] + groups[3]:
-        copy.start()
-    for copy in copies:
+    copies, at, seen = [], 0, set()
+
+    def add(source, target):
+        copies.append(pltpu.make_async_copy(source, target, sem.at[len(copies)]))
+        return copies[-1]
+
+    for piece, first, n, dy, dh, skip in blocks:
+        add(pieces[piece].at[pl.ds(first, n), :], wv.at[pl.ds(at + skip, n), :]).start()
+        if (dy, dh) not in seen:
+            seen.add((dy, dh))
+            ys, hs = lax.rem(pos[1] - dy + 4, 4), lax.rem(pos[2] - dh + 4, 4)
+            ch = 2 * ys + lax.div(hs, 2)
+            lanes = pl.ds(pl.multiple_of(lax.rem(hs, 2) * k, k), k)
+            x = lax.rem(ch, 4)
+            swapped = lax.rem(lax.div(ch, 4) + pos[4], 2)
+            to = pl.ds(at, k)
+            line = pl.ds(pl.multiple_of((4 * swapped + x) * HALO, HALO), HALO)
+            add(halo.at[line, lanes], tokv.at[pl.ds(0, HALO), to]).start()
+            for core in range(2):
+                line = pl.ds(pl.multiple_of((4 * core + x) * rows, rows), rows)
+                target = tokv.at[pl.ds(HALO + core * rows, rows), to]
+                copy = add(tokens[0].at[line, lanes], target)
+                pl.when(swapped == 0)(copy.start)
+                copy = pltpu.make_async_copy(tokens[1].at[line, lanes], target, sem.at[len(copies) - 1])
+                pl.when(swapped == 1)(copy.start)
+        if skip + n == k:
+            at += k
+    return copies
+
+
+def project_kernel(sizes, blocks, *refs):
+    rows, depth, width, modes, seq = sizes
+    pos, near, swapped, halo, *pieces = refs[:-4]
+    sums, tokv, wv, sem = refs[-4:]
+    for copy in fetched(sizes, pos, (near, swapped), halo, pieces, blocks, tokv, wv, sem):
         copy.wait()
-    for group, dy in enumerate((0, 1, -1, 2)):
-        for copy in groups[group]:
-            copy.wait()
-        at = pl.multiple_of(lax.rem(y - dy + 4, 4) * (4 * k), 4 * k)
-
-        @pl.loop(0, 3)
-        def _(j):
-            cols = pl.ds(pl.multiple_of(j * width, width), width)
-            part = jnp.dot(
-                tokv[:, pl.ds(at, 4 * k)], wv[pl.ds(at, 4 * k), cols], preferred_element_type=F32
-            )
-            for lh in range(width // 128):
-                at_lane = j * (width // 128) + lh
-                new = part[:, lh * 128 : lh * 128 + 128]
-                if group == 0:
-                    acc[at_lane] = new
-                elif group < 3:
-                    acc[at_lane] += new
-                else:
-                    acc[at_lane] = (acc[at_lane] + new).astype(BF16).astype(F32)
+
+    @pl.loop(0, 3)
+    def _(j):
+        cols = pl.ds(pl.multiple_of(j * width, width), width)
+        part = jnp.dot(tokv[...], wv[:, cols], preferred_element_type=F32)
+        for lh in range(width // 128):
+            sums[j * (width // 128) + lh] = part[:, lh * 128 : lh * 128 + 128]
+
+
+def state_kernel(sizes, blocks, *refs):
+    rows, depth, width, modes, seq = sizes
+    pos, near, swapped, halo, *pieces = refs[:-11]
+    sums, taps, decay, gate, product, inside, state, tokv, wv, acc, sem = refs[-11:]
+    c = pos[3]
+    for copy in fetched(sizes, pos, (near, swapped), halo, pieces, blocks, tokv, wv, sem):
+        copy.wait()
+
+    @pl.loop(0, 3)
+    def _(j):
+        cols = pl.ds(pl.multiple_of(j * width, width), width)
+        part = jnp.dot(tokv[...], wv[:, cols], preferred_element_type=F32)
+        for lh in range(width // 128):
+            chunk = j * (width // 128) + lh
+            new = part[:, lh * 128 : lh * 128 + 128]
+            acc[chunk] = (sums[chunk] + new).astype(BF16).astype(F32)
 
     steps = 2 * rows // SUB
     for lh in range(width // 128):
@@ -202,47 +206,93 @@
     seq = rows * 32
     sizes = (rows, depth, width, modes, seq)
     y, h, c = (lax.axis_index(a) for a in CTX)
-    pos = jnp.stack([y * 4 + h, y, h, c]).astype(jnp.int32)
-
-    with jax.named_scope("token_gather"):
-        tail = lax.ppermute(tokens[rows - HALO :], CTX, [(i, i + 1) for i in range(1, 31, 2)])
-        tok = lax.all_gather(jnp.concatenate([tail, tokens], 0), ("c", *CH), axis=0, tiled=True)
-
+    pos = jnp.stack([y * 4 + h, y, h, c, lax.axis_index("l")]).astype(jnp.int32)
+
+    tie = lax.optimization_barrier
     with jax.named_scope("weight_gather"):
         halves = w_in.reshape(k, 3, 2, width).transpose(2, 0, 1, 3).reshape(2, k, 3 * width)
         own = lax.all_to_all(halves, "c", 0, 0, tiled=True).reshape(2 * k, 3 * width)
-        behind, ahead, first, second = ring(own, "h")
-        opposite = jnp.concatenate([first, second], 0)
-        pieces = []
-        for piece in (own, behind, ahead, opposite):
-            pieces += [piece, *ring(piece, "y")]
+        beside, far = both_ways(own, "h"), both_ways(own, "y")
+    with jax.named_scope("token_swap"):
+        other = lax.ppermute(tokens, "l", [(0, 1), (1, 0)])
+        other, far = tie((other, far))
+    farther = onward(*far, "y")
+    beside, far, farther = tie((beside, far, farther))
+    with jax.named_scope("token_gather"):
+        near = lax.all_gather(tokens, ("c", "x"), axis=0, tiled=True)
+        swapped = lax.all_gather(other, ("c", "x"), axis=0, tiled=True)
+        tails = [t.reshape(2, 4, rows, group)[1, :, rows - HALO :] for t in (near, swapped)]
+        tail = jnp.stack(tails).reshape(8 * HALO, group)
+        halo = lax.ppermute(tail, ("y", "h"), [(i, i + 1) for i in range(15)])
+    with jax.named_scope("weight_rings"):
+        pair = jnp.concatenate(beside, 0)
+        far_pair, opposite = both_ways(pair, "y"), onward(*beside, "h")
+        far_pair, opposite = tie((far_pair, opposite))
+        opposite = jnp.concatenate(opposite, 0)
+        far_opposite, farther_pair = both_ways(opposite, "y"), onward(*far_pair, "y")
+        last = shifted(opposite, "y", 2)
+
+    two = 2 * k
+    half = k
+    early = [own, pair, opposite, *far, *far_pair, *farther]
+    early_blocks = [(0, 0, two, 0, 0, 0), (1, 0, two, 0, 1, 0), (1, two, two, 0, -1, 0), (2, 0, two, 0, 2, 0)]
+    for side, dy in enumerate((1, -1)):
+        early_blocks += [
+            (3 + side, 0, two, dy, 0, 0),
+            (5 + side, 0, two, dy, 1, 0),
+            (5 + side, two, two, dy, -1, 0),
+        ]
+    early_blocks += [(7, 0, half, 2, 0, 0), (8, 0, half, 2, 0, half)]
+    late = [*farther_pair, *far_opposite, last]
+    late_blocks = [
+        (0, 0, two, 2, 1, 0),
+        (1, 0, two, 2, -1, 0),
+        (2, 0, two, 1, 2, 0),
+        (3, 0, two, -1, 2, 0),
+        (4, 0, two, 2, 2, 0),
+    ]
 
     vmem = pl.BlockSpec(memory_space=pltpu.VMEM)
     smem = pl.BlockSpec(memory_space=pltpu.SMEM)
-    anywhere = pl.BlockSpec(memory_space=pl.ANY)
+    hbm = pl.BlockSpec(memory_space=pltpu.HBM)
     block = (2 * rows // SUB, SUB, width)
     full = jax.ShapeDtypeStruct(block, F32)
-    params = pltpu.CompilerParams(vmem_limit_bytes=40 * 2**20)
+    lines = 2 * rows + HALO
+    chunks = (3 * width // 128, lines, 128)
+
+    def held(n):
+        return [pltpu.VMEM((lines, n * two), BF16), pltpu.VMEM((n * two, 3 * width), BF16)]
+
+    def sems(blocks, n):
+        return pltpu.SemaphoreType.DMA((len(blocks) + 3 * n,))
+
+    sums = pl.pallas_call(
+        functools.partial(project_kernel, sizes, early_blocks),
+        out_shape=jax.ShapeDtypeStruct(chunks, F32),
+        in_specs=[smem] + [hbm] * (3 + len(early)),
+        out_specs=vmem,
+        scratch_shapes=[*held(11), sems(early_blocks, 11)],
+        compiler_params=pltpu.CompilerParams(vmem_limit_bytes=14 * 2**20),
+        cost_estimate=pl.CostEstimate(
+            flops=2 * lines * 11 * two * 3 * width, bytes_accessed=9_000_000, transcendentals=0
+        ),
+        name="project",
+    )(pos, near, swapped, halo, *early)
+    params = pltpu.CompilerParams(vmem_limit_bytes=12 * 2**20)
     gate, product, inside, state = pl.pallas_call(
-        functools.partial(project_kernel, sizes),
+        functools.partial(state_kernel, sizes, late_blocks),
         out_shape=(
             full,
             full,
             jax.ShapeDtypeStruct((modes, SUB, width), F32),
             jax.ShapeDtypeStruct((modes, width), F32),
         ),
-        in_specs=[smem] + [anywhere] * 21 + [vmem] * 2,
+        in_specs=[smem] + [hbm] * (3 + len(late)) + [vmem] * 3,
         out_specs=(vmem,) * 4,
-        scratch_shapes=[
-            pltpu.VMEM((2 * rows + HALO, depth), BF16),
-            pltpu.VMEM((depth, 3 * width), BF16),
-            pltpu.VMEM((3 * width // 128, 2 * rows + HALO, 128), F32),
-            pltpu.SemaphoreType.DMA((16,)),
-            pltpu.SemaphoreType.DMA((20,)),
-        ],
+        scratch_shapes=[*held(5), pltpu.VMEM(chunks, F32), sems(late_blocks, 5)],
         compiler_params=params,
-        name="project",
-    )(pos, tok, *pieces, taps, decay)
+        name="states",
+    )(pos, near, swapped, halo, *late, sums, taps, decay)
 
     with jax.named_scope("state_exchange"):
         states = lax.all_to_all(

time: 172 us -> 150 us (0.87); the launches traced: 168 us -> 149 us
  local copies, waits for them, and re-layouts: 28.8 us -> 17.7 us
  starting transfers between devices: 40.4 us -> 34.6 us
  other arithmetic: 1.75 us -> 0.01 us
    ppermute x20 -> x15, waiting for transfers between devices: 49.1 us -> 30.6 us  [shifted(): return lax.ppermute(array, axis, [(i, (i + step) % n) for i in range(n)])]
    unnamed x54 -> x45, local copies, waits for them, and re-layouts: 22.6 us -> 10.4 us
    all_gather x1 -> x2, waiting for transfers between devices: 0.01 us -> 8.44 us  [the longest x1 8.42 us: body(): swapped = lax.all_gather(other, ('c', 'x'), axis=0, tiled=True)]
    ppermute x20 -> x15, starting transfers between devices: 27.8 us -> 21.3 us  [shifted(): return lax.ppermute(array, axis, [(i, (i + step) % n) for i in range(n)])]
    ppermute x1 -> x2, waiting for transfers between devices: 0.85 us -> 5.71 us  [the longest x1 5.7 us: body(): other = lax.ppermute(tokens, 'l', [(0, 1), (1, 0)])]
    all_to_all x1, blocking collectives: 3.69 us -> 6.92 us  [body(): lax.all_to_all(halves, 'c', 0, 0, tiled=True).reshape(2 * k, 3 * width)]
    all_to_all x1, waiting for transfers between devices: 6.09 us -> 8.87 us  [body(): lax.all_to_all(jnp.broadcast_to(state, (16, *state.shape)), ('y', 'h'), 0...]
    all_to_all x1, blocking collectives: 8.53 us -> 6.54 us  [body(): both = lax.all_to_all(out, 'c', 0, 0, tiled=True)]
  transfers between devices with their start and end apart: 23 -> 20, of which waited for: 11 -> 10; matrix products, arithmetic and copies ran while one was open for 3% -> 5% of each run, Pallas kernels for 1% -> 5%
where the time goes in v4:
time: 150 us; the launch traced here: 149 us
  waiting for transfers between devices  54.4 us (36%)
  starting transfers between devices  34.6 us (23%)
  local copies, waits for them, and re-layouts  17.7 us (12%)
  Pallas kernels  15.6 us (10%)
  between operations  13.7 us (9%)
  blocking collectives  13.5 us (9%)
    ppermute x15, waiting for transfers between devices, shifted(): return lax.ppermute(array, axis, [(i, (i + step) % n) for i in range(n)])  30.6 us
    ppermute x15, starting transfers between devices, shifted(): return lax.ppermute(array, axis, [(i, (i + step) % n) for i in range(n)])  21.3 us
    unnamed x45, local copies, waits for them, and re-layouts  10.4 us
    all_to_all x1, waiting for transfers between devices, body(): lax.all_to_all(jnp.broadcast_to(state, (16, *state.shape)), ('y', 'h'), 0...  8.87 us
    all_gather x1, waiting for transfers between devices, body(): swapped = lax.all_gather(other, ('c', 'x'), axis=0, tiled=True)  8.42 us
    all_to_all x1, starting transfers between devices, body(): lax.all_to_all(jnp.broadcast_to(state, (16, *state.shape)), ('y', 'h'), 0...  7.88 us
    all_to_all x1, blocking collectives, body(): lax.all_to_all(halves, 'c', 0, 0, tiled=True).reshape(2 * k, 3 * width)  6.92 us
    all_to_all x1, blocking collectives, body(): both = lax.all_to_all(out, 'c', 0, 0, tiled=True)  6.54 us
  transfers between devices with their start and end apart: 20, of which 10 were waited for; matrix products, arithmetic and copies ran while one was open for 5% of the time, Pallas kernels for 5%

profile of v4, /device:TPU:1, one launch (start us, length us, event | category | flops | bytes accessed | tf_op | source)
XLA Modules:
  0.0 149.4 jit_solution(1780216524057405364)
XLA Ops:
  6.5 0.7 all-gather.3.cloned.1.call-update
  7.3 0.0 all-gather.5.cloned.1.call-start
  7.3 1.2 copy.11
  8.6 6.9 %all_to_all.15 = bf16[2,128,768]{1,2,0:T(8,128)(2,1)S(1)} all-to-all(bf16[2,128,768]{1,2,0:T(8,128)(2,1)S(1)} %bitcast.24), channel_id=1, replica_groups=mesh['y'=4,'h'=4,'c'=2,'l'=2,'x'=4] {'c'}, dimensions={0} | all-to-all | bytes 786432 | tf_op jit(solution)/shard_map/weight_gather/all_to_all | solution.py:214
  15.5 0.2 copy.13
  15.7 1.1 collective-permute-start.2
  16.7 0.5 collective-permute-start.1
  17.2 1.2 collective-permute-start
  18.4 5.7 %collective-permute-done = bf16[256,512]{1,0:T(8,128)(2,1)S(1)} collective-permute-done((bf16[256,512]{1,0:T(8,128)(2,1)S(1)}, bf16[256,512]{1,0:T(8,128)(2,1)S(1)}, u32[]{:S(2)}, u32[]{:S(2)}) %collective-permute-start) | collective-permute-done | bytes 262176 | tf_op jit(solution)/shard_map/token_swap/ppermute | solution.py:217
  24.1 2.0 %collective-permute-done.2.refs_8_ = bf16[256,768]{1,0:T(8,128)(2,1)S(1)} collective-permute-done((bf16[256,768]{1,0:T(8,128)(2,1)S(1)}, bf16[256,768]{1,0:T(8,128)(2,1)S(1)}, u32[]{:S(2)}, u32[]{:S(2)}) %collective-permute-start.2) | collective-permute-done | bytes 393248 | tf_op jit(solution)/shard_map/weight_gather/ppermute | solution.py:22
  26.1 1.9 %collective-permute-done.1.refs_7_ = bf16[256,768]{1,0:T(8,128)(2,1)S(1)} collective-permute-done((bf16[256,768]{1,0:T(8,128)(2,1)S(1)}, bf16[256,768]{1,0:T(8,128)(2,1)S(1)}, u32[]{:S(2)}, u32[]{:S(2)}) %collective-permute-start.1) | collective-permute-done | bytes 393248 | tf_op jit(solution)/shard_map/weight_gather/ppermute | solution.py:22
  28.0 0.0 all-gather.5.cloned.1.call-update
  28.0 6.2 %collective-permute-start.5 = (bf16[256,768]{1,0:T(8,128)(2,1)S(1)}, bf16[256,768]{1,0:T(8,128)(2,1)S(1)}, u32[]{:S(2)}, u32[]{:S(2)}) collective-permute-start(bf16[256,768]{1,0:T(8,128)(2,1)S(1)} %bitcast.20), channel_id=1, source_target_pairs={{0,48},{16,0},{32,16},{48,32},{1,49},{17,1},{33,17},{49,33},{2,50}... | collective-permute-start | bytes 1179656 | tf_op jit(solution)/shard_map/weight_gather/ppermute | solution.py:22
  34.2 0.0 collective-permute-start.4
  34.2 0.3 collective-permute-start.7
  34.5 1.2 collective-permute-start.6
  35.8 12.1 %collective-permute-done.5 = bf16[256,768]{1,0:T(8,128)(2,1)S(1)} collective-permute-done((bf16[256,768]{1,0:T(8,128)(2,1)S(1)}, bf16[256,768]{1,0:T(8,128)(2,1)S(1)}, u32[]{:S(2)}, u32[]{:S(2)}) %collective-permute-start.5) | collective-permute-done | bytes 393248 | tf_op jit(solution)/shard_map/weight_gather/ppermute | solution.py:22
  47.9 0.0 collective-permute-done.7.refs_12_
  48.0 0.7 collective-permute-start.9
  48.6 0.9 collective-permute-start.8
  49.5 0.9 copy-done.3
  50.4 4.4 %collective-permute-start.11 = (bf16[128,768]{1,0:T(8,128)(2,1)S(1)}, bf16[128,768]{1,0:T(8,128)(2,1)S(1)}, u32[]{:S(2)}, u32[]{:S(2)}) collective-permute-start(bf16[128,768]{1,0:T(8,128)(2,1)S(1)} %slice.29), channel_id=1, source_target_pairs={{0,48},{16,0},{32,16},{48,32},{1,49},{17,1},{33,17},{49,33},{2,50}... | collective-permute-start | bytes 589832 | tf_op jit(solution)/shard_map/weight_rings/ppermute | solution.py:22
  54.8 0.4 collective-permute-start.10
  55.2 3.0 %collective-permute-done.11 = bf16[128,768]{1,0:T(8,128)(2,1)S(1)} collective-permute-done((bf16[128,768]{1,0:T(8,128)(2,1)S(1)}, bf16[128,768]{1,0:T(8,128)(2,1)S(1)}, u32[]{:S(2)}, u32[]{:S(2)}) %collective-permute-start.11) | collective-permute-done | bytes 196640 | tf_op jit(solution)/shard_map/weight_rings/ppermute | solution.py:22
  58.2 3.4 %collective-permute-done.10 = bf16[128,768]{1,0:T(8,128)(2,1)} collective-permute-done((bf16[128,768]{1,0:T(8,128)(2,1)S(1)}, bf16[128,768]{1,0:T(8,128)(2,1)}, u32[]{:S(2)}, u32[]{:S(2)}) %collective-permute-start.10) | collective-permute-done | bytes 196640 | tf_op jit(solution)/shard_map/weight_rings/ppermute | solution.py:22
  61.6 0.0 collective-permute-done.9.refs_10_
  61.6 0.0 collective-permute-done.8.refs_9_
  61.6 0.0 all-gather.3.cloned.1.call-done.refs_1_
  61.7 1.0 slice.32
  62.7 8.4 %all-gather.5.cloned.1.call-done.refs_2_ = bf16[2048,512]{1,0:T(8,128)(2,1)} async-done(((bf16[256,512]{1,0:T(8,128)(2,1)}), bf16[2048,512]{1,0:T(8,128)(2,1)}) %all-gather.5.cloned.1.call-update) | async-done | bytes 2097168 | tf_op jit(solution)/shard_map/token_gather/all_gather | solution.py:223
  71.1 0.9 slice.33
  72.0 4.2 %collective-permute-start.3 = (bf16[128,512]{1,0:T(8,128)(2,1)S(1)}, bf16[128,512]{1,0:T(8,128)(2,1)S(1)}, u32[]{:S(2)}, u32[]{:S(2)}) collective-permute-start(bf16[128,512]{1,0:T(8,128)(2,1)S(1)} %bitcast.28), channel_id=1, source_target_pairs={{0,16},{16,32},{32,48},{48,64},{64,80},{80,96},{96,112},{112,128},... | collective-permute-start | bytes 393224 | tf_op jit(solution)/shard_map/token_gather/ppermute | solution.py:226
  76.2 1.6 %constant_dynamic-update-slice_fusion.3 = bf16[256,768]{1,0:T(8,128)(2,1)} fusion(bf16[128,768]{1,0:T(8,128)(2,1)} %collective-permute-done.10), kind=kLoop, calls=%fused_computation.4 | loop fusion | bytes 393216
  77.8 0.8 slice.31
  78.6 1.8 %slice.30 = bf16[256,768]{1,0:T(8,128)(2,1)} slice(bf16[512,768]{1,0:T(8,128)(2,1)} %collective-permute-done.8.refs_9_), slice={[0:256], [0:768]} | slice | bytes 786432 | tf_op jit(solution)/shard_map/weight_rings/slice | solution.py:31
  80.4 1.2 collective-permute-start.12
  81.6 1.5 collective-permute-start.13
  83.1 0.7 constant_dynamic-update-slice_fusion.2.refs_6_
  83.8 1.5 %collective-permute-start.16 = (bf16[256,768]{1,0:T(8,128)(2,1)}, bf16[256,768]{1,0:T(8,128)(2,1)}, u32[]{:S(2)}, u32[]{:S(2)}) collective-permute-start(bf16[256,768]{1,0:T(8,128)(2,1)} %constant_dynamic-update-slice_fusion.2.refs_6_), channel_id=1, source_target_pairs={{0,128},{64,192},{128,0},{192,64},{1,129},{65,193},{129,1},{193,65... | collective-permute-start | bytes 1179656 | tf_op jit(solution)/shard_map/weight_rings/ppermute | solution.py:22
  85.3 0.9 collective-permute-start.15
  86.2 0.0 collective-permute-done.3.refs_3_
  86.2 0.6 collective-permute-start.14
  86.8 0.1 stack.26.refs_0_.pos
  86.9 1.6 %copy-done.1 = bf16[2048,512]{1,0:T(8,128)(2,1)S(1)} copy-done((bf16[2048,512]{1,0:T(8,128)(2,1)S(1)}, bf16[2048,512]{1,0:T(8,128)(2,1)}, u32[]{:S(2)}) %copy-start.1) | copy-done | bytes 2097176
  88.5 1.1 copy-done.4
  89.6 1.0 copy-done.6
  90.6 1.0 copy-done.8
  91.6 0.9 copy-done.11
  92.5 0.9 copy-done.13
  93.5 6.3 %project.1.refs_9_ = f32[6,528,128]{2,1,0:T(8,128)S(1)} custom-call(s32[5]{0:T(128)S(1)} %stack.26.refs_0_.pos, bf16[2048,512]{1,0:T(8,128)(2,1)S(1)} %copy-done, bf16[2048,512]{1,0:T(8,128)(2,1)S(1)} %copy-done.1, bf16[128,512]{1,0:T(8,128)(2,1)S(1)} %collective-permute-done.3.refs_3_, bf16[256,768]{1,0:T(8,128)(2,1)S(1)} %bitcast.22, ...), custom_call_target="tpu_custom_call" | custom-call | flops 2283798528 | bytes 9000000 | tf_op jit(solution)/shard_map/project/pallas_call | solution.py:269
  99.8 0.0 copy-start.14
  99.8 0.0 copy-start.16
  99.8 0.0 collective-permute-done.12.refs_4_
  99.8 2.3 %collective-permute-done.16.refs_8_ = bf16[256,768]{1,0:T(8,128)(2,1)} collective-permute-done((bf16[256,768]{1,0:T(8,128)(2,1)}, bf16[256,768]{1,0:T(8,128)(2,1)}, u32[]{:S(2)}, u32[]{:S(2)}) %collective-permute-start.16) | collective-permute-done | bytes 393248 | tf_op jit(solution)/shard_map/weight_rings/ppermute | solution.py:22
  102.2 6.0 %collective-permute-done.15.refs_7_ = bf16[256,768]{1,0:T(8,128)(2,1)} collective-permute-done((bf16[256,768]{1,0:T(8,128)(2,1)}, bf16[256,768]{1,0:T(8,128)(2,1)}, u32[]{:S(2)}, u32[]{:S(2)}) %collective-permute-start.15) | collective-permute-done | bytes 393248 | tf_op jit(solution)/shard_map/weight_rings/ppermute | solution.py:22
  108.2 5.9 %states.1 = (f32[64,8,256]{2,1,0:T(8,128)S(1)}, f32[64,8,256]{2,1,0:T(8,128)S(1)}, f32[16,8,256]{2,1,0:T(8,128)S(1)}, f32[16,256]{1,0:T(8,128)S(1)}) custom-call(s32[5]{0:T(128)S(1)} %stack.26.refs_0_.pos, bf16[2048,512]{1,0:T(8,128)(2,1)S(1)} %copy-done, bf16[2048,512]{1,0:T(8,128)(2,1)S(1)} %copy-done.2, ...), custom_call_target="tpu_custom_call" | custom-call | tf_op jit(solution)/shard_map/states/pallas_call | solution.py:282
  114.1 0.7 broadcast_in_dim.3
  114.8 7.9 %all-to-all-start.1 = ((f32[16,16,256]{2,1,0:T(8,128)}), f32[16,16,256]{2,1,0:T(8,128)S(1)}, u32[]{:S(2)}, u32[]{:S(2)}) async-start(f32[16,16,256]{2,1,0:T(8,128)} %broadcast_in_dim.3), calls=%async_computation.1 | async-start | bytes 524288 | tf_op jit(solution)/shard_map/state_exchange/all_to_all | solution.py:298
  122.7 1.9 %local.1 = f32[64,8,256]{2,1,0:T(8,128)S(1)} custom-call(s32[5]{0:T(128)S(1)} %stack.26.refs_0_.pos, f32[64,8,256]{2,1,0:T(8,128)S(1)} %get-tuple-element.36.product, f32[16,512]{1,0:T(8,128)S(1)} %copy-done.14, f32[16,512]{1,0:T(8,128)S(1)} %copy-done.9, f32[1,512]{1,0:T(1,128)S(1)} %bitcast.23), custom_call_target="tpu_custom_call" | custom-call | flops 20000000 | bytes 1000000 | tf_op jit(solution)/shard_map/local/pallas_call | solution.py:301
  124.6 8.9 %all-to-all-done.1.states = f32[16,16,256]{2,1,0:T(8,128)S(1)} async-done(((f32[16,16,256]{2,1,0:T(8,128)}), f32[16,16,256]{2,1,0:T(8,128)S(1)}, u32[]{:S(2)}, u32[]{:S(2)}) %all-to-all-start.1) | async-done | bytes 262176 | tf_op jit(solution)/shard_map/state_exchange/all_to_all | solution.py:298
  133.5 1.5 %finish.1 = bf16[2,256,256]{2,1,0:T(8,128)(2,1)S(1)} custom-call(s32[5]{0:T(128)S(1)} %stack.26.refs_0_.pos, f32[64,8,256]{2,1,0:T(8,128)S(1)} %get-tuple-element.35.gate, f32[64,8,256]{2,1,0:T(8,128)S(1)} %local.1, f32[16,8,256]{2,1,0:T(8,128)S(1)} %get-tuple-element.37.inside, f32[16,16,256]{2,1,0:T(8,128)S(1)} %all-to-all-done.1.states, ...), custom_call_target="tpu_custom_call" | custom-call | tf_op jit(solution)/shard_map/finish/pallas_call | solution.py:310
  135.0 6.5 %all_to_all.16 = bf16[2,256,256]{2,1,0:T(8,128)(2,1)S(1)} all-to-all(bf16[2,256,256]{2,1,0:T(8,128)(2,1)S(1)} %finish.1), channel_id=1, replica_groups=mesh['y'=4,'h'=4,'c'=2,'l'=2,'x'=4] {'c'}, dimensions={0} | all-to-all | bytes 524288 | tf_op jit(solution)/shard_map/result_swap/all_to_all | solution.py:320
  141.6 0.1 copy.14
  141.7 0.8 copy.15
  (46 shorter events, 0.2 us)
Async XLA Ops:
  6.5 10.7 %copy-start.17 = (bf16[256,512]{1,0:T(8,128)(2,1)S(1)}, bf16[256,512]{1,0:T(8,128)(2,1)}, u32[]{:S(2)}) copy-start(bf16[256,512]{1,0:T(8,128)(2,1)} %param.6) | copy-start | bytes 786436
  6.5 55.1 %all-gather.3.cloned.1.call-start = ((), (), s32[]{:S(2)}) async-start(), calls=%async_computation.3 | async-start | bytes 2359296 | tf_op jit(solution)/shard_map/token_gather/all_gather | solution.py:222
  7.3 63.8 %all-gather.5.cloned.1.call-start = ((), (), s32[]{:S(2)}) async-start(), calls=%async_computation.4 | async-start | bytes 2359296 | tf_op jit(solution)/shard_map/token_gather/all_gather | solution.py:223
  15.7 10.4 %collective-permute-start.2 = (bf16[256,768]{1,0:T(8,128)(2,1)S(1)}, bf16[256,768]{1,0:T(8,128)(2,1)S(1)}, u32[]{:S(2)}, u32[]{:S(2)}) collective-permute-start(bf16[256,768]{1,0:T(8,128)(2,1)S(1)} %bitcast.18), channel_id=1, source_target_pairs={{0,192},{64,0},{128,64},{192,128},{1,193},{65,1},{129,65},{193,129... | collective-permute-start | bytes 1179656 | tf_op jit(solution)/shard_map/weight_gather/ppermute | solution.py:22
  16.7 11.2 %collective-permute-start.1 = (bf16[256,768]{1,0:T(8,128)(2,1)S(1)}, bf16[256,768]{1,0:T(8,128)(2,1)S(1)}, u32[]{:S(2)}, u32[]{:S(2)}) collective-permute-start(bf16[256,768]{1,0:T(8,128)(2,1)S(1)} %bitcast.19), channel_id=1, source_target_pairs={{0,64},{64,128},{128,192},{192,0},{1,65},{65,129},{129,193},{193,1... | collective-permute-start | bytes 1179656 | tf_op jit(solution)/shard_map/weight_gather/ppermute | solution.py:22
  17.2 6.9 %collective-permute-start = (bf16[256,512]{1,0:T(8,128)(2,1)S(1)}, bf16[256,512]{1,0:T(8,128)(2,1)S(1)}, u32[]{:S(2)}, u32[]{:S(2)}) collective-permute-start(bf16[256,512]{1,0:T(8,128)(2,1)S(1)} %copy-done.17), channel_id=1, source_target_pairs={{0,4},{4,0},{1,5},{5,1},{2,6},{6,2},{3,7},{7,3},{8,12},{12,8},{9,1... | collective-permute-start | bytes 786440 | tf_op jit(solution)/shard_map/token_swap/ppermute | solution.py:217
  24.1 3.9 %copy-start.18 = (bf16[256,512]{1,0:T(8,128)(2,1)}, bf16[256,512]{1,0:T(8,128)(2,1)S(1)}, u32[]{:S(2)}) copy-start(bf16[256,512]{1,0:T(8,128)(2,1)S(1)} %collective-permute-done) | copy-start | bytes 786436
  26.1 35.5 %copy-start.5 = (bf16[256,768]{1,0:T(8,128)(2,1)}, bf16[256,768]{1,0:T(8,128)(2,1)S(1)}, u32[]{:S(2)}) copy-start(bf16[256,768]{1,0:T(8,128)(2,1)S(1)} %collective-permute-done.2.refs_8_) | copy-start | bytes 1179652
  28.0 33.6 %copy-start.7 = (bf16[256,768]{1,0:T(8,128)(2,1)}, bf16[256,768]{1,0:T(8,128)(2,1)S(1)}, u32[]{:S(2)}) copy-start(bf16[256,768]{1,0:T(8,128)(2,1)S(1)} %collective-permute-done.1.refs_7_) | copy-start | bytes 1179652
  28.0 19.9 %collective-permute-start.5 = (bf16[256,768]{1,0:T(8,128)(2,1)S(1)}, bf16[256,768]{1,0:T(8,128)(2,1)S(1)}, u32[]{:S(2)}, u32[]{:S(2)}) collective-permute-start(bf16[256,768]{1,0:T(8,128)(2,1)S(1)} %bitcast.20), channel_id=1, source_target_pairs={{0,48},{16,0},{32,16},{48,32},{1,49},{17,1},{33,17},{49,33},{2,50}... | collective-permute-start | bytes 1179656 | tf_op jit(solution)/shard_map/weight_gather/ppermute | solution.py:22
  34.2 13.7 %collective-permute-start.4 = (bf16[256,768]{1,0:T(8,128)(2,1)S(1)}, bf16[256,768]{1,0:T(8,128)(2,1)S(1)}, u32[]{:S(2)}, u32[]{:S(2)}) collective-permute-start(bf16[256,768]{1,0:T(8,128)(2,1)S(1)} %bitcast.21), channel_id=1, source_target_pairs={{0,16},{16,32},{32,48},{48,0},{1,17},{17,33},{33,49},{49,1},{2,18}... | collective-permute-start | bytes 1179656 | tf_op jit(solution)/shard_map/weight_gather/ppermute | solution.py:22
  34.2 13.6 %collective-permute-start.7 = (bf16[128,768]{1,0:T(8,128)(2,1)S(1)}, bf16[128,768]{1,0:T(8,128)(2,1)S(1)}, u32[]{:S(2)}, u32[]{:S(2)}) collective-permute-start(bf16[128,768]{1,0:T(8,128)(2,1)S(1)} %slice.27), channel_id=1, source_target_pairs={{0,192},{64,0},{128,64},{192,128},{1,193},{65,1},{129,65},{193,129... | collective-permute-start | bytes 589832 | tf_op jit(solution)/shard_map/ppermute | solution.py:22
  34.5 13.3 %collective-permute-start.6 = (bf16[128,768]{1,0:T(8,128)(2,1)S(1)}, bf16[128,768]{1,0:T(8,128)(2,1)S(1)}, u32[]{:S(2)}, u32[]{:S(2)}) collective-permute-start(bf16[128,768]{1,0:T(8,128)(2,1)S(1)} %slice.26), channel_id=1, source_target_pairs={{0,64},{64,128},{128,192},{192,0},{1,65},{65,129},{129,193},{193,1... | collective-permute-start | bytes 589832 | tf_op jit(solution)/shard_map/ppermute | solution.py:22
  47.9 13.7 %copy-start.10 = (bf16[128,768]{1,0:T(8,128)(2,1)}, bf16[128,768]{1,0:T(8,128)(2,1)S(1)}, u32[]{:S(2)}) copy-start(bf16[128,768]{1,0:T(8,128)(2,1)S(1)} %collective-permute-done.7.refs_12_) | copy-start | bytes 589828
  47.9 13.7 %copy-start.12 = (bf16[128,768]{1,0:T(8,128)(2,1)}, bf16[128,768]{1,0:T(8,128)(2,1)S(1)}, u32[]{:S(2)}) copy-start(bf16[128,768]{1,0:T(8,128)(2,1)S(1)} %collective-permute-done.6.refs_11_) | copy-start | bytes 589828
  48.0 13.6 %collective-permute-start.9 = (bf16[512,768]{1,0:T(8,128)(2,1)S(1)}, bf16[512,768]{1,0:T(8,128)(2,1)S(1)}, u32[]{:S(2)}, u32[]{:S(2)}) collective-permute-start(bf16[512,768]{1,0:T(8,128)(2,1)S(1)} %constant_dynamic-update-slice_fusion.refs_5_), channel_id=1, source_target_pairs={{0,192},{64,0},{128,64},{192,128},{1,193},{65,1},{129,65},{193,129... | collective-permute-start | bytes 2359304 | tf_op jit(solution)/shard_map/weight_rings/ppermute | solution.py:22
  48.6 13.0 %collective-permute-start.8 = (bf16[512,768]{1,0:T(8,128)(2,1)S(1)}, bf16[512,768]{1,0:T(8,128)(2,1)}, u32[]{:S(2)}, u32[]{:S(2)}) collective-permute-start(bf16[512,768]{1,0:T(8,128)(2,1)S(1)} %constant_dynamic-update-slice_fusion.refs_5_), channel_id=1, source_target_pairs={{0,64},{64,128},{128,192},{192,0},{1,65},{65,129},{129,193},{193,1... | collective-permute-start | bytes 2359304 | tf_op jit(solution)/shard_map/weight_rings/ppermute | solution.py:22
  49.5 0.9 copy-start.3
  50.4 7.8 %collective-permute-start.11 = (bf16[128,768]{1,0:T(8,128)(2,1)S(1)}, bf16[128,768]{1,0:T(8,128)(2,1)S(1)}, u32[]{:S(2)}, u32[]{:S(2)}) collective-permute-start(bf16[128,768]{1,0:T(8,128)(2,1)S(1)} %slice.29), channel_id=1, source_target_pairs={{0,48},{16,0},{32,16},{48,32},{1,49},{17,1},{33,17},{49,33},{2,50}... | collective-permute-start | bytes 589832 | tf_op jit(solution)/shard_map/weight_rings/ppermute | solution.py:22
  54.8 6.7 %collective-permute-start.10 = (bf16[128,768]{1,0:T(8,128)(2,1)S(1)}, bf16[128,768]{1,0:T(8,128)(2,1)}, u32[]{:S(2)}, u32[]{:S(2)}) collective-permute-start(bf16[128,768]{1,0:T(8,128)(2,1)S(1)} %slice.28), channel_id=1, source_target_pairs={{0,16},{16,32},{32,48},{48,0},{1,17},{17,33},{33,49},{49,1},{2,18}... | collective-permute-start | bytes 589832 | tf_op jit(solution)/shard_map/weight_rings/ppermute | solution.py:22
  58.2 3.4 %copy-start.19 = (bf16[128,768]{1,0:T(8,128)(2,1)}, bf16[128,768]{1,0:T(8,128)(2,1)S(1)}, u32[]{:S(2)}) copy-start(bf16[128,768]{1,0:T(8,128)(2,1)S(1)} %collective-permute-done.11) | copy-start | bytes 589828
  61.6 25.2 %copy-start = (bf16[2048,512]{1,0:T(8,128)(2,1)S(1)}, bf16[2048,512]{1,0:T(8,128)(2,1)}, u32[]{:S(2)}) copy-start(bf16[2048,512]{1,0:T(8,128)(2,1)} %all-gather.3.cloned.1.call-done.refs_1_) | copy-start | bytes 6291460
  71.1 12.0 %copy-start.20 = (bf16[128,768]{1,0:T(8,128)(2,1)S(1)}, bf16[128,768]{1,0:T(8,128)(2,1)}, u32[]{:S(2)}) copy-start(bf16[128,768]{1,0:T(8,128)(2,1)} %copy-done.19) | copy-start | bytes 589828
  72.0 14.2 %collective-permute-start.3 = (bf16[128,512]{1,0:T(8,128)(2,1)S(1)}, bf16[128,512]{1,0:T(8,128)(2,1)S(1)}, u32[]{:S(2)}, u32[]{:S(2)}) collective-permute-start(bf16[128,512]{1,0:T(8,128)(2,1)S(1)} %bitcast.28), channel_id=1, source_target_pairs={{0,16},{16,32},{32,48},{48,64},{64,80},{80,96},{96,112},{112,128},... | collective-permute-start | bytes 393224 | tf_op jit(solution)/shard_map/token_gather/ppermute | solution.py:226
  80.4 19.4 %collective-permute-start.12 = (bf16[256,768]{1,0:T(8,128)(2,1)}, bf16[256,768]{1,0:T(8,128)(2,1)}, u32[]{:S(2)}, u32[]{:S(2)}) collective-permute-start(bf16[256,768]{1,0:T(8,128)(2,1)} %slice.30), channel_id=1, source_target_pairs={{0,64},{64,128},{128,192},{192,0},{1,65},{65,129},{129,193},{193,1... | collective-permute-start | bytes 1179656 | tf_op jit(solution)/shard_map/weight_rings/ppermute | solution.py:22
  81.6 18.2 %collective-permute-start.13 = (bf16[256,768]{1,0:T(8,128)(2,1)}, bf16[256,768]{1,0:T(8,128)(2,1)}, u32[]{:S(2)}, u32[]{:S(2)}) collective-permute-start(bf16[256,768]{1,0:T(8,128)(2,1)} %slice.31), channel_id=1, source_target_pairs={{0,192},{64,0},{128,64},{192,128},{1,193},{65,1},{129,65},{193,129... | collective-permute-start | bytes 1179656 | tf_op jit(solution)/shard_map/weight_rings/ppermute | solution.py:22
  83.8 18.4 %collective-permute-start.16 = (bf16[256,768]{1,0:T(8,128)(2,1)}, bf16[256,768]{1,0:T(8,128)(2,1)}, u32[]{:S(2)}, u32[]{:S(2)}) collective-permute-start(bf16[256,768]{1,0:T(8,128)(2,1)} %constant_dynamic-update-slice_fusion.2.refs_6_), channel_id=1, source_target_pairs={{0,128},{64,192},{128,0},{192,64},{1,129},{65,193},{129,1},{193,65... | collective-permute-start | bytes 1179656 | tf_op jit(solution)/shard_map/weight_rings/ppermute | solution.py:22
  85.3 22.8 %collective-permute-start.15 = (bf16[256,768]{1,0:T(8,128)(2,1)}, bf16[256,768]{1,0:T(8,128)(2,1)}, u32[]{:S(2)}, u32[]{:S(2)}) collective-permute-start(bf16[256,768]{1,0:T(8,128)(2,1)} %constant_dynamic-update-slice_fusion.2.refs_6_), channel_id=1, source_target_pairs={{0,192},{64,0},{128,64},{192,128},{1,193},{65,1},{129,65},{193,129... | collective-permute-start | bytes 1179656 | tf_op jit(solution)/shard_map/weight_rings/ppermute | solution.py:22
  86.2 22.0 %collective-permute-start.14 = (bf16[256,768]{1,0:T(8,128)(2,1)}, bf16[256,768]{1,0:T(8,128)(2,1)}, u32[]{:S(2)}, u32[]{:S(2)}) collective-permute-start(bf16[256,768]{1,0:T(8,128)(2,1)} %constant_dynamic-update-slice_fusion.2.refs_6_), channel_id=1, source_target_pairs={{0,64},{64,128},{128,192},{192,0},{1,65},{65,129},{129,193},{193,1... | collective-permute-start | bytes 1179656 | tf_op jit(solution)/shard_map/weight_rings/ppermute | solution.py:22
  86.9 1.6 %copy-start.1 = (bf16[2048,512]{1,0:T(8,128)(2,1)S(1)}, bf16[2048,512]{1,0:T(8,128)(2,1)}, u32[]{:S(2)}) copy-start(bf16[2048,512]{1,0:T(8,128)(2,1)} %all-gather.5.cloned.1.call-done.refs_2_) | copy-start | bytes 6291460
  88.5 1.1 copy-start.4
  89.6 1.0 copy-start.6
  90.6 1.0 copy-start.8
  91.6 0.9 copy-start.11
  92.5 0.9 copy-start.13
  93.4 14.7 %copy-start.2 = (bf16[2048,512]{1,0:T(8,128)(2,1)S(1)}, bf16[2048,512]{1,0:T(8,128)(2,1)}, u32[]{:S(2)}) copy-start(bf16[2048,512]{1,0:T(8,128)(2,1)} %all-gather.5.cloned.1.call-done.refs_2_) | copy-start | bytes 6291460
  93.4 14.7 %copy-start.9 = (f32[16,512]{1,0:T(8,128)S(1)}, f32[16,512]{1,0:T(8,128)}, u32[]{:S(2)}) copy-start(f32[16,512]{1,0:T(8,128)} %decay.3) | copy-start | bytes 98308
  93.5 14.7 %copy-start.15 = (f32[3,3,512]{2,1,0:T(4,128)S(1)}, f32[3,3,512]{2,1,0:T(4,128)}, u32[]{:S(2)}) copy-start(f32[3,3,512]{2,1,0:T(4,128)} %refs_10_.1) | copy-start | bytes 55300
  99.8 22.9 %copy-start.14 = (f32[16,512]{1,0:T(8,128)S(1)}, f32[16,512]{1,0:T(8,128)}, u32[]{:S(2)}) copy-start(f32[16,512]{1,0:T(8,128)} %gain.3) | copy-start | bytes 98308
  99.8 22.9 %copy-start.16 = (f32[512]{0:T(512)S(1)}, f32[512]{0:T(512)}, u32[]{:S(2)}) copy-start(f32[512]{0:T(512)} %param.11) | copy-start | bytes 6148
  114.8 18.6 %all-to-all-start.1 = ((f32[16,16,256]{2,1,0:T(8,128)}), f32[16,16,256]{2,1,0:T(8,128)S(1)}, u32[]{:S(2)}, u32[]{:S(2)}) async-start(f32[16,16,256]{2,1,0:T(8,128)} %broadcast_in_dim.3), calls=%async_computation.1 | async-start | bytes 524288 | tf_op jit(solution)/shard_map/state_exchange/all_to_all | solution.py:298
Sparse Core Ops, SparseCore 0:
  9.2 31.8 all-gather.2
  43.0 28.0 all-gather.4

commit v5 on v4

--- a/solution.py
+++ b/solution.py
@@ -31,9 +31,10 @@
     return shifted(behind[:half], axis, 1), shifted(ahead[half:], axis, -1)
 
 
-def fetched(sizes, pos, tokens, halo, pieces, blocks, tokv, wv, sem):
+def fetched(sizes, pos, tokens, pieces, blocks, tokv, wv, sem):
     rows, depth, width, modes, seq = sizes
     k = depth // 16
+    lines = rows + HALO
     copies, at, seen = [], 0, set()
 
     def add(source, target):
@@ -50,11 +51,12 @@
             x = lax.rem(ch, 4)
             swapped = lax.rem(lax.div(ch, 4) + pos[4], 2)
             to = pl.ds(at, k)
-            line = pl.ds(pl.multiple_of((4 * swapped + x) * HALO, HALO), HALO)
-            add(halo.at[line, lanes], tokv.at[pl.ds(0, HALO), to]).start()
             for core in range(2):
-                line = pl.ds(pl.multiple_of((4 * core + x) * rows, rows), rows)
-                target = tokv.at[pl.ds(HALO + core * rows, rows), to]
+                skipped = HALO * core
+                line = pl.ds(
+                    pl.multiple_of((4 * core + x) * lines + skipped, HALO), lines - skipped
+                )
+                target = tokv.at[pl.ds(core * lines, lines - skipped), to]
                 copy = add(tokens[0].at[line, lanes], target)
                 pl.when(swapped == 0)(copy.start)
                 copy = pltpu.make_async_copy(tokens[1].at[line, lanes], target, sem.at[len(copies) - 1])
@@ -66,9 +68,9 @@
 
 def project_kernel(sizes, blocks, *refs):
     rows, depth, width, modes, seq = sizes
-    pos, near, swapped, halo, *pieces = refs[:-4]
+    pos, near, swapped, *pieces = refs[:-4]
     sums, tokv, wv, sem = refs[-4:]
-    for copy in fetched(sizes, pos, (near, swapped), halo, pieces, blocks, tokv, wv, sem):
+    for copy in fetched(sizes, pos, (near, swapped), pieces, blocks, tokv, wv, sem):
         copy.wait()
 
     @pl.loop(0, 3)
@@ -81,10 +83,10 @@
 
 def state_kernel(sizes, blocks, *refs):
     rows, depth, width, modes, seq = sizes
-    pos, near, swapped, halo, *pieces = refs[:-11]
+    pos, near, swapped, *pieces = refs[:-11]
     sums, taps, decay, gate, product, inside, state, tokv, wv, acc, sem = refs[-11:]
     c = pos[3]
-    for copy in fetched(sizes, pos, (near, swapped), halo, pieces, blocks, tokv, wv, sem):
+    for copy in fetched(sizes, pos, (near, swapped), pieces, blocks, tokv, wv, sem):
         copy.wait()
 
     @pl.loop(0, 3)
@@ -214,16 +216,14 @@
         own = lax.all_to_all(halves, "c", 0, 0, tiled=True).reshape(2 * k, 3 * width)
         beside, far = both_ways(own, "h"), both_ways(own, "y")
     with jax.named_scope("token_swap"):
+        halo = lax.ppermute(tokens[rows - HALO :], CTX, [(i, i + 1) for i in range(1, 31, 2)])
+        tokens = jnp.concatenate([halo, tokens], 0)
         other = lax.ppermute(tokens, "l", [(0, 1), (1, 0)])
-        other, far = tie((other, far))
     farther = onward(*far, "y")
-    beside, far, farther = tie((beside, far, farther))
+    beside, far, farther, other = tie((beside, far, farther, other))
     with jax.named_scope("token_gather"):
         near = lax.all_gather(tokens, ("c", "x"), axis=0, tiled=True)
         swapped = lax.all_gather(other, ("c", "x"), axis=0, tiled=True)
-        tails = [t.reshape(2, 4, rows, group)[1, :, rows - HALO :] for t in (near, swapped)]
-        tail = jnp.stack(tails).reshape(8 * HALO, group)
-        halo = lax.ppermute(tail, ("y", "h"), [(i, i + 1) for i in range(15)])
     with jax.named_scope("weight_rings"):
         pair = jnp.concatenate(beside, 0)
         far_pair, opposite = both_ways(pair, "y"), onward(*beside, "h")
@@ -264,12 +264,12 @@
         return [pltpu.VMEM((lines, n * two), BF16), pltpu.VMEM((n * two, 3 * width), BF16)]
 
     def sems(blocks, n):
-        return pltpu.SemaphoreType.DMA((len(blocks) + 3 * n,))
+        return pltpu.SemaphoreType.DMA((len(blocks) + 2 * n,))
 
     sums = pl.pallas_call(
         functools.partial(project_kernel, sizes, early_blocks),
         out_shape=jax.ShapeDtypeStruct(chunks, F32),
-        in_specs=[smem] + [hbm] * (3 + len(early)),
+        in_specs=[smem] + [hbm] * (2 + len(early)),
         out_specs=vmem,
         scratch_shapes=[*held(11), sems(early_blocks, 11)],
         compiler_params=pltpu.CompilerParams(vmem_limit_bytes=14 * 2**20),
@@ -277,7 +277,7 @@
             flops=2 * lines * 11 * two * 3 * width, bytes_accessed=9_000_000, transcendentals=0
         ),
         name="project",
-    )(pos, near, swapped, halo, *early)
+    )(pos, near, swapped, *early)
     params = pltpu.CompilerParams(vmem_limit_bytes=12 * 2**20)
     gate, product, inside, state = pl.pallas_call(
         functools.partial(state_kernel, sizes, late_blocks),
@@ -287,12 +287,12 @@
             jax.ShapeDtypeStruct((modes, SUB, width), F32),
             jax.ShapeDtypeStruct((modes, width), F32),
         ),
-        in_specs=[smem] + [hbm] * (3 + len(late)) + [vmem] * 3,
+        in_specs=[smem] + [hbm] * (2 + len(late)) + [vmem] * 3,
         out_specs=(vmem,) * 4,
         scratch_shapes=[*held(5), pltpu.VMEM(chunks, F32), sems(late_blocks, 5)],
         compiler_params=params,
         name="states",
-    )(pos, near, swapped, halo, *late, sums, taps, decay)
+    )(pos, near, swapped, *late, sums, taps, decay)
 
     with jax.named_scope("state_exchange"):
         states = lax.all_to_all(

time: 150 us -> 147 us (0.980)
  waiting for transfers between devices: 54.4 us -> 50.1 us
  starting transfers between devices: 34.6 us -> 38.3 us
  blocking collectives: 13.5 us -> 12 us
    ppermute x1, waiting for transfers between devices: 5.7 us -> 14.5 us  [body(): other = lax.ppermute(tokens, 'l', [(0, 1), (1, 0)])]
    ppermute x15, waiting for transfers between devices: 30.6 us -> 23.4 us  [shifted(): return lax.ppermute(array, axis, [(i, (i + step) % n) for i in range(n)])]
    all_gather x1, waiting for transfers between devices: 8.42 us -> 1.91 us  [body(): swapped = lax.all_gather(other, ('c', 'x'), axis=0, tiled=True)]
    all_to_all x1, blocking collectives: 6.92 us -> 3.69 us  [body(): lax.all_to_all(halves, 'c', 0, 0, tiled=True).reshape(2 * k, 3 * width)]
    ppermute x1, starting transfers between devices: 4.18 us -> 6.27 us  [body(): lax.ppermute(tokens[rows - HALO:], CTX, [(i, i + 1) for i in range(1, 31,...]
    ppermute x15, starting transfers between devices: 21.3 us -> 23.1 us  [shifted(): return lax.ppermute(array, axis, [(i, (i + step) % n) for i in range(n)])]
    all_to_all x1, blocking collectives: 6.54 us -> 8.3 us  [body(): both = lax.all_to_all(out, 'c', 0, 0, tiled=True)]
    unnamed x45 -> x40, local copies, waits for them, and re-layouts: 10.4 us -> 8.81 us
  transfers between devices with their start and end apart: 20 -> 20, of which waited for: 10 -> 11; matrix products, arithmetic and copies ran while one was open for 5% -> 4% of each run, Pallas kernels for 5% -> 6%
where the time goes in v5:
time: 147 us
  waiting for transfers between devices  50.1 us (34%)
  starting transfers between devices  38.3 us (26%)
  local copies, waits for them, and re-layouts  16.7 us (11%)
  Pallas kernels  15.8 us (11%)
  between operations  13.7 us (9%)
  blocking collectives  12 us (8%)
    ppermute x15, waiting for transfers between devices, shifted(): return lax.ppermute(array, axis, [(i, (i + step) % n) for i in range(n)])  23.4 us
    ppermute x15, starting transfers between devices, shifted(): return lax.ppermute(array, axis, [(i, (i + step) % n) for i in range(n)])  23.1 us
    ppermute x1, waiting for transfers between devices, body(): other = lax.ppermute(tokens, 'l', [(0, 1), (1, 0)])  14.5 us
    all_to_all x1, waiting for transfers between devices, body(): lax.all_to_all(jnp.broadcast_to(state, (16, *state.shape)), ('y', 'h'), 0...  9.38 us
    unnamed x40, local copies, waits for them, and re-layouts  8.81 us
    all_to_all x1, blocking collectives, body(): both = lax.all_to_all(out, 'c', 0, 0, tiled=True)  8.3 us
    all_to_all x1, starting transfers between devices, body(): lax.all_to_all(jnp.broadcast_to(state, (16, *state.shape)), ('y', 'h'), 0...  8.13 us
    pallas_call x1, Pallas kernels, body(): pl.pallas_call(functools.partial(project_kernel, sizes, early_blocks), ou...  6.52 us
  transfers between devices with their start and end apart: 20, of which 11 were waited for; matrix products, arithmetic and copies ran while one was open for 4% of the time, Pallas kernels for 6%

profile of v5, /device:TPU:1, one launch (start us, length us, event | category | flops | bytes accessed | tf_op | source)
XLA Modules:
  0.0 146.5 jit_solution(320125986050909903)
XLA Ops:
  6.5 0.7 slice.21
  7.3 6.3 %collective-permute-start = (bf16[16,512]{1,0:T(8,128)(2,1)S(1)}, bf16[16,512]{1,0:T(8,128)(2,1)S(1)}, u32[]{:S(2)}, u32[]{:S(2)}) collective-permute-start(bf16[16,512]{1,0:T(8,128)(2,1)S(1)} %slice.21), channel_id=1, source_target_pairs={{8,16},{24,32},{40,48},{56,64},{72,80},{88,96},{104,112},{120,128}... | collective-permute-start | bytes 49160 | tf_op jit(solution)/shard_map/token_swap/ppermute | solution.py:219
  13.5 0.9 collective-permute-done
  14.4 1.0 constant_dynamic-update-slice_fusion
  15.4 0.7 copy-done.15
  16.1 0.0 all-gather.3.cloned.1.call-update
  16.1 0.0 all-gather.5.cloned.1.call-start
  16.2 1.2 copy.11
  17.5 3.7 %all_to_all.15 = bf16[2,128,768]{1,2,0:T(8,128)(2,1)S(1)} all-to-all(bf16[2,128,768]{1,2,0:T(8,128)(2,1)S(1)} %bitcast.19), channel_id=1, replica_groups=mesh['y'=4,'h'=4,'c'=2,'l'=2,'x'=4] {'c'}, dimensions={0} | all-to-all | bytes 786432 | tf_op jit(solution)/shard_map/weight_gather/all_to_all | solution.py:216
  21.2 0.2 copy.13
  21.4 5.9 %collective-permute-start.4 = (bf16[256,768]{1,0:T(8,128)(2,1)S(1)}, bf16[256,768]{1,0:T(8,128)(2,1)S(1)}, u32[]{:S(2)}, u32[]{:S(2)}) collective-permute-start(bf16[256,768]{1,0:T(8,128)(2,1)S(1)} %bitcast.13), channel_id=1, source_target_pairs={{0,192},{64,0},{128,64},{192,128},{1,193},{65,1},{129,65},{193,129... | collective-permute-start | bytes 1179656 | tf_op jit(solution)/shard_map/weight_gather/ppermute | solution.py:22
  27.2 0.0 collective-permute-start.3
  27.2 3.3 %collective-permute-start.2 = (bf16[256,768]{1,0:T(8,128)(2,1)S(1)}, bf16[256,768]{1,0:T(8,128)(2,1)S(1)}, u32[]{:S(2)}, u32[]{:S(2)}) collective-permute-start(bf16[256,768]{1,0:T(8,128)(2,1)S(1)} %bitcast.15), channel_id=1, source_target_pairs={{0,48},{16,0},{32,16},{48,32},{1,49},{17,1},{33,17},{49,33},{2,50}... | collective-permute-start | bytes 1179656 | tf_op jit(solution)/shard_map/weight_gather/ppermute | solution.py:22
  30.5 0.0 collective-permute-start.1
  30.5 0.7 collective-permute-start.7
  31.2 4.1 %collective-permute-done.4.refs_7_ = bf16[256,768]{1,0:T(8,128)(2,1)S(1)} collective-permute-done((bf16[256,768]{1,0:T(8,128)(2,1)S(1)}, bf16[256,768]{1,0:T(8,128)(2,1)S(1)}, u32[]{:S(2)}, u32[]{:S(2)}) %collective-permute-start.4) | collective-permute-done | bytes 393248 | tf_op jit(solution)/shard_map/weight_gather/ppermute | solution.py:22
  35.4 3.5 %collective-permute-start.6 = (bf16[128,768]{1,0:T(8,128)(2,1)S(1)}, bf16[128,768]{1,0:T(8,128)(2,1)S(1)}, u32[]{:S(2)}, u32[]{:S(2)}) collective-permute-start(bf16[128,768]{1,0:T(8,128)(2,1)S(1)} %slice.29), channel_id=1, source_target_pairs={{0,192},{64,0},{128,64},{192,128},{1,193},{65,1},{129,65},{193,129... | collective-permute-start | bytes 589832 | tf_op jit(solution)/shard_map/ppermute | solution.py:22
  38.8 0.0 collective-permute-done.3.refs_6_
  38.9 0.1 collective-permute-start.5
  39.0 14.5 %collective-permute-done.7 = bf16[272,512]{1,0:T(8,128)(2,1)S(1)} collective-permute-done((bf16[272,512]{1,0:T(8,128)(2,1)S(1)}, bf16[272,512]{1,0:T(8,128)(2,1)S(1)}, u32[]{:S(2)}, u32[]{:S(2)}) %collective-permute-start.7) | collective-permute-done | bytes 278560 | tf_op jit(solution)/shard_map/token_swap/ppermute | solution.py:221
  53.4 0.0 collective-permute-done.1
  53.5 0.0 collective-permute-done.5.refs_10_
  53.5 0.0 copy-start.8
  53.5 0.8 copy-done.17
  54.3 0.0 all-gather.5.cloned.1.call-update
  54.4 0.1 copy-done.13
  54.5 0.1 copy-done.14
  54.5 2.4 %collective-permute-start.9 = (bf16[512,768]{1,0:T(8,128)(2,1)S(1)}, bf16[512,768]{1,0:T(8,128)(2,1)S(1)}, u32[]{:S(2)}, u32[]{:S(2)}) collective-permute-start(bf16[512,768]{1,0:T(8,128)(2,1)S(1)} %constant_dynamic-update-slice_fusion.2.refs_4_), channel_id=1, source_target_pairs={{0,192},{64,0},{128,64},{192,128},{1,193},{65,1},{129,65},{193,129... | collective-permute-start | bytes 2359304 | tf_op jit(solution)/shard_map/weight_rings/ppermute | solution.py:22
  56.9 0.0 collective-permute-start.8
  56.9 0.9 slice.24
  57.9 0.9 slice.25
  58.8 3.9 %collective-permute-start.11 = (bf16[128,768]{1,0:T(8,128)(2,1)S(1)}, bf16[128,768]{1,0:T(8,128)(2,1)S(1)}, u32[]{:S(2)}, u32[]{:S(2)}) collective-permute-start(bf16[128,768]{1,0:T(8,128)(2,1)S(1)} %slice.25), channel_id=1, source_target_pairs={{0,48},{16,0},{32,16},{48,32},{1,49},{17,1},{33,17},{49,33},{2,50}... | collective-permute-start | bytes 589832 | tf_op jit(solution)/shard_map/weight_rings/ppermute | solution.py:22
  62.7 3.2 %collective-permute-done.11 = bf16[128,768]{1,0:T(8,128)(2,1)S(1)} collective-permute-done((bf16[128,768]{1,0:T(8,128)(2,1)S(1)}, bf16[128,768]{1,0:T(8,128)(2,1)S(1)}, u32[]{:S(2)}, u32[]{:S(2)}) %collective-permute-start.11) | collective-permute-done | bytes 196640 | tf_op jit(solution)/shard_map/weight_rings/ppermute | solution.py:22
  65.9 5.3 %collective-permute-done.10 = bf16[128,768]{1,0:T(8,128)(2,1)S(1)} collective-permute-done((bf16[128,768]{1,0:T(8,128)(2,1)S(1)}, bf16[128,768]{1,0:T(8,128)(2,1)S(1)}, u32[]{:S(2)}, u32[]{:S(2)}) %collective-permute-start.10) | collective-permute-done | bytes 196640 | tf_op jit(solution)/shard_map/weight_rings/ppermute | solution.py:22
  71.2 1.0 collective-permute-done.9.refs_9_
  72.2 3.0 %collective-permute-done.8.refs_8_ = bf16[512,768]{1,0:T(8,128)(2,1)S(1)} collective-permute-done((bf16[512,768]{1,0:T(8,128)(2,1)S(1)}, bf16[512,768]{1,0:T(8,128)(2,1)S(1)}, u32[]{:S(2)}, u32[]{:S(2)}) %collective-permute-start.8) | collective-permute-done | bytes 786464 | tf_op jit(solution)/shard_map/weight_rings/ppermute | solution.py:22
  75.2 0.8 slice.27
  76.0 0.8 slice.26
  76.7 2.7 %collective-permute-start.13 = (bf16[256,768]{1,0:T(8,128)(2,1)}, bf16[256,768]{1,0:T(8,128)(2,1)}, u32[]{:S(2)}, u32[]{:S(2)}) collective-permute-start(bf16[256,768]{1,0:T(8,128)(2,1)} %slice.27), channel_id=1, source_target_pairs={{0,192},{64,0},{128,64},{192,128},{1,193},{65,1},{129,65},{193,129... | collective-permute-start | bytes 1179656 | tf_op jit(solution)/shard_map/weight_rings/ppermute | solution.py:22
  79.4 0.7 constant_dynamic-update-slice_fusion.5
  80.1 0.7 constant_dynamic-update-slice_fusion.4.refs_5_
  80.8 1.2 collective-permute-start.15
  82.0 0.3 collective-permute-start.14
  82.3 0.1 stack.23.refs_0_.pos
  82.4 1.9 %all-gather.5.cloned.1.call-done.refs_2_ = bf16[2176,512]{1,0:T(8,128)(2,1)} async-done(((bf16[272,512]{1,0:T(8,128)(2,1)}), bf16[2176,512]{1,0:T(8,128)(2,1)}) %all-gather.5.cloned.1.call-update) | async-done | bytes 2228240 | tf_op jit(solution)/shard_map/token_gather/all_gather | solution.py:226
  84.3 1.6 %copy-done = bf16[2176,512]{1,0:T(8,128)(2,1)S(1)} copy-done((bf16[2176,512]{1,0:T(8,128)(2,1)S(1)}, bf16[2176,512]{1,0:T(8,128)(2,1)}, u32[]{:S(2)}) %copy-start) | copy-done | bytes 2228248
  85.9 1.6 %copy-done.2 = bf16[2176,512]{1,0:T(8,128)(2,1)S(1)} copy-done((bf16[2176,512]{1,0:T(8,128)(2,1)S(1)}, bf16[2176,512]{1,0:T(8,128)(2,1)}, u32[]{:S(2)}) %copy-start.2) | copy-done | bytes 2228248
  87.5 0.9 copy-done.7
  88.5 0.9 copy-done.9
  89.4 6.5 %project.1.refs_8_ = f32[6,528,128]{2,1,0:T(8,128)S(1)} custom-call(s32[5]{0:T(128)S(1)} %stack.23.refs_0_.pos, bf16[2176,512]{1,0:T(8,128)(2,1)S(1)} %copy-done, bf16[2176,512]{1,0:T(8,128)(2,1)S(1)} %copy-done.2, bf16[256,768]{1,0:T(8,128)(2,1)S(1)} %bitcast.17, bf16[512,768]{1,0:T(8,128)(2,1)S(1)} %constant_dynamic-update-slice_fusion.2.refs_4_, ...), custom_call_target="tpu_custom_call" | custom-call | flops 2283798528 | bytes 9000000 | tf_op jit(solution)/shard_map/project/pallas_call | solution.py:269
  95.9 0.0 copy-start.5
  95.9 0.0 copy-start.10
  95.9 0.0 copy-start.12
  96.0 5.9 %collective-permute-done.15.refs_6_ = bf16[256,768]{1,0:T(8,128)(2,1)} collective-permute-done((bf16[256,768]{1,0:T(8,128)(2,1)}, bf16[256,768]{1,0:T(8,128)(2,1)}, u32[]{:S(2)}, u32[]{:S(2)}) %collective-permute-start.15) | collective-permute-done | bytes 393248 | tf_op jit(solution)/shard_map/weight_rings/ppermute | solution.py:22
  101.9 1.0 collective-permute-done.14.refs_5_
  102.8 5.9 %states.1 = (f32[64,8,256]{2,1,0:T(8,128)S(1)}, f32[64,8,256]{2,1,0:T(8,128)S(1)}, f32[16,8,256]{2,1,0:T(8,128)S(1)}, f32[16,256]{1,0:T(8,128)S(1)}) custom-call(s32[5]{0:T(128)S(1)} %stack.23.refs_0_.pos, bf16[2176,512]{1,0:T(8,128)(2,1)S(1)} %copy-done.1, bf16[2176,512]{1,0:T(8,128)(2,1)S(1)} %copy-done.3, ...), custom_call_target="tpu_custom_call" | custom-call | tf_op jit(solution)/shard_map/states/pallas_call | solution.py:282
  108.7 0.7 broadcast_in_dim.3
  109.4 8.1 %all-to-all-start.1 = ((f32[16,16,256]{2,1,0:T(8,128)}), f32[16,16,256]{2,1,0:T(8,128)S(1)}, u32[]{:S(2)}, u32[]{:S(2)}) async-start(f32[16,16,256]{2,1,0:T(8,128)} %broadcast_in_dim.3), calls=%async_computation.1 | async-start | bytes 524288 | tf_op jit(solution)/shard_map/state_exchange/all_to_all | solution.py:298
  117.6 1.9 %local.1 = f32[64,8,256]{2,1,0:T(8,128)S(1)} custom-call(s32[5]{0:T(128)S(1)} %stack.23.refs_0_.pos, f32[64,8,256]{2,1,0:T(8,128)S(1)} %get-tuple-element.32.product, f32[16,512]{1,0:T(8,128)S(1)} %copy-done.10, f32[16,512]{1,0:T(8,128)S(1)} %copy-done.5, f32[1,512]{1,0:T(1,128)S(1)} %bitcast.18), custom_call_target="tpu_custom_call" | custom-call | flops 20000000 | bytes 1000000 | tf_op jit(solution)/shard_map/local/pallas_call | solution.py:301
  119.5 9.4 %all-to-all-done.1.states = f32[16,16,256]{2,1,0:T(8,128)S(1)} async-done(((f32[16,16,256]{2,1,0:T(8,128)}), f32[16,16,256]{2,1,0:T(8,128)S(1)}, u32[]{:S(2)}, u32[]{:S(2)}) %all-to-all-start.1) | async-done | bytes 262176 | tf_op jit(solution)/shard_map/state_exchange/all_to_all | solution.py:298
  128.9 1.5 %finish.1 = bf16[2,256,256]{2,1,0:T(8,128)(2,1)S(1)} custom-call(s32[5]{0:T(128)S(1)} %stack.23.refs_0_.pos, f32[64,8,256]{2,1,0:T(8,128)S(1)} %get-tuple-element.31.gate, f32[64,8,256]{2,1,0:T(8,128)S(1)} %local.1, f32[16,8,256]{2,1,0:T(8,128)S(1)} %get-tuple-element.33.inside, f32[16,16,256]{2,1,0:T(8,128)S(1)} %all-to-all-done.1.states, ...), custom_call_target="tpu_custom_call" | custom-call | tf_op jit(solution)/shard_map/finish/pallas_call | solution.py:310
  130.4 8.3 %all_to_all.16 = bf16[2,256,256]{2,1,0:T(8,128)(2,1)S(1)} all-to-all(bf16[2,256,256]{2,1,0:T(8,128)(2,1)S(1)} %finish.1), channel_id=1, replica_groups=mesh['y'=4,'h'=4,'c'=2,'l'=2,'x'=4] {'c'}, dimensions={0} | all-to-all | bytes 524288 | tf_op jit(solution)/shard_map/result_swap/all_to_all | solution.py:320
  138.7 0.1 copy.14
  138.8 0.8 copy.15
  (40 shorter events, 0.2 us)
Async XLA Ops:
  6.5 75.8 %all-gather.3.cloned.1.call-start = ((), (), s32[]{:S(2)}) async-start(), calls=%async_computation.3 | async-start | bytes 2506752 | tf_op jit(solution)/shard_map/token_gather/all_gather | solution.py:225
  7.3 7.1 %collective-permute-start = (bf16[16,512]{1,0:T(8,128)(2,1)S(1)}, bf16[16,512]{1,0:T(8,128)(2,1)S(1)}, u32[]{:S(2)}, u32[]{:S(2)}) collective-permute-start(bf16[16,512]{1,0:T(8,128)(2,1)S(1)} %slice.21), channel_id=1, source_target_pairs={{8,16},{24,32},{40,48},{56,64},{72,80},{88,96},{104,112},{120,128}... | collective-permute-start | bytes 49160 | tf_op jit(solution)/shard_map/token_swap/ppermute | solution.py:219
  15.4 0.7 copy-start.15
  16.1 14.4 %copy-start.16 = (bf16[272,512]{1,0:T(8,128)(2,1)S(1)}, bf16[272,512]{1,0:T(8,128)(2,1)}, u32[]{:S(2)}) copy-start(bf16[272,512]{1,0:T(8,128)(2,1)} %copy-done.15) | copy-start | bytes 835588
  16.1 68.1 %all-gather.5.cloned.1.call-start = ((), (), s32[]{:S(2)}) async-start(), calls=%async_computation.4 | async-start | bytes 2506752 | tf_op jit(solution)/shard_map/token_gather/all_gather | solution.py:226
  21.4 14.0 %collective-permute-start.4 = (bf16[256,768]{1,0:T(8,128)(2,1)S(1)}, bf16[256,768]{1,0:T(8,128)(2,1)S(1)}, u32[]{:S(2)}, u32[]{:S(2)}) collective-permute-start(bf16[256,768]{1,0:T(8,128)(2,1)S(1)} %bitcast.13), channel_id=1, source_target_pairs={{0,192},{64,0},{128,64},{192,128},{1,193},{65,1},{129,65},{193,129... | collective-permute-start | bytes 1179656 | tf_op jit(solution)/shard_map/weight_gather/ppermute | solution.py:22
  27.2 11.6 %collective-permute-start.3 = (bf16[256,768]{1,0:T(8,128)(2,1)S(1)}, bf16[256,768]{1,0:T(8,128)(2,1)S(1)}, u32[]{:S(2)}, u32[]{:S(2)}) collective-permute-start(bf16[256,768]{1,0:T(8,128)(2,1)S(1)} %bitcast.14), channel_id=1, source_target_pairs={{0,64},{64,128},{128,192},{192,0},{1,65},{65,129},{129,193},{193,1... | collective-permute-start | bytes 1179656 | tf_op jit(solution)/shard_map/weight_gather/ppermute | solution.py:22
  27.2 26.2 %collective-permute-start.2 = (bf16[256,768]{1,0:T(8,128)(2,1)S(1)}, bf16[256,768]{1,0:T(8,128)(2,1)S(1)}, u32[]{:S(2)}, u32[]{:S(2)}) collective-permute-start(bf16[256,768]{1,0:T(8,128)(2,1)S(1)} %bitcast.15), channel_id=1, source_target_pairs={{0,48},{16,0},{32,16},{48,32},{1,49},{17,1},{33,17},{49,33},{2,50}... | collective-permute-start | bytes 1179656 | tf_op jit(solution)/shard_map/weight_gather/ppermute | solution.py:22
  30.5 22.9 %collective-permute-start.1 = (bf16[256,768]{1,0:T(8,128)(2,1)S(1)}, bf16[256,768]{1,0:T(8,128)(2,1)S(1)}, u32[]{:S(2)}, u32[]{:S(2)}) collective-permute-start(bf16[256,768]{1,0:T(8,128)(2,1)S(1)} %bitcast.16), channel_id=1, source_target_pairs={{0,16},{16,32},{32,48},{48,0},{1,17},{17,33},{33,49},{49,1},{2,18}... | collective-permute-start | bytes 1179656 | tf_op jit(solution)/shard_map/weight_gather/ppermute | solution.py:22
  30.5 22.9 %collective-permute-start.7 = (bf16[272,512]{1,0:T(8,128)(2,1)S(1)}, bf16[272,512]{1,0:T(8,128)(2,1)S(1)}, u32[]{:S(2)}, u32[]{:S(2)}) collective-permute-start(bf16[272,512]{1,0:T(8,128)(2,1)S(1)} %copy-done.16), channel_id=1, source_target_pairs={{0,4},{4,0},{1,5},{5,1},{2,6},{6,2},{3,7},{7,3},{8,12},{12,8},{9,1... | collective-permute-start | bytes 835592 | tf_op jit(solution)/shard_map/token_swap/ppermute | solution.py:221
  35.4 18.1 %collective-permute-start.6 = (bf16[128,768]{1,0:T(8,128)(2,1)S(1)}, bf16[128,768]{1,0:T(8,128)(2,1)S(1)}, u32[]{:S(2)}, u32[]{:S(2)}) collective-permute-start(bf16[128,768]{1,0:T(8,128)(2,1)S(1)} %slice.29), channel_id=1, source_target_pairs={{0,192},{64,0},{128,64},{192,128},{1,193},{65,1},{129,65},{193,129... | collective-permute-start | bytes 589832 | tf_op jit(solution)/shard_map/ppermute | solution.py:22
  38.9 14.6 %collective-permute-start.5 = (bf16[128,768]{1,0:T(8,128)(2,1)S(1)}, bf16[128,768]{1,0:T(8,128)(2,1)S(1)}, u32[]{:S(2)}, u32[]{:S(2)}) collective-permute-start(bf16[128,768]{1,0:T(8,128)(2,1)S(1)} %slice.28), channel_id=1, source_target_pairs={{0,64},{64,128},{128,192},{192,0},{1,65},{65,129},{129,193},{193,1... | collective-permute-start | bytes 589832 | tf_op jit(solution)/shard_map/ppermute | solution.py:22
  53.4 0.9 copy-start.17
  53.4 1.0 copy-start.13
  53.4 1.1 copy-start.14
  53.5 1.0 copy-start.6
  53.5 1.0 copy-start.8
  54.5 17.7 %collective-permute-start.9 = (bf16[512,768]{1,0:T(8,128)(2,1)S(1)}, bf16[512,768]{1,0:T(8,128)(2,1)S(1)}, u32[]{:S(2)}, u32[]{:S(2)}) collective-permute-start(bf16[512,768]{1,0:T(8,128)(2,1)S(1)} %constant_dynamic-update-slice_fusion.2.refs_4_), channel_id=1, source_target_pairs={{0,192},{64,0},{128,64},{192,128},{1,193},{65,1},{129,65},{193,129... | collective-permute-start | bytes 2359304 | tf_op jit(solution)/shard_map/weight_rings/ppermute | solution.py:22
  56.9 18.3 %collective-permute-start.8 = (bf16[512,768]{1,0:T(8,128)(2,1)S(1)}, bf16[512,768]{1,0:T(8,128)(2,1)S(1)}, u32[]{:S(2)}, u32[]{:S(2)}) collective-permute-start(bf16[512,768]{1,0:T(8,128)(2,1)S(1)} %constant_dynamic-update-slice_fusion.2.refs_4_), channel_id=1, source_target_pairs={{0,64},{64,128},{128,192},{192,0},{1,65},{65,129},{129,193},{193,1... | collective-permute-start | bytes 2359304 | tf_op jit(solution)/shard_map/weight_rings/ppermute | solution.py:22
  58.8 7.1 %collective-permute-start.11 = (bf16[128,768]{1,0:T(8,128)(2,1)S(1)}, bf16[128,768]{1,0:T(8,128)(2,1)S(1)}, u32[]{:S(2)}, u32[]{:S(2)}) collective-permute-start(bf16[128,768]{1,0:T(8,128)(2,1)S(1)} %slice.25), channel_id=1, source_target_pairs={{0,48},{16,0},{32,16},{48,32},{1,49},{17,1},{33,17},{49,33},{2,50}... | collective-permute-start | bytes 589832 | tf_op jit(solution)/shard_map/weight_rings/ppermute | solution.py:22
  62.7 8.5 %collective-permute-start.10 = (bf16[128,768]{1,0:T(8,128)(2,1)S(1)}, bf16[128,768]{1,0:T(8,128)(2,1)S(1)}, u32[]{:S(2)}, u32[]{:S(2)}) collective-permute-start(bf16[128,768]{1,0:T(8,128)(2,1)S(1)} %slice.24), channel_id=1, source_target_pairs={{0,16},{16,32},{32,48},{48,0},{1,17},{17,33},{33,49},{49,1},{2,18}... | collective-permute-start | bytes 589832 | tf_op jit(solution)/shard_map/weight_rings/ppermute | solution.py:22
  76.7 19.2 %collective-permute-start.12 = (bf16[256,768]{1,0:T(8,128)(2,1)}, bf16[256,768]{1,0:T(8,128)(2,1)}, u32[]{:S(2)}, u32[]{:S(2)}) collective-permute-start(bf16[256,768]{1,0:T(8,128)(2,1)} %slice.26), channel_id=1, source_target_pairs={{0,64},{64,128},{128,192},{192,0},{1,65},{65,129},{129,193},{193,1... | collective-permute-start | bytes 1179656 | tf_op jit(solution)/shard_map/weight_rings/ppermute | solution.py:22
  76.7 19.2 %collective-permute-start.13 = (bf16[256,768]{1,0:T(8,128)(2,1)}, bf16[256,768]{1,0:T(8,128)(2,1)}, u32[]{:S(2)}, u32[]{:S(2)}) collective-permute-start(bf16[256,768]{1,0:T(8,128)(2,1)} %slice.27), channel_id=1, source_target_pairs={{0,192},{64,0},{128,64},{192,128},{1,193},{65,1},{129,65},{193,129... | collective-permute-start | bytes 1179656 | tf_op jit(solution)/shard_map/weight_rings/ppermute | solution.py:22
  80.8 15.2 %collective-permute-start.16 = (bf16[256,768]{1,0:T(8,128)(2,1)}, bf16[256,768]{1,0:T(8,128)(2,1)}, u32[]{:S(2)}, u32[]{:S(2)}) collective-permute-start(bf16[256,768]{1,0:T(8,128)(2,1)} %constant_dynamic-update-slice_fusion.4.refs_5_), channel_id=1, source_target_pairs={{0,128},{64,192},{128,0},{192,64},{1,129},{65,193},{129,1},{193,65... | collective-permute-start | bytes 1179656 | tf_op jit(solution)/shard_map/weight_rings/ppermute | solution.py:22
  80.8 21.1 %collective-permute-start.15 = (bf16[256,768]{1,0:T(8,128)(2,1)}, bf16[256,768]{1,0:T(8,128)(2,1)}, u32[]{:S(2)}, u32[]{:S(2)}) collective-permute-start(bf16[256,768]{1,0:T(8,128)(2,1)} %constant_dynamic-update-slice_fusion.4.refs_5_), channel_id=1, source_target_pairs={{0,192},{64,0},{128,64},{192,128},{1,193},{65,1},{129,65},{193,129... | collective-permute-start | bytes 1179656 | tf_op jit(solution)/shard_map/weight_rings/ppermute | solution.py:22
  82.0 20.8 %collective-permute-start.14 = (bf16[256,768]{1,0:T(8,128)(2,1)}, bf16[256,768]{1,0:T(8,128)(2,1)}, u32[]{:S(2)}, u32[]{:S(2)}) collective-permute-start(bf16[256,768]{1,0:T(8,128)(2,1)} %constant_dynamic-update-slice_fusion.4.refs_5_), channel_id=1, source_target_pairs={{0,64},{64,128},{128,192},{192,0},{1,65},{65,129},{129,193},{193,1... | collective-permute-start | bytes 1179656 | tf_op jit(solution)/shard_map/weight_rings/ppermute | solution.py:22
  84.3 1.6 %copy-start = (bf16[2176,512]{1,0:T(8,128)(2,1)S(1)}, bf16[2176,512]{1,0:T(8,128)(2,1)}, u32[]{:S(2)}) copy-start(bf16[2176,512]{1,0:T(8,128)(2,1)} %all-gather.3.cloned.1.call-done.refs_1_) | copy-start | bytes 6684676
  85.9 1.6 %copy-start.2 = (bf16[2176,512]{1,0:T(8,128)(2,1)S(1)}, bf16[2176,512]{1,0:T(8,128)(2,1)}, u32[]{:S(2)}) copy-start(bf16[2176,512]{1,0:T(8,128)(2,1)} %all-gather.5.cloned.1.call-done.refs_2_) | copy-start | bytes 6684676
  87.5 0.9 copy-start.7
  88.5 0.9 copy-start.9
  89.4 13.5 %copy-start.1 = (bf16[2176,512]{1,0:T(8,128)(2,1)S(1)}, bf16[2176,512]{1,0:T(8,128)(2,1)}, u32[]{:S(2)}) copy-start(bf16[2176,512]{1,0:T(8,128)(2,1)} %all-gather.3.cloned.1.call-done.refs_1_) | copy-start | bytes 6684676
  89.4 13.5 %copy-start.3 = (bf16[2176,512]{1,0:T(8,128)(2,1)S(1)}, bf16[2176,512]{1,0:T(8,128)(2,1)}, u32[]{:S(2)}) copy-start(bf16[2176,512]{1,0:T(8,128)(2,1)} %all-gather.5.cloned.1.call-done.refs_2_) | copy-start | bytes 6684676
  89.4 13.5 %copy-start.4 = (f32[16,512]{1,0:T(8,128)S(1)}, f32[16,512]{1,0:T(8,128)}, u32[]{:S(2)}) copy-start(f32[16,512]{1,0:T(8,128)} %decay.3) | copy-start | bytes 98308
  89.4 13.5 %copy-start.11 = (f32[3,3,512]{2,1,0:T(4,128)S(1)}, f32[3,3,512]{2,1,0:T(4,128)}, u32[]{:S(2)}) copy-start(f32[3,3,512]{2,1,0:T(4,128)} %refs_9_.1) | copy-start | bytes 55300
  95.9 21.7 %copy-start.5 = (f32[16,512]{1,0:T(8,128)S(1)}, f32[16,512]{1,0:T(8,128)}, u32[]{:S(2)}) copy-start(f32[16,512]{1,0:T(8,128)} %decay.3) | copy-start | bytes 98308
  95.9 21.7 %copy-start.10 = (f32[16,512]{1,0:T(8,128)S(1)}, f32[16,512]{1,0:T(8,128)}, u32[]{:S(2)}) copy-start(f32[16,512]{1,0:T(8,128)} %gain.3) | copy-start | bytes 98308
  95.9 21.7 %copy-start.12 = (f32[512]{0:T(512)S(1)}, f32[512]{0:T(512)}, u32[]{:S(2)}) copy-start(f32[512]{0:T(512)} %param.11) | copy-start | bytes 6148
  109.4 19.4 %all-to-all-start.1 = ((f32[16,16,256]{2,1,0:T(8,128)}), f32[16,16,256]{2,1,0:T(8,128)S(1)}, u32[]{:S(2)}, u32[]{:S(2)}) async-start(f32[16,16,256]{2,1,0:T(8,128)} %broadcast_in_dim.3), calls=%async_computation.1 | async-start | bytes 524288 | tf_op jit(solution)/shard_map/state_exchange/all_to_all | solution.py:298
Sparse Core Ops, SparseCore 0:
  16.2 32.1 all-gather.2
  54.5 29.7 all-gather.4

commit v6 on v5

--- a/solution.py
+++ b/solution.py
@@ -31,36 +31,31 @@
     return shifted(behind[:half], axis, 1), shifted(ahead[half:], axis, -1)
 
 
-def fetched(sizes, pos, tokens, pieces, blocks, tokv, wv, sem):
+def fetched(sizes, pos, tok, pieces, blocks, tokv, wv, sem):
     rows, depth, width, modes, seq = sizes
     k = depth // 16
     lines = rows + HALO
     copies, at, seen = [], 0, set()
 
-    def add(source, target):
+    def start(source, target):
         copies.append(pltpu.make_async_copy(source, target, sem.at[len(copies)]))
-        return copies[-1]
+        copies[-1].start()
 
     for piece, first, n, dy, dh, skip in blocks:
-        add(pieces[piece].at[pl.ds(first, n), :], wv.at[pl.ds(at + skip, n), :]).start()
+        start(pieces[piece].at[pl.ds(first, n), :], wv.at[pl.ds(at + skip, n), :])
         if (dy, dh) not in seen:
             seen.add((dy, dh))
             ys, hs = lax.rem(pos[1] - dy + 4, 4), lax.rem(pos[2] - dh + 4, 4)
             ch = 2 * ys + lax.div(hs, 2)
             lanes = pl.ds(pl.multiple_of(lax.rem(hs, 2) * k, k), k)
-            x = lax.rem(ch, 4)
-            swapped = lax.rem(lax.div(ch, 4) + pos[4], 2)
-            to = pl.ds(at, k)
+            part = 2 * lax.rem(ch, 4) + lax.rem(lax.div(ch, 4) + pos[4], 2)
             for core in range(2):
                 skipped = HALO * core
-                line = pl.ds(
-                    pl.multiple_of((4 * core + x) * lines + skipped, HALO), lines - skipped
+                line = pl.multiple_of((8 * core + part) * lines + skipped, HALO)
+                start(
+                    tok.at[pl.ds(line, lines - skipped), lanes],
+                    tokv.at[pl.ds(core * lines, lines - skipped), pl.ds(at, k)],
                 )
-                target = tokv.at[pl.ds(core * lines, lines - skipped), to]
-                copy = add(tokens[0].at[line, lanes], target)
-                pl.when(swapped == 0)(copy.start)
-                copy = pltpu.make_async_copy(tokens[1].at[line, lanes], target, sem.at[len(copies) - 1])
-                pl.when(swapped == 1)(copy.start)
         if skip + n == k:
             at += k
     return copies
@@ -68,9 +63,9 @@
 
 def project_kernel(sizes, blocks, *refs):
     rows, depth, width, modes, seq = sizes
-    pos, near, swapped, *pieces = refs[:-4]
+    pos, tok, *pieces = refs[:-4]
     sums, tokv, wv, sem = refs[-4:]
-    for copy in fetched(sizes, pos, (near, swapped), pieces, blocks, tokv, wv, sem):
+    for copy in fetched(sizes, pos, tok, pieces, blocks, tokv, wv, sem):
         copy.wait()
 
     @pl.loop(0, 3)
@@ -83,10 +78,10 @@
 
 def state_kernel(sizes, blocks, *refs):
     rows, depth, width, modes, seq = sizes
-    pos, near, swapped, *pieces = refs[:-11]
+    pos, tok, *pieces = refs[:-11]
     sums, taps, decay, gate, product, inside, state, tokv, wv, acc, sem = refs[-11:]
     c = pos[3]
-    for copy in fetched(sizes, pos, (near, swapped), pieces, blocks, tokv, wv, sem):
+    for copy in fetched(sizes, pos, tok, pieces, blocks, tokv, wv, sem):
         copy.wait()
 
     @pl.loop(0, 3)
@@ -214,27 +209,34 @@
     with jax.named_scope("weight_gather"):
         halves = w_in.reshape(k, 3, 2, width).transpose(2, 0, 1, 3).reshape(2, k, 3 * width)
         own = lax.all_to_all(halves, "c", 0, 0, tiled=True).reshape(2 * k, 3 * width)
-        beside, far = both_ways(own, "h"), both_ways(own, "y")
+        tail, own = tie((tokens[rows - HALO :], own))
     with jax.named_scope("token_swap"):
-        halo = lax.ppermute(tokens[rows - HALO :], CTX, [(i, i + 1) for i in range(1, 31, 2)])
-        tokens = jnp.concatenate([halo, tokens], 0)
         other = lax.ppermute(tokens, "l", [(0, 1), (1, 0)])
-    farther = onward(*far, "y")
-    beside, far, farther, other = tie((beside, far, farther, other))
+        route = [(4 * r + 2 + side, 4 * r + 4 + side) for r in range(15) for side in range(2)]
+        halo = lax.ppermute(tail, (*CTX, "l"), route)
+        other_halo = lax.ppermute(tail, (*CTX, "l"), [(i, j ^ 1) for i, j in route])
+    with jax.named_scope("weight_rings"):
+        farther = shifted(own, "y", 2)
+        far = both_ways(own, "y")
+        beside = both_ways(own, "h")
+    first = (halo, other_halo, other, farther, far, beside)
+    halo, other_halo, other, farther, far, beside = tie(first)
     with jax.named_scope("token_gather"):
-        near = lax.all_gather(tokens, ("c", "x"), axis=0, tiled=True)
-        swapped = lax.all_gather(other, ("c", "x"), axis=0, tiled=True)
+        wide = jnp.concatenate([halo, tokens, other_halo, other], 0)
+        tok = lax.all_gather(wide, ("c", "x"), axis=0, tiled=True)
     with jax.named_scope("weight_rings"):
+        two, half = 2 * k, k
         pair = jnp.concatenate(beside, 0)
         far_pair, opposite = both_ways(pair, "y"), onward(*beside, "h")
         far_pair, opposite = tie((far_pair, opposite))
         opposite = jnp.concatenate(opposite, 0)
-        far_opposite, farther_pair = both_ways(opposite, "y"), onward(*far_pair, "y")
         last = shifted(opposite, "y", 2)
-
-    two = 2 * k
-    half = k
-    early = [own, pair, opposite, *far, *far_pair, *farther]
+        farther_pair = onward(*far_pair, "y")
+        firsts = jnp.concatenate([p[:half] for p in far_pair], 0)
+        seconds = jnp.concatenate([p[two + half :] for p in far_pair], 0)
+        far_opposite = shifted(firsts, "h", 1), shifted(seconds, "h", -1)
+
+    early = [own, pair, opposite, *far, *far_pair, farther]
     early_blocks = [(0, 0, two, 0, 0, 0), (1, 0, two, 0, 1, 0), (1, two, two, 0, -1, 0), (2, 0, two, 0, 2, 0)]
     for side, dy in enumerate((1, -1)):
         early_blocks += [
@@ -242,13 +244,15 @@
             (5 + side, 0, two, dy, 1, 0),
             (5 + side, two, two, dy, -1, 0),
         ]
-    early_blocks += [(7, 0, half, 2, 0, 0), (8, 0, half, 2, 0, half)]
+    early_blocks += [(7, 0, two, 2, 0, 0)]
     late = [*farther_pair, *far_opposite, last]
     late_blocks = [
         (0, 0, two, 2, 1, 0),
         (1, 0, two, 2, -1, 0),
-        (2, 0, two, 1, 2, 0),
-        (3, 0, two, -1, 2, 0),
+        (2, 0, half, 1, 2, 0),
+        (3, 0, half, 1, 2, half),
+        (2, half, half, -1, 2, 0),
+        (3, half, half, -1, 2, half),
         (4, 0, two, 2, 2, 0),
     ]
 
@@ -269,7 +273,7 @@
     sums = pl.pallas_call(
         functools.partial(project_kernel, sizes, early_blocks),
         out_shape=jax.ShapeDtypeStruct(chunks, F32),
-        in_specs=[smem] + [hbm] * (2 + len(early)),
+        in_specs=[smem] + [hbm] * (1 + len(early)),
         out_specs=vmem,
         scratch_shapes=[*held(11), sems(early_blocks, 11)],
         compiler_params=pltpu.CompilerParams(vmem_limit_bytes=14 * 2**20),
@@ -277,7 +281,7 @@
             flops=2 * lines * 11 * two * 3 * width, bytes_accessed=9_000_000, transcendentals=0
         ),
         name="project",
-    )(pos, near, swapped, *early)
+    )(pos, tok, *early)
     params = pltpu.CompilerParams(vmem_limit_bytes=12 * 2**20)
     gate, product, inside, state = pl.pallas_call(
         functools.partial(state_kernel, sizes, late_blocks),
@@ -287,12 +291,12 @@
             jax.ShapeDtypeStruct((modes, SUB, width), F32),
             jax.ShapeDtypeStruct((modes, width), F32),
         ),
-        in_specs=[smem] + [hbm] * (2 + len(late)) + [vmem] * 3,
+        in_specs=[smem] + [hbm] * (1 + len(late)) + [vmem] * 3,
         out_specs=(vmem,) * 4,
         scratch_shapes=[*held(5), pltpu.VMEM(chunks, F32), sems(late_blocks, 5)],
         compiler_params=params,
         name="states",
-    )(pos, near, swapped, *late, sums, taps, decay)
+    )(pos, tok, *late, sums, taps, decay)
 
     with jax.named_scope("state_exchange"):
         states = lax.all_to_all(

time: 147 us -> 141 us (0.959)
  blocking collectives: 12 us -> 5.7 us
  local copies, waits for them, and re-layouts: 16.7 us -> 13.2 us
  other arithmetic: 0 us -> 2.42 us
  starting transfers between devices: 38.3 us -> 40.5 us
    ppermute x1, waiting for transfers between devices: 14.5 us -> 0.01 us  [body(): other = lax.ppermute(tokens, 'l', [(0, 1), (1, 0)])]
    ppermute x15 -> x14, waiting for transfers between devices: 23.4 us -> 34.1 us  [shifted(): return lax.ppermute(array, axis, [(i, (i + step) % n) for i in range(n)])]
    ppermute x15 -> x14, starting transfers between devices: 23.1 us -> 18.6 us  [shifted(): return lax.ppermute(array, axis, [(i, (i + step) % n) for i in range(n)])]
    all_to_all x0 -> x1, starting transfers between devices: none -> 4.41 us  [body(): lax.all_to_all(halves, 'c', 0, 0, tiled=True).reshape(2 * k, 3 * width)]
    all_to_all x1 -> x0, blocking collectives: 3.69 us -> none  [body(): lax.all_to_all(halves, 'c', 0, 0, tiled=True).reshape(2 * k, 3 * width)]
    all_to_all x1, blocking collectives: 8.3 us -> 5.7 us  [body(): both = lax.all_to_all(out, 'c', 0, 0, tiled=True)]
    concatenate x0 -> x3, other arithmetic: none -> 2.42 us  [the longest x1 0.85 us: body(): wide = jnp.concatenate([halo, tokens, other_halo, other], 0)]
    all_gather x2 -> x1, waiting for transfers between devices: 1.91 us -> 3.96 us  [body(): tok = lax.all_gather(wide, ('c', 'x'), axis=0, tiled=True)]
where the time goes in v6:
time: 141 us
  waiting for transfers between devices  49.5 us (35%)
  starting transfers between devices  40.5 us (29%)
  Pallas kernels  15.8 us (11%)
  between operations  13.6 us (10%)
  local copies, waits for them, and re-layouts  13.2 us (9%)
  blocking collectives  5.7 us (4%)
  other arithmetic  2.42 us (2%)
    ppermute x14, waiting for transfers between devices, shifted(): return lax.ppermute(array, axis, [(i, (i + step) % n) for i in range(n)])  34.1 us
    ppermute x14, starting transfers between devices, shifted(): return lax.ppermute(array, axis, [(i, (i + step) % n) for i in range(n)])  18.6 us
    all_to_all x1, waiting for transfers between devices, body(): lax.all_to_all(jnp.broadcast_to(state, (16, *state.shape)), ('y', 'h'), 0...  10.1 us
    unnamed x31, local copies, waits for them, and re-layouts  8.78 us
    all_to_all x1, starting transfers between devices, body(): lax.all_to_all(jnp.broadcast_to(state, (16, *state.shape)), ('y', 'h'), 0...  8.53 us
    pallas_call x1, Pallas kernels, body(): pl.pallas_call(functools.partial(project_kernel, sizes, early_blocks), ou...  6.26 us
    pallas_call x1, Pallas kernels, body(): pl.pallas_call(functools.partial(state_kernel, sizes, late_blocks), out_s...  6.18 us
    all_to_all x1, blocking collectives, body(): both = lax.all_to_all(out, 'c', 0, 0, tiled=True)  5.7 us
  transfers between devices with their start and end apart: 20, of which 11 were waited for; matrix products, arithmetic and copies ran while one was open for 4% of the time, Pallas kernels for 6%

profile of v6, /device:TPU:1, one launch (start us, length us, event | category | flops | bytes accessed | tf_op | source)
XLA Modules:
  0.0 140.8 jit_solution(9748811401005246333)
XLA Ops:
  6.5 2.5 %collective-permute-start.2 = (bf16[256,512]{1,0:T(8,128)(2,1)}, bf16[256,512]{1,0:T(8,128)(2,1)S(1)}, u32[]{:S(2)}, u32[]{:S(2)}) collective-permute-start(bf16[256,512]{1,0:T(8,128)(2,1)} %param.6), channel_id=1, source_target_pairs={{0,4},{4,0},{1,5},{5,1},{2,6},{6,2},{3,7},{7,3},{8,12},{12,8},{9,1... | collective-permute-start | bytes 786440 | tf_op jit(solution)/shard_map/token_swap/ppermute | solution.py:214
  9.0 1.2 copy.11
  10.2 0.8 copy.12
  11.0 4.4 %all-to-all-start = ((bf16[2,128,768]{1,2,0:T(8,128)(2,1)}), bf16[2,128,768]{1,2,0:T(8,128)(2,1)S(1)}, u32[]{:S(2)}, u32[]{:S(2)}) async-start(bf16[2,128,768]{1,2,0:T(8,128)(2,1)} %bitcast.7), calls=%async_computation | async-start | bytes 786432 | tf_op jit(solution)/shard_map/weight_gather/all_to_all | solution.py:211
  15.4 1.3 all-to-all-done
  16.7 0.2 copy.13
  16.9 4.7 %collective-permute-start.1 = (bf16[16,512]{1,0:T(8,128)(2,1)S(1)}, bf16[16,512]{1,0:T(8,128)(2,1)S(1)}, u32[]{:S(2)}, u32[]{:S(2)}) collective-permute-start(bf16[16,512]{1,0:T(8,128)(2,1)S(1)} %slice.27), channel_id=1, source_target_pairs={{8,20},{12,16},{24,36},{28,32},{40,52},{44,48},{56,68},{60,64},{72... | collective-permute-start | bytes 49160 | tf_op jit(solution)/shard_map/token_swap/ppermute | solution.py:217
  21.6 1.7 %collective-permute-start = (bf16[16,512]{1,0:T(8,128)(2,1)S(1)}, bf16[16,512]{1,0:T(8,128)(2,1)S(1)}, u32[]{:S(2)}, u32[]{:S(2)}) collective-permute-start(bf16[16,512]{1,0:T(8,128)(2,1)S(1)} %slice.27), channel_id=1, source_target_pairs={{8,16},{12,20},{24,32},{28,36},{40,48},{44,52},{56,64},{60,68},{72... | collective-permute-start | bytes 49160 | tf_op jit(solution)/shard_map/token_swap/ppermute | solution.py:216
  23.3 1.7 %collective-permute-start.7 = (bf16[256,768]{1,0:T(8,128)(2,1)S(1)}, bf16[256,768]{1,0:T(8,128)(2,1)S(1)}, u32[]{:S(2)}, u32[]{:S(2)}) collective-permute-start(bf16[256,768]{1,0:T(8,128)(2,1)S(1)} %bitcast.13), channel_id=1, source_target_pairs={{0,48},{16,0},{32,16},{48,32},{1,49},{17,1},{33,17},{49,33},{2,50}... | collective-permute-start | bytes 1179656 | tf_op jit(solution)/shard_map/weight_rings/ppermute | solution.py:22
  25.0 2.2 %collective-permute-start.6 = (bf16[256,768]{1,0:T(8,128)(2,1)S(1)}, bf16[256,768]{1,0:T(8,128)(2,1)S(1)}, u32[]{:S(2)}, u32[]{:S(2)}) collective-permute-start(bf16[256,768]{1,0:T(8,128)(2,1)S(1)} %bitcast.14), channel_id=1, source_target_pairs={{0,16},{16,32},{32,48},{48,0},{1,17},{17,33},{33,49},{49,1},{2,18}... | collective-permute-start | bytes 1179656 | tf_op jit(solution)/shard_map/weight_rings/ppermute | solution.py:22
  27.3 0.0 collective-permute-done.1
  27.3 2.7 %collective-permute-start.5 = (bf16[256,768]{1,0:T(8,128)(2,1)S(1)}, bf16[256,768]{1,0:T(8,128)(2,1)S(1)}, u32[]{:S(2)}, u32[]{:S(2)}) collective-permute-start(bf16[256,768]{1,0:T(8,128)(2,1)S(1)} %bitcast.15), channel_id=1, source_target_pairs={{0,192},{64,0},{128,64},{192,128},{1,193},{65,1},{129,65},{193,129... | collective-permute-start | bytes 1179656 | tf_op jit(solution)/shard_map/weight_rings/ppermute | solution.py:22
  30.0 0.0 collective-permute-start.4
  30.0 0.0 collective-permute-done.2
  30.0 1.6 %collective-permute-start.3 = (bf16[256,768]{1,0:T(8,128)(2,1)S(1)}, bf16[256,768]{1,0:T(8,128)(2,1)S(1)}, u32[]{:S(2)}, u32[]{:S(2)}) collective-permute-start(bf16[256,768]{1,0:T(8,128)(2,1)S(1)} %bitcast.17), channel_id=1, source_target_pairs={{0,128},{64,192},{128,0},{192,64},{1,129},{65,193},{129,1},{193,65... | collective-permute-start | bytes 1179656 | tf_op jit(solution)/shard_map/weight_rings/ppermute | solution.py:22
  31.7 9.2 %collective-permute-done.7 = bf16[256,768]{1,0:T(8,128)(2,1)S(1)} collective-permute-done((bf16[256,768]{1,0:T(8,128)(2,1)S(1)}, bf16[256,768]{1,0:T(8,128)(2,1)S(1)}, u32[]{:S(2)}, u32[]{:S(2)}) %collective-permute-start.7) | collective-permute-done | bytes 393248 | tf_op jit(solution)/shard_map/weight_rings/ppermute | solution.py:22
  40.9 5.6 %collective-permute-done.6 = bf16[256,768]{1,0:T(8,128)(2,1)S(1)} collective-permute-done((bf16[256,768]{1,0:T(8,128)(2,1)S(1)}, bf16[256,768]{1,0:T(8,128)(2,1)S(1)}, u32[]{:S(2)}, u32[]{:S(2)}) %collective-permute-start.6) | collective-permute-done | bytes 393248 | tf_op jit(solution)/shard_map/weight_rings/ppermute | solution.py:22
  46.5 0.0 collective-permute-done.5.refs_6_
  46.5 0.7 copy-done.2
  47.2 2.1 %collective-permute-done.4.refs_5_ = bf16[256,768]{1,0:T(8,128)(2,1)S(1)} collective-permute-done((bf16[256,768]{1,0:T(8,128)(2,1)S(1)}, bf16[256,768]{1,0:T(8,128)(2,1)S(1)}, u32[]{:S(2)}, u32[]{:S(2)}) %collective-permute-start.4) | collective-permute-done | bytes 393248 | tf_op jit(solution)/shard_map/weight_rings/ppermute | solution.py:22
  49.3 0.7 copy-done.4
  50.0 0.0 collective-permute-done.3.refs_9_
  50.0 0.8 copy-done.6
  50.8 0.8 pad_maximum_fusion
  51.7 0.0 all-gather.2.cloned.1.call-update
  51.7 0.7 collective-permute-start.9
  52.5 0.8 collective-permute-start.8
  53.3 0.4 collective-permute-start.11
  53.7 2.0 %collective-permute-start.10 = (bf16[128,768]{1,0:T(8,128)(2,1)S(1)}, bf16[128,768]{1,0:T(8,128)(2,1)S(1)}, u32[]{:S(2)}, u32[]{:S(2)}) collective-permute-start(bf16[128,768]{1,0:T(8,128)(2,1)S(1)} %slice.28), channel_id=1, source_target_pairs={{0,16},{16,32},{32,48},{48,0},{1,17},{17,33},{33,49},{49,1},{2,18}... | collective-permute-start | bytes 589832 | tf_op jit(solution)/shard_map/weight_rings/ppermute | solution.py:22
  55.8 9.3 %collective-permute-done.11 = bf16[128,768]{1,0:T(8,128)(2,1)S(1)} collective-permute-done((bf16[128,768]{1,0:T(8,128)(2,1)S(1)}, bf16[128,768]{1,0:T(8,128)(2,1)S(1)}, u32[]{:S(2)}, u32[]{:S(2)}) %collective-permute-start.11) | collective-permute-done | bytes 196640 | tf_op jit(solution)/shard_map/weight_rings/ppermute | solution.py:22
  65.1 0.4 collective-permute-done.10
  65.5 5.4 %collective-permute-done.9.refs_8_ = bf16[512,768]{1,0:T(8,128)(2,1)S(1)} collective-permute-done((bf16[512,768]{1,0:T(8,128)(2,1)S(1)}, bf16[512,768]{1,0:T(8,128)(2,1)S(1)}, u32[]{:S(2)}, u32[]{:S(2)}) %collective-permute-start.9) | collective-permute-done | bytes 786464 | tf_op jit(solution)/shard_map/weight_rings/ppermute | solution.py:22
  70.9 1.3 collective-permute-done.8.refs_7_
  72.2 0.8 slice.30
  73.0 0.8 slice.31
  73.8 0.1 fusion
  73.8 0.8 pad_maximum_fusion.1
  74.6 0.1 collective-permute-start.14
  74.7 0.8 pad_maximum_fusion.2
  75.5 3.5 %collective-permute-start.15 = (bf16[256,768]{1,0:T(8,128)(2,1)}, bf16[256,768]{1,0:T(8,128)(2,1)}, u32[]{:S(2)}, u32[]{:S(2)}) collective-permute-start(bf16[256,768]{1,0:T(8,128)(2,1)} %pad_maximum_fusion.2), channel_id=1, source_target_pairs={{0,48},{16,0},{32,16},{48,32},{1,49},{17,1},{33,17},{49,33},{2,50}... | collective-permute-start | bytes 1179656 | tf_op jit(solution)/shard_map/weight_rings/ppermute | solution.py:22
  79.0 0.3 collective-permute-start.13
  79.3 1.1 collective-permute-start.12
  80.5 1.3 collective-permute-start.16
  81.8 0.1 stack.23.refs_0_.pos
  81.9 4.0 %all-gather.2.cloned.1.call-done.refs_1_ = bf16[4352,512]{1,0:T(8,128)(2,1)} async-done(((bf16[544,512]{1,0:T(8,128)(2,1)}), bf16[4352,512]{1,0:T(8,128)(2,1)}) %all-gather.2.cloned.1.call-update) | async-done | bytes 4456464 | tf_op jit(solution)/shard_map/token_gather/all_gather | solution.py:226
  85.8 2.3 %copy-done = bf16[4352,512]{1,0:T(8,128)(2,1)S(1)} copy-done((bf16[4352,512]{1,0:T(8,128)(2,1)S(1)}, bf16[4352,512]{1,0:T(8,128)(2,1)}, u32[]{:S(2)}) %copy-start) | copy-done | bytes 4456472
  88.1 1.0 copy-done.3
  89.1 1.0 copy-done.5
  90.1 1.0 copy-done.7
  91.1 6.3 %project.1.refs_7_ = f32[6,528,128]{2,1,0:T(8,128)S(1)} custom-call(s32[5]{0:T(128)S(1)} %stack.23.refs_0_.pos, bf16[4352,512]{1,0:T(8,128)(2,1)S(1)} %copy-done, bf16[256,768]{1,0:T(8,128)(2,1)S(1)} %bitcast.18, bf16[512,768]{1,0:T(8,128)(2,1)S(1)} %constant_dynamic-update-slice_fusion.refs_3_, ...), custom_call_target="tpu_custom_call" | custom-call | flops 2283798528 | bytes 9000000 | tf_op jit(solution)/shard_map/project/pallas_call | solution.py:273
  97.3 0.0 copy-start.9
  97.4 0.0 copy-start.10
  97.4 0.0 copy-start.12
  97.4 0.0 collective-permute-done.14.refs_4_
  97.4 0.8 collective-permute-done.16.refs_6_
  98.2 6.2 %states.1 = (f32[64,8,256]{2,1,0:T(8,128)S(1)}, f32[64,8,256]{2,1,0:T(8,128)S(1)}, f32[16,8,256]{2,1,0:T(8,128)S(1)}, f32[16,256]{1,0:T(8,128)S(1)}) custom-call(s32[5]{0:T(128)S(1)} %stack.23.refs_0_.pos, bf16[4352,512]{1,0:T(8,128)(2,1)S(1)} %copy-done.1, bf16[256,768]{1,0:T(8,128)(2,1)} %collective-permute-done.12.refs_2_, ...), custom_call_target="tpu_custom_call" | custom-call | tf_op jit(solution)/shard_map/states/pallas_call | solution.py:286
  104.4 0.7 broadcast_in_dim.3
  105.1 8.5 %all-to-all-start.1 = ((f32[16,16,256]{2,1,0:T(8,128)}), f32[16,16,256]{2,1,0:T(8,128)S(1)}, u32[]{:S(2)}, u32[]{:S(2)}) async-start(f32[16,16,256]{2,1,0:T(8,128)} %broadcast_in_dim.3), calls=%async_computation.1 | async-start | bytes 524288 | tf_op jit(solution)/shard_map/state_exchange/all_to_all | solution.py:302
  113.7 1.9 %local.1 = f32[64,8,256]{2,1,0:T(8,128)S(1)} custom-call(s32[5]{0:T(128)S(1)} %stack.23.refs_0_.pos, f32[64,8,256]{2,1,0:T(8,128)S(1)} %get-tuple-element.38.product, f32[16,512]{1,0:T(8,128)S(1)} %copy-done.10, f32[16,512]{1,0:T(8,128)S(1)} %copy-done.9, f32[1,512]{1,0:T(1,128)S(1)} %bitcast.19), custom_call_target="tpu_custom_call" | custom-call | flops 20000000 | bytes 1000000 | tf_op jit(solution)/shard_map/local/pallas_call | solution.py:305
  115.6 10.1 %all-to-all-done.1.states = f32[16,16,256]{2,1,0:T(8,128)S(1)} async-done(((f32[16,16,256]{2,1,0:T(8,128)}), f32[16,16,256]{2,1,0:T(8,128)S(1)}, u32[]{:S(2)}, u32[]{:S(2)}) %all-to-all-start.1) | async-done | bytes 262176 | tf_op jit(solution)/shard_map/state_exchange/all_to_all | solution.py:302
  125.7 1.5 %finish.1 = bf16[2,256,256]{2,1,0:T(8,128)(2,1)S(1)} custom-call(s32[5]{0:T(128)S(1)} %stack.23.refs_0_.pos, f32[64,8,256]{2,1,0:T(8,128)S(1)} %get-tuple-element.37.gate, f32[64,8,256]{2,1,0:T(8,128)S(1)} %local.1, f32[16,8,256]{2,1,0:T(8,128)S(1)} %get-tuple-element.39.inside, f32[16,16,256]{2,1,0:T(8,128)S(1)} %all-to-all-done.1.states, ...), custom_call_target="tpu_custom_call" | custom-call | tf_op jit(solution)/shard_map/finish/pallas_call | solution.py:314
  127.2 5.7 %all_to_all.15 = bf16[2,256,256]{2,1,0:T(8,128)(2,1)S(1)} all-to-all(bf16[2,256,256]{2,1,0:T(8,128)(2,1)S(1)} %finish.1), channel_id=1, replica_groups=mesh['y'=4,'h'=4,'c'=2,'l'=2,'x'=4] {'c'}, dimensions={0} | all-to-all | bytes 524288 | tf_op jit(solution)/shard_map/result_swap/all_to_all | solution.py:324
  132.9 0.1 copy.14
  133.1 0.8 copy.15
  (30 shorter events, 0.2 us)
Async XLA Ops:
  6.5 8.9 %copy-start.13 = (bf16[256,512]{1,0:T(8,128)(2,1)S(1)}, bf16[256,512]{1,0:T(8,128)(2,1)}, u32[]{:S(2)}) copy-start(bf16[256,512]{1,0:T(8,128)(2,1)} %param.6) | copy-start | bytes 786436
  6.5 23.5 %collective-permute-start.2 = (bf16[256,512]{1,0:T(8,128)(2,1)}, bf16[256,512]{1,0:T(8,128)(2,1)S(1)}, u32[]{:S(2)}, u32[]{:S(2)}) collective-permute-start(bf16[256,512]{1,0:T(8,128)(2,1)} %param.6), channel_id=1, source_target_pairs={{0,4},{4,0},{1,5},{5,1},{2,6},{6,2},{3,7},{7,3},{8,12},{12,8},{9,1... | collective-permute-start | bytes 786440 | tf_op jit(solution)/shard_map/token_swap/ppermute | solution.py:214
  11.0 5.7 %all-to-all-start = ((bf16[2,128,768]{1,2,0:T(8,128)(2,1)}), bf16[2,128,768]{1,2,0:T(8,128)(2,1)S(1)}, u32[]{:S(2)}, u32[]{:S(2)}) async-start(bf16[2,128,768]{1,2,0:T(8,128)(2,1)} %bitcast.7), calls=%async_computation | async-start | bytes 786432 | tf_op jit(solution)/shard_map/weight_gather/all_to_all | solution.py:211
  15.4 70.4 %all-gather.2.cloned.1.call-start = ((), (), s32[]{:S(2)}) async-start(), calls=%async_computation.3 | async-start | bytes 5013504 | tf_op jit(solution)/shard_map/token_gather/all_gather | solution.py:226
  16.9 10.4 %collective-permute-start.1 = (bf16[16,512]{1,0:T(8,128)(2,1)S(1)}, bf16[16,512]{1,0:T(8,128)(2,1)S(1)}, u32[]{:S(2)}, u32[]{:S(2)}) collective-permute-start(bf16[16,512]{1,0:T(8,128)(2,1)S(1)} %slice.27), channel_id=1, source_target_pairs={{8,20},{12,16},{24,36},{28,32},{40,52},{44,48},{56,68},{60,64},{72... | collective-permute-start | bytes 49160 | tf_op jit(solution)/shard_map/token_swap/ppermute | solution.py:217
  21.6 8.4 %collective-permute-start = (bf16[16,512]{1,0:T(8,128)(2,1)S(1)}, bf16[16,512]{1,0:T(8,128)(2,1)S(1)}, u32[]{:S(2)}, u32[]{:S(2)}) collective-permute-start(bf16[16,512]{1,0:T(8,128)(2,1)S(1)} %slice.27), channel_id=1, source_target_pairs={{8,16},{12,20},{24,32},{28,36},{40,48},{44,52},{56,64},{60,68},{72... | collective-permute-start | bytes 49160 | tf_op jit(solution)/shard_map/token_swap/ppermute | solution.py:216
  23.3 17.5 %collective-permute-start.7 = (bf16[256,768]{1,0:T(8,128)(2,1)S(1)}, bf16[256,768]{1,0:T(8,128)(2,1)S(1)}, u32[]{:S(2)}, u32[]{:S(2)}) collective-permute-start(bf16[256,768]{1,0:T(8,128)(2,1)S(1)} %bitcast.13), channel_id=1, source_target_pairs={{0,48},{16,0},{32,16},{48,32},{1,49},{17,1},{33,17},{49,33},{2,50}... | collective-permute-start | bytes 1179656 | tf_op jit(solution)/shard_map/weight_rings/ppermute | solution.py:22
  25.0 21.5 %collective-permute-start.6 = (bf16[256,768]{1,0:T(8,128)(2,1)S(1)}, bf16[256,768]{1,0:T(8,128)(2,1)S(1)}, u32[]{:S(2)}, u32[]{:S(2)}) collective-permute-start(bf16[256,768]{1,0:T(8,128)(2,1)S(1)} %bitcast.14), channel_id=1, source_target_pairs={{0,16},{16,32},{32,48},{48,0},{1,17},{17,33},{33,49},{49,1},{2,18}... | collective-permute-start | bytes 1179656 | tf_op jit(solution)/shard_map/weight_rings/ppermute | solution.py:22
  27.3 19.2 %collective-permute-start.5 = (bf16[256,768]{1,0:T(8,128)(2,1)S(1)}, bf16[256,768]{1,0:T(8,128)(2,1)S(1)}, u32[]{:S(2)}, u32[]{:S(2)}) collective-permute-start(bf16[256,768]{1,0:T(8,128)(2,1)S(1)} %bitcast.15), channel_id=1, source_target_pairs={{0,192},{64,0},{128,64},{192,128},{1,193},{65,1},{129,65},{193,129... | collective-permute-start | bytes 1179656 | tf_op jit(solution)/shard_map/weight_rings/ppermute | solution.py:22
  30.0 19.3 %collective-permute-start.4 = (bf16[256,768]{1,0:T(8,128)(2,1)S(1)}, bf16[256,768]{1,0:T(8,128)(2,1)S(1)}, u32[]{:S(2)}, u32[]{:S(2)}) collective-permute-start(bf16[256,768]{1,0:T(8,128)(2,1)S(1)} %bitcast.16), channel_id=1, source_target_pairs={{0,64},{64,128},{128,192},{192,0},{1,65},{65,129},{129,193},{193,1... | collective-permute-start | bytes 1179656 | tf_op jit(solution)/shard_map/weight_rings/ppermute | solution.py:22
  30.0 20.0 %collective-permute-start.3 = (bf16[256,768]{1,0:T(8,128)(2,1)S(1)}, bf16[256,768]{1,0:T(8,128)(2,1)S(1)}, u32[]{:S(2)}, u32[]{:S(2)}) collective-permute-start(bf16[256,768]{1,0:T(8,128)(2,1)S(1)} %bitcast.17), channel_id=1, source_target_pairs={{0,128},{64,192},{128,0},{192,64},{1,129},{65,193},{129,1},{193,65... | collective-permute-start | bytes 1179656 | tf_op jit(solution)/shard_map/weight_rings/ppermute | solution.py:22
  46.5 0.8 copy-start.2
  49.3 0.7 copy-start.4
  50.0 0.8 copy-start.6
  51.7 19.2 %collective-permute-start.9 = (bf16[512,768]{1,0:T(8,128)(2,1)S(1)}, bf16[512,768]{1,0:T(8,128)(2,1)S(1)}, u32[]{:S(2)}, u32[]{:S(2)}) collective-permute-start(bf16[512,768]{1,0:T(8,128)(2,1)S(1)} %constant_dynamic-update-slice_fusion.refs_3_), channel_id=1, source_target_pairs={{0,192},{64,0},{128,64},{192,128},{1,193},{65,1},{129,65},{193,129... | collective-permute-start | bytes 2359304 | tf_op jit(solution)/shard_map/weight_rings/ppermute | solution.py:22
  52.5 19.7 %collective-permute-start.8 = (bf16[512,768]{1,0:T(8,128)(2,1)S(1)}, bf16[512,768]{1,0:T(8,128)(2,1)S(1)}, u32[]{:S(2)}, u32[]{:S(2)}) collective-permute-start(bf16[512,768]{1,0:T(8,128)(2,1)S(1)} %constant_dynamic-update-slice_fusion.refs_3_), channel_id=1, source_target_pairs={{0,64},{64,128},{128,192},{192,0},{1,65},{65,129},{129,193},{193,1... | collective-permute-start | bytes 2359304 | tf_op jit(solution)/shard_map/weight_rings/ppermute | solution.py:22
  53.3 11.8 %collective-permute-start.11 = (bf16[128,768]{1,0:T(8,128)(2,1)S(1)}, bf16[128,768]{1,0:T(8,128)(2,1)S(1)}, u32[]{:S(2)}, u32[]{:S(2)}) collective-permute-start(bf16[128,768]{1,0:T(8,128)(2,1)S(1)} %slice.29), channel_id=1, source_target_pairs={{0,48},{16,0},{32,16},{48,32},{1,49},{17,1},{33,17},{49,33},{2,50}... | collective-permute-start | bytes 589832 | tf_op jit(solution)/shard_map/weight_rings/ppermute | solution.py:22
  53.7 11.7 %collective-permute-start.10 = (bf16[128,768]{1,0:T(8,128)(2,1)S(1)}, bf16[128,768]{1,0:T(8,128)(2,1)S(1)}, u32[]{:S(2)}, u32[]{:S(2)}) collective-permute-start(bf16[128,768]{1,0:T(8,128)(2,1)S(1)} %slice.28), channel_id=1, source_target_pairs={{0,16},{16,32},{32,48},{48,0},{1,17},{17,33},{33,49},{49,1},{2,18}... | collective-permute-start | bytes 589832 | tf_op jit(solution)/shard_map/weight_rings/ppermute | solution.py:22
  74.6 22.8 %collective-permute-start.14 = (bf16[256,768]{1,0:T(8,128)(2,1)}, bf16[256,768]{1,0:T(8,128)(2,1)S(1)}, u32[]{:S(2)}, u32[]{:S(2)}) collective-permute-start(bf16[256,768]{1,0:T(8,128)(2,1)} %pad_maximum_fusion.1), channel_id=1, source_target_pairs={{0,16},{16,32},{32,48},{48,0},{1,17},{17,33},{33,49},{49,1},{2,18}... | collective-permute-start | bytes 1179656 | tf_op jit(solution)/shard_map/weight_rings/ppermute | solution.py:22
  75.5 21.9 %collective-permute-start.15 = (bf16[256,768]{1,0:T(8,128)(2,1)}, bf16[256,768]{1,0:T(8,128)(2,1)}, u32[]{:S(2)}, u32[]{:S(2)}) collective-permute-start(bf16[256,768]{1,0:T(8,128)(2,1)} %pad_maximum_fusion.2), channel_id=1, source_target_pairs={{0,48},{16,0},{32,16},{48,32},{1,49},{17,1},{33,17},{49,33},{2,50}... | collective-permute-start | bytes 1179656 | tf_op jit(solution)/shard_map/weight_rings/ppermute | solution.py:22
  79.0 18.5 %collective-permute-start.13 = (bf16[256,768]{1,0:T(8,128)(2,1)}, bf16[256,768]{1,0:T(8,128)(2,1)}, u32[]{:S(2)}, u32[]{:S(2)}) collective-permute-start(bf16[256,768]{1,0:T(8,128)(2,1)} %slice.31), channel_id=1, source_target_pairs={{0,192},{64,0},{128,64},{192,128},{1,193},{65,1},{129,65},{193,129... | collective-permute-start | bytes 1179656 | tf_op jit(solution)/shard_map/weight_rings/ppermute | solution.py:22
  79.3 18.1 %collective-permute-start.12 = (bf16[256,768]{1,0:T(8,128)(2,1)}, bf16[256,768]{1,0:T(8,128)(2,1)}, u32[]{:S(2)}, u32[]{:S(2)}) collective-permute-start(bf16[256,768]{1,0:T(8,128)(2,1)} %slice.30), channel_id=1, source_target_pairs={{0,64},{64,128},{128,192},{192,0},{1,65},{65,129},{129,193},{193,1... | collective-permute-start | bytes 1179656 | tf_op jit(solution)/shard_map/weight_rings/ppermute | solution.py:22
  80.5 17.8 %collective-permute-start.16 = (bf16[256,768]{1,0:T(8,128)(2,1)S(1)}, bf16[256,768]{1,0:T(8,128)(2,1)}, u32[]{:S(2)}, u32[]{:S(2)}) collective-permute-start(bf16[256,768]{1,0:T(8,128)(2,1)S(1)} %constant_dynamic-update-slice_fusion.2.refs_4_), channel_id=1, source_target_pairs={{0,128},{64,192},{128,0},{192,64},{1,129},{65,193},{129,1},{193,65... | collective-permute-start | bytes 1179656 | tf_op jit(solution)/shard_map/weight_rings/ppermute | solution.py:22
  85.8 2.3 %copy-start = (bf16[4352,512]{1,0:T(8,128)(2,1)S(1)}, bf16[4352,512]{1,0:T(8,128)(2,1)}, u32[]{:S(2)}) copy-start(bf16[4352,512]{1,0:T(8,128)(2,1)} %all-gather.2.cloned.1.call-done.refs_1_) | copy-start | bytes 13369348
  88.1 1.0 copy-start.3
  89.1 1.0 copy-start.5
  90.1 1.0 copy-start.7
  91.1 7.1 %copy-start.1 = (bf16[4352,512]{1,0:T(8,128)(2,1)S(1)}, bf16[4352,512]{1,0:T(8,128)(2,1)}, u32[]{:S(2)}) copy-start(bf16[4352,512]{1,0:T(8,128)(2,1)} %all-gather.2.cloned.1.call-done.refs_1_) | copy-start | bytes 13369348
  91.1 7.2 %copy-start.8 = (f32[16,512]{1,0:T(8,128)S(1)}, f32[16,512]{1,0:T(8,128)}, u32[]{:S(2)}) copy-start(f32[16,512]{1,0:T(8,128)} %decay.3) | copy-start | bytes 98308
  91.1 7.2 %copy-start.11 = (f32[3,3,512]{2,1,0:T(4,128)S(1)}, f32[3,3,512]{2,1,0:T(4,128)}, u32[]{:S(2)}) copy-start(f32[3,3,512]{2,1,0:T(4,128)} %refs_8_.1) | copy-start | bytes 55300
  97.3 16.3 %copy-start.9 = (f32[16,512]{1,0:T(8,128)S(1)}, f32[16,512]{1,0:T(8,128)}, u32[]{:S(2)}) copy-start(f32[16,512]{1,0:T(8,128)} %decay.3) | copy-start | bytes 98308
  97.4 16.3 %copy-start.10 = (f32[16,512]{1,0:T(8,128)S(1)}, f32[16,512]{1,0:T(8,128)}, u32[]{:S(2)}) copy-start(f32[16,512]{1,0:T(8,128)} %gain.3) | copy-start | bytes 98308
  97.4 16.3 %copy-start.12 = (f32[512]{0:T(512)S(1)}, f32[512]{0:T(512)}, u32[]{:S(2)}) copy-start(f32[512]{0:T(512)} %param.11) | copy-start | bytes 6148
  105.1 20.6 %all-to-all-start.1 = ((f32[16,16,256]{2,1,0:T(8,128)}), f32[16,16,256]{2,1,0:T(8,128)S(1)}, u32[]{:S(2)}, u32[]{:S(2)}) async-start(f32[16,16,256]{2,1,0:T(8,128)} %broadcast_in_dim.3), calls=%async_computation.1 | async-start | bytes 524288 | tf_op jit(solution)/shard_map/state_exchange/all_to_all | solution.py:302
Sparse Core Ops, SparseCore 0:
  51.8 33.9 all-gather.1

commit v7 on v6

--- a/solution.py
+++ b/solution.py
@@ -14,6 +14,7 @@
 F32 = jnp.float32
 BF16 = jnp.bfloat16
 HALO = 16
+SWAP = [(0, 1), (1, 0)]
 SUB = 8
 
 
@@ -22,6 +23,11 @@
     return lax.ppermute(array, axis, [(i, (i + step) % n) for i in range(n)])
 
 
+def in_order(mine_first, mine, theirs, axis):
+    first, second = jnp.where(mine_first, mine, theirs), jnp.where(mine_first, theirs, mine)
+    return jnp.concatenate([first, second], axis)
+
+
 def both_ways(piece, axis):
     return shifted(piece, axis, 1), shifted(piece, axis, -1)
 
@@ -31,31 +37,37 @@
     return shifted(behind[:half], axis, 1), shifted(ahead[half:], axis, -1)
 
 
-def fetched(sizes, pos, tok, pieces, blocks, tokv, wv, sem):
+def fetched(sizes, pos, near, swapped, pieces, blocks, tokv, wv, sem):
     rows, depth, width, modes, seq = sizes
     k = depth // 16
-    lines = rows + HALO
+    lines = rows + 2 * HALO
     copies, at, seen = [], 0, set()
 
-    def start(source, target):
+    def add(source, target):
         copies.append(pltpu.make_async_copy(source, target, sem.at[len(copies)]))
-        copies[-1].start()
+        return copies[-1]
 
     for piece, first, n, dy, dh, skip in blocks:
-        start(pieces[piece].at[pl.ds(first, n), :], wv.at[pl.ds(at + skip, n), :])
+        add(pieces[piece].at[pl.ds(first, n), :], wv.at[pl.ds(at + skip, n), :]).start()
         if (dy, dh) not in seen:
             seen.add((dy, dh))
             ys, hs = lax.rem(pos[1] - dy + 4, 4), lax.rem(pos[2] - dh + 4, 4)
             ch = 2 * ys + lax.div(hs, 2)
             lanes = pl.ds(pl.multiple_of(lax.rem(hs, 2) * k, k), k)
-            part = 2 * lax.rem(ch, 4) + lax.rem(lax.div(ch, 4) + pos[4], 2)
+            x = lax.rem(ch, 4)
+            other = lax.rem(lax.div(ch, 4) + pos[4], 2)
+            to = pl.ds(at, k)
+            line = pl.multiple_of(x * lines + HALO * other, HALO)
+            add(swapped.at[pl.ds(line, HALO), lanes], tokv.at[pl.ds(0, HALO), to]).start()
             for core in range(2):
-                skipped = HALO * core
-                line = pl.multiple_of((8 * core + part) * lines + skipped, HALO)
-                start(
-                    tok.at[pl.ds(line, lines - skipped), lanes],
-                    tokv.at[pl.ds(core * lines, lines - skipped), pl.ds(at, k)],
-                )
+                target = tokv.at[pl.ds(HALO + core * rows, rows), to]
+                line = pl.multiple_of((4 * core + x) * rows, rows)
+                copy = add(near.at[pl.ds(line, rows), lanes], target)
+                pl.when(other == 0)(copy.start)
+                line = pl.multiple_of((4 * core + x) * lines + 2 * HALO, HALO)
+                source = swapped.at[pl.ds(line, rows), lanes]
+                copy = pltpu.make_async_copy(source, target, sem.at[len(copies) - 1])
+                pl.when(other == 1)(copy.start)
         if skip + n == k:
             at += k
     return copies
@@ -63,9 +75,9 @@
 
 def project_kernel(sizes, blocks, *refs):
     rows, depth, width, modes, seq = sizes
-    pos, tok, *pieces = refs[:-4]
+    pos, near, swapped, *pieces = refs[:-4]
     sums, tokv, wv, sem = refs[-4:]
-    for copy in fetched(sizes, pos, tok, pieces, blocks, tokv, wv, sem):
+    for copy in fetched(sizes, pos, near, swapped, pieces, blocks, tokv, wv, sem):
         copy.wait()
 
     @pl.loop(0, 3)
@@ -78,10 +90,10 @@
 
 def state_kernel(sizes, blocks, *refs):
     rows, depth, width, modes, seq = sizes
-    pos, tok, *pieces = refs[:-11]
+    pos, near, swapped, *pieces = refs[:-11]
     sums, taps, decay, gate, product, inside, state, tokv, wv, acc, sem = refs[-11:]
     c = pos[3]
-    for copy in fetched(sizes, pos, tok, pieces, blocks, tokv, wv, sem):
+    for copy in fetched(sizes, pos, near, swapped, pieces, blocks, tokv, wv, sem):
         copy.wait()
 
     @pl.loop(0, 3)
@@ -159,7 +171,7 @@
         lax.fori_loop(0, steps, step, [jnp.zeros((SUB, 128), F32)] * modes, unroll=4)
 
 
-def finish_kernel(sizes, pos, gate, local, inside, states, gain, decay, out, start, whole):
+def finish_kernel(sizes, pos, gate, local, inside, states, gain, decay, mine_out, their_out, start, whole):
     rows, depth, width, modes, seq = sizes
     rank, c = pos[0], pos[3]
     steps = 2 * rows // SUB
@@ -189,8 +201,9 @@
             return waves
 
         lax.fori_loop(0, steps, step, waves, unroll=4)
-        for part in range(2):
-            out[part, :, lanes] = whole[lh, part * rows : part * rows + rows, :].astype(BF16)
+        for out, core in ((mine_out, c), (their_out, 1 - c)):
+            line = pl.ds(pl.multiple_of(core * rows, rows), rows)
+            out[:, lanes] = whole[lh, line, :].astype(BF16)
 
 
 def body(tokens, w_in, taps, modes_gain, decay, skip):
@@ -208,10 +221,12 @@
     tie = lax.optimization_barrier
     with jax.named_scope("weight_gather"):
         halves = w_in.reshape(k, 3, 2, width).transpose(2, 0, 1, 3).reshape(2, k, 3 * width)
-        own = lax.all_to_all(halves, "c", 0, 0, tiled=True).reshape(2 * k, 3 * width)
+        mine = lax.dynamic_index_in_dim(halves, c, 0, keepdims=False)
+        theirs = lax.ppermute(lax.dynamic_index_in_dim(halves, 1 - c, 0, keepdims=False), "c", SWAP)
+        own = in_order(c == 0, mine, theirs, 0)
         tail, own = tie((tokens[rows - HALO :], own))
     with jax.named_scope("token_swap"):
-        other = lax.ppermute(tokens, "l", [(0, 1), (1, 0)])
+        other = lax.ppermute(tokens, "l", SWAP)
         route = [(4 * r + 2 + side, 4 * r + 4 + side) for r in range(15) for side in range(2)]
         halo = lax.ppermute(tail, (*CTX, "l"), route)
         other_halo = lax.ppermute(tail, (*CTX, "l"), [(i, j ^ 1) for i, j in route])
@@ -222,8 +237,9 @@
     first = (halo, other_halo, other, farther, far, beside)
     halo, other_halo, other, farther, far, beside = tie(first)
     with jax.named_scope("token_gather"):
-        wide = jnp.concatenate([halo, tokens, other_halo, other], 0)
-        tok = lax.all_gather(wide, ("c", "x"), axis=0, tiled=True)
+        near = lax.all_gather(tokens, ("c", "x"), axis=0, tiled=True)
+        wide = jnp.concatenate([halo, other_halo, other], 0)
+        swapped = lax.all_gather(wide, ("c", "x"), axis=0, tiled=True)
     with jax.named_scope("weight_rings"):
         two, half = 2 * k, k
         pair = jnp.concatenate(beside, 0)
@@ -268,12 +284,12 @@
         return [pltpu.VMEM((lines, n * two), BF16), pltpu.VMEM((n * two, 3 * width), BF16)]
 
     def sems(blocks, n):
-        return pltpu.SemaphoreType.DMA((len(blocks) + 2 * n,))
+        return pltpu.SemaphoreType.DMA((len(blocks) + 3 * n,))
 
     sums = pl.pallas_call(
         functools.partial(project_kernel, sizes, early_blocks),
         out_shape=jax.ShapeDtypeStruct(chunks, F32),
-        in_specs=[smem] + [hbm] * (1 + len(early)),
+        in_specs=[smem] + [hbm] * (2 + len(early)),
         out_specs=vmem,
         scratch_shapes=[*held(11), sems(early_blocks, 11)],
         compiler_params=pltpu.CompilerParams(vmem_limit_bytes=14 * 2**20),
@@ -281,7 +297,7 @@
             flops=2 * lines * 11 * two * 3 * width, bytes_accessed=9_000_000, transcendentals=0
         ),
         name="project",
-    )(pos, tok, *early)
+    )(pos, near, swapped, *early)
     params = pltpu.CompilerParams(vmem_limit_bytes=12 * 2**20)
     gate, product, inside, state = pl.pallas_call(
         functools.partial(state_kernel, sizes, late_blocks),
@@ -291,12 +307,12 @@
             jax.ShapeDtypeStruct((modes, SUB, width), F32),
             jax.ShapeDtypeStruct((modes, width), F32),
         ),
-        in_specs=[smem] + [hbm] * (1 + len(late)) + [vmem] * 3,
+        in_specs=[smem] + [hbm] * (2 + len(late)) + [vmem] * 3,
         out_specs=(vmem,) * 4,
         scratch_shapes=[*held(5), pltpu.VMEM(chunks, F32), sems(late_blocks, 5)],
         compiler_params=params,
         name="states",
-    )(pos, tok, *late, sums, taps, decay)
+    )(pos, near, swapped, *late, sums, taps, decay)
 
     with jax.named_scope("state_exchange"):
         states = lax.all_to_all(
@@ -311,18 +327,17 @@
         cost_estimate=pl.CostEstimate(flops=20_000_000, bytes_accessed=1_000_000, transcendentals=0),
         name="local",
     )(pos, product, modes_gain, decay, skip.reshape(1, group))
-    out = pl.pallas_call(
+    mine, theirs = pl.pallas_call(
         functools.partial(finish_kernel, sizes),
-        out_shape=jax.ShapeDtypeStruct((2, rows, width), BF16),
+        out_shape=(jax.ShapeDtypeStruct((rows, width), BF16),) * 2,
         in_specs=[smem] + [vmem] * 6,
-        out_specs=vmem,
+        out_specs=(vmem, vmem),
         scratch_shapes=[pltpu.VMEM((modes, width), F32), pltpu.VMEM((width // 128, 2 * rows, 128), F32)],
         compiler_params=params,
         name="finish",
     )(pos, gate, local, inside, states, modes_gain, decay)
     with jax.named_scope("result_swap"):
-        both = lax.all_to_all(out, "c", 0, 0, tiled=True)
-        return both.transpose(1, 0, 2).reshape(rows, group)
+        return in_order(c == 0, mine, lax.ppermute(theirs, "c", SWAP), 1)
 
 
 def solution(mesh):

time: 141 us -> 133 us (0.943)
  blocking collectives: 5.7 us -> 0 us
  starting transfers between devices: 40.5 us -> 37.9 us
    all_to_all x1 -> x0, blocking collectives: 5.7 us -> none  [body(): both = lax.all_to_all(out, 'c', 0, 0, tiled=True)]
    ppermute x1 -> x3, starting transfers between devices: 2.47 us -> 7.29 us  [the longest x1 3.96 us: body(): return in_order(c == 0, mine, lax.ppermute(theirs, 'c', SWAP), 1)]
    all_to_all x1 -> x0, starting transfers between devices: 4.41 us -> none  [body(): lax.all_to_all(halves, 'c', 0, 0, tiled=True).reshape(2 * k, 3 * width)]
    all_gather x1 -> x2, waiting for transfers between devices: 3.96 us -> 0.01 us  [the longest x1 0.01 us: body(): near = lax.all_gather(tokens, ('c', 'x'), axis=0, tiled=True)]
    ppermute x14, waiting for transfers between devices: 34.1 us -> 36.6 us  [shifted(): return lax.ppermute(array, axis, [(i, (i + step) % n) for i in range(n)])]
    ppermute x1 -> x3, waiting for transfers between devices: 0.01 us -> 1.9 us  [the longest x1 0.99 us: body(): return in_order(c == 0, mine, lax.ppermute(theirs, 'c', SWAP), 1)]
    all_to_all x1, starting transfers between devices: 8.53 us -> 6.81 us  [body(): lax.all_to_all(jnp.broadcast_to(state, (16, *state.shape)), ('y', 'h'), 0...]
    unnamed x31 -> x33, local copies, waits for them, and re-layouts: 8.78 us -> 9.78 us
  transfers between devices with their start and end apart: 20 -> 22, of which waited for: 11 -> 13; matrix products, arithmetic and copies ran while one was open for 4% -> 4% of each run, Pallas kernels for 6% -> 6%
where the time goes in v7:
time: 133 us; the launch traced here: 132 us
  waiting for transfers between devices  48.6 us (37%)
  starting transfers between devices  37.9 us (28%)
  Pallas kernels  16.3 us (12%)
  between operations  13.7 us (10%)
  local copies, waits for them, and re-layouts  12.6 us (9%)
  other arithmetic  3.15 us (2%)
    ppermute x14, waiting for transfers between devices, shifted(): return lax.ppermute(array, axis, [(i, (i + step) % n) for i in range(n)])  36.6 us
    ppermute x14, starting transfers between devices, shifted(): return lax.ppermute(array, axis, [(i, (i + step) % n) for i in range(n)])  17.7 us
    unnamed x33, local copies, waits for them, and re-layouts  9.78 us
    all_to_all x1, waiting for transfers between devices, body(): lax.all_to_all(jnp.broadcast_to(state, (16, *state.shape)), ('y', 'h'), 0...  9.39 us
    all_to_all x1, starting transfers between devices, body(): lax.all_to_all(jnp.broadcast_to(state, (16, *state.shape)), ('y', 'h'), 0...  6.81 us
    pallas_call x1, Pallas kernels, body(): pl.pallas_call(functools.partial(project_kernel, sizes, early_blocks), ou...  6.57 us
    pallas_call x1, Pallas kernels, body(): pl.pallas_call(functools.partial(state_kernel, sizes, late_blocks), out_s...  6.29 us
    ppermute x1, starting transfers between devices, body(): other_halo = lax.ppermute(tail, (*CTX, 'l'), [(i, j ^ 1) for i, j in route])  4.77 us
  transfers between devices with their start and end apart: 22, of which 13 were waited for; matrix products, arithmetic and copies ran while one was open for 4% of the time, Pallas kernels for 6%

profile of v7, /device:TPU:1, one launch (start us, length us, event | category | flops | bytes accessed | tf_op | source)
XLA Modules:
  0.0 132.2 jit_solution(7681432493126503200)
XLA Ops:
  6.5 0.7 all-gather.3.cloned.1.call-update
  7.3 0.0 all-gather.5.cloned.1.call-start
  7.3 1.2 copy.10
  8.6 0.1 copy.13
  8.8 3.3 %collective-permute-start = (bf16[128,768]{1,0:T(8,128)(2,1)S(1)}, bf16[128,768]{1,0:T(8,128)(2,1)S(1)}, u32[]{:S(2)}, u32[]{:S(2)}) collective-permute-start(bf16[128,768]{1,0:T(8,128)(2,1)S(1)} %bitcast.17), channel_id=1, source_target_pairs={{0,8},{8,0},{1,9},{9,1},{2,10},{10,2},{3,11},{11,3},{4,12},{12,4},... | collective-permute-start | bytes 589832 | tf_op jit(solution)/shard_map/weight_gather/ppermute | solution.py:225
  12.1 0.0 collective-permute-start.3
  12.1 0.1 copy.12
  12.2 0.9 collective-permute-done
  13.2 4.8 %collective-permute-start.2 = (bf16[16,512]{1,0:T(8,128)(2,1)S(1)}, bf16[16,512]{1,0:T(8,128)(2,1)S(1)}, u32[]{:S(2)}, u32[]{:S(2)}) collective-permute-start(bf16[16,512]{1,0:T(8,128)(2,1)S(1)} %slice.27), channel_id=1, source_target_pairs={{8,20},{12,16},{24,36},{28,32},{40,52},{44,48},{56,68},{60,64},{72... | collective-permute-start | bytes 49160 | tf_op jit(solution)/shard_map/token_swap/ppermute | solution.py:232
  18.0 1.3 collective-permute-start.1
  19.3 1.7 %collective-permute-start.8 = (bf16[256,768]{1,0:T(8,128)(2,1)S(1)}, bf16[256,768]{1,0:T(8,128)(2,1)S(1)}, u32[]{:S(2)}, u32[]{:S(2)}) collective-permute-start(bf16[256,768]{1,0:T(8,128)(2,1)S(1)} %pad_maximum_fusion.refs_3_), channel_id=1, source_target_pairs={{0,48},{16,0},{32,16},{48,32},{1,49},{17,1},{33,17},{49,33},{2,50}... | collective-permute-start | bytes 1179656 | tf_op jit(solution)/shard_map/weight_rings/ppermute | solution.py:23
  21.0 1.8 %collective-permute-start.7 = (bf16[256,768]{1,0:T(8,128)(2,1)S(1)}, bf16[256,768]{1,0:T(8,128)(2,1)S(1)}, u32[]{:S(2)}, u32[]{:S(2)}) collective-permute-start(bf16[256,768]{1,0:T(8,128)(2,1)S(1)} %pad_maximum_fusion.refs_3_), channel_id=1, source_target_pairs={{0,16},{16,32},{32,48},{48,0},{1,17},{17,33},{33,49},{49,1},{2,18}... | collective-permute-start | bytes 1179656 | tf_op jit(solution)/shard_map/weight_rings/ppermute | solution.py:23
  22.8 0.0 collective-permute-done.2
  22.8 2.7 %collective-permute-start.6 = (bf16[256,768]{1,0:T(8,128)(2,1)S(1)}, bf16[256,768]{1,0:T(8,128)(2,1)S(1)}, u32[]{:S(2)}, u32[]{:S(2)}) collective-permute-start(bf16[256,768]{1,0:T(8,128)(2,1)S(1)} %pad_maximum_fusion.refs_3_), channel_id=1, source_target_pairs={{0,192},{64,0},{128,64},{192,128},{1,193},{65,1},{129,65},{193,129... | collective-permute-start | bytes 1179656 | tf_op jit(solution)/shard_map/weight_rings/ppermute | solution.py:23
  25.5 0.0 collective-permute-done.1
  25.5 1.6 %collective-permute-start.4 = (bf16[256,768]{1,0:T(8,128)(2,1)S(1)}, bf16[256,768]{1,0:T(8,128)(2,1)S(1)}, u32[]{:S(2)}, u32[]{:S(2)}) collective-permute-start(bf16[256,768]{1,0:T(8,128)(2,1)S(1)} %pad_maximum_fusion.refs_3_), channel_id=1, source_target_pairs={{0,128},{64,192},{128,0},{192,64},{1,129},{65,193},{129,1},{193,65... | collective-permute-start | bytes 1179656 | tf_op jit(solution)/shard_map/weight_rings/ppermute | solution.py:23
  27.2 11.2 %collective-permute-done.8 = bf16[256,768]{1,0:T(8,128)(2,1)S(1)} collective-permute-done((bf16[256,768]{1,0:T(8,128)(2,1)S(1)}, bf16[256,768]{1,0:T(8,128)(2,1)S(1)}, u32[]{:S(2)}, u32[]{:S(2)}) %collective-permute-start.8) | collective-permute-done | bytes 393248 | tf_op jit(solution)/shard_map/weight_rings/ppermute | solution.py:23
  38.4 0.9 collective-permute-done.7
  39.3 2.1 %collective-permute-done.6.refs_7_ = bf16[256,768]{1,0:T(8,128)(2,1)S(1)} collective-permute-done((bf16[256,768]{1,0:T(8,128)(2,1)S(1)}, bf16[256,768]{1,0:T(8,128)(2,1)S(1)}, u32[]{:S(2)}, u32[]{:S(2)}) %collective-permute-start.6) | collective-permute-done | bytes 393248 | tf_op jit(solution)/shard_map/weight_rings/ppermute | solution.py:23
  41.4 0.7 copy-done.3
  42.2 3.5 %collective-permute-done.5.refs_6_ = bf16[256,768]{1,0:T(8,128)(2,1)S(1)} collective-permute-done((bf16[256,768]{1,0:T(8,128)(2,1)S(1)}, bf16[256,768]{1,0:T(8,128)(2,1)S(1)}, u32[]{:S(2)}, u32[]{:S(2)}) %collective-permute-start.5) | collective-permute-done | bytes 393248 | tf_op jit(solution)/shard_map/weight_rings/ppermute | solution.py:23
  45.7 0.8 copy-done.5
  46.5 0.7 copy-done.7
  47.2 0.7 pad_maximum_fusion.3
  47.9 0.0 all-gather.5.cloned.1.call-update
  48.0 0.1 collective-permute-start.10
  48.1 1.5 %collective-permute-start.9 = (bf16[512,768]{1,0:T(8,128)(2,1)S(1)}, bf16[512,768]{1,0:T(8,128)(2,1)S(1)}, u32[]{:S(2)}, u32[]{:S(2)}) collective-permute-start(bf16[512,768]{1,0:T(8,128)(2,1)S(1)} %constant_dynamic-update-slice_fusion.refs_4_), channel_id=1, source_target_pairs={{0,64},{64,128},{128,192},{192,0},{1,65},{65,129},{129,193},{193,1... | collective-permute-start | bytes 2359304 | tf_op jit(solution)/shard_map/weight_rings/ppermute | solution.py:23
  49.6 0.1 collective-permute-start.12
  49.7 2.4 %collective-permute-start.11 = (bf16[128,768]{1,0:T(8,128)(2,1)S(1)}, bf16[128,768]{1,0:T(8,128)(2,1)S(1)}, u32[]{:S(2)}, u32[]{:S(2)}) collective-permute-start(bf16[128,768]{1,0:T(8,128)(2,1)S(1)} %slice.28), channel_id=1, source_target_pairs={{0,16},{16,32},{32,48},{48,0},{1,17},{17,33},{33,49},{49,1},{2,18}... | collective-permute-start | bytes 589832 | tf_op jit(solution)/shard_map/weight_rings/ppermute | solution.py:23
  52.1 7.8 %collective-permute-done.12 = bf16[128,768]{1,0:T(8,128)(2,1)S(1)} collective-permute-done((bf16[128,768]{1,0:T(8,128)(2,1)S(1)}, bf16[128,768]{1,0:T(8,128)(2,1)S(1)}, u32[]{:S(2)}, u32[]{:S(2)}) %collective-permute-start.12) | collective-permute-done | bytes 196640 | tf_op jit(solution)/shard_map/weight_rings/ppermute | solution.py:23
  59.9 1.4 %collective-permute-done.11 = bf16[128,768]{1,0:T(8,128)(2,1)S(1)} collective-permute-done((bf16[128,768]{1,0:T(8,128)(2,1)S(1)}, bf16[128,768]{1,0:T(8,128)(2,1)S(1)}, u32[]{:S(2)}, u32[]{:S(2)}) %collective-permute-start.11) | collective-permute-done | bytes 196640 | tf_op jit(solution)/shard_map/weight_rings/ppermute | solution.py:23
  61.3 5.6 %collective-permute-done.10.refs_9_ = bf16[512,768]{1,0:T(8,128)(2,1)S(1)} collective-permute-done((bf16[512,768]{1,0:T(8,128)(2,1)S(1)}, bf16[512,768]{1,0:T(8,128)(2,1)S(1)}, u32[]{:S(2)}, u32[]{:S(2)}) %collective-permute-start.10) | collective-permute-done | bytes 786464 | tf_op jit(solution)/shard_map/weight_rings/ppermute | solution.py:23
  66.9 1.3 collective-permute-done.9.refs_8_
  68.2 0.8 slice.30
  69.0 0.8 slice.31
  69.8 0.1 fusion
  69.8 0.8 pad_maximum_fusion.1
  70.6 0.0 collective-permute-start.15
  70.6 0.8 pad_maximum_fusion.2
  71.4 3.6 %collective-permute-start.16 = (bf16[256,768]{1,0:T(8,128)(2,1)}, bf16[256,768]{1,0:T(8,128)(2,1)}, u32[]{:S(2)}, u32[]{:S(2)}) collective-permute-start(bf16[256,768]{1,0:T(8,128)(2,1)} %pad_maximum_fusion.2), channel_id=1, source_target_pairs={{0,48},{16,0},{32,16},{48,32},{1,49},{17,1},{33,17},{49,33},{2,50}... | collective-permute-start | bytes 1179656 | tf_op jit(solution)/shard_map/weight_rings/ppermute | solution.py:23
  75.0 0.3 collective-permute-start.14
  75.3 1.2 collective-permute-start.13
  76.5 0.8 collective-permute-start.17
  77.3 0.1 stack.23.refs_0_.pos
  77.4 1.7 %copy-done = bf16[2304,512]{1,0:T(8,128)(2,1)S(1)} copy-done((bf16[2304,512]{1,0:T(8,128)(2,1)S(1)}, bf16[2304,512]{1,0:T(8,128)(2,1)}, u32[]{:S(2)}) %copy-start) | copy-done | bytes 2359320
  79.1 1.6 %copy-done.2 = bf16[2048,512]{1,0:T(8,128)(2,1)S(1)} copy-done((bf16[2048,512]{1,0:T(8,128)(2,1)S(1)}, bf16[2048,512]{1,0:T(8,128)(2,1)}, u32[]{:S(2)}) %copy-start.2) | copy-done | bytes 2097176
  80.7 1.0 copy-done.4
  81.6 1.0 copy-done.6
  82.6 1.0 copy-done.8
  83.6 6.6 %project.1.refs_8_ = f32[6,528,128]{2,1,0:T(8,128)S(1)} custom-call(s32[5]{0:T(128)S(1)} %stack.23.refs_0_.pos, bf16[2048,512]{1,0:T(8,128)(2,1)S(1)} %copy-done.2, bf16[2304,512]{1,0:T(8,128)(2,1)S(1)} %copy-done, bf16[256,768]{1,0:T(8,128)(2,1)S(1)} %pad_maximum_fusion.refs_3_, bf16[512,768]{1,0:T(8,128)(2,1)S(1)} %constant_dynamic-update-slice_fusion.refs_4_, ...), custom_call_target="tpu_custom_call" | custom-call | flops 2283798528 | bytes 9000000 | tf_op jit(solution)/shard_map/project/pallas_call | solution.py:289
  90.2 0.0 copy-start.10
  90.2 0.0 copy-start.11
  90.3 0.0 copy-start.13
  90.3 1.6 %collective-permute-done.16.refs_6_ = bf16[256,768]{1,0:T(8,128)(2,1)} collective-permute-done((bf16[256,768]{1,0:T(8,128)(2,1)}, bf16[256,768]{1,0:T(8,128)(2,1)}, u32[]{:S(2)}, u32[]{:S(2)}) %collective-permute-start.16) | collective-permute-done | bytes 393248 | tf_op jit(solution)/shard_map/weight_rings/ppermute | solution.py:23
  91.9 1.1 collective-permute-done.17.refs_7_
  93.0 6.3 %states.1 = (f32[64,8,256]{2,1,0:T(8,128)S(1)}, f32[64,8,256]{2,1,0:T(8,128)S(1)}, f32[16,8,256]{2,1,0:T(8,128)S(1)}, f32[16,256]{1,0:T(8,128)S(1)}) custom-call(s32[5]{0:T(128)S(1)} %stack.23.refs_0_.pos, bf16[2048,512]{1,0:T(8,128)(2,1)S(1)} %copy-done.2, bf16[2304,512]{1,0:T(8,128)(2,1)S(1)} %copy-done.1, ...), custom_call_target="tpu_custom_call" | custom-call | tf_op jit(solution)/shard_map/states/pallas_call | solution.py:302
  99.3 0.7 broadcast_in_dim.3
  100.0 6.8 %all-to-all-start = ((f32[16,16,256]{2,1,0:T(8,128)}), f32[16,16,256]{2,1,0:T(8,128)S(1)}, u32[]{:S(2)}, u32[]{:S(2)}) async-start(f32[16,16,256]{2,1,0:T(8,128)} %broadcast_in_dim.3), calls=%async_computation | async-start | bytes 524288 | tf_op jit(solution)/shard_map/state_exchange/all_to_all | solution.py:318
  106.9 1.9 %local.1 = f32[64,8,256]{2,1,0:T(8,128)S(1)} custom-call(s32[5]{0:T(128)S(1)} %stack.23.refs_0_.pos, f32[64,8,256]{2,1,0:T(8,128)S(1)} %get-tuple-element.40.product, f32[16,512]{1,0:T(8,128)S(1)} %copy-done.11, f32[16,512]{1,0:T(8,128)S(1)} %copy-done.10, f32[1,512]{1,0:T(1,128)S(1)} %bitcast.14), custom_call_target="tpu_custom_call" | custom-call | flops 20000000 | bytes 1000000 | tf_op jit(solution)/shard_map/local/pallas_call | solution.py:321
  108.7 9.4 %all-to-all-done.states = f32[16,16,256]{2,1,0:T(8,128)S(1)} async-done(((f32[16,16,256]{2,1,0:T(8,128)}), f32[16,16,256]{2,1,0:T(8,128)S(1)}, u32[]{:S(2)}, u32[]{:S(2)}) %all-to-all-start) | async-done | bytes 262176 | tf_op jit(solution)/shard_map/state_exchange/all_to_all | solution.py:318
  118.1 1.5 %finish.1 = (bf16[256,256]{1,0:T(8,128)(2,1)S(1)}, bf16[256,256]{1,0:T(8,128)(2,1)S(1)}) custom-call(s32[5]{0:T(128)S(1)} %stack.23.refs_0_.pos, f32[64,8,256]{2,1,0:T(8,128)S(1)} %get-tuple-element.39.gate, f32[64,8,256]{2,1,0:T(8,128)S(1)} %local.1, f32[16,8,256]{2,1,0:T(8,128)S(1)} %get-tuple-element.41.inside, f32[16,16,256]{2,1,0:T(8,128)S(1)} %all-to-all-done.states, ...), custom_call_target="tpu_custom_call" | custom-call | tf_op jit(solution)/shard_map/finish/pallas_call | solution.py:330
  119.7 4.0 %collective-permute-start.18 = (bf16[256,256]{1,0:T(8,128)(2,1)S(1)}, bf16[256,256]{1,0:T(8,128)(2,1)S(1)}, u32[]{:S(2)}, u32[]{:S(2)}) collective-permute-start(bf16[256,256]{1,0:T(8,128)(2,1)S(1)} %get-tuple-element.44), channel_id=1, source_target_pairs={{0,8},{8,0},{1,9},{9,1},{2,10},{10,2},{3,11},{11,3},{4,12},{12,4},... | collective-permute-start | bytes 393224 | tf_op jit(solution)/shard_map/result_swap/ppermute | solution.py:340
  123.6 1.0 collective-permute-done.18
  124.6 0.7 pad_maximum_fusion.4
  (40 shorter events, 0.3 us)
Async XLA Ops:
  6.5 5.6 %copy-start.14 = (bf16[256,512]{1,0:T(8,128)(2,1)S(1)}, bf16[256,512]{1,0:T(8,128)(2,1)}, u32[]{:S(2)}) copy-start(bf16[256,512]{1,0:T(8,128)(2,1)} %param.6) | copy-start | bytes 786436
  6.5 70.9 %all-gather.3.cloned.1.call-start = ((), (), s32[]{:S(2)}) async-start(), calls=%async_computation.1 | async-start | bytes 2359296 | tf_op jit(solution)/shard_map/token_gather/all_gather | solution.py:240
  7.3 70.1 %all-gather.5.cloned.1.call-start = ((), (), s32[]{:S(2)}) async-start(), calls=%async_computation.2 | async-start | bytes 2654208 | tf_op jit(solution)/shard_map/token_gather/all_gather | solution.py:242
  8.8 4.4 %collective-permute-start = (bf16[128,768]{1,0:T(8,128)(2,1)S(1)}, bf16[128,768]{1,0:T(8,128)(2,1)S(1)}, u32[]{:S(2)}, u32[]{:S(2)}) collective-permute-start(bf16[128,768]{1,0:T(8,128)(2,1)S(1)} %bitcast.17), channel_id=1, source_target_pairs={{0,8},{8,0},{1,9},{9,1},{2,10},{10,2},{3,11},{11,3},{4,12},{12,4},... | collective-permute-start | bytes 589832 | tf_op jit(solution)/shard_map/weight_gather/ppermute | solution.py:225
  12.1 13.4 %collective-permute-start.3 = (bf16[256,512]{1,0:T(8,128)(2,1)S(1)}, bf16[256,512]{1,0:T(8,128)(2,1)S(1)}, u32[]{:S(2)}, u32[]{:S(2)}) collective-permute-start(bf16[256,512]{1,0:T(8,128)(2,1)S(1)} %copy-done.14), channel_id=1, source_target_pairs={{0,4},{4,0},{1,5},{5,1},{2,6},{6,2},{3,7},{7,3},{8,12},{12,8},{9,1... | collective-permute-start | bytes 786440 | tf_op jit(solution)/shard_map/token_swap/ppermute | solution.py:229
  13.2 9.6 %collective-permute-start.2 = (bf16[16,512]{1,0:T(8,128)(2,1)S(1)}, bf16[16,512]{1,0:T(8,128)(2,1)S(1)}, u32[]{:S(2)}, u32[]{:S(2)}) collective-permute-start(bf16[16,512]{1,0:T(8,128)(2,1)S(1)} %slice.27), channel_id=1, source_target_pairs={{8,20},{12,16},{24,36},{28,32},{40,52},{44,48},{56,68},{60,64},{72... | collective-permute-start | bytes 49160 | tf_op jit(solution)/shard_map/token_swap/ppermute | solution.py:232
  18.0 7.5 %collective-permute-start.1 = (bf16[16,512]{1,0:T(8,128)(2,1)S(1)}, bf16[16,512]{1,0:T(8,128)(2,1)S(1)}, u32[]{:S(2)}, u32[]{:S(2)}) collective-permute-start(bf16[16,512]{1,0:T(8,128)(2,1)S(1)} %slice.27), channel_id=1, source_target_pairs={{8,16},{12,20},{24,32},{28,36},{40,48},{44,52},{56,64},{60,68},{72... | collective-permute-start | bytes 49160 | tf_op jit(solution)/shard_map/token_swap/ppermute | solution.py:231
  19.3 19.1 %collective-permute-start.8 = (bf16[256,768]{1,0:T(8,128)(2,1)S(1)}, bf16[256,768]{1,0:T(8,128)(2,1)S(1)}, u32[]{:S(2)}, u32[]{:S(2)}) collective-permute-start(bf16[256,768]{1,0:T(8,128)(2,1)S(1)} %pad_maximum_fusion.refs_3_), channel_id=1, source_target_pairs={{0,48},{16,0},{32,16},{48,32},{1,49},{17,1},{33,17},{49,33},{2,50}... | collective-permute-start | bytes 1179656 | tf_op jit(solution)/shard_map/weight_rings/ppermute | solution.py:23
  21.0 18.3 %collective-permute-start.7 = (bf16[256,768]{1,0:T(8,128)(2,1)S(1)}, bf16[256,768]{1,0:T(8,128)(2,1)S(1)}, u32[]{:S(2)}, u32[]{:S(2)}) collective-permute-start(bf16[256,768]{1,0:T(8,128)(2,1)S(1)} %pad_maximum_fusion.refs_3_), channel_id=1, source_target_pairs={{0,16},{16,32},{32,48},{48,0},{1,17},{17,33},{33,49},{49,1},{2,18}... | collective-permute-start | bytes 1179656 | tf_op jit(solution)/shard_map/weight_rings/ppermute | solution.py:23
  22.8 18.6 %collective-permute-start.6 = (bf16[256,768]{1,0:T(8,128)(2,1)S(1)}, bf16[256,768]{1,0:T(8,128)(2,1)S(1)}, u32[]{:S(2)}, u32[]{:S(2)}) collective-permute-start(bf16[256,768]{1,0:T(8,128)(2,1)S(1)} %pad_maximum_fusion.refs_3_), channel_id=1, source_target_pairs={{0,192},{64,0},{128,64},{192,128},{1,193},{65,1},{129,65},{193,129... | collective-permute-start | bytes 1179656 | tf_op jit(solution)/shard_map/weight_rings/ppermute | solution.py:23
  25.5 20.2 %collective-permute-start.5 = (bf16[256,768]{1,0:T(8,128)(2,1)S(1)}, bf16[256,768]{1,0:T(8,128)(2,1)S(1)}, u32[]{:S(2)}, u32[]{:S(2)}) collective-permute-start(bf16[256,768]{1,0:T(8,128)(2,1)S(1)} %pad_maximum_fusion.refs_3_), channel_id=1, source_target_pairs={{0,64},{64,128},{128,192},{192,0},{1,65},{65,129},{129,193},{193,1... | collective-permute-start | bytes 1179656 | tf_op jit(solution)/shard_map/weight_rings/ppermute | solution.py:23
  25.5 20.9 %collective-permute-start.4 = (bf16[256,768]{1,0:T(8,128)(2,1)S(1)}, bf16[256,768]{1,0:T(8,128)(2,1)S(1)}, u32[]{:S(2)}, u32[]{:S(2)}) collective-permute-start(bf16[256,768]{1,0:T(8,128)(2,1)S(1)} %pad_maximum_fusion.refs_3_), channel_id=1, source_target_pairs={{0,128},{64,192},{128,0},{192,64},{1,129},{65,193},{129,1},{193,65... | collective-permute-start | bytes 1179656 | tf_op jit(solution)/shard_map/weight_rings/ppermute | solution.py:23
  41.4 0.7 copy-start.3
  45.7 0.8 copy-start.5
  46.5 0.7 copy-start.7
  48.0 18.9 %collective-permute-start.10 = (bf16[512,768]{1,0:T(8,128)(2,1)S(1)}, bf16[512,768]{1,0:T(8,128)(2,1)S(1)}, u32[]{:S(2)}, u32[]{:S(2)}) collective-permute-start(bf16[512,768]{1,0:T(8,128)(2,1)S(1)} %constant_dynamic-update-slice_fusion.refs_4_), channel_id=1, source_target_pairs={{0,192},{64,0},{128,64},{192,128},{1,193},{65,1},{129,65},{193,129... | collective-permute-start | bytes 2359304 | tf_op jit(solution)/shard_map/weight_rings/ppermute | solution.py:23
  48.1 20.1 %collective-permute-start.9 = (bf16[512,768]{1,0:T(8,128)(2,1)S(1)}, bf16[512,768]{1,0:T(8,128)(2,1)S(1)}, u32[]{:S(2)}, u32[]{:S(2)}) collective-permute-start(bf16[512,768]{1,0:T(8,128)(2,1)S(1)} %constant_dynamic-update-slice_fusion.refs_4_), channel_id=1, source_target_pairs={{0,64},{64,128},{128,192},{192,0},{1,65},{65,129},{129,193},{193,1... | collective-permute-start | bytes 2359304 | tf_op jit(solution)/shard_map/weight_rings/ppermute | solution.py:23
  49.6 10.2 %collective-permute-start.12 = (bf16[128,768]{1,0:T(8,128)(2,1)S(1)}, bf16[128,768]{1,0:T(8,128)(2,1)S(1)}, u32[]{:S(2)}, u32[]{:S(2)}) collective-permute-start(bf16[128,768]{1,0:T(8,128)(2,1)S(1)} %slice.29), channel_id=1, source_target_pairs={{0,48},{16,0},{32,16},{48,32},{1,49},{17,1},{33,17},{49,33},{2,50}... | collective-permute-start | bytes 589832 | tf_op jit(solution)/shard_map/weight_rings/ppermute | solution.py:23
  49.7 11.6 %collective-permute-start.11 = (bf16[128,768]{1,0:T(8,128)(2,1)S(1)}, bf16[128,768]{1,0:T(8,128)(2,1)S(1)}, u32[]{:S(2)}, u32[]{:S(2)}) collective-permute-start(bf16[128,768]{1,0:T(8,128)(2,1)S(1)} %slice.28), channel_id=1, source_target_pairs={{0,16},{16,32},{32,48},{48,0},{1,17},{17,33},{33,49},{49,1},{2,18}... | collective-permute-start | bytes 589832 | tf_op jit(solution)/shard_map/weight_rings/ppermute | solution.py:23
  70.6 19.6 %collective-permute-start.15 = (bf16[256,768]{1,0:T(8,128)(2,1)}, bf16[256,768]{1,0:T(8,128)(2,1)S(1)}, u32[]{:S(2)}, u32[]{:S(2)}) collective-permute-start(bf16[256,768]{1,0:T(8,128)(2,1)} %pad_maximum_fusion.1), channel_id=1, source_target_pairs={{0,16},{16,32},{32,48},{48,0},{1,17},{17,33},{33,49},{49,1},{2,18}... | collective-permute-start | bytes 1179656 | tf_op jit(solution)/shard_map/weight_rings/ppermute | solution.py:23
  71.4 20.5 %collective-permute-start.16 = (bf16[256,768]{1,0:T(8,128)(2,1)}, bf16[256,768]{1,0:T(8,128)(2,1)}, u32[]{:S(2)}, u32[]{:S(2)}) collective-permute-start(bf16[256,768]{1,0:T(8,128)(2,1)} %pad_maximum_fusion.2), channel_id=1, source_target_pairs={{0,48},{16,0},{32,16},{48,32},{1,49},{17,1},{33,17},{49,33},{2,50}... | collective-permute-start | bytes 1179656 | tf_op jit(solution)/shard_map/weight_rings/ppermute | solution.py:23
  75.0 16.9 %collective-permute-start.14 = (bf16[256,768]{1,0:T(8,128)(2,1)}, bf16[256,768]{1,0:T(8,128)(2,1)}, u32[]{:S(2)}, u32[]{:S(2)}) collective-permute-start(bf16[256,768]{1,0:T(8,128)(2,1)} %slice.31), channel_id=1, source_target_pairs={{0,192},{64,0},{128,64},{192,128},{1,193},{65,1},{129,65},{193,129... | collective-permute-start | bytes 1179656 | tf_op jit(solution)/shard_map/weight_rings/ppermute | solution.py:23
  75.3 16.6 %collective-permute-start.13 = (bf16[256,768]{1,0:T(8,128)(2,1)}, bf16[256,768]{1,0:T(8,128)(2,1)}, u32[]{:S(2)}, u32[]{:S(2)}) collective-permute-start(bf16[256,768]{1,0:T(8,128)(2,1)} %slice.30), channel_id=1, source_target_pairs={{0,64},{64,128},{128,192},{192,0},{1,65},{65,129},{129,193},{193,1... | collective-permute-start | bytes 1179656 | tf_op jit(solution)/shard_map/weight_rings/ppermute | solution.py:23
  76.5 16.5 %collective-permute-start.17 = (bf16[256,768]{1,0:T(8,128)(2,1)S(1)}, bf16[256,768]{1,0:T(8,128)(2,1)}, u32[]{:S(2)}, u32[]{:S(2)}) collective-permute-start(bf16[256,768]{1,0:T(8,128)(2,1)S(1)} %constant_dynamic-update-slice_fusion.2.refs_5_), channel_id=1, source_target_pairs={{0,128},{64,192},{128,0},{192,64},{1,129},{65,193},{129,1},{193,65... | collective-permute-start | bytes 1179656 | tf_op jit(solution)/shard_map/weight_rings/ppermute | solution.py:23
  77.4 1.7 %copy-start = (bf16[2304,512]{1,0:T(8,128)(2,1)S(1)}, bf16[2304,512]{1,0:T(8,128)(2,1)}, u32[]{:S(2)}) copy-start(bf16[2304,512]{1,0:T(8,128)(2,1)} %all-gather.5.cloned.1.call-done.refs_2_) | copy-start | bytes 7077892
  79.1 1.6 %copy-start.2 = (bf16[2048,512]{1,0:T(8,128)(2,1)S(1)}, bf16[2048,512]{1,0:T(8,128)(2,1)}, u32[]{:S(2)}) copy-start(bf16[2048,512]{1,0:T(8,128)(2,1)} %all-gather.3.cloned.1.call-done.refs_1_) | copy-start | bytes 6291460
  80.6 1.0 copy-start.4
  81.6 1.0 copy-start.6
  82.6 1.0 copy-start.8
  83.6 9.3 %copy-start.1 = (bf16[2304,512]{1,0:T(8,128)(2,1)S(1)}, bf16[2304,512]{1,0:T(8,128)(2,1)}, u32[]{:S(2)}) copy-start(bf16[2304,512]{1,0:T(8,128)(2,1)} %all-gather.5.cloned.1.call-done.refs_2_) | copy-start | bytes 7077892
  83.6 9.3 %copy-start.9 = (f32[16,512]{1,0:T(8,128)S(1)}, f32[16,512]{1,0:T(8,128)}, u32[]{:S(2)}) copy-start(f32[16,512]{1,0:T(8,128)} %decay.3) | copy-start | bytes 98308
  83.6 9.3 %copy-start.12 = (f32[3,3,512]{2,1,0:T(4,128)S(1)}, f32[3,3,512]{2,1,0:T(4,128)}, u32[]{:S(2)}) copy-start(f32[3,3,512]{2,1,0:T(4,128)} %refs_9_.1) | copy-start | bytes 55300
  90.2 16.6 %copy-start.10 = (f32[16,512]{1,0:T(8,128)S(1)}, f32[16,512]{1,0:T(8,128)}, u32[]{:S(2)}) copy-start(f32[16,512]{1,0:T(8,128)} %decay.3) | copy-start | bytes 98308
  90.2 16.6 %copy-start.11 = (f32[16,512]{1,0:T(8,128)S(1)}, f32[16,512]{1,0:T(8,128)}, u32[]{:S(2)}) copy-start(f32[16,512]{1,0:T(8,128)} %gain.3) | copy-start | bytes 98308
  90.3 16.6 %copy-start.13 = (f32[512]{0:T(512)S(1)}, f32[512]{0:T(512)}, u32[]{:S(2)}) copy-start(f32[512]{0:T(512)} %param.11) | copy-start | bytes 6148
  100.0 18.1 %all-to-all-start = ((f32[16,16,256]{2,1,0:T(8,128)}), f32[16,16,256]{2,1,0:T(8,128)S(1)}, u32[]{:S(2)}, u32[]{:S(2)}) async-start(f32[16,16,256]{2,1,0:T(8,128)} %broadcast_in_dim.3), calls=%async_computation | async-start | bytes 524288 | tf_op jit(solution)/shard_map/state_exchange/all_to_all | solution.py:318
  119.7 4.9 %collective-permute-start.18 = (bf16[256,256]{1,0:T(8,128)(2,1)S(1)}, bf16[256,256]{1,0:T(8,128)(2,1)S(1)}, u32[]{:S(2)}, u32[]{:S(2)}) collective-permute-start(bf16[256,256]{1,0:T(8,128)(2,1)S(1)} %get-tuple-element.44), channel_id=1, source_target_pairs={{0,8},{8,0},{1,9},{9,1},{2,10},{10,2},{3,11},{11,3},{4,12},{12,4},... | collective-permute-start | bytes 393224 | tf_op jit(solution)/shard_map/result_swap/ppermute | solution.py:340
Sparse Core Ops, SparseCore 0:
  9.2 31.8 all-gather.2
  48.1 25.4 all-gather.4

commit v8 on v7

--- a/solution.py
+++ b/solution.py
@@ -37,47 +37,51 @@
     return shifted(behind[:half], axis, 1), shifted(ahead[half:], axis, -1)
 
 
-def fetched(sizes, pos, near, swapped, pieces, blocks, tokv, wv, sem):
+def token_copies(sizes, pos, near, swapped, runs, tokv, sem):
     rows, depth, width, modes, seq = sizes
     k = depth // 16
     lines = rows + 2 * HALO
-    copies, at, seen = [], 0, set()
+    copies, at = [], 0
 
     def add(source, target):
         copies.append(pltpu.make_async_copy(source, target, sem.at[len(copies)]))
         return copies[-1]
 
-    for piece, first, n, dy, dh, skip in blocks:
-        add(pieces[piece].at[pl.ds(first, n), :], wv.at[pl.ds(at + skip, n), :]).start()
-        if (dy, dh) not in seen:
-            seen.add((dy, dh))
-            ys, hs = lax.rem(pos[1] - dy + 4, 4), lax.rem(pos[2] - dh + 4, 4)
-            ch = 2 * ys + lax.div(hs, 2)
-            lanes = pl.ds(pl.multiple_of(lax.rem(hs, 2) * k, k), k)
-            x = lax.rem(ch, 4)
-            other = lax.rem(lax.div(ch, 4) + pos[4], 2)
-            to = pl.ds(at, k)
-            line = pl.multiple_of(x * lines + HALO * other, HALO)
-            add(swapped.at[pl.ds(line, HALO), lanes], tokv.at[pl.ds(0, HALO), to]).start()
-            for core in range(2):
-                target = tokv.at[pl.ds(HALO + core * rows, rows), to]
-                line = pl.multiple_of((4 * core + x) * rows, rows)
-                copy = add(near.at[pl.ds(line, rows), lanes], target)
-                pl.when(other == 0)(copy.start)
-                line = pl.multiple_of((4 * core + x) * lines + 2 * HALO, HALO)
-                source = swapped.at[pl.ds(line, rows), lanes]
-                copy = pltpu.make_async_copy(source, target, sem.at[len(copies) - 1])
-                pl.when(other == 1)(copy.start)
-        if skip + n == k:
-            at += k
+    for dy, dh, skip, n in runs:
+        ys, hs = lax.rem(pos[1] - dy + 4, 4), lax.rem(pos[2] - dh + 4, 4)
+        ch = 2 * ys + lax.div(hs, 2)
+        lanes = pl.ds(pl.multiple_of(lax.rem(hs, 2) * k + skip, 128), n)
+        x = lax.rem(ch, 4)
+        other = lax.rem(lax.div(ch, 4) + pos[4], 2)
+        to = pl.ds(at, n)
+        line = pl.multiple_of(x * lines + HALO * other, HALO)
+        add(swapped.at[pl.ds(line, HALO), lanes], tokv.at[pl.ds(0, HALO), to]).start()
+        for core in range(2):
+            target = tokv.at[pl.ds(HALO + core * rows, rows), to]
+            line = pl.multiple_of((4 * core + x) * rows, rows)
+            copy = add(near.at[pl.ds(line, rows), lanes], target)
+            pl.when(other == 0)(copy.start)
+            line = pl.multiple_of((4 * core + x) * lines + 2 * HALO, HALO)
+            source = swapped.at[pl.ds(line, rows), lanes]
+            copy = pltpu.make_async_copy(source, target, sem.at[len(copies) - 1])
+            pl.when(other == 1)(copy.start)
+        at += n
     return copies
 
 
-def project_kernel(sizes, blocks, *refs):
-    rows, depth, width, modes, seq = sizes
-    pos, near, swapped, *pieces = refs[:-4]
-    sums, tokv, wv, sem = refs[-4:]
-    for copy in fetched(sizes, pos, near, swapped, pieces, blocks, tokv, wv, sem):
+def project_kernel(sizes, early, late, *refs):
+    rows, depth, width, modes, seq = sizes
+    pos, near, swapped, *pieces = refs[:-7]
+    sums, late_tok, tokv, wv, tok_sem, late_sem, w_sem = refs[-7:]
+    copies, at = [], 0
+    for number, piece in enumerate(pieces):
+        n = piece.shape[0]
+        copies.append(pltpu.make_async_copy(piece, wv.at[pl.ds(at, n), :], w_sem.at[number]))
+        copies[-1].start()
+        at += n
+    copies += token_copies(sizes, pos, near, swapped, early, tokv, tok_sem)
+    late_copies = token_copies(sizes, pos, near, swapped, late, late_tok, late_sem)
+    for copy in copies:
         copy.wait()
 
     @pl.loop(0, 3)
@@ -87,19 +91,24 @@
         for lh in range(width // 128):
             sums[j * (width // 128) + lh] = part[:, lh * 128 : lh * 128 + 128]
 
-
-def state_kernel(sizes, blocks, *refs):
-    rows, depth, width, modes, seq = sizes
-    pos, near, swapped, *pieces = refs[:-11]
-    sums, taps, decay, gate, product, inside, state, tokv, wv, acc, sem = refs[-11:]
+    for copy in late_copies:
+        copy.wait()
+
+
+def state_kernel(sizes, *refs):
+    rows, depth, width, modes, seq = sizes
+    pos, late_tok, *pieces = refs[:-8]
+    sums, taps, decay, gate, product, inside, state, acc = refs[-8:]
     c = pos[3]
-    for copy in fetched(sizes, pos, near, swapped, pieces, blocks, tokv, wv, sem):
-        copy.wait()
+    k = depth // 16
 
     @pl.loop(0, 3)
     def _(j):
         cols = pl.ds(pl.multiple_of(j * width, width), width)
-        part = jnp.dot(tokv[...], wv[:, cols], preferred_element_type=F32)
+        part = sum(
+            jnp.dot(late_tok[:, i * k : i * k + k], piece[:, cols], preferred_element_type=F32)
+            for i, piece in enumerate(pieces)
+        )
         for lh in range(width // 128):
             chunk = j * (width // 128) + lh
             new = part[:, lh * 128 : lh * 128 + 128]
@@ -243,7 +252,7 @@
     with jax.named_scope("weight_rings"):
         two, half = 2 * k, k
         pair = jnp.concatenate(beside, 0)
-        far_pair, opposite = both_ways(pair, "y"), onward(*beside, "h")
+        far_pair, opposite = both_ways(pair, "y"), onward(pair[:two], pair[two:], "h")
         far_pair, opposite = tie((far_pair, opposite))
         opposite = jnp.concatenate(opposite, 0)
         last = shifted(opposite, "y", 2)
@@ -252,25 +261,17 @@
         seconds = jnp.concatenate([p[two + half :] for p in far_pair], 0)
         far_opposite = shifted(firsts, "h", 1), shifted(seconds, "h", -1)
 
-    early = [own, pair, opposite, *far, *far_pair, farther]
-    early_blocks = [(0, 0, two, 0, 0, 0), (1, 0, two, 0, 1, 0), (1, two, two, 0, -1, 0), (2, 0, two, 0, 2, 0)]
+    early = [own, pair, opposite]
+    early_runs = [(0, dh, 0, two) for dh in (0, 1, -1, 2)]
     for side, dy in enumerate((1, -1)):
-        early_blocks += [
-            (3 + side, 0, two, dy, 0, 0),
-            (5 + side, 0, two, dy, 1, 0),
-            (5 + side, two, two, dy, -1, 0),
-        ]
-    early_blocks += [(7, 0, two, 2, 0, 0)]
+        early += [far[side], far_pair[side]]
+        early_runs += [(dy, dh, 0, two) for dh in (0, 1, -1)]
+    early += [farther]
+    early_runs += [(2, 0, 0, two)]
     late = [*farther_pair, *far_opposite, last]
-    late_blocks = [
-        (0, 0, two, 2, 1, 0),
-        (1, 0, two, 2, -1, 0),
-        (2, 0, half, 1, 2, 0),
-        (3, 0, half, 1, 2, half),
-        (2, half, half, -1, 2, 0),
-        (3, half, half, -1, 2, half),
-        (4, 0, two, 2, 2, 0),
-    ]
+    late_runs = [(2, 1, 0, two), (2, -1, 0, two)]
+    late_runs += [(dy, 2, skip, half) for skip in (0, half) for dy in (1, -1)]
+    late_runs += [(2, 2, 0, two)]
 
     vmem = pl.BlockSpec(memory_space=pltpu.VMEM)
     smem = pl.BlockSpec(memory_space=pltpu.SMEM)
@@ -280,39 +281,45 @@
     lines = 2 * rows + HALO
     chunks = (3 * width // 128, lines, 128)
 
-    def held(n):
-        return [pltpu.VMEM((lines, n * two), BF16), pltpu.VMEM((n * two, 3 * width), BF16)]
-
-    def sems(blocks, n):
-        return pltpu.SemaphoreType.DMA((len(blocks) + 3 * n,))
-
-    sums = pl.pallas_call(
-        functools.partial(project_kernel, sizes, early_blocks),
-        out_shape=jax.ShapeDtypeStruct(chunks, F32),
+    def dma(n):
+        return pltpu.SemaphoreType.DMA((n,))
+
+    sums, late_tok = pl.pallas_call(
+        functools.partial(project_kernel, sizes, early_runs, late_runs),
+        out_shape=(
+            jax.ShapeDtypeStruct(chunks, F32),
+            jax.ShapeDtypeStruct((lines, 5 * two), BF16),
+        ),
         in_specs=[smem] + [hbm] * (2 + len(early)),
-        out_specs=vmem,
-        scratch_shapes=[*held(11), sems(early_blocks, 11)],
+        out_specs=(vmem, vmem),
+        scratch_shapes=[
+            pltpu.VMEM((lines, 11 * two), BF16),
+            pltpu.VMEM((11 * two, 3 * width), BF16),
+            dma(3 * len(early_runs)),
+            dma(3 * len(late_runs)),
+            dma(len(early)),
+        ],
         compiler_params=pltpu.CompilerParams(vmem_limit_bytes=14 * 2**20),
         cost_estimate=pl.CostEstimate(
             flops=2 * lines * 11 * two * 3 * width, bytes_accessed=9_000_000, transcendentals=0
         ),
         name="project",
     )(pos, near, swapped, *early)
-    params = pltpu.CompilerParams(vmem_limit_bytes=12 * 2**20)
+    params = pltpu.CompilerParams(vmem_limit_bytes=8 * 2**20)
     gate, product, inside, state = pl.pallas_call(
-        functools.partial(state_kernel, sizes, late_blocks),
+        functools.partial(state_kernel, sizes),
         out_shape=(
             full,
             full,
             jax.ShapeDtypeStruct((modes, SUB, width), F32),
             jax.ShapeDtypeStruct((modes, width), F32),
         ),
-        in_specs=[smem] + [hbm] * (2 + len(late)) + [vmem] * 3,
+        in_specs=[smem] + [vmem] * (4 + len(late)),
         out_specs=(vmem,) * 4,
-        scratch_shapes=[*held(5), pltpu.VMEM(chunks, F32), sems(late_blocks, 5)],
+        scratch_shapes=[pltpu.VMEM(chunks, F32)],
         compiler_params=params,
         name="states",
-    )(pos, near, swapped, *late, sums, taps, decay)
+    )(pos, late_tok, *late, sums, taps, decay)
 
     with jax.named_scope("state_exchange"):
         states = lax.all_to_all(

time: 133 us -> 131 us (0.985)
  Pallas kernels: 16.3 us -> 14.8 us
    unnamed x33 -> x31, local copies, waits for them, and re-layouts: 9.78 us -> 7.33 us
    slice x4, local copies, waits for them, and re-layouts: 1.57 us -> 3.42 us  [onward(): return (shifted(behind[:half], axis, 1), shifted(ahead[half:], axis, -1))]
    pallas_call x2, Pallas kernels: 12.9 us -> 11.4 us  [the longest x1 6.24 us: body(): pl.pallas_call(functools.partial(project_kernel, sizes, early_runs, late_...]
  transfers between devices with their start and end apart: 22 -> 22, of which waited for: 13 -> 13; matrix products, arithmetic and copies ran while one was open for 4% -> 6% of each run, Pallas kernels for 6% -> 6%
where the time goes in v8:
time: 131 us; the launch traced here: 130 us
  waiting for transfers between devices  48.9 us (37%)
  starting transfers between devices  37.9 us (29%)
  Pallas kernels  14.8 us (11%)
  between operations  13.7 us (10%)
  local copies, waits for them, and re-layouts  12 us (9%)
  other arithmetic  3.15 us (2%)
    ppermute x14, waiting for transfers between devices, shifted(): return lax.ppermute(array, axis, [(i, (i + step) % n) for i in range(n)])  36.9 us
    ppermute x14, starting transfers between devices, shifted(): return lax.ppermute(array, axis, [(i, (i + step) % n) for i in range(n)])  17.7 us
    all_to_all x1, waiting for transfers between devices, body(): lax.all_to_all(jnp.broadcast_to(state, (16, *state.shape)), ('y', 'h'), 0...  9.38 us
    unnamed x31, local copies, waits for them, and re-layouts  7.33 us
    all_to_all x1, starting transfers between devices, body(): lax.all_to_all(jnp.broadcast_to(state, (16, *state.shape)), ('y', 'h'), 0...  6.83 us
    pallas_call x1, Pallas kernels, body(): pl.pallas_call(functools.partial(project_kernel, sizes, early_runs, late_...  6.24 us
    pallas_call x1, Pallas kernels, body(): pl.pallas_call(functools.partial(state_kernel, sizes), out_shape=(full, f...  5.15 us
    ppermute x1, starting transfers between devices, body(): other_halo = lax.ppermute(tail, (*CTX, 'l'), [(i, j ^ 1) for i, j in route])  4.77 us
  transfers between devices with their start and end apart: 22, of which 13 were waited for; matrix products, arithmetic and copies ran while one was open for 6% of the time, Pallas kernels for 6%

profile of v8, /device:TPU:1, one launch (start us, length us, event | category | flops | bytes accessed | tf_op | source)
XLA Modules:
  0.0 130.4 jit_solution(7309234430383430729)
XLA Ops:
  6.5 0.7 all-gather.3.cloned.1.call-update
  7.3 0.0 all-gather.5.cloned.1.call-start
  7.3 1.2 copy.10
  8.6 0.1 copy.13
  8.8 3.3 %collective-permute-start = (bf16[128,768]{1,0:T(8,128)(2,1)S(1)}, bf16[128,768]{1,0:T(8,128)(2,1)S(1)}, u32[]{:S(2)}, u32[]{:S(2)}) collective-permute-start(bf16[128,768]{1,0:T(8,128)(2,1)S(1)} %bitcast.17), channel_id=1, source_target_pairs={{0,8},{8,0},{1,9},{9,1},{2,10},{10,2},{3,11},{11,3},{4,12},{12,4},... | collective-permute-start | bytes 589832 | tf_op jit(solution)/shard_map/weight_gather/ppermute | solution.py:234
  12.1 0.0 collective-permute-start.3
  12.1 0.1 copy.12
  12.2 0.9 collective-permute-done
  13.2 4.8 %collective-permute-start.2 = (bf16[16,512]{1,0:T(8,128)(2,1)S(1)}, bf16[16,512]{1,0:T(8,128)(2,1)S(1)}, u32[]{:S(2)}, u32[]{:S(2)}) collective-permute-start(bf16[16,512]{1,0:T(8,128)(2,1)S(1)} %slice.27), channel_id=1, source_target_pairs={{8,20},{12,16},{24,36},{28,32},{40,52},{44,48},{56,68},{60,64},{72... | collective-permute-start | bytes 49160 | tf_op jit(solution)/shard_map/token_swap/ppermute | solution.py:241
  18.0 1.3 collective-permute-start.1
  19.3 1.7 %collective-permute-start.8 = (bf16[256,768]{1,0:T(8,128)(2,1)S(1)}, bf16[256,768]{1,0:T(8,128)(2,1)S(1)}, u32[]{:S(2)}, u32[]{:S(2)}) collective-permute-start(bf16[256,768]{1,0:T(8,128)(2,1)S(1)} %pad_maximum_fusion.refs_3_), channel_id=1, source_target_pairs={{0,48},{16,0},{32,16},{48,32},{1,49},{17,1},{33,17},{49,33},{2,50}... | collective-permute-start | bytes 1179656 | tf_op jit(solution)/shard_map/weight_rings/ppermute | solution.py:23
  21.0 1.8 %collective-permute-start.7 = (bf16[256,768]{1,0:T(8,128)(2,1)S(1)}, bf16[256,768]{1,0:T(8,128)(2,1)S(1)}, u32[]{:S(2)}, u32[]{:S(2)}) collective-permute-start(bf16[256,768]{1,0:T(8,128)(2,1)S(1)} %pad_maximum_fusion.refs_3_), channel_id=1, source_target_pairs={{0,16},{16,32},{32,48},{48,0},{1,17},{17,33},{33,49},{49,1},{2,18}... | collective-permute-start | bytes 1179656 | tf_op jit(solution)/shard_map/weight_rings/ppermute | solution.py:23
  22.8 0.0 collective-permute-done.2
  22.8 2.7 %collective-permute-start.6 = (bf16[256,768]{1,0:T(8,128)(2,1)S(1)}, bf16[256,768]{1,0:T(8,128)(2,1)S(1)}, u32[]{:S(2)}, u32[]{:S(2)}) collective-permute-start(bf16[256,768]{1,0:T(8,128)(2,1)S(1)} %pad_maximum_fusion.refs_3_), channel_id=1, source_target_pairs={{0,192},{64,0},{128,64},{192,128},{1,193},{65,1},{129,65},{193,129... | collective-permute-start | bytes 1179656 | tf_op jit(solution)/shard_map/weight_rings/ppermute | solution.py:23
  25.5 0.0 collective-permute-done.1
  25.5 0.0 collective-permute-start.5
  25.5 0.0 collective-permute-done.3
  25.5 1.6 %collective-permute-start.4 = (bf16[256,768]{1,0:T(8,128)(2,1)S(1)}, bf16[256,768]{1,0:T(8,128)(2,1)S(1)}, u32[]{:S(2)}, u32[]{:S(2)}) collective-permute-start(bf16[256,768]{1,0:T(8,128)(2,1)S(1)} %pad_maximum_fusion.refs_3_), channel_id=1, source_target_pairs={{0,128},{64,192},{128,0},{192,64},{1,129},{65,193},{129,1},{193,65... | collective-permute-start | bytes 1179656 | tf_op jit(solution)/shard_map/weight_rings/ppermute | solution.py:23
  27.2 11.2 %collective-permute-done.8 = bf16[256,768]{1,0:T(8,128)(2,1)S(1)} collective-permute-done((bf16[256,768]{1,0:T(8,128)(2,1)S(1)}, bf16[256,768]{1,0:T(8,128)(2,1)S(1)}, u32[]{:S(2)}, u32[]{:S(2)}) %collective-permute-start.8) | collective-permute-done | bytes 393248 | tf_op jit(solution)/shard_map/weight_rings/ppermute | solution.py:23
  38.4 0.9 collective-permute-done.7
  39.3 2.1 %collective-permute-done.6.refs_8_ = bf16[256,768]{1,0:T(8,128)(2,1)S(1)} collective-permute-done((bf16[256,768]{1,0:T(8,128)(2,1)S(1)}, bf16[256,768]{1,0:T(8,128)(2,1)S(1)}, u32[]{:S(2)}, u32[]{:S(2)}) %collective-permute-start.6) | collective-permute-done | bytes 393248 | tf_op jit(solution)/shard_map/weight_rings/ppermute | solution.py:23
  41.4 4.3 %collective-permute-done.5.refs_6_ = bf16[256,768]{1,0:T(8,128)(2,1)S(1)} collective-permute-done((bf16[256,768]{1,0:T(8,128)(2,1)S(1)}, bf16[256,768]{1,0:T(8,128)(2,1)S(1)}, u32[]{:S(2)}, u32[]{:S(2)}) %collective-permute-start.5) | collective-permute-done | bytes 393248 | tf_op jit(solution)/shard_map/weight_rings/ppermute | solution.py:23
  45.7 0.8 copy-done.4
  46.5 0.7 pad_maximum_fusion.3
  47.2 0.0 all-gather.5.cloned.1.call-update
  47.3 0.1 collective-permute-start.10
  47.4 1.5 %collective-permute-start.9 = (bf16[512,768]{1,0:T(8,128)(2,1)S(1)}, bf16[512,768]{1,0:T(8,128)(2,1)S(1)}, u32[]{:S(2)}, u32[]{:S(2)}) collective-permute-start(bf16[512,768]{1,0:T(8,128)(2,1)S(1)} %constant_dynamic-update-slice_fusion.refs_4_), channel_id=1, source_target_pairs={{0,64},{64,128},{128,192},{192,0},{1,65},{65,129},{129,193},{193,1... | collective-permute-start | bytes 2359304 | tf_op jit(solution)/shard_map/weight_rings/ppermute | solution.py:23
  48.9 0.9 slice.28
  49.8 0.9 slice.29
  50.8 0.1 collective-permute-start.12
  50.9 2.4 %collective-permute-start.11 = (bf16[128,768]{1,0:T(8,128)(2,1)S(1)}, bf16[128,768]{1,0:T(8,128)(2,1)S(1)}, u32[]{:S(2)}, u32[]{:S(2)}) collective-permute-start(bf16[128,768]{1,0:T(8,128)(2,1)S(1)} %slice.28), channel_id=1, source_target_pairs={{0,16},{16,32},{32,48},{48,0},{1,17},{17,33},{33,49},{49,1},{2,18}... | collective-permute-start | bytes 589832 | tf_op jit(solution)/shard_map/weight_rings/ppermute | solution.py:23
  53.2 7.8 %collective-permute-done.12 = bf16[128,768]{1,0:T(8,128)(2,1)S(1)} collective-permute-done((bf16[128,768]{1,0:T(8,128)(2,1)S(1)}, bf16[128,768]{1,0:T(8,128)(2,1)S(1)}, u32[]{:S(2)}, u32[]{:S(2)}) %collective-permute-start.12) | collective-permute-done | bytes 196640 | tf_op jit(solution)/shard_map/weight_rings/ppermute | solution.py:23
  61.0 1.0 collective-permute-done.11
  62.0 4.2 %collective-permute-done.10.refs_9_ = bf16[512,768]{1,0:T(8,128)(2,1)S(1)} collective-permute-done((bf16[512,768]{1,0:T(8,128)(2,1)S(1)}, bf16[512,768]{1,0:T(8,128)(2,1)S(1)}, u32[]{:S(2)}, u32[]{:S(2)}) %collective-permute-start.10) | collective-permute-done | bytes 786464 | tf_op jit(solution)/shard_map/weight_rings/ppermute | solution.py:23
  66.3 1.2 collective-permute-done.9.refs_7_
  67.5 0.8 slice.30
  68.3 0.8 slice.31
  69.0 0.1 fusion
  69.1 0.8 pad_maximum_fusion.1
  69.9 0.8 pad_maximum_fusion.2
  70.7 3.6 %collective-permute-start.16 = (bf16[256,768]{1,0:T(8,128)(2,1)}, bf16[256,768]{1,0:T(8,128)(2,1)}, u32[]{:S(2)}, u32[]{:S(2)}) collective-permute-start(bf16[256,768]{1,0:T(8,128)(2,1)} %pad_maximum_fusion.2), channel_id=1, source_target_pairs={{0,48},{16,0},{32,16},{48,32},{1,49},{17,1},{33,17},{49,33},{2,50}... | collective-permute-start | bytes 1179656 | tf_op jit(solution)/shard_map/weight_rings/ppermute | solution.py:23
  74.3 0.3 collective-permute-start.14
  74.6 1.2 collective-permute-start.13
  75.8 0.8 collective-permute-start.17
  76.6 0.1 stack.23.refs_0_.pos
  76.7 1.7 %copy-done = bf16[2304,512]{1,0:T(8,128)(2,1)S(1)} copy-done((bf16[2304,512]{1,0:T(8,128)(2,1)S(1)}, bf16[2304,512]{1,0:T(8,128)(2,1)}, u32[]{:S(2)}) %copy-start) | copy-done | bytes 2359320
  78.4 1.6 %copy-done.1 = bf16[2048,512]{1,0:T(8,128)(2,1)S(1)} copy-done((bf16[2048,512]{1,0:T(8,128)(2,1)S(1)}, bf16[2048,512]{1,0:T(8,128)(2,1)}, u32[]{:S(2)}) %copy-start.1) | copy-done | bytes 2097176
  80.0 1.0 copy-done.3
  81.0 1.0 copy-done.5
  82.0 6.2 %project.1 = (f32[6,528,128]{2,1,0:T(8,128)S(1)}, bf16[528,1280]{1,0:T(8,128)(2,1)S(1)}) custom-call(s32[5]{0:T(128)S(1)} %stack.23.refs_0_.pos, bf16[2048,512]{1,0:T(8,128)(2,1)S(1)} %copy-done.1, bf16[2304,512]{1,0:T(8,128)(2,1)S(1)} %copy-done, bf16[256,768]{1,0:T(8,128)(2,1)S(1)} %pad_maximum_fusion.refs_3_, ...), custom_call_target="tpu_custom_call" | custom-call | flops 2283798528 | bytes 9000000 | tf_op jit(solution)/shard_map/project/pallas_call | solution.py:287
  88.2 0.0 collective-permute-done.15.refs_4_
  88.2 3.9 %collective-permute-done.16.refs_5_ = bf16[256,768]{1,0:T(8,128)(2,1)} collective-permute-done((bf16[256,768]{1,0:T(8,128)(2,1)}, bf16[256,768]{1,0:T(8,128)(2,1)}, u32[]{:S(2)}, u32[]{:S(2)}) %collective-permute-start.16) | collective-permute-done | bytes 393248 | tf_op jit(solution)/shard_map/weight_rings/ppermute | solution.py:23
  92.1 0.0 collective-permute-done.14.refs_3_
  92.1 0.1 collective-permute-done.17.refs_6_
  92.3 0.0 copy-start.10
  92.3 5.2 %states.1 = (f32[64,8,256]{2,1,0:T(8,128)S(1)}, f32[64,8,256]{2,1,0:T(8,128)S(1)}, f32[16,8,256]{2,1,0:T(8,128)S(1)}, f32[16,256]{1,0:T(8,128)S(1)}) custom-call(s32[5]{0:T(128)S(1)} %stack.23.refs_0_.pos, bf16[528,1280]{1,0:T(8,128)(2,1)S(1)} %get-tuple-element.41.refs_1_, bf16[256,768]{1,0:T(8,128)(2,1)} %collective-permute-done.13.refs_2_, ...), custom_call_target="tpu_custom_call" | custom-call | tf_op jit(solution)/shard_map/states/pallas_call | solution.py:309
  97.5 0.7 broadcast_in_dim.3
  98.2 6.8 %all-to-all-start = ((f32[16,16,256]{2,1,0:T(8,128)}), f32[16,16,256]{2,1,0:T(8,128)S(1)}, u32[]{:S(2)}, u32[]{:S(2)}) async-start(f32[16,16,256]{2,1,0:T(8,128)} %broadcast_in_dim.3), calls=%async_computation | async-start | bytes 524288 | tf_op jit(solution)/shard_map/state_exchange/all_to_all | solution.py:325
  105.1 1.9 %local.1 = f32[64,8,256]{2,1,0:T(8,128)S(1)} custom-call(s32[5]{0:T(128)S(1)} %stack.23.refs_0_.pos, f32[64,8,256]{2,1,0:T(8,128)S(1)} %get-tuple-element.44.product, f32[16,512]{1,0:T(8,128)S(1)} %copy-done.8, f32[16,512]{1,0:T(8,128)S(1)} %copy-done.7, f32[1,512]{1,0:T(1,128)S(1)} %bitcast.14), custom_call_target="tpu_custom_call" | custom-call | flops 20000000 | bytes 1000000 | tf_op jit(solution)/shard_map/local/pallas_call | solution.py:328
  106.9 9.4 %all-to-all-done.states = f32[16,16,256]{2,1,0:T(8,128)S(1)} async-done(((f32[16,16,256]{2,1,0:T(8,128)}), f32[16,16,256]{2,1,0:T(8,128)S(1)}, u32[]{:S(2)}, u32[]{:S(2)}) %all-to-all-start) | async-done | bytes 262176 | tf_op jit(solution)/shard_map/state_exchange/all_to_all | solution.py:325
  116.3 1.5 %finish.1 = (bf16[256,256]{1,0:T(8,128)(2,1)S(1)}, bf16[256,256]{1,0:T(8,128)(2,1)S(1)}) custom-call(s32[5]{0:T(128)S(1)} %stack.23.refs_0_.pos, f32[64,8,256]{2,1,0:T(8,128)S(1)} %get-tuple-element.43.gate, f32[64,8,256]{2,1,0:T(8,128)S(1)} %local.1, f32[16,8,256]{2,1,0:T(8,128)S(1)} %get-tuple-element.45.inside, f32[16,16,256]{2,1,0:T(8,128)S(1)} %all-to-all-done.states, ...), custom_call_target="tpu_custom_call" | custom-call | tf_op jit(solution)/shard_map/finish/pallas_call | solution.py:337
  117.8 3.9 %collective-permute-start.18 = (bf16[256,256]{1,0:T(8,128)(2,1)S(1)}, bf16[256,256]{1,0:T(8,128)(2,1)S(1)}, u32[]{:S(2)}, u32[]{:S(2)}) collective-permute-start(bf16[256,256]{1,0:T(8,128)(2,1)S(1)} %get-tuple-element.48), channel_id=1, source_target_pairs={{0,8},{8,0},{1,9},{9,1},{2,10},{10,2},{3,11},{11,3},{4,12},{12,4},... | collective-permute-start | bytes 393224 | tf_op jit(solution)/shard_map/result_swap/ppermute | solution.py:347
  121.8 1.0 collective-permute-done.18
  122.8 0.7 pad_maximum_fusion.4
  (38 shorter events, 0.3 us)
Async XLA Ops:
  6.5 5.6 %copy-start.13 = (bf16[256,512]{1,0:T(8,128)(2,1)S(1)}, bf16[256,512]{1,0:T(8,128)(2,1)}, u32[]{:S(2)}) copy-start(bf16[256,512]{1,0:T(8,128)(2,1)} %param.6) | copy-start | bytes 786436
  6.5 70.2 %all-gather.3.cloned.1.call-start = ((), (), s32[]{:S(2)}) async-start(), calls=%async_computation.1 | async-start | bytes 2359296 | tf_op jit(solution)/shard_map/token_gather/all_gather | solution.py:249
  7.3 69.4 %all-gather.5.cloned.1.call-start = ((), (), s32[]{:S(2)}) async-start(), calls=%async_computation.2 | async-start | bytes 2654208 | tf_op jit(solution)/shard_map/token_gather/all_gather | solution.py:251
  8.8 4.4 %collective-permute-start = (bf16[128,768]{1,0:T(8,128)(2,1)S(1)}, bf16[128,768]{1,0:T(8,128)(2,1)S(1)}, u32[]{:S(2)}, u32[]{:S(2)}) collective-permute-start(bf16[128,768]{1,0:T(8,128)(2,1)S(1)} %bitcast.17), channel_id=1, source_target_pairs={{0,8},{8,0},{1,9},{9,1},{2,10},{10,2},{3,11},{11,3},{4,12},{12,4},... | collective-permute-start | bytes 589832 | tf_op jit(solution)/shard_map/weight_gather/ppermute | solution.py:234
  12.1 13.4 %collective-permute-start.3 = (bf16[256,512]{1,0:T(8,128)(2,1)S(1)}, bf16[256,512]{1,0:T(8,128)(2,1)S(1)}, u32[]{:S(2)}, u32[]{:S(2)}) collective-permute-start(bf16[256,512]{1,0:T(8,128)(2,1)S(1)} %copy-done.13), channel_id=1, source_target_pairs={{0,4},{4,0},{1,5},{5,1},{2,6},{6,2},{3,7},{7,3},{8,12},{12,8},{9,1... | collective-permute-start | bytes 786440 | tf_op jit(solution)/shard_map/token_swap/ppermute | solution.py:238
  13.2 9.6 %collective-permute-start.2 = (bf16[16,512]{1,0:T(8,128)(2,1)S(1)}, bf16[16,512]{1,0:T(8,128)(2,1)S(1)}, u32[]{:S(2)}, u32[]{:S(2)}) collective-permute-start(bf16[16,512]{1,0:T(8,128)(2,1)S(1)} %slice.27), channel_id=1, source_target_pairs={{8,20},{12,16},{24,36},{28,32},{40,52},{44,48},{56,68},{60,64},{72... | collective-permute-start | bytes 49160 | tf_op jit(solution)/shard_map/token_swap/ppermute | solution.py:241
  18.0 7.5 %collective-permute-start.1 = (bf16[16,512]{1,0:T(8,128)(2,1)S(1)}, bf16[16,512]{1,0:T(8,128)(2,1)S(1)}, u32[]{:S(2)}, u32[]{:S(2)}) collective-permute-start(bf16[16,512]{1,0:T(8,128)(2,1)S(1)} %slice.27), channel_id=1, source_target_pairs={{8,16},{12,20},{24,32},{28,36},{40,48},{44,52},{56,64},{60,68},{72... | collective-permute-start | bytes 49160 | tf_op jit(solution)/shard_map/token_swap/ppermute | solution.py:240
  19.3 19.1 %collective-permute-start.8 = (bf16[256,768]{1,0:T(8,128)(2,1)S(1)}, bf16[256,768]{1,0:T(8,128)(2,1)S(1)}, u32[]{:S(2)}, u32[]{:S(2)}) collective-permute-start(bf16[256,768]{1,0:T(8,128)(2,1)S(1)} %pad_maximum_fusion.refs_3_), channel_id=1, source_target_pairs={{0,48},{16,0},{32,16},{48,32},{1,49},{17,1},{33,17},{49,33},{2,50}... | collective-permute-start | bytes 1179656 | tf_op jit(solution)/shard_map/weight_rings/ppermute | solution.py:23
  21.0 18.3 %collective-permute-start.7 = (bf16[256,768]{1,0:T(8,128)(2,1)S(1)}, bf16[256,768]{1,0:T(8,128)(2,1)S(1)}, u32[]{:S(2)}, u32[]{:S(2)}) collective-permute-start(bf16[256,768]{1,0:T(8,128)(2,1)S(1)} %pad_maximum_fusion.refs_3_), channel_id=1, source_target_pairs={{0,16},{16,32},{32,48},{48,0},{1,17},{17,33},{33,49},{49,1},{2,18}... | collective-permute-start | bytes 1179656 | tf_op jit(solution)/shard_map/weight_rings/ppermute | solution.py:23
  22.8 18.6 %collective-permute-start.6 = (bf16[256,768]{1,0:T(8,128)(2,1)S(1)}, bf16[256,768]{1,0:T(8,128)(2,1)S(1)}, u32[]{:S(2)}, u32[]{:S(2)}) collective-permute-start(bf16[256,768]{1,0:T(8,128)(2,1)S(1)} %pad_maximum_fusion.refs_3_), channel_id=1, source_target_pairs={{0,192},{64,0},{128,64},{192,128},{1,193},{65,1},{129,65},{193,129... | collective-permute-start | bytes 1179656 | tf_op jit(solution)/shard_map/weight_rings/ppermute | solution.py:23
  25.5 20.2 %collective-permute-start.5 = (bf16[256,768]{1,0:T(8,128)(2,1)S(1)}, bf16[256,768]{1,0:T(8,128)(2,1)S(1)}, u32[]{:S(2)}, u32[]{:S(2)}) collective-permute-start(bf16[256,768]{1,0:T(8,128)(2,1)S(1)} %pad_maximum_fusion.refs_3_), channel_id=1, source_target_pairs={{0,64},{64,128},{128,192},{192,0},{1,65},{65,129},{129,193},{193,1... | collective-permute-start | bytes 1179656 | tf_op jit(solution)/shard_map/weight_rings/ppermute | solution.py:23
  25.5 20.2 %collective-permute-start.4 = (bf16[256,768]{1,0:T(8,128)(2,1)S(1)}, bf16[256,768]{1,0:T(8,128)(2,1)S(1)}, u32[]{:S(2)}, u32[]{:S(2)}) collective-permute-start(bf16[256,768]{1,0:T(8,128)(2,1)S(1)} %pad_maximum_fusion.refs_3_), channel_id=1, source_target_pairs={{0,128},{64,192},{128,0},{192,64},{1,129},{65,193},{129,1},{193,65... | collective-permute-start | bytes 1179656 | tf_op jit(solution)/shard_map/weight_rings/ppermute | solution.py:23
  38.4 8.9 %copy-start.11 = (bf16[256,768]{1,0:T(8,128)(2,1)}, bf16[256,768]{1,0:T(8,128)(2,1)S(1)}, u32[]{:S(2)}) copy-start(bf16[256,768]{1,0:T(8,128)(2,1)S(1)} %collective-permute-done.8) | copy-start | bytes 1179652
  39.3 8.0 %copy-start.12 = (bf16[256,768]{1,0:T(8,128)(2,1)}, bf16[256,768]{1,0:T(8,128)(2,1)S(1)}, u32[]{:S(2)}) copy-start(bf16[256,768]{1,0:T(8,128)(2,1)S(1)} %collective-permute-done.7) | copy-start | bytes 1179652
  45.7 23.3 %copy-start.2 = (bf16[256,768]{1,0:T(8,128)(2,1)}, bf16[256,768]{1,0:T(8,128)(2,1)S(1)}, u32[]{:S(2)}) copy-start(bf16[256,768]{1,0:T(8,128)(2,1)S(1)} %collective-permute-done.5.refs_6_) | copy-start | bytes 1179652
  45.7 0.8 copy-start.4
  47.3 18.9 %collective-permute-start.10 = (bf16[512,768]{1,0:T(8,128)(2,1)S(1)}, bf16[512,768]{1,0:T(8,128)(2,1)S(1)}, u32[]{:S(2)}, u32[]{:S(2)}) collective-permute-start(bf16[512,768]{1,0:T(8,128)(2,1)S(1)} %constant_dynamic-update-slice_fusion.refs_4_), channel_id=1, source_target_pairs={{0,192},{64,0},{128,64},{192,128},{1,193},{65,1},{129,65},{193,129... | collective-permute-start | bytes 2359304 | tf_op jit(solution)/shard_map/weight_rings/ppermute | solution.py:23
  47.4 20.1 %collective-permute-start.9 = (bf16[512,768]{1,0:T(8,128)(2,1)S(1)}, bf16[512,768]{1,0:T(8,128)(2,1)S(1)}, u32[]{:S(2)}, u32[]{:S(2)}) collective-permute-start(bf16[512,768]{1,0:T(8,128)(2,1)S(1)} %constant_dynamic-update-slice_fusion.refs_4_), channel_id=1, source_target_pairs={{0,64},{64,128},{128,192},{192,0},{1,65},{65,129},{129,193},{193,1... | collective-permute-start | bytes 2359304 | tf_op jit(solution)/shard_map/weight_rings/ppermute | solution.py:23
  50.8 10.2 %collective-permute-start.12 = (bf16[128,768]{1,0:T(8,128)(2,1)S(1)}, bf16[128,768]{1,0:T(8,128)(2,1)S(1)}, u32[]{:S(2)}, u32[]{:S(2)}) collective-permute-start(bf16[128,768]{1,0:T(8,128)(2,1)S(1)} %slice.29), channel_id=1, source_target_pairs={{0,48},{16,0},{32,16},{48,32},{1,49},{17,1},{33,17},{49,33},{2,50}... | collective-permute-start | bytes 589832 | tf_op jit(solution)/shard_map/weight_rings/ppermute | solution.py:23
  50.9 11.2 %collective-permute-start.11 = (bf16[128,768]{1,0:T(8,128)(2,1)S(1)}, bf16[128,768]{1,0:T(8,128)(2,1)S(1)}, u32[]{:S(2)}, u32[]{:S(2)}) collective-permute-start(bf16[128,768]{1,0:T(8,128)(2,1)S(1)} %slice.28), channel_id=1, source_target_pairs={{0,16},{16,32},{32,48},{48,0},{1,17},{17,33},{33,49},{49,1},{2,18}... | collective-permute-start | bytes 589832 | tf_op jit(solution)/shard_map/weight_rings/ppermute | solution.py:23
  69.9 18.3 %collective-permute-start.15 = (bf16[256,768]{1,0:T(8,128)(2,1)}, bf16[256,768]{1,0:T(8,128)(2,1)}, u32[]{:S(2)}, u32[]{:S(2)}) collective-permute-start(bf16[256,768]{1,0:T(8,128)(2,1)} %pad_maximum_fusion.1), channel_id=1, source_target_pairs={{0,16},{16,32},{32,48},{48,0},{1,17},{17,33},{33,49},{49,1},{2,18}... | collective-permute-start | bytes 1179656 | tf_op jit(solution)/shard_map/weight_rings/ppermute | solution.py:23
  70.7 21.4 %collective-permute-start.16 = (bf16[256,768]{1,0:T(8,128)(2,1)}, bf16[256,768]{1,0:T(8,128)(2,1)}, u32[]{:S(2)}, u32[]{:S(2)}) collective-permute-start(bf16[256,768]{1,0:T(8,128)(2,1)} %pad_maximum_fusion.2), channel_id=1, source_target_pairs={{0,48},{16,0},{32,16},{48,32},{1,49},{17,1},{33,17},{49,33},{2,50}... | collective-permute-start | bytes 1179656 | tf_op jit(solution)/shard_map/weight_rings/ppermute | solution.py:23
  74.3 17.9 %collective-permute-start.14 = (bf16[256,768]{1,0:T(8,128)(2,1)}, bf16[256,768]{1,0:T(8,128)(2,1)}, u32[]{:S(2)}, u32[]{:S(2)}) collective-permute-start(bf16[256,768]{1,0:T(8,128)(2,1)} %slice.31), channel_id=1, source_target_pairs={{0,192},{64,0},{128,64},{192,128},{1,193},{65,1},{129,65},{193,129... | collective-permute-start | bytes 1179656 | tf_op jit(solution)/shard_map/weight_rings/ppermute | solution.py:23
  74.6 17.6 %collective-permute-start.13 = (bf16[256,768]{1,0:T(8,128)(2,1)}, bf16[256,768]{1,0:T(8,128)(2,1)}, u32[]{:S(2)}, u32[]{:S(2)}) collective-permute-start(bf16[256,768]{1,0:T(8,128)(2,1)} %slice.30), channel_id=1, source_target_pairs={{0,64},{64,128},{128,192},{192,0},{1,65},{65,129},{129,193},{193,1... | collective-permute-start | bytes 1179656 | tf_op jit(solution)/shard_map/weight_rings/ppermute | solution.py:23
  75.8 16.5 %collective-permute-start.17 = (bf16[256,768]{1,0:T(8,128)(2,1)S(1)}, bf16[256,768]{1,0:T(8,128)(2,1)}, u32[]{:S(2)}, u32[]{:S(2)}) collective-permute-start(bf16[256,768]{1,0:T(8,128)(2,1)S(1)} %constant_dynamic-update-slice_fusion.2.refs_5_), channel_id=1, source_target_pairs={{0,128},{64,192},{128,0},{192,64},{1,129},{65,193},{129,1},{193,65... | collective-permute-start | bytes 1179656 | tf_op jit(solution)/shard_map/weight_rings/ppermute | solution.py:23
  76.7 1.7 %copy-start = (bf16[2304,512]{1,0:T(8,128)(2,1)S(1)}, bf16[2304,512]{1,0:T(8,128)(2,1)}, u32[]{:S(2)}) copy-start(bf16[2304,512]{1,0:T(8,128)(2,1)} %all-gather.5.cloned.1.call-done.refs_2_) | copy-start | bytes 7077892
  78.4 1.6 %copy-start.1 = (bf16[2048,512]{1,0:T(8,128)(2,1)S(1)}, bf16[2048,512]{1,0:T(8,128)(2,1)}, u32[]{:S(2)}) copy-start(bf16[2048,512]{1,0:T(8,128)(2,1)} %all-gather.3.cloned.1.call-done.refs_1_) | copy-start | bytes 6291460
  80.0 1.0 copy-start.3
  81.0 1.0 copy-start.5
  81.9 10.3 %copy-start.6 = (f32[16,512]{1,0:T(8,128)S(1)}, f32[16,512]{1,0:T(8,128)}, u32[]{:S(2)}) copy-start(f32[16,512]{1,0:T(8,128)} %decay.3) | copy-start | bytes 98308
  81.9 10.3 %copy-start.9 = (f32[3,3,512]{2,1,0:T(4,128)S(1)}, f32[3,3,512]{2,1,0:T(4,128)}, u32[]{:S(2)}) copy-start(f32[3,3,512]{2,1,0:T(4,128)} %refs_8_.1) | copy-start | bytes 55300
  92.3 12.7 %copy-start.7 = (f32[16,512]{1,0:T(8,128)S(1)}, f32[16,512]{1,0:T(8,128)}, u32[]{:S(2)}) copy-start(f32[16,512]{1,0:T(8,128)} %decay.3) | copy-start | bytes 98308
  92.3 12.8 %copy-start.8 = (f32[16,512]{1,0:T(8,128)S(1)}, f32[16,512]{1,0:T(8,128)}, u32[]{:S(2)}) copy-start(f32[16,512]{1,0:T(8,128)} %gain.3) | copy-start | bytes 98308
  92.3 12.8 %copy-start.10 = (f32[512]{0:T(512)S(1)}, f32[512]{0:T(512)}, u32[]{:S(2)}) copy-start(f32[512]{0:T(512)} %param.11) | copy-start | bytes 6148
  98.2 18.1 %all-to-all-start = ((f32[16,16,256]{2,1,0:T(8,128)}), f32[16,16,256]{2,1,0:T(8,128)S(1)}, u32[]{:S(2)}, u32[]{:S(2)}) async-start(f32[16,16,256]{2,1,0:T(8,128)} %broadcast_in_dim.3), calls=%async_computation | async-start | bytes 524288 | tf_op jit(solution)/shard_map/state_exchange/all_to_all | solution.py:325
  117.8 4.9 %collective-permute-start.18 = (bf16[256,256]{1,0:T(8,128)(2,1)S(1)}, bf16[256,256]{1,0:T(8,128)(2,1)S(1)}, u32[]{:S(2)}, u32[]{:S(2)}) collective-permute-start(bf16[256,256]{1,0:T(8,128)(2,1)S(1)} %get-tuple-element.48), channel_id=1, source_target_pairs={{0,8},{8,0},{1,9},{9,1},{2,10},{10,2},{3,11},{11,3},{4,12},{12,4},... | collective-permute-start | bytes 393224 | tf_op jit(solution)/shard_map/result_swap/ppermute | solution.py:347
Sparse Core Ops, SparseCore 0:
  9.2 31.8 all-gather.2
  47.4 25.4 all-gather.4

commit v9 on v8

--- a/solution.py
+++ b/solution.py
@@ -32,9 +32,35 @@
     return shifted(piece, axis, 1), shifted(piece, axis, -1)
 
 
-def onward(behind, ahead, axis):
-    half = behind.shape[0] // 2
-    return shifted(behind[:half], axis, 1), shifted(ahead[half:], axis, -1)
+def relay_kernel(moves, count, *refs):
+    sources, targets, sem = refs[:count], refs[count:-1], refs[-1]
+    copies = []
+    for number, (source, first, n, target, at) in enumerate(moves):
+        copies.append(
+            pltpu.make_async_copy(
+                sources[source].at[pl.ds(first, n), :],
+                targets[target].at[pl.ds(at, n), :],
+                sem.at[number],
+            )
+        )
+        copies[-1].start()
+    for copy in copies:
+        copy.wait()
+
+
+def relayed(sources, moves, name):
+    heights = [max(at + n for _, _, n, target, at in moves if target == t) for t in range(1 + max(m[3] for m in moves))]
+    anywhere = pl.BlockSpec(memory_space=pl.ANY)
+    return pl.pallas_call(
+        functools.partial(relay_kernel, moves, len(sources)),
+        out_shape=[jax.ShapeDtypeStruct((h, sources[0].shape[1]), sources[0].dtype) for h in heights],
+        in_specs=[anywhere] * len(sources),
+        out_specs=[anywhere] * len(heights),
+        scratch_shapes=[pltpu.SemaphoreType.DMA((len(moves),))],
+        cost_estimate=pl.CostEstimate(flops=0, bytes_accessed=2_000_000, transcendentals=0),
+        compiler_params=pltpu.CompilerParams(vmem_limit_bytes=2**20),
+        name=name,
+    )(*sources)
 
 
 def token_copies(sizes, pos, near, swapped, runs, tokv, sem):
@@ -97,8 +123,8 @@
 
 def state_kernel(sizes, *refs):
     rows, depth, width, modes, seq = sizes
-    pos, late_tok, *pieces = refs[:-8]
-    sums, taps, decay, gate, product, inside, state, acc = refs[-8:]
+    pos, late_tok, *pieces = refs[:-9]
+    sums, taps, decay, gate, product, inside, states_out, acc, state = refs[-9:]
     c = pos[3]
     k = depth // 16
 
@@ -154,6 +180,8 @@
                 s = s + jnp.exp(-float(steps * by) * rates[m]) * later(s, by)
             inside[m, :, lanes] = later(s, 1)
             state[m : m + 1, lanes] = s[SUB - 1 :]
+    for r in range(16):
+        states_out[r] = state[...]
 
 
 def local_kernel(sizes, pos, product, gain, decay, skip, local):
@@ -251,14 +279,18 @@
         swapped = lax.all_gather(wide, ("c", "x"), axis=0, tiled=True)
     with jax.named_scope("weight_rings"):
         two, half = 2 * k, k
-        pair = jnp.concatenate(beside, 0)
-        far_pair, opposite = both_ways(pair, "y"), onward(pair[:two], pair[two:], "h")
+        moves = [(0, 0, two, 0, 0), (1, 0, two, 0, two), (0, 0, half, 1, 0), (1, half, half, 2, 0)]
+        pair, low, high = relayed(beside, moves, "relay_pair")
+        far_pair = both_ways(pair, "y")
+        opposite = shifted(low, "h", 1), shifted(high, "h", -1)
         far_pair, opposite = tie((far_pair, opposite))
-        opposite = jnp.concatenate(opposite, 0)
+        moves = [(0, 0, two, 0, 0), (1, two, two, 1, 0)]
+        moves += [(side, 0, half, 2, side * half) for side in range(2)]
+        moves += [(side, two + half, half, 3, side * half) for side in range(2)]
+        moves += [(2 + side, 0, half, 4, side * half) for side in range(2)]
+        behind, ahead, firsts, seconds, opposite = relayed([*far_pair, *opposite], moves, "relay_far")
         last = shifted(opposite, "y", 2)
-        farther_pair = onward(*far_pair, "y")
-        firsts = jnp.concatenate([p[:half] for p in far_pair], 0)
-        seconds = jnp.concatenate([p[two + half :] for p in far_pair], 0)
+        farther_pair = shifted(behind, "y", 1), shifted(ahead, "y", -1)
         far_opposite = shifted(firsts, "h", 1), shifted(seconds, "h", -1)
 
     early = [own, pair, opposite]
@@ -312,19 +344,17 @@
             full,
             full,
             jax.ShapeDtypeStruct((modes, SUB, width), F32),
-            jax.ShapeDtypeStruct((modes, width), F32),
+            jax.ShapeDtypeStruct((16, modes, width), F32),
         ),
         in_specs=[smem] + [vmem] * (4 + len(late)),
         out_specs=(vmem,) * 4,
-        scratch_shapes=[pltpu.VMEM(chunks, F32)],
+        scratch_shapes=[pltpu.VMEM(chunks, F32), pltpu.VMEM((modes, width), F32)],
         compiler_params=params,
         name="states",
     )(pos, late_tok, *late, sums, taps, decay)
 
     with jax.named_scope("state_exchange"):
-        states = lax.all_to_all(
-            jnp.broadcast_to(state, (16, *state.shape)), ("y", "h"), 0, 0, tiled=True
-        )
+        states = lax.all_to_all(state, ("y", "h"), 0, 0, tiled=True)
     local = pl.pallas_call(
         functools.partial(local_kernel, sizes),
         out_shape=full,

time: 131 us -> 127 us (0.969)
  local copies, waits for them, and re-layouts: 12 us -> 6.01 us
  waiting for transfers between devices: 48.9 us -> 53.5 us
  starting transfers between devices: 37.9 us -> 34.6 us
  Pallas kernels: 14.8 us -> 17.6 us
  other arithmetic: 3.15 us -> 1.62 us
    ppermute x14, waiting for transfers between devices: 36.9 us -> 40.8 us  [shifted(): return lax.ppermute(array, axis, [(i, (i + step) % n) for i in range(n)])]
    slice x5 -> x0, local copies, waits for them, and re-layouts: 3.48 us -> none  [the longest x4 3.42 us: onward(): return (shifted(behind[:half], axis, 1), shifted(ahead[half:], axis, -1))]
    all_to_all x1, starting transfers between devices: 6.83 us -> 3.53 us  [body(): states = lax.all_to_all(state, ('y', 'h'), 0, 0, tiled=True)]
    pallas_call x0 -> x2, Pallas kernels: none -> 2.3 us  [relayed(): pl.pallas_call(functools.partial(relay_kernel, moves, len(sources)), out_...]
    unnamed x31 -> x21, local copies, waits for them, and re-layouts: 7.33 us -> 5.57 us
    concatenate x2 -> x0, other arithmetic: 1.61 us -> none  [the longest x1 0.81 us: body(): firsts = jnp.concatenate([p[:half] for p in far_pair], 0)]
    ppermute x14, starting transfers between devices: 17.7 us -> 19.3 us  [shifted(): return lax.ppermute(array, axis, [(i, (i + step) % n) for i in range(n)])]
    ppermute x1, starting transfers between devices: 3.95 us -> 2.39 us  [body(): return in_order(c == 0, mine, lax.ppermute(theirs, 'c', SWAP), 1)]
  transfers between devices with their start and end apart: 22 -> 22, of which waited for: 13 -> 13; matrix products, arithmetic and copies ran while one was open for 6% -> 2% of each run, Pallas kernels for 6% -> 8%
where the time goes in v9:
time: 127 us
  waiting for transfers between devices  53.5 us (42%)
  starting transfers between devices  34.6 us (27%)
  Pallas kernels  17.6 us (14%)
  between operations  13.6 us (11%)
  local copies, waits for them, and re-layouts  6.01 us (5%)
  other arithmetic  1.62 us (1%)
    ppermute x14, waiting for transfers between devices, shifted(): return lax.ppermute(array, axis, [(i, (i + step) % n) for i in range(n)])  40.8 us
    ppermute x14, starting transfers between devices, shifted(): return lax.ppermute(array, axis, [(i, (i + step) % n) for i in range(n)])  19.3 us
    all_to_all x1, waiting for transfers between devices, body(): states = lax.all_to_all(state, ('y', 'h'), 0, 0, tiled=True)  10 us
    pallas_call x1, Pallas kernels, body(): pl.pallas_call(functools.partial(project_kernel, sizes, early_runs, late_...  6.06 us
    pallas_call x1, Pallas kernels, body(): pl.pallas_call(functools.partial(state_kernel, sizes), out_shape=(full, f...  5.88 us
    unnamed x21, local copies, waits for them, and re-layouts  5.57 us
    ppermute x1, starting transfers between devices, body(): other_halo = lax.ppermute(tail, (*CTX, 'l'), [(i, j ^ 1) for i, j in route])  4.77 us
    all_to_all x1, starting transfers between devices, body(): states = lax.all_to_all(state, ('y', 'h'), 0, 0, tiled=True)  3.53 us
  transfers between devices with their start and end apart: 22, of which 13 were waited for; matrix products, arithmetic and copies ran while one was open for 2% of the time, Pallas kernels for 8%

profile of v9, /device:TPU:1, one launch (start us, length us, event | category | flops | bytes accessed | tf_op | source)
XLA Modules:
  0.0 127.0 jit_solution(10439052421166815202)
XLA Ops:
  6.5 0.7 all-gather.3.cloned.1.call-update
  7.3 0.0 all-gather.5.cloned.1.call-start
  7.3 1.2 copy.10
  8.6 0.1 copy.13
  8.8 3.3 %collective-permute-start = (bf16[128,768]{1,0:T(8,128)(2,1)S(1)}, bf16[128,768]{1,0:T(8,128)(2,1)S(1)}, u32[]{:S(2)}, u32[]{:S(2)}) collective-permute-start(bf16[128,768]{1,0:T(8,128)(2,1)S(1)} %bitcast.17), channel_id=1, source_target_pairs={{0,8},{8,0},{1,9},{9,1},{2,10},{10,2},{3,11},{11,3},{4,12},{12,4},... | collective-permute-start | bytes 589832 | tf_op jit(solution)/shard_map/weight_gather/ppermute | solution.py:262
  12.1 0.0 collective-permute-start.3
  12.1 0.1 copy.12
  12.2 0.9 collective-permute-done
  13.2 4.8 %collective-permute-start.2 = (bf16[16,512]{1,0:T(8,128)(2,1)S(1)}, bf16[16,512]{1,0:T(8,128)(2,1)S(1)}, u32[]{:S(2)}, u32[]{:S(2)}) collective-permute-start(bf16[16,512]{1,0:T(8,128)(2,1)S(1)} %slice.3), channel_id=1, source_target_pairs={{8,20},{12,16},{24,36},{28,32},{40,52},{44,48},{56,68},{60,64},{72... | collective-permute-start | bytes 49160 | tf_op jit(solution)/shard_map/token_swap/ppermute | solution.py:269
  18.0 1.3 %collective-permute-start.1 = (bf16[16,512]{1,0:T(8,128)(2,1)S(1)}, bf16[16,512]{1,0:T(8,128)(2,1)S(1)}, u32[]{:S(2)}, u32[]{:S(2)}) collective-permute-start(bf16[16,512]{1,0:T(8,128)(2,1)S(1)} %slice.3), channel_id=1, source_target_pairs={{8,16},{12,20},{24,32},{28,36},{40,48},{44,52},{56,64},{60,68},{72... | collective-permute-start | bytes 49160 | tf_op jit(solution)/shard_map/token_swap/ppermute | solution.py:268
  19.3 1.7 %collective-permute-start.8 = (bf16[256,768]{1,0:T(8,128)(2,1)S(1)}, bf16[256,768]{1,0:T(8,128)(2,1)S(1)}, u32[]{:S(2)}, u32[]{:S(2)}) collective-permute-start(bf16[256,768]{1,0:T(8,128)(2,1)S(1)} %pad_maximum_fusion.refs_3_), channel_id=1, source_target_pairs={{0,48},{16,0},{32,16},{48,32},{1,49},{17,1},{33,17},{49,33},{2,50}... | collective-permute-start | bytes 1179656 | tf_op jit(solution)/shard_map/weight_rings/ppermute | solution.py:23
  21.0 1.8 %collective-permute-start.7 = (bf16[256,768]{1,0:T(8,128)(2,1)S(1)}, bf16[256,768]{1,0:T(8,128)(2,1)S(1)}, u32[]{:S(2)}, u32[]{:S(2)}) collective-permute-start(bf16[256,768]{1,0:T(8,128)(2,1)S(1)} %pad_maximum_fusion.refs_3_), channel_id=1, source_target_pairs={{0,16},{16,32},{32,48},{48,0},{1,17},{17,33},{33,49},{49,1},{2,18}... | collective-permute-start | bytes 1179656 | tf_op jit(solution)/shard_map/weight_rings/ppermute | solution.py:23
  22.8 0.0 collective-permute-done.2
  22.8 2.7 %collective-permute-start.6 = (bf16[256,768]{1,0:T(8,128)(2,1)S(1)}, bf16[256,768]{1,0:T(8,128)(2,1)S(1)}, u32[]{:S(2)}, u32[]{:S(2)}) collective-permute-start(bf16[256,768]{1,0:T(8,128)(2,1)S(1)} %pad_maximum_fusion.refs_3_), channel_id=1, source_target_pairs={{0,192},{64,0},{128,64},{192,128},{1,193},{65,1},{129,65},{193,129... | collective-permute-start | bytes 1179656 | tf_op jit(solution)/shard_map/weight_rings/ppermute | solution.py:23
  25.5 0.0 collective-permute-done.1
  25.5 0.0 collective-permute-start.5
  25.5 0.0 collective-permute-done.3
  25.5 1.6 %collective-permute-start.4 = (bf16[256,768]{1,0:T(8,128)(2,1)S(1)}, bf16[256,768]{1,0:T(8,128)(2,1)S(1)}, u32[]{:S(2)}, u32[]{:S(2)}) collective-permute-start(bf16[256,768]{1,0:T(8,128)(2,1)S(1)} %pad_maximum_fusion.refs_3_), channel_id=1, source_target_pairs={{0,128},{64,192},{128,0},{192,64},{1,129},{65,193},{129,1},{193,65... | collective-permute-start | bytes 1179656 | tf_op jit(solution)/shard_map/weight_rings/ppermute | solution.py:23
  27.2 11.2 %collective-permute-done.8.refs_1_ = bf16[256,768]{1,0:T(8,128)(2,1)S(1)} collective-permute-done((bf16[256,768]{1,0:T(8,128)(2,1)S(1)}, bf16[256,768]{1,0:T(8,128)(2,1)S(1)}, u32[]{:S(2)}, u32[]{:S(2)}) %collective-permute-start.8) | collective-permute-done | bytes 393248 | tf_op jit(solution)/shard_map/weight_rings/ppermute | solution.py:23
  38.4 0.9 collective-permute-done.7.refs_0_
  39.3 2.1 %collective-permute-done.6.refs_8_ = bf16[256,768]{1,0:T(8,128)(2,1)S(1)} collective-permute-done((bf16[256,768]{1,0:T(8,128)(2,1)S(1)}, bf16[256,768]{1,0:T(8,128)(2,1)S(1)}, u32[]{:S(2)}, u32[]{:S(2)}) %collective-permute-start.6) | collective-permute-done | bytes 393248 | tf_op jit(solution)/shard_map/weight_rings/ppermute | solution.py:23
  41.4 4.3 %collective-permute-done.5.refs_6_ = bf16[256,768]{1,0:T(8,128)(2,1)S(1)} collective-permute-done((bf16[256,768]{1,0:T(8,128)(2,1)S(1)}, bf16[256,768]{1,0:T(8,128)(2,1)S(1)}, u32[]{:S(2)}, u32[]{:S(2)}) %collective-permute-start.5) | collective-permute-done | bytes 393248 | tf_op jit(solution)/shard_map/weight_rings/ppermute | solution.py:23
  45.7 0.0 collective-permute-done.4.refs_10_
  45.7 0.8 pad_maximum_fusion.1
  46.5 0.1 copy-done.2
  46.6 0.0 all-gather.5.cloned.1.call-update
  46.6 0.9 relay_pair.1
  47.5 0.1 collective-permute-start.10
  47.6 1.5 %collective-permute-start.9 = (bf16[512,768]{1,0:T(8,128)(2,1)S(1)}, bf16[512,768]{1,0:T(8,128)(2,1)S(1)}, u32[]{:S(2)}, u32[]{:S(2)}) collective-permute-start(bf16[512,768]{1,0:T(8,128)(2,1)S(1)} %get-tuple-element.42.refs_4_), channel_id=1, source_target_pairs={{0,64},{64,128},{128,192},{192,0},{1,65},{65,129},{129,193},{193,1... | collective-permute-start | bytes 2359304 | tf_op jit(solution)/shard_map/weight_rings/ppermute | solution.py:23
  49.1 0.7 collective-permute-start.11
  49.8 2.9 %collective-permute-start.12 = (bf16[128,768]{1,0:T(8,128)(2,1)S(1)}, bf16[128,768]{1,0:T(8,128)(2,1)S(1)}, u32[]{:S(2)}, u32[]{:S(2)}) collective-permute-start(bf16[128,768]{1,0:T(8,128)(2,1)S(1)} %get-tuple-element.44), channel_id=1, source_target_pairs={{0,48},{16,0},{32,16},{48,32},{1,49},{17,1},{33,17},{49,33},{2,50}... | collective-permute-start | bytes 589832 | tf_op jit(solution)/shard_map/weight_rings/ppermute | solution.py:23
  52.7 6.2 %collective-permute-done.11.refs_2_ = bf16[128,768]{1,0:T(8,128)(2,1)S(1)} collective-permute-done((bf16[128,768]{1,0:T(8,128)(2,1)S(1)}, bf16[128,768]{1,0:T(8,128)(2,1)S(1)}, u32[]{:S(2)}, u32[]{:S(2)}) %collective-permute-start.11) | collective-permute-done | bytes 196640 | tf_op jit(solution)/shard_map/weight_rings/ppermute | solution.py:23
  58.8 3.8 %collective-permute-done.12.refs_3_ = bf16[128,768]{1,0:T(8,128)(2,1)S(1)} collective-permute-done((bf16[128,768]{1,0:T(8,128)(2,1)S(1)}, bf16[128,768]{1,0:T(8,128)(2,1)S(1)}, u32[]{:S(2)}, u32[]{:S(2)}) %collective-permute-start.12) | collective-permute-done | bytes 196640 | tf_op jit(solution)/shard_map/weight_rings/ppermute | solution.py:23
  62.6 3.9 %collective-permute-done.10.refs_1_.refs_9_ = bf16[512,768]{1,0:T(8,128)(2,1)S(1)} collective-permute-done((bf16[512,768]{1,0:T(8,128)(2,1)S(1)}, bf16[512,768]{1,0:T(8,128)(2,1)S(1)}, u32[]{:S(2)}, u32[]{:S(2)}) %collective-permute-start.10) | collective-permute-done | bytes 786464 | tf_op jit(solution)/shard_map/weight_rings/ppermute | solution.py:23
  66.5 1.2 collective-permute-done.9.refs_0_.refs_7_
  67.7 1.4 %relay_far.1 = (bf16[256,768]{1,0:T(8,128)(2,1)}, bf16[256,768]{1,0:T(8,128)(2,1)}, bf16[256,768]{1,0:T(8,128)(2,1)}, bf16[256,768]{1,0:T(8,128)(2,1)}, bf16[256,768]{1,0:T(8,128)(2,1)}) custom-call(bf16[512,768]{1,0:T(8,128)(2,1)S(1)} %collective-permute-done.9.refs_0_.refs_7_, bf16[512,768]{1,0:T(8,128)(2,1)S(1)} %collective-permute-done.10.refs_1_.refs_9_, ...), custom_call_target="tpu_custom_call" | custom-call | bytes 2000000 | tf_op jit(solution)/shard_map/weight_rings/relay_far/pallas_call | solution.py:54
  69.0 0.1 collective-permute-start.13
  69.1 2.7 %collective-permute-start.14 = (bf16[256,768]{1,0:T(8,128)(2,1)}, bf16[256,768]{1,0:T(8,128)(2,1)}, u32[]{:S(2)}, u32[]{:S(2)}) collective-permute-start(bf16[256,768]{1,0:T(8,128)(2,1)} %get-tuple-element.55), channel_id=1, source_target_pairs={{0,192},{64,0},{128,64},{192,128},{1,193},{65,1},{129,65},{193,129... | collective-permute-start | bytes 1179656 | tf_op jit(solution)/shard_map/weight_rings/ppermute | solution.py:23
  71.8 0.0 collective-permute-start.15
  71.8 3.6 %collective-permute-start.16 = (bf16[256,768]{1,0:T(8,128)(2,1)}, bf16[256,768]{1,0:T(8,128)(2,1)}, u32[]{:S(2)}, u32[]{:S(2)}) collective-permute-start(bf16[256,768]{1,0:T(8,128)(2,1)} %get-tuple-element.57), channel_id=1, source_target_pairs={{0,48},{16,0},{32,16},{48,32},{1,49},{17,1},{33,17},{49,33},{2,50}... | collective-permute-start | bytes 1179656 | tf_op jit(solution)/shard_map/weight_rings/ppermute | solution.py:23
  75.4 0.0 collective-permute-start.17
  75.4 0.1 stack.23.refs_0_.pos
  75.5 1.7 %copy-done = bf16[2304,512]{1,0:T(8,128)(2,1)S(1)} copy-done((bf16[2304,512]{1,0:T(8,128)(2,1)S(1)}, bf16[2304,512]{1,0:T(8,128)(2,1)}, u32[]{:S(2)}) %copy-start) | copy-done | bytes 2359320
  77.1 1.6 %copy-done.1 = bf16[2048,512]{1,0:T(8,128)(2,1)S(1)} copy-done((bf16[2048,512]{1,0:T(8,128)(2,1)S(1)}, bf16[2048,512]{1,0:T(8,128)(2,1)}, u32[]{:S(2)}) %copy-start.1) | copy-done | bytes 2097176
  78.7 1.0 copy-done.3
  79.7 6.1 %project.1 = (f32[6,528,128]{2,1,0:T(8,128)S(1)}, bf16[528,1280]{1,0:T(8,128)(2,1)S(1)}) custom-call(s32[5]{0:T(128)S(1)} %stack.23.refs_0_.pos, bf16[2048,512]{1,0:T(8,128)(2,1)S(1)} %copy-done.1, bf16[2304,512]{1,0:T(8,128)(2,1)S(1)} %copy-done, bf16[256,768]{1,0:T(8,128)(2,1)S(1)} %pad_maximum_fusion.refs_3_, ...), custom_call_target="tpu_custom_call" | custom-call | flops 2283798528 | bytes 9000000 | tf_op jit(solution)/shard_map/project/pallas_call | solution.py:319
  85.8 0.0 collective-permute-done.13.refs_2_
  85.8 0.0 collective-permute-done.14.refs_3_
  85.8 4.1 %collective-permute-done.15.refs_4_ = bf16[256,768]{1,0:T(8,128)(2,1)} collective-permute-done((bf16[256,768]{1,0:T(8,128)(2,1)}, bf16[256,768]{1,0:T(8,128)(2,1)}, u32[]{:S(2)}, u32[]{:S(2)}) %collective-permute-start.15) | collective-permute-done | bytes 393248 | tf_op jit(solution)/shard_map/weight_rings/ppermute | solution.py:23
  89.9 3.2 %collective-permute-done.16.refs_5_ = bf16[256,768]{1,0:T(8,128)(2,1)} collective-permute-done((bf16[256,768]{1,0:T(8,128)(2,1)}, bf16[256,768]{1,0:T(8,128)(2,1)}, u32[]{:S(2)}, u32[]{:S(2)}) %collective-permute-start.16) | collective-permute-done | bytes 393248 | tf_op jit(solution)/shard_map/weight_rings/ppermute | solution.py:23
  93.1 0.0 collective-permute-done.17.refs_6_
  93.1 0.0 copy-done.4
  93.1 0.0 copy-start.5
  93.1 0.0 copy-start.6
  93.1 0.0 copy-start.8
  93.2 5.9 %states.1 = (f32[64,8,256]{2,1,0:T(8,128)S(1)}, f32[64,8,256]{2,1,0:T(8,128)S(1)}, f32[16,8,256]{2,1,0:T(8,128)S(1)}, f32[16,16,256]{2,1,0:T(8,128)}) custom-call(s32[5]{0:T(128)S(1)} %stack.23.refs_0_.pos, bf16[528,1280]{1,0:T(8,128)(2,1)S(1)} %get-tuple-element.53.refs_1_, bf16[256,768]{1,0:T(8,128)(2,1)} %collective-permute-done.13.refs_2_, ...), custom_call_target="tpu_custom_call" | custom-call | tf_op jit(solution)/shard_map/states/pallas_call | solution.py:341
  99.0 3.5 %all-to-all-start = ((f32[16,16,256]{2,1,0:T(8,128)}), f32[16,16,256]{2,1,0:T(8,128)S(1)}, u32[]{:S(2)}, u32[]{:S(2)}) async-start(f32[16,16,256]{2,1,0:T(8,128)} %get-tuple-element.62), calls=%async_computation | async-start | bytes 524288 | tf_op jit(solution)/shard_map/state_exchange/all_to_all | solution.py:357
  102.6 0.0 copy-done.5
  102.6 1.9 %local.1 = f32[64,8,256]{2,1,0:T(8,128)S(1)} custom-call(s32[5]{0:T(128)S(1)} %stack.23.refs_0_.pos, f32[64,8,256]{2,1,0:T(8,128)S(1)} %get-tuple-element.60.product, f32[16,512]{1,0:T(8,128)S(1)} %copy-done.6, f32[16,512]{1,0:T(8,128)S(1)} %copy-done.5, f32[1,512]{1,0:T(1,128)S(1)} %bitcast.14), custom_call_target="tpu_custom_call" | custom-call | flops 20000000 | bytes 1000000 | tf_op jit(solution)/shard_map/local/pallas_call | solution.py:358
  104.5 10.0 %all-to-all-done.states = f32[16,16,256]{2,1,0:T(8,128)S(1)} async-done(((f32[16,16,256]{2,1,0:T(8,128)}), f32[16,16,256]{2,1,0:T(8,128)S(1)}, u32[]{:S(2)}, u32[]{:S(2)}) %all-to-all-start) | async-done | bytes 262176 | tf_op jit(solution)/shard_map/state_exchange/all_to_all | solution.py:357
  114.5 1.5 %finish.1 = (bf16[256,256]{1,0:T(8,128)(2,1)S(1)}, bf16[256,256]{1,0:T(8,128)(2,1)S(1)}) custom-call(s32[5]{0:T(128)S(1)} %stack.23.refs_0_.pos, f32[64,8,256]{2,1,0:T(8,128)S(1)} %get-tuple-element.59.gate, f32[64,8,256]{2,1,0:T(8,128)S(1)} %local.1, f32[16,8,256]{2,1,0:T(8,128)S(1)} %get-tuple-element.61.inside, f32[16,16,256]{2,1,0:T(8,128)S(1)} %all-to-all-done.states, ...), custom_call_target="tpu_custom_call" | custom-call | tf_op jit(solution)/shard_map/finish/pallas_call | solution.py:367
  116.1 2.4 %collective-permute-start.18 = (bf16[256,256]{1,0:T(8,128)(2,1)S(1)}, bf16[256,256]{1,0:T(8,128)(2,1)S(1)}, u32[]{:S(2)}, u32[]{:S(2)}) collective-permute-start(bf16[256,256]{1,0:T(8,128)(2,1)S(1)} %get-tuple-element.64), channel_id=1, source_target_pairs={{0,8},{8,0},{1,9},{9,1},{2,10},{10,2},{3,11},{11,3},{4,12},{12,4},... | collective-permute-start | bytes 393224 | tf_op jit(solution)/shard_map/result_swap/ppermute | solution.py:377
  118.4 1.0 collective-permute-done.18
  119.5 0.7 pad_maximum_fusion.2
  (20 shorter events, 0.2 us)
Async XLA Ops:
  6.5 5.6 %copy-start.9 = (bf16[256,512]{1,0:T(8,128)(2,1)S(1)}, bf16[256,512]{1,0:T(8,128)(2,1)}, u32[]{:S(2)}) copy-start(bf16[256,512]{1,0:T(8,128)(2,1)} %param.6) | copy-start | bytes 786436
  6.5 68.9 %all-gather.3.cloned.1.call-start = ((), (), s32[]{:S(2)}) async-start(), calls=%async_computation.1 | async-start | bytes 2359296 | tf_op jit(solution)/shard_map/token_gather/all_gather | solution.py:277
  7.3 68.2 %all-gather.5.cloned.1.call-start = ((), (), s32[]{:S(2)}) async-start(), calls=%async_computation.2 | async-start | bytes 2654208 | tf_op jit(solution)/shard_map/token_gather/all_gather | solution.py:279
  8.8 4.4 %collective-permute-start = (bf16[128,768]{1,0:T(8,128)(2,1)S(1)}, bf16[128,768]{1,0:T(8,128)(2,1)S(1)}, u32[]{:S(2)}, u32[]{:S(2)}) collective-permute-start(bf16[128,768]{1,0:T(8,128)(2,1)S(1)} %bitcast.17), channel_id=1, source_target_pairs={{0,8},{8,0},{1,9},{9,1},{2,10},{10,2},{3,11},{11,3},{4,12},{12,4},... | collective-permute-start | bytes 589832 | tf_op jit(solution)/shard_map/weight_gather/ppermute | solution.py:262
  12.1 13.4 %collective-permute-start.3 = (bf16[256,512]{1,0:T(8,128)(2,1)S(1)}, bf16[256,512]{1,0:T(8,128)(2,1)S(1)}, u32[]{:S(2)}, u32[]{:S(2)}) collective-permute-start(bf16[256,512]{1,0:T(8,128)(2,1)S(1)} %copy-done.9), channel_id=1, source_target_pairs={{0,4},{4,0},{1,5},{5,1},{2,6},{6,2},{3,7},{7,3},{8,12},{12,8},{9,1... | collective-permute-start | bytes 786440 | tf_op jit(solution)/shard_map/token_swap/ppermute | solution.py:266
  13.2 9.6 %collective-permute-start.2 = (bf16[16,512]{1,0:T(8,128)(2,1)S(1)}, bf16[16,512]{1,0:T(8,128)(2,1)S(1)}, u32[]{:S(2)}, u32[]{:S(2)}) collective-permute-start(bf16[16,512]{1,0:T(8,128)(2,1)S(1)} %slice.3), channel_id=1, source_target_pairs={{8,20},{12,16},{24,36},{28,32},{40,52},{44,48},{56,68},{60,64},{72... | collective-permute-start | bytes 49160 | tf_op jit(solution)/shard_map/token_swap/ppermute | solution.py:269
  18.0 7.5 %collective-permute-start.1 = (bf16[16,512]{1,0:T(8,128)(2,1)S(1)}, bf16[16,512]{1,0:T(8,128)(2,1)S(1)}, u32[]{:S(2)}, u32[]{:S(2)}) collective-permute-start(bf16[16,512]{1,0:T(8,128)(2,1)S(1)} %slice.3), channel_id=1, source_target_pairs={{8,16},{12,20},{24,32},{28,36},{40,48},{44,52},{56,64},{60,68},{72... | collective-permute-start | bytes 49160 | tf_op jit(solution)/shard_map/token_swap/ppermute | solution.py:268
  19.3 19.1 %collective-permute-start.8 = (bf16[256,768]{1,0:T(8,128)(2,1)S(1)}, bf16[256,768]{1,0:T(8,128)(2,1)S(1)}, u32[]{:S(2)}, u32[]{:S(2)}) collective-permute-start(bf16[256,768]{1,0:T(8,128)(2,1)S(1)} %pad_maximum_fusion.refs_3_), channel_id=1, source_target_pairs={{0,48},{16,0},{32,16},{48,32},{1,49},{17,1},{33,17},{49,33},{2,50}... | collective-permute-start | bytes 1179656 | tf_op jit(solution)/shard_map/weight_rings/ppermute | solution.py:23
  21.0 18.3 %collective-permute-start.7 = (bf16[256,768]{1,0:T(8,128)(2,1)S(1)}, bf16[256,768]{1,0:T(8,128)(2,1)S(1)}, u32[]{:S(2)}, u32[]{:S(2)}) collective-permute-start(bf16[256,768]{1,0:T(8,128)(2,1)S(1)} %pad_maximum_fusion.refs_3_), channel_id=1, source_target_pairs={{0,16},{16,32},{32,48},{48,0},{1,17},{17,33},{33,49},{49,1},{2,18}... | collective-permute-start | bytes 1179656 | tf_op jit(solution)/shard_map/weight_rings/ppermute | solution.py:23
  22.8 18.6 %collective-permute-start.6 = (bf16[256,768]{1,0:T(8,128)(2,1)S(1)}, bf16[256,768]{1,0:T(8,128)(2,1)S(1)}, u32[]{:S(2)}, u32[]{:S(2)}) collective-permute-start(bf16[256,768]{1,0:T(8,128)(2,1)S(1)} %pad_maximum_fusion.refs_3_), channel_id=1, source_target_pairs={{0,192},{64,0},{128,64},{192,128},{1,193},{65,1},{129,65},{193,129... | collective-permute-start | bytes 1179656 | tf_op jit(solution)/shard_map/weight_rings/ppermute | solution.py:23
  25.5 20.2 %collective-permute-start.5 = (bf16[256,768]{1,0:T(8,128)(2,1)S(1)}, bf16[256,768]{1,0:T(8,128)(2,1)S(1)}, u32[]{:S(2)}, u32[]{:S(2)}) collective-permute-start(bf16[256,768]{1,0:T(8,128)(2,1)S(1)} %pad_maximum_fusion.refs_3_), channel_id=1, source_target_pairs={{0,64},{64,128},{128,192},{192,0},{1,65},{65,129},{129,193},{193,1... | collective-permute-start | bytes 1179656 | tf_op jit(solution)/shard_map/weight_rings/ppermute | solution.py:23
  25.5 20.2 %collective-permute-start.4 = (bf16[256,768]{1,0:T(8,128)(2,1)S(1)}, bf16[256,768]{1,0:T(8,128)(2,1)S(1)}, u32[]{:S(2)}, u32[]{:S(2)}) collective-permute-start(bf16[256,768]{1,0:T(8,128)(2,1)S(1)} %pad_maximum_fusion.refs_3_), channel_id=1, source_target_pairs={{0,128},{64,192},{128,0},{192,64},{1,129},{65,193},{129,1},{193,65... | collective-permute-start | bytes 1179656 | tf_op jit(solution)/shard_map/weight_rings/ppermute | solution.py:23
  45.7 0.9 copy-start.2
  47.5 18.9 %collective-permute-start.10 = (bf16[512,768]{1,0:T(8,128)(2,1)S(1)}, bf16[512,768]{1,0:T(8,128)(2,1)S(1)}, u32[]{:S(2)}, u32[]{:S(2)}) collective-permute-start(bf16[512,768]{1,0:T(8,128)(2,1)S(1)} %get-tuple-element.42.refs_4_), channel_id=1, source_target_pairs={{0,192},{64,0},{128,64},{192,128},{1,193},{65,1},{129,65},{193,129... | collective-permute-start | bytes 2359304 | tf_op jit(solution)/shard_map/weight_rings/ppermute | solution.py:23
  47.6 20.0 %collective-permute-start.9 = (bf16[512,768]{1,0:T(8,128)(2,1)S(1)}, bf16[512,768]{1,0:T(8,128)(2,1)S(1)}, u32[]{:S(2)}, u32[]{:S(2)}) collective-permute-start(bf16[512,768]{1,0:T(8,128)(2,1)S(1)} %get-tuple-element.42.refs_4_), channel_id=1, source_target_pairs={{0,64},{64,128},{128,192},{192,0},{1,65},{65,129},{129,193},{193,1... | collective-permute-start | bytes 2359304 | tf_op jit(solution)/shard_map/weight_rings/ppermute | solution.py:23
  49.1 9.7 %collective-permute-start.11 = (bf16[128,768]{1,0:T(8,128)(2,1)S(1)}, bf16[128,768]{1,0:T(8,128)(2,1)S(1)}, u32[]{:S(2)}, u32[]{:S(2)}) collective-permute-start(bf16[128,768]{1,0:T(8,128)(2,1)S(1)} %get-tuple-element.43), channel_id=1, source_target_pairs={{0,16},{16,32},{32,48},{48,0},{1,17},{17,33},{33,49},{49,1},{2,18}... | collective-permute-start | bytes 589832 | tf_op jit(solution)/shard_map/weight_rings/ppermute | solution.py:23
  49.8 12.8 %collective-permute-start.12 = (bf16[128,768]{1,0:T(8,128)(2,1)S(1)}, bf16[128,768]{1,0:T(8,128)(2,1)S(1)}, u32[]{:S(2)}, u32[]{:S(2)}) collective-permute-start(bf16[128,768]{1,0:T(8,128)(2,1)S(1)} %get-tuple-element.44), channel_id=1, source_target_pairs={{0,48},{16,0},{32,16},{48,32},{1,49},{17,1},{33,17},{49,33},{2,50}... | collective-permute-start | bytes 589832 | tf_op jit(solution)/shard_map/weight_rings/ppermute | solution.py:23
  69.0 16.8 %collective-permute-start.13 = (bf16[256,768]{1,0:T(8,128)(2,1)}, bf16[256,768]{1,0:T(8,128)(2,1)}, u32[]{:S(2)}, u32[]{:S(2)}) collective-permute-start(bf16[256,768]{1,0:T(8,128)(2,1)} %get-tuple-element.54), channel_id=1, source_target_pairs={{0,64},{64,128},{128,192},{192,0},{1,65},{65,129},{129,193},{193,1... | collective-permute-start | bytes 1179656 | tf_op jit(solution)/shard_map/weight_rings/ppermute | solution.py:23
  69.1 16.7 %collective-permute-start.14 = (bf16[256,768]{1,0:T(8,128)(2,1)}, bf16[256,768]{1,0:T(8,128)(2,1)}, u32[]{:S(2)}, u32[]{:S(2)}) collective-permute-start(bf16[256,768]{1,0:T(8,128)(2,1)} %get-tuple-element.55), channel_id=1, source_target_pairs={{0,192},{64,0},{128,64},{192,128},{1,193},{65,1},{129,65},{193,129... | collective-permute-start | bytes 1179656 | tf_op jit(solution)/shard_map/weight_rings/ppermute | solution.py:23
  71.8 18.1 %collective-permute-start.15 = (bf16[256,768]{1,0:T(8,128)(2,1)}, bf16[256,768]{1,0:T(8,128)(2,1)}, u32[]{:S(2)}, u32[]{:S(2)}) collective-permute-start(bf16[256,768]{1,0:T(8,128)(2,1)} %get-tuple-element.56), channel_id=1, source_target_pairs={{0,16},{16,32},{32,48},{48,0},{1,17},{17,33},{33,49},{49,1},{2,18}... | collective-permute-start | bytes 1179656 | tf_op jit(solution)/shard_map/weight_rings/ppermute | solution.py:23
  71.8 21.3 %collective-permute-start.16 = (bf16[256,768]{1,0:T(8,128)(2,1)}, bf16[256,768]{1,0:T(8,128)(2,1)}, u32[]{:S(2)}, u32[]{:S(2)}) collective-permute-start(bf16[256,768]{1,0:T(8,128)(2,1)} %get-tuple-element.57), channel_id=1, source_target_pairs={{0,48},{16,0},{32,16},{48,32},{1,49},{17,1},{33,17},{49,33},{2,50}... | collective-permute-start | bytes 1179656 | tf_op jit(solution)/shard_map/weight_rings/ppermute | solution.py:23
  75.4 17.7 %collective-permute-start.17 = (bf16[256,768]{1,0:T(8,128)(2,1)}, bf16[256,768]{1,0:T(8,128)(2,1)}, u32[]{:S(2)}, u32[]{:S(2)}) collective-permute-start(bf16[256,768]{1,0:T(8,128)(2,1)} %get-tuple-element.49.refs_5_), channel_id=1, source_target_pairs={{0,128},{64,192},{128,0},{192,64},{1,129},{65,193},{129,1},{193,65... | collective-permute-start | bytes 1179656 | tf_op jit(solution)/shard_map/weight_rings/ppermute | solution.py:23
  75.5 1.7 %copy-start = (bf16[2304,512]{1,0:T(8,128)(2,1)S(1)}, bf16[2304,512]{1,0:T(8,128)(2,1)}, u32[]{:S(2)}) copy-start(bf16[2304,512]{1,0:T(8,128)(2,1)} %all-gather.5.cloned.1.call-done.refs_2_) | copy-start | bytes 7077892
  77.1 1.6 %copy-start.1 = (bf16[2048,512]{1,0:T(8,128)(2,1)S(1)}, bf16[2048,512]{1,0:T(8,128)(2,1)}, u32[]{:S(2)}) copy-start(bf16[2048,512]{1,0:T(8,128)(2,1)} %all-gather.3.cloned.1.call-done.refs_1_) | copy-start | bytes 6291460
  78.7 1.0 copy-start.3
  79.7 13.4 %copy-start.4 = (f32[16,512]{1,0:T(8,128)S(1)}, f32[16,512]{1,0:T(8,128)}, u32[]{:S(2)}) copy-start(f32[16,512]{1,0:T(8,128)} %decay.3) | copy-start | bytes 98308
  79.7 13.4 %copy-start.7 = (f32[3,3,512]{2,1,0:T(4,128)S(1)}, f32[3,3,512]{2,1,0:T(4,128)}, u32[]{:S(2)}) copy-start(f32[3,3,512]{2,1,0:T(4,128)} %refs_8_.1) | copy-start | bytes 55300
  93.1 9.5 %copy-start.5 = (f32[16,512]{1,0:T(8,128)S(1)}, f32[16,512]{1,0:T(8,128)}, u32[]{:S(2)}) copy-start(f32[16,512]{1,0:T(8,128)} %decay.3) | copy-start | bytes 98308
  93.1 9.5 %copy-start.6 = (f32[16,512]{1,0:T(8,128)S(1)}, f32[16,512]{1,0:T(8,128)}, u32[]{:S(2)}) copy-start(f32[16,512]{1,0:T(8,128)} %gain.3) | copy-start | bytes 98308
  93.1 9.5 %copy-start.8 = (f32[512]{0:T(512)S(1)}, f32[512]{0:T(512)}, u32[]{:S(2)}) copy-start(f32[512]{0:T(512)} %param.11) | copy-start | bytes 6148
  99.0 15.5 %all-to-all-start = ((f32[16,16,256]{2,1,0:T(8,128)}), f32[16,16,256]{2,1,0:T(8,128)S(1)}, u32[]{:S(2)}, u32[]{:S(2)}) async-start(f32[16,16,256]{2,1,0:T(8,128)} %get-tuple-element.62), calls=%async_computation | async-start | bytes 524288 | tf_op jit(solution)/shard_map/state_exchange/all_to_all | solution.py:357
  116.1 3.4 %collective-permute-start.18 = (bf16[256,256]{1,0:T(8,128)(2,1)S(1)}, bf16[256,256]{1,0:T(8,128)(2,1)S(1)}, u32[]{:S(2)}, u32[]{:S(2)}) collective-permute-start(bf16[256,256]{1,0:T(8,128)(2,1)S(1)} %get-tuple-element.64), channel_id=1, source_target_pairs={{0,8},{8,0},{1,9},{9,1},{2,10},{10,2},{3,11},{11,3},{4,12},{12,4},... | collective-permute-start | bytes 393224 | tf_op jit(solution)/shard_map/result_swap/ppermute | solution.py:377
Sparse Core Ops, SparseCore 0:
  9.2 31.8 all-gather.2
  46.7 25.4 all-gather.4

commit v10 on v9

--- a/solution.py
+++ b/solution.py
@@ -121,80 +121,98 @@
         copy.wait()
 
 
-def state_kernel(sizes, *refs):
-    rows, depth, width, modes, seq = sizes
-    pos, late_tok, *pieces = refs[:-9]
-    sums, taps, decay, gate, product, inside, states_out, acc, state = refs[-9:]
-    c = pos[3]
+def late_products(sizes, signals, late_tok, pieces, sums, acc):
+    rows, depth, width, modes, seq = sizes
     k = depth // 16
-
-    @pl.loop(0, 3)
+    first, last = signals
+    halves = width // 128
+
+    @pl.loop(first, last)
     def _(j):
         cols = pl.ds(pl.multiple_of(j * width, width), width)
         part = sum(
             jnp.dot(late_tok[:, i * k : i * k + k], piece[:, cols], preferred_element_type=F32)
             for i, piece in enumerate(pieces)
         )
-        for lh in range(width // 128):
-            chunk = j * (width // 128) + lh
+        for lh in range(halves):
             new = part[:, lh * 128 : lh * 128 + 128]
-            acc[chunk] = (sums[chunk] + new).astype(BF16).astype(F32)
-
+            acc[(j - first) * halves + lh] = (sums[j * halves + lh] + new).astype(BF16).astype(F32)
+
+
+def filtered(sizes, signals, lh, acc, taps, mine):
+    rows, depth, width, modes, seq = sizes
+    steps = 2 * rows // SUB
+    halves = width // 128
+    count = signals[1] - signals[0]
+    weights = [[taps[lag, j : j + 1, mine] for j in range(*signals)] for lag in range(3)]
+
+    def read(start):
+        return [acc[j * halves + lh, pl.ds(start, SUB, stride=steps), :] for j in range(count)]
+
+    def features(now, last, before):
+        return [
+            weights[0][j] * now[j] + weights[1][j] * last[j] + weights[2][j] * before[j]
+            for j in range(count)
+        ]
+
+    return read, features
+
+
+def state_kernel(sizes, *refs):
+    rows, depth, width, modes, seq = sizes
+    pos, late_tok, *pieces = refs[:-8]
+    sums, taps, decay, product, gated, states_out, acc, state = refs[-8:]
+    c = pos[3]
+    late_products(sizes, (0, 1), late_tok, pieces, sums, gated)
+    late_products(sizes, (1, 3), late_tok, pieces, sums, acc)
     steps = 2 * rows // SUB
     for lh in range(width // 128):
         mine = pl.ds(pl.multiple_of(c * width + lh * 128, 128), 128)
         lanes = pl.ds(lh * 128, 128)
-        weights = [[taps[lag, j : j + 1, mine] for j in range(3)] for lag in range(3)]
+        read, features = filtered(sizes, (1, 3), lh, acc, taps, mine)
         rates = [jnp.broadcast_to(decay[m : m + 1, mine] / seq, (SUB, 128)) for m in range(modes)]
         factors = [jnp.exp(-rate) for rate in rates]
-
-        def read(start):
-            return [
-                acc[j * (width // 128) + lh, pl.ds(start, SUB, stride=steps), :]
-                for j in range(3)
-            ]
 
         def step(t, carry):
             before, last, states = carry
             now = read(HALO + t)
-            f = [
-                weights[0][j] * now[j] + weights[1][j] * last[j] + weights[2][j] * before[j]
-                for j in range(3)
-            ]
-            p = f[1] * f[2]
-            gate[t, :, lanes] = f[0]
+            f = features(now, last, before)
+            p = f[0] * f[1]
             product[t, :, lanes] = p
             return last, now, [a * s + p for a, s in zip(factors, states)]
 
         zero = jnp.zeros((SUB, 128), F32)
         carry = (read(HALO - 2), read(HALO - 1), [zero] * modes)
-        states = lax.fori_loop(0, steps, step, carry, unroll=4)[2]
-        line = lax.broadcasted_iota(jnp.int32, (SUB, 128), 0)
-
-        def later(value, by):
-            return jnp.where(line >= by, pltpu.roll(value, by, 0), 0.0)
-
+        states = lax.fori_loop(0, steps, step, carry, unroll=8)[2]
+        line = lax.broadcasted_iota(jnp.int32, (SUB, 128), 0).astype(F32)
+        left = (SUB - 1.0 - line) * float(steps)
         for m in range(modes):
-            s = states[m]
-            for by in (1, 2, 4):
-                s = s + jnp.exp(-float(steps * by) * rates[m]) * later(s, by)
-            inside[m, :, lanes] = later(s, 1)
-            state[m : m + 1, lanes] = s[SUB - 1 :]
+            total = jnp.sum(jnp.exp(-rates[m] * left) * states[m], axis=0, keepdims=True)
+            state[m : m + 1, lanes] = total
     for r in range(16):
         states_out[r] = state[...]
 
 
-def local_kernel(sizes, pos, product, gain, decay, skip, local):
+def local_kernel(sizes, pos, gated, taps, product, gain, decay, skip, gate, local, inside):
     rows, depth, width, modes, seq = sizes
     c = pos[3]
     steps = 2 * rows // SUB
     for lh in range(width // 128):
         mine = pl.ds(pl.multiple_of(c * width + lh * 128, 128), 128)
         lanes = pl.ds(lh * 128, 128)
+        read, features = filtered(sizes, (0, 1), lh, gated, taps, mine)
         rates = [jnp.broadcast_to(decay[m : m + 1, mine] / seq, (SUB, 128)) for m in range(modes)]
         factors = [jnp.exp(-rate) for rate in rates]
         heights = [gain[m : m + 1, mine] * jnp.sqrt(2.0 * rates[m]) for m in range(modes)]
         direct = jnp.broadcast_to(skip[:, mine], (SUB, 128))
+
+        def gates(t, carry):
+            before, last = carry
+            now = read(HALO + t)
+            gate[t, :, lanes] = features(now, last, before)[0]
+            return last, now
+
+        lax.fori_loop(0, steps, gates, (read(HALO - 2), read(HALO - 1)), unroll=8)
 
         def step(t, states):
             p = product[t, :, lanes]
@@ -205,7 +223,17 @@
             local[t, :, lanes] = parts[0] + direct * p
             return states
 
-        lax.fori_loop(0, steps, step, [jnp.zeros((SUB, 128), F32)] * modes, unroll=4)
+        states = lax.fori_loop(0, steps, step, [jnp.zeros((SUB, 128), F32)] * modes, unroll=4)
+        line = lax.broadcasted_iota(jnp.int32, (SUB, 128), 0)
+
+        def later(value, by):
+            return jnp.where(line >= by, pltpu.roll(value, by, 0), 0.0)
+
+        for m in range(modes):
+            s = states[m]
+            for by in (1, 2, 4):
+                s = s + jnp.exp(-float(steps * by) * rates[m]) * later(s, by)
+            inside[m, :, lanes] = later(s, 1)
 
 
 def finish_kernel(sizes, pos, gate, local, inside, states, gain, decay, mine_out, their_out, start, whole):
@@ -271,8 +299,8 @@
         farther = shifted(own, "y", 2)
         far = both_ways(own, "y")
         beside = both_ways(own, "h")
-    first = (halo, other_halo, other, farther, far, beside)
-    halo, other_halo, other, farther, far, beside = tie(first)
+    first = (halo, other_halo, other, farther, beside, far)
+    halo, other_halo, other, farther, beside, far = tie(first)
     with jax.named_scope("token_gather"):
         near = lax.all_gather(tokens, ("c", "x"), axis=0, tiled=True)
         wide = jnp.concatenate([halo, other_halo, other], 0)
@@ -300,10 +328,9 @@
         early_runs += [(dy, dh, 0, two) for dh in (0, 1, -1)]
     early += [farther]
     early_runs += [(2, 0, 0, two)]
-    late = [*farther_pair, *far_opposite, last]
-    late_runs = [(2, 1, 0, two), (2, -1, 0, two)]
-    late_runs += [(dy, 2, skip, half) for skip in (0, half) for dy in (1, -1)]
-    late_runs += [(2, 2, 0, two)]
+    late = [*far_opposite, *farther_pair, last]
+    late_runs = [(dy, 2, skip, half) for skip in (0, half) for dy in (1, -1)]
+    late_runs += [(2, 1, 0, two), (2, -1, 0, two), (2, 2, 0, two)]
 
     vmem = pl.BlockSpec(memory_space=pltpu.VMEM)
     smem = pl.BlockSpec(memory_space=pltpu.SMEM)
@@ -338,32 +365,36 @@
         name="project",
     )(pos, near, swapped, *early)
     params = pltpu.CompilerParams(vmem_limit_bytes=8 * 2**20)
-    gate, product, inside, state = pl.pallas_call(
+    product, gated, state = pl.pallas_call(
         functools.partial(state_kernel, sizes),
         out_shape=(
             full,
-            full,
-            jax.ShapeDtypeStruct((modes, SUB, width), F32),
+            jax.ShapeDtypeStruct((width // 128, lines, 128), F32),
             jax.ShapeDtypeStruct((16, modes, width), F32),
         ),
         in_specs=[smem] + [vmem] * (4 + len(late)),
-        out_specs=(vmem,) * 4,
-        scratch_shapes=[pltpu.VMEM(chunks, F32), pltpu.VMEM((modes, width), F32)],
+        out_specs=(vmem,) * 3,
+        scratch_shapes=[
+            pltpu.VMEM((2 * width // 128, lines, 128), F32),
+            pltpu.VMEM((modes, width), F32),
+        ],
         compiler_params=params,
         name="states",
     )(pos, late_tok, *late, sums, taps, decay)
 
     with jax.named_scope("state_exchange"):
         states = lax.all_to_all(state, ("y", "h"), 0, 0, tiled=True)
-    local = pl.pallas_call(
+    gate, local, inside = pl.pallas_call(
         functools.partial(local_kernel, sizes),
-        out_shape=full,
-        in_specs=[smem] + [vmem] * 4,
-        out_specs=vmem,
+        out_shape=(full, full, jax.ShapeDtypeStruct((modes, SUB, width), F32)),
+        in_specs=[smem] + [vmem] * 6,
+        out_specs=(vmem,) * 3,
         compiler_params=params,
-        cost_estimate=pl.CostEstimate(flops=20_000_000, bytes_accessed=1_000_000, transcendentals=0),
+        cost_estimate=pl.CostEstimate(
+            flops=30_000_000, bytes_accessed=2_000_000, transcendentals=0
+        ),
         name="local",
-    )(pos, product, modes_gain, decay, skip.reshape(1, group))
+    )(pos, gated, taps, product, modes_gain, decay, skip.reshape(1, group))
     mine, theirs = pl.pallas_call(
         functools.partial(finish_kernel, sizes),
         out_shape=(jax.ShapeDtypeStruct((rows, width), BF16),) * 2,

time: 127 us -> 131 us (1.031)
  starting transfers between devices: 34.6 us -> 48.2 us
  waiting for transfers between devices: 53.5 us -> 44 us
    ppermute x14, waiting for transfers between devices: 40.8 us -> 32.5 us  [shifted(): return lax.ppermute(array, axis, [(i, (i + step) % n) for i in range(n)])]
    ppermute x14, starting transfers between devices: 19.3 us -> 25.3 us  [shifted(): return lax.ppermute(array, axis, [(i, (i + step) % n) for i in range(n)])]
    all_to_all x1, starting transfers between devices: 3.53 us -> 7.63 us  [body(): states = lax.all_to_all(state, ('y', 'h'), 0, 0, tiled=True)]
    ppermute x1, starting transfers between devices: 2.39 us -> 5.9 us  [body(): return in_order(c == 0, mine, lax.ppermute(theirs, 'c', SWAP), 1)]
    all_to_all x1, waiting for transfers between devices: 10 us -> 8.68 us  [body(): states = lax.all_to_all(state, ('y', 'h'), 0, 0, tiled=True)]
    unnamed x21 -> x23, local copies, waits for them, and re-layouts: 5.57 us -> 5.59 us
  transfers between devices with their start and end apart: 22 -> 22, of which waited for: 13 -> 12; matrix products, arithmetic and copies ran while one was open for 2% -> 2% of each run, Pallas kernels for 8% -> 8%
where the time goes in v10:
time: 131 us
  starting transfers between devices  48.2 us (37%)
  waiting for transfers between devices  44 us (34%)
  Pallas kernels  17.5 us (13%)
  between operations  13.6 us (10%)
  local copies, waits for them, and re-layouts  6.03 us (5%)
  other arithmetic  1.59 us (1%)
    ppermute x14, waiting for transfers between devices, shifted(): return lax.ppermute(array, axis, [(i, (i + step) % n) for i in range(n)])  32.5 us
    ppermute x14, starting transfers between devices, shifted(): return lax.ppermute(array, axis, [(i, (i + step) % n) for i in range(n)])  25.3 us
    all_to_all x1, waiting for transfers between devices, body(): states = lax.all_to_all(state, ('y', 'h'), 0, 0, tiled=True)  8.68 us
    all_to_all x1, starting transfers between devices, body(): states = lax.all_to_all(state, ('y', 'h'), 0, 0, tiled=True)  7.63 us
    pallas_call x1, Pallas kernels, body(): pl.pallas_call(functools.partial(project_kernel, sizes, early_runs, late_...  6.05 us
    ppermute x1, starting transfers between devices, body(): return in_order(c == 0, mine, lax.ppermute(theirs, 'c', SWAP), 1)  5.9 us
    unnamed x23, local copies, waits for them, and re-layouts  5.59 us
    pallas_call x1, Pallas kernels, body(): pl.pallas_call(functools.partial(state_kernel, sizes), out_shape=(full, j...  5.14 us
  transfers between devices with their start and end apart: 22, of which 12 were waited for; matrix products, arithmetic and copies ran while one was open for 2% of the time, Pallas kernels for 8%

profile of v10, /device:TPU:1, one launch (start us, length us, event | category | flops | bytes accessed | tf_op | source)
XLA Modules:
  0.0 130.9 jit_solution(11257735973002969373)
XLA Ops:
  6.5 0.7 all-gather.3.cloned.1.call-update
  7.3 0.0 all-gather.5.cloned.1.call-start
  7.3 1.2 copy.10
  8.6 0.1 copy.13
  8.8 3.3 %collective-permute-start = (bf16[128,768]{1,0:T(8,128)(2,1)S(1)}, bf16[128,768]{1,0:T(8,128)(2,1)S(1)}, u32[]{:S(2)}, u32[]{:S(2)}) collective-permute-start(bf16[128,768]{1,0:T(8,128)(2,1)S(1)} %bitcast.17), channel_id=1, source_target_pairs={{0,8},{8,0},{1,9},{9,1},{2,10},{10,2},{3,11},{11,3},{4,12},{12,4},... | collective-permute-start | bytes 589832 | tf_op jit(solution)/shard_map/weight_gather/ppermute | solution.py:290
  12.1 0.0 collective-permute-start.3
  12.1 0.1 copy.12
  12.2 0.9 collective-permute-done
  13.2 4.8 %collective-permute-start.2 = (bf16[16,512]{1,0:T(8,128)(2,1)S(1)}, bf16[16,512]{1,0:T(8,128)(2,1)S(1)}, u32[]{:S(2)}, u32[]{:S(2)}) collective-permute-start(bf16[16,512]{1,0:T(8,128)(2,1)S(1)} %slice.3), channel_id=1, source_target_pairs={{8,20},{12,16},{24,36},{28,32},{40,52},{44,48},{56,68},{60,64},{72... | collective-permute-start | bytes 49160 | tf_op jit(solution)/shard_map/token_swap/ppermute | solution.py:297
  18.0 1.3 collective-permute-start.1
  19.3 2.8 %collective-permute-start.8 = (bf16[256,768]{1,0:T(8,128)(2,1)S(1)}, bf16[256,768]{1,0:T(8,128)(2,1)S(1)}, u32[]{:S(2)}, u32[]{:S(2)}) collective-permute-start(bf16[256,768]{1,0:T(8,128)(2,1)S(1)} %pad_maximum_fusion.refs_3_), channel_id=1, source_target_pairs={{0,192},{64,0},{128,64},{192,128},{1,193},{65,1},{129,65},{193,129... | collective-permute-start | bytes 1179656 | tf_op jit(solution)/shard_map/weight_rings/ppermute | solution.py:23
  22.1 0.0 collective-permute-start.7
  22.1 0.0 collective-permute-done.2
  22.1 1.0 collective-permute-start.6
  23.1 0.0 collective-permute-done.1
  23.1 2.4 %collective-permute-start.5 = (bf16[256,768]{1,0:T(8,128)(2,1)S(1)}, bf16[256,768]{1,0:T(8,128)(2,1)S(1)}, u32[]{:S(2)}, u32[]{:S(2)}) collective-permute-start(bf16[256,768]{1,0:T(8,128)(2,1)S(1)} %pad_maximum_fusion.refs_3_), channel_id=1, source_target_pairs={{0,16},{16,32},{32,48},{48,0},{1,17},{17,33},{33,49},{49,1},{2,18}... | collective-permute-start | bytes 1179656 | tf_op jit(solution)/shard_map/weight_rings/ppermute | solution.py:23
  25.5 0.0 collective-permute-done.3
  25.5 1.6 %collective-permute-start.4 = (bf16[256,768]{1,0:T(8,128)(2,1)S(1)}, bf16[256,768]{1,0:T(8,128)(2,1)S(1)}, u32[]{:S(2)}, u32[]{:S(2)}) collective-permute-start(bf16[256,768]{1,0:T(8,128)(2,1)S(1)} %pad_maximum_fusion.refs_3_), channel_id=1, source_target_pairs={{0,128},{64,192},{128,0},{192,64},{1,129},{65,193},{129,1},{193,65... | collective-permute-start | bytes 1179656 | tf_op jit(solution)/shard_map/weight_rings/ppermute | solution.py:23
  27.2 0.3 collective-permute-done.8.refs_8_
  27.4 12.2 %collective-permute-done.7.refs_6_ = bf16[256,768]{1,0:T(8,128)(2,1)S(1)} collective-permute-done((bf16[256,768]{1,0:T(8,128)(2,1)S(1)}, bf16[256,768]{1,0:T(8,128)(2,1)S(1)}, u32[]{:S(2)}, u32[]{:S(2)}) %collective-permute-start.7) | collective-permute-done | bytes 393248 | tf_op jit(solution)/shard_map/weight_rings/ppermute | solution.py:23
  39.6 0.6 collective-permute-done.6.refs_1_
  40.3 0.0 collective-permute-done.5.refs_0_
  40.3 0.0 collective-permute-done.4.refs_10_
  40.3 0.8 pad_maximum_fusion.1
  41.1 0.1 copy-done.2
  41.1 0.0 all-gather.5.cloned.1.call-update
  41.2 0.9 relay_pair.1
  42.1 2.3 %collective-permute-start.10 = (bf16[512,768]{1,0:T(8,128)(2,1)S(1)}, bf16[512,768]{1,0:T(8,128)(2,1)S(1)}, u32[]{:S(2)}, u32[]{:S(2)}) collective-permute-start(bf16[512,768]{1,0:T(8,128)(2,1)S(1)} %get-tuple-element.44.refs_4_), channel_id=1, source_target_pairs={{0,192},{64,0},{128,64},{192,128},{1,193},{65,1},{129,65},{193,129... | collective-permute-start | bytes 2359304 | tf_op jit(solution)/shard_map/weight_rings/ppermute | solution.py:23
  44.4 0.7 collective-permute-start.9
  45.1 4.0 %collective-permute-start.11 = (bf16[128,768]{1,0:T(8,128)(2,1)S(1)}, bf16[128,768]{1,0:T(8,128)(2,1)S(1)}, u32[]{:S(2)}, u32[]{:S(2)}) collective-permute-start(bf16[128,768]{1,0:T(8,128)(2,1)S(1)} %get-tuple-element.45), channel_id=1, source_target_pairs={{0,16},{16,32},{32,48},{48,0},{1,17},{17,33},{33,49},{49,1},{2,18}... | collective-permute-start | bytes 589832 | tf_op jit(solution)/shard_map/weight_rings/ppermute | solution.py:23
  49.1 0.0 collective-permute-start.12
  49.1 6.3 %collective-permute-done.11.refs_2_ = bf16[128,768]{1,0:T(8,128)(2,1)S(1)} collective-permute-done((bf16[128,768]{1,0:T(8,128)(2,1)S(1)}, bf16[128,768]{1,0:T(8,128)(2,1)S(1)}, u32[]{:S(2)}, u32[]{:S(2)}) %collective-permute-start.11) | collective-permute-done | bytes 196640 | tf_op jit(solution)/shard_map/weight_rings/ppermute | solution.py:23
  55.4 5.0 %collective-permute-done.12.refs_3_ = bf16[128,768]{1,0:T(8,128)(2,1)S(1)} collective-permute-done((bf16[128,768]{1,0:T(8,128)(2,1)S(1)}, bf16[128,768]{1,0:T(8,128)(2,1)S(1)}, u32[]{:S(2)}, u32[]{:S(2)}) %collective-permute-start.12) | collective-permute-done | bytes 196640 | tf_op jit(solution)/shard_map/weight_rings/ppermute | solution.py:23
  60.4 0.0 collective-permute-done.10.refs_1_.refs_9_
  60.4 1.2 collective-permute-done.9.refs_0_.refs_7_
  61.5 1.4 %relay_far.1 = (bf16[256,768]{1,0:T(8,128)(2,1)}, bf16[256,768]{1,0:T(8,128)(2,1)}, bf16[256,768]{1,0:T(8,128)(2,1)}, bf16[256,768]{1,0:T(8,128)(2,1)}, bf16[256,768]{1,0:T(8,128)(2,1)}) custom-call(bf16[512,768]{1,0:T(8,128)(2,1)S(1)} %collective-permute-done.9.refs_0_.refs_7_, bf16[512,768]{1,0:T(8,128)(2,1)S(1)} %collective-permute-done.10.refs_1_.refs_9_, ...), custom_call_target="tpu_custom_call" | custom-call | bytes 2000000 | tf_op jit(solution)/shard_map/weight_rings/relay_far/pallas_call | solution.py:54
  62.9 7.8 %collective-permute-start.13 = (bf16[256,768]{1,0:T(8,128)(2,1)}, bf16[256,768]{1,0:T(8,128)(2,1)}, u32[]{:S(2)}, u32[]{:S(2)}) collective-permute-start(bf16[256,768]{1,0:T(8,128)(2,1)} %get-tuple-element.56), channel_id=1, source_target_pairs={{0,16},{16,32},{32,48},{48,0},{1,17},{17,33},{33,49},{49,1},{2,18}... | collective-permute-start | bytes 1179656 | tf_op jit(solution)/shard_map/weight_rings/ppermute | solution.py:23
  70.7 0.0 collective-permute-start.14
  70.7 0.0 collective-permute-start.15
  70.7 2.7 %collective-permute-start.16 = (bf16[256,768]{1,0:T(8,128)(2,1)}, bf16[256,768]{1,0:T(8,128)(2,1)}, u32[]{:S(2)}, u32[]{:S(2)}) collective-permute-start(bf16[256,768]{1,0:T(8,128)(2,1)} %get-tuple-element.59), channel_id=1, source_target_pairs={{0,192},{64,0},{128,64},{192,128},{1,193},{65,1},{129,65},{193,129... | collective-permute-start | bytes 1179656 | tf_op jit(solution)/shard_map/weight_rings/ppermute | solution.py:23
  73.4 0.0 collective-permute-start.17
  73.4 0.1 stack.23.refs_0_.pos
  73.5 0.2 all-gather.5.cloned.1.call-done.refs_2_
  73.6 1.7 %copy-done = bf16[2304,512]{1,0:T(8,128)(2,1)S(1)} copy-done((bf16[2304,512]{1,0:T(8,128)(2,1)S(1)}, bf16[2304,512]{1,0:T(8,128)(2,1)}, u32[]{:S(2)}) %copy-start) | copy-done | bytes 2359320
  75.3 1.6 %copy-done.1 = bf16[2048,512]{1,0:T(8,128)(2,1)S(1)} copy-done((bf16[2048,512]{1,0:T(8,128)(2,1)S(1)}, bf16[2048,512]{1,0:T(8,128)(2,1)}, u32[]{:S(2)}) %copy-start.1) | copy-done | bytes 2097176
  76.9 1.0 copy-done.3
  77.9 6.1 %project.1 = (f32[6,528,128]{2,1,0:T(8,128)S(1)}, bf16[528,1280]{1,0:T(8,128)(2,1)S(1)}) custom-call(s32[5]{0:T(128)S(1)} %stack.23.refs_0_.pos, bf16[2048,512]{1,0:T(8,128)(2,1)S(1)} %copy-done.1, bf16[2304,512]{1,0:T(8,128)(2,1)S(1)} %copy-done, bf16[256,768]{1,0:T(8,128)(2,1)S(1)} %pad_maximum_fusion.refs_3_, ...), custom_call_target="tpu_custom_call" | custom-call | flops 2283798528 | bytes 9000000 | tf_op jit(solution)/shard_map/project/pallas_call | solution.py:346
  84.0 4.3 %collective-permute-done.13.refs_2_ = bf16[256,768]{1,0:T(8,128)(2,1)} collective-permute-done((bf16[256,768]{1,0:T(8,128)(2,1)}, bf16[256,768]{1,0:T(8,128)(2,1)}, u32[]{:S(2)}, u32[]{:S(2)}) %collective-permute-start.13) | collective-permute-done | bytes 393248 | tf_op jit(solution)/shard_map/weight_rings/ppermute | solution.py:23
  88.3 0.0 collective-permute-done.14.refs_3_
  88.3 2.6 %collective-permute-done.15.refs_4_ = bf16[256,768]{1,0:T(8,128)(2,1)} collective-permute-done((bf16[256,768]{1,0:T(8,128)(2,1)}, bf16[256,768]{1,0:T(8,128)(2,1)}, u32[]{:S(2)}, u32[]{:S(2)}) %collective-permute-start.15) | collective-permute-done | bytes 393248 | tf_op jit(solution)/shard_map/weight_rings/ppermute | solution.py:23
  90.9 0.0 collective-permute-done.16.refs_5_
  90.9 0.0 collective-permute-done.17.refs_6_
  90.9 0.0 copy-start.5
  90.9 0.0 copy-start.6
  90.9 0.0 copy-start.8
  90.9 0.0 copy-start.9
  90.9 5.1 %states.1 = (f32[64,8,256]{2,1,0:T(8,128)S(1)}, f32[2,528,128]{2,1,0:T(8,128)S(1)}, f32[16,16,256]{2,1,0:T(8,128)}) custom-call(s32[5]{0:T(128)S(1)} %stack.23.refs_0_.pos, bf16[528,1280]{1,0:T(8,128)(2,1)S(1)} %get-tuple-element.55.refs_1_, bf16[256,768]{1,0:T(8,128)(2,1)} %collective-permute-done.13.refs_2_, ...), custom_call_target="tpu_custom_call" | custom-call | tf_op jit(solution)/shard_map/states/pallas_call | solution.py:368
  96.1 7.6 %all-to-all-start = ((f32[16,16,256]{2,1,0:T(8,128)}), f32[16,16,256]{2,1,0:T(8,128)S(1)}, u32[]{:S(2)}, u32[]{:S(2)}) async-start(f32[16,16,256]{2,1,0:T(8,128)} %get-tuple-element.66), calls=%async_computation | async-start | bytes 524288 | tf_op jit(solution)/shard_map/state_exchange/all_to_all | solution.py:386
  103.8 2.5 %local.1 = (f32[64,8,256]{2,1,0:T(8,128)S(1)}, f32[64,8,256]{2,1,0:T(8,128)S(1)}, f32[16,8,256]{2,1,0:T(8,128)S(1)}) custom-call(s32[5]{0:T(128)S(1)} %stack.23.refs_0_.pos, f32[2,528,128]{2,1,0:T(8,128)S(1)} %get-tuple-element.61.gated, f32[3,3,512]{2,1,0:T(4,128)S(1)} %copy-done.8, f32[64,8,256]{2,1,0:T(8,128)S(1)} %get-tuple-element.62.product, ...), custom_call_target="tpu_custom_call" | custom-call | flops 30000000 | bytes 2000000 | tf_op jit(solution)/shard_map/local/pallas_call | solution.py:387
  106.2 8.7 %all-to-all-done.states = f32[16,16,256]{2,1,0:T(8,128)S(1)} async-done(((f32[16,16,256]{2,1,0:T(8,128)}), f32[16,16,256]{2,1,0:T(8,128)S(1)}, u32[]{:S(2)}, u32[]{:S(2)}) %all-to-all-start) | async-done | bytes 262176 | tf_op jit(solution)/shard_map/state_exchange/all_to_all | solution.py:386
  114.9 1.5 %finish.1 = (bf16[256,256]{1,0:T(8,128)(2,1)S(1)}, bf16[256,256]{1,0:T(8,128)(2,1)S(1)}) custom-call(s32[5]{0:T(128)S(1)} %stack.23.refs_0_.pos, f32[64,8,256]{2,1,0:T(8,128)S(1)} %get-tuple-element.63.gate, f32[64,8,256]{2,1,0:T(8,128)S(1)} %get-tuple-element.64.local, f32[16,8,256]{2,1,0:T(8,128)S(1)} %get-tuple-element.65.inside, ...), custom_call_target="tpu_custom_call" | custom-call | tf_op jit(solution)/shard_map/finish/pallas_call | solution.py:398
  116.5 5.9 %collective-permute-start.18 = (bf16[256,256]{1,0:T(8,128)(2,1)S(1)}, bf16[256,256]{1,0:T(8,128)(2,1)S(1)}, u32[]{:S(2)}, u32[]{:S(2)}) collective-permute-start(bf16[256,256]{1,0:T(8,128)(2,1)S(1)} %get-tuple-element.68), channel_id=1, source_target_pairs={{0,8},{8,0},{1,9},{9,1},{2,10},{10,2},{3,11},{11,3},{4,12},{12,4},... | collective-permute-start | bytes 393224 | tf_op jit(solution)/shard_map/result_swap/ppermute | solution.py:408
  122.4 1.0 collective-permute-done.18
  123.4 0.7 pad_maximum_fusion.2
  (22 shorter events, 0.2 us)
Async XLA Ops:
  6.5 5.6 %copy-start.10 = (bf16[256,512]{1,0:T(8,128)(2,1)S(1)}, bf16[256,512]{1,0:T(8,128)(2,1)}, u32[]{:S(2)}) copy-start(bf16[256,512]{1,0:T(8,128)(2,1)} %param.6) | copy-start | bytes 786436
  6.5 66.9 %all-gather.3.cloned.1.call-start = ((), (), s32[]{:S(2)}) async-start(), calls=%async_computation.1 | async-start | bytes 2359296 | tf_op jit(solution)/shard_map/token_gather/all_gather | solution.py:305
  7.3 66.4 %all-gather.5.cloned.1.call-start = ((), (), s32[]{:S(2)}) async-start(), calls=%async_computation.2 | async-start | bytes 2654208 | tf_op jit(solution)/shard_map/token_gather/all_gather | solution.py:307
  8.8 4.4 %collective-permute-start = (bf16[128,768]{1,0:T(8,128)(2,1)S(1)}, bf16[128,768]{1,0:T(8,128)(2,1)S(1)}, u32[]{:S(2)}, u32[]{:S(2)}) collective-permute-start(bf16[128,768]{1,0:T(8,128)(2,1)S(1)} %bitcast.17), channel_id=1, source_target_pairs={{0,8},{8,0},{1,9},{9,1},{2,10},{10,2},{3,11},{11,3},{4,12},{12,4},... | collective-permute-start | bytes 589832 | tf_op jit(solution)/shard_map/weight_gather/ppermute | solution.py:290
  12.1 13.4 %collective-permute-start.3 = (bf16[256,512]{1,0:T(8,128)(2,1)S(1)}, bf16[256,512]{1,0:T(8,128)(2,1)S(1)}, u32[]{:S(2)}, u32[]{:S(2)}) collective-permute-start(bf16[256,512]{1,0:T(8,128)(2,1)S(1)} %copy-done.10), channel_id=1, source_target_pairs={{0,4},{4,0},{1,5},{5,1},{2,6},{6,2},{3,7},{7,3},{8,12},{12,8},{9,1... | collective-permute-start | bytes 786440 | tf_op jit(solution)/shard_map/token_swap/ppermute | solution.py:294
  13.2 8.9 %collective-permute-start.2 = (bf16[16,512]{1,0:T(8,128)(2,1)S(1)}, bf16[16,512]{1,0:T(8,128)(2,1)S(1)}, u32[]{:S(2)}, u32[]{:S(2)}) collective-permute-start(bf16[16,512]{1,0:T(8,128)(2,1)S(1)} %slice.3), channel_id=1, source_target_pairs={{8,20},{12,16},{24,36},{28,32},{40,52},{44,48},{56,68},{60,64},{72... | collective-permute-start | bytes 49160 | tf_op jit(solution)/shard_map/token_swap/ppermute | solution.py:297
  18.0 5.1 %collective-permute-start.1 = (bf16[16,512]{1,0:T(8,128)(2,1)S(1)}, bf16[16,512]{1,0:T(8,128)(2,1)S(1)}, u32[]{:S(2)}, u32[]{:S(2)}) collective-permute-start(bf16[16,512]{1,0:T(8,128)(2,1)S(1)} %slice.3), channel_id=1, source_target_pairs={{8,16},{12,20},{24,32},{28,36},{40,48},{44,52},{56,64},{60,68},{72... | collective-permute-start | bytes 49160 | tf_op jit(solution)/shard_map/token_swap/ppermute | solution.py:296
  19.3 8.1 %collective-permute-start.8 = (bf16[256,768]{1,0:T(8,128)(2,1)S(1)}, bf16[256,768]{1,0:T(8,128)(2,1)S(1)}, u32[]{:S(2)}, u32[]{:S(2)}) collective-permute-start(bf16[256,768]{1,0:T(8,128)(2,1)S(1)} %pad_maximum_fusion.refs_3_), channel_id=1, source_target_pairs={{0,192},{64,0},{128,64},{192,128},{1,193},{65,1},{129,65},{193,129... | collective-permute-start | bytes 1179656 | tf_op jit(solution)/shard_map/weight_rings/ppermute | solution.py:23
  22.1 17.5 %collective-permute-start.7 = (bf16[256,768]{1,0:T(8,128)(2,1)S(1)}, bf16[256,768]{1,0:T(8,128)(2,1)S(1)}, u32[]{:S(2)}, u32[]{:S(2)}) collective-permute-start(bf16[256,768]{1,0:T(8,128)(2,1)S(1)} %pad_maximum_fusion.refs_3_), channel_id=1, source_target_pairs={{0,64},{64,128},{128,192},{192,0},{1,65},{65,129},{129,193},{193,1... | collective-permute-start | bytes 1179656 | tf_op jit(solution)/shard_map/weight_rings/ppermute | solution.py:23
  22.1 18.2 %collective-permute-start.6 = (bf16[256,768]{1,0:T(8,128)(2,1)S(1)}, bf16[256,768]{1,0:T(8,128)(2,1)S(1)}, u32[]{:S(2)}, u32[]{:S(2)}) collective-permute-start(bf16[256,768]{1,0:T(8,128)(2,1)S(1)} %pad_maximum_fusion.refs_3_), channel_id=1, source_target_pairs={{0,48},{16,0},{32,16},{48,32},{1,49},{17,1},{33,17},{49,33},{2,50}... | collective-permute-start | bytes 1179656 | tf_op jit(solution)/shard_map/weight_rings/ppermute | solution.py:23
  23.1 17.1 %collective-permute-start.5 = (bf16[256,768]{1,0:T(8,128)(2,1)S(1)}, bf16[256,768]{1,0:T(8,128)(2,1)S(1)}, u32[]{:S(2)}, u32[]{:S(2)}) collective-permute-start(bf16[256,768]{1,0:T(8,128)(2,1)S(1)} %pad_maximum_fusion.refs_3_), channel_id=1, source_target_pairs={{0,16},{16,32},{32,48},{48,0},{1,17},{17,33},{33,49},{49,1},{2,18}... | collective-permute-start | bytes 1179656 | tf_op jit(solution)/shard_map/weight_rings/ppermute | solution.py:23
  25.5 14.8 %collective-permute-start.4 = (bf16[256,768]{1,0:T(8,128)(2,1)S(1)}, bf16[256,768]{1,0:T(8,128)(2,1)S(1)}, u32[]{:S(2)}, u32[]{:S(2)}) collective-permute-start(bf16[256,768]{1,0:T(8,128)(2,1)S(1)} %pad_maximum_fusion.refs_3_), channel_id=1, source_target_pairs={{0,128},{64,192},{128,0},{192,64},{1,129},{65,193},{129,1},{193,65... | collective-permute-start | bytes 1179656 | tf_op jit(solution)/shard_map/weight_rings/ppermute | solution.py:23
  40.3 0.9 copy-start.2
  42.1 18.3 %collective-permute-start.10 = (bf16[512,768]{1,0:T(8,128)(2,1)S(1)}, bf16[512,768]{1,0:T(8,128)(2,1)S(1)}, u32[]{:S(2)}, u32[]{:S(2)}) collective-permute-start(bf16[512,768]{1,0:T(8,128)(2,1)S(1)} %get-tuple-element.44.refs_4_), channel_id=1, source_target_pairs={{0,192},{64,0},{128,64},{192,128},{1,193},{65,1},{129,65},{193,129... | collective-permute-start | bytes 2359304 | tf_op jit(solution)/shard_map/weight_rings/ppermute | solution.py:23
  44.4 17.1 %collective-permute-start.9 = (bf16[512,768]{1,0:T(8,128)(2,1)S(1)}, bf16[512,768]{1,0:T(8,128)(2,1)S(1)}, u32[]{:S(2)}, u32[]{:S(2)}) collective-permute-start(bf16[512,768]{1,0:T(8,128)(2,1)S(1)} %get-tuple-element.44.refs_4_), channel_id=1, source_target_pairs={{0,64},{64,128},{128,192},{192,0},{1,65},{65,129},{129,193},{193,1... | collective-permute-start | bytes 2359304 | tf_op jit(solution)/shard_map/weight_rings/ppermute | solution.py:23
  45.1 10.3 %collective-permute-start.11 = (bf16[128,768]{1,0:T(8,128)(2,1)S(1)}, bf16[128,768]{1,0:T(8,128)(2,1)S(1)}, u32[]{:S(2)}, u32[]{:S(2)}) collective-permute-start(bf16[128,768]{1,0:T(8,128)(2,1)S(1)} %get-tuple-element.45), channel_id=1, source_target_pairs={{0,16},{16,32},{32,48},{48,0},{1,17},{17,33},{33,49},{49,1},{2,18}... | collective-permute-start | bytes 589832 | tf_op jit(solution)/shard_map/weight_rings/ppermute | solution.py:23
  49.1 11.3 %collective-permute-start.12 = (bf16[128,768]{1,0:T(8,128)(2,1)S(1)}, bf16[128,768]{1,0:T(8,128)(2,1)S(1)}, u32[]{:S(2)}, u32[]{:S(2)}) collective-permute-start(bf16[128,768]{1,0:T(8,128)(2,1)S(1)} %get-tuple-element.46), channel_id=1, source_target_pairs={{0,48},{16,0},{32,16},{48,32},{1,49},{17,1},{33,17},{49,33},{2,50}... | collective-permute-start | bytes 589832 | tf_op jit(solution)/shard_map/weight_rings/ppermute | solution.py:23
  62.9 25.4 %collective-permute-start.13 = (bf16[256,768]{1,0:T(8,128)(2,1)}, bf16[256,768]{1,0:T(8,128)(2,1)}, u32[]{:S(2)}, u32[]{:S(2)}) collective-permute-start(bf16[256,768]{1,0:T(8,128)(2,1)} %get-tuple-element.56), channel_id=1, source_target_pairs={{0,16},{16,32},{32,48},{48,0},{1,17},{17,33},{33,49},{49,1},{2,18}... | collective-permute-start | bytes 1179656 | tf_op jit(solution)/shard_map/weight_rings/ppermute | solution.py:23
  70.7 17.6 %collective-permute-start.14 = (bf16[256,768]{1,0:T(8,128)(2,1)}, bf16[256,768]{1,0:T(8,128)(2,1)}, u32[]{:S(2)}, u32[]{:S(2)}) collective-permute-start(bf16[256,768]{1,0:T(8,128)(2,1)} %get-tuple-element.57), channel_id=1, source_target_pairs={{0,48},{16,0},{32,16},{48,32},{1,49},{17,1},{33,17},{49,33},{2,50}... | collective-permute-start | bytes 1179656 | tf_op jit(solution)/shard_map/weight_rings/ppermute | solution.py:23
  70.7 20.2 %collective-permute-start.15 = (bf16[256,768]{1,0:T(8,128)(2,1)}, bf16[256,768]{1,0:T(8,128)(2,1)}, u32[]{:S(2)}, u32[]{:S(2)}) collective-permute-start(bf16[256,768]{1,0:T(8,128)(2,1)} %get-tuple-element.58), channel_id=1, source_target_pairs={{0,64},{64,128},{128,192},{192,0},{1,65},{65,129},{129,193},{193,1... | collective-permute-start | bytes 1179656 | tf_op jit(solution)/shard_map/weight_rings/ppermute | solution.py:23
  70.7 20.2 %collective-permute-start.16 = (bf16[256,768]{1,0:T(8,128)(2,1)}, bf16[256,768]{1,0:T(8,128)(2,1)}, u32[]{:S(2)}, u32[]{:S(2)}) collective-permute-start(bf16[256,768]{1,0:T(8,128)(2,1)} %get-tuple-element.59), channel_id=1, source_target_pairs={{0,192},{64,0},{128,64},{192,128},{1,193},{65,1},{129,65},{193,129... | collective-permute-start | bytes 1179656 | tf_op jit(solution)/shard_map/weight_rings/ppermute | solution.py:23
  73.4 17.5 %collective-permute-start.17 = (bf16[256,768]{1,0:T(8,128)(2,1)}, bf16[256,768]{1,0:T(8,128)(2,1)}, u32[]{:S(2)}, u32[]{:S(2)}) collective-permute-start(bf16[256,768]{1,0:T(8,128)(2,1)} %get-tuple-element.51.refs_5_), channel_id=1, source_target_pairs={{0,128},{64,192},{128,0},{192,64},{1,129},{65,193},{129,1},{193,65... | collective-permute-start | bytes 1179656 | tf_op jit(solution)/shard_map/weight_rings/ppermute | solution.py:23
  73.6 1.7 %copy-start = (bf16[2304,512]{1,0:T(8,128)(2,1)S(1)}, bf16[2304,512]{1,0:T(8,128)(2,1)}, u32[]{:S(2)}) copy-start(bf16[2304,512]{1,0:T(8,128)(2,1)} %all-gather.5.cloned.1.call-done.refs_2_) | copy-start | bytes 7077892
  75.3 1.6 %copy-start.1 = (bf16[2048,512]{1,0:T(8,128)(2,1)S(1)}, bf16[2048,512]{1,0:T(8,128)(2,1)}, u32[]{:S(2)}) copy-start(bf16[2048,512]{1,0:T(8,128)(2,1)} %all-gather.3.cloned.1.call-done.refs_1_) | copy-start | bytes 6291460
  76.9 1.0 copy-start.3
  77.9 13.0 %copy-start.4 = (f32[16,512]{1,0:T(8,128)S(1)}, f32[16,512]{1,0:T(8,128)}, u32[]{:S(2)}) copy-start(f32[16,512]{1,0:T(8,128)} %decay.3) | copy-start | bytes 98308
  77.9 13.0 %copy-start.7 = (f32[3,3,512]{2,1,0:T(4,128)S(1)}, f32[3,3,512]{2,1,0:T(4,128)}, u32[]{:S(2)}) copy-start(f32[3,3,512]{2,1,0:T(4,128)} %taps.1) | copy-start | bytes 55300
  90.9 12.8 %copy-start.5 = (f32[16,512]{1,0:T(8,128)S(1)}, f32[16,512]{1,0:T(8,128)}, u32[]{:S(2)}) copy-start(f32[16,512]{1,0:T(8,128)} %decay.3) | copy-start | bytes 98308
  90.9 12.8 %copy-start.6 = (f32[16,512]{1,0:T(8,128)S(1)}, f32[16,512]{1,0:T(8,128)}, u32[]{:S(2)}) copy-start(f32[16,512]{1,0:T(8,128)} %gain.3) | copy-start | bytes 98308
  90.9 12.8 %copy-start.8 = (f32[3,3,512]{2,1,0:T(4,128)S(1)}, f32[3,3,512]{2,1,0:T(4,128)}, u32[]{:S(2)}) copy-start(f32[3,3,512]{2,1,0:T(4,128)} %taps.1) | copy-start | bytes 55300
  90.9 12.8 %copy-start.9 = (f32[512]{0:T(512)S(1)}, f32[512]{0:T(512)}, u32[]{:S(2)}) copy-start(f32[512]{0:T(512)} %param.11) | copy-start | bytes 6148
  96.1 18.8 %all-to-all-start = ((f32[16,16,256]{2,1,0:T(8,128)}), f32[16,16,256]{2,1,0:T(8,128)S(1)}, u32[]{:S(2)}, u32[]{:S(2)}) async-start(f32[16,16,256]{2,1,0:T(8,128)} %get-tuple-element.66), calls=%async_computation | async-start | bytes 524288 | tf_op jit(solution)/shard_map/state_exchange/all_to_all | solution.py:386
  116.5 6.9 %collective-permute-start.18 = (bf16[256,256]{1,0:T(8,128)(2,1)S(1)}, bf16[256,256]{1,0:T(8,128)(2,1)S(1)}, u32[]{:S(2)}, u32[]{:S(2)}) collective-permute-start(bf16[256,256]{1,0:T(8,128)(2,1)S(1)} %get-tuple-element.68), channel_id=1, source_target_pairs={{0,8},{8,0},{1,9},{9,1},{2,10},{10,2},{3,11},{11,3},{4,12},{12,4},... | collective-permute-start | bytes 393224 | tf_op jit(solution)/shard_map/result_swap/ppermute | solution.py:408
Sparse Core Ops, SparseCore 0:
  9.2 32.1 all-gather.2
  43.3 30.2 all-gather.4

commit v11 on v10

--- a/solution.py
+++ b/solution.py
@@ -299,8 +299,8 @@
         farther = shifted(own, "y", 2)
         far = both_ways(own, "y")
         beside = both_ways(own, "h")
-    first = (halo, other_halo, other, farther, beside, far)
-    halo, other_halo, other, farther, beside, far = tie(first)
+    first = (halo, other_halo, other, farther, far, beside)
+    halo, other_halo, other, farther, far, beside = tie(first)
     with jax.named_scope("token_gather"):
         near = lax.all_gather(tokens, ("c", "x"), axis=0, tiled=True)
         wide = jnp.concatenate([halo, other_halo, other], 0)
@@ -328,9 +328,10 @@
         early_runs += [(dy, dh, 0, two) for dh in (0, 1, -1)]
     early += [farther]
     early_runs += [(2, 0, 0, two)]
-    late = [*far_opposite, *farther_pair, last]
-    late_runs = [(dy, 2, skip, half) for skip in (0, half) for dy in (1, -1)]
-    late_runs += [(2, 1, 0, two), (2, -1, 0, two), (2, 2, 0, two)]
+    late = [*farther_pair, *far_opposite, last]
+    late_runs = [(2, 1, 0, two), (2, -1, 0, two)]
+    late_runs += [(dy, 2, skip, half) for skip in (0, half) for dy in (1, -1)]
+    late_runs += [(2, 2, 0, two)]
 
     vmem = pl.BlockSpec(memory_space=pltpu.VMEM)
     smem = pl.BlockSpec(memory_space=pltpu.SMEM)

time: 131 us -> 127 us (0.969)
  starting transfers between devices: 48.2 us -> 34.6 us
  waiting for transfers between devices: 44 us -> 52.9 us
    ppermute x14, waiting for transfers between devices: 32.5 us -> 40.8 us  [shifted(): return lax.ppermute(array, axis, [(i, (i + step) % n) for i in range(n)])]
    ppermute x14, starting transfers between devices: 25.3 us -> 19.3 us  [shifted(): return lax.ppermute(array, axis, [(i, (i + step) % n) for i in range(n)])]
    all_to_all x1, starting transfers between devices: 7.63 us -> 3.53 us  [body(): states = lax.all_to_all(state, ('y', 'h'), 0, 0, tiled=True)]
    ppermute x1, starting transfers between devices: 5.9 us -> 2.39 us  [body(): return in_order(c == 0, mine, lax.ppermute(theirs, 'c', SWAP), 1)]
  transfers between devices with their start and end apart: 22 -> 22, of which waited for: 12 -> 13; matrix products, arithmetic and copies ran while one was open for 2% -> 2% of each run, Pallas kernels for 8% -> 9%
where the time goes in v11:
time: 127 us; the launch traced here: 126 us
  waiting for transfers between devices  52.9 us (42%)
  starting transfers between devices  34.6 us (27%)
  Pallas kernels  17.5 us (14%)
  between operations  13.6 us (11%)
  local copies, waits for them, and re-layouts  6.03 us (5%)
  other arithmetic  1.59 us (1%)
    ppermute x14, waiting for transfers between devices, shifted(): return lax.ppermute(array, axis, [(i, (i + step) % n) for i in range(n)])  40.8 us
    ppermute x14, starting transfers between devices, shifted(): return lax.ppermute(array, axis, [(i, (i + step) % n) for i in range(n)])  19.3 us
    all_to_all x1, waiting for transfers between devices, body(): states = lax.all_to_all(state, ('y', 'h'), 0, 0, tiled=True)  9.42 us
    pallas_call x1, Pallas kernels, body(): pl.pallas_call(functools.partial(project_kernel, sizes, early_runs, late_...  6.05 us
    unnamed x23, local copies, waits for them, and re-layouts  5.59 us
    pallas_call x1, Pallas kernels, body(): pl.pallas_call(functools.partial(state_kernel, sizes), out_shape=(full, j...  5.14 us
    ppermute x1, starting transfers between devices, body(): other_halo = lax.ppermute(tail, (*CTX, 'l'), [(i, j ^ 1) for i, j in route])  4.77 us
    all_to_all x1, starting transfers between devices, body(): states = lax.all_to_all(state, ('y', 'h'), 0, 0, tiled=True)  3.53 us
  transfers between devices with their start and end apart: 22, of which 13 were waited for; matrix products, arithmetic and copies ran while one was open for 2% of the time, Pallas kernels for 9%

profile of v11, /device:TPU:1, one launch (start us, length us, event | category | flops | bytes accessed | tf_op | source)
XLA Modules:
  0.0 126.3 jit_solution(9947426771327382902)
XLA Ops:
  6.5 0.0 all-gather.3.cloned.1.call-start
  6.5 0.7 all-gather.3.cloned.1.call-update
  7.3 0.0 all-gather.5.cloned.1.call-start
  7.3 1.2 copy.10
  8.6 0.1 copy.13
  8.8 3.3 %collective-permute-start = (bf16[128,768]{1,0:T(8,128)(2,1)S(1)}, bf16[128,768]{1,0:T(8,128)(2,1)S(1)}, u32[]{:S(2)}, u32[]{:S(2)}) collective-permute-start(bf16[128,768]{1,0:T(8,128)(2,1)S(1)} %bitcast.17), channel_id=1, source_target_pairs={{0,8},{8,0},{1,9},{9,1},{2,10},{10,2},{3,11},{11,3},{4,12},{12,4},... | collective-permute-start | bytes 589832 | tf_op jit(solution)/shard_map/weight_gather/ppermute | solution.py:290
  12.1 0.0 collective-permute-start.3
  12.1 0.1 copy.12
  12.2 0.9 collective-permute-done
  13.2 4.8 %collective-permute-start.2 = (bf16[16,512]{1,0:T(8,128)(2,1)S(1)}, bf16[16,512]{1,0:T(8,128)(2,1)S(1)}, u32[]{:S(2)}, u32[]{:S(2)}) collective-permute-start(bf16[16,512]{1,0:T(8,128)(2,1)S(1)} %slice.3), channel_id=1, source_target_pairs={{8,20},{12,16},{24,36},{28,32},{40,52},{44,48},{56,68},{60,64},{72... | collective-permute-start | bytes 49160 | tf_op jit(solution)/shard_map/token_swap/ppermute | solution.py:297
  18.0 1.3 %collective-permute-start.1 = (bf16[16,512]{1,0:T(8,128)(2,1)S(1)}, bf16[16,512]{1,0:T(8,128)(2,1)S(1)}, u32[]{:S(2)}, u32[]{:S(2)}) collective-permute-start(bf16[16,512]{1,0:T(8,128)(2,1)S(1)} %slice.3), channel_id=1, source_target_pairs={{8,16},{12,20},{24,32},{28,36},{40,48},{44,52},{56,64},{60,68},{72... | collective-permute-start | bytes 49160 | tf_op jit(solution)/shard_map/token_swap/ppermute | solution.py:296
  19.3 1.7 %collective-permute-start.8 = (bf16[256,768]{1,0:T(8,128)(2,1)S(1)}, bf16[256,768]{1,0:T(8,128)(2,1)S(1)}, u32[]{:S(2)}, u32[]{:S(2)}) collective-permute-start(bf16[256,768]{1,0:T(8,128)(2,1)S(1)} %pad_maximum_fusion.refs_3_), channel_id=1, source_target_pairs={{0,48},{16,0},{32,16},{48,32},{1,49},{17,1},{33,17},{49,33},{2,50}... | collective-permute-start | bytes 1179656 | tf_op jit(solution)/shard_map/weight_rings/ppermute | solution.py:23
  21.0 1.8 %collective-permute-start.7 = (bf16[256,768]{1,0:T(8,128)(2,1)S(1)}, bf16[256,768]{1,0:T(8,128)(2,1)S(1)}, u32[]{:S(2)}, u32[]{:S(2)}) collective-permute-start(bf16[256,768]{1,0:T(8,128)(2,1)S(1)} %pad_maximum_fusion.refs_3_), channel_id=1, source_target_pairs={{0,16},{16,32},{32,48},{48,0},{1,17},{17,33},{33,49},{49,1},{2,18}... | collective-permute-start | bytes 1179656 | tf_op jit(solution)/shard_map/weight_rings/ppermute | solution.py:23
  22.8 0.0 collective-permute-done.2
  22.8 2.7 %collective-permute-start.6 = (bf16[256,768]{1,0:T(8,128)(2,1)S(1)}, bf16[256,768]{1,0:T(8,128)(2,1)S(1)}, u32[]{:S(2)}, u32[]{:S(2)}) collective-permute-start(bf16[256,768]{1,0:T(8,128)(2,1)S(1)} %pad_maximum_fusion.refs_3_), channel_id=1, source_target_pairs={{0,192},{64,0},{128,64},{192,128},{1,193},{65,1},{129,65},{193,129... | collective-permute-start | bytes 1179656 | tf_op jit(solution)/shard_map/weight_rings/ppermute | solution.py:23
  25.5 0.0 collective-permute-done.1
  25.5 0.0 collective-permute-start.5
  25.5 0.0 collective-permute-done.3
  25.5 1.6 %collective-permute-start.4 = (bf16[256,768]{1,0:T(8,128)(2,1)S(1)}, bf16[256,768]{1,0:T(8,128)(2,1)S(1)}, u32[]{:S(2)}, u32[]{:S(2)}) collective-permute-start(bf16[256,768]{1,0:T(8,128)(2,1)S(1)} %pad_maximum_fusion.refs_3_), channel_id=1, source_target_pairs={{0,128},{64,192},{128,0},{192,64},{1,129},{65,193},{129,1},{193,65... | collective-permute-start | bytes 1179656 | tf_op jit(solution)/shard_map/weight_rings/ppermute | solution.py:23
  27.2 11.2 %collective-permute-done.8.refs_1_ = bf16[256,768]{1,0:T(8,128)(2,1)S(1)} collective-permute-done((bf16[256,768]{1,0:T(8,128)(2,1)S(1)}, bf16[256,768]{1,0:T(8,128)(2,1)S(1)}, u32[]{:S(2)}, u32[]{:S(2)}) %collective-permute-start.8) | collective-permute-done | bytes 393248 | tf_op jit(solution)/shard_map/weight_rings/ppermute | solution.py:23
  38.4 0.9 collective-permute-done.7.refs_0_
  39.3 2.1 %collective-permute-done.6.refs_8_ = bf16[256,768]{1,0:T(8,128)(2,1)S(1)} collective-permute-done((bf16[256,768]{1,0:T(8,128)(2,1)S(1)}, bf16[256,768]{1,0:T(8,128)(2,1)S(1)}, u32[]{:S(2)}, u32[]{:S(2)}) %collective-permute-start.6) | collective-permute-done | bytes 393248 | tf_op jit(solution)/shard_map/weight_rings/ppermute | solution.py:23
  41.4 4.3 %collective-permute-done.5.refs_6_ = bf16[256,768]{1,0:T(8,128)(2,1)S(1)} collective-permute-done((bf16[256,768]{1,0:T(8,128)(2,1)S(1)}, bf16[256,768]{1,0:T(8,128)(2,1)S(1)}, u32[]{:S(2)}, u32[]{:S(2)}) %collective-permute-start.5) | collective-permute-done | bytes 393248 | tf_op jit(solution)/shard_map/weight_rings/ppermute | solution.py:23
  45.7 0.0 collective-permute-done.4.refs_10_
  45.7 0.8 pad_maximum_fusion.1
  46.5 0.1 copy-done.2
  46.6 0.0 all-gather.5.cloned.1.call-update
  46.6 0.9 relay_pair.1
  47.5 0.1 collective-permute-start.10
  47.6 1.5 %collective-permute-start.9 = (bf16[512,768]{1,0:T(8,128)(2,1)S(1)}, bf16[512,768]{1,0:T(8,128)(2,1)S(1)}, u32[]{:S(2)}, u32[]{:S(2)}) collective-permute-start(bf16[512,768]{1,0:T(8,128)(2,1)S(1)} %get-tuple-element.44.refs_4_), channel_id=1, source_target_pairs={{0,64},{64,128},{128,192},{192,0},{1,65},{65,129},{129,193},{193,1... | collective-permute-start | bytes 2359304 | tf_op jit(solution)/shard_map/weight_rings/ppermute | solution.py:23
  49.1 0.7 collective-permute-start.11
  49.7 2.9 %collective-permute-start.12 = (bf16[128,768]{1,0:T(8,128)(2,1)S(1)}, bf16[128,768]{1,0:T(8,128)(2,1)S(1)}, u32[]{:S(2)}, u32[]{:S(2)}) collective-permute-start(bf16[128,768]{1,0:T(8,128)(2,1)S(1)} %get-tuple-element.46), channel_id=1, source_target_pairs={{0,48},{16,0},{32,16},{48,32},{1,49},{17,1},{33,17},{49,33},{2,50}... | collective-permute-start | bytes 589832 | tf_op jit(solution)/shard_map/weight_rings/ppermute | solution.py:23
  52.6 6.2 %collective-permute-done.11.refs_2_ = bf16[128,768]{1,0:T(8,128)(2,1)S(1)} collective-permute-done((bf16[128,768]{1,0:T(8,128)(2,1)S(1)}, bf16[128,768]{1,0:T(8,128)(2,1)S(1)}, u32[]{:S(2)}, u32[]{:S(2)}) %collective-permute-start.11) | collective-permute-done | bytes 196640 | tf_op jit(solution)/shard_map/weight_rings/ppermute | solution.py:23
  58.8 3.8 %collective-permute-done.12.refs_3_ = bf16[128,768]{1,0:T(8,128)(2,1)S(1)} collective-permute-done((bf16[128,768]{1,0:T(8,128)(2,1)S(1)}, bf16[128,768]{1,0:T(8,128)(2,1)S(1)}, u32[]{:S(2)}, u32[]{:S(2)}) %collective-permute-start.12) | collective-permute-done | bytes 196640 | tf_op jit(solution)/shard_map/weight_rings/ppermute | solution.py:23
  62.6 3.9 %collective-permute-done.10.refs_1_.refs_9_ = bf16[512,768]{1,0:T(8,128)(2,1)S(1)} collective-permute-done((bf16[512,768]{1,0:T(8,128)(2,1)S(1)}, bf16[512,768]{1,0:T(8,128)(2,1)S(1)}, u32[]{:S(2)}, u32[]{:S(2)}) %collective-permute-start.10) | collective-permute-done | bytes 786464 | tf_op jit(solution)/shard_map/weight_rings/ppermute | solution.py:23
  66.4 1.2 collective-permute-done.9.refs_0_.refs_7_
  67.6 1.4 %relay_far.1 = (bf16[256,768]{1,0:T(8,128)(2,1)}, bf16[256,768]{1,0:T(8,128)(2,1)}, bf16[256,768]{1,0:T(8,128)(2,1)}, bf16[256,768]{1,0:T(8,128)(2,1)}, bf16[256,768]{1,0:T(8,128)(2,1)}) custom-call(bf16[512,768]{1,0:T(8,128)(2,1)S(1)} %collective-permute-done.9.refs_0_.refs_7_, bf16[512,768]{1,0:T(8,128)(2,1)S(1)} %collective-permute-done.10.refs_1_.refs_9_, ...), custom_call_target="tpu_custom_call" | custom-call | bytes 2000000 | tf_op jit(solution)/shard_map/weight_rings/relay_far/pallas_call | solution.py:54
  69.0 0.1 collective-permute-start.13
  69.1 2.7 %collective-permute-start.14 = (bf16[256,768]{1,0:T(8,128)(2,1)}, bf16[256,768]{1,0:T(8,128)(2,1)}, u32[]{:S(2)}, u32[]{:S(2)}) collective-permute-start(bf16[256,768]{1,0:T(8,128)(2,1)} %get-tuple-element.57), channel_id=1, source_target_pairs={{0,192},{64,0},{128,64},{192,128},{1,193},{65,1},{129,65},{193,129... | collective-permute-start | bytes 1179656 | tf_op jit(solution)/shard_map/weight_rings/ppermute | solution.py:23
  71.8 0.0 collective-permute-start.15
  71.8 3.6 %collective-permute-start.16 = (bf16[256,768]{1,0:T(8,128)(2,1)}, bf16[256,768]{1,0:T(8,128)(2,1)}, u32[]{:S(2)}, u32[]{:S(2)}) collective-permute-start(bf16[256,768]{1,0:T(8,128)(2,1)} %get-tuple-element.59), channel_id=1, source_target_pairs={{0,48},{16,0},{32,16},{48,32},{1,49},{17,1},{33,17},{49,33},{2,50}... | collective-permute-start | bytes 1179656 | tf_op jit(solution)/shard_map/weight_rings/ppermute | solution.py:23
  75.3 0.0 collective-permute-start.17
  75.3 0.1 stack.23.refs_0_.pos
  75.4 1.7 %copy-done = bf16[2304,512]{1,0:T(8,128)(2,1)S(1)} copy-done((bf16[2304,512]{1,0:T(8,128)(2,1)S(1)}, bf16[2304,512]{1,0:T(8,128)(2,1)}, u32[]{:S(2)}) %copy-start) | copy-done | bytes 2359320
  77.1 1.6 %copy-done.1 = bf16[2048,512]{1,0:T(8,128)(2,1)S(1)} copy-done((bf16[2048,512]{1,0:T(8,128)(2,1)S(1)}, bf16[2048,512]{1,0:T(8,128)(2,1)}, u32[]{:S(2)}) %copy-start.1) | copy-done | bytes 2097176
  78.7 1.0 copy-done.3
  79.7 6.1 %project.1 = (f32[6,528,128]{2,1,0:T(8,128)S(1)}, bf16[528,1280]{1,0:T(8,128)(2,1)S(1)}) custom-call(s32[5]{0:T(128)S(1)} %stack.23.refs_0_.pos, bf16[2048,512]{1,0:T(8,128)(2,1)S(1)} %copy-done.1, bf16[2304,512]{1,0:T(8,128)(2,1)S(1)} %copy-done, bf16[256,768]{1,0:T(8,128)(2,1)S(1)} %pad_maximum_fusion.refs_3_, ...), custom_call_target="tpu_custom_call" | custom-call | flops 2283798528 | bytes 9000000 | tf_op jit(solution)/shard_map/project/pallas_call | solution.py:347
  85.8 0.0 collective-permute-done.13.refs_2_
  85.8 0.0 collective-permute-done.14.refs_3_
  85.8 4.1 %collective-permute-done.15.refs_4_ = bf16[256,768]{1,0:T(8,128)(2,1)} collective-permute-done((bf16[256,768]{1,0:T(8,128)(2,1)}, bf16[256,768]{1,0:T(8,128)(2,1)}, u32[]{:S(2)}, u32[]{:S(2)}) %collective-permute-start.15) | collective-permute-done | bytes 393248 | tf_op jit(solution)/shard_map/weight_rings/ppermute | solution.py:23
  89.9 3.2 %collective-permute-done.16.refs_5_ = bf16[256,768]{1,0:T(8,128)(2,1)} collective-permute-done((bf16[256,768]{1,0:T(8,128)(2,1)}, bf16[256,768]{1,0:T(8,128)(2,1)}, u32[]{:S(2)}, u32[]{:S(2)}) %collective-permute-start.16) | collective-permute-done | bytes 393248 | tf_op jit(solution)/shard_map/weight_rings/ppermute | solution.py:23
  93.1 0.0 collective-permute-done.17.refs_6_
  93.1 0.0 copy-start.5
  93.1 0.0 copy-start.6
  93.1 0.0 copy-start.8
  93.1 0.0 copy-start.9
  93.1 5.1 %states.1 = (f32[64,8,256]{2,1,0:T(8,128)S(1)}, f32[2,528,128]{2,1,0:T(8,128)S(1)}, f32[16,16,256]{2,1,0:T(8,128)}) custom-call(s32[5]{0:T(128)S(1)} %stack.23.refs_0_.pos, bf16[528,1280]{1,0:T(8,128)(2,1)S(1)} %get-tuple-element.55.refs_1_, bf16[256,768]{1,0:T(8,128)(2,1)} %collective-permute-done.13.refs_2_, ...), custom_call_target="tpu_custom_call" | custom-call | tf_op jit(solution)/shard_map/states/pallas_call | solution.py:369
  98.3 3.5 %all-to-all-start = ((f32[16,16,256]{2,1,0:T(8,128)}), f32[16,16,256]{2,1,0:T(8,128)S(1)}, u32[]{:S(2)}, u32[]{:S(2)}) async-start(f32[16,16,256]{2,1,0:T(8,128)} %get-tuple-element.66), calls=%async_computation | async-start | bytes 524288 | tf_op jit(solution)/shard_map/state_exchange/all_to_all | solution.py:387
  101.9 2.5 %local.1 = (f32[64,8,256]{2,1,0:T(8,128)S(1)}, f32[64,8,256]{2,1,0:T(8,128)S(1)}, f32[16,8,256]{2,1,0:T(8,128)S(1)}) custom-call(s32[5]{0:T(128)S(1)} %stack.23.refs_0_.pos, f32[2,528,128]{2,1,0:T(8,128)S(1)} %get-tuple-element.61.gated, f32[3,3,512]{2,1,0:T(4,128)S(1)} %copy-done.8, f32[64,8,256]{2,1,0:T(8,128)S(1)} %get-tuple-element.62.product, ...), custom_call_target="tpu_custom_call" | custom-call | flops 30000000 | bytes 2000000 | tf_op jit(solution)/shard_map/local/pallas_call | solution.py:388
  104.3 9.4 %all-to-all-done.states = f32[16,16,256]{2,1,0:T(8,128)S(1)} async-done(((f32[16,16,256]{2,1,0:T(8,128)}), f32[16,16,256]{2,1,0:T(8,128)S(1)}, u32[]{:S(2)}, u32[]{:S(2)}) %all-to-all-start) | async-done | bytes 262176 | tf_op jit(solution)/shard_map/state_exchange/all_to_all | solution.py:387
  113.8 1.5 %finish.1 = (bf16[256,256]{1,0:T(8,128)(2,1)S(1)}, bf16[256,256]{1,0:T(8,128)(2,1)S(1)}) custom-call(s32[5]{0:T(128)S(1)} %stack.23.refs_0_.pos, f32[64,8,256]{2,1,0:T(8,128)S(1)} %get-tuple-element.63.gate, f32[64,8,256]{2,1,0:T(8,128)S(1)} %get-tuple-element.64.local, f32[16,8,256]{2,1,0:T(8,128)S(1)} %get-tuple-element.65.inside, ...), custom_call_target="tpu_custom_call" | custom-call | tf_op jit(solution)/shard_map/finish/pallas_call | solution.py:399
  115.3 2.4 %collective-permute-start.18 = (bf16[256,256]{1,0:T(8,128)(2,1)S(1)}, bf16[256,256]{1,0:T(8,128)(2,1)S(1)}, u32[]{:S(2)}, u32[]{:S(2)}) collective-permute-start(bf16[256,256]{1,0:T(8,128)(2,1)S(1)} %get-tuple-element.68), channel_id=1, source_target_pairs={{0,8},{8,0},{1,9},{9,1},{2,10},{10,2},{3,11},{11,3},{4,12},{12,4},... | collective-permute-start | bytes 393224 | tf_op jit(solution)/shard_map/result_swap/ppermute | solution.py:409
  117.7 1.0 collective-permute-done.18
  118.7 0.7 pad_maximum_fusion.2
  (22 shorter events, 0.2 us)
Async XLA Ops:
  6.5 5.6 %copy-start.10 = (bf16[256,512]{1,0:T(8,128)(2,1)S(1)}, bf16[256,512]{1,0:T(8,128)(2,1)}, u32[]{:S(2)}) copy-start(bf16[256,512]{1,0:T(8,128)(2,1)} %param.6) | copy-start | bytes 786436
  6.5 68.9 %all-gather.3.cloned.1.call-start = ((), (), s32[]{:S(2)}) async-start(), calls=%async_computation.1 | async-start | bytes 2359296 | tf_op jit(solution)/shard_map/token_gather/all_gather | solution.py:305
  7.3 68.2 %all-gather.5.cloned.1.call-start = ((), (), s32[]{:S(2)}) async-start(), calls=%async_computation.2 | async-start | bytes 2654208 | tf_op jit(solution)/shard_map/token_gather/all_gather | solution.py:307
  8.8 4.4 %collective-permute-start = (bf16[128,768]{1,0:T(8,128)(2,1)S(1)}, bf16[128,768]{1,0:T(8,128)(2,1)S(1)}, u32[]{:S(2)}, u32[]{:S(2)}) collective-permute-start(bf16[128,768]{1,0:T(8,128)(2,1)S(1)} %bitcast.17), channel_id=1, source_target_pairs={{0,8},{8,0},{1,9},{9,1},{2,10},{10,2},{3,11},{11,3},{4,12},{12,4},... | collective-permute-start | bytes 589832 | tf_op jit(solution)/shard_map/weight_gather/ppermute | solution.py:290
  12.1 13.4 %collective-permute-start.3 = (bf16[256,512]{1,0:T(8,128)(2,1)S(1)}, bf16[256,512]{1,0:T(8,128)(2,1)S(1)}, u32[]{:S(2)}, u32[]{:S(2)}) collective-permute-start(bf16[256,512]{1,0:T(8,128)(2,1)S(1)} %copy-done.10), channel_id=1, source_target_pairs={{0,4},{4,0},{1,5},{5,1},{2,6},{6,2},{3,7},{7,3},{8,12},{12,8},{9,1... | collective-permute-start | bytes 786440 | tf_op jit(solution)/shard_map/token_swap/ppermute | solution.py:294
  13.2 9.6 %collective-permute-start.2 = (bf16[16,512]{1,0:T(8,128)(2,1)S(1)}, bf16[16,512]{1,0:T(8,128)(2,1)S(1)}, u32[]{:S(2)}, u32[]{:S(2)}) collective-permute-start(bf16[16,512]{1,0:T(8,128)(2,1)S(1)} %slice.3), channel_id=1, source_target_pairs={{8,20},{12,16},{24,36},{28,32},{40,52},{44,48},{56,68},{60,64},{72... | collective-permute-start | bytes 49160 | tf_op jit(solution)/shard_map/token_swap/ppermute | solution.py:297
  18.0 7.5 %collective-permute-start.1 = (bf16[16,512]{1,0:T(8,128)(2,1)S(1)}, bf16[16,512]{1,0:T(8,128)(2,1)S(1)}, u32[]{:S(2)}, u32[]{:S(2)}) collective-permute-start(bf16[16,512]{1,0:T(8,128)(2,1)S(1)} %slice.3), channel_id=1, source_target_pairs={{8,16},{12,20},{24,32},{28,36},{40,48},{44,52},{56,64},{60,68},{72... | collective-permute-start | bytes 49160 | tf_op jit(solution)/shard_map/token_swap/ppermute | solution.py:296
  19.3 19.1 %collective-permute-start.8 = (bf16[256,768]{1,0:T(8,128)(2,1)S(1)}, bf16[256,768]{1,0:T(8,128)(2,1)S(1)}, u32[]{:S(2)}, u32[]{:S(2)}) collective-permute-start(bf16[256,768]{1,0:T(8,128)(2,1)S(1)} %pad_maximum_fusion.refs_3_), channel_id=1, source_target_pairs={{0,48},{16,0},{32,16},{48,32},{1,49},{17,1},{33,17},{49,33},{2,50}... | collective-permute-start | bytes 1179656 | tf_op jit(solution)/shard_map/weight_rings/ppermute | solution.py:23
  21.0 18.3 %collective-permute-start.7 = (bf16[256,768]{1,0:T(8,128)(2,1)S(1)}, bf16[256,768]{1,0:T(8,128)(2,1)S(1)}, u32[]{:S(2)}, u32[]{:S(2)}) collective-permute-start(bf16[256,768]{1,0:T(8,128)(2,1)S(1)} %pad_maximum_fusion.refs_3_), channel_id=1, source_target_pairs={{0,16},{16,32},{32,48},{48,0},{1,17},{17,33},{33,49},{49,1},{2,18}... | collective-permute-start | bytes 1179656 | tf_op jit(solution)/shard_map/weight_rings/ppermute | solution.py:23
  22.8 18.6 %collective-permute-start.6 = (bf16[256,768]{1,0:T(8,128)(2,1)S(1)}, bf16[256,768]{1,0:T(8,128)(2,1)S(1)}, u32[]{:S(2)}, u32[]{:S(2)}) collective-permute-start(bf16[256,768]{1,0:T(8,128)(2,1)S(1)} %pad_maximum_fusion.refs_3_), channel_id=1, source_target_pairs={{0,192},{64,0},{128,64},{192,128},{1,193},{65,1},{129,65},{193,129... | collective-permute-start | bytes 1179656 | tf_op jit(solution)/shard_map/weight_rings/ppermute | solution.py:23
  25.5 20.2 %collective-permute-start.5 = (bf16[256,768]{1,0:T(8,128)(2,1)S(1)}, bf16[256,768]{1,0:T(8,128)(2,1)S(1)}, u32[]{:S(2)}, u32[]{:S(2)}) collective-permute-start(bf16[256,768]{1,0:T(8,128)(2,1)S(1)} %pad_maximum_fusion.refs_3_), channel_id=1, source_target_pairs={{0,64},{64,128},{128,192},{192,0},{1,65},{65,129},{129,193},{193,1... | collective-permute-start | bytes 1179656 | tf_op jit(solution)/shard_map/weight_rings/ppermute | solution.py:23
  25.5 20.2 %collective-permute-start.4 = (bf16[256,768]{1,0:T(8,128)(2,1)S(1)}, bf16[256,768]{1,0:T(8,128)(2,1)S(1)}, u32[]{:S(2)}, u32[]{:S(2)}) collective-permute-start(bf16[256,768]{1,0:T(8,128)(2,1)S(1)} %pad_maximum_fusion.refs_3_), channel_id=1, source_target_pairs={{0,128},{64,192},{128,0},{192,64},{1,129},{65,193},{129,1},{193,65... | collective-permute-start | bytes 1179656 | tf_op jit(solution)/shard_map/weight_rings/ppermute | solution.py:23
  45.7 0.9 copy-start.2
  47.5 18.9 %collective-permute-start.10 = (bf16[512,768]{1,0:T(8,128)(2,1)S(1)}, bf16[512,768]{1,0:T(8,128)(2,1)S(1)}, u32[]{:S(2)}, u32[]{:S(2)}) collective-permute-start(bf16[512,768]{1,0:T(8,128)(2,1)S(1)} %get-tuple-element.44.refs_4_), channel_id=1, source_target_pairs={{0,192},{64,0},{128,64},{192,128},{1,193},{65,1},{129,65},{193,129... | collective-permute-start | bytes 2359304 | tf_op jit(solution)/shard_map/weight_rings/ppermute | solution.py:23
  47.6 20.0 %collective-permute-start.9 = (bf16[512,768]{1,0:T(8,128)(2,1)S(1)}, bf16[512,768]{1,0:T(8,128)(2,1)S(1)}, u32[]{:S(2)}, u32[]{:S(2)}) collective-permute-start(bf16[512,768]{1,0:T(8,128)(2,1)S(1)} %get-tuple-element.44.refs_4_), channel_id=1, source_target_pairs={{0,64},{64,128},{128,192},{192,0},{1,65},{65,129},{129,193},{193,1... | collective-permute-start | bytes 2359304 | tf_op jit(solution)/shard_map/weight_rings/ppermute | solution.py:23
  49.1 9.7 %collective-permute-start.11 = (bf16[128,768]{1,0:T(8,128)(2,1)S(1)}, bf16[128,768]{1,0:T(8,128)(2,1)S(1)}, u32[]{:S(2)}, u32[]{:S(2)}) collective-permute-start(bf16[128,768]{1,0:T(8,128)(2,1)S(1)} %get-tuple-element.45), channel_id=1, source_target_pairs={{0,16},{16,32},{32,48},{48,0},{1,17},{17,33},{33,49},{49,1},{2,18}... | collective-permute-start | bytes 589832 | tf_op jit(solution)/shard_map/weight_rings/ppermute | solution.py:23
  49.7 12.8 %collective-permute-start.12 = (bf16[128,768]{1,0:T(8,128)(2,1)S(1)}, bf16[128,768]{1,0:T(8,128)(2,1)S(1)}, u32[]{:S(2)}, u32[]{:S(2)}) collective-permute-start(bf16[128,768]{1,0:T(8,128)(2,1)S(1)} %get-tuple-element.46), channel_id=1, source_target_pairs={{0,48},{16,0},{32,16},{48,32},{1,49},{17,1},{33,17},{49,33},{2,50}... | collective-permute-start | bytes 589832 | tf_op jit(solution)/shard_map/weight_rings/ppermute | solution.py:23
  69.0 16.7 %collective-permute-start.13 = (bf16[256,768]{1,0:T(8,128)(2,1)}, bf16[256,768]{1,0:T(8,128)(2,1)}, u32[]{:S(2)}, u32[]{:S(2)}) collective-permute-start(bf16[256,768]{1,0:T(8,128)(2,1)} %get-tuple-element.56), channel_id=1, source_target_pairs={{0,64},{64,128},{128,192},{192,0},{1,65},{65,129},{129,193},{193,1... | collective-permute-start | bytes 1179656 | tf_op jit(solution)/shard_map/weight_rings/ppermute | solution.py:23
  69.1 16.7 %collective-permute-start.14 = (bf16[256,768]{1,0:T(8,128)(2,1)}, bf16[256,768]{1,0:T(8,128)(2,1)}, u32[]{:S(2)}, u32[]{:S(2)}) collective-permute-start(bf16[256,768]{1,0:T(8,128)(2,1)} %get-tuple-element.57), channel_id=1, source_target_pairs={{0,192},{64,0},{128,64},{192,128},{1,193},{65,1},{129,65},{193,129... | collective-permute-start | bytes 1179656 | tf_op jit(solution)/shard_map/weight_rings/ppermute | solution.py:23
  71.8 18.1 %collective-permute-start.15 = (bf16[256,768]{1,0:T(8,128)(2,1)}, bf16[256,768]{1,0:T(8,128)(2,1)}, u32[]{:S(2)}, u32[]{:S(2)}) collective-permute-start(bf16[256,768]{1,0:T(8,128)(2,1)} %get-tuple-element.58), channel_id=1, source_target_pairs={{0,16},{16,32},{32,48},{48,0},{1,17},{17,33},{33,49},{49,1},{2,18}... | collective-permute-start | bytes 1179656 | tf_op jit(solution)/shard_map/weight_rings/ppermute | solution.py:23
  71.8 21.3 %collective-permute-start.16 = (bf16[256,768]{1,0:T(8,128)(2,1)}, bf16[256,768]{1,0:T(8,128)(2,1)}, u32[]{:S(2)}, u32[]{:S(2)}) collective-permute-start(bf16[256,768]{1,0:T(8,128)(2,1)} %get-tuple-element.59), channel_id=1, source_target_pairs={{0,48},{16,0},{32,16},{48,32},{1,49},{17,1},{33,17},{49,33},{2,50}... | collective-permute-start | bytes 1179656 | tf_op jit(solution)/shard_map/weight_rings/ppermute | solution.py:23
  75.3 17.7 %collective-permute-start.17 = (bf16[256,768]{1,0:T(8,128)(2,1)}, bf16[256,768]{1,0:T(8,128)(2,1)}, u32[]{:S(2)}, u32[]{:S(2)}) collective-permute-start(bf16[256,768]{1,0:T(8,128)(2,1)} %get-tuple-element.51.refs_5_), channel_id=1, source_target_pairs={{0,128},{64,192},{128,0},{192,64},{1,129},{65,193},{129,1},{193,65... | collective-permute-start | bytes 1179656 | tf_op jit(solution)/shard_map/weight_rings/ppermute | solution.py:23
  75.4 1.7 %copy-start = (bf16[2304,512]{1,0:T(8,128)(2,1)S(1)}, bf16[2304,512]{1,0:T(8,128)(2,1)}, u32[]{:S(2)}) copy-start(bf16[2304,512]{1,0:T(8,128)(2,1)} %all-gather.5.cloned.1.call-done.refs_2_) | copy-start | bytes 7077892
  77.1 1.6 %copy-start.1 = (bf16[2048,512]{1,0:T(8,128)(2,1)S(1)}, bf16[2048,512]{1,0:T(8,128)(2,1)}, u32[]{:S(2)}) copy-start(bf16[2048,512]{1,0:T(8,128)(2,1)} %all-gather.3.cloned.1.call-done.refs_1_) | copy-start | bytes 6291460
  78.7 1.0 copy-start.3
  79.7 13.4 %copy-start.4 = (f32[16,512]{1,0:T(8,128)S(1)}, f32[16,512]{1,0:T(8,128)}, u32[]{:S(2)}) copy-start(f32[16,512]{1,0:T(8,128)} %decay.3) | copy-start | bytes 98308
  79.7 13.4 %copy-start.7 = (f32[3,3,512]{2,1,0:T(4,128)S(1)}, f32[3,3,512]{2,1,0:T(4,128)}, u32[]{:S(2)}) copy-start(f32[3,3,512]{2,1,0:T(4,128)} %taps.1) | copy-start | bytes 55300
  93.1 8.7 %copy-start.5 = (f32[16,512]{1,0:T(8,128)S(1)}, f32[16,512]{1,0:T(8,128)}, u32[]{:S(2)}) copy-start(f32[16,512]{1,0:T(8,128)} %decay.3) | copy-start | bytes 98308
  93.1 8.7 %copy-start.6 = (f32[16,512]{1,0:T(8,128)S(1)}, f32[16,512]{1,0:T(8,128)}, u32[]{:S(2)}) copy-start(f32[16,512]{1,0:T(8,128)} %gain.3) | copy-start | bytes 98308
  93.1 8.7 %copy-start.8 = (f32[3,3,512]{2,1,0:T(4,128)S(1)}, f32[3,3,512]{2,1,0:T(4,128)}, u32[]{:S(2)}) copy-start(f32[3,3,512]{2,1,0:T(4,128)} %taps.1) | copy-start | bytes 55300
  93.1 8.7 %copy-start.9 = (f32[512]{0:T(512)S(1)}, f32[512]{0:T(512)}, u32[]{:S(2)}) copy-start(f32[512]{0:T(512)} %param.11) | copy-start | bytes 6148
  98.3 15.5 %all-to-all-start = ((f32[16,16,256]{2,1,0:T(8,128)}), f32[16,16,256]{2,1,0:T(8,128)S(1)}, u32[]{:S(2)}, u32[]{:S(2)}) async-start(f32[16,16,256]{2,1,0:T(8,128)} %get-tuple-element.66), calls=%async_computation | async-start | bytes 524288 | tf_op jit(solution)/shard_map/state_exchange/all_to_all | solution.py:387
  115.3 3.4 %collective-permute-start.18 = (bf16[256,256]{1,0:T(8,128)(2,1)S(1)}, bf16[256,256]{1,0:T(8,128)(2,1)S(1)}, u32[]{:S(2)}, u32[]{:S(2)}) collective-permute-start(bf16[256,256]{1,0:T(8,128)(2,1)S(1)} %get-tuple-element.68), channel_id=1, source_target_pairs={{0,8},{8,0},{1,9},{9,1},{2,10},{10,2},{3,11},{11,3},{4,12},{12,4},... | collective-permute-start | bytes 393224 | tf_op jit(solution)/shard_map/result_swap/ppermute | solution.py:409
Sparse Core Ops, SparseCore 0:
  9.2 31.8 all-gather.2
  46.7 25.4 all-gather.4

commit v12 on v11

--- a/solution.py
+++ b/solution.py
@@ -289,21 +289,20 @@
         mine = lax.dynamic_index_in_dim(halves, c, 0, keepdims=False)
         theirs = lax.ppermute(lax.dynamic_index_in_dim(halves, 1 - c, 0, keepdims=False), "c", SWAP)
         own = in_order(c == 0, mine, theirs, 0)
-        tail, own = tie((tokens[rows - HALO :], own))
     with jax.named_scope("token_swap"):
         other = lax.ppermute(tokens, "l", SWAP)
-        route = [(4 * r + 2 + side, 4 * r + 4 + side) for r in range(15) for side in range(2)]
-        halo = lax.ppermute(tail, (*CTX, "l"), route)
-        other_halo = lax.ppermute(tail, (*CTX, "l"), [(i, j ^ 1) for i, j in route])
     with jax.named_scope("weight_rings"):
         farther = shifted(own, "y", 2)
         far = both_ways(own, "y")
         beside = both_ways(own, "h")
-    first = (halo, other_halo, other, farther, far, beside)
-    halo, other_halo, other, farther, far, beside = tie(first)
+        other, far = tie((other, far))
+        tails = jnp.concatenate([tokens[rows - HALO :], other[rows - HALO :]], 0)
+        halos = lax.ppermute(tails, CTX, [(i, i + 1) for i in range(1, 31, 2)])
+    first = (halos, other, farther, far, beside)
+    halos, other, farther, far, beside = tie(first)
     with jax.named_scope("token_gather"):
         near = lax.all_gather(tokens, ("c", "x"), axis=0, tiled=True)
-        wide = jnp.concatenate([halo, other_halo, other], 0)
+        wide = jnp.concatenate([halos, other], 0)
         swapped = lax.all_gather(wide, ("c", "x"), axis=0, tiled=True)
     with jax.named_scope("weight_rings"):
         two, half = 2 * k, k

time: 127 us -> 122 us (0.961)
  waiting for transfers between devices: 52.9 us -> 31.6 us
  starting transfers between devices: 34.6 us -> 51.1 us
    ppermute x14, waiting for transfers between devices: 40.8 us -> 13.2 us  [shifted(): return lax.ppermute(array, axis, [(i, (i + step) % n) for i in range(n)])]
    ppermute x14, starting transfers between devices: 19.3 us -> 28.1 us  [shifted(): return lax.ppermute(array, axis, [(i, (i + step) % n) for i in range(n)])]
    all_to_all x1, starting transfers between devices: 3.53 us -> 9.28 us  [body(): states = lax.all_to_all(state, ('y', 'h'), 0, 0, tiled=True)]
    ppermute x2 -> x1, waiting for transfers between devices: 0.01 us -> 3.44 us  [body(): halos = lax.ppermute(tails, CTX, [(i, i + 1) for i in range(1, 31, 2)])]
    ppermute x1, waiting for transfers between devices: 0.01 us -> 1.95 us  [body(): other = lax.ppermute(tokens, 'l', SWAP)]
    all_gather x1, waiting for transfers between devices: 0.01 us -> 1.7 us  [body(): swapped = lax.all_gather(wide, ('c', 'x'), axis=0, tiled=True)]
    ppermute x2 -> x1, starting transfers between devices: 6.06 us -> 6.87 us  [body(): halos = lax.ppermute(tails, CTX, [(i, i + 1) for i in range(1, 31, 2)])]
  transfers between devices with their start and end apart: 22 -> 21, of which waited for: 13 -> 10; matrix products, arithmetic and copies ran while one was open for 2% -> 2% of each run, Pallas kernels for 9% -> 9%
where the time goes in v12:
time: 122 us; the launch traced here: 121 us
  starting transfers between devices  51.1 us (42%)
  waiting for transfers between devices  31.6 us (26%)
  Pallas kernels  17.5 us (14%)
  between operations  13.7 us (11%)
  local copies, waits for them, and re-layouts  5.95 us (5%)
  other arithmetic  1.53 us (1%)
    ppermute x14, starting transfers between devices, shifted(): return lax.ppermute(array, axis, [(i, (i + step) % n) for i in range(n)])  28.1 us
    ppermute x14, waiting for transfers between devices, shifted(): return lax.ppermute(array, axis, [(i, (i + step) % n) for i in range(n)])  13.2 us
    all_to_all x1, starting transfers between devices, body(): states = lax.all_to_all(state, ('y', 'h'), 0, 0, tiled=True)  9.28 us
    all_to_all x1, waiting for transfers between devices, body(): states = lax.all_to_all(state, ('y', 'h'), 0, 0, tiled=True)  8.67 us
    ppermute x1, starting transfers between devices, body(): halos = lax.ppermute(tails, CTX, [(i, i + 1) for i in range(1, 31, 2)])  6.87 us
    pallas_call x1, Pallas kernels, body(): pl.pallas_call(functools.partial(project_kernel, sizes, early_runs, late_...  6.06 us
    unnamed x23, local copies, waits for them, and re-layouts  5.5 us
    pallas_call x1, Pallas kernels, body(): pl.pallas_call(functools.partial(state_kernel, sizes), out_shape=(full, j...  5.13 us
  transfers between devices with their start and end apart: 21, of which 10 were waited for; matrix products, arithmetic and copies ran while one was open for 2% of the time, Pallas kernels for 9%

profile of v12, /device:TPU:1, one launch (start us, length us, event | category | flops | bytes accessed | tf_op | source)
XLA Modules:
  0.0 121.4 jit_solution(9057983995913011962)
XLA Ops:
  6.5 0.0 all-gather.3.cloned.1.call-start
  6.5 0.7 all-gather.3.cloned.1.call-update
  7.3 0.0 all-gather.5.cloned.1.call-start
  7.3 1.2 %copy.10 = bf16[128,3,512]{0,2,1:T(8,128)(2,1)S(1)} copy(bf16[128,3,512]{2,0,1:T(8,128)(2,1)} %param.7) | data formatting | bytes 786432 | tf_op args[1]
  8.6 0.1 copy.13
  8.8 3.3 %collective-permute-start.1 = (bf16[128,768]{1,0:T(8,128)(2,1)S(1)}, bf16[128,768]{1,0:T(8,128)(2,1)S(1)}, u32[]{:S(2)}, u32[]{:S(2)}) collective-permute-start(bf16[128,768]{1,0:T(8,128)(2,1)S(1)} %bitcast.17), channel_id=1, source_target_pairs={{0,8},{8,0},{1,9},{9,1},{2,10},{10,2},{3,11},{11,3},{4,12},{12,4},... | collective-permute-start | bytes 589832 | tf_op jit(solution)/shard_map/weight_gather/ppermute | solution.py:290
  12.1 0.0 copy-done.10
  12.1 0.0 collective-permute-start
  12.1 0.1 copy.12
  12.2 0.9 collective-permute-done.1
  13.2 1.8 %collective-permute-start.3 = (bf16[256,768]{1,0:T(8,128)(2,1)S(1)}, bf16[256,768]{1,0:T(8,128)(2,1)S(1)}, u32[]{:S(2)}, u32[]{:S(2)}) collective-permute-start(bf16[256,768]{1,0:T(8,128)(2,1)S(1)} %pad_maximum_fusion.refs_3_), channel_id=1, source_target_pairs={{0,192},{64,0},{128,64},{192,128},{1,193},{65,1},{129,65},{193,129... | collective-permute-start | bytes 1179656 | tf_op jit(solution)/shard_map/weight_rings/ppermute | solution.py:23
  15.1 0.0 collective-permute-start.2
  15.1 5.3 %collective-permute-start.7 = (bf16[256,768]{1,0:T(8,128)(2,1)S(1)}, bf16[256,768]{1,0:T(8,128)(2,1)S(1)}, u32[]{:S(2)}, u32[]{:S(2)}) collective-permute-start(bf16[256,768]{1,0:T(8,128)(2,1)S(1)} %pad_maximum_fusion.refs_3_), channel_id=1, source_target_pairs={{0,48},{16,0},{32,16},{48,32},{1,49},{17,1},{33,17},{49,33},{2,50}... | collective-permute-start | bytes 1179656 | tf_op jit(solution)/shard_map/weight_rings/ppermute | solution.py:23
  20.3 0.0 collective-permute-start.6
  20.3 1.9 %collective-permute-done = bf16[256,512]{1,0:T(8,128)(2,1)S(1)} collective-permute-done((bf16[256,512]{1,0:T(8,128)(2,1)S(1)}, bf16[256,512]{1,0:T(8,128)(2,1)S(1)}, u32[]{:S(2)}, u32[]{:S(2)}) %collective-permute-start) | collective-permute-done | bytes 262176 | tf_op jit(solution)/shard_map/token_swap/ppermute | solution.py:293
  22.3 7.6 %collective-permute-start.5 = (bf16[256,768]{1,0:T(8,128)(2,1)S(1)}, bf16[256,768]{1,0:T(8,128)(2,1)S(1)}, u32[]{:S(2)}, u32[]{:S(2)}) collective-permute-start(bf16[256,768]{1,0:T(8,128)(2,1)S(1)} %pad_maximum_fusion.refs_3_), channel_id=1, source_target_pairs={{0,128},{64,192},{128,0},{192,64},{1,129},{65,193},{129,1},{193,65... | collective-permute-start | bytes 1179656 | tf_op jit(solution)/shard_map/weight_rings/ppermute | solution.py:23
  29.9 0.0 collective-permute-done.3.refs_8_
  29.9 0.0 collective-permute-done.2.refs_6_
  29.9 6.9 %collective-permute-start.4 = (bf16[32,512]{1,0:T(8,128)(2,1)S(1)}, bf16[32,512]{1,0:T(8,128)(2,1)S(1)}, u32[]{:S(2)}, u32[]{:S(2)}) collective-permute-start(bf16[32,512]{1,0:T(8,128)(2,1)S(1)} %pad_maximum_fusion.3), channel_id=1, source_target_pairs={{8,16},{24,32},{40,48},{56,64},{72,80},{88,96},{104,112},{120,128}... | collective-permute-start | bytes 98312 | tf_op jit(solution)/shard_map/weight_rings/ppermute | solution.py:300
  36.8 0.0 collective-permute-done.7.refs_1_
  36.8 0.0 collective-permute-done.6.refs_0_
  36.8 0.5 collective-permute-done.5.refs_10_
  37.3 3.4 %collective-permute-done.4 = bf16[32,512]{1,0:T(8,128)(2,1)S(1)} collective-permute-done((bf16[32,512]{1,0:T(8,128)(2,1)S(1)}, bf16[32,512]{1,0:T(8,128)(2,1)S(1)}, u32[]{:S(2)}, u32[]{:S(2)}) %collective-permute-start.4) | collective-permute-done | bytes 32800 | tf_op jit(solution)/shard_map/weight_rings/ppermute | solution.py:300
  40.7 0.7 pad_maximum_fusion.1
  41.5 0.0 all-gather.5.cloned.1.call-update
  41.5 0.9 relay_pair.1
  42.4 0.1 collective-permute-start.9
  42.5 1.5 %collective-permute-start.8 = (bf16[512,768]{1,0:T(8,128)(2,1)S(1)}, bf16[512,768]{1,0:T(8,128)(2,1)S(1)}, u32[]{:S(2)}, u32[]{:S(2)}) collective-permute-start(bf16[512,768]{1,0:T(8,128)(2,1)S(1)} %get-tuple-element.44.refs_4_), channel_id=1, source_target_pairs={{0,64},{64,128},{128,192},{192,0},{1,65},{65,129},{129,193},{193,1... | collective-permute-start | bytes 2359304 | tf_op jit(solution)/shard_map/weight_rings/ppermute | solution.py:23
  44.1 0.4 collective-permute-start.10
  44.5 3.2 %collective-permute-start.11 = (bf16[128,768]{1,0:T(8,128)(2,1)S(1)}, bf16[128,768]{1,0:T(8,128)(2,1)S(1)}, u32[]{:S(2)}, u32[]{:S(2)}) collective-permute-start(bf16[128,768]{1,0:T(8,128)(2,1)S(1)} %get-tuple-element.46), channel_id=1, source_target_pairs={{0,48},{16,0},{32,16},{48,32},{1,49},{17,1},{33,17},{49,33},{2,50}... | collective-permute-start | bytes 589832 | tf_op jit(solution)/shard_map/weight_rings/ppermute | solution.py:23
  47.6 3.1 %collective-permute-done.10.refs_2_ = bf16[128,768]{1,0:T(8,128)(2,1)S(1)} collective-permute-done((bf16[128,768]{1,0:T(8,128)(2,1)S(1)}, bf16[128,768]{1,0:T(8,128)(2,1)S(1)}, u32[]{:S(2)}, u32[]{:S(2)}) %collective-permute-start.10) | collective-permute-done | bytes 196640 | tf_op jit(solution)/shard_map/weight_rings/ppermute | solution.py:23
  50.8 0.2 collective-permute-done.11.refs_3_
  51.0 9.4 %collective-permute-done.9.refs_1_.refs_9_ = bf16[512,768]{1,0:T(8,128)(2,1)S(1)} collective-permute-done((bf16[512,768]{1,0:T(8,128)(2,1)S(1)}, bf16[512,768]{1,0:T(8,128)(2,1)S(1)}, u32[]{:S(2)}, u32[]{:S(2)}) %collective-permute-start.9) | collective-permute-done | bytes 786464 | tf_op jit(solution)/shard_map/weight_rings/ppermute | solution.py:23
  60.4 0.0 collective-permute-done.8.refs_0_.refs_7_
  60.4 1.4 %relay_far.1 = (bf16[256,768]{1,0:T(8,128)(2,1)}, bf16[256,768]{1,0:T(8,128)(2,1)}, bf16[256,768]{1,0:T(8,128)(2,1)}, bf16[256,768]{1,0:T(8,128)(2,1)}, bf16[256,768]{1,0:T(8,128)(2,1)}) custom-call(bf16[512,768]{1,0:T(8,128)(2,1)S(1)} %collective-permute-done.8.refs_0_.refs_7_, bf16[512,768]{1,0:T(8,128)(2,1)S(1)} %collective-permute-done.9.refs_1_.refs_9_, ...), custom_call_target="tpu_custom_call" | custom-call | bytes 2000000 | tf_op jit(solution)/shard_map/weight_rings/relay_far/pallas_call | solution.py:54
  61.7 1.6 %collective-permute-start.12 = (bf16[256,768]{1,0:T(8,128)(2,1)}, bf16[256,768]{1,0:T(8,128)(2,1)}, u32[]{:S(2)}, u32[]{:S(2)}) collective-permute-start(bf16[256,768]{1,0:T(8,128)(2,1)} %get-tuple-element.56), channel_id=1, source_target_pairs={{0,64},{64,128},{128,192},{192,0},{1,65},{65,129},{129,193},{193,1... | collective-permute-start | bytes 1179656 | tf_op jit(solution)/shard_map/weight_rings/ppermute | solution.py:23
  63.3 1.6 %collective-permute-start.13 = (bf16[256,768]{1,0:T(8,128)(2,1)}, bf16[256,768]{1,0:T(8,128)(2,1)}, u32[]{:S(2)}, u32[]{:S(2)}) collective-permute-start(bf16[256,768]{1,0:T(8,128)(2,1)} %get-tuple-element.57), channel_id=1, source_target_pairs={{0,192},{64,0},{128,64},{192,128},{1,193},{65,1},{129,65},{193,129... | collective-permute-start | bytes 1179656 | tf_op jit(solution)/shard_map/weight_rings/ppermute | solution.py:23
  64.9 2.4 %collective-permute-start.14 = (bf16[256,768]{1,0:T(8,128)(2,1)}, bf16[256,768]{1,0:T(8,128)(2,1)}, u32[]{:S(2)}, u32[]{:S(2)}) collective-permute-start(bf16[256,768]{1,0:T(8,128)(2,1)} %get-tuple-element.58), channel_id=1, source_target_pairs={{0,16},{16,32},{32,48},{48,0},{1,17},{17,33},{33,49},{49,1},{2,18}... | collective-permute-start | bytes 1179656 | tf_op jit(solution)/shard_map/weight_rings/ppermute | solution.py:23
  67.3 1.2 %collective-permute-start.15 = (bf16[256,768]{1,0:T(8,128)(2,1)}, bf16[256,768]{1,0:T(8,128)(2,1)}, u32[]{:S(2)}, u32[]{:S(2)}) collective-permute-start(bf16[256,768]{1,0:T(8,128)(2,1)} %get-tuple-element.59), channel_id=1, source_target_pairs={{0,48},{16,0},{32,16},{48,32},{1,49},{17,1},{33,17},{49,33},{2,50}... | collective-permute-start | bytes 1179656 | tf_op jit(solution)/shard_map/weight_rings/ppermute | solution.py:23
  68.5 1.4 %collective-permute-start.16 = (bf16[256,768]{1,0:T(8,128)(2,1)}, bf16[256,768]{1,0:T(8,128)(2,1)}, u32[]{:S(2)}, u32[]{:S(2)}) collective-permute-start(bf16[256,768]{1,0:T(8,128)(2,1)} %get-tuple-element.51.refs_5_), channel_id=1, source_target_pairs={{0,128},{64,192},{128,0},{192,64},{1,129},{65,193},{129,1},{193,65... | collective-permute-start | bytes 1179656 | tf_op jit(solution)/shard_map/weight_rings/ppermute | solution.py:23
  69.9 0.1 stack.23.refs_0_.pos
  70.0 1.7 %all-gather.5.cloned.1.call-done.refs_2_ = bf16[2304,512]{1,0:T(8,128)(2,1)} async-done(((bf16[288,512]{1,0:T(8,128)(2,1)}), bf16[2304,512]{1,0:T(8,128)(2,1)}) %all-gather.5.cloned.1.call-update) | async-done | bytes 2359312 | tf_op jit(solution)/shard_map/token_gather/all_gather | solution.py:306
  71.7 1.7 %copy-done = bf16[2304,512]{1,0:T(8,128)(2,1)S(1)} copy-done((bf16[2304,512]{1,0:T(8,128)(2,1)S(1)}, bf16[2304,512]{1,0:T(8,128)(2,1)}, u32[]{:S(2)}) %copy-start) | copy-done | bytes 2359320
  73.4 1.6 %copy-done.1 = bf16[2048,512]{1,0:T(8,128)(2,1)S(1)} copy-done((bf16[2048,512]{1,0:T(8,128)(2,1)S(1)}, bf16[2048,512]{1,0:T(8,128)(2,1)}, u32[]{:S(2)}) %copy-start.1) | copy-done | bytes 2097176
  74.9 1.0 copy-done.3
  75.9 6.1 %project.1 = (f32[6,528,128]{2,1,0:T(8,128)S(1)}, bf16[528,1280]{1,0:T(8,128)(2,1)S(1)}) custom-call(s32[5]{0:T(128)S(1)} %stack.23.refs_0_.pos, bf16[2048,512]{1,0:T(8,128)(2,1)S(1)} %copy-done.1, bf16[2304,512]{1,0:T(8,128)(2,1)S(1)} %copy-done, bf16[256,768]{1,0:T(8,128)(2,1)S(1)} %pad_maximum_fusion.refs_3_, ...), custom_call_target="tpu_custom_call" | custom-call | flops 2283798528 | bytes 9000000 | tf_op jit(solution)/shard_map/project/pallas_call | solution.py:346
  82.0 0.0 collective-permute-done.12.refs_2_
  82.0 0.0 collective-permute-done.13.refs_3_
  82.0 0.0 collective-permute-done.14.refs_4_
  82.0 0.0 collective-permute-done.15.refs_5_
  82.1 0.0 collective-permute-done.16.refs_6_
  82.1 0.0 copy-done.4
  82.1 0.0 copy-start.5
  82.1 0.0 copy-start.6
  82.1 0.0 copy-start.8
  82.1 0.0 copy-start.9
  82.1 5.1 %states.1 = (f32[64,8,256]{2,1,0:T(8,128)S(1)}, f32[2,528,128]{2,1,0:T(8,128)S(1)}, f32[16,16,256]{2,1,0:T(8,128)}) custom-call(s32[5]{0:T(128)S(1)} %stack.23.refs_0_.pos, bf16[528,1280]{1,0:T(8,128)(2,1)S(1)} %get-tuple-element.55.refs_1_, bf16[256,768]{1,0:T(8,128)(2,1)} %collective-permute-done.12.refs_2_, ...), custom_call_target="tpu_custom_call" | custom-call | tf_op jit(solution)/shard_map/states/pallas_call | solution.py:368
  87.3 9.3 %all-to-all-start = ((f32[16,16,256]{2,1,0:T(8,128)}), f32[16,16,256]{2,1,0:T(8,128)S(1)}, u32[]{:S(2)}, u32[]{:S(2)}) async-start(f32[16,16,256]{2,1,0:T(8,128)} %get-tuple-element.66), calls=%async_computation | async-start | bytes 524288 | tf_op jit(solution)/shard_map/state_exchange/all_to_all | solution.py:386
  96.6 2.5 %local.1 = (f32[64,8,256]{2,1,0:T(8,128)S(1)}, f32[64,8,256]{2,1,0:T(8,128)S(1)}, f32[16,8,256]{2,1,0:T(8,128)S(1)}) custom-call(s32[5]{0:T(128)S(1)} %stack.23.refs_0_.pos, f32[2,528,128]{2,1,0:T(8,128)S(1)} %get-tuple-element.61.gated, f32[3,3,512]{2,1,0:T(4,128)S(1)} %copy-done.8, f32[64,8,256]{2,1,0:T(8,128)S(1)} %get-tuple-element.62.product, ...), custom_call_target="tpu_custom_call" | custom-call | flops 30000000 | bytes 2000000 | tf_op jit(solution)/shard_map/local/pallas_call | solution.py:387
  99.1 8.7 %all-to-all-done.states = f32[16,16,256]{2,1,0:T(8,128)S(1)} async-done(((f32[16,16,256]{2,1,0:T(8,128)}), f32[16,16,256]{2,1,0:T(8,128)S(1)}, u32[]{:S(2)}, u32[]{:S(2)}) %all-to-all-start) | async-done | bytes 262176 | tf_op jit(solution)/shard_map/state_exchange/all_to_all | solution.py:386
  107.7 1.5 %finish.1 = (bf16[256,256]{1,0:T(8,128)(2,1)S(1)}, bf16[256,256]{1,0:T(8,128)(2,1)S(1)}) custom-call(s32[5]{0:T(128)S(1)} %stack.23.refs_0_.pos, f32[64,8,256]{2,1,0:T(8,128)S(1)} %get-tuple-element.63.gate, f32[64,8,256]{2,1,0:T(8,128)S(1)} %get-tuple-element.64.local, f32[16,8,256]{2,1,0:T(8,128)S(1)} %get-tuple-element.65.inside, ...), custom_call_target="tpu_custom_call" | custom-call | tf_op jit(solution)/shard_map/finish/pallas_call | solution.py:398
  109.3 3.5 %collective-permute-start.17 = (bf16[256,256]{1,0:T(8,128)(2,1)S(1)}, bf16[256,256]{1,0:T(8,128)(2,1)S(1)}, u32[]{:S(2)}, u32[]{:S(2)}) collective-permute-start(bf16[256,256]{1,0:T(8,128)(2,1)S(1)} %get-tuple-element.68), channel_id=1, source_target_pairs={{0,8},{8,0},{1,9},{9,1},{2,10},{10,2},{3,11},{11,3},{4,12},{12,4},... | collective-permute-start | bytes 393224 | tf_op jit(solution)/shard_map/result_swap/ppermute | solution.py:408
  112.8 1.0 collective-permute-done.17
  113.8 0.7 pad_maximum_fusion.2
  (22 shorter events, 0.2 us)
Async XLA Ops:
  6.5 5.6 %copy-start.10 = (bf16[256,512]{1,0:T(8,128)(2,1)S(1)}, bf16[256,512]{1,0:T(8,128)(2,1)}, u32[]{:S(2)}) copy-start(bf16[256,512]{1,0:T(8,128)(2,1)} %param.6) | copy-start | bytes 786436
  6.5 63.4 %all-gather.3.cloned.1.call-start = ((), (), s32[]{:S(2)}) async-start(), calls=%async_computation.1 | async-start | bytes 2359296 | tf_op jit(solution)/shard_map/token_gather/all_gather | solution.py:304
  7.3 64.4 %all-gather.5.cloned.1.call-start = ((), (), s32[]{:S(2)}) async-start(), calls=%async_computation.2 | async-start | bytes 2654208 | tf_op jit(solution)/shard_map/token_gather/all_gather | solution.py:306
  8.8 4.4 %collective-permute-start.1 = (bf16[128,768]{1,0:T(8,128)(2,1)S(1)}, bf16[128,768]{1,0:T(8,128)(2,1)S(1)}, u32[]{:S(2)}, u32[]{:S(2)}) collective-permute-start(bf16[128,768]{1,0:T(8,128)(2,1)S(1)} %bitcast.17), channel_id=1, source_target_pairs={{0,8},{8,0},{1,9},{9,1},{2,10},{10,2},{3,11},{11,3},{4,12},{12,4},... | collective-permute-start | bytes 589832 | tf_op jit(solution)/shard_map/weight_gather/ppermute | solution.py:290
  12.1 10.2 %collective-permute-start = (bf16[256,512]{1,0:T(8,128)(2,1)S(1)}, bf16[256,512]{1,0:T(8,128)(2,1)S(1)}, u32[]{:S(2)}, u32[]{:S(2)}) collective-permute-start(bf16[256,512]{1,0:T(8,128)(2,1)S(1)} %copy-done.10), channel_id=1, source_target_pairs={{0,4},{4,0},{1,5},{5,1},{2,6},{6,2},{3,7},{7,3},{8,12},{12,8},{9,1... | collective-permute-start | bytes 786440 | tf_op jit(solution)/shard_map/token_swap/ppermute | solution.py:293
  13.2 16.7 %collective-permute-start.3 = (bf16[256,768]{1,0:T(8,128)(2,1)S(1)}, bf16[256,768]{1,0:T(8,128)(2,1)S(1)}, u32[]{:S(2)}, u32[]{:S(2)}) collective-permute-start(bf16[256,768]{1,0:T(8,128)(2,1)S(1)} %pad_maximum_fusion.refs_3_), channel_id=1, source_target_pairs={{0,192},{64,0},{128,64},{192,128},{1,193},{65,1},{129,65},{193,129... | collective-permute-start | bytes 1179656 | tf_op jit(solution)/shard_map/weight_rings/ppermute | solution.py:23
  15.1 14.8 %collective-permute-start.2 = (bf16[256,768]{1,0:T(8,128)(2,1)S(1)}, bf16[256,768]{1,0:T(8,128)(2,1)S(1)}, u32[]{:S(2)}, u32[]{:S(2)}) collective-permute-start(bf16[256,768]{1,0:T(8,128)(2,1)S(1)} %pad_maximum_fusion.refs_3_), channel_id=1, source_target_pairs={{0,64},{64,128},{128,192},{192,0},{1,65},{65,129},{129,193},{193,1... | collective-permute-start | bytes 1179656 | tf_op jit(solution)/shard_map/weight_rings/ppermute | solution.py:23
  15.1 21.7 %collective-permute-start.7 = (bf16[256,768]{1,0:T(8,128)(2,1)S(1)}, bf16[256,768]{1,0:T(8,128)(2,1)S(1)}, u32[]{:S(2)}, u32[]{:S(2)}) collective-permute-start(bf16[256,768]{1,0:T(8,128)(2,1)S(1)} %pad_maximum_fusion.refs_3_), channel_id=1, source_target_pairs={{0,48},{16,0},{32,16},{48,32},{1,49},{17,1},{33,17},{49,33},{2,50}... | collective-permute-start | bytes 1179656 | tf_op jit(solution)/shard_map/weight_rings/ppermute | solution.py:23
  20.3 16.5 %collective-permute-start.6 = (bf16[256,768]{1,0:T(8,128)(2,1)S(1)}, bf16[256,768]{1,0:T(8,128)(2,1)S(1)}, u32[]{:S(2)}, u32[]{:S(2)}) collective-permute-start(bf16[256,768]{1,0:T(8,128)(2,1)S(1)} %pad_maximum_fusion.refs_3_), channel_id=1, source_target_pairs={{0,16},{16,32},{32,48},{48,0},{1,17},{17,33},{33,49},{49,1},{2,18}... | collective-permute-start | bytes 1179656 | tf_op jit(solution)/shard_map/weight_rings/ppermute | solution.py:23
  22.3 15.0 %collective-permute-start.5 = (bf16[256,768]{1,0:T(8,128)(2,1)S(1)}, bf16[256,768]{1,0:T(8,128)(2,1)S(1)}, u32[]{:S(2)}, u32[]{:S(2)}) collective-permute-start(bf16[256,768]{1,0:T(8,128)(2,1)S(1)} %pad_maximum_fusion.refs_3_), channel_id=1, source_target_pairs={{0,128},{64,192},{128,0},{192,64},{1,129},{65,193},{129,1},{193,65... | collective-permute-start | bytes 1179656 | tf_op jit(solution)/shard_map/weight_rings/ppermute | solution.py:23
  29.9 10.8 %collective-permute-start.4 = (bf16[32,512]{1,0:T(8,128)(2,1)S(1)}, bf16[32,512]{1,0:T(8,128)(2,1)S(1)}, u32[]{:S(2)}, u32[]{:S(2)}) collective-permute-start(bf16[32,512]{1,0:T(8,128)(2,1)S(1)} %pad_maximum_fusion.3), channel_id=1, source_target_pairs={{8,16},{24,32},{40,48},{56,64},{72,80},{88,96},{104,112},{120,128}... | collective-permute-start | bytes 98312 | tf_op jit(solution)/shard_map/weight_rings/ppermute | solution.py:300
  37.3 4.2 %copy-start.2 = (bf16[256,768]{1,0:T(8,128)(2,1)}, bf16[256,768]{1,0:T(8,128)(2,1)S(1)}, u32[]{:S(2)}) copy-start(bf16[256,768]{1,0:T(8,128)(2,1)S(1)} %collective-permute-done.5.refs_10_) | copy-start | bytes 1179652
  42.4 17.9 %collective-permute-start.9 = (bf16[512,768]{1,0:T(8,128)(2,1)S(1)}, bf16[512,768]{1,0:T(8,128)(2,1)S(1)}, u32[]{:S(2)}, u32[]{:S(2)}) collective-permute-start(bf16[512,768]{1,0:T(8,128)(2,1)S(1)} %get-tuple-element.44.refs_4_), channel_id=1, source_target_pairs={{0,192},{64,0},{128,64},{192,128},{1,193},{65,1},{129,65},{193,129... | collective-permute-start | bytes 2359304 | tf_op jit(solution)/shard_map/weight_rings/ppermute | solution.py:23
  42.5 17.9 %collective-permute-start.8 = (bf16[512,768]{1,0:T(8,128)(2,1)S(1)}, bf16[512,768]{1,0:T(8,128)(2,1)S(1)}, u32[]{:S(2)}, u32[]{:S(2)}) collective-permute-start(bf16[512,768]{1,0:T(8,128)(2,1)S(1)} %get-tuple-element.44.refs_4_), channel_id=1, source_target_pairs={{0,64},{64,128},{128,192},{192,0},{1,65},{65,129},{129,193},{193,1... | collective-permute-start | bytes 2359304 | tf_op jit(solution)/shard_map/weight_rings/ppermute | solution.py:23
  44.1 6.7 %collective-permute-start.10 = (bf16[128,768]{1,0:T(8,128)(2,1)S(1)}, bf16[128,768]{1,0:T(8,128)(2,1)S(1)}, u32[]{:S(2)}, u32[]{:S(2)}) collective-permute-start(bf16[128,768]{1,0:T(8,128)(2,1)S(1)} %get-tuple-element.45), channel_id=1, source_target_pairs={{0,16},{16,32},{32,48},{48,0},{1,17},{17,33},{33,49},{49,1},{2,18}... | collective-permute-start | bytes 589832 | tf_op jit(solution)/shard_map/weight_rings/ppermute | solution.py:23
  44.5 6.5 %collective-permute-start.11 = (bf16[128,768]{1,0:T(8,128)(2,1)S(1)}, bf16[128,768]{1,0:T(8,128)(2,1)S(1)}, u32[]{:S(2)}, u32[]{:S(2)}) collective-permute-start(bf16[128,768]{1,0:T(8,128)(2,1)S(1)} %get-tuple-element.46), channel_id=1, source_target_pairs={{0,48},{16,0},{32,16},{48,32},{1,49},{17,1},{33,17},{49,33},{2,50}... | collective-permute-start | bytes 589832 | tf_op jit(solution)/shard_map/weight_rings/ppermute | solution.py:23
  61.7 20.3 %collective-permute-start.12 = (bf16[256,768]{1,0:T(8,128)(2,1)}, bf16[256,768]{1,0:T(8,128)(2,1)}, u32[]{:S(2)}, u32[]{:S(2)}) collective-permute-start(bf16[256,768]{1,0:T(8,128)(2,1)} %get-tuple-element.56), channel_id=1, source_target_pairs={{0,64},{64,128},{128,192},{192,0},{1,65},{65,129},{129,193},{193,1... | collective-permute-start | bytes 1179656 | tf_op jit(solution)/shard_map/weight_rings/ppermute | solution.py:23
  63.3 18.7 %collective-permute-start.13 = (bf16[256,768]{1,0:T(8,128)(2,1)}, bf16[256,768]{1,0:T(8,128)(2,1)}, u32[]{:S(2)}, u32[]{:S(2)}) collective-permute-start(bf16[256,768]{1,0:T(8,128)(2,1)} %get-tuple-element.57), channel_id=1, source_target_pairs={{0,192},{64,0},{128,64},{192,128},{1,193},{65,1},{129,65},{193,129... | collective-permute-start | bytes 1179656 | tf_op jit(solution)/shard_map/weight_rings/ppermute | solution.py:23
  64.9 17.1 %collective-permute-start.14 = (bf16[256,768]{1,0:T(8,128)(2,1)}, bf16[256,768]{1,0:T(8,128)(2,1)}, u32[]{:S(2)}, u32[]{:S(2)}) collective-permute-start(bf16[256,768]{1,0:T(8,128)(2,1)} %get-tuple-element.58), channel_id=1, source_target_pairs={{0,16},{16,32},{32,48},{48,0},{1,17},{17,33},{33,49},{49,1},{2,18}... | collective-permute-start | bytes 1179656 | tf_op jit(solution)/shard_map/weight_rings/ppermute | solution.py:23
  67.3 14.7 %collective-permute-start.15 = (bf16[256,768]{1,0:T(8,128)(2,1)}, bf16[256,768]{1,0:T(8,128)(2,1)}, u32[]{:S(2)}, u32[]{:S(2)}) collective-permute-start(bf16[256,768]{1,0:T(8,128)(2,1)} %get-tuple-element.59), channel_id=1, source_target_pairs={{0,48},{16,0},{32,16},{48,32},{1,49},{17,1},{33,17},{49,33},{2,50}... | collective-permute-start | bytes 1179656 | tf_op jit(solution)/shard_map/weight_rings/ppermute | solution.py:23
  68.5 13.5 %collective-permute-start.16 = (bf16[256,768]{1,0:T(8,128)(2,1)}, bf16[256,768]{1,0:T(8,128)(2,1)}, u32[]{:S(2)}, u32[]{:S(2)}) collective-permute-start(bf16[256,768]{1,0:T(8,128)(2,1)} %get-tuple-element.51.refs_5_), channel_id=1, source_target_pairs={{0,128},{64,192},{128,0},{192,64},{1,129},{65,193},{129,1},{193,65... | collective-permute-start | bytes 1179656 | tf_op jit(solution)/shard_map/weight_rings/ppermute | solution.py:23
  71.7 1.7 %copy-start = (bf16[2304,512]{1,0:T(8,128)(2,1)S(1)}, bf16[2304,512]{1,0:T(8,128)(2,1)}, u32[]{:S(2)}) copy-start(bf16[2304,512]{1,0:T(8,128)(2,1)} %all-gather.5.cloned.1.call-done.refs_2_) | copy-start | bytes 7077892
  73.4 1.6 %copy-start.1 = (bf16[2048,512]{1,0:T(8,128)(2,1)S(1)}, bf16[2048,512]{1,0:T(8,128)(2,1)}, u32[]{:S(2)}) copy-start(bf16[2048,512]{1,0:T(8,128)(2,1)} %all-gather.3.cloned.1.call-done.refs_1_) | copy-start | bytes 6291460
  74.9 1.0 copy-start.3
  75.9 6.1 %copy-start.4 = (f32[16,512]{1,0:T(8,128)S(1)}, f32[16,512]{1,0:T(8,128)}, u32[]{:S(2)}) copy-start(f32[16,512]{1,0:T(8,128)} %decay.3) | copy-start | bytes 98308
  75.9 6.1 %copy-start.7 = (f32[3,3,512]{2,1,0:T(4,128)S(1)}, f32[3,3,512]{2,1,0:T(4,128)}, u32[]{:S(2)}) copy-start(f32[3,3,512]{2,1,0:T(4,128)} %taps.1) | copy-start | bytes 55300
  82.1 14.5 %copy-start.5 = (f32[16,512]{1,0:T(8,128)S(1)}, f32[16,512]{1,0:T(8,128)}, u32[]{:S(2)}) copy-start(f32[16,512]{1,0:T(8,128)} %decay.3) | copy-start | bytes 98308
  82.1 14.5 %copy-start.6 = (f32[16,512]{1,0:T(8,128)S(1)}, f32[16,512]{1,0:T(8,128)}, u32[]{:S(2)}) copy-start(f32[16,512]{1,0:T(8,128)} %gain.3) | copy-start | bytes 98308
  82.1 14.5 %copy-start.8 = (f32[3,3,512]{2,1,0:T(4,128)S(1)}, f32[3,3,512]{2,1,0:T(4,128)}, u32[]{:S(2)}) copy-start(f32[3,3,512]{2,1,0:T(4,128)} %taps.1) | copy-start | bytes 55300
  82.1 14.5 %copy-start.9 = (f32[512]{0:T(512)S(1)}, f32[512]{0:T(512)}, u32[]{:S(2)}) copy-start(f32[512]{0:T(512)} %param.11) | copy-start | bytes 6148
  87.3 20.5 %all-to-all-start = ((f32[16,16,256]{2,1,0:T(8,128)}), f32[16,16,256]{2,1,0:T(8,128)S(1)}, u32[]{:S(2)}, u32[]{:S(2)}) async-start(f32[16,16,256]{2,1,0:T(8,128)} %get-tuple-element.66), calls=%async_computation | async-start | bytes 524288 | tf_op jit(solution)/shard_map/state_exchange/all_to_all | solution.py:386
  109.3 4.5 %collective-permute-start.17 = (bf16[256,256]{1,0:T(8,128)(2,1)S(1)}, bf16[256,256]{1,0:T(8,128)(2,1)S(1)}, u32[]{:S(2)}, u32[]{:S(2)}) collective-permute-start(bf16[256,256]{1,0:T(8,128)(2,1)S(1)} %get-tuple-element.68), channel_id=1, source_target_pairs={{0,8},{8,0},{1,9},{9,1},{2,10},{10,2},{3,11},{11,3},{4,12},{12,4},... | collective-permute-start | bytes 393224 | tf_op jit(solution)/shard_map/result_swap/ppermute | solution.py:408
Sparse Core Ops, SparseCore 0:
  9.2 31.8 all-gather.2
  43.0 28.6 all-gather.4

commit v13 on v12

--- a/solution.py
+++ b/solution.py
@@ -160,8 +160,8 @@
 
 def state_kernel(sizes, *refs):
     rows, depth, width, modes, seq = sizes
-    pos, late_tok, *pieces = refs[:-8]
-    sums, taps, decay, product, gated, states_out, acc, state = refs[-8:]
+    pos, late_tok, *pieces = refs[:-7]
+    sums, taps, decay, product, gated, state, acc = refs[-7:]
     c = pos[3]
     late_products(sizes, (0, 1), late_tok, pieces, sums, gated)
     late_products(sizes, (1, 3), late_tok, pieces, sums, acc)
@@ -189,8 +189,6 @@
         for m in range(modes):
             total = jnp.sum(jnp.exp(-rates[m] * left) * states[m], axis=0, keepdims=True)
             state[m : m + 1, lanes] = total
-    for r in range(16):
-        states_out[r] = state[...]
 
 
 def local_kernel(sizes, pos, gated, taps, product, gain, decay, skip, gate, local, inside):
@@ -236,18 +234,36 @@
             inside[m, :, lanes] = later(s, 1)
 
 
-def finish_kernel(sizes, pos, gate, local, inside, states, gain, decay, mine_out, their_out, start, whole):
-    rows, depth, width, modes, seq = sizes
-    rank, c = pos[0], pos[3]
+def combine_kernel(sizes, pos, *refs):
+    rows, depth, width, modes, seq = sizes
+    *states, decay, inner, total = refs
+    h, c = pos[2], pos[3]
+    rate = decay[:, pl.ds(pl.multiple_of(c * width, width), width)] / seq * float(2 * rows)
+    entering = jnp.zeros((modes, width), F32)
+    left = jnp.zeros((modes, width), F32)
+    for d, state in enumerate(states):
+        after = (3 - lax.rem(h - d + 4, 4)).astype(F32)
+        left += jnp.exp(-rate * after) * state[...]
+        if d > 0:
+            entering += jnp.where(d <= h, jnp.exp(-rate * float(d - 1)) * state[...], 0.0)
+    inner[...] = entering
+    total[...] = left
+
+
+def finish_kernel(sizes, pos, gate, local, inside, inner, *refs):
+    rows, depth, width, modes, seq = sizes
+    *totals, gain, decay, mine_out, their_out, start, whole = refs
+    h, c = pos[2], pos[3]
     steps = 2 * rows // SUB
     length = 2 * rows
     for lh in range(width // 128):
         mine = pl.ds(pl.multiple_of(c * width + lh * 128, 128), 128)
         lanes = pl.ds(lh * 128, 128)
-        over = jnp.exp(-float(length) * (decay[:, mine] / seq))
-        entering = jnp.zeros((modes, 128), F32)
-        for r in range(16):
-            entering = jnp.where(r < rank, over * entering + states[r, :, lanes], entering)
+        over = decay[:, mine] / seq * float(length)
+        outer = jnp.zeros((modes, 128), F32)
+        for d, total in enumerate(totals):
+            outer += jnp.exp(-over * float(4 * d)) * total[:, lanes]
+        entering = inner[:, lanes] + jnp.exp(-over * h.astype(F32)) * outer
         start[:, lanes] = entering
         line = lax.broadcasted_iota(jnp.int32, (SUB, 128), 0).astype(F32) * float(steps)
         factors, waves = [], []
@@ -370,20 +386,28 @@
         out_shape=(
             full,
             jax.ShapeDtypeStruct((width // 128, lines, 128), F32),
-            jax.ShapeDtypeStruct((16, modes, width), F32),
+            jax.ShapeDtypeStruct((modes, width), F32),
         ),
         in_specs=[smem] + [vmem] * (4 + len(late)),
         out_specs=(vmem,) * 3,
-        scratch_shapes=[
-            pltpu.VMEM((2 * width // 128, lines, 128), F32),
-            pltpu.VMEM((modes, width), F32),
-        ],
+        scratch_shapes=[pltpu.VMEM((2 * width // 128, lines, 128), F32)],
         compiler_params=params,
         name="states",
     )(pos, late_tok, *late, sums, taps, decay)
 
     with jax.named_scope("state_exchange"):
-        states = lax.all_to_all(state, ("y", "h"), 0, 0, tiled=True)
+        states = [state, *(shifted(state, "h", d) for d in (1, 2, 3))]
+        inner, total = pl.pallas_call(
+            functools.partial(combine_kernel, sizes),
+            out_shape=(jax.ShapeDtypeStruct((modes, width), F32),) * 2,
+            in_specs=[smem] + [vmem] * 5,
+            out_specs=(vmem, vmem),
+            compiler_params=params,
+            name="combine",
+        )(pos, *states, decay)
+        totals = [
+            lax.ppermute(total, "y", [(i, i + d) for i in range(4 - d)]) for d in (1, 2, 3)
+        ]
     gate, local, inside = pl.pallas_call(
         functools.partial(local_kernel, sizes),
         out_shape=(full, full, jax.ShapeDtypeStruct((modes, SUB, width), F32)),
@@ -398,12 +422,12 @@
     mine, theirs = pl.pallas_call(
         functools.partial(finish_kernel, sizes),
         out_shape=(jax.ShapeDtypeStruct((rows, width), BF16),) * 2,
-        in_specs=[smem] + [vmem] * 6,
+        in_specs=[smem] + [vmem] * 9,
         out_specs=(vmem, vmem),
         scratch_shapes=[pltpu.VMEM((modes, width), F32), pltpu.VMEM((width // 128, 2 * rows, 128), F32)],
         compiler_params=params,
         name="finish",
-    )(pos, gate, local, inside, states, modes_gain, decay)
+    )(pos, gate, local, inside, inner, *totals, modes_gain, decay)
     with jax.named_scope("result_swap"):
         return in_order(c == 0, mine, lax.ppermute(theirs, "c", SWAP), 1)
 

time: 122 us -> 126 us (1.033)
  starting transfers between devices: 51.1 us -> 61.7 us
  waiting for transfers between devices: 31.6 us -> 25.6 us
    all_to_all x1 -> x0, starting transfers between devices: 9.28 us -> none  [body(): states = lax.all_to_all(state, ('y', 'h'), 0, 0, tiled=True)]
    all_to_all x1 -> x0, waiting for transfers between devices: 8.67 us -> none  [body(): states = lax.all_to_all(state, ('y', 'h'), 0, 0, tiled=True)]
    ppermute x0 -> x3, starting transfers between devices: none -> 8.14 us  [body(): lax.ppermute(total, 'y', [(i, i + d) for i in range(4 - d)])]
    ppermute x14 -> x17, starting transfers between devices: 28.1 us -> 36 us  [shifted(): return lax.ppermute(array, axis, [(i, (i + step) % n) for i in range(n)])]
    ppermute x1, starting transfers between devices: 3.49 us -> 7.37 us  [body(): return in_order(c == 0, mine, lax.ppermute(theirs, 'c', SWAP), 1)]
    ppermute x14 -> x17, waiting for transfers between devices: 13.2 us -> 15.8 us  [shifted(): return lax.ppermute(array, axis, [(i, (i + step) % n) for i in range(n)])]
    unnamed x23 -> x19, local copies, waits for them, and re-layouts: 5.5 us -> 5.49 us
  transfers between devices with their start and end apart: 21 -> 26, of which waited for: 10 -> 10; matrix products, arithmetic and copies ran while one was open for 2% -> 2% of each run, Pallas kernels for 9% -> 9%
where the time goes in v13:
time: 126 us
  starting transfers between devices  61.7 us (49%)
  waiting for transfers between devices  25.6 us (20%)
  Pallas kernels  17.3 us (14%)
  between operations  13.7 us (11%)
  local copies, waits for them, and re-layouts  5.94 us (5%)
  other arithmetic  1.55 us (1%)
    ppermute x17, starting transfers between devices, shifted(): return lax.ppermute(array, axis, [(i, (i + step) % n) for i in range(n)])  36 us
    ppermute x17, waiting for transfers between devices, shifted(): return lax.ppermute(array, axis, [(i, (i + step) % n) for i in range(n)])  15.8 us
    ppermute x3, starting transfers between devices, body(): lax.ppermute(total, 'y', [(i, i + d) for i in range(4 - d)])  8.14 us
    ppermute x1, starting transfers between devices, body(): return in_order(c == 0, mine, lax.ppermute(theirs, 'c', SWAP), 1)  7.37 us
    ppermute x1, starting transfers between devices, body(): halos = lax.ppermute(tails, CTX, [(i, i + 1) for i in range(1, 31, 2)])  6.87 us
    pallas_call x1, Pallas kernels, body(): pl.pallas_call(functools.partial(project_kernel, sizes, early_runs, late_...  6.06 us
    unnamed x19, local copies, waits for them, and re-layouts  5.49 us
    pallas_call x1, Pallas kernels, body(): pl.pallas_call(functools.partial(state_kernel, sizes), out_shape=(full, j...  4.4 us
  transfers between devices with their start and end apart: 26, of which 10 were waited for; matrix products, arithmetic and copies ran while one was open for 2% of the time, Pallas kernels for 9%

profile of v13, /device:TPU:1, one launch (start us, length us, event | category | flops | bytes accessed | tf_op | source)
XLA Modules:
  0.0 125.8 jit_solution(4681702277619090622)
XLA Ops:
  6.5 0.7 all-gather.3.cloned.1.call-update
  7.3 0.0 all-gather.5.cloned.1.call-start
  7.3 1.2 copy.10
  8.6 0.1 copy.13
  8.8 3.3 %collective-permute-start.1 = (bf16[128,768]{1,0:T(8,128)(2,1)S(1)}, bf16[128,768]{1,0:T(8,128)(2,1)S(1)}, u32[]{:S(2)}, u32[]{:S(2)}) collective-permute-start(bf16[128,768]{1,0:T(8,128)(2,1)S(1)} %bitcast.17), channel_id=1, source_target_pairs={{0,8},{8,0},{1,9},{9,1},{2,10},{10,2},{3,11},{11,3},{4,12},{12,4},... | collective-permute-start | bytes 589832 | tf_op jit(solution)/shard_map/weight_gather/ppermute | solution.py:306
  12.1 0.1 copy.12
  12.2 0.9 collective-permute-done.1
  13.2 1.8 %collective-permute-start.3 = (bf16[256,768]{1,0:T(8,128)(2,1)S(1)}, bf16[256,768]{1,0:T(8,128)(2,1)S(1)}, u32[]{:S(2)}, u32[]{:S(2)}) collective-permute-start(bf16[256,768]{1,0:T(8,128)(2,1)S(1)} %pad_maximum_fusion.refs_3_), channel_id=1, source_target_pairs={{0,192},{64,0},{128,64},{192,128},{1,193},{65,1},{129,65},{193,129... | collective-permute-start | bytes 1179656 | tf_op jit(solution)/shard_map/weight_rings/ppermute | solution.py:23
  15.1 0.0 collective-permute-start.2
  15.1 5.3 %collective-permute-start.7 = (bf16[256,768]{1,0:T(8,128)(2,1)S(1)}, bf16[256,768]{1,0:T(8,128)(2,1)S(1)}, u32[]{:S(2)}, u32[]{:S(2)}) collective-permute-start(bf16[256,768]{1,0:T(8,128)(2,1)S(1)} %pad_maximum_fusion.refs_3_), channel_id=1, source_target_pairs={{0,48},{16,0},{32,16},{48,32},{1,49},{17,1},{33,17},{49,33},{2,50}... | collective-permute-start | bytes 1179656 | tf_op jit(solution)/shard_map/weight_rings/ppermute | solution.py:23
  20.3 0.0 collective-permute-start.6
  20.3 1.9 %collective-permute-done = bf16[256,512]{1,0:T(8,128)(2,1)S(1)} collective-permute-done((bf16[256,512]{1,0:T(8,128)(2,1)S(1)}, bf16[256,512]{1,0:T(8,128)(2,1)S(1)}, u32[]{:S(2)}, u32[]{:S(2)}) %collective-permute-start) | collective-permute-done | bytes 262176 | tf_op jit(solution)/shard_map/token_swap/ppermute | solution.py:309
  22.3 7.6 %collective-permute-start.5 = (bf16[256,768]{1,0:T(8,128)(2,1)S(1)}, bf16[256,768]{1,0:T(8,128)(2,1)S(1)}, u32[]{:S(2)}, u32[]{:S(2)}) collective-permute-start(bf16[256,768]{1,0:T(8,128)(2,1)S(1)} %pad_maximum_fusion.refs_3_), channel_id=1, source_target_pairs={{0,128},{64,192},{128,0},{192,64},{1,129},{65,193},{129,1},{193,65... | collective-permute-start | bytes 1179656 | tf_op jit(solution)/shard_map/weight_rings/ppermute | solution.py:23
  29.9 6.9 %collective-permute-start.4 = (bf16[32,512]{1,0:T(8,128)(2,1)S(1)}, bf16[32,512]{1,0:T(8,128)(2,1)S(1)}, u32[]{:S(2)}, u32[]{:S(2)}) collective-permute-start(bf16[32,512]{1,0:T(8,128)(2,1)S(1)} %pad_maximum_fusion.3), channel_id=1, source_target_pairs={{8,16},{24,32},{40,48},{56,64},{72,80},{88,96},{104,112},{120,128}... | collective-permute-start | bytes 98312 | tf_op jit(solution)/shard_map/weight_rings/ppermute | solution.py:316
  36.8 0.0 collective-permute-done.7.refs_1_
  36.8 0.0 collective-permute-done.6.refs_0_
  36.8 0.5 collective-permute-done.5.refs_10_
  37.3 3.4 %collective-permute-done.4 = bf16[32,512]{1,0:T(8,128)(2,1)S(1)} collective-permute-done((bf16[32,512]{1,0:T(8,128)(2,1)S(1)}, bf16[32,512]{1,0:T(8,128)(2,1)S(1)}, u32[]{:S(2)}, u32[]{:S(2)}) %collective-permute-start.4) | collective-permute-done | bytes 32800 | tf_op jit(solution)/shard_map/weight_rings/ppermute | solution.py:316
  40.7 0.7 pad_maximum_fusion.1
  41.5 0.0 all-gather.5.cloned.1.call-update
  41.5 0.9 relay_pair.1
  42.4 0.1 collective-permute-start.9
  42.5 1.5 %collective-permute-start.8 = (bf16[512,768]{1,0:T(8,128)(2,1)S(1)}, bf16[512,768]{1,0:T(8,128)(2,1)S(1)}, u32[]{:S(2)}, u32[]{:S(2)}) collective-permute-start(bf16[512,768]{1,0:T(8,128)(2,1)S(1)} %get-tuple-element.46.refs_4_), channel_id=1, source_target_pairs={{0,64},{64,128},{128,192},{192,0},{1,65},{65,129},{129,193},{193,1... | collective-permute-start | bytes 2359304 | tf_op jit(solution)/shard_map/weight_rings/ppermute | solution.py:23
  44.1 0.4 collective-permute-start.10
  44.5 3.2 %collective-permute-start.11 = (bf16[128,768]{1,0:T(8,128)(2,1)S(1)}, bf16[128,768]{1,0:T(8,128)(2,1)S(1)}, u32[]{:S(2)}, u32[]{:S(2)}) collective-permute-start(bf16[128,768]{1,0:T(8,128)(2,1)S(1)} %get-tuple-element.48), channel_id=1, source_target_pairs={{0,48},{16,0},{32,16},{48,32},{1,49},{17,1},{33,17},{49,33},{2,50}... | collective-permute-start | bytes 589832 | tf_op jit(solution)/shard_map/weight_rings/ppermute | solution.py:23
  47.6 3.1 %collective-permute-done.10.refs_2_ = bf16[128,768]{1,0:T(8,128)(2,1)S(1)} collective-permute-done((bf16[128,768]{1,0:T(8,128)(2,1)S(1)}, bf16[128,768]{1,0:T(8,128)(2,1)S(1)}, u32[]{:S(2)}, u32[]{:S(2)}) %collective-permute-start.10) | collective-permute-done | bytes 196640 | tf_op jit(solution)/shard_map/weight_rings/ppermute | solution.py:23
  50.8 0.2 collective-permute-done.11.refs_3_
  51.0 9.4 %collective-permute-done.9.refs_1_.refs_9_ = bf16[512,768]{1,0:T(8,128)(2,1)S(1)} collective-permute-done((bf16[512,768]{1,0:T(8,128)(2,1)S(1)}, bf16[512,768]{1,0:T(8,128)(2,1)S(1)}, u32[]{:S(2)}, u32[]{:S(2)}) %collective-permute-start.9) | collective-permute-done | bytes 786464 | tf_op jit(solution)/shard_map/weight_rings/ppermute | solution.py:23
  60.4 0.0 collective-permute-done.8.refs_0_.refs_7_
  60.4 1.4 %relay_far.1 = (bf16[256,768]{1,0:T(8,128)(2,1)}, bf16[256,768]{1,0:T(8,128)(2,1)}, bf16[256,768]{1,0:T(8,128)(2,1)}, bf16[256,768]{1,0:T(8,128)(2,1)}, bf16[256,768]{1,0:T(8,128)(2,1)}) custom-call(bf16[512,768]{1,0:T(8,128)(2,1)S(1)} %collective-permute-done.8.refs_0_.refs_7_, bf16[512,768]{1,0:T(8,128)(2,1)S(1)} %collective-permute-done.9.refs_1_.refs_9_, ...), custom_call_target="tpu_custom_call" | custom-call | bytes 2000000 | tf_op jit(solution)/shard_map/weight_rings/relay_far/pallas_call | solution.py:54
  61.8 1.6 %collective-permute-start.12 = (bf16[256,768]{1,0:T(8,128)(2,1)}, bf16[256,768]{1,0:T(8,128)(2,1)}, u32[]{:S(2)}, u32[]{:S(2)}) collective-permute-start(bf16[256,768]{1,0:T(8,128)(2,1)} %get-tuple-element.58), channel_id=1, source_target_pairs={{0,64},{64,128},{128,192},{192,0},{1,65},{65,129},{129,193},{193,1... | collective-permute-start | bytes 1179656 | tf_op jit(solution)/shard_map/weight_rings/ppermute | solution.py:23
  63.3 1.6 %collective-permute-start.13 = (bf16[256,768]{1,0:T(8,128)(2,1)}, bf16[256,768]{1,0:T(8,128)(2,1)}, u32[]{:S(2)}, u32[]{:S(2)}) collective-permute-start(bf16[256,768]{1,0:T(8,128)(2,1)} %get-tuple-element.59), channel_id=1, source_target_pairs={{0,192},{64,0},{128,64},{192,128},{1,193},{65,1},{129,65},{193,129... | collective-permute-start | bytes 1179656 | tf_op jit(solution)/shard_map/weight_rings/ppermute | solution.py:23
  65.0 2.4 %collective-permute-start.14 = (bf16[256,768]{1,0:T(8,128)(2,1)}, bf16[256,768]{1,0:T(8,128)(2,1)}, u32[]{:S(2)}, u32[]{:S(2)}) collective-permute-start(bf16[256,768]{1,0:T(8,128)(2,1)} %get-tuple-element.60), channel_id=1, source_target_pairs={{0,16},{16,32},{32,48},{48,0},{1,17},{17,33},{33,49},{49,1},{2,18}... | collective-permute-start | bytes 1179656 | tf_op jit(solution)/shard_map/weight_rings/ppermute | solution.py:23
  67.3 1.2 collective-permute-start.15
  68.5 1.4 %collective-permute-start.16 = (bf16[256,768]{1,0:T(8,128)(2,1)}, bf16[256,768]{1,0:T(8,128)(2,1)}, u32[]{:S(2)}, u32[]{:S(2)}) collective-permute-start(bf16[256,768]{1,0:T(8,128)(2,1)} %get-tuple-element.53.refs_5_), channel_id=1, source_target_pairs={{0,128},{64,192},{128,0},{192,64},{1,129},{65,193},{129,1},{193,65... | collective-permute-start | bytes 1179656 | tf_op jit(solution)/shard_map/weight_rings/ppermute | solution.py:23
  69.9 0.1 stack.23.refs_0_.pos
  70.0 1.7 %all-gather.5.cloned.1.call-done.refs_2_ = bf16[2304,512]{1,0:T(8,128)(2,1)} async-done(((bf16[288,512]{1,0:T(8,128)(2,1)}), bf16[2304,512]{1,0:T(8,128)(2,1)}) %all-gather.5.cloned.1.call-update) | async-done | bytes 2359312 | tf_op jit(solution)/shard_map/token_gather/all_gather | solution.py:322
  71.7 1.7 %copy-done = bf16[2304,512]{1,0:T(8,128)(2,1)S(1)} copy-done((bf16[2304,512]{1,0:T(8,128)(2,1)S(1)}, bf16[2304,512]{1,0:T(8,128)(2,1)}, u32[]{:S(2)}) %copy-start) | copy-done | bytes 2359320
  73.4 1.6 %copy-done.1 = bf16[2048,512]{1,0:T(8,128)(2,1)S(1)} copy-done((bf16[2048,512]{1,0:T(8,128)(2,1)S(1)}, bf16[2048,512]{1,0:T(8,128)(2,1)}, u32[]{:S(2)}) %copy-start.1) | copy-done | bytes 2097176
  75.0 1.0 copy-done.4
  76.0 6.1 %project.1 = (f32[6,528,128]{2,1,0:T(8,128)S(1)}, bf16[528,1280]{1,0:T(8,128)(2,1)S(1)}) custom-call(s32[5]{0:T(128)S(1)} %stack.23.refs_0_.pos, bf16[2048,512]{1,0:T(8,128)(2,1)S(1)} %copy-done.1, bf16[2304,512]{1,0:T(8,128)(2,1)S(1)} %copy-done, bf16[256,768]{1,0:T(8,128)(2,1)S(1)} %pad_maximum_fusion.refs_3_, ...), custom_call_target="tpu_custom_call" | custom-call | flops 2283798528 | bytes 9000000 | tf_op jit(solution)/shard_map/project/pallas_call | solution.py:362
  82.0 0.0 collective-permute-done.12.refs_2_
  82.0 0.0 collective-permute-done.14.refs_4_
  82.1 0.0 collective-permute-done.15.refs_5_
  82.1 0.0 copy-start.5
  82.1 0.0 copy-start.7
  82.1 4.4 %states.1 = (f32[64,8,256]{2,1,0:T(8,128)S(1)}, f32[2,528,128]{2,1,0:T(8,128)S(1)}, f32[16,256]{1,0:T(8,128)S(1)}) custom-call(s32[5]{0:T(128)S(1)} %stack.23.refs_0_.pos, bf16[528,1280]{1,0:T(8,128)(2,1)S(1)} %get-tuple-element.57.refs_1_, bf16[256,768]{1,0:T(8,128)(2,1)} %collective-permute-done.12.refs_2_, ...), custom_call_target="tpu_custom_call" | custom-call | tf_op jit(solution)/shard_map/states/pallas_call | solution.py:384
  86.5 3.9 %collective-permute-start.19 = (f32[16,256]{1,0:T(8,128)S(1)}, f32[16,256]{1,0:T(8,128)S(1)}, u32[]{:S(2)}, u32[]{:S(2)}) collective-permute-start(f32[16,256]{1,0:T(8,128)S(1)} %get-tuple-element.68.refs_0_), channel_id=1, source_target_pairs={{0,48},{16,0},{32,16},{48,32},{1,49},{17,1},{33,17},{49,33},{2,50}... | collective-permute-start | bytes 49160 | tf_op jit(solution)/shard_map/state_exchange/ppermute | solution.py:23
  90.4 1.7 %collective-permute-start.18 = (f32[16,256]{1,0:T(8,128)S(1)}, f32[16,256]{1,0:T(8,128)S(1)}, u32[]{:S(2)}, u32[]{:S(2)}) collective-permute-start(f32[16,256]{1,0:T(8,128)S(1)} %get-tuple-element.68.refs_0_), channel_id=1, source_target_pairs={{0,32},{16,48},{32,0},{48,16},{1,33},{17,49},{33,1},{49,17},{2,34}... | collective-permute-start | bytes 49160 | tf_op jit(solution)/shard_map/state_exchange/ppermute | solution.py:23
  92.2 2.3 %collective-permute-start.17 = (f32[16,256]{1,0:T(8,128)S(1)}, f32[16,256]{1,0:T(8,128)S(1)}, u32[]{:S(2)}, u32[]{:S(2)}) collective-permute-start(f32[16,256]{1,0:T(8,128)S(1)} %get-tuple-element.68.refs_0_), channel_id=1, source_target_pairs={{0,16},{16,32},{32,48},{48,0},{1,17},{17,33},{33,49},{49,1},{2,18}... | collective-permute-start | bytes 49160 | tf_op jit(solution)/shard_map/state_exchange/ppermute | solution.py:23
  94.4 0.0 collective-permute-done.19.refs_3_
  94.4 2.6 %collective-permute-done.18.refs_2_ = f32[16,256]{1,0:T(8,128)S(1)} collective-permute-done((f32[16,256]{1,0:T(8,128)S(1)}, f32[16,256]{1,0:T(8,128)S(1)}, u32[]{:S(2)}, u32[]{:S(2)}) %collective-permute-start.18) | collective-permute-done | bytes 16416 | tf_op jit(solution)/shard_map/state_exchange/ppermute | solution.py:23
  97.0 0.0 collective-permute-done.17.refs_1_
  97.0 0.6 combine.1
  97.6 4.4 %collective-permute-start.22 = (f32[16,256]{1,0:T(8,128)S(1)}, f32[16,256]{1,0:T(8,128)S(1)}, u32[]{:S(2)}, u32[]{:S(2)}) collective-permute-start(f32[16,256]{1,0:T(8,128)S(1)} %get-tuple-element.70), channel_id=1, source_target_pairs={{0,192},{1,193},{2,194},{3,195},{4,196},{5,197},{6,198},{7,199},{8... | collective-permute-start | bytes 49160 | tf_op jit(solution)/shard_map/state_exchange/ppermute | solution.py:409
  102.0 1.3 %collective-permute-start.21 = (f32[16,256]{1,0:T(8,128)S(1)}, f32[16,256]{1,0:T(8,128)S(1)}, u32[]{:S(2)}, u32[]{:S(2)}) collective-permute-start(f32[16,256]{1,0:T(8,128)S(1)} %get-tuple-element.70), channel_id=1, source_target_pairs={{0,128},{64,192},{1,129},{65,193},{2,130},{66,194},{3,131},{67,195... | collective-permute-start | bytes 49160 | tf_op jit(solution)/shard_map/state_exchange/ppermute | solution.py:409
  103.3 2.5 %collective-permute-start.20 = (f32[16,256]{1,0:T(8,128)S(1)}, f32[16,256]{1,0:T(8,128)S(1)}, u32[]{:S(2)}, u32[]{:S(2)}) collective-permute-start(f32[16,256]{1,0:T(8,128)S(1)} %get-tuple-element.70), channel_id=1, source_target_pairs={{0,64},{64,128},{128,192},{1,65},{65,129},{129,193},{2,66},{66,130... | collective-permute-start | bytes 49160 | tf_op jit(solution)/shard_map/state_exchange/ppermute | solution.py:409
  105.8 2.5 %local.1 = (f32[64,8,256]{2,1,0:T(8,128)S(1)}, f32[64,8,256]{2,1,0:T(8,128)S(1)}, f32[16,8,256]{2,1,0:T(8,128)S(1)}) custom-call(s32[5]{0:T(128)S(1)} %stack.23.refs_0_.pos, f32[2,528,128]{2,1,0:T(8,128)S(1)} %get-tuple-element.63.gated, f32[3,3,512]{2,1,0:T(4,128)S(1)} %copy-done.6, f32[64,8,256]{2,1,0:T(8,128)S(1)} %get-tuple-element.64.product, ...), custom_call_target="tpu_custom_call" | custom-call | flops 30000000 | bytes 2000000 | tf_op jit(solution)/shard_map/local/pallas_call | solution.py:411
  108.3 0.0 collective-permute-done.21.refs_1_
  108.3 0.0 collective-permute-done.20.refs_0_
  108.3 1.5 %finish.1 = (bf16[256,256]{1,0:T(8,128)(2,1)S(1)}, bf16[256,256]{1,0:T(8,128)(2,1)S(1)}) custom-call(s32[5]{0:T(128)S(1)} %stack.23.refs_0_.pos, f32[64,8,256]{2,1,0:T(8,128)S(1)} %get-tuple-element.65.gate, f32[64,8,256]{2,1,0:T(8,128)S(1)} %get-tuple-element.66.local, f32[16,8,256]{2,1,0:T(8,128)S(1)} %get-tuple-element.67.inside, ...), custom_call_target="tpu_custom_call" | custom-call | tf_op jit(solution)/shard_map/finish/pallas_call | solution.py:422
  109.8 7.4 %collective-permute-start.23 = (bf16[256,256]{1,0:T(8,128)(2,1)S(1)}, bf16[256,256]{1,0:T(8,128)(2,1)S(1)}, u32[]{:S(2)}, u32[]{:S(2)}) collective-permute-start(bf16[256,256]{1,0:T(8,128)(2,1)S(1)} %get-tuple-element.72), channel_id=1, source_target_pairs={{0,8},{8,0},{1,9},{9,1},{2,10},{10,2},{3,11},{11,3},{4,12},{12,4},... | collective-permute-start | bytes 393224 | tf_op jit(solution)/shard_map/result_swap/ppermute | solution.py:432
  117.2 1.0 collective-permute-done.23
  118.2 0.7 pad_maximum_fusion.2
  (29 shorter events, 0.2 us)
Async XLA Ops:
  6.5 5.6 %copy-start.8 = (bf16[256,512]{1,0:T(8,128)(2,1)S(1)}, bf16[256,512]{1,0:T(8,128)(2,1)}, u32[]{:S(2)}) copy-start(bf16[256,512]{1,0:T(8,128)(2,1)} %param.6) | copy-start | bytes 786436
  6.5 63.5 %all-gather.3.cloned.1.call-start = ((), (), s32[]{:S(2)}) async-start(), calls=%async_computation | async-start | bytes 2359296 | tf_op jit(solution)/shard_map/token_gather/all_gather | solution.py:320
  7.3 64.4 %all-gather.5.cloned.1.call-start = ((), (), s32[]{:S(2)}) async-start(), calls=%async_computation.1 | async-start | bytes 2654208 | tf_op jit(solution)/shard_map/token_gather/all_gather | solution.py:322
  8.8 4.4 %collective-permute-start.1 = (bf16[128,768]{1,0:T(8,128)(2,1)S(1)}, bf16[128,768]{1,0:T(8,128)(2,1)S(1)}, u32[]{:S(2)}, u32[]{:S(2)}) collective-permute-start(bf16[128,768]{1,0:T(8,128)(2,1)S(1)} %bitcast.17), channel_id=1, source_target_pairs={{0,8},{8,0},{1,9},{9,1},{2,10},{10,2},{3,11},{11,3},{4,12},{12,4},... | collective-permute-start | bytes 589832 | tf_op jit(solution)/shard_map/weight_gather/ppermute | solution.py:306
  12.1 10.2 %collective-permute-start = (bf16[256,512]{1,0:T(8,128)(2,1)S(1)}, bf16[256,512]{1,0:T(8,128)(2,1)S(1)}, u32[]{:S(2)}, u32[]{:S(2)}) collective-permute-start(bf16[256,512]{1,0:T(8,128)(2,1)S(1)} %copy-done.8), channel_id=1, source_target_pairs={{0,4},{4,0},{1,5},{5,1},{2,6},{6,2},{3,7},{7,3},{8,12},{12,8},{9,1... | collective-permute-start | bytes 786440 | tf_op jit(solution)/shard_map/token_swap/ppermute | solution.py:309
  13.2 16.7 %collective-permute-start.3 = (bf16[256,768]{1,0:T(8,128)(2,1)S(1)}, bf16[256,768]{1,0:T(8,128)(2,1)S(1)}, u32[]{:S(2)}, u32[]{:S(2)}) collective-permute-start(bf16[256,768]{1,0:T(8,128)(2,1)S(1)} %pad_maximum_fusion.refs_3_), channel_id=1, source_target_pairs={{0,192},{64,0},{128,64},{192,128},{1,193},{65,1},{129,65},{193,129... | collective-permute-start | bytes 1179656 | tf_op jit(solution)/shard_map/weight_rings/ppermute | solution.py:23
  15.1 14.8 %collective-permute-start.2 = (bf16[256,768]{1,0:T(8,128)(2,1)S(1)}, bf16[256,768]{1,0:T(8,128)(2,1)S(1)}, u32[]{:S(2)}, u32[]{:S(2)}) collective-permute-start(bf16[256,768]{1,0:T(8,128)(2,1)S(1)} %pad_maximum_fusion.refs_3_), channel_id=1, source_target_pairs={{0,64},{64,128},{128,192},{192,0},{1,65},{65,129},{129,193},{193,1... | collective-permute-start | bytes 1179656 | tf_op jit(solution)/shard_map/weight_rings/ppermute | solution.py:23
  15.1 21.7 %collective-permute-start.7 = (bf16[256,768]{1,0:T(8,128)(2,1)S(1)}, bf16[256,768]{1,0:T(8,128)(2,1)S(1)}, u32[]{:S(2)}, u32[]{:S(2)}) collective-permute-start(bf16[256,768]{1,0:T(8,128)(2,1)S(1)} %pad_maximum_fusion.refs_3_), channel_id=1, source_target_pairs={{0,48},{16,0},{32,16},{48,32},{1,49},{17,1},{33,17},{49,33},{2,50}... | collective-permute-start | bytes 1179656 | tf_op jit(solution)/shard_map/weight_rings/ppermute | solution.py:23
  20.3 16.5 %collective-permute-start.6 = (bf16[256,768]{1,0:T(8,128)(2,1)S(1)}, bf16[256,768]{1,0:T(8,128)(2,1)S(1)}, u32[]{:S(2)}, u32[]{:S(2)}) collective-permute-start(bf16[256,768]{1,0:T(8,128)(2,1)S(1)} %pad_maximum_fusion.refs_3_), channel_id=1, source_target_pairs={{0,16},{16,32},{32,48},{48,0},{1,17},{17,33},{33,49},{49,1},{2,18}... | collective-permute-start | bytes 1179656 | tf_op jit(solution)/shard_map/weight_rings/ppermute | solution.py:23
  22.3 15.0 %collective-permute-start.5 = (bf16[256,768]{1,0:T(8,128)(2,1)S(1)}, bf16[256,768]{1,0:T(8,128)(2,1)S(1)}, u32[]{:S(2)}, u32[]{:S(2)}) collective-permute-start(bf16[256,768]{1,0:T(8,128)(2,1)S(1)} %pad_maximum_fusion.refs_3_), channel_id=1, source_target_pairs={{0,128},{64,192},{128,0},{192,64},{1,129},{65,193},{129,1},{193,65... | collective-permute-start | bytes 1179656 | tf_op jit(solution)/shard_map/weight_rings/ppermute | solution.py:23
  29.9 10.8 %collective-permute-start.4 = (bf16[32,512]{1,0:T(8,128)(2,1)S(1)}, bf16[32,512]{1,0:T(8,128)(2,1)S(1)}, u32[]{:S(2)}, u32[]{:S(2)}) collective-permute-start(bf16[32,512]{1,0:T(8,128)(2,1)S(1)} %pad_maximum_fusion.3), channel_id=1, source_target_pairs={{8,16},{24,32},{40,48},{56,64},{72,80},{88,96},{104,112},{120,128}... | collective-permute-start | bytes 98312 | tf_op jit(solution)/shard_map/weight_rings/ppermute | solution.py:316
  37.3 4.2 %copy-start.3 = (bf16[256,768]{1,0:T(8,128)(2,1)}, bf16[256,768]{1,0:T(8,128)(2,1)S(1)}, u32[]{:S(2)}) copy-start(bf16[256,768]{1,0:T(8,128)(2,1)S(1)} %collective-permute-done.5.refs_10_) | copy-start | bytes 1179652
  42.4 17.9 %collective-permute-start.9 = (bf16[512,768]{1,0:T(8,128)(2,1)S(1)}, bf16[512,768]{1,0:T(8,128)(2,1)S(1)}, u32[]{:S(2)}, u32[]{:S(2)}) collective-permute-start(bf16[512,768]{1,0:T(8,128)(2,1)S(1)} %get-tuple-element.46.refs_4_), channel_id=1, source_target_pairs={{0,192},{64,0},{128,64},{192,128},{1,193},{65,1},{129,65},{193,129... | collective-permute-start | bytes 2359304 | tf_op jit(solution)/shard_map/weight_rings/ppermute | solution.py:23
  42.5 17.9 %collective-permute-start.8 = (bf16[512,768]{1,0:T(8,128)(2,1)S(1)}, bf16[512,768]{1,0:T(8,128)(2,1)S(1)}, u32[]{:S(2)}, u32[]{:S(2)}) collective-permute-start(bf16[512,768]{1,0:T(8,128)(2,1)S(1)} %get-tuple-element.46.refs_4_), channel_id=1, source_target_pairs={{0,64},{64,128},{128,192},{192,0},{1,65},{65,129},{129,193},{193,1... | collective-permute-start | bytes 2359304 | tf_op jit(solution)/shard_map/weight_rings/ppermute | solution.py:23
  44.1 6.7 %collective-permute-start.10 = (bf16[128,768]{1,0:T(8,128)(2,1)S(1)}, bf16[128,768]{1,0:T(8,128)(2,1)S(1)}, u32[]{:S(2)}, u32[]{:S(2)}) collective-permute-start(bf16[128,768]{1,0:T(8,128)(2,1)S(1)} %get-tuple-element.47), channel_id=1, source_target_pairs={{0,16},{16,32},{32,48},{48,0},{1,17},{17,33},{33,49},{49,1},{2,18}... | collective-permute-start | bytes 589832 | tf_op jit(solution)/shard_map/weight_rings/ppermute | solution.py:23
  44.5 6.5 %collective-permute-start.11 = (bf16[128,768]{1,0:T(8,128)(2,1)S(1)}, bf16[128,768]{1,0:T(8,128)(2,1)S(1)}, u32[]{:S(2)}, u32[]{:S(2)}) collective-permute-start(bf16[128,768]{1,0:T(8,128)(2,1)S(1)} %get-tuple-element.48), channel_id=1, source_target_pairs={{0,48},{16,0},{32,16},{48,32},{1,49},{17,1},{33,17},{49,33},{2,50}... | collective-permute-start | bytes 589832 | tf_op jit(solution)/shard_map/weight_rings/ppermute | solution.py:23
  61.8 20.3 %collective-permute-start.12 = (bf16[256,768]{1,0:T(8,128)(2,1)}, bf16[256,768]{1,0:T(8,128)(2,1)}, u32[]{:S(2)}, u32[]{:S(2)}) collective-permute-start(bf16[256,768]{1,0:T(8,128)(2,1)} %get-tuple-element.58), channel_id=1, source_target_pairs={{0,64},{64,128},{128,192},{192,0},{1,65},{65,129},{129,193},{193,1... | collective-permute-start | bytes 1179656 | tf_op jit(solution)/shard_map/weight_rings/ppermute | solution.py:23
  63.3 18.7 %collective-permute-start.13 = (bf16[256,768]{1,0:T(8,128)(2,1)}, bf16[256,768]{1,0:T(8,128)(2,1)}, u32[]{:S(2)}, u32[]{:S(2)}) collective-permute-start(bf16[256,768]{1,0:T(8,128)(2,1)} %get-tuple-element.59), channel_id=1, source_target_pairs={{0,192},{64,0},{128,64},{192,128},{1,193},{65,1},{129,65},{193,129... | collective-permute-start | bytes 1179656 | tf_op jit(solution)/shard_map/weight_rings/ppermute | solution.py:23
  65.0 17.1 %collective-permute-start.14 = (bf16[256,768]{1,0:T(8,128)(2,1)}, bf16[256,768]{1,0:T(8,128)(2,1)}, u32[]{:S(2)}, u32[]{:S(2)}) collective-permute-start(bf16[256,768]{1,0:T(8,128)(2,1)} %get-tuple-element.60), channel_id=1, source_target_pairs={{0,16},{16,32},{32,48},{48,0},{1,17},{17,33},{33,49},{49,1},{2,18}... | collective-permute-start | bytes 1179656 | tf_op jit(solution)/shard_map/weight_rings/ppermute | solution.py:23
  67.3 14.7 %collective-permute-start.15 = (bf16[256,768]{1,0:T(8,128)(2,1)}, bf16[256,768]{1,0:T(8,128)(2,1)}, u32[]{:S(2)}, u32[]{:S(2)}) collective-permute-start(bf16[256,768]{1,0:T(8,128)(2,1)} %get-tuple-element.61), channel_id=1, source_target_pairs={{0,48},{16,0},{32,16},{48,32},{1,49},{17,1},{33,17},{49,33},{2,50}... | collective-permute-start | bytes 1179656 | tf_op jit(solution)/shard_map/weight_rings/ppermute | solution.py:23
  68.5 13.5 %collective-permute-start.16 = (bf16[256,768]{1,0:T(8,128)(2,1)}, bf16[256,768]{1,0:T(8,128)(2,1)}, u32[]{:S(2)}, u32[]{:S(2)}) collective-permute-start(bf16[256,768]{1,0:T(8,128)(2,1)} %get-tuple-element.53.refs_5_), channel_id=1, source_target_pairs={{0,128},{64,192},{128,0},{192,64},{1,129},{65,193},{129,1},{193,65... | collective-permute-start | bytes 1179656 | tf_op jit(solution)/shard_map/weight_rings/ppermute | solution.py:23
  71.7 1.7 %copy-start = (bf16[2304,512]{1,0:T(8,128)(2,1)S(1)}, bf16[2304,512]{1,0:T(8,128)(2,1)}, u32[]{:S(2)}) copy-start(bf16[2304,512]{1,0:T(8,128)(2,1)} %all-gather.5.cloned.1.call-done.refs_2_) | copy-start | bytes 7077892
  73.4 1.6 %copy-start.1 = (bf16[2048,512]{1,0:T(8,128)(2,1)S(1)}, bf16[2048,512]{1,0:T(8,128)(2,1)}, u32[]{:S(2)}) copy-start(bf16[2048,512]{1,0:T(8,128)(2,1)} %all-gather.3.cloned.1.call-done.refs_1_) | copy-start | bytes 6291460
  75.0 1.0 copy-start.4
  76.0 6.1 %copy-start.2 = (f32[16,512]{1,0:T(8,128)S(1)}, f32[16,512]{1,0:T(8,128)}, u32[]{:S(2)}) copy-start(f32[16,512]{1,0:T(8,128)} %refs_4_.3) | copy-start | bytes 98308
  76.0 6.1 %copy-start.6 = (f32[3,3,512]{2,1,0:T(4,128)S(1)}, f32[3,3,512]{2,1,0:T(4,128)}, u32[]{:S(2)}) copy-start(f32[3,3,512]{2,1,0:T(4,128)} %taps.1) | copy-start | bytes 55300
  82.1 23.7 %copy-start.5 = (f32[16,512]{1,0:T(8,128)S(1)}, f32[16,512]{1,0:T(8,128)}, u32[]{:S(2)}) copy-start(f32[16,512]{1,0:T(8,128)} %refs_3_.1) | copy-start | bytes 98308
  82.1 23.7 %copy-start.7 = (f32[512]{0:T(512)S(1)}, f32[512]{0:T(512)}, u32[]{:S(2)}) copy-start(f32[512]{0:T(512)} %param.11) | copy-start | bytes 6148
  86.5 7.9 %collective-permute-start.19 = (f32[16,256]{1,0:T(8,128)S(1)}, f32[16,256]{1,0:T(8,128)S(1)}, u32[]{:S(2)}, u32[]{:S(2)}) collective-permute-start(f32[16,256]{1,0:T(8,128)S(1)} %get-tuple-element.68.refs_0_), channel_id=1, source_target_pairs={{0,48},{16,0},{32,16},{48,32},{1,49},{17,1},{33,17},{49,33},{2,50}... | collective-permute-start | bytes 49160 | tf_op jit(solution)/shard_map/state_exchange/ppermute | solution.py:23
  90.4 6.6 %collective-permute-start.18 = (f32[16,256]{1,0:T(8,128)S(1)}, f32[16,256]{1,0:T(8,128)S(1)}, u32[]{:S(2)}, u32[]{:S(2)}) collective-permute-start(f32[16,256]{1,0:T(8,128)S(1)} %get-tuple-element.68.refs_0_), channel_id=1, source_target_pairs={{0,32},{16,48},{32,0},{48,16},{1,33},{17,49},{33,1},{49,17},{2,34}... | collective-permute-start | bytes 49160 | tf_op jit(solution)/shard_map/state_exchange/ppermute | solution.py:23
  92.2 4.9 %collective-permute-start.17 = (f32[16,256]{1,0:T(8,128)S(1)}, f32[16,256]{1,0:T(8,128)S(1)}, u32[]{:S(2)}, u32[]{:S(2)}) collective-permute-start(f32[16,256]{1,0:T(8,128)S(1)} %get-tuple-element.68.refs_0_), channel_id=1, source_target_pairs={{0,16},{16,32},{32,48},{48,0},{1,17},{17,33},{33,49},{49,1},{2,18}... | collective-permute-start | bytes 49160 | tf_op jit(solution)/shard_map/state_exchange/ppermute | solution.py:23
  97.6 10.7 %collective-permute-start.22 = (f32[16,256]{1,0:T(8,128)S(1)}, f32[16,256]{1,0:T(8,128)S(1)}, u32[]{:S(2)}, u32[]{:S(2)}) collective-permute-start(f32[16,256]{1,0:T(8,128)S(1)} %get-tuple-element.70), channel_id=1, source_target_pairs={{0,192},{1,193},{2,194},{3,195},{4,196},{5,197},{6,198},{7,199},{8... | collective-permute-start | bytes 49160 | tf_op jit(solution)/shard_map/state_exchange/ppermute | solution.py:409
  102.0 6.3 %collective-permute-start.21 = (f32[16,256]{1,0:T(8,128)S(1)}, f32[16,256]{1,0:T(8,128)S(1)}, u32[]{:S(2)}, u32[]{:S(2)}) collective-permute-start(f32[16,256]{1,0:T(8,128)S(1)} %get-tuple-element.70), channel_id=1, source_target_pairs={{0,128},{64,192},{1,129},{65,193},{2,130},{66,194},{3,131},{67,195... | collective-permute-start | bytes 49160 | tf_op jit(solution)/shard_map/state_exchange/ppermute | solution.py:409
  103.3 5.0 %collective-permute-start.20 = (f32[16,256]{1,0:T(8,128)S(1)}, f32[16,256]{1,0:T(8,128)S(1)}, u32[]{:S(2)}, u32[]{:S(2)}) collective-permute-start(f32[16,256]{1,0:T(8,128)S(1)} %get-tuple-element.70), channel_id=1, source_target_pairs={{0,64},{64,128},{128,192},{1,65},{65,129},{129,193},{2,66},{66,130... | collective-permute-start | bytes 49160 | tf_op jit(solution)/shard_map/state_exchange/ppermute | solution.py:409
  109.8 8.4 %collective-permute-start.23 = (bf16[256,256]{1,0:T(8,128)(2,1)S(1)}, bf16[256,256]{1,0:T(8,128)(2,1)S(1)}, u32[]{:S(2)}, u32[]{:S(2)}) collective-permute-start(bf16[256,256]{1,0:T(8,128)(2,1)S(1)} %get-tuple-element.72), channel_id=1, source_target_pairs={{0,8},{8,0},{1,9},{9,1},{2,10},{10,2},{3,11},{11,3},{4,12},{12,4},... | collective-permute-start | bytes 393224 | tf_op jit(solution)/shard_map/result_swap/ppermute | solution.py:432
Sparse Core Ops, SparseCore 0:
  9.2 31.8 all-gather.2
  43.0 28.6 all-gather.4

commit v14 on v12

--- a/solution.py
+++ b/solution.py
@@ -289,20 +289,21 @@
         mine = lax.dynamic_index_in_dim(halves, c, 0, keepdims=False)
         theirs = lax.ppermute(lax.dynamic_index_in_dim(halves, 1 - c, 0, keepdims=False), "c", SWAP)
         own = in_order(c == 0, mine, theirs, 0)
-    with jax.named_scope("token_swap"):
-        other = lax.ppermute(tokens, "l", SWAP)
+    with jax.named_scope("token_halo"):
+        route = [(i, i + 1) for i in range(1, 31, 2)]
+        halo = lax.ppermute(tokens[rows - HALO :], CTX, route)
     with jax.named_scope("weight_rings"):
         farther = shifted(own, "y", 2)
         far = both_ways(own, "y")
         beside = both_ways(own, "h")
-        other, far = tie((other, far))
-        tails = jnp.concatenate([tokens[rows - HALO :], other[rows - HALO :]], 0)
-        halos = lax.ppermute(tails, CTX, [(i, i + 1) for i in range(1, 31, 2)])
-    first = (halos, other, farther, far, beside)
-    halos, other, farther, far, beside = tie(first)
+        halo, far = tie((halo, far))
+    with jax.named_scope("token_swap"):
+        other = lax.ppermute(jnp.concatenate([halo, tokens], 0), "l", SWAP)
+    first = (halo, other, farther, far, beside)
+    halo, other, farther, far, beside = tie(first)
     with jax.named_scope("token_gather"):
         near = lax.all_gather(tokens, ("c", "x"), axis=0, tiled=True)
-        wide = jnp.concatenate([halos, other], 0)
+        wide = jnp.concatenate([halo, other], 0)
         swapped = lax.all_gather(wide, ("c", "x"), axis=0, tiled=True)
     with jax.named_scope("weight_rings"):
         two, half = 2 * k, k

time: 122 us -> 130 us (1.066)
  waiting for transfers between devices: 31.6 us -> 49.4 us
  starting transfers between devices: 51.1 us -> 41.4 us
    ppermute x14, waiting for transfers between devices: 13.2 us -> 31.5 us  [shifted(): return lax.ppermute(array, axis, [(i, (i + step) % n) for i in range(n)])]
    ppermute x14, starting transfers between devices: 28.1 us -> 21.9 us  [shifted(): return lax.ppermute(array, axis, [(i, (i + step) % n) for i in range(n)])]
    all_to_all x1, starting transfers between devices: 9.28 us -> 3.73 us  [body(): states = lax.all_to_all(state, ('y', 'h'), 0, 0, tiled=True)]
    ppermute x1, starting transfers between devices: 3.49 us -> 6.18 us  [body(): return in_order(c == 0, mine, lax.ppermute(theirs, 'c', SWAP), 1)]
    ppermute x2, waiting for transfers between devices: 5.39 us -> 7.19 us  [the longest x1 7.18 us: body(): other = lax.ppermute(jnp.concatenate([halo, tokens], 0), 'l', SWAP)]
    all_gather x1, waiting for transfers between devices: 1.7 us -> 0.01 us  [body(): swapped = lax.all_gather(wide, ('c', 'x'), axis=0, tiled=True)]
  transfers between devices with their start and end apart: 21 -> 21, of which waited for: 10 -> 10; matrix products, arithmetic and copies ran while one was open for 2% -> 2% of each run, Pallas kernels for 9% -> 8%
where the time goes in v14:
time: 130 us; the launch traced here: 129 us
  waiting for transfers between devices  49.4 us (38%)
  starting transfers between devices  41.4 us (32%)
  Pallas kernels  17.5 us (13%)
  between operations  13.6 us (10%)
  local copies, waits for them, and re-layouts  5.95 us (5%)
  other arithmetic  1.55 us (1%)
    ppermute x14, waiting for transfers between devices, shifted(): return lax.ppermute(array, axis, [(i, (i + step) % n) for i in range(n)])  31.5 us
    ppermute x14, starting transfers between devices, shifted(): return lax.ppermute(array, axis, [(i, (i + step) % n) for i in range(n)])  21.9 us
    all_to_all x1, waiting for transfers between devices, body(): states = lax.all_to_all(state, ('y', 'h'), 0, 0, tiled=True)  8.1 us
    ppermute x1, waiting for transfers between devices, body(): other = lax.ppermute(jnp.concatenate([halo, tokens], 0), 'l', SWAP)  7.18 us
    ppermute x1, starting transfers between devices, body(): return in_order(c == 0, mine, lax.ppermute(theirs, 'c', SWAP), 1)  6.18 us
    pallas_call x1, Pallas kernels, body(): pl.pallas_call(functools.partial(project_kernel, sizes, early_runs, late_...  6.05 us
    unnamed x23, local copies, waits for them, and re-layouts  5.51 us
    pallas_call x1, Pallas kernels, body(): pl.pallas_call(functools.partial(state_kernel, sizes), out_shape=(full, j...  5.13 us
  transfers between devices with their start and end apart: 21, of which 10 were waited for; matrix products, arithmetic and copies ran while one was open for 2% of the time, Pallas kernels for 8%

profile of v14, /device:TPU:1, one launch (start us, length us, event | category | flops | bytes accessed | tf_op | source)
XLA Modules:
  0.0 129.4 jit_solution(6976099556976574050)
XLA Ops:
  6.5 0.0 all-gather.3.cloned.1.call-start
  6.5 0.7 all-gather.3.cloned.1.call-update
  7.3 0.0 all-gather.5.cloned.1.call-start
  7.3 1.2 copy.10
  8.5 0.0 copy-start.10
  8.6 0.1 copy.13
  8.8 3.3 %collective-permute-start.1 = (bf16[128,768]{1,0:T(8,128)(2,1)S(1)}, bf16[128,768]{1,0:T(8,128)(2,1)S(1)}, u32[]{:S(2)}, u32[]{:S(2)}) collective-permute-start(bf16[128,768]{1,0:T(8,128)(2,1)S(1)} %bitcast.17), channel_id=1, source_target_pairs={{0,8},{8,0},{1,9},{9,1},{2,10},{10,2},{3,11},{11,3},{4,12},{12,4},... | collective-permute-start | bytes 589832 | tf_op jit(solution)/shard_map/weight_gather/ppermute | solution.py:290
  12.1 0.1 copy.12
  12.2 0.9 collective-permute-done.1
  13.2 1.1 collective-permute-start.3
  14.3 0.5 collective-permute-start.2
  14.8 0.0 copy-done.10
  14.8 5.0 %collective-permute-start = (bf16[16,512]{1,0:T(8,128)(2,1)S(1)}, bf16[16,512]{1,0:T(8,128)(2,1)S(1)}, u32[]{:S(2)}, u32[]{:S(2)}) collective-permute-start(bf16[16,512]{1,0:T(8,128)(2,1)S(1)} %slice.3), channel_id=1, source_target_pairs={{8,16},{24,32},{40,48},{56,64},{72,80},{88,96},{104,112},{120,128}... | collective-permute-start | bytes 49160 | tf_op jit(solution)/shard_map/token_halo/ppermute | solution.py:294
  19.8 2.0 %collective-permute-start.7 = (bf16[256,768]{1,0:T(8,128)(2,1)S(1)}, bf16[256,768]{1,0:T(8,128)(2,1)S(1)}, u32[]{:S(2)}, u32[]{:S(2)}) collective-permute-start(bf16[256,768]{1,0:T(8,128)(2,1)S(1)} %pad_maximum_fusion.refs_3_), channel_id=1, source_target_pairs={{0,48},{16,0},{32,16},{48,32},{1,49},{17,1},{33,17},{49,33},{2,50}... | collective-permute-start | bytes 1179656 | tf_op jit(solution)/shard_map/weight_rings/ppermute | solution.py:23
  21.7 2.4 %collective-permute-start.6 = (bf16[256,768]{1,0:T(8,128)(2,1)S(1)}, bf16[256,768]{1,0:T(8,128)(2,1)S(1)}, u32[]{:S(2)}, u32[]{:S(2)}) collective-permute-start(bf16[256,768]{1,0:T(8,128)(2,1)S(1)} %pad_maximum_fusion.refs_3_), channel_id=1, source_target_pairs={{0,16},{16,32},{32,48},{48,0},{1,17},{17,33},{33,49},{49,1},{2,18}... | collective-permute-start | bytes 1179656 | tf_op jit(solution)/shard_map/weight_rings/ppermute | solution.py:23
  24.1 0.0 collective-permute-done
  24.1 1.9 %collective-permute-start.5 = (bf16[256,768]{1,0:T(8,128)(2,1)S(1)}, bf16[256,768]{1,0:T(8,128)(2,1)S(1)}, u32[]{:S(2)}, u32[]{:S(2)}) collective-permute-start(bf16[256,768]{1,0:T(8,128)(2,1)S(1)} %pad_maximum_fusion.refs_3_), channel_id=1, source_target_pairs={{0,128},{64,192},{128,0},{192,64},{1,129},{65,193},{129,1},{193,65... | collective-permute-start | bytes 1179656 | tf_op jit(solution)/shard_map/weight_rings/ppermute | solution.py:23
  26.1 0.0 collective-permute-done.3.refs_8_
  26.1 0.0 collective-permute-done.2.refs_6_
  26.1 1.2 collective-permute-start.4
  27.3 10.5 %collective-permute-done.7.refs_1_ = bf16[256,768]{1,0:T(8,128)(2,1)S(1)} collective-permute-done((bf16[256,768]{1,0:T(8,128)(2,1)S(1)}, bf16[256,768]{1,0:T(8,128)(2,1)S(1)}, u32[]{:S(2)}, u32[]{:S(2)}) %collective-permute-start.7) | collective-permute-done | bytes 393248 | tf_op jit(solution)/shard_map/weight_rings/ppermute | solution.py:23
  37.8 0.0 collective-permute-done.6.refs_0_
  37.8 0.0 collective-permute-done.5.refs_10_
  37.8 7.2 %collective-permute-done.4 = bf16[272,512]{1,0:T(8,128)(2,1)S(1)} collective-permute-done((bf16[272,512]{1,0:T(8,128)(2,1)S(1)}, bf16[272,512]{1,0:T(8,128)(2,1)S(1)}, u32[]{:S(2)}, u32[]{:S(2)}) %collective-permute-start.4) | collective-permute-done | bytes 278560 | tf_op jit(solution)/shard_map/token_swap/ppermute | solution.py:301
  45.0 0.7 pad_maximum_fusion.1
  45.7 0.0 copy-done.2
  45.7 0.0 all-gather.5.cloned.1.call-update
  45.8 0.9 relay_pair.1
  46.7 4.2 %collective-permute-start.9 = (bf16[512,768]{1,0:T(8,128)(2,1)S(1)}, bf16[512,768]{1,0:T(8,128)(2,1)S(1)}, u32[]{:S(2)}, u32[]{:S(2)}) collective-permute-start(bf16[512,768]{1,0:T(8,128)(2,1)S(1)} %get-tuple-element.44.refs_4_), channel_id=1, source_target_pairs={{0,192},{64,0},{128,64},{192,128},{1,193},{65,1},{129,65},{193,129... | collective-permute-start | bytes 2359304 | tf_op jit(solution)/shard_map/weight_rings/ppermute | solution.py:23
  50.9 0.0 collective-permute-start.8
  50.9 1.2 collective-permute-start.10
  52.2 2.3 %collective-permute-start.11 = (bf16[128,768]{1,0:T(8,128)(2,1)S(1)}, bf16[128,768]{1,0:T(8,128)(2,1)S(1)}, u32[]{:S(2)}, u32[]{:S(2)}) collective-permute-start(bf16[128,768]{1,0:T(8,128)(2,1)S(1)} %get-tuple-element.46), channel_id=1, source_target_pairs={{0,48},{16,0},{32,16},{48,32},{1,49},{17,1},{33,17},{49,33},{2,50}... | collective-permute-start | bytes 589832 | tf_op jit(solution)/shard_map/weight_rings/ppermute | solution.py:23
  54.5 5.4 %collective-permute-done.10.refs_2_ = bf16[128,768]{1,0:T(8,128)(2,1)S(1)} collective-permute-done((bf16[128,768]{1,0:T(8,128)(2,1)S(1)}, bf16[128,768]{1,0:T(8,128)(2,1)S(1)}, u32[]{:S(2)}, u32[]{:S(2)}) %collective-permute-start.10) | collective-permute-done | bytes 196640 | tf_op jit(solution)/shard_map/weight_rings/ppermute | solution.py:23
  59.9 0.6 collective-permute-done.11.refs_3_
  60.5 7.4 %collective-permute-done.9.refs_1_.refs_9_ = bf16[512,768]{1,0:T(8,128)(2,1)S(1)} collective-permute-done((bf16[512,768]{1,0:T(8,128)(2,1)S(1)}, bf16[512,768]{1,0:T(8,128)(2,1)S(1)}, u32[]{:S(2)}, u32[]{:S(2)}) %collective-permute-start.9) | collective-permute-done | bytes 786464 | tf_op jit(solution)/shard_map/weight_rings/ppermute | solution.py:23
  67.8 3.7 %collective-permute-done.8.refs_0_.refs_7_ = bf16[512,768]{1,0:T(8,128)(2,1)S(1)} collective-permute-done((bf16[512,768]{1,0:T(8,128)(2,1)S(1)}, bf16[512,768]{1,0:T(8,128)(2,1)S(1)}, u32[]{:S(2)}, u32[]{:S(2)}) %collective-permute-start.8) | collective-permute-done | bytes 786464 | tf_op jit(solution)/shard_map/weight_rings/ppermute | solution.py:23
  71.6 1.4 %relay_far.1 = (bf16[256,768]{1,0:T(8,128)(2,1)}, bf16[256,768]{1,0:T(8,128)(2,1)}, bf16[256,768]{1,0:T(8,128)(2,1)}, bf16[256,768]{1,0:T(8,128)(2,1)}, bf16[256,768]{1,0:T(8,128)(2,1)}) custom-call(bf16[512,768]{1,0:T(8,128)(2,1)S(1)} %collective-permute-done.8.refs_0_.refs_7_, bf16[512,768]{1,0:T(8,128)(2,1)S(1)} %collective-permute-done.9.refs_1_.refs_9_, ...), custom_call_target="tpu_custom_call" | custom-call | bytes 2000000 | tf_op jit(solution)/shard_map/weight_rings/relay_far/pallas_call | solution.py:54
  72.9 0.1 collective-permute-start.12
  73.0 2.7 %collective-permute-start.13 = (bf16[256,768]{1,0:T(8,128)(2,1)}, bf16[256,768]{1,0:T(8,128)(2,1)}, u32[]{:S(2)}, u32[]{:S(2)}) collective-permute-start(bf16[256,768]{1,0:T(8,128)(2,1)} %get-tuple-element.57), channel_id=1, source_target_pairs={{0,192},{64,0},{128,64},{192,128},{1,193},{65,1},{129,65},{193,129... | collective-permute-start | bytes 1179656 | tf_op jit(solution)/shard_map/weight_rings/ppermute | solution.py:23
  75.7 0.6 collective-permute-start.14
  76.3 3.0 %collective-permute-start.15 = (bf16[256,768]{1,0:T(8,128)(2,1)}, bf16[256,768]{1,0:T(8,128)(2,1)}, u32[]{:S(2)}, u32[]{:S(2)}) collective-permute-start(bf16[256,768]{1,0:T(8,128)(2,1)} %get-tuple-element.59), channel_id=1, source_target_pairs={{0,48},{16,0},{32,16},{48,32},{1,49},{17,1},{33,17},{49,33},{2,50}... | collective-permute-start | bytes 1179656 | tf_op jit(solution)/shard_map/weight_rings/ppermute | solution.py:23
  79.3 0.0 collective-permute-start.16
  79.3 0.1 stack.23.refs_0_.pos
  79.4 1.7 %copy-done = bf16[2304,512]{1,0:T(8,128)(2,1)S(1)} copy-done((bf16[2304,512]{1,0:T(8,128)(2,1)S(1)}, bf16[2304,512]{1,0:T(8,128)(2,1)}, u32[]{:S(2)}) %copy-start) | copy-done | bytes 2359320
  81.0 1.6 %copy-done.1 = bf16[2048,512]{1,0:T(8,128)(2,1)S(1)} copy-done((bf16[2048,512]{1,0:T(8,128)(2,1)S(1)}, bf16[2048,512]{1,0:T(8,128)(2,1)}, u32[]{:S(2)}) %copy-start.1) | copy-done | bytes 2097176
  82.6 1.0 copy-done.3
  83.6 6.0 %project.1 = (f32[6,528,128]{2,1,0:T(8,128)S(1)}, bf16[528,1280]{1,0:T(8,128)(2,1)S(1)}) custom-call(s32[5]{0:T(128)S(1)} %stack.23.refs_0_.pos, bf16[2048,512]{1,0:T(8,128)(2,1)S(1)} %copy-done.1, bf16[2304,512]{1,0:T(8,128)(2,1)S(1)} %copy-done, bf16[256,768]{1,0:T(8,128)(2,1)S(1)} %pad_maximum_fusion.refs_3_, ...), custom_call_target="tpu_custom_call" | custom-call | flops 2283798528 | bytes 9000000 | tf_op jit(solution)/shard_map/project/pallas_call | solution.py:347
  89.7 3.8 %collective-permute-done.12.refs_2_ = bf16[256,768]{1,0:T(8,128)(2,1)} collective-permute-done((bf16[256,768]{1,0:T(8,128)(2,1)}, bf16[256,768]{1,0:T(8,128)(2,1)}, u32[]{:S(2)}, u32[]{:S(2)}) %collective-permute-start.12) | collective-permute-done | bytes 393248 | tf_op jit(solution)/shard_map/weight_rings/ppermute | solution.py:23
  93.5 0.0 collective-permute-done.13.refs_3_
  93.5 0.0 collective-permute-done.14.refs_4_
  93.5 0.0 collective-permute-done.15.refs_5_
  93.5 0.0 collective-permute-done.16.refs_6_
  93.6 0.0 copy-start.5
  93.6 0.0 copy-start.6
  93.6 0.0 copy-start.8
  93.6 0.0 copy-start.9
  93.6 5.1 %states.1 = (f32[64,8,256]{2,1,0:T(8,128)S(1)}, f32[2,528,128]{2,1,0:T(8,128)S(1)}, f32[16,16,256]{2,1,0:T(8,128)}) custom-call(s32[5]{0:T(128)S(1)} %stack.23.refs_0_.pos, bf16[528,1280]{1,0:T(8,128)(2,1)S(1)} %get-tuple-element.55.refs_1_, bf16[256,768]{1,0:T(8,128)(2,1)} %collective-permute-done.12.refs_2_, ...), custom_call_target="tpu_custom_call" | custom-call | tf_op jit(solution)/shard_map/states/pallas_call | solution.py:369
  98.8 3.7 %all-to-all-start = ((f32[16,16,256]{2,1,0:T(8,128)}), f32[16,16,256]{2,1,0:T(8,128)S(1)}, u32[]{:S(2)}, u32[]{:S(2)}) async-start(f32[16,16,256]{2,1,0:T(8,128)} %get-tuple-element.66), calls=%async_computation | async-start | bytes 524288 | tf_op jit(solution)/shard_map/state_exchange/all_to_all | solution.py:387
  102.5 2.5 %local.1 = (f32[64,8,256]{2,1,0:T(8,128)S(1)}, f32[64,8,256]{2,1,0:T(8,128)S(1)}, f32[16,8,256]{2,1,0:T(8,128)S(1)}) custom-call(s32[5]{0:T(128)S(1)} %stack.23.refs_0_.pos, f32[2,528,128]{2,1,0:T(8,128)S(1)} %get-tuple-element.61.gated, f32[3,3,512]{2,1,0:T(4,128)S(1)} %copy-done.8, f32[64,8,256]{2,1,0:T(8,128)S(1)} %get-tuple-element.62.product, ...), custom_call_target="tpu_custom_call" | custom-call | flops 30000000 | bytes 2000000 | tf_op jit(solution)/shard_map/local/pallas_call | solution.py:388
  105.0 8.1 %all-to-all-done.states = f32[16,16,256]{2,1,0:T(8,128)S(1)} async-done(((f32[16,16,256]{2,1,0:T(8,128)}), f32[16,16,256]{2,1,0:T(8,128)S(1)}, u32[]{:S(2)}, u32[]{:S(2)}) %all-to-all-start) | async-done | bytes 262176 | tf_op jit(solution)/shard_map/state_exchange/all_to_all | solution.py:387
  113.1 1.5 %finish.1 = (bf16[256,256]{1,0:T(8,128)(2,1)S(1)}, bf16[256,256]{1,0:T(8,128)(2,1)S(1)}) custom-call(s32[5]{0:T(128)S(1)} %stack.23.refs_0_.pos, f32[64,8,256]{2,1,0:T(8,128)S(1)} %get-tuple-element.63.gate, f32[64,8,256]{2,1,0:T(8,128)S(1)} %get-tuple-element.64.local, f32[16,8,256]{2,1,0:T(8,128)S(1)} %get-tuple-element.65.inside, ...), custom_call_target="tpu_custom_call" | custom-call | tf_op jit(solution)/shard_map/finish/pallas_call | solution.py:399
  114.6 6.2 %collective-permute-start.17 = (bf16[256,256]{1,0:T(8,128)(2,1)S(1)}, bf16[256,256]{1,0:T(8,128)(2,1)S(1)}, u32[]{:S(2)}, u32[]{:S(2)}) collective-permute-start(bf16[256,256]{1,0:T(8,128)(2,1)S(1)} %get-tuple-element.68), channel_id=1, source_target_pairs={{0,8},{8,0},{1,9},{9,1},{2,10},{10,2},{3,11},{11,3},{4,12},{12,4},... | collective-permute-start | bytes 393224 | tf_op jit(solution)/shard_map/result_swap/ppermute | solution.py:409
  120.8 1.0 collective-permute-done.17
  121.8 0.7 pad_maximum_fusion.3
  (21 shorter events, 0.2 us)
Async XLA Ops:
  6.5 72.8 %all-gather.3.cloned.1.call-start = ((), (), s32[]{:S(2)}) async-start(), calls=%async_computation.1 | async-start | bytes 2359296 | tf_op jit(solution)/shard_map/token_gather/all_gather | solution.py:305
  7.3 72.1 %all-gather.5.cloned.1.call-start = ((), (), s32[]{:S(2)}) async-start(), calls=%async_computation.2 | async-start | bytes 2654208 | tf_op jit(solution)/shard_map/token_gather/all_gather | solution.py:307
  8.5 6.3 %copy-start.10 = (bf16[256,512]{1,0:T(8,128)(2,1)S(1)}, bf16[256,512]{1,0:T(8,128)(2,1)}, u32[]{:S(2)}) copy-start(bf16[256,512]{1,0:T(8,128)(2,1)} %param.6) | copy-start | bytes 786436
  8.8 4.4 %collective-permute-start.1 = (bf16[128,768]{1,0:T(8,128)(2,1)S(1)}, bf16[128,768]{1,0:T(8,128)(2,1)S(1)}, u32[]{:S(2)}, u32[]{:S(2)}) collective-permute-start(bf16[128,768]{1,0:T(8,128)(2,1)S(1)} %bitcast.17), channel_id=1, source_target_pairs={{0,8},{8,0},{1,9},{9,1},{2,10},{10,2},{3,11},{11,3},{4,12},{12,4},... | collective-permute-start | bytes 589832 | tf_op jit(solution)/shard_map/weight_gather/ppermute | solution.py:290
  13.2 12.8 %collective-permute-start.3 = (bf16[256,768]{1,0:T(8,128)(2,1)S(1)}, bf16[256,768]{1,0:T(8,128)(2,1)S(1)}, u32[]{:S(2)}, u32[]{:S(2)}) collective-permute-start(bf16[256,768]{1,0:T(8,128)(2,1)S(1)} %pad_maximum_fusion.refs_3_), channel_id=1, source_target_pairs={{0,192},{64,0},{128,64},{192,128},{1,193},{65,1},{129,65},{193,129... | collective-permute-start | bytes 1179656 | tf_op jit(solution)/shard_map/weight_rings/ppermute | solution.py:23
  14.3 11.7 %collective-permute-start.2 = (bf16[256,768]{1,0:T(8,128)(2,1)S(1)}, bf16[256,768]{1,0:T(8,128)(2,1)S(1)}, u32[]{:S(2)}, u32[]{:S(2)}) collective-permute-start(bf16[256,768]{1,0:T(8,128)(2,1)S(1)} %pad_maximum_fusion.refs_3_), channel_id=1, source_target_pairs={{0,64},{64,128},{128,192},{192,0},{1,65},{65,129},{129,193},{193,1... | collective-permute-start | bytes 1179656 | tf_op jit(solution)/shard_map/weight_rings/ppermute | solution.py:23
  14.8 9.4 %collective-permute-start = (bf16[16,512]{1,0:T(8,128)(2,1)S(1)}, bf16[16,512]{1,0:T(8,128)(2,1)S(1)}, u32[]{:S(2)}, u32[]{:S(2)}) collective-permute-start(bf16[16,512]{1,0:T(8,128)(2,1)S(1)} %slice.3), channel_id=1, source_target_pairs={{8,16},{24,32},{40,48},{56,64},{72,80},{88,96},{104,112},{120,128}... | collective-permute-start | bytes 49160 | tf_op jit(solution)/shard_map/token_halo/ppermute | solution.py:294
  19.8 18.1 %collective-permute-start.7 = (bf16[256,768]{1,0:T(8,128)(2,1)S(1)}, bf16[256,768]{1,0:T(8,128)(2,1)S(1)}, u32[]{:S(2)}, u32[]{:S(2)}) collective-permute-start(bf16[256,768]{1,0:T(8,128)(2,1)S(1)} %pad_maximum_fusion.refs_3_), channel_id=1, source_target_pairs={{0,48},{16,0},{32,16},{48,32},{1,49},{17,1},{33,17},{49,33},{2,50}... | collective-permute-start | bytes 1179656 | tf_op jit(solution)/shard_map/weight_rings/ppermute | solution.py:23
  21.7 16.1 %collective-permute-start.6 = (bf16[256,768]{1,0:T(8,128)(2,1)S(1)}, bf16[256,768]{1,0:T(8,128)(2,1)S(1)}, u32[]{:S(2)}, u32[]{:S(2)}) collective-permute-start(bf16[256,768]{1,0:T(8,128)(2,1)S(1)} %pad_maximum_fusion.refs_3_), channel_id=1, source_target_pairs={{0,16},{16,32},{32,48},{48,0},{1,17},{17,33},{33,49},{49,1},{2,18}... | collective-permute-start | bytes 1179656 | tf_op jit(solution)/shard_map/weight_rings/ppermute | solution.py:23
  24.1 13.7 %collective-permute-start.5 = (bf16[256,768]{1,0:T(8,128)(2,1)S(1)}, bf16[256,768]{1,0:T(8,128)(2,1)S(1)}, u32[]{:S(2)}, u32[]{:S(2)}) collective-permute-start(bf16[256,768]{1,0:T(8,128)(2,1)S(1)} %pad_maximum_fusion.refs_3_), channel_id=1, source_target_pairs={{0,128},{64,192},{128,0},{192,64},{1,129},{65,193},{129,1},{193,65... | collective-permute-start | bytes 1179656 | tf_op jit(solution)/shard_map/weight_rings/ppermute | solution.py:23
  26.1 18.9 %collective-permute-start.4 = (bf16[272,512]{1,0:T(8,128)(2,1)S(1)}, bf16[272,512]{1,0:T(8,128)(2,1)S(1)}, u32[]{:S(2)}, u32[]{:S(2)}) collective-permute-start(bf16[272,512]{1,0:T(8,128)(2,1)S(1)} %pad_maximum_fusion.2), channel_id=1, source_target_pairs={{0,4},{4,0},{1,5},{5,1},{2,6},{6,2},{3,7},{7,3},{8,12},{12,8},{9,1... | collective-permute-start | bytes 835592 | tf_op jit(solution)/shard_map/token_swap/ppermute | solution.py:301
  37.8 7.9 %copy-start.2 = (bf16[256,768]{1,0:T(8,128)(2,1)}, bf16[256,768]{1,0:T(8,128)(2,1)S(1)}, u32[]{:S(2)}) copy-start(bf16[256,768]{1,0:T(8,128)(2,1)S(1)} %collective-permute-done.5.refs_10_) | copy-start | bytes 1179652
  46.7 21.1 %collective-permute-start.9 = (bf16[512,768]{1,0:T(8,128)(2,1)S(1)}, bf16[512,768]{1,0:T(8,128)(2,1)S(1)}, u32[]{:S(2)}, u32[]{:S(2)}) collective-permute-start(bf16[512,768]{1,0:T(8,128)(2,1)S(1)} %get-tuple-element.44.refs_4_), channel_id=1, source_target_pairs={{0,192},{64,0},{128,64},{192,128},{1,193},{65,1},{129,65},{193,129... | collective-permute-start | bytes 2359304 | tf_op jit(solution)/shard_map/weight_rings/ppermute | solution.py:23
  50.9 20.7 %collective-permute-start.8 = (bf16[512,768]{1,0:T(8,128)(2,1)S(1)}, bf16[512,768]{1,0:T(8,128)(2,1)S(1)}, u32[]{:S(2)}, u32[]{:S(2)}) collective-permute-start(bf16[512,768]{1,0:T(8,128)(2,1)S(1)} %get-tuple-element.44.refs_4_), channel_id=1, source_target_pairs={{0,64},{64,128},{128,192},{192,0},{1,65},{65,129},{129,193},{193,1... | collective-permute-start | bytes 2359304 | tf_op jit(solution)/shard_map/weight_rings/ppermute | solution.py:23
  50.9 9.0 %collective-permute-start.10 = (bf16[128,768]{1,0:T(8,128)(2,1)S(1)}, bf16[128,768]{1,0:T(8,128)(2,1)S(1)}, u32[]{:S(2)}, u32[]{:S(2)}) collective-permute-start(bf16[128,768]{1,0:T(8,128)(2,1)S(1)} %get-tuple-element.45), channel_id=1, source_target_pairs={{0,16},{16,32},{32,48},{48,0},{1,17},{17,33},{33,49},{49,1},{2,18}... | collective-permute-start | bytes 589832 | tf_op jit(solution)/shard_map/weight_rings/ppermute | solution.py:23
  52.2 8.3 %collective-permute-start.11 = (bf16[128,768]{1,0:T(8,128)(2,1)S(1)}, bf16[128,768]{1,0:T(8,128)(2,1)S(1)}, u32[]{:S(2)}, u32[]{:S(2)}) collective-permute-start(bf16[128,768]{1,0:T(8,128)(2,1)S(1)} %get-tuple-element.46), channel_id=1, source_target_pairs={{0,48},{16,0},{32,16},{48,32},{1,49},{17,1},{33,17},{49,33},{2,50}... | collective-permute-start | bytes 589832 | tf_op jit(solution)/shard_map/weight_rings/ppermute | solution.py:23
  72.9 20.6 %collective-permute-start.12 = (bf16[256,768]{1,0:T(8,128)(2,1)}, bf16[256,768]{1,0:T(8,128)(2,1)}, u32[]{:S(2)}, u32[]{:S(2)}) collective-permute-start(bf16[256,768]{1,0:T(8,128)(2,1)} %get-tuple-element.56), channel_id=1, source_target_pairs={{0,64},{64,128},{128,192},{192,0},{1,65},{65,129},{129,193},{193,1... | collective-permute-start | bytes 1179656 | tf_op jit(solution)/shard_map/weight_rings/ppermute | solution.py:23
  73.0 20.5 %collective-permute-start.13 = (bf16[256,768]{1,0:T(8,128)(2,1)}, bf16[256,768]{1,0:T(8,128)(2,1)}, u32[]{:S(2)}, u32[]{:S(2)}) collective-permute-start(bf16[256,768]{1,0:T(8,128)(2,1)} %get-tuple-element.57), channel_id=1, source_target_pairs={{0,192},{64,0},{128,64},{192,128},{1,193},{65,1},{129,65},{193,129... | collective-permute-start | bytes 1179656 | tf_op jit(solution)/shard_map/weight_rings/ppermute | solution.py:23
  75.7 17.8 %collective-permute-start.14 = (bf16[256,768]{1,0:T(8,128)(2,1)}, bf16[256,768]{1,0:T(8,128)(2,1)}, u32[]{:S(2)}, u32[]{:S(2)}) collective-permute-start(bf16[256,768]{1,0:T(8,128)(2,1)} %get-tuple-element.58), channel_id=1, source_target_pairs={{0,16},{16,32},{32,48},{48,0},{1,17},{17,33},{33,49},{49,1},{2,18}... | collective-permute-start | bytes 1179656 | tf_op jit(solution)/shard_map/weight_rings/ppermute | solution.py:23
  76.3 17.3 %collective-permute-start.15 = (bf16[256,768]{1,0:T(8,128)(2,1)}, bf16[256,768]{1,0:T(8,128)(2,1)}, u32[]{:S(2)}, u32[]{:S(2)}) collective-permute-start(bf16[256,768]{1,0:T(8,128)(2,1)} %get-tuple-element.59), channel_id=1, source_target_pairs={{0,48},{16,0},{32,16},{48,32},{1,49},{17,1},{33,17},{49,33},{2,50}... | collective-permute-start | bytes 1179656 | tf_op jit(solution)/shard_map/weight_rings/ppermute | solution.py:23
  79.3 14.3 %collective-permute-start.16 = (bf16[256,768]{1,0:T(8,128)(2,1)}, bf16[256,768]{1,0:T(8,128)(2,1)}, u32[]{:S(2)}, u32[]{:S(2)}) collective-permute-start(bf16[256,768]{1,0:T(8,128)(2,1)} %get-tuple-element.51.refs_5_), channel_id=1, source_target_pairs={{0,128},{64,192},{128,0},{192,64},{1,129},{65,193},{129,1},{193,65... | collective-permute-start | bytes 1179656 | tf_op jit(solution)/shard_map/weight_rings/ppermute | solution.py:23
  79.4 1.7 %copy-start = (bf16[2304,512]{1,0:T(8,128)(2,1)S(1)}, bf16[2304,512]{1,0:T(8,128)(2,1)}, u32[]{:S(2)}) copy-start(bf16[2304,512]{1,0:T(8,128)(2,1)} %all-gather.5.cloned.1.call-done.refs_2_) | copy-start | bytes 7077892
  81.0 1.6 %copy-start.1 = (bf16[2048,512]{1,0:T(8,128)(2,1)S(1)}, bf16[2048,512]{1,0:T(8,128)(2,1)}, u32[]{:S(2)}) copy-start(bf16[2048,512]{1,0:T(8,128)(2,1)} %all-gather.3.cloned.1.call-done.refs_1_) | copy-start | bytes 6291460
  82.6 1.0 copy-start.3
  83.6 9.9 %copy-start.4 = (f32[16,512]{1,0:T(8,128)S(1)}, f32[16,512]{1,0:T(8,128)}, u32[]{:S(2)}) copy-start(f32[16,512]{1,0:T(8,128)} %decay.3) | copy-start | bytes 98308
  83.6 9.9 %copy-start.7 = (f32[3,3,512]{2,1,0:T(4,128)S(1)}, f32[3,3,512]{2,1,0:T(4,128)}, u32[]{:S(2)}) copy-start(f32[3,3,512]{2,1,0:T(4,128)} %taps.1) | copy-start | bytes 55300
  93.6 8.9 %copy-start.5 = (f32[16,512]{1,0:T(8,128)S(1)}, f32[16,512]{1,0:T(8,128)}, u32[]{:S(2)}) copy-start(f32[16,512]{1,0:T(8,128)} %decay.3) | copy-start | bytes 98308
  93.6 8.9 %copy-start.6 = (f32[16,512]{1,0:T(8,128)S(1)}, f32[16,512]{1,0:T(8,128)}, u32[]{:S(2)}) copy-start(f32[16,512]{1,0:T(8,128)} %gain.3) | copy-start | bytes 98308
  93.6 8.9 %copy-start.8 = (f32[3,3,512]{2,1,0:T(4,128)S(1)}, f32[3,3,512]{2,1,0:T(4,128)}, u32[]{:S(2)}) copy-start(f32[3,3,512]{2,1,0:T(4,128)} %taps.1) | copy-start | bytes 55300
  93.6 8.9 %copy-start.9 = (f32[512]{0:T(512)S(1)}, f32[512]{0:T(512)}, u32[]{:S(2)}) copy-start(f32[512]{0:T(512)} %param.11) | copy-start | bytes 6148
  98.8 14.3 %all-to-all-start = ((f32[16,16,256]{2,1,0:T(8,128)}), f32[16,16,256]{2,1,0:T(8,128)S(1)}, u32[]{:S(2)}, u32[]{:S(2)}) async-start(f32[16,16,256]{2,1,0:T(8,128)} %get-tuple-element.66), calls=%async_computation | async-start | bytes 524288 | tf_op jit(solution)/shard_map/state_exchange/all_to_all | solution.py:387
  114.6 7.2 %collective-permute-start.17 = (bf16[256,256]{1,0:T(8,128)(2,1)S(1)}, bf16[256,256]{1,0:T(8,128)(2,1)S(1)}, u32[]{:S(2)}, u32[]{:S(2)}) collective-permute-start(bf16[256,256]{1,0:T(8,128)(2,1)S(1)} %get-tuple-element.68), channel_id=1, source_target_pairs={{0,8},{8,0},{1,9},{9,1},{2,10},{10,2},{3,11},{11,3},{4,12},{12,4},... | collective-permute-start | bytes 393224 | tf_op jit(solution)/shard_map/result_swap/ppermute | solution.py:409
Sparse Core Ops, SparseCore 0:
  9.2 31.8 all-gather.2
  45.9 30.2 all-gather.4

commit v15 on v12

--- a/solution.py
+++ b/solution.py
@@ -290,7 +290,8 @@
         theirs = lax.ppermute(lax.dynamic_index_in_dim(halves, 1 - c, 0, keepdims=False), "c", SWAP)
         own = in_order(c == 0, mine, theirs, 0)
     with jax.named_scope("token_swap"):
-        other = lax.ppermute(tokens, "l", SWAP)
+        both = lax.all_to_all(jnp.broadcast_to(tokens, (2, rows, group)), "l", 0, 0)
+        other = lax.dynamic_index_in_dim(both, 1 - lax.axis_index("l"), 0, keepdims=False)
     with jax.named_scope("weight_rings"):
         farther = shifted(own, "y", 2)
         far = both_ways(own, "y")

time: 122 us -> 127 us (1.041)
  waiting for transfers between devices: 31.6 us -> 44.9 us
  starting transfers between devices: 51.1 us -> 41.2 us
    ppermute x14, waiting for transfers between devices: 13.2 us -> 25.9 us  [shifted(): return lax.ppermute(array, axis, [(i, (i + step) % n) for i in range(n)])]
    all_to_all x0 -> x1, waiting for transfers between devices: none -> 7.6 us  [body(): both = lax.all_to_all(jnp.broadcast_to(tokens, (2, rows, group)), 'l', 0, 0)]
    ppermute x14, starting transfers between devices: 28.1 us -> 21 us  [shifted(): return lax.ppermute(array, axis, [(i, (i + step) % n) for i in range(n)])]
    all_to_all x1, starting transfers between devices: 9.28 us -> 3.53 us  [body(): states = lax.all_to_all(state, ('y', 'h'), 0, 0, tiled=True)]
    all_to_all x0 -> x1, starting transfers between devices: none -> 3.49 us  [body(): both = lax.all_to_all(jnp.broadcast_to(tokens, (2, rows, group)), 'l', 0, 0)]
    ppermute x1, waiting for transfers between devices: 3.44 us -> 1.49 us  [body(): halos = lax.ppermute(tails, CTX, [(i, i + 1) for i in range(1, 31, 2)])]
    ppermute x1 -> x0, waiting for transfers between devices: 1.95 us -> none  [body(): other = lax.ppermute(tokens, 'l', SWAP)]
    all_gather x1, waiting for transfers between devices: 1.7 us -> 0.01 us  [body(): swapped = lax.all_gather(wide, ('c', 'x'), axis=0, tiled=True)]
  transfers between devices with their start and end apart: 21 -> 21, of which waited for: 10 -> 10; matrix products, arithmetic and copies ran while one was open for 2% -> 3% of each run, Pallas kernels for 9% -> 9%
where the time goes in v15:
time: 127 us; the launch traced here: 126 us
  waiting for transfers between devices  44.9 us (35%)
  starting transfers between devices  41.2 us (32%)
  Pallas kernels  17.5 us (14%)
  between operations  13.7 us (11%)
  local copies, waits for them, and re-layouts  6.81 us (5%)
  other arithmetic  1.54 us (1%)
    ppermute x14, waiting for transfers between devices, shifted(): return lax.ppermute(array, axis, [(i, (i + step) % n) for i in range(n)])  25.9 us
    ppermute x14, starting transfers between devices, shifted(): return lax.ppermute(array, axis, [(i, (i + step) % n) for i in range(n)])  21 us
    all_to_all x1, waiting for transfers between devices, body(): states = lax.all_to_all(state, ('y', 'h'), 0, 0, tiled=True)  8.13 us
    all_to_all x1, waiting for transfers between devices, body(): both = lax.all_to_all(jnp.broadcast_to(tokens, (2, rows, group)), 'l', 0, 0)  7.6 us
    pallas_call x1, Pallas kernels, body(): pl.pallas_call(functools.partial(project_kernel, sizes, early_runs, late_...  6.05 us
    ppermute x1, starting transfers between devices, body(): halos = lax.ppermute(tails, CTX, [(i, i + 1) for i in range(1, 31, 2)])  5.78 us
    unnamed x23, local copies, waits for them, and re-layouts  5.51 us
    pallas_call x1, Pallas kernels, body(): pl.pallas_call(functools.partial(state_kernel, sizes), out_shape=(full, j...  5.13 us
  transfers between devices with their start and end apart: 21, of which 10 were waited for; matrix products, arithmetic and copies ran while one was open for 3% of the time, Pallas kernels for 9%

profile of v15, /device:TPU:1, one launch (start us, length us, event | category | flops | bytes accessed | tf_op | source)
XLA Modules:
  0.0 125.6 jit_solution(10788021227938452693)
XLA Ops:
  6.5 0.0 all-gather.3.cloned.1.call-start
  6.5 0.7 all-gather.3.cloned.1.call-update
  7.3 1.2 copy.10
  8.6 0.1 copy.13
  8.7 3.3 %collective-permute-start = (bf16[128,768]{1,0:T(8,128)(2,1)S(1)}, bf16[128,768]{1,0:T(8,128)(2,1)S(1)}, u32[]{:S(2)}, u32[]{:S(2)}) collective-permute-start(bf16[128,768]{1,0:T(8,128)(2,1)S(1)} %bitcast.19), channel_id=1, source_target_pairs={{0,8},{8,0},{1,9},{9,1},{2,10},{10,2},{3,11},{11,3},{4,12},{12,4},... | collective-permute-start | bytes 589832 | tf_op jit(solution)/shard_map/weight_gather/ppermute | solution.py:290
  12.0 0.8 broadcast_in_dim.3
  12.9 3.5 %all-to-all-start = ((bf16[2,256,512]{2,1,0:T(8,128)(2,1)}), bf16[2,256,512]{2,1,0:T(8,128)(2,1)S(1)}, u32[]{:S(2)}, u32[]{:S(2)}) async-start(bf16[2,256,512]{2,1,0:T(8,128)(2,1)} %broadcast_in_dim.3), calls=%async_computation | async-start | bytes 1048576 | tf_op jit(solution)/shard_map/token_swap/all_to_all | solution.py:293
  16.4 0.0 all-gather.5.cloned.1.call-start
  16.4 0.1 copy.12
  16.6 0.0 collective-permute-done
  16.7 1.1 collective-permute-start.2
  17.7 0.5 collective-permute-start.1
  18.2 5.6 %collective-permute-start.6 = (bf16[256,768]{1,0:T(8,128)(2,1)S(1)}, bf16[256,768]{1,0:T(8,128)(2,1)S(1)}, u32[]{:S(2)}, u32[]{:S(2)}) collective-permute-start(bf16[256,768]{1,0:T(8,128)(2,1)S(1)} %pad_maximum_fusion.refs_3_), channel_id=1, source_target_pairs={{0,48},{16,0},{32,16},{48,32},{1,49},{17,1},{33,17},{49,33},{2,50}... | collective-permute-start | bytes 1179656 | tf_op jit(solution)/shard_map/weight_rings/ppermute | solution.py:23
  23.8 0.0 collective-permute-start.5
  23.8 1.6 %collective-permute-start.4 = (bf16[256,768]{1,0:T(8,128)(2,1)S(1)}, bf16[256,768]{1,0:T(8,128)(2,1)S(1)}, u32[]{:S(2)}, u32[]{:S(2)}) collective-permute-start(bf16[256,768]{1,0:T(8,128)(2,1)S(1)} %pad_maximum_fusion.refs_3_), channel_id=1, source_target_pairs={{0,128},{64,192},{128,0},{192,64},{1,129},{65,193},{129,1},{193,65... | collective-permute-start | bytes 1179656 | tf_op jit(solution)/shard_map/weight_rings/ppermute | solution.py:23
  25.4 7.6 %all-to-all-done = bf16[2,256,512]{2,1,0:T(8,128)(2,1)S(1)} async-done(((bf16[2,256,512]{2,1,0:T(8,128)(2,1)}), bf16[2,256,512]{2,1,0:T(8,128)(2,1)S(1)}, u32[]{:S(2)}, u32[]{:S(2)}) %all-to-all-start) | async-done | bytes 524320 | tf_op jit(solution)/shard_map/token_swap/all_to_all | solution.py:293
  33.0 0.0 collective-permute-done.2.refs_8_
  33.1 4.8 %collective-permute-done.1.refs_6_ = bf16[256,768]{1,0:T(8,128)(2,1)S(1)} collective-permute-done((bf16[256,768]{1,0:T(8,128)(2,1)S(1)}, bf16[256,768]{1,0:T(8,128)(2,1)S(1)}, u32[]{:S(2)}, u32[]{:S(2)}) %collective-permute-start.1) | collective-permute-done | bytes 393248 | tf_op jit(solution)/shard_map/weight_rings/ppermute | solution.py:23
  37.9 5.8 %collective-permute-start.3 = (bf16[32,512]{1,0:T(8,128)(2,1)S(1)}, bf16[32,512]{1,0:T(8,128)(2,1)S(1)}, u32[]{:S(2)}, u32[]{:S(2)}) collective-permute-start(bf16[32,512]{1,0:T(8,128)(2,1)S(1)} %pad_maximum_fusion.3), channel_id=1, source_target_pairs={{8,16},{24,32},{40,48},{56,64},{72,80},{88,96},{104,112},{120,128}... | collective-permute-start | bytes 98312 | tf_op jit(solution)/shard_map/weight_rings/ppermute | solution.py:301
  43.7 0.0 collective-permute-done.6.refs_1_
  43.7 0.0 collective-permute-done.5.refs_0_
  43.7 0.0 collective-permute-done.4.refs_10_
  43.7 0.0 copy-start.2
  43.7 1.5 %collective-permute-done.3 = bf16[32,512]{1,0:T(8,128)(2,1)S(1)} collective-permute-done((bf16[32,512]{1,0:T(8,128)(2,1)S(1)}, bf16[32,512]{1,0:T(8,128)(2,1)S(1)}, u32[]{:S(2)}, u32[]{:S(2)}) %collective-permute-start.3) | collective-permute-done | bytes 32800 | tf_op jit(solution)/shard_map/weight_rings/ppermute | solution.py:301
  45.2 0.7 pad_maximum_fusion.1
  46.0 0.0 all-gather.5.cloned.1.call-update
  46.0 0.9 relay_pair.1
  46.9 2.4 %collective-permute-start.8 = (bf16[512,768]{1,0:T(8,128)(2,1)S(1)}, bf16[512,768]{1,0:T(8,128)(2,1)S(1)}, u32[]{:S(2)}, u32[]{:S(2)}) collective-permute-start(bf16[512,768]{1,0:T(8,128)(2,1)S(1)} %get-tuple-element.44.refs_4_), channel_id=1, source_target_pairs={{0,192},{64,0},{128,64},{192,128},{1,193},{65,1},{129,65},{193,129... | collective-permute-start | bytes 2359304 | tf_op jit(solution)/shard_map/weight_rings/ppermute | solution.py:23
  49.3 0.0 collective-permute-start.7
  49.3 2.8 %collective-permute-start.9 = (bf16[128,768]{1,0:T(8,128)(2,1)S(1)}, bf16[128,768]{1,0:T(8,128)(2,1)S(1)}, u32[]{:S(2)}, u32[]{:S(2)}) collective-permute-start(bf16[128,768]{1,0:T(8,128)(2,1)S(1)} %get-tuple-element.45), channel_id=1, source_target_pairs={{0,16},{16,32},{32,48},{48,0},{1,17},{17,33},{33,49},{49,1},{2,18}... | collective-permute-start | bytes 589832 | tf_op jit(solution)/shard_map/weight_rings/ppermute | solution.py:23
  52.1 0.8 collective-permute-start.10
  52.9 3.2 %collective-permute-done.9.refs_2_ = bf16[128,768]{1,0:T(8,128)(2,1)S(1)} collective-permute-done((bf16[128,768]{1,0:T(8,128)(2,1)S(1)}, bf16[128,768]{1,0:T(8,128)(2,1)S(1)}, u32[]{:S(2)}, u32[]{:S(2)}) %collective-permute-start.9) | collective-permute-done | bytes 196640 | tf_op jit(solution)/shard_map/weight_rings/ppermute | solution.py:23
  56.1 2.8 %collective-permute-done.10.refs_3_ = bf16[128,768]{1,0:T(8,128)(2,1)S(1)} collective-permute-done((bf16[128,768]{1,0:T(8,128)(2,1)S(1)}, bf16[128,768]{1,0:T(8,128)(2,1)S(1)}, u32[]{:S(2)}, u32[]{:S(2)}) %collective-permute-start.10) | collective-permute-done | bytes 196640 | tf_op jit(solution)/shard_map/weight_rings/ppermute | solution.py:23
  58.9 6.1 %collective-permute-done.8.refs_1_.refs_9_ = bf16[512,768]{1,0:T(8,128)(2,1)S(1)} collective-permute-done((bf16[512,768]{1,0:T(8,128)(2,1)S(1)}, bf16[512,768]{1,0:T(8,128)(2,1)S(1)}, u32[]{:S(2)}, u32[]{:S(2)}) %collective-permute-start.8) | collective-permute-done | bytes 786464 | tf_op jit(solution)/shard_map/weight_rings/ppermute | solution.py:23
  65.0 3.2 %collective-permute-done.7.refs_0_.refs_7_ = bf16[512,768]{1,0:T(8,128)(2,1)S(1)} collective-permute-done((bf16[512,768]{1,0:T(8,128)(2,1)S(1)}, bf16[512,768]{1,0:T(8,128)(2,1)S(1)}, u32[]{:S(2)}, u32[]{:S(2)}) %collective-permute-start.7) | collective-permute-done | bytes 786464 | tf_op jit(solution)/shard_map/weight_rings/ppermute | solution.py:23
  68.3 1.4 %relay_far.1 = (bf16[256,768]{1,0:T(8,128)(2,1)}, bf16[256,768]{1,0:T(8,128)(2,1)}, bf16[256,768]{1,0:T(8,128)(2,1)}, bf16[256,768]{1,0:T(8,128)(2,1)}, bf16[256,768]{1,0:T(8,128)(2,1)}) custom-call(bf16[512,768]{1,0:T(8,128)(2,1)S(1)} %collective-permute-done.7.refs_0_.refs_7_, bf16[512,768]{1,0:T(8,128)(2,1)S(1)} %collective-permute-done.8.refs_1_.refs_9_, ...), custom_call_target="tpu_custom_call" | custom-call | bytes 2000000 | tf_op jit(solution)/shard_map/weight_rings/relay_far/pallas_call | solution.py:54
  69.6 0.1 collective-permute-start.11
  69.7 2.7 %collective-permute-start.12 = (bf16[256,768]{1,0:T(8,128)(2,1)}, bf16[256,768]{1,0:T(8,128)(2,1)}, u32[]{:S(2)}, u32[]{:S(2)}) collective-permute-start(bf16[256,768]{1,0:T(8,128)(2,1)} %get-tuple-element.57), channel_id=1, source_target_pairs={{0,192},{64,0},{128,64},{192,128},{1,193},{65,1},{129,65},{193,129... | collective-permute-start | bytes 1179656 | tf_op jit(solution)/shard_map/weight_rings/ppermute | solution.py:23
  72.4 1.7 %collective-permute-start.13 = (bf16[256,768]{1,0:T(8,128)(2,1)}, bf16[256,768]{1,0:T(8,128)(2,1)}, u32[]{:S(2)}, u32[]{:S(2)}) collective-permute-start(bf16[256,768]{1,0:T(8,128)(2,1)} %get-tuple-element.58), channel_id=1, source_target_pairs={{0,16},{16,32},{32,48},{48,0},{1,17},{17,33},{33,49},{49,1},{2,18}... | collective-permute-start | bytes 1179656 | tf_op jit(solution)/shard_map/weight_rings/ppermute | solution.py:23
  74.1 1.8 %collective-permute-start.14 = (bf16[256,768]{1,0:T(8,128)(2,1)}, bf16[256,768]{1,0:T(8,128)(2,1)}, u32[]{:S(2)}, u32[]{:S(2)}) collective-permute-start(bf16[256,768]{1,0:T(8,128)(2,1)} %get-tuple-element.59), channel_id=1, source_target_pairs={{0,48},{16,0},{32,16},{48,32},{1,49},{17,1},{33,17},{49,33},{2,50}... | collective-permute-start | bytes 1179656 | tf_op jit(solution)/shard_map/weight_rings/ppermute | solution.py:23
  76.0 0.0 collective-permute-start.15
  76.0 0.1 stack.23.refs_0_.pos
  76.1 1.7 %copy-done = bf16[2304,512]{1,0:T(8,128)(2,1)S(1)} copy-done((bf16[2304,512]{1,0:T(8,128)(2,1)S(1)}, bf16[2304,512]{1,0:T(8,128)(2,1)}, u32[]{:S(2)}) %copy-start) | copy-done | bytes 2359320
  77.7 1.6 %copy-done.1 = bf16[2048,512]{1,0:T(8,128)(2,1)S(1)} copy-done((bf16[2048,512]{1,0:T(8,128)(2,1)S(1)}, bf16[2048,512]{1,0:T(8,128)(2,1)}, u32[]{:S(2)}) %copy-start.1) | copy-done | bytes 2097176
  79.3 1.0 copy-done.3
  80.3 6.0 %project.1 = (f32[6,528,128]{2,1,0:T(8,128)S(1)}, bf16[528,1280]{1,0:T(8,128)(2,1)S(1)}) custom-call(s32[5]{0:T(128)S(1)} %stack.23.refs_0_.pos, bf16[2048,512]{1,0:T(8,128)(2,1)S(1)} %copy-done.1, bf16[2304,512]{1,0:T(8,128)(2,1)S(1)} %copy-done, bf16[256,768]{1,0:T(8,128)(2,1)S(1)} %pad_maximum_fusion.refs_3_, ...), custom_call_target="tpu_custom_call" | custom-call | flops 2283798528 | bytes 9000000 | tf_op jit(solution)/shard_map/project/pallas_call | solution.py:347
  86.4 0.0 collective-permute-done.11.refs_2_
  86.4 0.0 collective-permute-done.12.refs_3_
  86.4 5.7 %collective-permute-done.13.refs_4_ = bf16[256,768]{1,0:T(8,128)(2,1)} collective-permute-done((bf16[256,768]{1,0:T(8,128)(2,1)}, bf16[256,768]{1,0:T(8,128)(2,1)}, u32[]{:S(2)}, u32[]{:S(2)}) %collective-permute-start.13) | collective-permute-done | bytes 393248 | tf_op jit(solution)/shard_map/weight_rings/ppermute | solution.py:23
  92.1 0.0 collective-permute-done.14.refs_5_
  92.1 0.0 collective-permute-done.15.refs_6_
  92.1 0.0 copy-done.4
  92.1 0.0 copy-start.5
  92.2 0.0 copy-start.6
  92.2 0.0 copy-start.8
  92.2 0.0 copy-start.9
  92.2 5.1 %states.1 = (f32[64,8,256]{2,1,0:T(8,128)S(1)}, f32[2,528,128]{2,1,0:T(8,128)S(1)}, f32[16,16,256]{2,1,0:T(8,128)}) custom-call(s32[5]{0:T(128)S(1)} %stack.23.refs_0_.pos, bf16[528,1280]{1,0:T(8,128)(2,1)S(1)} %get-tuple-element.55.refs_1_, bf16[256,768]{1,0:T(8,128)(2,1)} %collective-permute-done.11.refs_2_, ...), custom_call_target="tpu_custom_call" | custom-call | tf_op jit(solution)/shard_map/states/pallas_call | solution.py:369
  97.3 3.5 %all-to-all-start.1 = ((f32[16,16,256]{2,1,0:T(8,128)}), f32[16,16,256]{2,1,0:T(8,128)S(1)}, u32[]{:S(2)}, u32[]{:S(2)}) async-start(f32[16,16,256]{2,1,0:T(8,128)} %get-tuple-element.66), calls=%async_computation.1 | async-start | bytes 524288 | tf_op jit(solution)/shard_map/state_exchange/all_to_all | solution.py:387
  100.9 2.5 %local.1 = (f32[64,8,256]{2,1,0:T(8,128)S(1)}, f32[64,8,256]{2,1,0:T(8,128)S(1)}, f32[16,8,256]{2,1,0:T(8,128)S(1)}) custom-call(s32[5]{0:T(128)S(1)} %stack.23.refs_0_.pos, f32[2,528,128]{2,1,0:T(8,128)S(1)} %get-tuple-element.61.gated, f32[3,3,512]{2,1,0:T(4,128)S(1)} %copy-done.8, f32[64,8,256]{2,1,0:T(8,128)S(1)} %get-tuple-element.62.product, ...), custom_call_target="tpu_custom_call" | custom-call | flops 30000000 | bytes 2000000 | tf_op jit(solution)/shard_map/local/pallas_call | solution.py:388
  103.4 8.1 %all-to-all-done.1.states = f32[16,16,256]{2,1,0:T(8,128)S(1)} async-done(((f32[16,16,256]{2,1,0:T(8,128)}), f32[16,16,256]{2,1,0:T(8,128)S(1)}, u32[]{:S(2)}, u32[]{:S(2)}) %all-to-all-start.1) | async-done | bytes 262176 | tf_op jit(solution)/shard_map/state_exchange/all_to_all | solution.py:387
  111.5 1.5 %finish.1 = (bf16[256,256]{1,0:T(8,128)(2,1)S(1)}, bf16[256,256]{1,0:T(8,128)(2,1)S(1)}) custom-call(s32[5]{0:T(128)S(1)} %stack.23.refs_0_.pos, f32[64,8,256]{2,1,0:T(8,128)S(1)} %get-tuple-element.63.gate, f32[64,8,256]{2,1,0:T(8,128)S(1)} %get-tuple-element.64.local, f32[16,8,256]{2,1,0:T(8,128)S(1)} %get-tuple-element.65.inside, ...), custom_call_target="tpu_custom_call" | custom-call | tf_op jit(solution)/shard_map/finish/pallas_call | solution.py:399
  113.0 4.0 %collective-permute-start.16 = (bf16[256,256]{1,0:T(8,128)(2,1)S(1)}, bf16[256,256]{1,0:T(8,128)(2,1)S(1)}, u32[]{:S(2)}, u32[]{:S(2)}) collective-permute-start(bf16[256,256]{1,0:T(8,128)(2,1)S(1)} %get-tuple-element.68), channel_id=1, source_target_pairs={{0,8},{8,0},{1,9},{9,1},{2,10},{10,2},{3,11},{11,3},{4,12},{12,4},... | collective-permute-start | bytes 393224 | tf_op jit(solution)/shard_map/result_swap/ppermute | solution.py:409
  117.1 1.0 collective-permute-done.16
  118.1 0.7 pad_maximum_fusion.2
  (24 shorter events, 0.2 us)
Async XLA Ops:
  6.5 5.5 %copy-start.10 = (bf16[256,512]{1,0:T(8,128)(2,1)S(1)}, bf16[256,512]{1,0:T(8,128)(2,1)}, u32[]{:S(2)}) copy-start(bf16[256,512]{1,0:T(8,128)(2,1)} %param.6) | copy-start | bytes 786436
  6.5 69.5 %all-gather.3.cloned.1.call-start = ((), (), s32[]{:S(2)}) async-start(), calls=%async_computation.2 | async-start | bytes 2359296 | tf_op jit(solution)/shard_map/token_gather/all_gather | solution.py:305
  8.7 7.9 %collective-permute-start = (bf16[128,768]{1,0:T(8,128)(2,1)S(1)}, bf16[128,768]{1,0:T(8,128)(2,1)S(1)}, u32[]{:S(2)}, u32[]{:S(2)}) collective-permute-start(bf16[128,768]{1,0:T(8,128)(2,1)S(1)} %bitcast.19), channel_id=1, source_target_pairs={{0,8},{8,0},{1,9},{9,1},{2,10},{10,2},{3,11},{11,3},{4,12},{12,4},... | collective-permute-start | bytes 589832 | tf_op jit(solution)/shard_map/weight_gather/ppermute | solution.py:290
  12.9 20.1 %all-to-all-start = ((bf16[2,256,512]{2,1,0:T(8,128)(2,1)}), bf16[2,256,512]{2,1,0:T(8,128)(2,1)S(1)}, u32[]{:S(2)}, u32[]{:S(2)}) async-start(bf16[2,256,512]{2,1,0:T(8,128)(2,1)} %broadcast_in_dim.3), calls=%async_computation | async-start | bytes 1048576 | tf_op jit(solution)/shard_map/token_swap/all_to_all | solution.py:293
  16.4 59.7 %all-gather.5.cloned.1.call-start = ((), (), s32[]{:S(2)}) async-start(), calls=%async_computation.3 | async-start | bytes 2654208 | tf_op jit(solution)/shard_map/token_gather/all_gather | solution.py:307
  16.7 16.4 %collective-permute-start.2 = (bf16[256,768]{1,0:T(8,128)(2,1)S(1)}, bf16[256,768]{1,0:T(8,128)(2,1)S(1)}, u32[]{:S(2)}, u32[]{:S(2)}) collective-permute-start(bf16[256,768]{1,0:T(8,128)(2,1)S(1)} %pad_maximum_fusion.refs_3_), channel_id=1, source_target_pairs={{0,192},{64,0},{128,64},{192,128},{1,193},{65,1},{129,65},{193,129... | collective-permute-start | bytes 1179656 | tf_op jit(solution)/shard_map/weight_rings/ppermute | solution.py:23
  17.7 20.2 %collective-permute-start.1 = (bf16[256,768]{1,0:T(8,128)(2,1)S(1)}, bf16[256,768]{1,0:T(8,128)(2,1)S(1)}, u32[]{:S(2)}, u32[]{:S(2)}) collective-permute-start(bf16[256,768]{1,0:T(8,128)(2,1)S(1)} %pad_maximum_fusion.refs_3_), channel_id=1, source_target_pairs={{0,64},{64,128},{128,192},{192,0},{1,65},{65,129},{129,193},{193,1... | collective-permute-start | bytes 1179656 | tf_op jit(solution)/shard_map/weight_rings/ppermute | solution.py:23
  18.2 25.5 %collective-permute-start.6 = (bf16[256,768]{1,0:T(8,128)(2,1)S(1)}, bf16[256,768]{1,0:T(8,128)(2,1)S(1)}, u32[]{:S(2)}, u32[]{:S(2)}) collective-permute-start(bf16[256,768]{1,0:T(8,128)(2,1)S(1)} %pad_maximum_fusion.refs_3_), channel_id=1, source_target_pairs={{0,48},{16,0},{32,16},{48,32},{1,49},{17,1},{33,17},{49,33},{2,50}... | collective-permute-start | bytes 1179656 | tf_op jit(solution)/shard_map/weight_rings/ppermute | solution.py:23
  23.8 19.9 %collective-permute-start.5 = (bf16[256,768]{1,0:T(8,128)(2,1)S(1)}, bf16[256,768]{1,0:T(8,128)(2,1)S(1)}, u32[]{:S(2)}, u32[]{:S(2)}) collective-permute-start(bf16[256,768]{1,0:T(8,128)(2,1)S(1)} %pad_maximum_fusion.refs_3_), channel_id=1, source_target_pairs={{0,16},{16,32},{32,48},{48,0},{1,17},{17,33},{33,49},{49,1},{2,18}... | collective-permute-start | bytes 1179656 | tf_op jit(solution)/shard_map/weight_rings/ppermute | solution.py:23
  23.8 20.0 %collective-permute-start.4 = (bf16[256,768]{1,0:T(8,128)(2,1)S(1)}, bf16[256,768]{1,0:T(8,128)(2,1)S(1)}, u32[]{:S(2)}, u32[]{:S(2)}) collective-permute-start(bf16[256,768]{1,0:T(8,128)(2,1)S(1)} %pad_maximum_fusion.refs_3_), channel_id=1, source_target_pairs={{0,128},{64,192},{128,0},{192,64},{1,129},{65,193},{129,1},{193,65... | collective-permute-start | bytes 1179656 | tf_op jit(solution)/shard_map/weight_rings/ppermute | solution.py:23
  37.9 7.3 %collective-permute-start.3 = (bf16[32,512]{1,0:T(8,128)(2,1)S(1)}, bf16[32,512]{1,0:T(8,128)(2,1)S(1)}, u32[]{:S(2)}, u32[]{:S(2)}) collective-permute-start(bf16[32,512]{1,0:T(8,128)(2,1)S(1)} %pad_maximum_fusion.3), channel_id=1, source_target_pairs={{8,16},{24,32},{40,48},{56,64},{72,80},{88,96},{104,112},{120,128}... | collective-permute-start | bytes 98312 | tf_op jit(solution)/shard_map/weight_rings/ppermute | solution.py:301
  43.7 2.2 %copy-start.2 = (bf16[256,768]{1,0:T(8,128)(2,1)}, bf16[256,768]{1,0:T(8,128)(2,1)S(1)}, u32[]{:S(2)}) copy-start(bf16[256,768]{1,0:T(8,128)(2,1)S(1)} %collective-permute-done.4.refs_10_) | copy-start | bytes 1179652
  46.9 18.1 %collective-permute-start.8 = (bf16[512,768]{1,0:T(8,128)(2,1)S(1)}, bf16[512,768]{1,0:T(8,128)(2,1)S(1)}, u32[]{:S(2)}, u32[]{:S(2)}) collective-permute-start(bf16[512,768]{1,0:T(8,128)(2,1)S(1)} %get-tuple-element.44.refs_4_), channel_id=1, source_target_pairs={{0,192},{64,0},{128,64},{192,128},{1,193},{65,1},{129,65},{193,129... | collective-permute-start | bytes 2359304 | tf_op jit(solution)/shard_map/weight_rings/ppermute | solution.py:23
  49.3 18.9 %collective-permute-start.7 = (bf16[512,768]{1,0:T(8,128)(2,1)S(1)}, bf16[512,768]{1,0:T(8,128)(2,1)S(1)}, u32[]{:S(2)}, u32[]{:S(2)}) collective-permute-start(bf16[512,768]{1,0:T(8,128)(2,1)S(1)} %get-tuple-element.44.refs_4_), channel_id=1, source_target_pairs={{0,64},{64,128},{128,192},{192,0},{1,65},{65,129},{129,193},{193,1... | collective-permute-start | bytes 2359304 | tf_op jit(solution)/shard_map/weight_rings/ppermute | solution.py:23
  49.3 6.8 %collective-permute-start.9 = (bf16[128,768]{1,0:T(8,128)(2,1)S(1)}, bf16[128,768]{1,0:T(8,128)(2,1)S(1)}, u32[]{:S(2)}, u32[]{:S(2)}) collective-permute-start(bf16[128,768]{1,0:T(8,128)(2,1)S(1)} %get-tuple-element.45), channel_id=1, source_target_pairs={{0,16},{16,32},{32,48},{48,0},{1,17},{17,33},{33,49},{49,1},{2,18}... | collective-permute-start | bytes 589832 | tf_op jit(solution)/shard_map/weight_rings/ppermute | solution.py:23
  52.1 6.8 %collective-permute-start.10 = (bf16[128,768]{1,0:T(8,128)(2,1)S(1)}, bf16[128,768]{1,0:T(8,128)(2,1)S(1)}, u32[]{:S(2)}, u32[]{:S(2)}) collective-permute-start(bf16[128,768]{1,0:T(8,128)(2,1)S(1)} %get-tuple-element.46), channel_id=1, source_target_pairs={{0,48},{16,0},{32,16},{48,32},{1,49},{17,1},{33,17},{49,33},{2,50}... | collective-permute-start | bytes 589832 | tf_op jit(solution)/shard_map/weight_rings/ppermute | solution.py:23
  69.6 16.7 %collective-permute-start.11 = (bf16[256,768]{1,0:T(8,128)(2,1)}, bf16[256,768]{1,0:T(8,128)(2,1)}, u32[]{:S(2)}, u32[]{:S(2)}) collective-permute-start(bf16[256,768]{1,0:T(8,128)(2,1)} %get-tuple-element.56), channel_id=1, source_target_pairs={{0,64},{64,128},{128,192},{192,0},{1,65},{65,129},{129,193},{193,1... | collective-permute-start | bytes 1179656 | tf_op jit(solution)/shard_map/weight_rings/ppermute | solution.py:23
  69.7 16.7 %collective-permute-start.12 = (bf16[256,768]{1,0:T(8,128)(2,1)}, bf16[256,768]{1,0:T(8,128)(2,1)}, u32[]{:S(2)}, u32[]{:S(2)}) collective-permute-start(bf16[256,768]{1,0:T(8,128)(2,1)} %get-tuple-element.57), channel_id=1, source_target_pairs={{0,192},{64,0},{128,64},{192,128},{1,193},{65,1},{129,65},{193,129... | collective-permute-start | bytes 1179656 | tf_op jit(solution)/shard_map/weight_rings/ppermute | solution.py:23
  72.4 19.7 %collective-permute-start.13 = (bf16[256,768]{1,0:T(8,128)(2,1)}, bf16[256,768]{1,0:T(8,128)(2,1)}, u32[]{:S(2)}, u32[]{:S(2)}) collective-permute-start(bf16[256,768]{1,0:T(8,128)(2,1)} %get-tuple-element.58), channel_id=1, source_target_pairs={{0,16},{16,32},{32,48},{48,0},{1,17},{17,33},{33,49},{49,1},{2,18}... | collective-permute-start | bytes 1179656 | tf_op jit(solution)/shard_map/weight_rings/ppermute | solution.py:23
  74.1 18.0 %collective-permute-start.14 = (bf16[256,768]{1,0:T(8,128)(2,1)}, bf16[256,768]{1,0:T(8,128)(2,1)}, u32[]{:S(2)}, u32[]{:S(2)}) collective-permute-start(bf16[256,768]{1,0:T(8,128)(2,1)} %get-tuple-element.59), channel_id=1, source_target_pairs={{0,48},{16,0},{32,16},{48,32},{1,49},{17,1},{33,17},{49,33},{2,50}... | collective-permute-start | bytes 1179656 | tf_op jit(solution)/shard_map/weight_rings/ppermute | solution.py:23
  76.0 16.2 %collective-permute-start.15 = (bf16[256,768]{1,0:T(8,128)(2,1)}, bf16[256,768]{1,0:T(8,128)(2,1)}, u32[]{:S(2)}, u32[]{:S(2)}) collective-permute-start(bf16[256,768]{1,0:T(8,128)(2,1)} %get-tuple-element.51.refs_5_), channel_id=1, source_target_pairs={{0,128},{64,192},{128,0},{192,64},{1,129},{65,193},{129,1},{193,65... | collective-permute-start | bytes 1179656 | tf_op jit(solution)/shard_map/weight_rings/ppermute | solution.py:23
  76.1 1.7 %copy-start = (bf16[2304,512]{1,0:T(8,128)(2,1)S(1)}, bf16[2304,512]{1,0:T(8,128)(2,1)}, u32[]{:S(2)}) copy-start(bf16[2304,512]{1,0:T(8,128)(2,1)} %all-gather.5.cloned.1.call-done.refs_2_) | copy-start | bytes 7077892
  77.7 1.6 %copy-start.1 = (bf16[2048,512]{1,0:T(8,128)(2,1)S(1)}, bf16[2048,512]{1,0:T(8,128)(2,1)}, u32[]{:S(2)}) copy-start(bf16[2048,512]{1,0:T(8,128)(2,1)} %all-gather.3.cloned.1.call-done.refs_1_) | copy-start | bytes 6291460
  79.3 1.0 copy-start.3
  80.3 11.8 %copy-start.4 = (f32[16,512]{1,0:T(8,128)S(1)}, f32[16,512]{1,0:T(8,128)}, u32[]{:S(2)}) copy-start(f32[16,512]{1,0:T(8,128)} %decay.3) | copy-start | bytes 98308
  80.3 11.8 %copy-start.7 = (f32[3,3,512]{2,1,0:T(4,128)S(1)}, f32[3,3,512]{2,1,0:T(4,128)}, u32[]{:S(2)}) copy-start(f32[3,3,512]{2,1,0:T(4,128)} %taps.1) | copy-start | bytes 55300
  92.1 8.7 %copy-start.5 = (f32[16,512]{1,0:T(8,128)S(1)}, f32[16,512]{1,0:T(8,128)}, u32[]{:S(2)}) copy-start(f32[16,512]{1,0:T(8,128)} %decay.3) | copy-start | bytes 98308
  92.2 8.7 %copy-start.6 = (f32[16,512]{1,0:T(8,128)S(1)}, f32[16,512]{1,0:T(8,128)}, u32[]{:S(2)}) copy-start(f32[16,512]{1,0:T(8,128)} %gain.3) | copy-start | bytes 98308
  92.2 8.7 %copy-start.8 = (f32[3,3,512]{2,1,0:T(4,128)S(1)}, f32[3,3,512]{2,1,0:T(4,128)}, u32[]{:S(2)}) copy-start(f32[3,3,512]{2,1,0:T(4,128)} %taps.1) | copy-start | bytes 55300
  92.2 8.7 %copy-start.9 = (f32[512]{0:T(512)S(1)}, f32[512]{0:T(512)}, u32[]{:S(2)}) copy-start(f32[512]{0:T(512)} %param.11) | copy-start | bytes 6148
  97.3 14.2 %all-to-all-start.1 = ((f32[16,16,256]{2,1,0:T(8,128)}), f32[16,16,256]{2,1,0:T(8,128)S(1)}, u32[]{:S(2)}, u32[]{:S(2)}) async-start(f32[16,16,256]{2,1,0:T(8,128)} %get-tuple-element.66), calls=%async_computation.1 | async-start | bytes 524288 | tf_op jit(solution)/shard_map/state_exchange/all_to_all | solution.py:387
  113.0 5.0 %collective-permute-start.16 = (bf16[256,256]{1,0:T(8,128)(2,1)S(1)}, bf16[256,256]{1,0:T(8,128)(2,1)S(1)}, u32[]{:S(2)}, u32[]{:S(2)}) collective-permute-start(bf16[256,256]{1,0:T(8,128)(2,1)S(1)} %get-tuple-element.68), channel_id=1, source_target_pairs={{0,8},{8,0},{1,9},{9,1},{2,10},{10,2},{3,11},{11,3},{4,12},{12,4},... | collective-permute-start | bytes 393224 | tf_op jit(solution)/shard_map/result_swap/ppermute | solution.py:409
Sparse Core Ops, SparseCore 0:
  9.2 31.8 all-gather.2
  46.1 29.5 all-gather.4

commit v16 on v12

--- a/solution.py
+++ b/solution.py
@@ -123,17 +123,17 @@
 
 def late_products(sizes, signals, late_tok, pieces, sums, acc):
     rows, depth, width, modes, seq = sizes
-    k = depth // 16
     first, last = signals
     halves = width // 128
 
     @pl.loop(first, last)
     def _(j):
         cols = pl.ds(pl.multiple_of(j * width, width), width)
-        part = sum(
-            jnp.dot(late_tok[:, i * k : i * k + k], piece[:, cols], preferred_element_type=F32)
-            for i, piece in enumerate(pieces)
-        )
+        part, at = 0.0, 0
+        for piece in pieces:
+            n = piece.shape[0]
+            part += jnp.dot(late_tok[:, at : at + n], piece[:, cols], preferred_element_type=F32)
+            at += n
         for lh in range(halves):
             new = part[:, lh * 128 : lh * 128 + 128]
             acc[(j - first) * halves + lh] = (sums[j * halves + lh] + new).astype(BF16).astype(F32)
@@ -292,14 +292,13 @@
     with jax.named_scope("token_swap"):
         other = lax.ppermute(tokens, "l", SWAP)
     with jax.named_scope("weight_rings"):
-        farther = shifted(own, "y", 2)
         far = both_ways(own, "y")
         beside = both_ways(own, "h")
         other, far = tie((other, far))
         tails = jnp.concatenate([tokens[rows - HALO :], other[rows - HALO :]], 0)
         halos = lax.ppermute(tails, CTX, [(i, i + 1) for i in range(1, 31, 2)])
-    first = (halos, other, farther, far, beside)
-    halos, other, farther, far, beside = tie(first)
+    first = (halos, other, far, beside)
+    halos, other, far, beside = tie(first)
     with jax.named_scope("token_gather"):
         near = lax.all_gather(tokens, ("c", "x"), axis=0, tiled=True)
         wide = jnp.concatenate([halos, other], 0)
@@ -315,7 +314,10 @@
         moves += [(side, 0, half, 2, side * half) for side in range(2)]
         moves += [(side, two + half, half, 3, side * half) for side in range(2)]
         moves += [(2 + side, 0, half, 4, side * half) for side in range(2)]
-        behind, ahead, firsts, seconds, opposite = relayed([*far_pair, *opposite], moves, "relay_far")
+        moves += [(4 + side, side * half, half, side, two) for side in range(2)]
+        behind, ahead, firsts, seconds, opposite = relayed(
+            [*far_pair, *opposite, *far], moves, "relay_far"
+        )
         last = shifted(opposite, "y", 2)
         farther_pair = shifted(behind, "y", 1), shifted(ahead, "y", -1)
         far_opposite = shifted(firsts, "h", 1), shifted(seconds, "h", -1)
@@ -325,10 +327,8 @@
     for side, dy in enumerate((1, -1)):
         early += [far[side], far_pair[side]]
         early_runs += [(dy, dh, 0, two) for dh in (0, 1, -1)]
-    early += [farther]
-    early_runs += [(2, 0, 0, two)]
     late = [*farther_pair, *far_opposite, last]
-    late_runs = [(2, 1, 0, two), (2, -1, 0, two)]
+    late_runs = [(2, 1, 0, two), (2, 0, 0, half), (2, -1, 0, two), (2, 0, half, half)]
     late_runs += [(dy, 2, skip, half) for skip in (0, half) for dy in (1, -1)]
     late_runs += [(2, 2, 0, two)]
 
@@ -347,20 +347,20 @@
         functools.partial(project_kernel, sizes, early_runs, late_runs),
         out_shape=(
             jax.ShapeDtypeStruct(chunks, F32),
-            jax.ShapeDtypeStruct((lines, 5 * two), BF16),
+            jax.ShapeDtypeStruct((lines, 6 * two), BF16),
         ),
         in_specs=[smem] + [hbm] * (2 + len(early)),
         out_specs=(vmem, vmem),
         scratch_shapes=[
-            pltpu.VMEM((lines, 11 * two), BF16),
-            pltpu.VMEM((11 * two, 3 * width), BF16),
+            pltpu.VMEM((lines, 10 * two), BF16),
+            pltpu.VMEM((10 * two, 3 * width), BF16),
             dma(3 * len(early_runs)),
             dma(3 * len(late_runs)),
             dma(len(early)),
         ],
         compiler_params=pltpu.CompilerParams(vmem_limit_bytes=14 * 2**20),
         cost_estimate=pl.CostEstimate(
-            flops=2 * lines * 11 * two * 3 * width, bytes_accessed=9_000_000, transcendentals=0
+            flops=2 * lines * 10 * two * 3 * width, bytes_accessed=9_000_000, transcendentals=0
         ),
         name="project",
     )(pos, near, swapped, *early)

time: 122 us -> 128 us (1.049)
  waiting for transfers between devices: 31.6 us -> 48.4 us
  starting transfers between devices: 51.1 us -> 40.6 us
    ppermute x14 -> x13, waiting for transfers between devices: 13.2 us -> 28.7 us  [shifted(): return lax.ppermute(array, axis, [(i, (i + step) % n) for i in range(n)])]
    ppermute x14 -> x13, starting transfers between devices: 28.1 us -> 18.9 us  [shifted(): return lax.ppermute(array, axis, [(i, (i + step) % n) for i in range(n)])]
    ppermute x1, waiting for transfers between devices: 1.95 us -> 9.11 us  [body(): other = lax.ppermute(tokens, 'l', SWAP)]
    all_to_all x1, starting transfers between devices: 9.28 us -> 4.58 us  [body(): states = lax.all_to_all(state, ('y', 'h'), 0, 0, tiled=True)]
    ppermute x1, waiting for transfers between devices: 3.44 us -> 0.01 us  [body(): halos = lax.ppermute(tails, CTX, [(i, i + 1) for i in range(1, 31, 2)])]
    ppermute x1, starting transfers between devices: 3.49 us -> 5.42 us  [body(): return in_order(c == 0, mine, lax.ppermute(theirs, 'c', SWAP), 1)]
    all_gather x1, waiting for transfers between devices: 1.7 us -> 0.01 us  [body(): swapped = lax.all_gather(wide, ('c', 'x'), axis=0, tiled=True)]
    unnamed x23 -> x19, local copies, waits for them, and re-layouts: 5.5 us -> 4.51 us
  transfers between devices with their start and end apart: 21 -> 20, of which waited for: 10 -> 9; matrix products, arithmetic and copies ran while one was open for 2% -> 2% of each run, Pallas kernels for 9% -> 9%
where the time goes in v16:
time: 128 us; the launch traced here: 127 us
  waiting for transfers between devices  48.4 us (38%)
  starting transfers between devices  40.6 us (32%)
  Pallas kernels  18 us (14%)
  between operations  13.6 us (11%)
  local copies, waits for them, and re-layouts  4.95 us (4%)
  other arithmetic  1.56 us (1%)
    ppermute x13, waiting for transfers between devices, shifted(): return lax.ppermute(array, axis, [(i, (i + step) % n) for i in range(n)])  28.7 us
    ppermute x13, starting transfers between devices, shifted(): return lax.ppermute(array, axis, [(i, (i + step) % n) for i in range(n)])  18.9 us
    ppermute x1, waiting for transfers between devices, body(): other = lax.ppermute(tokens, 'l', SWAP)  9.11 us
    all_to_all x1, waiting for transfers between devices, body(): states = lax.all_to_all(state, ('y', 'h'), 0, 0, tiled=True)  7.96 us
    ppermute x1, starting transfers between devices, body(): halos = lax.ppermute(tails, CTX, [(i, i + 1) for i in range(1, 31, 2)])  7.15 us
    pallas_call x1, Pallas kernels, body(): pl.pallas_call(functools.partial(project_kernel, sizes, early_runs, late_...  5.9 us
    pallas_call x1, Pallas kernels, body(): pl.pallas_call(functools.partial(state_kernel, sizes), out_shape=(full, j...  5.6 us
    ppermute x1, starting transfers between devices, body(): return in_order(c == 0, mine, lax.ppermute(theirs, 'c', SWAP), 1)  5.42 us
  transfers between devices with their start and end apart: 20, of which 9 were waited for; matrix products, arithmetic and copies ran while one was open for 2% of the time, Pallas kernels for 9%

profile of v16, /device:TPU:1, one launch (start us, length us, event | category | flops | bytes accessed | tf_op | source)
XLA Modules:
  0.0 127.2 jit_solution(9582771006894942657)
XLA Ops:
  6.5 0.0 all-gather.3.cloned.1.call-start
  6.5 0.7 all-gather.3.cloned.1.call-update
  7.3 0.0 all-gather.5.cloned.1.call-start
  7.3 1.2 copy.10
  8.5 0.0 copy-start.8
  8.6 0.1 copy.13
  8.8 3.3 %collective-permute-start.1 = (bf16[128,768]{1,0:T(8,128)(2,1)S(1)}, bf16[128,768]{1,0:T(8,128)(2,1)S(1)}, u32[]{:S(2)}, u32[]{:S(2)}) collective-permute-start(bf16[128,768]{1,0:T(8,128)(2,1)S(1)} %bitcast.17), channel_id=1, source_target_pairs={{0,8},{8,0},{1,9},{9,1},{2,10},{10,2},{3,11},{11,3},{4,12},{12,4},... | collective-permute-start | bytes 589832 | tf_op jit(solution)/shard_map/weight_gather/ppermute | solution.py:290
  12.1 0.1 copy.12
  12.2 0.9 collective-permute-done.1
  13.2 1.1 collective-permute-start.3
  14.3 0.5 collective-permute-start.2
  14.8 0.0 copy-done.8
  14.8 1.2 collective-permute-start
  16.0 5.1 %collective-permute-start.6 = (bf16[256,768]{1,0:T(8,128)(2,1)S(1)}, bf16[256,768]{1,0:T(8,128)(2,1)S(1)}, u32[]{:S(2)}, u32[]{:S(2)}) collective-permute-start(bf16[256,768]{1,0:T(8,128)(2,1)S(1)} %pad_maximum_fusion.refs_3_), channel_id=1, source_target_pairs={{0,48},{16,0},{32,16},{48,32},{1,49},{17,1},{33,17},{49,33},{2,50}... | collective-permute-start | bytes 1179656 | tf_op jit(solution)/shard_map/weight_rings/ppermute | solution.py:23
  21.1 0.0 collective-permute-start.5
  21.1 9.1 %collective-permute-done = bf16[256,512]{1,0:T(8,128)(2,1)S(1)} collective-permute-done((bf16[256,512]{1,0:T(8,128)(2,1)S(1)}, bf16[256,512]{1,0:T(8,128)(2,1)S(1)}, u32[]{:S(2)}, u32[]{:S(2)}) %collective-permute-start) | collective-permute-done | bytes 262176 | tf_op jit(solution)/shard_map/token_swap/ppermute | solution.py:293
  30.2 0.0 collective-permute-done.3.refs_5_.refs_8_
  30.2 0.0 collective-permute-done.2.refs_4_.refs_6_
  30.2 7.2 %collective-permute-start.4 = (bf16[32,512]{1,0:T(8,128)(2,1)S(1)}, bf16[32,512]{1,0:T(8,128)(2,1)S(1)}, u32[]{:S(2)}, u32[]{:S(2)}) collective-permute-start(bf16[32,512]{1,0:T(8,128)(2,1)S(1)} %pad_maximum_fusion.3), channel_id=1, source_target_pairs={{8,16},{24,32},{40,48},{56,64},{72,80},{88,96},{104,112},{120,128}... | collective-permute-start | bytes 98312 | tf_op jit(solution)/shard_map/weight_rings/ppermute | solution.py:299
  37.4 0.0 collective-permute-done.6.refs_1_
  37.4 6.4 %collective-permute-done.5.refs_0_ = bf16[256,768]{1,0:T(8,128)(2,1)S(1)} collective-permute-done((bf16[256,768]{1,0:T(8,128)(2,1)S(1)}, bf16[256,768]{1,0:T(8,128)(2,1)S(1)}, u32[]{:S(2)}, u32[]{:S(2)}) %collective-permute-start.5) | collective-permute-done | bytes 393248 | tf_op jit(solution)/shard_map/weight_rings/ppermute | solution.py:23
  43.8 0.0 collective-permute-done.4
  43.8 0.7 pad_maximum_fusion.1
  44.5 0.0 all-gather.5.cloned.1.call-update
  44.5 0.9 relay_pair.1
  45.5 2.3 %collective-permute-start.8 = (bf16[512,768]{1,0:T(8,128)(2,1)S(1)}, bf16[512,768]{1,0:T(8,128)(2,1)S(1)}, u32[]{:S(2)}, u32[]{:S(2)}) collective-permute-start(bf16[512,768]{1,0:T(8,128)(2,1)S(1)} %get-tuple-element.43.refs_4_), channel_id=1, source_target_pairs={{0,192},{64,0},{128,64},{192,128},{1,193},{65,1},{129,65},{193,129... | collective-permute-start | bytes 2359304 | tf_op jit(solution)/shard_map/weight_rings/ppermute | solution.py:23
  47.8 0.0 collective-permute-start.7
  47.8 0.0 collective-permute-start.9
  47.8 3.6 %collective-permute-start.10 = (bf16[128,768]{1,0:T(8,128)(2,1)S(1)}, bf16[128,768]{1,0:T(8,128)(2,1)S(1)}, u32[]{:S(2)}, u32[]{:S(2)}) collective-permute-start(bf16[128,768]{1,0:T(8,128)(2,1)S(1)} %get-tuple-element.45), channel_id=1, source_target_pairs={{0,48},{16,0},{32,16},{48,32},{1,49},{17,1},{33,17},{49,33},{2,50}... | collective-permute-start | bytes 589832 | tf_op jit(solution)/shard_map/weight_rings/ppermute | solution.py:23
  51.4 5.7 %collective-permute-done.9.refs_2_ = bf16[128,768]{1,0:T(8,128)(2,1)S(1)} collective-permute-done((bf16[128,768]{1,0:T(8,128)(2,1)S(1)}, bf16[128,768]{1,0:T(8,128)(2,1)S(1)}, u32[]{:S(2)}, u32[]{:S(2)}) %collective-permute-start.9) | collective-permute-done | bytes 196640 | tf_op jit(solution)/shard_map/weight_rings/ppermute | solution.py:23
  57.1 0.0 collective-permute-done.10.refs_3_
  57.1 5.6 %collective-permute-done.8.refs_1_.refs_9_ = bf16[512,768]{1,0:T(8,128)(2,1)S(1)} collective-permute-done((bf16[512,768]{1,0:T(8,128)(2,1)S(1)}, bf16[512,768]{1,0:T(8,128)(2,1)S(1)}, u32[]{:S(2)}, u32[]{:S(2)}) %collective-permute-start.8) | collective-permute-done | bytes 786464 | tf_op jit(solution)/shard_map/weight_rings/ppermute | solution.py:23
  62.8 3.2 %collective-permute-done.7.refs_0_.refs_7_ = bf16[512,768]{1,0:T(8,128)(2,1)S(1)} collective-permute-done((bf16[512,768]{1,0:T(8,128)(2,1)S(1)}, bf16[512,768]{1,0:T(8,128)(2,1)S(1)}, u32[]{:S(2)}, u32[]{:S(2)}) %collective-permute-start.7) | collective-permute-done | bytes 786464 | tf_op jit(solution)/shard_map/weight_rings/ppermute | solution.py:23
  65.9 1.6 %relay_far.1 = (bf16[384,768]{1,0:T(8,128)(2,1)}, bf16[384,768]{1,0:T(8,128)(2,1)}, bf16[256,768]{1,0:T(8,128)(2,1)}, bf16[256,768]{1,0:T(8,128)(2,1)}, bf16[256,768]{1,0:T(8,128)(2,1)}) custom-call(bf16[512,768]{1,0:T(8,128)(2,1)S(1)} %collective-permute-done.7.refs_0_.refs_7_, bf16[512,768]{1,0:T(8,128)(2,1)S(1)} %collective-permute-done.8.refs_1_.refs_9_, ...), custom_call_target="tpu_custom_call" | custom-call | bytes 2000000 | tf_op jit(solution)/shard_map/weight_rings/relay_far/pallas_call | solution.py:54
  67.5 0.1 collective-permute-start.11
  67.6 2.7 %collective-permute-start.12 = (bf16[384,768]{1,0:T(8,128)(2,1)}, bf16[384,768]{1,0:T(8,128)(2,1)}, u32[]{:S(2)}, u32[]{:S(2)}) collective-permute-start(bf16[384,768]{1,0:T(8,128)(2,1)} %get-tuple-element.55), channel_id=1, source_target_pairs={{0,192},{64,0},{128,64},{192,128},{1,193},{65,1},{129,65},{193,129... | collective-permute-start | bytes 1769480 | tf_op jit(solution)/shard_map/weight_rings/ppermute | solution.py:23
  70.3 1.7 %collective-permute-start.13 = (bf16[256,768]{1,0:T(8,128)(2,1)}, bf16[256,768]{1,0:T(8,128)(2,1)}, u32[]{:S(2)}, u32[]{:S(2)}) collective-permute-start(bf16[256,768]{1,0:T(8,128)(2,1)} %get-tuple-element.56), channel_id=1, source_target_pairs={{0,16},{16,32},{32,48},{48,0},{1,17},{17,33},{33,49},{49,1},{2,18}... | collective-permute-start | bytes 1179656 | tf_op jit(solution)/shard_map/weight_rings/ppermute | solution.py:23
  71.9 1.9 %collective-permute-start.14 = (bf16[256,768]{1,0:T(8,128)(2,1)}, bf16[256,768]{1,0:T(8,128)(2,1)}, u32[]{:S(2)}, u32[]{:S(2)}) collective-permute-start(bf16[256,768]{1,0:T(8,128)(2,1)} %get-tuple-element.57), channel_id=1, source_target_pairs={{0,48},{16,0},{32,16},{48,32},{1,49},{17,1},{33,17},{49,33},{2,50}... | collective-permute-start | bytes 1179656 | tf_op jit(solution)/shard_map/weight_rings/ppermute | solution.py:23
  73.9 0.0 collective-permute-start.15
  73.9 0.1 stack.23.refs_0_.pos
  74.0 1.7 %copy-done = bf16[2304,512]{1,0:T(8,128)(2,1)S(1)} copy-done((bf16[2304,512]{1,0:T(8,128)(2,1)S(1)}, bf16[2304,512]{1,0:T(8,128)(2,1)}, u32[]{:S(2)}) %copy-start) | copy-done | bytes 2359320
  75.6 1.6 %copy-done.1 = bf16[2048,512]{1,0:T(8,128)(2,1)S(1)} copy-done((bf16[2048,512]{1,0:T(8,128)(2,1)S(1)}, bf16[2048,512]{1,0:T(8,128)(2,1)}, u32[]{:S(2)}) %copy-start.1) | copy-done | bytes 2097176
  77.2 5.9 %project.1 = (f32[6,528,128]{2,1,0:T(8,128)S(1)}, bf16[528,1536]{1,0:T(8,128)(2,1)S(1)}) custom-call(s32[5]{0:T(128)S(1)} %stack.23.refs_0_.pos, bf16[2048,512]{1,0:T(8,128)(2,1)S(1)} %copy-done.1, bf16[2304,512]{1,0:T(8,128)(2,1)S(1)} %copy-done, bf16[256,768]{1,0:T(8,128)(2,1)S(1)} %pad_maximum_fusion.refs_3_, ...), custom_call_target="tpu_custom_call" | custom-call | flops 2076180480 | bytes 9000000 | tf_op jit(solution)/shard_map/project/pallas_call | solution.py:346
  83.1 0.0 collective-permute-done.13.refs_4_
  83.1 7.8 %collective-permute-done.14.refs_5_ = bf16[256,768]{1,0:T(8,128)(2,1)} collective-permute-done((bf16[256,768]{1,0:T(8,128)(2,1)}, bf16[256,768]{1,0:T(8,128)(2,1)}, u32[]{:S(2)}, u32[]{:S(2)}) %collective-permute-start.14) | collective-permute-done | bytes 393248 | tf_op jit(solution)/shard_map/weight_rings/ppermute | solution.py:23
  90.9 0.0 collective-permute-done.15.refs_6_
  90.9 0.0 collective-permute-done.11.refs_2_
  90.9 0.0 collective-permute-done.12.refs_3_
  91.0 0.0 copy-start.3
  91.0 0.0 copy-start.4
  91.0 0.0 copy-start.6
  91.0 0.0 copy-start.7
  91.0 5.6 %states.1 = (f32[64,8,256]{2,1,0:T(8,128)S(1)}, f32[2,528,128]{2,1,0:T(8,128)S(1)}, f32[16,16,256]{2,1,0:T(8,128)}) custom-call(s32[5]{0:T(128)S(1)} %stack.23.refs_0_.pos, bf16[528,1536]{1,0:T(8,128)(2,1)S(1)} %get-tuple-element.53.refs_1_, bf16[384,768]{1,0:T(8,128)(2,1)} %collective-permute-done.11.refs_2_, ...), custom_call_target="tpu_custom_call" | custom-call | tf_op jit(solution)/shard_map/states/pallas_call | solution.py:368
  96.6 4.6 %all-to-all-start = ((f32[16,16,256]{2,1,0:T(8,128)}), f32[16,16,256]{2,1,0:T(8,128)S(1)}, u32[]{:S(2)}, u32[]{:S(2)}) async-start(f32[16,16,256]{2,1,0:T(8,128)} %get-tuple-element.64), calls=%async_computation | async-start | bytes 524288 | tf_op jit(solution)/shard_map/state_exchange/all_to_all | solution.py:386
  101.2 0.0 copy-done.3
  101.2 0.0 copy-done.4
  101.2 0.0 copy-done.6
  101.2 0.0 copy-done.7
  101.2 2.5 %local.1 = (f32[64,8,256]{2,1,0:T(8,128)S(1)}, f32[64,8,256]{2,1,0:T(8,128)S(1)}, f32[16,8,256]{2,1,0:T(8,128)S(1)}) custom-call(s32[5]{0:T(128)S(1)} %stack.23.refs_0_.pos, f32[2,528,128]{2,1,0:T(8,128)S(1)} %get-tuple-element.59.gated, f32[3,3,512]{2,1,0:T(4,128)S(1)} %copy-done.6, f32[64,8,256]{2,1,0:T(8,128)S(1)} %get-tuple-element.60.product, ...), custom_call_target="tpu_custom_call" | custom-call | flops 30000000 | bytes 2000000 | tf_op jit(solution)/shard_map/local/pallas_call | solution.py:387
  103.7 8.0 %all-to-all-done.states = f32[16,16,256]{2,1,0:T(8,128)S(1)} async-done(((f32[16,16,256]{2,1,0:T(8,128)}), f32[16,16,256]{2,1,0:T(8,128)S(1)}, u32[]{:S(2)}, u32[]{:S(2)}) %all-to-all-start) | async-done | bytes 262176 | tf_op jit(solution)/shard_map/state_exchange/all_to_all | solution.py:386
  111.7 1.5 %finish.1 = (bf16[256,256]{1,0:T(8,128)(2,1)S(1)}, bf16[256,256]{1,0:T(8,128)(2,1)S(1)}) custom-call(s32[5]{0:T(128)S(1)} %stack.23.refs_0_.pos, f32[64,8,256]{2,1,0:T(8,128)S(1)} %get-tuple-element.61.gate, f32[64,8,256]{2,1,0:T(8,128)S(1)} %get-tuple-element.62.local, f32[16,8,256]{2,1,0:T(8,128)S(1)} %get-tuple-element.63.inside, ...), custom_call_target="tpu_custom_call" | custom-call | tf_op jit(solution)/shard_map/finish/pallas_call | solution.py:398
  113.2 5.4 %collective-permute-start.16 = (bf16[256,256]{1,0:T(8,128)(2,1)S(1)}, bf16[256,256]{1,0:T(8,128)(2,1)S(1)}, u32[]{:S(2)}, u32[]{:S(2)}) collective-permute-start(bf16[256,256]{1,0:T(8,128)(2,1)S(1)} %get-tuple-element.66), channel_id=1, source_target_pairs={{0,8},{8,0},{1,9},{9,1},{2,10},{10,2},{3,11},{11,3},{4,12},{12,4},... | collective-permute-start | bytes 393224 | tf_op jit(solution)/shard_map/result_swap/ppermute | solution.py:408
  118.6 1.0 collective-permute-done.16
  119.7 0.7 pad_maximum_fusion.2
  (16 shorter events, 0.2 us)
Async XLA Ops:
  6.5 67.4 %all-gather.3.cloned.1.call-start = ((), (), s32[]{:S(2)}) async-start(), calls=%async_computation.1 | async-start | bytes 2359296 | tf_op jit(solution)/shard_map/token_gather/all_gather | solution.py:303
  7.3 66.7 %all-gather.5.cloned.1.call-start = ((), (), s32[]{:S(2)}) async-start(), calls=%async_computation.2 | async-start | bytes 2654208 | tf_op jit(solution)/shard_map/token_gather/all_gather | solution.py:305
  8.5 6.3 %copy-start.8 = (bf16[256,512]{1,0:T(8,128)(2,1)S(1)}, bf16[256,512]{1,0:T(8,128)(2,1)}, u32[]{:S(2)}) copy-start(bf16[256,512]{1,0:T(8,128)(2,1)} %param.6) | copy-start | bytes 786436
  8.8 4.4 %collective-permute-start.1 = (bf16[128,768]{1,0:T(8,128)(2,1)S(1)}, bf16[128,768]{1,0:T(8,128)(2,1)S(1)}, u32[]{:S(2)}, u32[]{:S(2)}) collective-permute-start(bf16[128,768]{1,0:T(8,128)(2,1)S(1)} %bitcast.17), channel_id=1, source_target_pairs={{0,8},{8,0},{1,9},{9,1},{2,10},{10,2},{3,11},{11,3},{4,12},{12,4},... | collective-permute-start | bytes 589832 | tf_op jit(solution)/shard_map/weight_gather/ppermute | solution.py:290
  13.2 17.0 %collective-permute-start.3 = (bf16[256,768]{1,0:T(8,128)(2,1)S(1)}, bf16[256,768]{1,0:T(8,128)(2,1)S(1)}, u32[]{:S(2)}, u32[]{:S(2)}) collective-permute-start(bf16[256,768]{1,0:T(8,128)(2,1)S(1)} %pad_maximum_fusion.refs_3_), channel_id=1, source_target_pairs={{0,192},{64,0},{128,64},{192,128},{1,193},{65,1},{129,65},{193,129... | collective-permute-start | bytes 1179656 | tf_op jit(solution)/shard_map/weight_rings/ppermute | solution.py:23
  14.3 15.9 %collective-permute-start.2 = (bf16[256,768]{1,0:T(8,128)(2,1)S(1)}, bf16[256,768]{1,0:T(8,128)(2,1)S(1)}, u32[]{:S(2)}, u32[]{:S(2)}) collective-permute-start(bf16[256,768]{1,0:T(8,128)(2,1)S(1)} %pad_maximum_fusion.refs_3_), channel_id=1, source_target_pairs={{0,64},{64,128},{128,192},{192,0},{1,65},{65,129},{129,193},{193,1... | collective-permute-start | bytes 1179656 | tf_op jit(solution)/shard_map/weight_rings/ppermute | solution.py:23
  14.8 15.4 %collective-permute-start = (bf16[256,512]{1,0:T(8,128)(2,1)S(1)}, bf16[256,512]{1,0:T(8,128)(2,1)S(1)}, u32[]{:S(2)}, u32[]{:S(2)}) collective-permute-start(bf16[256,512]{1,0:T(8,128)(2,1)S(1)} %copy-done.8), channel_id=1, source_target_pairs={{0,4},{4,0},{1,5},{5,1},{2,6},{6,2},{3,7},{7,3},{8,12},{12,8},{9,1... | collective-permute-start | bytes 786440 | tf_op jit(solution)/shard_map/token_swap/ppermute | solution.py:293
  16.0 21.4 %collective-permute-start.6 = (bf16[256,768]{1,0:T(8,128)(2,1)S(1)}, bf16[256,768]{1,0:T(8,128)(2,1)S(1)}, u32[]{:S(2)}, u32[]{:S(2)}) collective-permute-start(bf16[256,768]{1,0:T(8,128)(2,1)S(1)} %pad_maximum_fusion.refs_3_), channel_id=1, source_target_pairs={{0,48},{16,0},{32,16},{48,32},{1,49},{17,1},{33,17},{49,33},{2,50}... | collective-permute-start | bytes 1179656 | tf_op jit(solution)/shard_map/weight_rings/ppermute | solution.py:23
  21.1 22.7 %collective-permute-start.5 = (bf16[256,768]{1,0:T(8,128)(2,1)S(1)}, bf16[256,768]{1,0:T(8,128)(2,1)S(1)}, u32[]{:S(2)}, u32[]{:S(2)}) collective-permute-start(bf16[256,768]{1,0:T(8,128)(2,1)S(1)} %pad_maximum_fusion.refs_3_), channel_id=1, source_target_pairs={{0,16},{16,32},{32,48},{48,0},{1,17},{17,33},{33,49},{49,1},{2,18}... | collective-permute-start | bytes 1179656 | tf_op jit(solution)/shard_map/weight_rings/ppermute | solution.py:23
  30.2 13.5 %collective-permute-start.4 = (bf16[32,512]{1,0:T(8,128)(2,1)S(1)}, bf16[32,512]{1,0:T(8,128)(2,1)S(1)}, u32[]{:S(2)}, u32[]{:S(2)}) collective-permute-start(bf16[32,512]{1,0:T(8,128)(2,1)S(1)} %pad_maximum_fusion.3), channel_id=1, source_target_pairs={{8,16},{24,32},{40,48},{56,64},{72,80},{88,96},{104,112},{120,128}... | collective-permute-start | bytes 98312 | tf_op jit(solution)/shard_map/weight_rings/ppermute | solution.py:299
  45.5 17.3 %collective-permute-start.8 = (bf16[512,768]{1,0:T(8,128)(2,1)S(1)}, bf16[512,768]{1,0:T(8,128)(2,1)S(1)}, u32[]{:S(2)}, u32[]{:S(2)}) collective-permute-start(bf16[512,768]{1,0:T(8,128)(2,1)S(1)} %get-tuple-element.43.refs_4_), channel_id=1, source_target_pairs={{0,192},{64,0},{128,64},{192,128},{1,193},{65,1},{129,65},{193,129... | collective-permute-start | bytes 2359304 | tf_op jit(solution)/shard_map/weight_rings/ppermute | solution.py:23
  47.8 18.1 %collective-permute-start.7 = (bf16[512,768]{1,0:T(8,128)(2,1)S(1)}, bf16[512,768]{1,0:T(8,128)(2,1)S(1)}, u32[]{:S(2)}, u32[]{:S(2)}) collective-permute-start(bf16[512,768]{1,0:T(8,128)(2,1)S(1)} %get-tuple-element.43.refs_4_), channel_id=1, source_target_pairs={{0,64},{64,128},{128,192},{192,0},{1,65},{65,129},{129,193},{193,1... | collective-permute-start | bytes 2359304 | tf_op jit(solution)/shard_map/weight_rings/ppermute | solution.py:23
  47.8 9.3 %collective-permute-start.9 = (bf16[128,768]{1,0:T(8,128)(2,1)S(1)}, bf16[128,768]{1,0:T(8,128)(2,1)S(1)}, u32[]{:S(2)}, u32[]{:S(2)}) collective-permute-start(bf16[128,768]{1,0:T(8,128)(2,1)S(1)} %get-tuple-element.44), channel_id=1, source_target_pairs={{0,16},{16,32},{32,48},{48,0},{1,17},{17,33},{33,49},{49,1},{2,18}... | collective-permute-start | bytes 589832 | tf_op jit(solution)/shard_map/weight_rings/ppermute | solution.py:23
  47.8 9.3 %collective-permute-start.10 = (bf16[128,768]{1,0:T(8,128)(2,1)S(1)}, bf16[128,768]{1,0:T(8,128)(2,1)S(1)}, u32[]{:S(2)}, u32[]{:S(2)}) collective-permute-start(bf16[128,768]{1,0:T(8,128)(2,1)S(1)} %get-tuple-element.45), channel_id=1, source_target_pairs={{0,48},{16,0},{32,16},{48,32},{1,49},{17,1},{33,17},{49,33},{2,50}... | collective-permute-start | bytes 589832 | tf_op jit(solution)/shard_map/weight_rings/ppermute | solution.py:23
  67.5 23.4 %collective-permute-start.11 = (bf16[384,768]{1,0:T(8,128)(2,1)}, bf16[384,768]{1,0:T(8,128)(2,1)}, u32[]{:S(2)}, u32[]{:S(2)}) collective-permute-start(bf16[384,768]{1,0:T(8,128)(2,1)} %get-tuple-element.54), channel_id=1, source_target_pairs={{0,64},{64,128},{128,192},{192,0},{1,65},{65,129},{129,193},{193,1... | collective-permute-start | bytes 1769480 | tf_op jit(solution)/shard_map/weight_rings/ppermute | solution.py:23
  67.6 23.3 %collective-permute-start.12 = (bf16[384,768]{1,0:T(8,128)(2,1)}, bf16[384,768]{1,0:T(8,128)(2,1)}, u32[]{:S(2)}, u32[]{:S(2)}) collective-permute-start(bf16[384,768]{1,0:T(8,128)(2,1)} %get-tuple-element.55), channel_id=1, source_target_pairs={{0,192},{64,0},{128,64},{192,128},{1,193},{65,1},{129,65},{193,129... | collective-permute-start | bytes 1769480 | tf_op jit(solution)/shard_map/weight_rings/ppermute | solution.py:23
  70.3 12.8 %collective-permute-start.13 = (bf16[256,768]{1,0:T(8,128)(2,1)}, bf16[256,768]{1,0:T(8,128)(2,1)}, u32[]{:S(2)}, u32[]{:S(2)}) collective-permute-start(bf16[256,768]{1,0:T(8,128)(2,1)} %get-tuple-element.56), channel_id=1, source_target_pairs={{0,16},{16,32},{32,48},{48,0},{1,17},{17,33},{33,49},{49,1},{2,18}... | collective-permute-start | bytes 1179656 | tf_op jit(solution)/shard_map/weight_rings/ppermute | solution.py:23
  71.9 19.0 %collective-permute-start.14 = (bf16[256,768]{1,0:T(8,128)(2,1)}, bf16[256,768]{1,0:T(8,128)(2,1)}, u32[]{:S(2)}, u32[]{:S(2)}) collective-permute-start(bf16[256,768]{1,0:T(8,128)(2,1)} %get-tuple-element.57), channel_id=1, source_target_pairs={{0,48},{16,0},{32,16},{48,32},{1,49},{17,1},{33,17},{49,33},{2,50}... | collective-permute-start | bytes 1179656 | tf_op jit(solution)/shard_map/weight_rings/ppermute | solution.py:23
  73.9 17.1 %collective-permute-start.15 = (bf16[256,768]{1,0:T(8,128)(2,1)}, bf16[256,768]{1,0:T(8,128)(2,1)}, u32[]{:S(2)}, u32[]{:S(2)}) collective-permute-start(bf16[256,768]{1,0:T(8,128)(2,1)} %get-tuple-element.52.refs_5_), channel_id=1, source_target_pairs={{0,128},{64,192},{128,0},{192,64},{1,129},{65,193},{129,1},{193,65... | collective-permute-start | bytes 1179656 | tf_op jit(solution)/shard_map/weight_rings/ppermute | solution.py:23
  73.9 1.7 %copy-start = (bf16[2304,512]{1,0:T(8,128)(2,1)S(1)}, bf16[2304,512]{1,0:T(8,128)(2,1)}, u32[]{:S(2)}) copy-start(bf16[2304,512]{1,0:T(8,128)(2,1)} %all-gather.5.cloned.1.call-done.refs_2_) | copy-start | bytes 7077892
  75.6 1.6 %copy-start.1 = (bf16[2048,512]{1,0:T(8,128)(2,1)S(1)}, bf16[2048,512]{1,0:T(8,128)(2,1)}, u32[]{:S(2)}) copy-start(bf16[2048,512]{1,0:T(8,128)(2,1)} %all-gather.3.cloned.1.call-done.refs_1_) | copy-start | bytes 6291460
  77.2 13.7 %copy-start.2 = (f32[16,512]{1,0:T(8,128)S(1)}, f32[16,512]{1,0:T(8,128)}, u32[]{:S(2)}) copy-start(f32[16,512]{1,0:T(8,128)} %decay.3) | copy-start | bytes 98308
  77.2 13.7 %copy-start.5 = (f32[3,3,512]{2,1,0:T(4,128)S(1)}, f32[3,3,512]{2,1,0:T(4,128)}, u32[]{:S(2)}) copy-start(f32[3,3,512]{2,1,0:T(4,128)} %taps.1) | copy-start | bytes 55300
  91.0 10.2 %copy-start.3 = (f32[16,512]{1,0:T(8,128)S(1)}, f32[16,512]{1,0:T(8,128)}, u32[]{:S(2)}) copy-start(f32[16,512]{1,0:T(8,128)} %decay.3) | copy-start | bytes 98308
  91.0 10.2 %copy-start.4 = (f32[16,512]{1,0:T(8,128)S(1)}, f32[16,512]{1,0:T(8,128)}, u32[]{:S(2)}) copy-start(f32[16,512]{1,0:T(8,128)} %gain.3) | copy-start | bytes 98308
  91.0 10.2 %copy-start.6 = (f32[3,3,512]{2,1,0:T(4,128)S(1)}, f32[3,3,512]{2,1,0:T(4,128)}, u32[]{:S(2)}) copy-start(f32[3,3,512]{2,1,0:T(4,128)} %taps.1) | copy-start | bytes 55300
  91.0 10.2 %copy-start.7 = (f32[512]{0:T(512)S(1)}, f32[512]{0:T(512)}, u32[]{:S(2)}) copy-start(f32[512]{0:T(512)} %param.11) | copy-start | bytes 6148
  96.6 15.1 %all-to-all-start = ((f32[16,16,256]{2,1,0:T(8,128)}), f32[16,16,256]{2,1,0:T(8,128)S(1)}, u32[]{:S(2)}, u32[]{:S(2)}) async-start(f32[16,16,256]{2,1,0:T(8,128)} %get-tuple-element.64), calls=%async_computation | async-start | bytes 524288 | tf_op jit(solution)/shard_map/state_exchange/all_to_all | solution.py:386
  113.2 6.4 %collective-permute-start.16 = (bf16[256,256]{1,0:T(8,128)(2,1)S(1)}, bf16[256,256]{1,0:T(8,128)(2,1)S(1)}, u32[]{:S(2)}, u32[]{:S(2)}) collective-permute-start(bf16[256,256]{1,0:T(8,128)(2,1)S(1)} %get-tuple-element.66), channel_id=1, source_target_pairs={{0,8},{8,0},{1,9},{9,1},{2,10},{10,2},{3,11},{11,3},{4,12},{12,4},... | collective-permute-start | bytes 393224 | tf_op jit(solution)/shard_map/result_swap/ppermute | solution.py:408
Sparse Core Ops, SparseCore 0:
  9.2 31.8 all-gather.2
  44.6 27.3 all-gather.4

commit v17 on v12

--- a/solution.py
+++ b/solution.py
@@ -189,8 +189,9 @@
         for m in range(modes):
             total = jnp.sum(jnp.exp(-rates[m] * left) * states[m], axis=0, keepdims=True)
             state[m : m + 1, lanes] = total
+    sent = state[...].astype(BF16)
     for r in range(16):
-        states_out[r] = state[...]
+        states_out[r] = sent
 
 
 def local_kernel(sizes, pos, gated, taps, product, gain, decay, skip, gate, local, inside):
@@ -247,7 +248,7 @@
         over = jnp.exp(-float(length) * (decay[:, mine] / seq))
         entering = jnp.zeros((modes, 128), F32)
         for r in range(16):
-            entering = jnp.where(r < rank, over * entering + states[r, :, lanes], entering)
+            entering = jnp.where(r < rank, over * entering + states[r, :, lanes].astype(F32), entering)
         start[:, lanes] = entering
         line = lax.broadcasted_iota(jnp.int32, (SUB, 128), 0).astype(F32) * float(steps)
         factors, waves = [], []
@@ -370,7 +371,7 @@
         out_shape=(
             full,
             jax.ShapeDtypeStruct((width // 128, lines, 128), F32),
-            jax.ShapeDtypeStruct((16, modes, width), F32),
+            jax.ShapeDtypeStruct((16, modes, width), BF16),
         ),
         in_specs=[smem] + [vmem] * (4 + len(late)),
         out_specs=(vmem,) * 3,

time: 122 us -> 120 us (0.984)
  waiting for transfers between devices: 31.6 us -> 30 us
    all_to_all x1, waiting for transfers between devices: 8.67 us -> 7 us  [body(): states = lax.all_to_all(state, ('y', 'h'), 0, 0, tiled=True)]
where the time goes in v17:
time: 120 us
  starting transfers between devices  51.3 us (43%)
  waiting for transfers between devices  30 us (25%)
  Pallas kernels  17.4 us (14%)
  between operations  13.7 us (11%)
  local copies, waits for them, and re-layouts  5.95 us (5%)
  other arithmetic  1.53 us (1%)
    ppermute x14, starting transfers between devices, shifted(): return lax.ppermute(array, axis, [(i, (i + step) % n) for i in range(n)])  28.1 us
    ppermute x14, waiting for transfers between devices, shifted(): return lax.ppermute(array, axis, [(i, (i + step) % n) for i in range(n)])  13.2 us
    all_to_all x1, starting transfers between devices, body(): states = lax.all_to_all(state, ('y', 'h'), 0, 0, tiled=True)  9.28 us
    all_to_all x1, waiting for transfers between devices, body(): states = lax.all_to_all(state, ('y', 'h'), 0, 0, tiled=True)  7 us
    ppermute x1, starting transfers between devices, body(): halos = lax.ppermute(tails, CTX, [(i, i + 1) for i in range(1, 31, 2)])  6.87 us
    pallas_call x1, Pallas kernels, body(): pl.pallas_call(functools.partial(project_kernel, sizes, early_runs, late_...  6.06 us
    unnamed x23, local copies, waits for them, and re-layouts  5.5 us
    pallas_call x1, Pallas kernels, body(): pl.pallas_call(functools.partial(state_kernel, sizes), out_shape=(full, j...  5.08 us
  transfers between devices with their start and end apart: 21, of which 10 were waited for; matrix products, arithmetic and copies ran while one was open for 2% of the time, Pallas kernels for 9%

profile of v17, /device:TPU:1, one launch (start us, length us, event | category | flops | bytes accessed | tf_op | source)
XLA Modules:
  0.0 119.8 jit_solution(7133749999480275872)
XLA Ops:
  6.5 0.0 all-gather.3.cloned.1.call-start
  6.5 0.7 all-gather.3.cloned.1.call-update
  7.3 0.0 all-gather.5.cloned.1.call-start
  7.3 1.2 %copy.10 = bf16[128,3,512]{0,2,1:T(8,128)(2,1)S(1)} copy(bf16[128,3,512]{2,0,1:T(8,128)(2,1)} %param.7) | data formatting | bytes 786432 | tf_op args[1]
  8.6 0.1 copy.13
  8.8 3.3 %collective-permute-start.1 = (bf16[128,768]{1,0:T(8,128)(2,1)S(1)}, bf16[128,768]{1,0:T(8,128)(2,1)S(1)}, u32[]{:S(2)}, u32[]{:S(2)}) collective-permute-start(bf16[128,768]{1,0:T(8,128)(2,1)S(1)} %bitcast.17), channel_id=1, source_target_pairs={{0,8},{8,0},{1,9},{9,1},{2,10},{10,2},{3,11},{11,3},{4,12},{12,4},... | collective-permute-start | bytes 589832 | tf_op jit(solution)/shard_map/weight_gather/ppermute | solution.py:291
  12.1 0.0 copy-done.10
  12.1 0.0 collective-permute-start
  12.1 0.1 copy.12
  12.2 0.9 collective-permute-done.1
  13.2 1.8 %collective-permute-start.3 = (bf16[256,768]{1,0:T(8,128)(2,1)S(1)}, bf16[256,768]{1,0:T(8,128)(2,1)S(1)}, u32[]{:S(2)}, u32[]{:S(2)}) collective-permute-start(bf16[256,768]{1,0:T(8,128)(2,1)S(1)} %pad_maximum_fusion.refs_3_), channel_id=1, source_target_pairs={{0,192},{64,0},{128,64},{192,128},{1,193},{65,1},{129,65},{193,129... | collective-permute-start | bytes 1179656 | tf_op jit(solution)/shard_map/weight_rings/ppermute | solution.py:23
  15.1 0.0 collective-permute-start.2
  15.1 5.3 %collective-permute-start.7 = (bf16[256,768]{1,0:T(8,128)(2,1)S(1)}, bf16[256,768]{1,0:T(8,128)(2,1)S(1)}, u32[]{:S(2)}, u32[]{:S(2)}) collective-permute-start(bf16[256,768]{1,0:T(8,128)(2,1)S(1)} %pad_maximum_fusion.refs_3_), channel_id=1, source_target_pairs={{0,48},{16,0},{32,16},{48,32},{1,49},{17,1},{33,17},{49,33},{2,50}... | collective-permute-start | bytes 1179656 | tf_op jit(solution)/shard_map/weight_rings/ppermute | solution.py:23
  20.3 0.0 collective-permute-start.6
  20.3 1.9 %collective-permute-done = bf16[256,512]{1,0:T(8,128)(2,1)S(1)} collective-permute-done((bf16[256,512]{1,0:T(8,128)(2,1)S(1)}, bf16[256,512]{1,0:T(8,128)(2,1)S(1)}, u32[]{:S(2)}, u32[]{:S(2)}) %collective-permute-start) | collective-permute-done | bytes 262176 | tf_op jit(solution)/shard_map/token_swap/ppermute | solution.py:294
  22.3 7.6 %collective-permute-start.5 = (bf16[256,768]{1,0:T(8,128)(2,1)S(1)}, bf16[256,768]{1,0:T(8,128)(2,1)S(1)}, u32[]{:S(2)}, u32[]{:S(2)}) collective-permute-start(bf16[256,768]{1,0:T(8,128)(2,1)S(1)} %pad_maximum_fusion.refs_3_), channel_id=1, source_target_pairs={{0,128},{64,192},{128,0},{192,64},{1,129},{65,193},{129,1},{193,65... | collective-permute-start | bytes 1179656 | tf_op jit(solution)/shard_map/weight_rings/ppermute | solution.py:23
  29.9 0.0 collective-permute-done.3.refs_8_
  29.9 0.0 collective-permute-done.2.refs_6_
  29.9 6.9 %collective-permute-start.4 = (bf16[32,512]{1,0:T(8,128)(2,1)S(1)}, bf16[32,512]{1,0:T(8,128)(2,1)S(1)}, u32[]{:S(2)}, u32[]{:S(2)}) collective-permute-start(bf16[32,512]{1,0:T(8,128)(2,1)S(1)} %pad_maximum_fusion.3), channel_id=1, source_target_pairs={{8,16},{24,32},{40,48},{56,64},{72,80},{88,96},{104,112},{120,128}... | collective-permute-start | bytes 98312 | tf_op jit(solution)/shard_map/weight_rings/ppermute | solution.py:301
  36.8 0.0 collective-permute-done.7.refs_1_
  36.8 0.0 collective-permute-done.6.refs_0_
  36.8 0.5 collective-permute-done.5.refs_10_
  37.3 3.4 %collective-permute-done.4 = bf16[32,512]{1,0:T(8,128)(2,1)S(1)} collective-permute-done((bf16[32,512]{1,0:T(8,128)(2,1)S(1)}, bf16[32,512]{1,0:T(8,128)(2,1)S(1)}, u32[]{:S(2)}, u32[]{:S(2)}) %collective-permute-start.4) | collective-permute-done | bytes 32800 | tf_op jit(solution)/shard_map/weight_rings/ppermute | solution.py:301
  40.7 0.7 pad_maximum_fusion.1
  41.5 0.0 copy-done.2
  41.5 0.0 all-gather.5.cloned.1.call-update
  41.5 0.9 relay_pair.1
  42.4 0.1 collective-permute-start.9
  42.5 1.5 %collective-permute-start.8 = (bf16[512,768]{1,0:T(8,128)(2,1)S(1)}, bf16[512,768]{1,0:T(8,128)(2,1)S(1)}, u32[]{:S(2)}, u32[]{:S(2)}) collective-permute-start(bf16[512,768]{1,0:T(8,128)(2,1)S(1)} %get-tuple-element.44.refs_4_), channel_id=1, source_target_pairs={{0,64},{64,128},{128,192},{192,0},{1,65},{65,129},{129,193},{193,1... | collective-permute-start | bytes 2359304 | tf_op jit(solution)/shard_map/weight_rings/ppermute | solution.py:23
  44.1 0.4 collective-permute-start.10
  44.5 3.2 %collective-permute-start.11 = (bf16[128,768]{1,0:T(8,128)(2,1)S(1)}, bf16[128,768]{1,0:T(8,128)(2,1)S(1)}, u32[]{:S(2)}, u32[]{:S(2)}) collective-permute-start(bf16[128,768]{1,0:T(8,128)(2,1)S(1)} %get-tuple-element.46), channel_id=1, source_target_pairs={{0,48},{16,0},{32,16},{48,32},{1,49},{17,1},{33,17},{49,33},{2,50}... | collective-permute-start | bytes 589832 | tf_op jit(solution)/shard_map/weight_rings/ppermute | solution.py:23
  47.6 3.1 %collective-permute-done.10.refs_2_ = bf16[128,768]{1,0:T(8,128)(2,1)S(1)} collective-permute-done((bf16[128,768]{1,0:T(8,128)(2,1)S(1)}, bf16[128,768]{1,0:T(8,128)(2,1)S(1)}, u32[]{:S(2)}, u32[]{:S(2)}) %collective-permute-start.10) | collective-permute-done | bytes 196640 | tf_op jit(solution)/shard_map/weight_rings/ppermute | solution.py:23
  50.8 0.2 collective-permute-done.11.refs_3_
  51.0 9.4 %collective-permute-done.9.refs_1_.refs_9_ = bf16[512,768]{1,0:T(8,128)(2,1)S(1)} collective-permute-done((bf16[512,768]{1,0:T(8,128)(2,1)S(1)}, bf16[512,768]{1,0:T(8,128)(2,1)S(1)}, u32[]{:S(2)}, u32[]{:S(2)}) %collective-permute-start.9) | collective-permute-done | bytes 786464 | tf_op jit(solution)/shard_map/weight_rings/ppermute | solution.py:23
  60.4 0.0 collective-permute-done.8.refs_0_.refs_7_
  60.4 1.4 %relay_far.1 = (bf16[256,768]{1,0:T(8,128)(2,1)}, bf16[256,768]{1,0:T(8,128)(2,1)}, bf16[256,768]{1,0:T(8,128)(2,1)}, bf16[256,768]{1,0:T(8,128)(2,1)}, bf16[256,768]{1,0:T(8,128)(2,1)}) custom-call(bf16[512,768]{1,0:T(8,128)(2,1)S(1)} %collective-permute-done.8.refs_0_.refs_7_, bf16[512,768]{1,0:T(8,128)(2,1)S(1)} %collective-permute-done.9.refs_1_.refs_9_, ...), custom_call_target="tpu_custom_call" | custom-call | bytes 2000000 | tf_op jit(solution)/shard_map/weight_rings/relay_far/pallas_call | solution.py:54
  61.7 1.6 %collective-permute-start.12 = (bf16[256,768]{1,0:T(8,128)(2,1)}, bf16[256,768]{1,0:T(8,128)(2,1)}, u32[]{:S(2)}, u32[]{:S(2)}) collective-permute-start(bf16[256,768]{1,0:T(8,128)(2,1)} %get-tuple-element.56), channel_id=1, source_target_pairs={{0,64},{64,128},{128,192},{192,0},{1,65},{65,129},{129,193},{193,1... | collective-permute-start | bytes 1179656 | tf_op jit(solution)/shard_map/weight_rings/ppermute | solution.py:23
  63.3 1.6 %collective-permute-start.13 = (bf16[256,768]{1,0:T(8,128)(2,1)}, bf16[256,768]{1,0:T(8,128)(2,1)}, u32[]{:S(2)}, u32[]{:S(2)}) collective-permute-start(bf16[256,768]{1,0:T(8,128)(2,1)} %get-tuple-element.57), channel_id=1, source_target_pairs={{0,192},{64,0},{128,64},{192,128},{1,193},{65,1},{129,65},{193,129... | collective-permute-start | bytes 1179656 | tf_op jit(solution)/shard_map/weight_rings/ppermute | solution.py:23
  64.9 2.4 %collective-permute-start.14 = (bf16[256,768]{1,0:T(8,128)(2,1)}, bf16[256,768]{1,0:T(8,128)(2,1)}, u32[]{:S(2)}, u32[]{:S(2)}) collective-permute-start(bf16[256,768]{1,0:T(8,128)(2,1)} %get-tuple-element.58), channel_id=1, source_target_pairs={{0,16},{16,32},{32,48},{48,0},{1,17},{17,33},{33,49},{49,1},{2,18}... | collective-permute-start | bytes 1179656 | tf_op jit(solution)/shard_map/weight_rings/ppermute | solution.py:23
  67.3 1.2 %collective-permute-start.15 = (bf16[256,768]{1,0:T(8,128)(2,1)}, bf16[256,768]{1,0:T(8,128)(2,1)}, u32[]{:S(2)}, u32[]{:S(2)}) collective-permute-start(bf16[256,768]{1,0:T(8,128)(2,1)} %get-tuple-element.59), channel_id=1, source_target_pairs={{0,48},{16,0},{32,16},{48,32},{1,49},{17,1},{33,17},{49,33},{2,50}... | collective-permute-start | bytes 1179656 | tf_op jit(solution)/shard_map/weight_rings/ppermute | solution.py:23
  68.5 1.4 %collective-permute-start.16 = (bf16[256,768]{1,0:T(8,128)(2,1)}, bf16[256,768]{1,0:T(8,128)(2,1)}, u32[]{:S(2)}, u32[]{:S(2)}) collective-permute-start(bf16[256,768]{1,0:T(8,128)(2,1)} %get-tuple-element.51.refs_5_), channel_id=1, source_target_pairs={{0,128},{64,192},{128,0},{192,64},{1,129},{65,193},{129,1},{193,65... | collective-permute-start | bytes 1179656 | tf_op jit(solution)/shard_map/weight_rings/ppermute | solution.py:23
  69.9 0.1 stack.23.refs_0_.pos
  70.0 1.7 %all-gather.5.cloned.1.call-done.refs_2_ = bf16[2304,512]{1,0:T(8,128)(2,1)} async-done(((bf16[288,512]{1,0:T(8,128)(2,1)}), bf16[2304,512]{1,0:T(8,128)(2,1)}) %all-gather.5.cloned.1.call-update) | async-done | bytes 2359312 | tf_op jit(solution)/shard_map/token_gather/all_gather | solution.py:307
  71.7 1.7 %copy-done = bf16[2304,512]{1,0:T(8,128)(2,1)S(1)} copy-done((bf16[2304,512]{1,0:T(8,128)(2,1)S(1)}, bf16[2304,512]{1,0:T(8,128)(2,1)}, u32[]{:S(2)}) %copy-start) | copy-done | bytes 2359320
  73.4 1.6 %copy-done.1 = bf16[2048,512]{1,0:T(8,128)(2,1)S(1)} copy-done((bf16[2048,512]{1,0:T(8,128)(2,1)S(1)}, bf16[2048,512]{1,0:T(8,128)(2,1)}, u32[]{:S(2)}) %copy-start.1) | copy-done | bytes 2097176
  74.9 1.0 copy-done.3
  75.9 6.1 %project.1 = (f32[6,528,128]{2,1,0:T(8,128)S(1)}, bf16[528,1280]{1,0:T(8,128)(2,1)S(1)}) custom-call(s32[5]{0:T(128)S(1)} %stack.23.refs_0_.pos, bf16[2048,512]{1,0:T(8,128)(2,1)S(1)} %copy-done.1, bf16[2304,512]{1,0:T(8,128)(2,1)S(1)} %copy-done, bf16[256,768]{1,0:T(8,128)(2,1)S(1)} %pad_maximum_fusion.refs_3_, ...), custom_call_target="tpu_custom_call" | custom-call | flops 2283798528 | bytes 9000000 | tf_op jit(solution)/shard_map/project/pallas_call | solution.py:347
  82.0 0.0 collective-permute-done.12.refs_2_
  82.0 0.0 collective-permute-done.13.refs_3_
  82.0 0.0 collective-permute-done.14.refs_4_
  82.0 0.0 collective-permute-done.15.refs_5_
  82.1 0.0 collective-permute-done.16.refs_6_
  82.1 0.0 copy-start.5
  82.1 0.0 copy-start.6
  82.1 0.0 copy-start.8
  82.1 0.0 copy-start.9
  82.1 5.1 %states.1 = (f32[64,8,256]{2,1,0:T(8,128)S(1)}, f32[2,528,128]{2,1,0:T(8,128)S(1)}, bf16[16,16,256]{2,1,0:T(8,128)(2,1)}) custom-call(s32[5]{0:T(128)S(1)} %stack.23.refs_0_.pos, bf16[528,1280]{1,0:T(8,128)(2,1)S(1)} %get-tuple-element.55.refs_1_, bf16[256,768]{1,0:T(8,128)(2,1)} %collective-permute-done.12.refs_2_, ...), custom_call_target="tpu_custom_call" | custom-call | tf_op jit(solution)/shard_map/states/pallas_call | solution.py:369
  87.2 9.3 %all-to-all-start = ((bf16[16,16,256]{2,1,0:T(8,128)(2,1)}), bf16[16,16,256]{2,1,0:T(8,128)(2,1)S(1)}, u32[]{:S(2)}, u32[]{:S(2)}) async-start(bf16[16,16,256]{2,1,0:T(8,128)(2,1)} %get-tuple-element.66), calls=%async_computation | async-start | bytes 262144 | tf_op jit(solution)/shard_map/state_exchange/all_to_all | solution.py:387
  96.5 2.5 %local.1 = (f32[64,8,256]{2,1,0:T(8,128)S(1)}, f32[64,8,256]{2,1,0:T(8,128)S(1)}, f32[16,8,256]{2,1,0:T(8,128)S(1)}) custom-call(s32[5]{0:T(128)S(1)} %stack.23.refs_0_.pos, f32[2,528,128]{2,1,0:T(8,128)S(1)} %get-tuple-element.61.gated, f32[3,3,512]{2,1,0:T(4,128)S(1)} %copy-done.8, f32[64,8,256]{2,1,0:T(8,128)S(1)} %get-tuple-element.62.product, ...), custom_call_target="tpu_custom_call" | custom-call | flops 30000000 | bytes 2000000 | tf_op jit(solution)/shard_map/local/pallas_call | solution.py:388
  99.0 7.0 %all-to-all-done.states = bf16[16,16,256]{2,1,0:T(8,128)(2,1)S(1)} async-done(((bf16[16,16,256]{2,1,0:T(8,128)(2,1)}), bf16[16,16,256]{2,1,0:T(8,128)(2,1)S(1)}, u32[]{:S(2)}, u32[]{:S(2)}) %all-to-all-start) | async-done | bytes 131104 | tf_op jit(solution)/shard_map/state_exchange/all_to_all | solution.py:387
  106.0 1.5 %finish.1 = (bf16[256,256]{1,0:T(8,128)(2,1)S(1)}, bf16[256,256]{1,0:T(8,128)(2,1)S(1)}) custom-call(s32[5]{0:T(128)S(1)} %stack.23.refs_0_.pos, f32[64,8,256]{2,1,0:T(8,128)S(1)} %get-tuple-element.63.gate, f32[64,8,256]{2,1,0:T(8,128)S(1)} %get-tuple-element.64.local, f32[16,8,256]{2,1,0:T(8,128)S(1)} %get-tuple-element.65.inside, ...), custom_call_target="tpu_custom_call" | custom-call | tf_op jit(solution)/shard_map/finish/pallas_call | solution.py:399
  107.6 3.7 %collective-permute-start.17 = (bf16[256,256]{1,0:T(8,128)(2,1)S(1)}, bf16[256,256]{1,0:T(8,128)(2,1)S(1)}, u32[]{:S(2)}, u32[]{:S(2)}) collective-permute-start(bf16[256,256]{1,0:T(8,128)(2,1)S(1)} %get-tuple-element.68), channel_id=1, source_target_pairs={{0,8},{8,0},{1,9},{9,1},{2,10},{10,2},{3,11},{11,3},{4,12},{12,4},... | collective-permute-start | bytes 393224 | tf_op jit(solution)/shard_map/result_swap/ppermute | solution.py:409
  111.2 1.0 collective-permute-done.17
  112.3 0.7 pad_maximum_fusion.2
  (22 shorter events, 0.2 us)
Async XLA Ops:
  6.5 5.6 %copy-start.10 = (bf16[256,512]{1,0:T(8,128)(2,1)S(1)}, bf16[256,512]{1,0:T(8,128)(2,1)}, u32[]{:S(2)}) copy-start(bf16[256,512]{1,0:T(8,128)(2,1)} %param.6) | copy-start | bytes 786436
  6.5 63.4 %all-gather.3.cloned.1.call-start = ((), (), s32[]{:S(2)}) async-start(), calls=%async_computation.1 | async-start | bytes 2359296 | tf_op jit(solution)/shard_map/token_gather/all_gather | solution.py:305
  7.3 64.4 %all-gather.5.cloned.1.call-start = ((), (), s32[]{:S(2)}) async-start(), calls=%async_computation.2 | async-start | bytes 2654208 | tf_op jit(solution)/shard_map/token_gather/all_gather | solution.py:307
  8.8 4.4 %collective-permute-start.1 = (bf16[128,768]{1,0:T(8,128)(2,1)S(1)}, bf16[128,768]{1,0:T(8,128)(2,1)S(1)}, u32[]{:S(2)}, u32[]{:S(2)}) collective-permute-start(bf16[128,768]{1,0:T(8,128)(2,1)S(1)} %bitcast.17), channel_id=1, source_target_pairs={{0,8},{8,0},{1,9},{9,1},{2,10},{10,2},{3,11},{11,3},{4,12},{12,4},... | collective-permute-start | bytes 589832 | tf_op jit(solution)/shard_map/weight_gather/ppermute | solution.py:291
  12.1 10.2 %collective-permute-start = (bf16[256,512]{1,0:T(8,128)(2,1)S(1)}, bf16[256,512]{1,0:T(8,128)(2,1)S(1)}, u32[]{:S(2)}, u32[]{:S(2)}) collective-permute-start(bf16[256,512]{1,0:T(8,128)(2,1)S(1)} %copy-done.10), channel_id=1, source_target_pairs={{0,4},{4,0},{1,5},{5,1},{2,6},{6,2},{3,7},{7,3},{8,12},{12,8},{9,1... | collective-permute-start | bytes 786440 | tf_op jit(solution)/shard_map/token_swap/ppermute | solution.py:294
  13.2 16.7 %collective-permute-start.3 = (bf16[256,768]{1,0:T(8,128)(2,1)S(1)}, bf16[256,768]{1,0:T(8,128)(2,1)S(1)}, u32[]{:S(2)}, u32[]{:S(2)}) collective-permute-start(bf16[256,768]{1,0:T(8,128)(2,1)S(1)} %pad_maximum_fusion.refs_3_), channel_id=1, source_target_pairs={{0,192},{64,0},{128,64},{192,128},{1,193},{65,1},{129,65},{193,129... | collective-permute-start | bytes 1179656 | tf_op jit(solution)/shard_map/weight_rings/ppermute | solution.py:23
  15.1 14.8 %collective-permute-start.2 = (bf16[256,768]{1,0:T(8,128)(2,1)S(1)}, bf16[256,768]{1,0:T(8,128)(2,1)S(1)}, u32[]{:S(2)}, u32[]{:S(2)}) collective-permute-start(bf16[256,768]{1,0:T(8,128)(2,1)S(1)} %pad_maximum_fusion.refs_3_), channel_id=1, source_target_pairs={{0,64},{64,128},{128,192},{192,0},{1,65},{65,129},{129,193},{193,1... | collective-permute-start | bytes 1179656 | tf_op jit(solution)/shard_map/weight_rings/ppermute | solution.py:23
  15.1 21.7 %collective-permute-start.7 = (bf16[256,768]{1,0:T(8,128)(2,1)S(1)}, bf16[256,768]{1,0:T(8,128)(2,1)S(1)}, u32[]{:S(2)}, u32[]{:S(2)}) collective-permute-start(bf16[256,768]{1,0:T(8,128)(2,1)S(1)} %pad_maximum_fusion.refs_3_), channel_id=1, source_target_pairs={{0,48},{16,0},{32,16},{48,32},{1,49},{17,1},{33,17},{49,33},{2,50}... | collective-permute-start | bytes 1179656 | tf_op jit(solution)/shard_map/weight_rings/ppermute | solution.py:23
  20.3 16.5 %collective-permute-start.6 = (bf16[256,768]{1,0:T(8,128)(2,1)S(1)}, bf16[256,768]{1,0:T(8,128)(2,1)S(1)}, u32[]{:S(2)}, u32[]{:S(2)}) collective-permute-start(bf16[256,768]{1,0:T(8,128)(2,1)S(1)} %pad_maximum_fusion.refs_3_), channel_id=1, source_target_pairs={{0,16},{16,32},{32,48},{48,0},{1,17},{17,33},{33,49},{49,1},{2,18}... | collective-permute-start | bytes 1179656 | tf_op jit(solution)/shard_map/weight_rings/ppermute | solution.py:23
  22.3 15.0 %collective-permute-start.5 = (bf16[256,768]{1,0:T(8,128)(2,1)S(1)}, bf16[256,768]{1,0:T(8,128)(2,1)S(1)}, u32[]{:S(2)}, u32[]{:S(2)}) collective-permute-start(bf16[256,768]{1,0:T(8,128)(2,1)S(1)} %pad_maximum_fusion.refs_3_), channel_id=1, source_target_pairs={{0,128},{64,192},{128,0},{192,64},{1,129},{65,193},{129,1},{193,65... | collective-permute-start | bytes 1179656 | tf_op jit(solution)/shard_map/weight_rings/ppermute | solution.py:23
  29.9 10.8 %collective-permute-start.4 = (bf16[32,512]{1,0:T(8,128)(2,1)S(1)}, bf16[32,512]{1,0:T(8,128)(2,1)S(1)}, u32[]{:S(2)}, u32[]{:S(2)}) collective-permute-start(bf16[32,512]{1,0:T(8,128)(2,1)S(1)} %pad_maximum_fusion.3), channel_id=1, source_target_pairs={{8,16},{24,32},{40,48},{56,64},{72,80},{88,96},{104,112},{120,128}... | collective-permute-start | bytes 98312 | tf_op jit(solution)/shard_map/weight_rings/ppermute | solution.py:301
  37.3 4.2 %copy-start.2 = (bf16[256,768]{1,0:T(8,128)(2,1)}, bf16[256,768]{1,0:T(8,128)(2,1)S(1)}, u32[]{:S(2)}) copy-start(bf16[256,768]{1,0:T(8,128)(2,1)S(1)} %collective-permute-done.5.refs_10_) | copy-start | bytes 1179652
  42.4 17.9 %collective-permute-start.9 = (bf16[512,768]{1,0:T(8,128)(2,1)S(1)}, bf16[512,768]{1,0:T(8,128)(2,1)S(1)}, u32[]{:S(2)}, u32[]{:S(2)}) collective-permute-start(bf16[512,768]{1,0:T(8,128)(2,1)S(1)} %get-tuple-element.44.refs_4_), channel_id=1, source_target_pairs={{0,192},{64,0},{128,64},{192,128},{1,193},{65,1},{129,65},{193,129... | collective-permute-start | bytes 2359304 | tf_op jit(solution)/shard_map/weight_rings/ppermute | solution.py:23
  42.5 17.9 %collective-permute-start.8 = (bf16[512,768]{1,0:T(8,128)(2,1)S(1)}, bf16[512,768]{1,0:T(8,128)(2,1)S(1)}, u32[]{:S(2)}, u32[]{:S(2)}) collective-permute-start(bf16[512,768]{1,0:T(8,128)(2,1)S(1)} %get-tuple-element.44.refs_4_), channel_id=1, source_target_pairs={{0,64},{64,128},{128,192},{192,0},{1,65},{65,129},{129,193},{193,1... | collective-permute-start | bytes 2359304 | tf_op jit(solution)/shard_map/weight_rings/ppermute | solution.py:23
  44.1 6.7 %collective-permute-start.10 = (bf16[128,768]{1,0:T(8,128)(2,1)S(1)}, bf16[128,768]{1,0:T(8,128)(2,1)S(1)}, u32[]{:S(2)}, u32[]{:S(2)}) collective-permute-start(bf16[128,768]{1,0:T(8,128)(2,1)S(1)} %get-tuple-element.45), channel_id=1, source_target_pairs={{0,16},{16,32},{32,48},{48,0},{1,17},{17,33},{33,49},{49,1},{2,18}... | collective-permute-start | bytes 589832 | tf_op jit(solution)/shard_map/weight_rings/ppermute | solution.py:23
  44.5 6.5 %collective-permute-start.11 = (bf16[128,768]{1,0:T(8,128)(2,1)S(1)}, bf16[128,768]{1,0:T(8,128)(2,1)S(1)}, u32[]{:S(2)}, u32[]{:S(2)}) collective-permute-start(bf16[128,768]{1,0:T(8,128)(2,1)S(1)} %get-tuple-element.46), channel_id=1, source_target_pairs={{0,48},{16,0},{32,16},{48,32},{1,49},{17,1},{33,17},{49,33},{2,50}... | collective-permute-start | bytes 589832 | tf_op jit(solution)/shard_map/weight_rings/ppermute | solution.py:23
  61.7 20.3 %collective-permute-start.12 = (bf16[256,768]{1,0:T(8,128)(2,1)}, bf16[256,768]{1,0:T(8,128)(2,1)}, u32[]{:S(2)}, u32[]{:S(2)}) collective-permute-start(bf16[256,768]{1,0:T(8,128)(2,1)} %get-tuple-element.56), channel_id=1, source_target_pairs={{0,64},{64,128},{128,192},{192,0},{1,65},{65,129},{129,193},{193,1... | collective-permute-start | bytes 1179656 | tf_op jit(solution)/shard_map/weight_rings/ppermute | solution.py:23
  63.3 18.7 %collective-permute-start.13 = (bf16[256,768]{1,0:T(8,128)(2,1)}, bf16[256,768]{1,0:T(8,128)(2,1)}, u32[]{:S(2)}, u32[]{:S(2)}) collective-permute-start(bf16[256,768]{1,0:T(8,128)(2,1)} %get-tuple-element.57), channel_id=1, source_target_pairs={{0,192},{64,0},{128,64},{192,128},{1,193},{65,1},{129,65},{193,129... | collective-permute-start | bytes 1179656 | tf_op jit(solution)/shard_map/weight_rings/ppermute | solution.py:23
  64.9 17.1 %collective-permute-start.14 = (bf16[256,768]{1,0:T(8,128)(2,1)}, bf16[256,768]{1,0:T(8,128)(2,1)}, u32[]{:S(2)}, u32[]{:S(2)}) collective-permute-start(bf16[256,768]{1,0:T(8,128)(2,1)} %get-tuple-element.58), channel_id=1, source_target_pairs={{0,16},{16,32},{32,48},{48,0},{1,17},{17,33},{33,49},{49,1},{2,18}... | collective-permute-start | bytes 1179656 | tf_op jit(solution)/shard_map/weight_rings/ppermute | solution.py:23
  67.3 14.7 %collective-permute-start.15 = (bf16[256,768]{1,0:T(8,128)(2,1)}, bf16[256,768]{1,0:T(8,128)(2,1)}, u32[]{:S(2)}, u32[]{:S(2)}) collective-permute-start(bf16[256,768]{1,0:T(8,128)(2,1)} %get-tuple-element.59), channel_id=1, source_target_pairs={{0,48},{16,0},{32,16},{48,32},{1,49},{17,1},{33,17},{49,33},{2,50}... | collective-permute-start | bytes 1179656 | tf_op jit(solution)/shard_map/weight_rings/ppermute | solution.py:23
  68.5 13.5 %collective-permute-start.16 = (bf16[256,768]{1,0:T(8,128)(2,1)}, bf16[256,768]{1,0:T(8,128)(2,1)}, u32[]{:S(2)}, u32[]{:S(2)}) collective-permute-start(bf16[256,768]{1,0:T(8,128)(2,1)} %get-tuple-element.51.refs_5_), channel_id=1, source_target_pairs={{0,128},{64,192},{128,0},{192,64},{1,129},{65,193},{129,1},{193,65... | collective-permute-start | bytes 1179656 | tf_op jit(solution)/shard_map/weight_rings/ppermute | solution.py:23
  71.7 1.7 %copy-start = (bf16[2304,512]{1,0:T(8,128)(2,1)S(1)}, bf16[2304,512]{1,0:T(8,128)(2,1)}, u32[]{:S(2)}) copy-start(bf16[2304,512]{1,0:T(8,128)(2,1)} %all-gather.5.cloned.1.call-done.refs_2_) | copy-start | bytes 7077892
  73.4 1.6 %copy-start.1 = (bf16[2048,512]{1,0:T(8,128)(2,1)S(1)}, bf16[2048,512]{1,0:T(8,128)(2,1)}, u32[]{:S(2)}) copy-start(bf16[2048,512]{1,0:T(8,128)(2,1)} %all-gather.3.cloned.1.call-done.refs_1_) | copy-start | bytes 6291460
  74.9 1.0 copy-start.3
  75.9 6.1 %copy-start.4 = (f32[16,512]{1,0:T(8,128)S(1)}, f32[16,512]{1,0:T(8,128)}, u32[]{:S(2)}) copy-start(f32[16,512]{1,0:T(8,128)} %decay.3) | copy-start | bytes 98308
  75.9 6.1 %copy-start.7 = (f32[3,3,512]{2,1,0:T(4,128)S(1)}, f32[3,3,512]{2,1,0:T(4,128)}, u32[]{:S(2)}) copy-start(f32[3,3,512]{2,1,0:T(4,128)} %taps.1) | copy-start | bytes 55300
  82.1 14.4 %copy-start.5 = (f32[16,512]{1,0:T(8,128)S(1)}, f32[16,512]{1,0:T(8,128)}, u32[]{:S(2)}) copy-start(f32[16,512]{1,0:T(8,128)} %decay.3) | copy-start | bytes 98308
  82.1 14.4 %copy-start.6 = (f32[16,512]{1,0:T(8,128)S(1)}, f32[16,512]{1,0:T(8,128)}, u32[]{:S(2)}) copy-start(f32[16,512]{1,0:T(8,128)} %gain.3) | copy-start | bytes 98308
  82.1 14.4 %copy-start.8 = (f32[3,3,512]{2,1,0:T(4,128)S(1)}, f32[3,3,512]{2,1,0:T(4,128)}, u32[]{:S(2)}) copy-start(f32[3,3,512]{2,1,0:T(4,128)} %taps.1) | copy-start | bytes 55300
  82.1 14.4 %copy-start.9 = (f32[512]{0:T(512)S(1)}, f32[512]{0:T(512)}, u32[]{:S(2)}) copy-start(f32[512]{0:T(512)} %param.11) | copy-start | bytes 6148
  87.2 18.8 %all-to-all-start = ((bf16[16,16,256]{2,1,0:T(8,128)(2,1)}), bf16[16,16,256]{2,1,0:T(8,128)(2,1)S(1)}, u32[]{:S(2)}, u32[]{:S(2)}) async-start(bf16[16,16,256]{2,1,0:T(8,128)(2,1)} %get-tuple-element.66), calls=%async_computation | async-start | bytes 262144 | tf_op jit(solution)/shard_map/state_exchange/all_to_all | solution.py:387
  107.6 4.7 %collective-permute-start.17 = (bf16[256,256]{1,0:T(8,128)(2,1)S(1)}, bf16[256,256]{1,0:T(8,128)(2,1)S(1)}, u32[]{:S(2)}, u32[]{:S(2)}) collective-permute-start(bf16[256,256]{1,0:T(8,128)(2,1)S(1)} %get-tuple-element.68), channel_id=1, source_target_pairs={{0,8},{8,0},{1,9},{9,1},{2,10},{10,2},{3,11},{11,3},{4,12},{12,4},... | collective-permute-start | bytes 393224 | tf_op jit(solution)/shard_map/result_swap/ppermute | solution.py:409
Sparse Core Ops, SparseCore 0:
  9.2 31.8 all-gather.2
  43.0 28.6 all-gather.4

commit v18 on v17

--- a/solution.py
+++ b/solution.py
@@ -328,10 +328,9 @@
         early_runs += [(dy, dh, 0, two) for dh in (0, 1, -1)]
     early += [farther]
     early_runs += [(2, 0, 0, two)]
-    late = [*farther_pair, *far_opposite, last]
-    late_runs = [(2, 1, 0, two), (2, -1, 0, two)]
+    late = [*farther_pair, last, *far_opposite]
+    late_runs = [(2, 1, 0, two), (2, -1, 0, two), (2, 2, 0, two)]
     late_runs += [(dy, 2, skip, half) for skip in (0, half) for dy in (1, -1)]
-    late_runs += [(2, 2, 0, two)]
 
     vmem = pl.BlockSpec(memory_space=pltpu.VMEM)
     smem = pl.BlockSpec(memory_space=pltpu.SMEM)

time: 120 us -> 120 us (level)
  no operation moved by 1% of the time
where the time goes in v18:
time: 120 us
  starting transfers between devices  51.3 us (43%)
  waiting for transfers between devices  30 us (25%)
  Pallas kernels  17.4 us (14%)
  between operations  13.7 us (11%)
  local copies, waits for them, and re-layouts  5.95 us (5%)
  other arithmetic  1.53 us (1%)
    ppermute x14, starting transfers between devices, shifted(): return lax.ppermute(array, axis, [(i, (i + step) % n) for i in range(n)])  28.1 us
    ppermute x14, waiting for transfers between devices, shifted(): return lax.ppermute(array, axis, [(i, (i + step) % n) for i in range(n)])  13.2 us
    all_to_all x1, starting transfers between devices, body(): states = lax.all_to_all(state, ('y', 'h'), 0, 0, tiled=True)  9.28 us
    all_to_all x1, waiting for transfers between devices, body(): states = lax.all_to_all(state, ('y', 'h'), 0, 0, tiled=True)  7 us
    ppermute x1, starting transfers between devices, body(): halos = lax.ppermute(tails, CTX, [(i, i + 1) for i in range(1, 31, 2)])  6.87 us
    pallas_call x1, Pallas kernels, body(): pl.pallas_call(functools.partial(project_kernel, sizes, early_runs, late_...  6.06 us
    unnamed x23, local copies, waits for them, and re-layouts  5.5 us
    pallas_call x1, Pallas kernels, body(): pl.pallas_call(functools.partial(state_kernel, sizes), out_shape=(full, j...  5.08 us
  transfers between devices with their start and end apart: 21, of which 10 were waited for; matrix products, arithmetic and copies ran while one was open for 2% of the time, Pallas kernels for 9%

profile of v18, /device:TPU:1, one launch (start us, length us, event | category | flops | bytes accessed | tf_op | source)
XLA Modules:
  0.0 119.8 jit_solution(16893790236980734318)
XLA Ops:
  6.5 0.0 all-gather.3.cloned.1.call-start
  6.5 0.7 all-gather.3.cloned.1.call-update
  7.3 0.0 all-gather.5.cloned.1.call-start
  7.3 1.2 %copy.10 = bf16[128,3,512]{0,2,1:T(8,128)(2,1)S(1)} copy(bf16[128,3,512]{2,0,1:T(8,128)(2,1)} %param.7) | data formatting | bytes 786432 | tf_op args[1]
  8.6 0.1 copy.13
  8.8 3.3 %collective-permute-start.1 = (bf16[128,768]{1,0:T(8,128)(2,1)S(1)}, bf16[128,768]{1,0:T(8,128)(2,1)S(1)}, u32[]{:S(2)}, u32[]{:S(2)}) collective-permute-start(bf16[128,768]{1,0:T(8,128)(2,1)S(1)} %bitcast.17), channel_id=1, source_target_pairs={{0,8},{8,0},{1,9},{9,1},{2,10},{10,2},{3,11},{11,3},{4,12},{12,4},... | collective-permute-start | bytes 589832 | tf_op jit(solution)/shard_map/weight_gather/ppermute | solution.py:291
  12.1 0.0 copy-done.10
  12.1 0.0 collective-permute-start
  12.1 0.1 copy.12
  12.2 0.9 collective-permute-done.1
  13.2 1.8 %collective-permute-start.3 = (bf16[256,768]{1,0:T(8,128)(2,1)S(1)}, bf16[256,768]{1,0:T(8,128)(2,1)S(1)}, u32[]{:S(2)}, u32[]{:S(2)}) collective-permute-start(bf16[256,768]{1,0:T(8,128)(2,1)S(1)} %pad_maximum_fusion.refs_3_), channel_id=1, source_target_pairs={{0,192},{64,0},{128,64},{192,128},{1,193},{65,1},{129,65},{193,129... | collective-permute-start | bytes 1179656 | tf_op jit(solution)/shard_map/weight_rings/ppermute | solution.py:23
  15.1 0.0 collective-permute-start.2
  15.1 5.3 %collective-permute-start.7 = (bf16[256,768]{1,0:T(8,128)(2,1)S(1)}, bf16[256,768]{1,0:T(8,128)(2,1)S(1)}, u32[]{:S(2)}, u32[]{:S(2)}) collective-permute-start(bf16[256,768]{1,0:T(8,128)(2,1)S(1)} %pad_maximum_fusion.refs_3_), channel_id=1, source_target_pairs={{0,48},{16,0},{32,16},{48,32},{1,49},{17,1},{33,17},{49,33},{2,50}... | collective-permute-start | bytes 1179656 | tf_op jit(solution)/shard_map/weight_rings/ppermute | solution.py:23
  20.3 0.0 collective-permute-start.6
  20.3 1.9 %collective-permute-done = bf16[256,512]{1,0:T(8,128)(2,1)S(1)} collective-permute-done((bf16[256,512]{1,0:T(8,128)(2,1)S(1)}, bf16[256,512]{1,0:T(8,128)(2,1)S(1)}, u32[]{:S(2)}, u32[]{:S(2)}) %collective-permute-start) | collective-permute-done | bytes 262176 | tf_op jit(solution)/shard_map/token_swap/ppermute | solution.py:294
  22.3 7.6 %collective-permute-start.5 = (bf16[256,768]{1,0:T(8,128)(2,1)S(1)}, bf16[256,768]{1,0:T(8,128)(2,1)S(1)}, u32[]{:S(2)}, u32[]{:S(2)}) collective-permute-start(bf16[256,768]{1,0:T(8,128)(2,1)S(1)} %pad_maximum_fusion.refs_3_), channel_id=1, source_target_pairs={{0,128},{64,192},{128,0},{192,64},{1,129},{65,193},{129,1},{193,65... | collective-permute-start | bytes 1179656 | tf_op jit(solution)/shard_map/weight_rings/ppermute | solution.py:23
  29.9 0.0 collective-permute-done.3.refs_8_
  29.9 0.0 collective-permute-done.2.refs_6_
  29.9 6.9 %collective-permute-start.4 = (bf16[32,512]{1,0:T(8,128)(2,1)S(1)}, bf16[32,512]{1,0:T(8,128)(2,1)S(1)}, u32[]{:S(2)}, u32[]{:S(2)}) collective-permute-start(bf16[32,512]{1,0:T(8,128)(2,1)S(1)} %pad_maximum_fusion.3), channel_id=1, source_target_pairs={{8,16},{24,32},{40,48},{56,64},{72,80},{88,96},{104,112},{120,128}... | collective-permute-start | bytes 98312 | tf_op jit(solution)/shard_map/weight_rings/ppermute | solution.py:301
  36.8 0.0 collective-permute-done.7.refs_1_
  36.8 0.0 collective-permute-done.6.refs_0_
  36.8 0.5 collective-permute-done.5.refs_10_
  37.3 3.4 %collective-permute-done.4 = bf16[32,512]{1,0:T(8,128)(2,1)S(1)} collective-permute-done((bf16[32,512]{1,0:T(8,128)(2,1)S(1)}, bf16[32,512]{1,0:T(8,128)(2,1)S(1)}, u32[]{:S(2)}, u32[]{:S(2)}) %collective-permute-start.4) | collective-permute-done | bytes 32800 | tf_op jit(solution)/shard_map/weight_rings/ppermute | solution.py:301
  40.7 0.7 pad_maximum_fusion.1
  41.5 0.0 copy-done.2
  41.5 0.0 all-gather.5.cloned.1.call-update
  41.5 0.9 relay_pair.1
  42.4 0.1 collective-permute-start.9
  42.5 1.5 %collective-permute-start.8 = (bf16[512,768]{1,0:T(8,128)(2,1)S(1)}, bf16[512,768]{1,0:T(8,128)(2,1)S(1)}, u32[]{:S(2)}, u32[]{:S(2)}) collective-permute-start(bf16[512,768]{1,0:T(8,128)(2,1)S(1)} %get-tuple-element.44.refs_4_), channel_id=1, source_target_pairs={{0,64},{64,128},{128,192},{192,0},{1,65},{65,129},{129,193},{193,1... | collective-permute-start | bytes 2359304 | tf_op jit(solution)/shard_map/weight_rings/ppermute | solution.py:23
  44.1 0.4 collective-permute-start.10
  44.5 3.2 %collective-permute-start.11 = (bf16[128,768]{1,0:T(8,128)(2,1)S(1)}, bf16[128,768]{1,0:T(8,128)(2,1)S(1)}, u32[]{:S(2)}, u32[]{:S(2)}) collective-permute-start(bf16[128,768]{1,0:T(8,128)(2,1)S(1)} %get-tuple-element.46), channel_id=1, source_target_pairs={{0,48},{16,0},{32,16},{48,32},{1,49},{17,1},{33,17},{49,33},{2,50}... | collective-permute-start | bytes 589832 | tf_op jit(solution)/shard_map/weight_rings/ppermute | solution.py:23
  47.6 3.1 %collective-permute-done.10.refs_2_ = bf16[128,768]{1,0:T(8,128)(2,1)S(1)} collective-permute-done((bf16[128,768]{1,0:T(8,128)(2,1)S(1)}, bf16[128,768]{1,0:T(8,128)(2,1)S(1)}, u32[]{:S(2)}, u32[]{:S(2)}) %collective-permute-start.10) | collective-permute-done | bytes 196640 | tf_op jit(solution)/shard_map/weight_rings/ppermute | solution.py:23
  50.8 0.2 collective-permute-done.11.refs_3_
  51.0 9.4 %collective-permute-done.9.refs_1_.refs_9_ = bf16[512,768]{1,0:T(8,128)(2,1)S(1)} collective-permute-done((bf16[512,768]{1,0:T(8,128)(2,1)S(1)}, bf16[512,768]{1,0:T(8,128)(2,1)S(1)}, u32[]{:S(2)}, u32[]{:S(2)}) %collective-permute-start.9) | collective-permute-done | bytes 786464 | tf_op jit(solution)/shard_map/weight_rings/ppermute | solution.py:23
  60.4 0.0 collective-permute-done.8.refs_0_.refs_7_
  60.4 1.4 %relay_far.1 = (bf16[256,768]{1,0:T(8,128)(2,1)}, bf16[256,768]{1,0:T(8,128)(2,1)}, bf16[256,768]{1,0:T(8,128)(2,1)}, bf16[256,768]{1,0:T(8,128)(2,1)}, bf16[256,768]{1,0:T(8,128)(2,1)}) custom-call(bf16[512,768]{1,0:T(8,128)(2,1)S(1)} %collective-permute-done.8.refs_0_.refs_7_, bf16[512,768]{1,0:T(8,128)(2,1)S(1)} %collective-permute-done.9.refs_1_.refs_9_, ...), custom_call_target="tpu_custom_call" | custom-call | bytes 2000000 | tf_op jit(solution)/shard_map/weight_rings/relay_far/pallas_call | solution.py:54
  61.7 1.6 %collective-permute-start.12 = (bf16[256,768]{1,0:T(8,128)(2,1)}, bf16[256,768]{1,0:T(8,128)(2,1)}, u32[]{:S(2)}, u32[]{:S(2)}) collective-permute-start(bf16[256,768]{1,0:T(8,128)(2,1)} %get-tuple-element.56), channel_id=1, source_target_pairs={{0,64},{64,128},{128,192},{192,0},{1,65},{65,129},{129,193},{193,1... | collective-permute-start | bytes 1179656 | tf_op jit(solution)/shard_map/weight_rings/ppermute | solution.py:23
  63.3 1.6 %collective-permute-start.13 = (bf16[256,768]{1,0:T(8,128)(2,1)}, bf16[256,768]{1,0:T(8,128)(2,1)}, u32[]{:S(2)}, u32[]{:S(2)}) collective-permute-start(bf16[256,768]{1,0:T(8,128)(2,1)} %get-tuple-element.57), channel_id=1, source_target_pairs={{0,192},{64,0},{128,64},{192,128},{1,193},{65,1},{129,65},{193,129... | collective-permute-start | bytes 1179656 | tf_op jit(solution)/shard_map/weight_rings/ppermute | solution.py:23
  64.9 2.4 %collective-permute-start.15 = (bf16[256,768]{1,0:T(8,128)(2,1)}, bf16[256,768]{1,0:T(8,128)(2,1)}, u32[]{:S(2)}, u32[]{:S(2)}) collective-permute-start(bf16[256,768]{1,0:T(8,128)(2,1)} %get-tuple-element.58), channel_id=1, source_target_pairs={{0,16},{16,32},{32,48},{48,0},{1,17},{17,33},{33,49},{49,1},{2,18}... | collective-permute-start | bytes 1179656 | tf_op jit(solution)/shard_map/weight_rings/ppermute | solution.py:23
  67.3 1.2 %collective-permute-start.16 = (bf16[256,768]{1,0:T(8,128)(2,1)}, bf16[256,768]{1,0:T(8,128)(2,1)}, u32[]{:S(2)}, u32[]{:S(2)}) collective-permute-start(bf16[256,768]{1,0:T(8,128)(2,1)} %get-tuple-element.59), channel_id=1, source_target_pairs={{0,48},{16,0},{32,16},{48,32},{1,49},{17,1},{33,17},{49,33},{2,50}... | collective-permute-start | bytes 1179656 | tf_op jit(solution)/shard_map/weight_rings/ppermute | solution.py:23
  68.5 1.4 %collective-permute-start.14 = (bf16[256,768]{1,0:T(8,128)(2,1)}, bf16[256,768]{1,0:T(8,128)(2,1)}, u32[]{:S(2)}, u32[]{:S(2)}) collective-permute-start(bf16[256,768]{1,0:T(8,128)(2,1)} %get-tuple-element.51.refs_5_), channel_id=1, source_target_pairs={{0,128},{64,192},{128,0},{192,64},{1,129},{65,193},{129,1},{193,65... | collective-permute-start | bytes 1179656 | tf_op jit(solution)/shard_map/weight_rings/ppermute | solution.py:23
  69.9 0.1 stack.23.refs_0_.pos
  70.0 1.7 %all-gather.5.cloned.1.call-done.refs_2_ = bf16[2304,512]{1,0:T(8,128)(2,1)} async-done(((bf16[288,512]{1,0:T(8,128)(2,1)}), bf16[2304,512]{1,0:T(8,128)(2,1)}) %all-gather.5.cloned.1.call-update) | async-done | bytes 2359312 | tf_op jit(solution)/shard_map/token_gather/all_gather | solution.py:307
  71.7 1.7 %copy-done = bf16[2304,512]{1,0:T(8,128)(2,1)S(1)} copy-done((bf16[2304,512]{1,0:T(8,128)(2,1)S(1)}, bf16[2304,512]{1,0:T(8,128)(2,1)}, u32[]{:S(2)}) %copy-start) | copy-done | bytes 2359320
  73.4 1.6 %copy-done.1 = bf16[2048,512]{1,0:T(8,128)(2,1)S(1)} copy-done((bf16[2048,512]{1,0:T(8,128)(2,1)S(1)}, bf16[2048,512]{1,0:T(8,128)(2,1)}, u32[]{:S(2)}) %copy-start.1) | copy-done | bytes 2097176
  74.9 1.0 copy-done.3
  75.9 6.1 %project.1 = (f32[6,528,128]{2,1,0:T(8,128)S(1)}, bf16[528,1280]{1,0:T(8,128)(2,1)S(1)}) custom-call(s32[5]{0:T(128)S(1)} %stack.23.refs_0_.pos, bf16[2048,512]{1,0:T(8,128)(2,1)S(1)} %copy-done.1, bf16[2304,512]{1,0:T(8,128)(2,1)S(1)} %copy-done, bf16[256,768]{1,0:T(8,128)(2,1)S(1)} %pad_maximum_fusion.refs_3_, ...), custom_call_target="tpu_custom_call" | custom-call | flops 2283798528 | bytes 9000000 | tf_op jit(solution)/shard_map/project/pallas_call | solution.py:346
  82.0 0.0 collective-permute-done.12.refs_2_
  82.0 0.0 collective-permute-done.13.refs_3_
  82.0 0.0 collective-permute-done.15.refs_5_
  82.0 0.0 collective-permute-done.16.refs_6_
  82.1 0.0 collective-permute-done.14.refs_4_
  82.1 0.0 copy-start.5
  82.1 0.0 copy-start.6
  82.1 0.0 copy-start.8
  82.1 0.0 copy-start.9
  82.1 5.1 %states.1 = (f32[64,8,256]{2,1,0:T(8,128)S(1)}, f32[2,528,128]{2,1,0:T(8,128)S(1)}, bf16[16,16,256]{2,1,0:T(8,128)(2,1)}) custom-call(s32[5]{0:T(128)S(1)} %stack.23.refs_0_.pos, bf16[528,1280]{1,0:T(8,128)(2,1)S(1)} %get-tuple-element.55.refs_1_, bf16[256,768]{1,0:T(8,128)(2,1)} %collective-permute-done.12.refs_2_, ...), custom_call_target="tpu_custom_call" | custom-call | tf_op jit(solution)/shard_map/states/pallas_call | solution.py:368
  87.2 9.3 %all-to-all-start = ((bf16[16,16,256]{2,1,0:T(8,128)(2,1)}), bf16[16,16,256]{2,1,0:T(8,128)(2,1)S(1)}, u32[]{:S(2)}, u32[]{:S(2)}) async-start(bf16[16,16,256]{2,1,0:T(8,128)(2,1)} %get-tuple-element.66), calls=%async_computation | async-start | bytes 262144 | tf_op jit(solution)/shard_map/state_exchange/all_to_all | solution.py:386
  96.5 2.5 %local.1 = (f32[64,8,256]{2,1,0:T(8,128)S(1)}, f32[64,8,256]{2,1,0:T(8,128)S(1)}, f32[16,8,256]{2,1,0:T(8,128)S(1)}) custom-call(s32[5]{0:T(128)S(1)} %stack.23.refs_0_.pos, f32[2,528,128]{2,1,0:T(8,128)S(1)} %get-tuple-element.61.gated, f32[3,3,512]{2,1,0:T(4,128)S(1)} %copy-done.8, f32[64,8,256]{2,1,0:T(8,128)S(1)} %get-tuple-element.62.product, ...), custom_call_target="tpu_custom_call" | custom-call | flops 30000000 | bytes 2000000 | tf_op jit(solution)/shard_map/local/pallas_call | solution.py:387
  99.0 7.0 %all-to-all-done.states = bf16[16,16,256]{2,1,0:T(8,128)(2,1)S(1)} async-done(((bf16[16,16,256]{2,1,0:T(8,128)(2,1)}), bf16[16,16,256]{2,1,0:T(8,128)(2,1)S(1)}, u32[]{:S(2)}, u32[]{:S(2)}) %all-to-all-start) | async-done | bytes 131104 | tf_op jit(solution)/shard_map/state_exchange/all_to_all | solution.py:386
  106.0 1.5 %finish.1 = (bf16[256,256]{1,0:T(8,128)(2,1)S(1)}, bf16[256,256]{1,0:T(8,128)(2,1)S(1)}) custom-call(s32[5]{0:T(128)S(1)} %stack.23.refs_0_.pos, f32[64,8,256]{2,1,0:T(8,128)S(1)} %get-tuple-element.63.gate, f32[64,8,256]{2,1,0:T(8,128)S(1)} %get-tuple-element.64.local, f32[16,8,256]{2,1,0:T(8,128)S(1)} %get-tuple-element.65.inside, ...), custom_call_target="tpu_custom_call" | custom-call | tf_op jit(solution)/shard_map/finish/pallas_call | solution.py:398
  107.6 3.7 %collective-permute-start.17 = (bf16[256,256]{1,0:T(8,128)(2,1)S(1)}, bf16[256,256]{1,0:T(8,128)(2,1)S(1)}, u32[]{:S(2)}, u32[]{:S(2)}) collective-permute-start(bf16[256,256]{1,0:T(8,128)(2,1)S(1)} %get-tuple-element.68), channel_id=1, source_target_pairs={{0,8},{8,0},{1,9},{9,1},{2,10},{10,2},{3,11},{11,3},{4,12},{12,4},... | collective-permute-start | bytes 393224 | tf_op jit(solution)/shard_map/result_swap/ppermute | solution.py:408
  111.2 1.0 collective-permute-done.17
  112.3 0.7 pad_maximum_fusion.2
  (22 shorter events, 0.2 us)
Async XLA Ops:
  6.5 5.6 %copy-start.10 = (bf16[256,512]{1,0:T(8,128)(2,1)S(1)}, bf16[256,512]{1,0:T(8,128)(2,1)}, u32[]{:S(2)}) copy-start(bf16[256,512]{1,0:T(8,128)(2,1)} %param.6) | copy-start | bytes 786436
  6.5 63.4 %all-gather.3.cloned.1.call-start = ((), (), s32[]{:S(2)}) async-start(), calls=%async_computation.1 | async-start | bytes 2359296 | tf_op jit(solution)/shard_map/token_gather/all_gather | solution.py:305
  7.3 64.4 %all-gather.5.cloned.1.call-start = ((), (), s32[]{:S(2)}) async-start(), calls=%async_computation.2 | async-start | bytes 2654208 | tf_op jit(solution)/shard_map/token_gather/all_gather | solution.py:307
  8.8 4.4 %collective-permute-start.1 = (bf16[128,768]{1,0:T(8,128)(2,1)S(1)}, bf16[128,768]{1,0:T(8,128)(2,1)S(1)}, u32[]{:S(2)}, u32[]{:S(2)}) collective-permute-start(bf16[128,768]{1,0:T(8,128)(2,1)S(1)} %bitcast.17), channel_id=1, source_target_pairs={{0,8},{8,0},{1,9},{9,1},{2,10},{10,2},{3,11},{11,3},{4,12},{12,4},... | collective-permute-start | bytes 589832 | tf_op jit(solution)/shard_map/weight_gather/ppermute | solution.py:291
  12.1 10.2 %collective-permute-start = (bf16[256,512]{1,0:T(8,128)(2,1)S(1)}, bf16[256,512]{1,0:T(8,128)(2,1)S(1)}, u32[]{:S(2)}, u32[]{:S(2)}) collective-permute-start(bf16[256,512]{1,0:T(8,128)(2,1)S(1)} %copy-done.10), channel_id=1, source_target_pairs={{0,4},{4,0},{1,5},{5,1},{2,6},{6,2},{3,7},{7,3},{8,12},{12,8},{9,1... | collective-permute-start | bytes 786440 | tf_op jit(solution)/shard_map/token_swap/ppermute | solution.py:294
  13.2 16.7 %collective-permute-start.3 = (bf16[256,768]{1,0:T(8,128)(2,1)S(1)}, bf16[256,768]{1,0:T(8,128)(2,1)S(1)}, u32[]{:S(2)}, u32[]{:S(2)}) collective-permute-start(bf16[256,768]{1,0:T(8,128)(2,1)S(1)} %pad_maximum_fusion.refs_3_), channel_id=1, source_target_pairs={{0,192},{64,0},{128,64},{192,128},{1,193},{65,1},{129,65},{193,129... | collective-permute-start | bytes 1179656 | tf_op jit(solution)/shard_map/weight_rings/ppermute | solution.py:23
  15.1 14.8 %collective-permute-start.2 = (bf16[256,768]{1,0:T(8,128)(2,1)S(1)}, bf16[256,768]{1,0:T(8,128)(2,1)S(1)}, u32[]{:S(2)}, u32[]{:S(2)}) collective-permute-start(bf16[256,768]{1,0:T(8,128)(2,1)S(1)} %pad_maximum_fusion.refs_3_), channel_id=1, source_target_pairs={{0,64},{64,128},{128,192},{192,0},{1,65},{65,129},{129,193},{193,1... | collective-permute-start | bytes 1179656 | tf_op jit(solution)/shard_map/weight_rings/ppermute | solution.py:23
  15.1 21.7 %collective-permute-start.7 = (bf16[256,768]{1,0:T(8,128)(2,1)S(1)}, bf16[256,768]{1,0:T(8,128)(2,1)S(1)}, u32[]{:S(2)}, u32[]{:S(2)}) collective-permute-start(bf16[256,768]{1,0:T(8,128)(2,1)S(1)} %pad_maximum_fusion.refs_3_), channel_id=1, source_target_pairs={{0,48},{16,0},{32,16},{48,32},{1,49},{17,1},{33,17},{49,33},{2,50}... | collective-permute-start | bytes 1179656 | tf_op jit(solution)/shard_map/weight_rings/ppermute | solution.py:23
  20.3 16.5 %collective-permute-start.6 = (bf16[256,768]{1,0:T(8,128)(2,1)S(1)}, bf16[256,768]{1,0:T(8,128)(2,1)S(1)}, u32[]{:S(2)}, u32[]{:S(2)}) collective-permute-start(bf16[256,768]{1,0:T(8,128)(2,1)S(1)} %pad_maximum_fusion.refs_3_), channel_id=1, source_target_pairs={{0,16},{16,32},{32,48},{48,0},{1,17},{17,33},{33,49},{49,1},{2,18}... | collective-permute-start | bytes 1179656 | tf_op jit(solution)/shard_map/weight_rings/ppermute | solution.py:23
  22.3 15.0 %collective-permute-start.5 = (bf16[256,768]{1,0:T(8,128)(2,1)S(1)}, bf16[256,768]{1,0:T(8,128)(2,1)S(1)}, u32[]{:S(2)}, u32[]{:S(2)}) collective-permute-start(bf16[256,768]{1,0:T(8,128)(2,1)S(1)} %pad_maximum_fusion.refs_3_), channel_id=1, source_target_pairs={{0,128},{64,192},{128,0},{192,64},{1,129},{65,193},{129,1},{193,65... | collective-permute-start | bytes 1179656 | tf_op jit(solution)/shard_map/weight_rings/ppermute | solution.py:23
  29.9 10.8 %collective-permute-start.4 = (bf16[32,512]{1,0:T(8,128)(2,1)S(1)}, bf16[32,512]{1,0:T(8,128)(2,1)S(1)}, u32[]{:S(2)}, u32[]{:S(2)}) collective-permute-start(bf16[32,512]{1,0:T(8,128)(2,1)S(1)} %pad_maximum_fusion.3), channel_id=1, source_target_pairs={{8,16},{24,32},{40,48},{56,64},{72,80},{88,96},{104,112},{120,128}... | collective-permute-start | bytes 98312 | tf_op jit(solution)/shard_map/weight_rings/ppermute | solution.py:301
  37.3 4.2 %copy-start.2 = (bf16[256,768]{1,0:T(8,128)(2,1)}, bf16[256,768]{1,0:T(8,128)(2,1)S(1)}, u32[]{:S(2)}) copy-start(bf16[256,768]{1,0:T(8,128)(2,1)S(1)} %collective-permute-done.5.refs_10_) | copy-start | bytes 1179652
  42.4 17.9 %collective-permute-start.9 = (bf16[512,768]{1,0:T(8,128)(2,1)S(1)}, bf16[512,768]{1,0:T(8,128)(2,1)S(1)}, u32[]{:S(2)}, u32[]{:S(2)}) collective-permute-start(bf16[512,768]{1,0:T(8,128)(2,1)S(1)} %get-tuple-element.44.refs_4_), channel_id=1, source_target_pairs={{0,192},{64,0},{128,64},{192,128},{1,193},{65,1},{129,65},{193,129... | collective-permute-start | bytes 2359304 | tf_op jit(solution)/shard_map/weight_rings/ppermute | solution.py:23
  42.5 17.9 %collective-permute-start.8 = (bf16[512,768]{1,0:T(8,128)(2,1)S(1)}, bf16[512,768]{1,0:T(8,128)(2,1)S(1)}, u32[]{:S(2)}, u32[]{:S(2)}) collective-permute-start(bf16[512,768]{1,0:T(8,128)(2,1)S(1)} %get-tuple-element.44.refs_4_), channel_id=1, source_target_pairs={{0,64},{64,128},{128,192},{192,0},{1,65},{65,129},{129,193},{193,1... | collective-permute-start | bytes 2359304 | tf_op jit(solution)/shard_map/weight_rings/ppermute | solution.py:23
  44.1 6.7 %collective-permute-start.10 = (bf16[128,768]{1,0:T(8,128)(2,1)S(1)}, bf16[128,768]{1,0:T(8,128)(2,1)S(1)}, u32[]{:S(2)}, u32[]{:S(2)}) collective-permute-start(bf16[128,768]{1,0:T(8,128)(2,1)S(1)} %get-tuple-element.45), channel_id=1, source_target_pairs={{0,16},{16,32},{32,48},{48,0},{1,17},{17,33},{33,49},{49,1},{2,18}... | collective-permute-start | bytes 589832 | tf_op jit(solution)/shard_map/weight_rings/ppermute | solution.py:23
  44.5 6.5 %collective-permute-start.11 = (bf16[128,768]{1,0:T(8,128)(2,1)S(1)}, bf16[128,768]{1,0:T(8,128)(2,1)S(1)}, u32[]{:S(2)}, u32[]{:S(2)}) collective-permute-start(bf16[128,768]{1,0:T(8,128)(2,1)S(1)} %get-tuple-element.46), channel_id=1, source_target_pairs={{0,48},{16,0},{32,16},{48,32},{1,49},{17,1},{33,17},{49,33},{2,50}... | collective-permute-start | bytes 589832 | tf_op jit(solution)/shard_map/weight_rings/ppermute | solution.py:23
  61.7 20.3 %collective-permute-start.12 = (bf16[256,768]{1,0:T(8,128)(2,1)}, bf16[256,768]{1,0:T(8,128)(2,1)}, u32[]{:S(2)}, u32[]{:S(2)}) collective-permute-start(bf16[256,768]{1,0:T(8,128)(2,1)} %get-tuple-element.56), channel_id=1, source_target_pairs={{0,64},{64,128},{128,192},{192,0},{1,65},{65,129},{129,193},{193,1... | collective-permute-start | bytes 1179656 | tf_op jit(solution)/shard_map/weight_rings/ppermute | solution.py:23
  63.3 18.7 %collective-permute-start.13 = (bf16[256,768]{1,0:T(8,128)(2,1)}, bf16[256,768]{1,0:T(8,128)(2,1)}, u32[]{:S(2)}, u32[]{:S(2)}) collective-permute-start(bf16[256,768]{1,0:T(8,128)(2,1)} %get-tuple-element.57), channel_id=1, source_target_pairs={{0,192},{64,0},{128,64},{192,128},{1,193},{65,1},{129,65},{193,129... | collective-permute-start | bytes 1179656 | tf_op jit(solution)/shard_map/weight_rings/ppermute | solution.py:23
  64.9 17.1 %collective-permute-start.15 = (bf16[256,768]{1,0:T(8,128)(2,1)}, bf16[256,768]{1,0:T(8,128)(2,1)}, u32[]{:S(2)}, u32[]{:S(2)}) collective-permute-start(bf16[256,768]{1,0:T(8,128)(2,1)} %get-tuple-element.58), channel_id=1, source_target_pairs={{0,16},{16,32},{32,48},{48,0},{1,17},{17,33},{33,49},{49,1},{2,18}... | collective-permute-start | bytes 1179656 | tf_op jit(solution)/shard_map/weight_rings/ppermute | solution.py:23
  67.3 14.7 %collective-permute-start.16 = (bf16[256,768]{1,0:T(8,128)(2,1)}, bf16[256,768]{1,0:T(8,128)(2,1)}, u32[]{:S(2)}, u32[]{:S(2)}) collective-permute-start(bf16[256,768]{1,0:T(8,128)(2,1)} %get-tuple-element.59), channel_id=1, source_target_pairs={{0,48},{16,0},{32,16},{48,32},{1,49},{17,1},{33,17},{49,33},{2,50}... | collective-permute-start | bytes 1179656 | tf_op jit(solution)/shard_map/weight_rings/ppermute | solution.py:23
  68.5 13.5 %collective-permute-start.14 = (bf16[256,768]{1,0:T(8,128)(2,1)}, bf16[256,768]{1,0:T(8,128)(2,1)}, u32[]{:S(2)}, u32[]{:S(2)}) collective-permute-start(bf16[256,768]{1,0:T(8,128)(2,1)} %get-tuple-element.51.refs_5_), channel_id=1, source_target_pairs={{0,128},{64,192},{128,0},{192,64},{1,129},{65,193},{129,1},{193,65... | collective-permute-start | bytes 1179656 | tf_op jit(solution)/shard_map/weight_rings/ppermute | solution.py:23
  71.7 1.7 %copy-start = (bf16[2304,512]{1,0:T(8,128)(2,1)S(1)}, bf16[2304,512]{1,0:T(8,128)(2,1)}, u32[]{:S(2)}) copy-start(bf16[2304,512]{1,0:T(8,128)(2,1)} %all-gather.5.cloned.1.call-done.refs_2_) | copy-start | bytes 7077892
  73.4 1.6 %copy-start.1 = (bf16[2048,512]{1,0:T(8,128)(2,1)S(1)}, bf16[2048,512]{1,0:T(8,128)(2,1)}, u32[]{:S(2)}) copy-start(bf16[2048,512]{1,0:T(8,128)(2,1)} %all-gather.3.cloned.1.call-done.refs_1_) | copy-start | bytes 6291460
  74.9 1.0 copy-start.3
  75.9 6.1 %copy-start.4 = (f32[16,512]{1,0:T(8,128)S(1)}, f32[16,512]{1,0:T(8,128)}, u32[]{:S(2)}) copy-start(f32[16,512]{1,0:T(8,128)} %decay.3) | copy-start | bytes 98308
  75.9 6.1 %copy-start.7 = (f32[3,3,512]{2,1,0:T(4,128)S(1)}, f32[3,3,512]{2,1,0:T(4,128)}, u32[]{:S(2)}) copy-start(f32[3,3,512]{2,1,0:T(4,128)} %taps.1) | copy-start | bytes 55300
  82.1 14.4 %copy-start.5 = (f32[16,512]{1,0:T(8,128)S(1)}, f32[16,512]{1,0:T(8,128)}, u32[]{:S(2)}) copy-start(f32[16,512]{1,0:T(8,128)} %decay.3) | copy-start | bytes 98308
  82.1 14.4 %copy-start.6 = (f32[16,512]{1,0:T(8,128)S(1)}, f32[16,512]{1,0:T(8,128)}, u32[]{:S(2)}) copy-start(f32[16,512]{1,0:T(8,128)} %gain.3) | copy-start | bytes 98308
  82.1 14.4 %copy-start.8 = (f32[3,3,512]{2,1,0:T(4,128)S(1)}, f32[3,3,512]{2,1,0:T(4,128)}, u32[]{:S(2)}) copy-start(f32[3,3,512]{2,1,0:T(4,128)} %taps.1) | copy-start | bytes 55300
  82.1 14.4 %copy-start.9 = (f32[512]{0:T(512)S(1)}, f32[512]{0:T(512)}, u32[]{:S(2)}) copy-start(f32[512]{0:T(512)} %param.11) | copy-start | bytes 6148
  87.2 18.8 %all-to-all-start = ((bf16[16,16,256]{2,1,0:T(8,128)(2,1)}), bf16[16,16,256]{2,1,0:T(8,128)(2,1)S(1)}, u32[]{:S(2)}, u32[]{:S(2)}) async-start(bf16[16,16,256]{2,1,0:T(8,128)(2,1)} %get-tuple-element.66), calls=%async_computation | async-start | bytes 262144 | tf_op jit(solution)/shard_map/state_exchange/all_to_all | solution.py:386
  107.6 4.7 %collective-permute-start.17 = (bf16[256,256]{1,0:T(8,128)(2,1)S(1)}, bf16[256,256]{1,0:T(8,128)(2,1)S(1)}, u32[]{:S(2)}, u32[]{:S(2)}) collective-permute-start(bf16[256,256]{1,0:T(8,128)(2,1)S(1)} %get-tuple-element.68), channel_id=1, source_target_pairs={{0,8},{8,0},{1,9},{9,1},{2,10},{10,2},{3,11},{11,3},{4,12},{12,4},... | collective-permute-start | bytes 393224 | tf_op jit(solution)/shard_map/result_swap/ppermute | solution.py:408
Sparse Core Ops, SparseCore 0:
  9.2 31.8 all-gather.2
  43.0 28.6 all-gather.4

commit v19 on v17

--- a/solution.py
+++ b/solution.py
@@ -296,7 +296,7 @@
         farther = shifted(own, "y", 2)
         far = both_ways(own, "y")
         beside = both_ways(own, "h")
-        other, far = tie((other, far))
+        other, farther = tie((other, farther))
         tails = jnp.concatenate([tokens[rows - HALO :], other[rows - HALO :]], 0)
         halos = lax.ppermute(tails, CTX, [(i, i + 1) for i in range(1, 31, 2)])
     first = (halos, other, farther, far, beside)

time: 120 us -> 122 us (1.017)
  waiting for transfers between devices: 30 us -> 41.8 us
  starting transfers between devices: 51.3 us -> 40.9 us
    ppermute x14, waiting for transfers between devices: 13.2 us -> 31.4 us  [shifted(): return lax.ppermute(array, axis, [(i, (i + step) % n) for i in range(n)])]
    ppermute x14, starting transfers between devices: 28.1 us -> 23 us  [shifted(): return lax.ppermute(array, axis, [(i, (i + step) % n) for i in range(n)])]
    all_to_all x1, starting transfers between devices: 9.28 us -> 5.7 us  [body(): states = lax.all_to_all(state, ('y', 'h'), 0, 0, tiled=True)]
    ppermute x1, waiting for transfers between devices: 3.44 us -> 0.01 us  [body(): halos = lax.ppermute(tails, CTX, [(i, i + 1) for i in range(1, 31, 2)])]
    ppermute x1, starting transfers between devices: 6.87 us -> 5 us  [body(): halos = lax.ppermute(tails, CTX, [(i, i + 1) for i in range(1, 31, 2)])]
    all_gather x1, waiting for transfers between devices: 1.7 us -> 0.01 us  [body(): swapped = lax.all_gather(wide, ('c', 'x'), axis=0, tiled=True)]
  transfers between devices with their start and end apart: 21 -> 21, of which waited for: 10 -> 13; matrix products, arithmetic and copies ran while one was open for 2% -> 2% of each run, Pallas kernels for 9% -> 9%
where the time goes in v19:
time: 122 us; the launch traced here: 121 us
  waiting for transfers between devices  41.8 us (34%)
  starting transfers between devices  40.9 us (34%)
  Pallas kernels  17.4 us (14%)
  between operations  13.6 us (11%)
  local copies, waits for them, and re-layouts  6.02 us (5%)
  other arithmetic  1.6 us (1%)
    ppermute x14, waiting for transfers between devices, shifted(): return lax.ppermute(array, axis, [(i, (i + step) % n) for i in range(n)])  31.4 us
    ppermute x14, starting transfers between devices, shifted(): return lax.ppermute(array, axis, [(i, (i + step) % n) for i in range(n)])  23 us
    all_to_all x1, waiting for transfers between devices, body(): states = lax.all_to_all(state, ('y', 'h'), 0, 0, tiled=True)  7 us
    pallas_call x1, Pallas kernels, body(): pl.pallas_call(functools.partial(project_kernel, sizes, early_runs, late_...  6.06 us
    all_to_all x1, starting transfers between devices, body(): states = lax.all_to_all(state, ('y', 'h'), 0, 0, tiled=True)  5.7 us
    unnamed x23, local copies, waits for them, and re-layouts  5.57 us
    pallas_call x1, Pallas kernels, body(): pl.pallas_call(functools.partial(state_kernel, sizes), out_shape=(full, j...  5.09 us
    ppermute x1, starting transfers between devices, body(): halos = lax.ppermute(tails, CTX, [(i, i + 1) for i in range(1, 31, 2)])  5 us
  transfers between devices with their start and end apart: 21, of which 13 were waited for; matrix products, arithmetic and copies ran while one was open for 2% of the time, Pallas kernels for 9%

profile of v19, /device:TPU:1, one launch (start us, length us, event | category | flops | bytes accessed | tf_op | source)
XLA Modules:
  0.0 121.4 jit_solution(6950079167706757449)
XLA Ops:
  6.5 0.0 all-gather.3.cloned.1.call-start
  6.5 0.7 all-gather.3.cloned.1.call-update
  7.3 0.0 all-gather.5.cloned.1.call-start
  7.3 1.2 copy.10
  8.6 0.1 copy.13
  8.8 3.3 %collective-permute-start.1 = (bf16[128,768]{1,0:T(8,128)(2,1)S(1)}, bf16[128,768]{1,0:T(8,128)(2,1)S(1)}, u32[]{:S(2)}, u32[]{:S(2)}) collective-permute-start(bf16[128,768]{1,0:T(8,128)(2,1)S(1)} %bitcast.17), channel_id=1, source_target_pairs={{0,8},{8,0},{1,9},{9,1},{2,10},{10,2},{3,11},{11,3},{4,12},{12,4},... | collective-permute-start | bytes 589832 | tf_op jit(solution)/shard_map/weight_gather/ppermute | solution.py:291
  12.1 0.0 copy-done.10
  12.1 0.0 collective-permute-start
  12.1 0.1 copy.12
  12.2 0.9 collective-permute-done.1
  13.2 2.0 %collective-permute-start.2 = (bf16[256,768]{1,0:T(8,128)(2,1)S(1)}, bf16[256,768]{1,0:T(8,128)(2,1)S(1)}, u32[]{:S(2)}, u32[]{:S(2)}) collective-permute-start(bf16[256,768]{1,0:T(8,128)(2,1)S(1)} %pad_maximum_fusion.refs_3_), channel_id=1, source_target_pairs={{0,128},{64,192},{128,0},{192,64},{1,129},{65,193},{129,1},{193,65... | collective-permute-start | bytes 1179656 | tf_op jit(solution)/shard_map/weight_rings/ppermute | solution.py:23
  15.3 5.3 %collective-permute-start.7 = (bf16[256,768]{1,0:T(8,128)(2,1)S(1)}, bf16[256,768]{1,0:T(8,128)(2,1)S(1)}, u32[]{:S(2)}, u32[]{:S(2)}) collective-permute-start(bf16[256,768]{1,0:T(8,128)(2,1)S(1)} %pad_maximum_fusion.refs_3_), channel_id=1, source_target_pairs={{0,48},{16,0},{32,16},{48,32},{1,49},{17,1},{33,17},{49,33},{2,50}... | collective-permute-start | bytes 1179656 | tf_op jit(solution)/shard_map/weight_rings/ppermute | solution.py:23
  20.5 0.0 collective-permute-start.6
  20.5 0.8 collective-permute-start.5
  21.3 0.8 collective-permute-done
  22.1 0.0 collective-permute-start.4
  22.1 3.0 %collective-permute-done.2.refs_10_ = bf16[256,768]{1,0:T(8,128)(2,1)S(1)} collective-permute-done((bf16[256,768]{1,0:T(8,128)(2,1)S(1)}, bf16[256,768]{1,0:T(8,128)(2,1)S(1)}, u32[]{:S(2)}, u32[]{:S(2)}) %collective-permute-start.2) | collective-permute-done | bytes 393248 | tf_op jit(solution)/shard_map/weight_rings/ppermute | solution.py:23
  25.2 5.0 %collective-permute-start.3 = (bf16[32,512]{1,0:T(8,128)(2,1)S(1)}, bf16[32,512]{1,0:T(8,128)(2,1)S(1)}, u32[]{:S(2)}, u32[]{:S(2)}) collective-permute-start(bf16[32,512]{1,0:T(8,128)(2,1)S(1)} %pad_maximum_fusion.3), channel_id=1, source_target_pairs={{8,16},{24,32},{40,48},{56,64},{72,80},{88,96},{104,112},{120,128}... | collective-permute-start | bytes 98312 | tf_op jit(solution)/shard_map/weight_rings/ppermute | solution.py:301
  30.2 6.9 %collective-permute-done.7.refs_1_ = bf16[256,768]{1,0:T(8,128)(2,1)S(1)} collective-permute-done((bf16[256,768]{1,0:T(8,128)(2,1)S(1)}, bf16[256,768]{1,0:T(8,128)(2,1)S(1)}, u32[]{:S(2)}, u32[]{:S(2)}) %collective-permute-start.7) | collective-permute-done | bytes 393248 | tf_op jit(solution)/shard_map/weight_rings/ppermute | solution.py:23
  37.1 0.0 collective-permute-done.6.refs_0_
  37.1 0.0 collective-permute-done.5.refs_8_
  37.1 1.2 collective-permute-done.4.refs_6_
  38.3 0.0 collective-permute-done.3
  38.3 0.8 pad_maximum_fusion.1
  39.1 0.1 copy-done.2
  39.1 0.0 all-gather.5.cloned.1.call-update
  39.2 0.9 relay_pair.1
  40.1 5.0 %collective-permute-start.9 = (bf16[512,768]{1,0:T(8,128)(2,1)S(1)}, bf16[512,768]{1,0:T(8,128)(2,1)S(1)}, u32[]{:S(2)}, u32[]{:S(2)}) collective-permute-start(bf16[512,768]{1,0:T(8,128)(2,1)S(1)} %get-tuple-element.42.refs_4_), channel_id=1, source_target_pairs={{0,192},{64,0},{128,64},{192,128},{1,193},{65,1},{129,65},{193,129... | collective-permute-start | bytes 2359304 | tf_op jit(solution)/shard_map/weight_rings/ppermute | solution.py:23
  45.1 0.0 collective-permute-start.8
  45.1 0.0 collective-permute-start.10
  45.1 3.6 %collective-permute-start.11 = (bf16[128,768]{1,0:T(8,128)(2,1)S(1)}, bf16[128,768]{1,0:T(8,128)(2,1)S(1)}, u32[]{:S(2)}, u32[]{:S(2)}) collective-permute-start(bf16[128,768]{1,0:T(8,128)(2,1)S(1)} %get-tuple-element.44), channel_id=1, source_target_pairs={{0,48},{16,0},{32,16},{48,32},{1,49},{17,1},{33,17},{49,33},{2,50}... | collective-permute-start | bytes 589832 | tf_op jit(solution)/shard_map/weight_rings/ppermute | solution.py:23
  48.7 5.2 %collective-permute-done.10.refs_2_ = bf16[128,768]{1,0:T(8,128)(2,1)S(1)} collective-permute-done((bf16[128,768]{1,0:T(8,128)(2,1)S(1)}, bf16[128,768]{1,0:T(8,128)(2,1)S(1)}, u32[]{:S(2)}, u32[]{:S(2)}) %collective-permute-start.10) | collective-permute-done | bytes 196640 | tf_op jit(solution)/shard_map/weight_rings/ppermute | solution.py:23
  53.9 2.7 %collective-permute-done.11.refs_3_ = bf16[128,768]{1,0:T(8,128)(2,1)S(1)} collective-permute-done((bf16[128,768]{1,0:T(8,128)(2,1)S(1)}, bf16[128,768]{1,0:T(8,128)(2,1)S(1)}, u32[]{:S(2)}, u32[]{:S(2)}) %collective-permute-start.11) | collective-permute-done | bytes 196640 | tf_op jit(solution)/shard_map/weight_rings/ppermute | solution.py:23
  56.6 4.2 %collective-permute-done.9.refs_1_.refs_9_ = bf16[512,768]{1,0:T(8,128)(2,1)S(1)} collective-permute-done((bf16[512,768]{1,0:T(8,128)(2,1)S(1)}, bf16[512,768]{1,0:T(8,128)(2,1)S(1)}, u32[]{:S(2)}, u32[]{:S(2)}) %collective-permute-start.9) | collective-permute-done | bytes 786464 | tf_op jit(solution)/shard_map/weight_rings/ppermute | solution.py:23
  60.8 3.2 %collective-permute-done.8.refs_0_.refs_7_ = bf16[512,768]{1,0:T(8,128)(2,1)S(1)} collective-permute-done((bf16[512,768]{1,0:T(8,128)(2,1)S(1)}, bf16[512,768]{1,0:T(8,128)(2,1)S(1)}, u32[]{:S(2)}, u32[]{:S(2)}) %collective-permute-start.8) | collective-permute-done | bytes 786464 | tf_op jit(solution)/shard_map/weight_rings/ppermute | solution.py:23
  64.0 1.4 %relay_far.1 = (bf16[256,768]{1,0:T(8,128)(2,1)}, bf16[256,768]{1,0:T(8,128)(2,1)}, bf16[256,768]{1,0:T(8,128)(2,1)}, bf16[256,768]{1,0:T(8,128)(2,1)}, bf16[256,768]{1,0:T(8,128)(2,1)}) custom-call(bf16[512,768]{1,0:T(8,128)(2,1)S(1)} %collective-permute-done.8.refs_0_.refs_7_, bf16[512,768]{1,0:T(8,128)(2,1)S(1)} %collective-permute-done.9.refs_1_.refs_9_, ...), custom_call_target="tpu_custom_call" | custom-call | bytes 2000000 | tf_op jit(solution)/shard_map/weight_rings/relay_far/pallas_call | solution.py:54
  65.4 0.1 collective-permute-start.12
  65.5 2.7 %collective-permute-start.13 = (bf16[256,768]{1,0:T(8,128)(2,1)}, bf16[256,768]{1,0:T(8,128)(2,1)}, u32[]{:S(2)}, u32[]{:S(2)}) collective-permute-start(bf16[256,768]{1,0:T(8,128)(2,1)} %get-tuple-element.55), channel_id=1, source_target_pairs={{0,192},{64,0},{128,64},{192,128},{1,193},{65,1},{129,65},{193,129... | collective-permute-start | bytes 1179656 | tf_op jit(solution)/shard_map/weight_rings/ppermute | solution.py:23
  68.1 0.0 collective-permute-start.14
  68.1 3.6 %collective-permute-start.15 = (bf16[256,768]{1,0:T(8,128)(2,1)}, bf16[256,768]{1,0:T(8,128)(2,1)}, u32[]{:S(2)}, u32[]{:S(2)}) collective-permute-start(bf16[256,768]{1,0:T(8,128)(2,1)} %get-tuple-element.57), channel_id=1, source_target_pairs={{0,48},{16,0},{32,16},{48,32},{1,49},{17,1},{33,17},{49,33},{2,50}... | collective-permute-start | bytes 1179656 | tf_op jit(solution)/shard_map/weight_rings/ppermute | solution.py:23
  71.7 0.0 collective-permute-start.16
  71.7 0.1 stack.23.refs_0_.pos
  71.8 1.7 %copy-done = bf16[2304,512]{1,0:T(8,128)(2,1)S(1)} copy-done((bf16[2304,512]{1,0:T(8,128)(2,1)S(1)}, bf16[2304,512]{1,0:T(8,128)(2,1)}, u32[]{:S(2)}) %copy-start) | copy-done | bytes 2359320
  73.5 1.6 %copy-done.1 = bf16[2048,512]{1,0:T(8,128)(2,1)S(1)} copy-done((bf16[2048,512]{1,0:T(8,128)(2,1)S(1)}, bf16[2048,512]{1,0:T(8,128)(2,1)}, u32[]{:S(2)}) %copy-start.1) | copy-done | bytes 2097176
  75.1 1.0 copy-done.3
  76.1 6.1 %project.1 = (f32[6,528,128]{2,1,0:T(8,128)S(1)}, bf16[528,1280]{1,0:T(8,128)(2,1)S(1)}) custom-call(s32[5]{0:T(128)S(1)} %stack.23.refs_0_.pos, bf16[2048,512]{1,0:T(8,128)(2,1)S(1)} %copy-done.1, bf16[2304,512]{1,0:T(8,128)(2,1)S(1)} %copy-done, bf16[256,768]{1,0:T(8,128)(2,1)S(1)} %pad_maximum_fusion.refs_3_, ...), custom_call_target="tpu_custom_call" | custom-call | flops 2283798528 | bytes 9000000 | tf_op jit(solution)/shard_map/project/pallas_call | solution.py:347
  82.1 0.0 collective-permute-done.12.refs_2_
  82.1 0.0 collective-permute-done.13.refs_3_
  82.2 3.5 %collective-permute-done.14.refs_4_ = bf16[256,768]{1,0:T(8,128)(2,1)} collective-permute-done((bf16[256,768]{1,0:T(8,128)(2,1)}, bf16[256,768]{1,0:T(8,128)(2,1)}, u32[]{:S(2)}, u32[]{:S(2)}) %collective-permute-start.14) | collective-permute-done | bytes 393248 | tf_op jit(solution)/shard_map/weight_rings/ppermute | solution.py:23
  85.7 1.4 %collective-permute-done.15.refs_5_ = bf16[256,768]{1,0:T(8,128)(2,1)} collective-permute-done((bf16[256,768]{1,0:T(8,128)(2,1)}, bf16[256,768]{1,0:T(8,128)(2,1)}, u32[]{:S(2)}, u32[]{:S(2)}) %collective-permute-start.15) | collective-permute-done | bytes 393248 | tf_op jit(solution)/shard_map/weight_rings/ppermute | solution.py:23
  87.1 0.0 collective-permute-done.16.refs_6_
  87.1 0.0 copy-done.4
  87.1 0.0 copy-done.7
  87.1 0.0 copy-start.6
  87.1 0.0 copy-start.8
  87.1 0.0 copy-start.9
  87.1 5.1 %states.1 = (f32[64,8,256]{2,1,0:T(8,128)S(1)}, f32[2,528,128]{2,1,0:T(8,128)S(1)}, bf16[16,16,256]{2,1,0:T(8,128)(2,1)}) custom-call(s32[5]{0:T(128)S(1)} %stack.23.refs_0_.pos, bf16[528,1280]{1,0:T(8,128)(2,1)S(1)} %get-tuple-element.53.refs_1_, bf16[256,768]{1,0:T(8,128)(2,1)} %collective-permute-done.12.refs_2_, ...), custom_call_target="tpu_custom_call" | custom-call | tf_op jit(solution)/shard_map/states/pallas_call | solution.py:369
  92.2 5.7 %all-to-all-start = ((bf16[16,16,256]{2,1,0:T(8,128)(2,1)}), bf16[16,16,256]{2,1,0:T(8,128)(2,1)S(1)}, u32[]{:S(2)}, u32[]{:S(2)}) async-start(bf16[16,16,256]{2,1,0:T(8,128)(2,1)} %get-tuple-element.64), calls=%async_computation | async-start | bytes 262144 | tf_op jit(solution)/shard_map/state_exchange/all_to_all | solution.py:387
  98.0 2.5 %local.1 = (f32[64,8,256]{2,1,0:T(8,128)S(1)}, f32[64,8,256]{2,1,0:T(8,128)S(1)}, f32[16,8,256]{2,1,0:T(8,128)S(1)}) custom-call(s32[5]{0:T(128)S(1)} %stack.23.refs_0_.pos, f32[2,528,128]{2,1,0:T(8,128)S(1)} %get-tuple-element.59.gated, f32[3,3,512]{2,1,0:T(4,128)S(1)} %copy-done.8, f32[64,8,256]{2,1,0:T(8,128)S(1)} %get-tuple-element.60.product, ...), custom_call_target="tpu_custom_call" | custom-call | flops 30000000 | bytes 2000000 | tf_op jit(solution)/shard_map/local/pallas_call | solution.py:388
  100.4 7.0 %all-to-all-done.states = bf16[16,16,256]{2,1,0:T(8,128)(2,1)S(1)} async-done(((bf16[16,16,256]{2,1,0:T(8,128)(2,1)}), bf16[16,16,256]{2,1,0:T(8,128)(2,1)S(1)}, u32[]{:S(2)}, u32[]{:S(2)}) %all-to-all-start) | async-done | bytes 131104 | tf_op jit(solution)/shard_map/state_exchange/all_to_all | solution.py:387
  107.4 1.5 %finish.1 = (bf16[256,256]{1,0:T(8,128)(2,1)S(1)}, bf16[256,256]{1,0:T(8,128)(2,1)S(1)}) custom-call(s32[5]{0:T(128)S(1)} %stack.23.refs_0_.pos, f32[64,8,256]{2,1,0:T(8,128)S(1)} %get-tuple-element.61.gate, f32[64,8,256]{2,1,0:T(8,128)S(1)} %get-tuple-element.62.local, f32[16,8,256]{2,1,0:T(8,128)S(1)} %get-tuple-element.63.inside, ...), custom_call_target="tpu_custom_call" | custom-call | tf_op jit(solution)/shard_map/finish/pallas_call | solution.py:399
  109.0 3.9 %collective-permute-start.17 = (bf16[256,256]{1,0:T(8,128)(2,1)S(1)}, bf16[256,256]{1,0:T(8,128)(2,1)S(1)}, u32[]{:S(2)}, u32[]{:S(2)}) collective-permute-start(bf16[256,256]{1,0:T(8,128)(2,1)S(1)} %get-tuple-element.66), channel_id=1, source_target_pairs={{0,8},{8,0},{1,9},{9,1},{2,10},{10,2},{3,11},{11,3},{4,12},{12,4},... | collective-permute-start | bytes 393224 | tf_op jit(solution)/shard_map/result_swap/ppermute | solution.py:409
  112.8 1.0 collective-permute-done.17
  113.9 0.7 pad_maximum_fusion.2
  (22 shorter events, 0.2 us)
Async XLA Ops:
  6.5 5.6 %copy-start.10 = (bf16[256,512]{1,0:T(8,128)(2,1)S(1)}, bf16[256,512]{1,0:T(8,128)(2,1)}, u32[]{:S(2)}) copy-start(bf16[256,512]{1,0:T(8,128)(2,1)} %param.6) | copy-start | bytes 786436
  6.5 65.3 %all-gather.3.cloned.1.call-start = ((), (), s32[]{:S(2)}) async-start(), calls=%async_computation.1 | async-start | bytes 2359296 | tf_op jit(solution)/shard_map/token_gather/all_gather | solution.py:305
  7.3 64.6 %all-gather.5.cloned.1.call-start = ((), (), s32[]{:S(2)}) async-start(), calls=%async_computation.2 | async-start | bytes 2654208 | tf_op jit(solution)/shard_map/token_gather/all_gather | solution.py:307
  8.8 4.4 %collective-permute-start.1 = (bf16[128,768]{1,0:T(8,128)(2,1)S(1)}, bf16[128,768]{1,0:T(8,128)(2,1)S(1)}, u32[]{:S(2)}, u32[]{:S(2)}) collective-permute-start(bf16[128,768]{1,0:T(8,128)(2,1)S(1)} %bitcast.17), channel_id=1, source_target_pairs={{0,8},{8,0},{1,9},{9,1},{2,10},{10,2},{3,11},{11,3},{4,12},{12,4},... | collective-permute-start | bytes 589832 | tf_op jit(solution)/shard_map/weight_gather/ppermute | solution.py:291
  12.1 10.0 %collective-permute-start = (bf16[256,512]{1,0:T(8,128)(2,1)S(1)}, bf16[256,512]{1,0:T(8,128)(2,1)S(1)}, u32[]{:S(2)}, u32[]{:S(2)}) collective-permute-start(bf16[256,512]{1,0:T(8,128)(2,1)S(1)} %copy-done.10), channel_id=1, source_target_pairs={{0,4},{4,0},{1,5},{5,1},{2,6},{6,2},{3,7},{7,3},{8,12},{12,8},{9,1... | collective-permute-start | bytes 786440 | tf_op jit(solution)/shard_map/token_swap/ppermute | solution.py:294
  13.2 11.9 %collective-permute-start.2 = (bf16[256,768]{1,0:T(8,128)(2,1)S(1)}, bf16[256,768]{1,0:T(8,128)(2,1)S(1)}, u32[]{:S(2)}, u32[]{:S(2)}) collective-permute-start(bf16[256,768]{1,0:T(8,128)(2,1)S(1)} %pad_maximum_fusion.refs_3_), channel_id=1, source_target_pairs={{0,128},{64,192},{128,0},{192,64},{1,129},{65,193},{129,1},{193,65... | collective-permute-start | bytes 1179656 | tf_op jit(solution)/shard_map/weight_rings/ppermute | solution.py:23
  15.3 21.8 %collective-permute-start.7 = (bf16[256,768]{1,0:T(8,128)(2,1)S(1)}, bf16[256,768]{1,0:T(8,128)(2,1)S(1)}, u32[]{:S(2)}, u32[]{:S(2)}) collective-permute-start(bf16[256,768]{1,0:T(8,128)(2,1)S(1)} %pad_maximum_fusion.refs_3_), channel_id=1, source_target_pairs={{0,48},{16,0},{32,16},{48,32},{1,49},{17,1},{33,17},{49,33},{2,50}... | collective-permute-start | bytes 1179656 | tf_op jit(solution)/shard_map/weight_rings/ppermute | solution.py:23
  20.5 16.6 %collective-permute-start.6 = (bf16[256,768]{1,0:T(8,128)(2,1)S(1)}, bf16[256,768]{1,0:T(8,128)(2,1)S(1)}, u32[]{:S(2)}, u32[]{:S(2)}) collective-permute-start(bf16[256,768]{1,0:T(8,128)(2,1)S(1)} %pad_maximum_fusion.refs_3_), channel_id=1, source_target_pairs={{0,16},{16,32},{32,48},{48,0},{1,17},{17,33},{33,49},{49,1},{2,18}... | collective-permute-start | bytes 1179656 | tf_op jit(solution)/shard_map/weight_rings/ppermute | solution.py:23
  20.5 16.6 %collective-permute-start.5 = (bf16[256,768]{1,0:T(8,128)(2,1)S(1)}, bf16[256,768]{1,0:T(8,128)(2,1)S(1)}, u32[]{:S(2)}, u32[]{:S(2)}) collective-permute-start(bf16[256,768]{1,0:T(8,128)(2,1)S(1)} %pad_maximum_fusion.refs_3_), channel_id=1, source_target_pairs={{0,192},{64,0},{128,64},{192,128},{1,193},{65,1},{129,65},{193,129... | collective-permute-start | bytes 1179656 | tf_op jit(solution)/shard_map/weight_rings/ppermute | solution.py:23
  22.1 16.2 %collective-permute-start.4 = (bf16[256,768]{1,0:T(8,128)(2,1)S(1)}, bf16[256,768]{1,0:T(8,128)(2,1)S(1)}, u32[]{:S(2)}, u32[]{:S(2)}) collective-permute-start(bf16[256,768]{1,0:T(8,128)(2,1)S(1)} %pad_maximum_fusion.refs_3_), channel_id=1, source_target_pairs={{0,64},{64,128},{128,192},{192,0},{1,65},{65,129},{129,193},{193,1... | collective-permute-start | bytes 1179656 | tf_op jit(solution)/shard_map/weight_rings/ppermute | solution.py:23
  25.2 13.1 %collective-permute-start.3 = (bf16[32,512]{1,0:T(8,128)(2,1)S(1)}, bf16[32,512]{1,0:T(8,128)(2,1)S(1)}, u32[]{:S(2)}, u32[]{:S(2)}) collective-permute-start(bf16[32,512]{1,0:T(8,128)(2,1)S(1)} %pad_maximum_fusion.3), channel_id=1, source_target_pairs={{8,16},{24,32},{40,48},{56,64},{72,80},{88,96},{104,112},{120,128}... | collective-permute-start | bytes 98312 | tf_op jit(solution)/shard_map/weight_rings/ppermute | solution.py:301
  38.3 0.9 copy-start.2
  40.1 20.7 %collective-permute-start.9 = (bf16[512,768]{1,0:T(8,128)(2,1)S(1)}, bf16[512,768]{1,0:T(8,128)(2,1)S(1)}, u32[]{:S(2)}, u32[]{:S(2)}) collective-permute-start(bf16[512,768]{1,0:T(8,128)(2,1)S(1)} %get-tuple-element.42.refs_4_), channel_id=1, source_target_pairs={{0,192},{64,0},{128,64},{192,128},{1,193},{65,1},{129,65},{193,129... | collective-permute-start | bytes 2359304 | tf_op jit(solution)/shard_map/weight_rings/ppermute | solution.py:23
  45.1 18.9 %collective-permute-start.8 = (bf16[512,768]{1,0:T(8,128)(2,1)S(1)}, bf16[512,768]{1,0:T(8,128)(2,1)S(1)}, u32[]{:S(2)}, u32[]{:S(2)}) collective-permute-start(bf16[512,768]{1,0:T(8,128)(2,1)S(1)} %get-tuple-element.42.refs_4_), channel_id=1, source_target_pairs={{0,64},{64,128},{128,192},{192,0},{1,65},{65,129},{129,193},{193,1... | collective-permute-start | bytes 2359304 | tf_op jit(solution)/shard_map/weight_rings/ppermute | solution.py:23
  45.1 8.8 %collective-permute-start.10 = (bf16[128,768]{1,0:T(8,128)(2,1)S(1)}, bf16[128,768]{1,0:T(8,128)(2,1)S(1)}, u32[]{:S(2)}, u32[]{:S(2)}) collective-permute-start(bf16[128,768]{1,0:T(8,128)(2,1)S(1)} %get-tuple-element.43), channel_id=1, source_target_pairs={{0,16},{16,32},{32,48},{48,0},{1,17},{17,33},{33,49},{49,1},{2,18}... | collective-permute-start | bytes 589832 | tf_op jit(solution)/shard_map/weight_rings/ppermute | solution.py:23
  45.1 11.4 %collective-permute-start.11 = (bf16[128,768]{1,0:T(8,128)(2,1)S(1)}, bf16[128,768]{1,0:T(8,128)(2,1)S(1)}, u32[]{:S(2)}, u32[]{:S(2)}) collective-permute-start(bf16[128,768]{1,0:T(8,128)(2,1)S(1)} %get-tuple-element.44), channel_id=1, source_target_pairs={{0,48},{16,0},{32,16},{48,32},{1,49},{17,1},{33,17},{49,33},{2,50}... | collective-permute-start | bytes 589832 | tf_op jit(solution)/shard_map/weight_rings/ppermute | solution.py:23
  65.4 16.7 %collective-permute-start.12 = (bf16[256,768]{1,0:T(8,128)(2,1)}, bf16[256,768]{1,0:T(8,128)(2,1)}, u32[]{:S(2)}, u32[]{:S(2)}) collective-permute-start(bf16[256,768]{1,0:T(8,128)(2,1)} %get-tuple-element.54), channel_id=1, source_target_pairs={{0,64},{64,128},{128,192},{192,0},{1,65},{65,129},{129,193},{193,1... | collective-permute-start | bytes 1179656 | tf_op jit(solution)/shard_map/weight_rings/ppermute | solution.py:23
  65.5 16.7 %collective-permute-start.13 = (bf16[256,768]{1,0:T(8,128)(2,1)}, bf16[256,768]{1,0:T(8,128)(2,1)}, u32[]{:S(2)}, u32[]{:S(2)}) collective-permute-start(bf16[256,768]{1,0:T(8,128)(2,1)} %get-tuple-element.55), channel_id=1, source_target_pairs={{0,192},{64,0},{128,64},{192,128},{1,193},{65,1},{129,65},{193,129... | collective-permute-start | bytes 1179656 | tf_op jit(solution)/shard_map/weight_rings/ppermute | solution.py:23
  68.1 17.5 %collective-permute-start.14 = (bf16[256,768]{1,0:T(8,128)(2,1)}, bf16[256,768]{1,0:T(8,128)(2,1)}, u32[]{:S(2)}, u32[]{:S(2)}) collective-permute-start(bf16[256,768]{1,0:T(8,128)(2,1)} %get-tuple-element.56), channel_id=1, source_target_pairs={{0,16},{16,32},{32,48},{48,0},{1,17},{17,33},{33,49},{49,1},{2,18}... | collective-permute-start | bytes 1179656 | tf_op jit(solution)/shard_map/weight_rings/ppermute | solution.py:23
  68.1 18.9 %collective-permute-start.15 = (bf16[256,768]{1,0:T(8,128)(2,1)}, bf16[256,768]{1,0:T(8,128)(2,1)}, u32[]{:S(2)}, u32[]{:S(2)}) collective-permute-start(bf16[256,768]{1,0:T(8,128)(2,1)} %get-tuple-element.57), channel_id=1, source_target_pairs={{0,48},{16,0},{32,16},{48,32},{1,49},{17,1},{33,17},{49,33},{2,50}... | collective-permute-start | bytes 1179656 | tf_op jit(solution)/shard_map/weight_rings/ppermute | solution.py:23
  71.7 15.3 %collective-permute-start.16 = (bf16[256,768]{1,0:T(8,128)(2,1)}, bf16[256,768]{1,0:T(8,128)(2,1)}, u32[]{:S(2)}, u32[]{:S(2)}) collective-permute-start(bf16[256,768]{1,0:T(8,128)(2,1)} %get-tuple-element.49.refs_5_), channel_id=1, source_target_pairs={{0,128},{64,192},{128,0},{192,64},{1,129},{65,193},{129,1},{193,65... | collective-permute-start | bytes 1179656 | tf_op jit(solution)/shard_map/weight_rings/ppermute | solution.py:23
  71.8 1.7 %copy-start = (bf16[2304,512]{1,0:T(8,128)(2,1)S(1)}, bf16[2304,512]{1,0:T(8,128)(2,1)}, u32[]{:S(2)}) copy-start(bf16[2304,512]{1,0:T(8,128)(2,1)} %all-gather.5.cloned.1.call-done.refs_2_) | copy-start | bytes 7077892
  73.5 1.6 %copy-start.1 = (bf16[2048,512]{1,0:T(8,128)(2,1)S(1)}, bf16[2048,512]{1,0:T(8,128)(2,1)}, u32[]{:S(2)}) copy-start(bf16[2048,512]{1,0:T(8,128)(2,1)} %all-gather.3.cloned.1.call-done.refs_1_) | copy-start | bytes 6291460
  75.1 1.0 copy-start.3
  76.1 11.0 %copy-start.4 = (f32[16,512]{1,0:T(8,128)S(1)}, f32[16,512]{1,0:T(8,128)}, u32[]{:S(2)}) copy-start(f32[16,512]{1,0:T(8,128)} %decay.3) | copy-start | bytes 98308
  76.1 11.0 %copy-start.7 = (f32[3,3,512]{2,1,0:T(4,128)S(1)}, f32[3,3,512]{2,1,0:T(4,128)}, u32[]{:S(2)}) copy-start(f32[3,3,512]{2,1,0:T(4,128)} %taps.1) | copy-start | bytes 55300
  87.1 10.8 %copy-start.5 = (f32[16,512]{1,0:T(8,128)S(1)}, f32[16,512]{1,0:T(8,128)}, u32[]{:S(2)}) copy-start(f32[16,512]{1,0:T(8,128)} %decay.3) | copy-start | bytes 98308
  87.1 10.8 %copy-start.6 = (f32[16,512]{1,0:T(8,128)S(1)}, f32[16,512]{1,0:T(8,128)}, u32[]{:S(2)}) copy-start(f32[16,512]{1,0:T(8,128)} %gain.3) | copy-start | bytes 98308
  87.1 10.8 %copy-start.8 = (f32[3,3,512]{2,1,0:T(4,128)S(1)}, f32[3,3,512]{2,1,0:T(4,128)}, u32[]{:S(2)}) copy-start(f32[3,3,512]{2,1,0:T(4,128)} %taps.1) | copy-start | bytes 55300
  87.1 10.8 %copy-start.9 = (f32[512]{0:T(512)S(1)}, f32[512]{0:T(512)}, u32[]{:S(2)}) copy-start(f32[512]{0:T(512)} %param.11) | copy-start | bytes 6148
  92.2 15.2 %all-to-all-start = ((bf16[16,16,256]{2,1,0:T(8,128)(2,1)}), bf16[16,16,256]{2,1,0:T(8,128)(2,1)S(1)}, u32[]{:S(2)}, u32[]{:S(2)}) async-start(bf16[16,16,256]{2,1,0:T(8,128)(2,1)} %get-tuple-element.64), calls=%async_computation | async-start | bytes 262144 | tf_op jit(solution)/shard_map/state_exchange/all_to_all | solution.py:387
  109.0 4.9 %collective-permute-start.17 = (bf16[256,256]{1,0:T(8,128)(2,1)S(1)}, bf16[256,256]{1,0:T(8,128)(2,1)S(1)}, u32[]{:S(2)}, u32[]{:S(2)}) collective-permute-start(bf16[256,256]{1,0:T(8,128)(2,1)S(1)} %get-tuple-element.66), channel_id=1, source_target_pairs={{0,8},{8,0},{1,9},{9,1},{2,10},{10,2},{3,11},{11,3},{4,12},{12,4},... | collective-permute-start | bytes 393224 | tf_op jit(solution)/shard_map/result_swap/ppermute | solution.py:409
Sparse Core Ops, SparseCore 0:
  9.2 31.8 all-gather.2
  43.0 28.4 all-gather.4
